TPU v7x, 32 devices: a whole 2x2x4 slice. The times are simulated.
32 devices in a mesh: seq: 8 (over z, y), head: 4 (over x, core).
Axes of the slice: x: 2, y: 2, z: 4, core: 2. Of those that a mesh axis runs over, the one named last changes fastest.
Arguments:
- queries: bfloat16 [2048, 8192], P('seq', 'head'), may hold values from -6 to 6
- keys: bfloat16 [2048, 8192], P('seq', 'head'), may hold values from -6 to 6
- values: bfloat16 [2048, 8192], P('seq', 'head'), may hold values from -20 to 20
- out_grad: bfloat16 [2048, 8192], P('seq', 'head'), may hold values from -6 to 6
- norm_gain: bfloat16 [8192], P('head'), may hold values from 0.099609375 to 1.8984375
Outputs:
- query_grad: bfloat16 [2048, 8192], P('seq', 'head')
- key_grad: bfloat16 [2048, 8192], P('seq', 'head')
- value_grad: bfloat16 [2048, 8192], P('seq', 'head')
All inputs are finite; a program needn't handle non-finite values.
Results may differ from a plain program's by a relative error of at most 0.0058.
Values sent between devices are 32-bit elements; how exact they have to be, the bound alone decides.
No kernel may reach another device: no remote copies, remote signals or barrier semaphores. Data moves between devices by JAX's collectives and lax.ppermute only.
A program may use at most 192 MiB of HBM per device.

v0:
```python
import jax
import jax.numpy as jnp
from jax import lax
from jax.sharding import PartitionSpec as P

DH = 128
GROUP = 256


def carried_in(part, axis, combine, identity, reverse):
    count = lax.axis_size(axis)
    place = lax.axis_index(axis)
    ahead = count - 1 - place if reverse else place
    gathered = lax.all_gather(part, axis)
    state = jnp.zeros_like(part) + jnp.asarray(identity, part.dtype)

    def one(turn, state):
        source = count - 1 - turn if reverse else turn
        return combine(state, lax.dynamic_index_in_dim(gathered, source, 0, False))

    return lax.fori_loop(0, ahead, one, state)


def add_terms(earlier, later):
    return earlier + later


def causal_mask(count):
    rows = lax.broadcasted_iota(jnp.int32, (count, count), 0)
    cols = lax.broadcasted_iota(jnp.int32, (count, count), 1)
    return (rows >= cols).astype(jnp.float32)


def shards(queries, keys, values, out_grad, norm_gain):
    tokens, width = queries.shape
    blocks = tokens // GROUP
    heads = width // DH
    f32 = jnp.float32
    bf16 = jnp.bfloat16

    def to_heads(array):
        return jnp.transpose(array.reshape(blocks, GROUP, heads, DH), (2, 0, 1, 3))

    def to_rows(array):
        return jnp.transpose(array, (1, 2, 0, 3)).reshape(tokens, width)

    query_h, key_h, value_h = (to_heads(queries), to_heads(keys), to_heads(values))
    grad_h = to_heads(out_grad)
    masking = causal_mask(GROUP)
    block_states = jnp.einsum("hncd,hnce->hnde", key_h, value_h, preferred_element_type=f32)
    device_state = jnp.sum(block_states, axis=1)
    earlier = carried_in(device_state, "seq", add_terms, jnp.zeros_like(device_state), False)
    prior = earlier[:, None] + jnp.cumsum(block_states, axis=1) - block_states
    prior_bf = prior.astype(bf16)
    scores = jnp.einsum("hncd,hnkd->hnck", query_h, key_h, preferred_element_type=f32)
    masked = (scores * masking).astype(bf16)
    attn = jnp.einsum("hnck,hnkd->hncd", masked, value_h, preferred_element_type=f32)
    attn = attn + jnp.einsum("hncd,hnde->hnce", query_h, prior_bf, preferred_element_type=f32)
    gain_h = norm_gain.astype(f32).reshape(heads, 1, 1, DH)
    scaled = gain_h * grad_h.astype(f32)
    square_part = jnp.sum(attn * attn, axis=(0, 3))
    cross_part = jnp.sum(scaled * attn, axis=(0, 3))
    square_sum, cross_sum = lax.psum((square_part, cross_part), "head")
    features = lax.axis_size("head") * width
    inverse = lax.rsqrt(square_sum / features + 1e-05)[None, :, :, None]
    cross = (cross_sum / features)[None, :, :, None]
    delta = (inverse * scaled - attn * inverse * inverse * inverse * cross).astype(bf16)
    dscore = jnp.einsum("hnce,hnke->hnck", delta, value_h, preferred_element_type=f32)
    dscore = (dscore * masking).astype(bf16)
    query_grad = jnp.einsum("hnck,hnkd->hncd", dscore, key_h, preferred_element_type=f32)
    query_grad = query_grad + jnp.einsum(
        "hnce,hnde->hncd", delta, prior_bf, preferred_element_type=f32
    )
    grad_states = jnp.einsum("hncd,hnce->hnde", query_h, delta, preferred_element_type=f32)
    grad_device = jnp.sum(grad_states, axis=1)
    after = carried_in(grad_device, "seq", add_terms, jnp.zeros_like(grad_device), True)
    later = after[:, None] + grad_device[:, None] - jnp.cumsum(grad_states, axis=1)
    later_bf = later.astype(bf16)
    key_grad = jnp.einsum("hnck,hncd->hnkd", dscore, query_h, preferred_element_type=f32)
    key_grad = key_grad + jnp.einsum(
        "hnce,hnde->hncd", value_h, later_bf, preferred_element_type=f32
    )
    value_grad = jnp.einsum("hnck,hnce->hnke", masked, delta, preferred_element_type=f32)
    value_grad = value_grad + jnp.einsum(
        "hncd,hnde->hnce", key_h, later_bf, preferred_element_type=f32
    )
    return (
        to_rows(query_grad.astype(bf16)),
        to_rows(key_grad.astype(bf16)),
        to_rows(value_grad.astype(bf16)),
    )


def solution(mesh):
    return jax.shard_map(
        shards,
        mesh=mesh,
        in_specs=(
            P("seq", "head"),
            P("seq", "head"),
            P("seq", "head"),
            P("seq", "head"),
            P("head"),
        ),
        out_specs=(P("seq", "head"), P("seq", "head"), P("seq", "head")),
        check_vma=False,
    )
```

profile of v0, /device:TPU:0, one launch (start us, length us, event | category | flops | bytes accessed | tf_op | source)
XLA Modules:
  0.0 321.7 jit_solution(68841763806856211)
XLA Ops:
  7.2 1.5 copy.59
  8.8 0.2 bitcast_bitcast_fusion.1
  9.0 0.2 copy.60
  9.2 0.9 copy-done.7
  10.1 1.6 fusion.13
  11.7 1.5 copy.58
  13.2 2.6 copy.31
  15.9 0.2 bitcast_bitcast_fusion
  16.1 0.7 multiply_convert_fusion.1
  16.8 1.3 copy-done
  18.1 2.2 fusion.18
  20.3 119.1 %all-gather.5.cloned.1.call-done = f32[128,128,128]{2,1,0:T(8,128)} async-done(((f32[16,128,128]{2,1,0:T(8,128)}), f32[128,128,128]{2,1,0:T(8,128)}) %all-gather.5.cloned.1.call-update) | async-done | bytes 8388624 | tf_op jit(solution)/shard_map/all_gather | solution.py:14
  139.5 0.1 broadcast.23.clone
  139.6 1.5 fusion.4
  141.1 0.4 copy-done.1
  141.5 2.4 fusion.3
  143.9 1.3 copy-done.2
  145.2 0.3 multiply_reduce_fusion
  145.5 6.1 %all-reduce = (f32[1,256]{1,0:T(1,128)S(1)}, f32[1,256]{1,0:T(1,128)S(1)}) all-reduce(f32[1,256]{1,0:T(1,128)S(1)} %bitcast.147, f32[1,256]{1,0:T(1,128)S(1)} %bitcast.148), channel_id=1, replica_groups=mesh['seq'=8,'head'=4] {'head'}, use_global_device_ids=true, to_apply=%region_5.6 | all-reduce | flops 512 | bytes 4096 | tf_op jit(solution)/shard_map/psum | solution.py:63
  151.7 2.8 fusion.6
  154.4 1.4 convolution_bitcast_fusion
  155.9 2.5 copy.36
  158.4 1.2 bitcast_bitcast_fusion.2
  159.6 0.8 multiply_convert_fusion
  160.4 0.4 copy-done.8
  160.8 0.8 fusion.20
  161.7 0.5 copy-done.3
  162.2 0.4 add_convert_fusion
  162.7 1.4 copy.39
  164.1 3.6 %fusion.32 = f32[16,256,128]{1,2,0:T(8,128)} fusion(bf16[16,256,128]{1,2,0:T(8,128)(2,1)S(1)} %fusion.6, bf16[16,256,256]{2,1,0:T(8,128)(2,1)} %copy-done), kind=kOutput, calls=%fused_computation.54 | convolution fusion | flops 268435456 | bytes 5242880 | tf_op jit(solution)/shard_map/hnck,hnce->hnke/dot_general | solution.py:83
  167.7 1.9 fusion.7
  169.6 122.4 %all-gather.7.cloned.1.call-done = f32[128,128,128]{2,1,0:T(8,128)} async-done(((f32[16,128,128]{2,1,0:T(8,128)}), f32[128,128,128]{2,1,0:T(8,128)}) %all-gather.7.cloned.1.call-update) | async-done | bytes 8388624 | tf_op jit(solution)/shard_map/all_gather | solution.py:14
  291.9 0.1 broadcast.23
  292.0 10.6 %while.23 = (s32[]{:T(128)}, f32[16,128,128]{2,1,0:T(8,128)S(1)}, s32[]{:T(128)}, f32[8,16,128,128]{3,2,1,0:T(8,128)}, s32[]{:T(128)}, /*index=5*/s32[]{:T(128)}, s32[]{:T(128)}, s32[]{:T(128)}) while((s32[]{:T(128)}, f32[16,128,128]{2,1,0:T(8,128)S(1)}, s32[]{:T(128)}, f32[8,16,128,128]{3,2,1,0:T(8,128)}, s32[]{:T(128)}, ...), condition=%wide.region_7.8_spmd, body=%wide.region_6.7_spmd.sunk | while | flops 262150 | bytes 3145871 | solution.py:21
  292.1 1.5 bitcast_add_fusion.8
  293.6 1.5 bitcast_add_fusion.8
  295.1 1.5 bitcast_add_fusion.8
  296.6 1.5 bitcast_add_fusion.8
  298.1 1.5 bitcast_add_fusion.8
  299.6 1.5 bitcast_add_fusion.8
  301.1 1.5 bitcast_add_fusion.8
  302.6 1.3 copy.37
  303.9 1.8 fusion.5
  305.8 0.4 copy-done.10
  306.2 1.5 fusion
  307.6 2.4 copy.41
  310.0 2.5 fusion.1
  312.6 2.3 copy.40
  (35 shorter events, 0.3 us)
Async XLA Ops:
  7.2 132.3 %all-gather.5.cloned.1.call-start = ((), (), s32[]{:S(2)}) async-start(), calls=%async_computation | async-start | bytes 9437184 | tf_op jit(solution)/shard_map/all_gather | solution.py:14
  7.2 1.8 copy-start.15
  8.8 7.3 %copy-start.5 = (bf16[32,8,16,128]{3,2,1,0:T(8,128)(2,1)}, bf16[32,8,16,128]{3,2,1,0:T(8,128)(2,1)S(1)}, u32[]{:S(2)}) copy-start(bf16[32,8,16,128]{3,2,1,0:T(8,128)(2,1)S(1)} %copy.59) | copy-start | bytes 3145732
  9.0 1.1 copy-start.7
  11.7 280.3 %all-gather.7.cloned.1.call-start = ((), (), s32[]{:S(2)}) async-start(), calls=%async_computation.1 | async-start | bytes 9437184 | tf_op jit(solution)/shard_map/all_gather | solution.py:14
  13.2 2.7 copy-start.16
  16.8 1.3 copy-start
  139.6 1.9 copy-start.1
  141.1 2.8 copy-start.11
  143.9 1.3 copy-start.2
  159.6 1.2 copy-start.8
  160.8 1.4 copy-start.3
  160.8 1.4 copy-start.12
  164.1 3.6 %copy-start.4 = (bf16[16,256,256]{2,1,0:T(8,128)(2,1)S(1)}, bf16[16,256,256]{2,1,0:T(8,128)(2,1)}, u32[]{:S(2)}) copy-start(bf16[16,256,256]{2,1,0:T(8,128)(2,1)} %copy-done.3) | copy-start | bytes 6291460
  164.1 3.6 %copy-start.14 = (bf16[16,256,128]{2,0,1:T(8,128)(2,1)S(1)}, bf16[16,256,128]{2,0,1:T(8,128)(2,1)}, u32[]{:S(2)}) copy-start(bf16[16,256,128]{2,0,1:T(8,128)(2,1)} %bitcast_bitcast_fusion.2) | copy-start | bytes 3145732
  302.6 3.2 copy-start.6
  303.9 2.2 copy-start.10
  306.2 1.5 copy-start.13
  307.6 2.4 copy-start.9
Sparse Core Ops, SparseCore 0:
  11.8 127.6 all-gather.4
  158.6 133.3 all-gather.6
where the time goes:
time: 322 us
  waiting for transfers between devices  242 us (75%)
  local copies, waits for them, and re-layouts  22.8 us (7%)
  matrix products  19.8 us (6%)
  other arithmetic  16.8 us (5%)
  between operations  14.3 us (4%)
  blocking collectives  6.15 us (2%)
    all_gather x2, waiting for transfers between devices, carried_in(): gathered = lax.all_gather(part, axis)  241 us
    unnamed x40, local copies, waits for them, and re-layouts  14.6 us
    add x7, other arithmetic, add_terms(): return earlier + later  10.4 us
  transfers between devices with their start and end apart: 2, of which 2 were waited for; matrix products, arithmetic and copies ran while one was open for 5% of the time, Pallas kernels for 0%

commit v1 on v0

v1 whole, which is shorter than its diff:
```python
import functools

import jax
import jax.numpy as jnp
from jax import lax
from jax.experimental import pallas as pl
from jax.experimental.pallas import tpu as pltpu
from jax.sharding import PartitionSpec as P

DH = 128
GROUP = 256
CHUNKS = 4
EPS = 1e-05
F32 = jnp.float32
BF16 = jnp.bfloat16


def dot(a, b, ca, cb):
    return lax.dot_general(a, b, (((ca,), (cb,)), ((), ())), preferred_element_type=F32)


def head(ref, j):
    return ref[:, j * DH:(j + 1) * DH]


def causal():
    rows = lax.broadcasted_iota(jnp.int32, (GROUP, GROUP), 0)
    cols = lax.broadcasted_iota(jnp.int32, (GROUP, GROUP), 1)
    return rows >= cols


def masked(scores, mask):
    return jnp.where(mask, scores, 0.0).astype(BF16)


def call(body, place, ins, outs, grid=(1,), aliases=None, flops=0):
    size = sum(a.size * a.dtype.itemsize // 2 for a, _, _ in ins)
    return pl.pallas_call(
        body,
        grid_spec=pltpu.PrefetchScalarGridSpec(
            num_scalar_prefetch=1,
            grid=grid,
            in_specs=[pl.BlockSpec(b, m) for _, b, m in ins],
            out_specs=[pl.BlockSpec(b, m) for _, _, b, m in outs],
        ),
        out_shape=[jax.ShapeDtypeStruct(s, d) for s, d, _, _ in outs],
        input_output_aliases=aliases or {},
        compiler_params=pltpu.CompilerParams(vmem_limit_bytes=24 * 1024 * 1024),
        cost_estimate=pl.CostEstimate(flops=flops, bytes_accessed=size, transcendentals=0),
    )(place, *[a for a, _, _ in ins])


def states_body(per, place, a, b, *outs):
    for c, out in enumerate(outs):
        for j in range(per):
            h = c * per + j
            out[j] = dot(head(a, h), head(b, h), 0, 0)


def local_body(heads, place, q, k, v, scores, attn):
    mask = causal()
    for j in range(heads):
        s = masked(dot(head(q, j), head(k, j), 1, 1), mask)
        scores[j] = s
        attn[:, j * DH:(j + 1) * DH] = dot(s, head(v, j), 1, 0)


def attn_body(per, first, last, place, al_k, al_o, q_k, q_o, g_k, g_o, n_k, n_o, e, r, other, *refs):
    if not first:
        sq_in, cr_in, *refs = refs
    at_k, at_o, sb_k, sb_o, *stats = refs
    second = place[0] == 1
    square = jnp.zeros((GROUP, DH), F32) if first else sq_in[...]
    cross = jnp.zeros((GROUP, DH), F32) if first else cr_in[...]
    for j in range(per):
        kept = jnp.where(second, e[j] + r[j], e[j]).astype(BF16)
        sb_k[j] = kept
        sb_o[j] = other[j].astype(BF16)
        for al, q, g, n, sb, at in (
            (al_k, q_k, g_k, n_k, sb_k, at_k),
            (al_o, q_o, g_o, n_o, sb_o, at_o),
        ):
            x = head(al, j) + dot(head(q, j), sb[j], 1, 0)
            at[:, j * DH:(j + 1) * DH] = x
            scaled = head(n, j).astype(F32) * head(g, j).astype(F32)
            square = square + x * x
            cross = cross + scaled * x
    if last:
        stats[0][0:1] = jnp.sum(square.T, axis=0, keepdims=True)
        stats[0][1:2] = jnp.sum(cross.T, axis=0, keepdims=True)
    else:
        stats[0][...] = square
        stats[1][...] = cross


def delta_body(per, chunks, parts, features, place, *refs):
    stats = refs[:parts]
    attn = refs[parts:parts + chunks]
    q, g, n, d = refs[parts + chunks:parts + chunks + 4]
    outs = refs[parts + chunks + 4:]
    total = stats[0][...]
    for s in stats[1:]:
        total = total + s[...]
    inverse = lax.rsqrt(total[0:1] / features + EPS)
    slope = inverse * inverse * inverse * (total[1:2] / features)
    inverse = jnp.broadcast_to(inverse, (DH, GROUP)).T
    slope = jnp.broadcast_to(slope, (DH, GROUP)).T
    for c in range(chunks):
        for j in range(per):
            h = c * per + j
            scaled = head(n, h).astype(F32) * head(g, h).astype(F32)
            x = (inverse * scaled - head(attn[c], j) * slope).astype(BF16)
            d[:, h * DH:(h + 1) * DH] = x
            outs[c][j] = dot(head(q, h), x, 0, 0)


def grads_body(per, aliased, place, *refs):
    (q_k, q_o, k_k, k_o, v_k, v_o, s_k, s_o, d_k, d_o, sb_k, sb_o) = refs[:12]
    qg_k, qg_o, kg_k, kg_o, vg_k, vg_o = refs[12:]
    mask = causal()
    for j in range(per):
        at = slice(j * DH, (j + 1) * DH)
        for q, k, v, s, d, sb, qg, kg, vg in (
            (q_k, k_k, v_k, s_k, d_k, sb_k, qg_k, kg_k, vg_k),
            (q_o, k_o, v_o, s_o, d_o, sb_o, qg_o, kg_o, vg_o),
        ):
            do = head(d, j)
            ds = masked(dot(do, head(v, j), 1, 1), mask)
            qg[:, at] = (dot(ds, head(k, j), 1, 0) + dot(do, sb[j], 1, 1)).astype(BF16)
            kg[:, at] = dot(ds, head(q, j), 0, 0)
            vg[:, at] = dot(s[j], do, 0, 0)


def solution(mesh):
    count = mesh.shape["seq"]
    parts = mesh.shape["head"]
    long = count // 2
    swap = [(i, i ^ 1) for i in range(count)]

    def hop(array, near, far, reverse):
        pairs = []
        for z in range(long):
            to = z + far
            if to < long and near(z):
                for y in range(2):
                    pairs.append((2 * z + y, 2 * to + y))
        if reverse:
            pairs = [(count - 1 - a, count - 1 - b) for a, b in pairs]
        return lax.ppermute(array, "seq", pairs)

    def along(part, reverse):
        if long <= 4:
            carry, send = None, part
            for z in range(long - 1):
                got = hop(send, lambda at: at == z, 1, reverse)
                carry = got if carry is None else carry + got
                send = carry + part
            return jnp.zeros_like(part) if carry is None else carry
        carry = hop(part, lambda at: True, 1, reverse)
        far = 1
        while far < long:
            carry = carry + hop(carry, lambda at: True, far, reverse)
            far *= 2
        return carry

    def scan(kept, sent, leads, reverse):
        out = []
        for a, b in zip(kept, sent):
            r = lax.ppermute(b, "seq", swap)
            e = along(a + r, reverse)
            other = lax.ppermute(jnp.where(leads, e + a, e), "seq", swap)
            out.append((e, r, other))
        return out

    def shards(queries, keys, values, out_grad, norm_gain):
        tokens, width = queries.shape
        heads = width // DH
        half = heads // 2
        per = half // CHUNKS
        wide = half * DH
        narrow = per * DH
        y = lax.axis_index("seq") % 2
        place = y.astype(jnp.int32).reshape(1)
        turned = 1 - place
        gain = norm_gain.reshape(1, width)
        mac = 2 * GROUP * DH

        kept_half = lambda i, s: (0, s[0])
        sent_half = lambda i, s: (0, 1 - s[0])
        whole2 = lambda i, s: (0, 0)
        whole3 = lambda i, s: (0, 0, 0)

        def at_k(c):
            return lambda i, s: (0, s[0] * CHUNKS + c)

        def at_o(c):
            return lambda i, s: (0, (1 - s[0]) * CHUNKS + c)

        def at_k3(c):
            return lambda i, s: (s[0] * CHUNKS + c, 0, 0)

        def at_o3(c):
            return lambda i, s: ((1 - s[0]) * CHUNKS + c, 0, 0)

        def states(a, b, index):
            return call(
                functools.partial(states_body, per), place,
                [(a, (tokens, wide), index), (b, (tokens, wide), index)],
                [((per, DH, DH), F32, (per, DH, DH), whole3)] * CHUNKS,
                flops=half * mac * DH,
            )

        sent = states(keys, values, sent_half)
        kept = states(keys, values, kept_half)

        group = 4
        scores, attn_local = call(
            functools.partial(local_body, group), place,
            [(a, (tokens, group * DH), lambda i, s: (0, i)) for a in (queries, keys, values)],
            [
                ((heads, GROUP, GROUP), BF16, (group, GROUP, GROUP), lambda i, s: (i, 0, 0)),
                ((tokens, width), F32, (tokens, group * DH), lambda i, s: (0, i)),
            ],
            grid=(heads // group,), flops=2 * heads * mac * GROUP,
        )

        before = scan(kept, sent, y == 0, False)

        block = (tokens, narrow)
        square = cross = None
        attns, priors = [], []
        for c in range(CHUNKS):
            e, r, other = before[c]
            first, last = c == 0, c == CHUNKS - 1
            ins = []
            for a in (attn_local, queries, out_grad):
                ins += [(a, block, at_k(c)), (a, block, at_o(c))]
            ins += [(gain, (1, narrow), at_k(c)), (gain, (1, narrow), at_o(c))]
            ins += [(a, (per, DH, DH), whole3) for a in (e, r, other)]
            if not first:
                ins += [(a, (GROUP, DH), whole2) for a in (square, cross)]
            outs = [(block, F32, block, whole2)] * 2 + [((per, DH, DH), BF16, (per, DH, DH), whole3)] * 2
            if last:
                outs += [((2, GROUP), F32, (2, GROUP), whole2)]
            else:
                outs += [((GROUP, DH), F32, (GROUP, DH), whole2)] * 2
            a_k, a_o, s_k, s_o, *stats = call(
                functools.partial(attn_body, per, first, last), place, ins, outs, flops=2 * per * mac * DH)
            attns.append((a_k, a_o))
            priors.append((s_k, s_o))
            if last:
                mine = stats[0]
            else:
                square, cross = stats

        sums = [mine]
        for step in range(1, parts):
            sums.append(lax.ppermute(mine, "head", [(i, (i + step) % parts) for i in range(parts)]))

        def delta(which, index):
            ins = [(a, (2, GROUP), whole2) for a in sums]
            ins += [(attns[c][which], block, whole2) for c in range(CHUNKS)]
            ins += [(queries, (tokens, wide), index), (out_grad, (tokens, wide), index), (gain, (1, wide), index)]
            outs = [((tokens, wide), BF16, (tokens, wide), whole2)]
            outs += [((per, DH, DH), F32, (per, DH, DH), whole3)] * CHUNKS
            d, *g = call(
                functools.partial(delta_body, per, CHUNKS, parts, float(parts * width)), place, ins, outs,
                flops=half * mac * DH)
            return d, g

        d_o, sent = delta(1, sent_half)
        d_k, kept = delta(0, kept_half)
        after = scan(kept, sent, y == 1, True)

        grads = []
        for c in range(CHUNKS):
            ins = []
            for a in (queries, keys, values):
                ins += [(a, block, at_k(c)), (a, block, at_o(c))]
            ins += [(scores, (per, GROUP, GROUP), at_k3(c)), (scores, (per, GROUP, GROUP), at_o3(c))]
            here = lambda i, s, c=c: (0, c)
            ins += [(d_k, block, here), (d_o, block, here)]
            ins += [(a, (per, DH, DH), whole3) for a in priors[c]]
            outs = [(block, BF16, block, whole2)] * 2 + [(block, F32, block, whole2)] * 4
            grads.append(call(
                functools.partial(grads_body, per, c > 0), place, ins, outs,
                flops=2 * per * mac * (4 * GROUP + DH)))

        kg = vg = qg = None
        for c in range(CHUNKS):
            e, r, other = after[c]
            kg, vg, qg = finish(c, per, narrow, tokens, width, place, keys, values, grads[c], e, r, other, kg, vg, qg)
        return qg, kg, vg

    def finish(c, per, narrow, tokens, width, place, keys, values, grads, e, r, other, *done):
        qg_k, qg_o, kl_k, kl_o, vl_k, vl_o = grads
        block = (tokens, narrow)
        mine = lambda i, s: (0, jnp.where(i == 0, s[0], 1 - s[0]) * CHUNKS + c)
        whole2 = lambda i, s: (0, 0)
        whole3 = lambda i, s: (0, 0, 0)
        ins = [(a, block, whole2) for a in (qg_k, qg_o, kl_k, kl_o, vl_k, vl_o)]
        ins += [(a, block, mine) for a in (keys, values)]
        ins += [(a, (per, DH, DH), whole3) for a in (e, r, other)]
        aliases = {}
        if done[0] is not None:
            for n, a in enumerate(done):
                aliases[len(ins) + 1] = n
                ins.append((a, (8, 128), whole2))
        outs = [((tokens, width), BF16, block, mine)] * 3

        def body(place, qk, qo, kk, ko, vk, vo, k, v, e, r, other, *refs):
            kg, vg, qg = refs[-3:]
            mine = pl.program_id(0) == 0

            def one(q_in, k_in, v_in, state):
                qg[...] = q_in[...]
                for j in range(per):
                    at = slice(j * DH, (j + 1) * DH)
                    later = state(j).astype(BF16)
                    kg[:, at] = (k_in[:, at] + dot(v[:, at], later, 1, 1)).astype(BF16)
                    vg[:, at] = (v_in[:, at] + dot(k[:, at], later, 1, 0)).astype(BF16)

            @pl.when(mine)
            def _():
                one(qk, kk, vk, lambda j: jnp.where(place[0] == 0, e[j] + r[j], e[j]))

            @pl.when(jnp.logical_not(mine))
            def _():
                one(qo, ko, vo, lambda j: other[j])

        return call(body, place, ins, outs, grid=(2,), aliases=aliases, flops=4 * per * 2 * GROUP * DH * DH)

    return jax.shard_map(
        shards,
        mesh=mesh,
        in_specs=(
            P("seq", "head"),
            P("seq", "head"),
            P("seq", "head"),
            P("seq", "head"),
            P("head"),
        ),
        out_specs=(P("seq", "head"), P("seq", "head"), P("seq", "head")),
        check_vma=False,
    )
```

time: 322 us -> 112 us (0.35)
  waiting for transfers between devices: 242 us -> 19.7 us
  starting transfers between devices: 0.08 us -> 50.5 us
  matrix products: 19.8 us -> 0 us
  Pallas kernels: 0 us -> 19.5 us
  local copies, waits for them, and re-layouts: 22.8 us -> 7.79 us
  between operations: 14.3 us -> 1.71 us
  blocking collectives: 6.15 us -> 0 us
  other arithmetic: 16.8 us -> 12.3 us
    all_gather x2 -> x0, waiting for transfers between devices: 241 us -> none  [carried_in(): gathered = lax.all_gather(part, axis)]
    ppermute x0 -> x43, starting transfers between devices: none -> 50.5 us  [the longest x24 30.1 us: hop(): return lax.ppermute(array, 'seq', pairs)]
    dot_general x12 -> x0, matrix products: 19.8 us -> none  [the longest x1 3.57 us: shards(): jnp.einsum('hnck,hnce->hnke', masked, delta, preferred_element_type=f32)]
    ppermute x0 -> x43, waiting for transfers between devices: none -> 19.7 us  [the longest x8 8.36 us: scan(): r = lax.ppermute(b, 'seq', swap)]
    pallas_call x0 -> x17, Pallas kernels: none -> 19.5 us  [call(): pl.pallas_call(body, grid_spec=pltpu.PrefetchScalarGridSpec(num_scalar_pr...]
    unnamed x40 -> x110, local copies, waits for them, and re-layouts: 14.6 us -> 7.78 us
    psum x1 -> x0, blocking collectives: 6.15 us -> none  [shards(): square_sum, cross_sum = lax.psum((square_part, cross_part), 'head')]
    convert_element_type x3 -> x0, other arithmetic: 3.35 us -> none  [the longest x1 1.83 us: shards(): later_bf = later.astype(bf16)]
  transfers between devices with their start and end apart: 2 -> 43, of which waited for: 2 -> 13; matrix products, arithmetic and copies ran while one was open for 5% -> 11% of each run, Pallas kernels for 0% -> 14%
where the time goes in v1:
time: 112 us
  starting transfers between devices  50.5 us (45%)
  waiting for transfers between devices  19.7 us (18%)
  Pallas kernels  19.5 us (17%)
  other arithmetic  12.3 us (11%)
  local copies, waits for them, and re-layouts  7.79 us (7%)
  between operations  1.71 us (2%)
    ppermute x24, starting transfers between devices, hop(): return lax.ppermute(array, 'seq', pairs)  30.1 us
    pallas_call x17, Pallas kernels, call(): pl.pallas_call(body, grid_spec=pltpu.PrefetchScalarGridSpec(num_scalar_pr...  19.5 us
    add x16, other arithmetic, along(): send = carry + part  9.95 us
    ppermute x8, starting transfers between devices, scan(): other = lax.ppermute(jnp.where(leads, e + a, e), 'seq', swap)  9.41 us
    ppermute x8, starting transfers between devices, scan(): r = lax.ppermute(b, 'seq', swap)  9.19 us
    ppermute x8, waiting for transfers between devices, scan(): r = lax.ppermute(b, 'seq', swap)  8.36 us
    ppermute x24, waiting for transfers between devices, hop(): return lax.ppermute(array, 'seq', pairs)  7.84 us
    unnamed x110, local copies, waits for them, and re-layouts  7.78 us
  transfers between devices with their start and end apart: 43, of which 13 were waited for; matrix products, arithmetic and copies ran while one was open for 11% of the time, Pallas kernels for 14%

profile of v1, /device:TPU:0, one launch (start us, length us, event | category | flops | bytes accessed | tf_op | source)
XLA Modules:
  0.0 111.5 jit_solution(14177288936577118415)
XLA Ops:
  0.7 1.2 %copy-done.1 = bf16[256,2048]{1,0:T(8,128)(2,1)S(1)} copy-done((bf16[256,2048]{1,0:T(8,128)(2,1)S(1)}, bf16[256,2048]{1,0:T(8,128)(2,1)}, u32[]{:S(2)}) %copy-start.1) | copy-done | bytes 1048600
  1.9 1.2 %copy-done.3 = bf16[256,2048]{1,0:T(8,128)(2,1)S(1)} copy-done((bf16[256,2048]{1,0:T(8,128)(2,1)S(1)}, bf16[256,2048]{1,0:T(8,128)(2,1)}, u32[]{:S(2)}) %copy-start.3) | copy-done | bytes 1048600
  3.5 3.0 %collective-permute-start.15 = (f32[2,128,128]{2,1,0:T(8,128)S(1)}, f32[2,128,128]{2,1,0:T(8,128)S(1)}, u32[]{:S(2)}, u32[]{:S(2)}) collective-permute-start(f32[2,128,128]{2,1,0:T(8,128)S(1)} %get-tuple-element.91), channel_id=1, source_target_pairs={{0,4},{4,0},{8,12},{12,8},{16,20},{20,16},{24,28},{28,24},{1,5},{5... | collective-permute-start | bytes 393224 | tf_op jit(solution)/shard_map/ppermute | solution.py:169
  6.6 1.9 %collective-permute-start.5 = (f32[2,128,128]{2,1,0:T(8,128)S(1)}, f32[2,128,128]{2,1,0:T(8,128)S(1)}, u32[]{:S(2)}, u32[]{:S(2)}) collective-permute-start(f32[2,128,128]{2,1,0:T(8,128)S(1)} %get-tuple-element.87), channel_id=1, source_target_pairs={{0,4},{4,0},{8,12},{12,8},{16,20},{20,16},{24,28},{28,24},{1,5},{5... | collective-permute-start | bytes 393224 | tf_op jit(solution)/shard_map/ppermute | solution.py:169
  9.1 1.8 %collective-permute-done.15.r = f32[2,128,128]{2,1,0:T(8,128)S(1)} collective-permute-done((f32[2,128,128]{2,1,0:T(8,128)S(1)}, f32[2,128,128]{2,1,0:T(8,128)S(1)}, u32[]{:S(2)}, u32[]{:S(2)}) %collective-permute-start.15) | collective-permute-done | bytes 131104 | tf_op jit(solution)/shard_map/ppermute | solution.py:169
  10.9 4.0 %collective-permute-start.16 = (f32[2,128,128]{2,1,0:T(8,128)S(1)}, f32[2,128,128]{2,1,0:T(8,128)S(1)}, u32[]{:S(2)}, u32[]{:S(2)}) collective-permute-start(f32[2,128,128]{2,1,0:T(8,128)S(1)} %add.167), channel_id=1, source_target_pairs={{0,8},{4,12},{1,9},{5,13},{2,10},{6,14},{3,11},{7,15}} | collective-permute-start | bytes 393224 | tf_op jit(solution)/shard_map/ppermute | solution.py:149
  14.9 3.5 %collective-permute-done.10.r = f32[2,128,128]{2,1,0:T(8,128)S(1)} collective-permute-done((f32[2,128,128]{2,1,0:T(8,128)S(1)}, f32[2,128,128]{2,1,0:T(8,128)S(1)}, u32[]{:S(2)}, u32[]{:S(2)}) %collective-permute-start.10) | collective-permute-done | bytes 131104 | tf_op jit(solution)/shard_map/ppermute | solution.py:169
  18.5 3.7 %collective-permute-start.11 = (f32[2,128,128]{2,1,0:T(8,128)S(1)}, f32[2,128,128]{2,1,0:T(8,128)S(1)}, u32[]{:S(2)}, u32[]{:S(2)}) collective-permute-start(f32[2,128,128]{2,1,0:T(8,128)S(1)} %add.161), channel_id=1, source_target_pairs={{0,8},{4,12},{1,9},{5,13},{2,10},{6,14},{3,11},{7,15}} | collective-permute-start | bytes 393224 | tf_op jit(solution)/shard_map/ppermute | solution.py:149
  22.2 1.3 %collective-permute-start.6 = (f32[2,128,128]{2,1,0:T(8,128)S(1)}, f32[2,128,128]{2,1,0:T(8,128)S(1)}, u32[]{:S(2)}, u32[]{:S(2)}) collective-permute-start(f32[2,128,128]{2,1,0:T(8,128)S(1)} %add.155), channel_id=1, source_target_pairs={{0,8},{4,12},{1,9},{5,13},{2,10},{6,14},{3,11},{7,15}} | collective-permute-start | bytes 393224 | tf_op jit(solution)/shard_map/ppermute | solution.py:149
  23.6 1.3 %collective-permute-start.1 = (f32[2,128,128]{2,1,0:T(8,128)S(1)}, f32[2,128,128]{2,1,0:T(8,128)S(1)}, u32[]{:S(2)}, u32[]{:S(2)}) collective-permute-start(f32[2,128,128]{2,1,0:T(8,128)S(1)} %add.149), channel_id=1, source_target_pairs={{0,8},{4,12},{1,9},{5,13},{2,10},{6,14},{3,11},{7,15}} | collective-permute-start | bytes 393224 | tf_op jit(solution)/shard_map/ppermute | solution.py:149
  26.9 1.3 %collective-permute-done.6 = f32[2,128,128]{2,1,0:T(8,128)S(1)} collective-permute-done((f32[2,128,128]{2,1,0:T(8,128)S(1)}, f32[2,128,128]{2,1,0:T(8,128)S(1)}, u32[]{:S(2)}, u32[]{:S(2)}) %collective-permute-start.6) | collective-permute-done | bytes 131104 | tf_op jit(solution)/shard_map/ppermute | solution.py:149
  32.2 1.1 fusion.6
  33.9 1.0 fusion.7
  35.7 1.6 %collective-permute-start.19 = (f32[2,128,128]{2,1,0:T(8,128)S(1)}, f32[2,128,128]{2,1,0:T(8,128)S(1)}, u32[]{:S(2)}, u32[]{:S(2)}) collective-permute-start(f32[2,128,128]{2,1,0:T(8,128)S(1)} %get-tuple-element.177), channel_id=1, source_target_pairs={{0,4},{4,0},{8,12},{12,8},{16,20},{20,16},{24,28},{28,24},{1,5},{5... | collective-permute-start | bytes 393224 | tf_op jit(solution)/shard_map/ppermute | solution.py:171
  37.9 1.6 %collective-permute-start.9 = (f32[2,128,128]{2,1,0:T(8,128)S(1)}, f32[2,128,128]{2,1,0:T(8,128)S(1)}, u32[]{:S(2)}, u32[]{:S(2)}) collective-permute-start(f32[2,128,128]{2,1,0:T(8,128)S(1)} %get-tuple-element.185), channel_id=1, source_target_pairs={{0,4},{4,0},{8,12},{12,8},{16,20},{20,16},{24,28},{28,24},{1,5},{5... | collective-permute-start | bytes 393224 | tf_op jit(solution)/shard_map/ppermute | solution.py:171
  40.2 3.0 %shard_map.76 = (bf16[16,256,256]{2,1,0:T(8,128)(2,1)S(1)}, f32[256,2048]{1,0:T(8,128)S(1)}) custom-call(s32[1]{0:T(128)} %bitcast.place, bf16[256,2048]{1,0:T(8,128)(2,1)S(1)} %copy-done, bf16[256,2048]{1,0:T(8,128)(2,1)S(1)} %copy-done.2, bf16[256,2048]{1,0:T(8,128)(2,1)S(1)} %copy-done.4), custom_call_target="tpu_custom_call" | custom-call | flops 536870912 | bytes 1572864 | tf_op jit(solution)/shard_map/pallas_call | solution.py:38
  48.1 1.6 %collective-permute-start.21 = (f32[2,256]{1,0:T(2,128)S(1)}, f32[2,256]{1,0:T(2,128)S(1)}, u32[]{:S(2)}, u32[]{:S(2)}) collective-permute-start(f32[2,256]{1,0:T(2,128)S(1)} %get-tuple-element.98.refs_0_), channel_id=1, source_target_pairs={{0,2},{1,3},{2,0},{3,1},{4,6},{5,7},{6,4},{7,5},{8,10},{9,11},{10,... | collective-permute-start | bytes 6152 | tf_op jit(solution)/shard_map/ppermute | solution.py:258
  49.8 1.9 %collective-permute-done.21.refs_2_ = f32[2,256]{1,0:T(2,128)S(1)} collective-permute-done((f32[2,256]{1,0:T(2,128)S(1)}, f32[2,256]{1,0:T(2,128)S(1)}, u32[]{:S(2)}, u32[]{:S(2)}) %collective-permute-start.21) | collective-permute-done | bytes 2080 | tf_op jit(solution)/shard_map/ppermute | solution.py:258
  54.1 1.5 %collective-permute-start.23 = (f32[2,128,128]{2,1,0:T(8,128)S(1)}, f32[2,128,128]{2,1,0:T(8,128)S(1)}, u32[]{:S(2)}, u32[]{:S(2)}) collective-permute-start(f32[2,128,128]{2,1,0:T(8,128)S(1)} %get-tuple-element.118), channel_id=1, source_target_pairs={{0,4},{4,0},{8,12},{12,8},{16,20},{20,16},{24,28},{28,24},{1,5},{5... | collective-permute-start | bytes 393224 | tf_op jit(solution)/shard_map/ppermute | solution.py:169
  56.1 1.5 %collective-permute-start.33 = (f32[2,128,128]{2,1,0:T(8,128)S(1)}, f32[2,128,128]{2,1,0:T(8,128)S(1)}, u32[]{:S(2)}, u32[]{:S(2)}) collective-permute-start(f32[2,128,128]{2,1,0:T(8,128)S(1)} %get-tuple-element.138), channel_id=1, source_target_pairs={{0,4},{4,0},{8,12},{12,8},{16,20},{20,16},{24,28},{28,24},{1,5},{5... | collective-permute-start | bytes 393224 | tf_op jit(solution)/shard_map/ppermute | solution.py:169
  61.2 2.1 %collective-permute-done.28.r = f32[2,128,128]{2,1,0:T(8,128)S(1)} collective-permute-done((f32[2,128,128]{2,1,0:T(8,128)S(1)}, f32[2,128,128]{2,1,0:T(8,128)S(1)}, u32[]{:S(2)}, u32[]{:S(2)}) %collective-permute-start.28) | collective-permute-done | bytes 131104 | tf_op jit(solution)/shard_map/ppermute | solution.py:169
  64.0 1.3 %collective-permute-start.29 = (f32[2,128,128]{2,1,0:T(8,128)}, f32[2,128,128]{2,1,0:T(8,128)}, u32[]{:S(2)}, u32[]{:S(2)}) collective-permute-start(f32[2,128,128]{2,1,0:T(8,128)} %add.179), channel_id=1, source_target_pairs={{28,20},{24,16},{29,21},{25,17},{30,22},{26,18},{31,23},{27,19}} | collective-permute-start | bytes 393224 | tf_op jit(solution)/shard_map/ppermute | solution.py:149
  66.0 1.3 %collective-permute-start.34 = (f32[2,128,128]{2,1,0:T(8,128)}, f32[2,128,128]{2,1,0:T(8,128)}, u32[]{:S(2)}, u32[]{:S(2)}) collective-permute-start(f32[2,128,128]{2,1,0:T(8,128)} %add.185), channel_id=1, source_target_pairs={{28,20},{24,16},{29,21},{25,17},{30,22},{26,18},{31,23},{27,19}} | collective-permute-start | bytes 393224 | tf_op jit(solution)/shard_map/ppermute | solution.py:149
  68.6 1.3 %collective-permute-start.39 = (f32[2,128,128]{2,1,0:T(8,128)}, f32[2,128,128]{2,1,0:T(8,128)}, u32[]{:S(2)}, u32[]{:S(2)}) collective-permute-start(f32[2,128,128]{2,1,0:T(8,128)} %add.191), channel_id=1, source_target_pairs={{28,20},{24,16},{29,21},{25,17},{30,22},{26,18},{31,23},{27,19}} | collective-permute-start | bytes 393224 | tf_op jit(solution)/shard_map/ppermute | solution.py:149
  70.7 1.3 %collective-permute-start.25 = (f32[2,128,128]{2,1,0:T(8,128)}, f32[2,128,128]{2,1,0:T(8,128)}, u32[]{:S(2)}, u32[]{:S(2)}) collective-permute-start(f32[2,128,128]{2,1,0:T(8,128)} %add.174), channel_id=1, source_target_pairs={{20,12},{16,8},{21,13},{17,9},{22,14},{18,10},{23,15},{19,11}} | collective-permute-start | bytes 393224 | tf_op jit(solution)/shard_map/ppermute | solution.py:149
  72.0 1.0 add.180
  73.9 1.0 add.186
  75.7 1.0 add.192
  77.3 1.1 fusion.3
  78.4 1.4 %collective-permute-start.26 = (f32[2,128,128]{2,1,0:T(8,128)S(1)}, f32[2,128,128]{2,1,0:T(8,128)S(1)}, u32[]{:S(2)}, u32[]{:S(2)}) collective-permute-start(f32[2,128,128]{2,1,0:T(8,128)S(1)} %get-tuple-element.175), channel_id=1, source_target_pairs={{12,4},{8,0},{13,5},{9,1},{14,6},{10,2},{15,7},{11,3}} | collective-permute-start | bytes 393224 | tf_op jit(solution)/shard_map/ppermute | solution.py:149
  79.9 1.0 fusion.2
  80.9 1.6 %collective-permute-start.31 = (f32[2,128,128]{2,1,0:T(8,128)S(1)}, f32[2,128,128]{2,1,0:T(8,128)S(1)}, u32[]{:S(2)}, u32[]{:S(2)}) collective-permute-start(f32[2,128,128]{2,1,0:T(8,128)S(1)} %get-tuple-element.171), channel_id=1, source_target_pairs={{12,4},{8,0},{13,5},{9,1},{14,6},{10,2},{15,7},{11,3}} | collective-permute-start | bytes 393224 | tf_op jit(solution)/shard_map/ppermute | solution.py:149
  82.5 1.0 fusion.1
  83.5 1.3 %collective-permute-start.36 = (f32[2,128,128]{2,1,0:T(8,128)S(1)}, f32[2,128,128]{2,1,0:T(8,128)S(1)}, u32[]{:S(2)}, u32[]{:S(2)}) collective-permute-start(f32[2,128,128]{2,1,0:T(8,128)S(1)} %get-tuple-element.167), channel_id=1, source_target_pairs={{12,4},{8,0},{13,5},{9,1},{14,6},{10,2},{15,7},{11,3}} | collective-permute-start | bytes 393224 | tf_op jit(solution)/shard_map/ppermute | solution.py:149
  84.8 1.0 fusion
  85.8 1.5 %collective-permute-start.41 = (f32[2,128,128]{2,1,0:T(8,128)S(1)}, f32[2,128,128]{2,1,0:T(8,128)S(1)}, u32[]{:S(2)}, u32[]{:S(2)}) collective-permute-start(f32[2,128,128]{2,1,0:T(8,128)S(1)} %get-tuple-element.163), channel_id=1, source_target_pairs={{12,4},{8,0},{13,5},{9,1},{14,6},{10,2},{15,7},{11,3}} | collective-permute-start | bytes 393224 | tf_op jit(solution)/shard_map/ppermute | solution.py:149
  87.3 5.2 %collective-permute-done.31 = f32[2,128,128]{2,1,0:T(8,128)S(1)} collective-permute-done((f32[2,128,128]{2,1,0:T(8,128)S(1)}, f32[2,128,128]{2,1,0:T(8,128)S(1)}, u32[]{:S(2)}, u32[]{:S(2)}) %collective-permute-start.31) | collective-permute-done | bytes 131104 | tf_op jit(solution)/shard_map/ppermute | solution.py:149
  92.5 1.6 %collective-permute-start.32 = (f32[2,128,128]{2,1,0:T(8,128)S(1)}, f32[2,128,128]{2,1,0:T(8,128)S(1)}, u32[]{:S(2)}, u32[]{:S(2)}) collective-permute-start(f32[2,128,128]{2,1,0:T(8,128)S(1)} %get-tuple-element.169), channel_id=1, source_target_pairs={{0,4},{4,0},{8,12},{12,8},{16,20},{20,16},{24,28},{28,24},{1,5},{5... | collective-permute-start | bytes 393224 | tf_op jit(solution)/shard_map/ppermute | solution.py:171
  94.1 1.4 %collective-permute-start.37 = (f32[2,128,128]{2,1,0:T(8,128)S(1)}, f32[2,128,128]{2,1,0:T(8,128)S(1)}, u32[]{:S(2)}, u32[]{:S(2)}) collective-permute-start(f32[2,128,128]{2,1,0:T(8,128)S(1)} %get-tuple-element.165), channel_id=1, source_target_pairs={{0,4},{4,0},{8,12},{12,8},{16,20},{20,16},{24,28},{28,24},{1,5},{5... | collective-permute-start | bytes 393224 | tf_op jit(solution)/shard_map/ppermute | solution.py:171
  95.8 1.6 %collective-permute-start.42 = (f32[2,128,128]{2,1,0:T(8,128)S(1)}, f32[2,128,128]{2,1,0:T(8,128)S(1)}, u32[]{:S(2)}, u32[]{:S(2)}) collective-permute-start(f32[2,128,128]{2,1,0:T(8,128)S(1)} %get-tuple-element.161), channel_id=1, source_target_pairs={{0,4},{4,0},{8,12},{12,8},{16,20},{20,16},{24,28},{28,24},{1,5},{5... | collective-permute-start | bytes 393224 | tf_op jit(solution)/shard_map/ppermute | solution.py:171
  98.0 1.4 %shard_map.88 = (bf16[256,256]{1,0:T(8,128)(2,1)S(1)}, bf16[256,256]{1,0:T(8,128)(2,1)S(1)}, f32[256,256]{1,0:T(8,128)S(1)}, f32[256,256]{1,0:T(8,128)S(1)}, f32...) custom-call(s32[1]{0:T(128)} %bitcast.place, bf16[256,2048]{1,0:T(8,128)(2,1)S(1)} %copy-done, bf16[256,2048]{1,0:T(8,128)(2,1)S(1)} %copy-done, ...), custom_call_target="tpu_custom_call" | custom-call | flops 301989888 | bytes 5832704 | tf_op jit(solution)/shard_map/pallas_call | solution.py:38
  99.5 1.4 %shard_map.87 = (bf16[256,256]{1,0:T(8,128)(2,1)S(1)}, bf16[256,256]{1,0:T(8,128)(2,1)S(1)}, f32[256,256]{1,0:T(8,128)S(1)}, f32[256,256]{1,0:T(8,128)S(1)}, f32...) custom-call(s32[1]{0:T(128)} %bitcast.place, bf16[256,2048]{1,0:T(8,128)(2,1)S(1)} %copy-done, bf16[256,2048]{1,0:T(8,128)(2,1)S(1)} %copy-done, ...), custom_call_target="tpu_custom_call" | custom-call | flops 301989888 | bytes 5832704 | tf_op jit(solution)/shard_map/pallas_call | solution.py:38
  100.9 1.4 %shard_map.86 = (bf16[256,256]{1,0:T(8,128)(2,1)S(1)}, bf16[256,256]{1,0:T(8,128)(2,1)S(1)}, f32[256,256]{1,0:T(8,128)S(1)}, f32[256,256]{1,0:T(8,128)S(1)}, f32...) custom-call(s32[1]{0:T(128)} %bitcast.place, bf16[256,2048]{1,0:T(8,128)(2,1)S(1)} %copy-done, bf16[256,2048]{1,0:T(8,128)(2,1)S(1)} %copy-done, ...), custom_call_target="tpu_custom_call" | custom-call | flops 301989888 | bytes 5832704 | tf_op jit(solution)/shard_map/pallas_call | solution.py:38
  102.3 1.4 %shard_map.85 = (bf16[256,256]{1,0:T(8,128)(2,1)S(1)}, bf16[256,256]{1,0:T(8,128)(2,1)S(1)}, f32[256,256]{1,0:T(8,128)S(1)}, f32[256,256]{1,0:T(8,128)S(1)}, f32...) custom-call(s32[1]{0:T(128)} %bitcast.place, bf16[256,2048]{1,0:T(8,128)(2,1)S(1)} %copy-done, bf16[256,2048]{1,0:T(8,128)(2,1)S(1)} %copy-done, ...), custom_call_target="tpu_custom_call" | custom-call | flops 301989888 | bytes 5832704 | tf_op jit(solution)/shard_map/pallas_call | solution.py:38
  103.7 1.4 %shard_map.89 = (bf16[256,2048]{1,0:T(8,128)(2,1)}, bf16[256,2048]{1,0:T(8,128)(2,1)}, bf16[256,2048]{1,0:T(8,128)(2,1)}) custom-call(s32[1]{0:T(128)} %bitcast.place, bf16[256,256]{1,0:T(8,128)(2,1)S(1)} %get-tuple-element.141.qk, bf16[256,256]{1,0:T(8,128)(2,1)S(1)} %get-tuple-element.142.qo, f32[256,256]{1,0:T(8,128)S(1)} %get-tuple-element.143.kk, ...), custom_call_target="tpu_custom_call" | custom-call | flops 67108864 | bytes 1900544 | tf_op jit(solution)/shard_map/pallas_call | solution.py:38
  105.2 2.1 %shard_map.90 = (bf16[256,2048]{1,0:T(8,128)(2,1)}, bf16[256,2048]{1,0:T(8,128)(2,1)}, bf16[256,2048]{1,0:T(8,128)(2,1)}) custom-call(s32[1]{0:T(128)} %bitcast.place, bf16[256,256]{1,0:T(8,128)(2,1)S(1)} %get-tuple-element.131.qk, bf16[256,256]{1,0:T(8,128)(2,1)S(1)} %get-tuple-element.132.qo, ...), custom_call_target="tpu_custom_call", output_to_operand_aliasing={{0}: (12, {}), {1}: (13, {}), {2}: (14, {})} | custom-call | flops 67108864 | bytes 3473408 | tf_op jit(solution)/shard_map/pallas_call | solution.py:38
  107.3 2.1 %shard_map.91 = (bf16[256,2048]{1,0:T(8,128)(2,1)}, bf16[256,2048]{1,0:T(8,128)(2,1)}, bf16[256,2048]{1,0:T(8,128)(2,1)}) custom-call(s32[1]{0:T(128)} %bitcast.place, bf16[256,256]{1,0:T(8,128)(2,1)S(1)} %get-tuple-element.121.qk, bf16[256,256]{1,0:T(8,128)(2,1)S(1)} %get-tuple-element.122.qo, ...), custom_call_target="tpu_custom_call", output_to_operand_aliasing={{0}: (12, {}), {1}: (13, {}), {2}: (14, {})} | custom-call | flops 67108864 | bytes 3473408 | tf_op jit(solution)/shard_map/pallas_call | solution.py:38
  109.4 2.1 %shard_map.92 = (bf16[256,2048]{1,0:T(8,128)(2,1)}, bf16[256,2048]{1,0:T(8,128)(2,1)}, bf16[256,2048]{1,0:T(8,128)(2,1)}) custom-call(s32[1]{0:T(128)} %bitcast.place, bf16[256,256]{1,0:T(8,128)(2,1)S(1)} %get-tuple-element.111.qk, bf16[256,256]{1,0:T(8,128)(2,1)S(1)} %get-tuple-element.112.qo, ...), custom_call_target="tpu_custom_call", output_to_operand_aliasing={{0}: (12, {}), {1}: (13, {}), {2}: (14, {})} | custom-call | flops 67108864 | bytes 3473408 | tf_op jit(solution)/shard_map/pallas_call | solution.py:38
  (198 shorter events, 27.4 us)
Async XLA Ops:
  3.5 7.4 %collective-permute-start.15 = (f32[2,128,128]{2,1,0:T(8,128)S(1)}, f32[2,128,128]{2,1,0:T(8,128)S(1)}, u32[]{:S(2)}, u32[]{:S(2)}) collective-permute-start(f32[2,128,128]{2,1,0:T(8,128)S(1)} %get-tuple-element.91), channel_id=1, source_target_pairs={{0,4},{4,0},{8,12},{12,8},{16,20},{20,16},{24,28},{28,24},{1,5},{5... | collective-permute-start | bytes 393224 | tf_op jit(solution)/shard_map/ppermute | solution.py:169
  6.5 17.0 %collective-permute-start = (f32[2,128,128]{2,1,0:T(8,128)S(1)}, f32[2,128,128]{2,1,0:T(8,128)S(1)}, u32[]{:S(2)}, u32[]{:S(2)}) collective-permute-start(f32[2,128,128]{2,1,0:T(8,128)S(1)} %get-tuple-element.85), channel_id=1, source_target_pairs={{0,4},{4,0},{8,12},{12,8},{16,20},{20,16},{24,28},{28,24},{1,5},{5... | collective-permute-start | bytes 393224 | tf_op jit(solution)/shard_map/ppermute | solution.py:169
  6.6 15.6 %collective-permute-start.5 = (f32[2,128,128]{2,1,0:T(8,128)S(1)}, f32[2,128,128]{2,1,0:T(8,128)S(1)}, u32[]{:S(2)}, u32[]{:S(2)}) collective-permute-start(f32[2,128,128]{2,1,0:T(8,128)S(1)} %get-tuple-element.87), channel_id=1, source_target_pairs={{0,4},{4,0},{8,12},{12,8},{16,20},{20,16},{24,28},{28,24},{1,5},{5... | collective-permute-start | bytes 393224 | tf_op jit(solution)/shard_map/ppermute | solution.py:169
  8.5 9.9 %collective-permute-start.10 = (f32[2,128,128]{2,1,0:T(8,128)S(1)}, f32[2,128,128]{2,1,0:T(8,128)S(1)}, u32[]{:S(2)}, u32[]{:S(2)}) collective-permute-start(f32[2,128,128]{2,1,0:T(8,128)S(1)} %get-tuple-element.89), channel_id=1, source_target_pairs={{0,4},{4,0},{8,12},{12,8},{16,20},{20,16},{24,28},{28,24},{1,5},{5... | collective-permute-start | bytes 393224 | tf_op jit(solution)/shard_map/ppermute | solution.py:169
  10.9 14.1 %collective-permute-start.16 = (f32[2,128,128]{2,1,0:T(8,128)S(1)}, f32[2,128,128]{2,1,0:T(8,128)S(1)}, u32[]{:S(2)}, u32[]{:S(2)}) collective-permute-start(f32[2,128,128]{2,1,0:T(8,128)S(1)} %add.167), channel_id=1, source_target_pairs={{0,8},{4,12},{1,9},{5,13},{2,10},{6,14},{3,11},{7,15}} | collective-permute-start | bytes 393224 | tf_op jit(solution)/shard_map/ppermute | solution.py:149
  18.5 7.6 %collective-permute-start.11 = (f32[2,128,128]{2,1,0:T(8,128)S(1)}, f32[2,128,128]{2,1,0:T(8,128)S(1)}, u32[]{:S(2)}, u32[]{:S(2)}) collective-permute-start(f32[2,128,128]{2,1,0:T(8,128)S(1)} %add.161), channel_id=1, source_target_pairs={{0,8},{4,12},{1,9},{5,13},{2,10},{6,14},{3,11},{7,15}} | collective-permute-start | bytes 393224 | tf_op jit(solution)/shard_map/ppermute | solution.py:149
  22.2 6.0 %collective-permute-start.6 = (f32[2,128,128]{2,1,0:T(8,128)S(1)}, f32[2,128,128]{2,1,0:T(8,128)S(1)}, u32[]{:S(2)}, u32[]{:S(2)}) collective-permute-start(f32[2,128,128]{2,1,0:T(8,128)S(1)} %add.155), channel_id=1, source_target_pairs={{0,8},{4,12},{1,9},{5,13},{2,10},{6,14},{3,11},{7,15}} | collective-permute-start | bytes 393224 | tf_op jit(solution)/shard_map/ppermute | solution.py:149
  23.6 6.0 %collective-permute-start.1 = (f32[2,128,128]{2,1,0:T(8,128)S(1)}, f32[2,128,128]{2,1,0:T(8,128)S(1)}, u32[]{:S(2)}, u32[]{:S(2)}) collective-permute-start(f32[2,128,128]{2,1,0:T(8,128)S(1)} %add.149), channel_id=1, source_target_pairs={{0,8},{4,12},{1,9},{5,13},{2,10},{6,14},{3,11},{7,15}} | collective-permute-start | bytes 393224 | tf_op jit(solution)/shard_map/ppermute | solution.py:149
  25.0 5.4 %collective-permute-start.17 = (f32[2,128,128]{2,1,0:T(8,128)S(1)}, f32[2,128,128]{2,1,0:T(8,128)S(1)}, u32[]{:S(2)}, u32[]{:S(2)}) collective-permute-start(f32[2,128,128]{2,1,0:T(8,128)S(1)} %add.168), channel_id=1, source_target_pairs={{8,16},{12,20},{9,17},{13,21},{10,18},{14,22},{11,19},{15,23}} | collective-permute-start | bytes 393224 | tf_op jit(solution)/shard_map/ppermute | solution.py:149
  26.1 5.1 %collective-permute-start.12 = (f32[2,128,128]{2,1,0:T(8,128)S(1)}, f32[2,128,128]{2,1,0:T(8,128)S(1)}, u32[]{:S(2)}, u32[]{:S(2)}) collective-permute-start(f32[2,128,128]{2,1,0:T(8,128)S(1)} %add.162), channel_id=1, source_target_pairs={{8,16},{12,20},{9,17},{13,21},{10,18},{14,22},{11,19},{15,23}} | collective-permute-start | bytes 393224 | tf_op jit(solution)/shard_map/ppermute | solution.py:149
  28.3 3.9 %collective-permute-start.7 = (f32[2,128,128]{2,1,0:T(8,128)S(1)}, f32[2,128,128]{2,1,0:T(8,128)S(1)}, u32[]{:S(2)}, u32[]{:S(2)}) collective-permute-start(f32[2,128,128]{2,1,0:T(8,128)S(1)} %add.156), channel_id=1, source_target_pairs={{8,16},{12,20},{9,17},{13,21},{10,18},{14,22},{11,19},{15,23}} | collective-permute-start | bytes 393224 | tf_op jit(solution)/shard_map/ppermute | solution.py:149
  29.7 4.3 %collective-permute-start.2 = (f32[2,128,128]{2,1,0:T(8,128)S(1)}, f32[2,128,128]{2,1,0:T(8,128)S(1)}, u32[]{:S(2)}, u32[]{:S(2)}) collective-permute-start(f32[2,128,128]{2,1,0:T(8,128)S(1)} %add.150), channel_id=1, source_target_pairs={{8,16},{12,20},{9,17},{13,21},{10,18},{14,22},{11,19},{15,23}} | collective-permute-start | bytes 393224 | tf_op jit(solution)/shard_map/ppermute | solution.py:149
  30.4 5.2 %collective-permute-start.18 = (f32[2,128,128]{2,1,0:T(8,128)S(1)}, f32[2,128,128]{2,1,0:T(8,128)S(1)}, u32[]{:S(2)}, u32[]{:S(2)}) collective-permute-start(f32[2,128,128]{2,1,0:T(8,128)S(1)} %get-tuple-element.179), channel_id=1, source_target_pairs={{16,24},{20,28},{17,25},{21,29},{18,26},{22,30},{19,27},{23,31}} | collective-permute-start | bytes 393224 | tf_op jit(solution)/shard_map/ppermute | solution.py:149
  31.3 5.9 %collective-permute-start.13 = (f32[2,128,128]{2,1,0:T(8,128)S(1)}, f32[2,128,128]{2,1,0:T(8,128)S(1)}, u32[]{:S(2)}, u32[]{:S(2)}) collective-permute-start(f32[2,128,128]{2,1,0:T(8,128)S(1)} %get-tuple-element.183), channel_id=1, source_target_pairs={{16,24},{20,28},{17,25},{21,29},{18,26},{22,30},{19,27},{23,31}} | collective-permute-start | bytes 393224 | tf_op jit(solution)/shard_map/ppermute | solution.py:149
  33.3 4.6 %collective-permute-start.8 = (f32[2,128,128]{2,1,0:T(8,128)S(1)}, f32[2,128,128]{2,1,0:T(8,128)S(1)}, u32[]{:S(2)}, u32[]{:S(2)}) collective-permute-start(f32[2,128,128]{2,1,0:T(8,128)S(1)} %get-tuple-element.187), channel_id=1, source_target_pairs={{16,24},{20,28},{17,25},{21,29},{18,26},{22,30},{19,27},{23,31}} | collective-permute-start | bytes 393224 | tf_op jit(solution)/shard_map/ppermute | solution.py:149
  34.9 4.6 %collective-permute-start.3 = (f32[2,128,128]{2,1,0:T(8,128)S(1)}, f32[2,128,128]{2,1,0:T(8,128)S(1)}, u32[]{:S(2)}, u32[]{:S(2)}) collective-permute-start(f32[2,128,128]{2,1,0:T(8,128)S(1)} %get-tuple-element.191), channel_id=1, source_target_pairs={{16,24},{20,28},{17,25},{21,29},{18,26},{22,30},{19,27},{23,31}} | collective-permute-start | bytes 393224 | tf_op jit(solution)/shard_map/ppermute | solution.py:149
  35.7 7.5 %collective-permute-start.19 = (f32[2,128,128]{2,1,0:T(8,128)S(1)}, f32[2,128,128]{2,1,0:T(8,128)S(1)}, u32[]{:S(2)}, u32[]{:S(2)}) collective-permute-start(f32[2,128,128]{2,1,0:T(8,128)S(1)} %get-tuple-element.177), channel_id=1, source_target_pairs={{0,4},{4,0},{8,12},{12,8},{16,20},{20,16},{24,28},{28,24},{1,5},{5... | collective-permute-start | bytes 393224 | tf_op jit(solution)/shard_map/ppermute | solution.py:171
  37.3 7.5 %collective-permute-start.14 = (f32[2,128,128]{2,1,0:T(8,128)S(1)}, f32[2,128,128]{2,1,0:T(8,128)S(1)}, u32[]{:S(2)}, u32[]{:S(2)}) collective-permute-start(f32[2,128,128]{2,1,0:T(8,128)S(1)} %get-tuple-element.181), channel_id=1, source_target_pairs={{0,4},{4,0},{8,12},{12,8},{16,20},{20,16},{24,28},{28,24},{1,5},{5... | collective-permute-start | bytes 393224 | tf_op jit(solution)/shard_map/ppermute | solution.py:171
  37.9 8.5 %collective-permute-start.9 = (f32[2,128,128]{2,1,0:T(8,128)S(1)}, f32[2,128,128]{2,1,0:T(8,128)S(1)}, u32[]{:S(2)}, u32[]{:S(2)}) collective-permute-start(f32[2,128,128]{2,1,0:T(8,128)S(1)} %get-tuple-element.185), channel_id=1, source_target_pairs={{0,4},{4,0},{8,12},{12,8},{16,20},{20,16},{24,28},{28,24},{1,5},{5... | collective-permute-start | bytes 393224 | tf_op jit(solution)/shard_map/ppermute | solution.py:171
  39.5 8.1 %collective-permute-start.4 = (f32[2,128,128]{2,1,0:T(8,128)S(1)}, f32[2,128,128]{2,1,0:T(8,128)S(1)}, u32[]{:S(2)}, u32[]{:S(2)}) collective-permute-start(f32[2,128,128]{2,1,0:T(8,128)S(1)} %get-tuple-element.189), channel_id=1, source_target_pairs={{0,4},{4,0},{8,12},{12,8},{16,20},{20,16},{24,28},{28,24},{1,5},{5... | collective-permute-start | bytes 393224 | tf_op jit(solution)/shard_map/ppermute | solution.py:171
  48.0 1.8 %collective-permute-start.22 = (f32[2,256]{1,0:T(2,128)S(1)}, f32[2,256]{1,0:T(2,128)S(1)}, u32[]{:S(2)}, u32[]{:S(2)}) collective-permute-start(f32[2,256]{1,0:T(2,128)S(1)} %get-tuple-element.98.refs_0_), channel_id=1, source_target_pairs={{0,3},{1,0},{2,1},{3,2},{4,7},{5,4},{6,5},{7,6},{8,11},{9,8},{10,9... | collective-permute-start | bytes 6152 | tf_op jit(solution)/shard_map/ppermute | solution.py:258
  48.1 3.7 %collective-permute-start.21 = (f32[2,256]{1,0:T(2,128)S(1)}, f32[2,256]{1,0:T(2,128)S(1)}, u32[]{:S(2)}, u32[]{:S(2)}) collective-permute-start(f32[2,256]{1,0:T(2,128)S(1)} %get-tuple-element.98.refs_0_), channel_id=1, source_target_pairs={{0,2},{1,3},{2,0},{3,1},{4,6},{5,7},{6,4},{7,5},{8,10},{9,11},{10,... | collective-permute-start | bytes 6152 | tf_op jit(solution)/shard_map/ppermute | solution.py:258
  49.7 3.0 %collective-permute-start.20 = (f32[2,256]{1,0:T(2,128)S(1)}, f32[2,256]{1,0:T(2,128)S(1)}, u32[]{:S(2)}, u32[]{:S(2)}) collective-permute-start(f32[2,256]{1,0:T(2,128)S(1)} %get-tuple-element.98.refs_0_), channel_id=1, source_target_pairs={{0,1},{1,2},{2,3},{3,0},{4,5},{5,6},{6,7},{7,4},{8,9},{9,10},{10,1... | collective-permute-start | bytes 6152 | tf_op jit(solution)/shard_map/ppermute | solution.py:258
  54.1 6.4 %collective-permute-start.23 = (f32[2,128,128]{2,1,0:T(8,128)S(1)}, f32[2,128,128]{2,1,0:T(8,128)S(1)}, u32[]{:S(2)}, u32[]{:S(2)}) collective-permute-start(f32[2,128,128]{2,1,0:T(8,128)S(1)} %get-tuple-element.118), channel_id=1, source_target_pairs={{0,4},{4,0},{8,12},{12,8},{16,20},{20,16},{24,28},{28,24},{1,5},{5... | collective-permute-start | bytes 393224 | tf_op jit(solution)/shard_map/ppermute | solution.py:169
  55.6 7.7 %collective-permute-start.28 = (f32[2,128,128]{2,1,0:T(8,128)S(1)}, f32[2,128,128]{2,1,0:T(8,128)S(1)}, u32[]{:S(2)}, u32[]{:S(2)}) collective-permute-start(f32[2,128,128]{2,1,0:T(8,128)S(1)} %get-tuple-element.128), channel_id=1, source_target_pairs={{0,4},{4,0},{8,12},{12,8},{16,20},{20,16},{24,28},{28,24},{1,5},{5... | collective-permute-start | bytes 393224 | tf_op jit(solution)/shard_map/ppermute | solution.py:169
  56.1 9.2 %collective-permute-start.33 = (f32[2,128,128]{2,1,0:T(8,128)S(1)}, f32[2,128,128]{2,1,0:T(8,128)S(1)}, u32[]{:S(2)}, u32[]{:S(2)}) collective-permute-start(f32[2,128,128]{2,1,0:T(8,128)S(1)} %get-tuple-element.138), channel_id=1, source_target_pairs={{0,4},{4,0},{8,12},{12,8},{16,20},{20,16},{24,28},{28,24},{1,5},{5... | collective-permute-start | bytes 393224 | tf_op jit(solution)/shard_map/ppermute | solution.py:169
  57.6 9.7 %collective-permute-start.38 = (f32[2,128,128]{2,1,0:T(8,128)S(1)}, f32[2,128,128]{2,1,0:T(8,128)S(1)}, u32[]{:S(2)}, u32[]{:S(2)}) collective-permute-start(f32[2,128,128]{2,1,0:T(8,128)S(1)} %get-tuple-element.148), channel_id=1, source_target_pairs={{0,4},{4,0},{8,12},{12,8},{16,20},{20,16},{24,28},{28,24},{1,5},{5... | collective-permute-start | bytes 393224 | tf_op jit(solution)/shard_map/ppermute | solution.py:169
  60.6 9.4 %collective-permute-start.24 = (f32[2,128,128]{2,1,0:T(8,128)S(1)}, f32[2,128,128]{2,1,0:T(8,128)S(1)}, u32[]{:S(2)}, u32[]{:S(2)}) collective-permute-start(f32[2,128,128]{2,1,0:T(8,128)S(1)} %add.173), channel_id=1, source_target_pairs={{28,20},{24,16},{29,21},{25,17},{30,22},{26,18},{31,23},{27,19}} | collective-permute-start | bytes 393224 | tf_op jit(solution)/shard_map/ppermute | solution.py:149
  64.0 8.0 %collective-permute-start.29 = (f32[2,128,128]{2,1,0:T(8,128)}, f32[2,128,128]{2,1,0:T(8,128)}, u32[]{:S(2)}, u32[]{:S(2)}) collective-permute-start(f32[2,128,128]{2,1,0:T(8,128)} %add.179), channel_id=1, source_target_pairs={{28,20},{24,16},{29,21},{25,17},{30,22},{26,18},{31,23},{27,19}} | collective-permute-start | bytes 393224 | tf_op jit(solution)/shard_map/ppermute | solution.py:149
  66.0 7.9 %collective-permute-start.34 = (f32[2,128,128]{2,1,0:T(8,128)}, f32[2,128,128]{2,1,0:T(8,128)}, u32[]{:S(2)}, u32[]{:S(2)}) collective-permute-start(f32[2,128,128]{2,1,0:T(8,128)} %add.185), channel_id=1, source_target_pairs={{28,20},{24,16},{29,21},{25,17},{30,22},{26,18},{31,23},{27,19}} | collective-permute-start | bytes 393224 | tf_op jit(solution)/shard_map/ppermute | solution.py:149
  68.6 7.0 %collective-permute-start.39 = (f32[2,128,128]{2,1,0:T(8,128)}, f32[2,128,128]{2,1,0:T(8,128)}, u32[]{:S(2)}, u32[]{:S(2)}) collective-permute-start(f32[2,128,128]{2,1,0:T(8,128)} %add.191), channel_id=1, source_target_pairs={{28,20},{24,16},{29,21},{25,17},{30,22},{26,18},{31,23},{27,19}} | collective-permute-start | bytes 393224 | tf_op jit(solution)/shard_map/ppermute | solution.py:149
  70.7 6.7 %collective-permute-start.25 = (f32[2,128,128]{2,1,0:T(8,128)}, f32[2,128,128]{2,1,0:T(8,128)}, u32[]{:S(2)}, u32[]{:S(2)}) collective-permute-start(f32[2,128,128]{2,1,0:T(8,128)} %add.174), channel_id=1, source_target_pairs={{20,12},{16,8},{21,13},{17,9},{22,14},{18,10},{23,15},{19,11}} | collective-permute-start | bytes 393224 | tf_op jit(solution)/shard_map/ppermute | solution.py:149
  72.0 20.5 %copy-start.29 = (f32[2,128,128]{2,1,0:T(8,128)S(1)}, f32[2,128,128]{2,1,0:T(8,128)}, u32[]{:S(2)}) copy-start(f32[2,128,128]{2,1,0:T(8,128)} %copy-done.28) | copy-start | bytes 393220
  73.0 21.1 %copy-start.25 = (f32[2,128,128]{2,1,0:T(8,128)S(1)}, f32[2,128,128]{2,1,0:T(8,128)}, u32[]{:S(2)}) copy-start(f32[2,128,128]{2,1,0:T(8,128)} %copy-done.24) | copy-start | bytes 393220
  73.0 6.8 %collective-permute-start.30 = (f32[2,128,128]{2,1,0:T(8,128)S(1)}, f32[2,128,128]{2,1,0:T(8,128)S(1)}, u32[]{:S(2)}, u32[]{:S(2)}) collective-permute-start(f32[2,128,128]{2,1,0:T(8,128)S(1)} %add.180), channel_id=1, source_target_pairs={{20,12},{16,8},{21,13},{17,9},{22,14},{18,10},{23,15},{19,11}} | collective-permute-start | bytes 393224 | tf_op jit(solution)/shard_map/ppermute | solution.py:149
  74.8 20.9 %copy-start.21 = (f32[2,128,128]{2,1,0:T(8,128)S(1)}, f32[2,128,128]{2,1,0:T(8,128)}, u32[]{:S(2)}) copy-start(f32[2,128,128]{2,1,0:T(8,128)} %copy-done.20) | copy-start | bytes 393220
  74.8 7.6 %collective-permute-start.35 = (f32[2,128,128]{2,1,0:T(8,128)S(1)}, f32[2,128,128]{2,1,0:T(8,128)S(1)}, u32[]{:S(2)}, u32[]{:S(2)}) collective-permute-start(f32[2,128,128]{2,1,0:T(8,128)S(1)} %add.186), channel_id=1, source_target_pairs={{20,12},{16,8},{21,13},{17,9},{22,14},{18,10},{23,15},{19,11}} | collective-permute-start | bytes 393224 | tf_op jit(solution)/shard_map/ppermute | solution.py:149
  76.7 8.1 %collective-permute-start.40 = (f32[2,128,128]{2,1,0:T(8,128)S(1)}, f32[2,128,128]{2,1,0:T(8,128)S(1)}, u32[]{:S(2)}, u32[]{:S(2)}) collective-permute-start(f32[2,128,128]{2,1,0:T(8,128)S(1)} %add.192), channel_id=1, source_target_pairs={{20,12},{16,8},{21,13},{17,9},{22,14},{18,10},{23,15},{19,11}} | collective-permute-start | bytes 393224 | tf_op jit(solution)/shard_map/ppermute | solution.py:149
  78.4 19.0 %copy-start.17 = (f32[2,128,128]{2,1,0:T(8,128)S(1)}, f32[2,128,128]{2,1,0:T(8,128)}, u32[]{:S(2)}) copy-start(f32[2,128,128]{2,1,0:T(8,128)} %copy-done.16) | copy-start | bytes 393220
  78.4 19.0 %collective-permute-start.26 = (f32[2,128,128]{2,1,0:T(8,128)S(1)}, f32[2,128,128]{2,1,0:T(8,128)S(1)}, u32[]{:S(2)}, u32[]{:S(2)}) collective-permute-start(f32[2,128,128]{2,1,0:T(8,128)S(1)} %get-tuple-element.175), channel_id=1, source_target_pairs={{12,4},{8,0},{13,5},{9,1},{14,6},{10,2},{15,7},{11,3}} | collective-permute-start | bytes 393224 | tf_op jit(solution)/shard_map/ppermute | solution.py:149
  80.9 17.1 %copy-start.6 = (bf16[16,256,256]{2,1,0:T(8,128)(2,1)S(1)}, bf16[16,256,256]{2,1,0:T(8,128)(2,1)}, u32[]{:S(2)}) copy-start(bf16[16,256,256]{2,1,0:T(8,128)(2,1)} %copy-done.5) | copy-start | bytes 6291460
  80.9 11.6 %collective-permute-start.31 = (f32[2,128,128]{2,1,0:T(8,128)S(1)}, f32[2,128,128]{2,1,0:T(8,128)S(1)}, u32[]{:S(2)}, u32[]{:S(2)}) collective-permute-start(f32[2,128,128]{2,1,0:T(8,128)S(1)} %get-tuple-element.171), channel_id=1, source_target_pairs={{12,4},{8,0},{13,5},{9,1},{14,6},{10,2},{15,7},{11,3}} | collective-permute-start | bytes 393224 | tf_op jit(solution)/shard_map/ppermute | solution.py:149
  83.5 10.6 %collective-permute-start.36 = (f32[2,128,128]{2,1,0:T(8,128)S(1)}, f32[2,128,128]{2,1,0:T(8,128)S(1)}, u32[]{:S(2)}, u32[]{:S(2)}) collective-permute-start(f32[2,128,128]{2,1,0:T(8,128)S(1)} %get-tuple-element.167), channel_id=1, source_target_pairs={{12,4},{8,0},{13,5},{9,1},{14,6},{10,2},{15,7},{11,3}} | collective-permute-start | bytes 393224 | tf_op jit(solution)/shard_map/ppermute | solution.py:149
  85.8 10.0 %collective-permute-start.41 = (f32[2,128,128]{2,1,0:T(8,128)S(1)}, f32[2,128,128]{2,1,0:T(8,128)S(1)}, u32[]{:S(2)}, u32[]{:S(2)}) collective-permute-start(f32[2,128,128]{2,1,0:T(8,128)S(1)} %get-tuple-element.163), channel_id=1, source_target_pairs={{12,4},{8,0},{13,5},{9,1},{14,6},{10,2},{15,7},{11,3}} | collective-permute-start | bytes 393224 | tf_op jit(solution)/shard_map/ppermute | solution.py:149
  92.5 14.8 %collective-permute-start.32 = (f32[2,128,128]{2,1,0:T(8,128)S(1)}, f32[2,128,128]{2,1,0:T(8,128)S(1)}, u32[]{:S(2)}, u32[]{:S(2)}) collective-permute-start(f32[2,128,128]{2,1,0:T(8,128)S(1)} %get-tuple-element.169), channel_id=1, source_target_pairs={{0,4},{4,0},{8,12},{12,8},{16,20},{20,16},{24,28},{28,24},{1,5},{5... | collective-permute-start | bytes 393224 | tf_op jit(solution)/shard_map/ppermute | solution.py:171
  94.1 11.0 %collective-permute-start.37 = (f32[2,128,128]{2,1,0:T(8,128)S(1)}, f32[2,128,128]{2,1,0:T(8,128)S(1)}, u32[]{:S(2)}, u32[]{:S(2)}) collective-permute-start(f32[2,128,128]{2,1,0:T(8,128)S(1)} %get-tuple-element.165), channel_id=1, source_target_pairs={{0,4},{4,0},{8,12},{12,8},{16,20},{20,16},{24,28},{28,24},{1,5},{5... | collective-permute-start | bytes 393224 | tf_op jit(solution)/shard_map/ppermute | solution.py:171
  95.8 7.9 %collective-permute-start.42 = (f32[2,128,128]{2,1,0:T(8,128)S(1)}, f32[2,128,128]{2,1,0:T(8,128)S(1)}, u32[]{:S(2)}, u32[]{:S(2)}) collective-permute-start(f32[2,128,128]{2,1,0:T(8,128)S(1)} %get-tuple-element.161), channel_id=1, source_target_pairs={{0,4},{4,0},{8,12},{12,8},{16,20},{20,16},{24,28},{28,24},{1,5},{5... | collective-permute-start | bytes 393224 | tf_op jit(solution)/shard_map/ppermute | solution.py:171
  97.4 12.0 %collective-permute-start.27 = (f32[2,128,128]{2,1,0:T(8,128)S(1)}, f32[2,128,128]{2,1,0:T(8,128)S(1)}, u32[]{:S(2)}, u32[]{:S(2)}) collective-permute-start(f32[2,128,128]{2,1,0:T(8,128)S(1)} %get-tuple-element.173), channel_id=1, source_target_pairs={{0,4},{4,0},{8,12},{12,8},{16,20},{20,16},{24,28},{28,24},{1,5},{5... | collective-permute-start | bytes 393224 | tf_op jit(solution)/shard_map/ppermute | solution.py:171
  (50 other events, 341.2 us)

commit v2 on v1

--- a/solution.py
+++ b/solution.py
@@ -33,36 +33,71 @@
     return jnp.where(mask, scores, 0.0).astype(BF16)
 
 
-def call(body, place, ins, outs, grid=(1,), aliases=None, flops=0):
+def call(body, place, ins, outs, grid=(1,), aliases=None, flops=0, grant=12):
     size = sum(a.size * a.dtype.itemsize // 2 for a, _, _ in ins)
     return pl.pallas_call(
         body,
         grid_spec=pltpu.PrefetchScalarGridSpec(
             num_scalar_prefetch=1,
             grid=grid,
-            in_specs=[pl.BlockSpec(b, m) for _, b, m in ins],
+            in_specs=[pl.BlockSpec(b, m) if b else pl.BlockSpec(memory_space=pl.ANY) for _, b, m in ins],
             out_specs=[pl.BlockSpec(b, m) for _, _, b, m in outs],
         ),
         out_shape=[jax.ShapeDtypeStruct(s, d) for s, d, _, _ in outs],
         input_output_aliases=aliases or {},
-        compiler_params=pltpu.CompilerParams(vmem_limit_bytes=24 * 1024 * 1024),
+        compiler_params=pltpu.CompilerParams(vmem_limit_bytes=grant * 1024 * 1024),
         cost_estimate=pl.CostEstimate(flops=flops, bytes_accessed=size, transcendentals=0),
     )(place, *[a for a, _, _ in ins])
 
 
-def states_body(per, place, a, b, *outs):
+def states_body(per, skip, place, a, b, *outs):
     for c, out in enumerate(outs):
         for j in range(per):
-            h = c * per + j
+            h = (skip + c) * per + j
             out[j] = dot(head(a, h), head(b, h), 0, 0)
 
 
-def local_body(heads, place, q, k, v, scores, attn):
+def local_body(per, chunks, heads, place, q, k, v, *refs):
+    outs, scores, attn = refs[:chunks], refs[chunks], refs[chunks + 1]
+    for turn in range(2):
+        @pl.when(pl.program_id(0) == turn)
+        def _():
+            for j in range(heads):
+                h = turn * heads + j
+                outs[h // per][h % per] = dot(head(k, j), head(v, j), 0, 0)
     mask = causal()
     for j in range(heads):
         s = masked(dot(head(q, j), head(k, j), 1, 1), mask)
         scores[j] = s
         attn[:, j * DH:(j + 1) * DH] = dot(s, head(v, j), 1, 0)
+
+
+def step_body(ready, sends, back, older, lately, ties, place, *refs):
+    refs = list(refs)
+    y, z = place[0], place[1]
+    if ready:
+        mine = refs.pop(0)[...] + refs.pop(0)[...]
+    if sends:
+        items = [refs.pop(0)[...] if there else mine for there in older]
+        send = items[0]
+        for at in range(1, len(items)):
+            send = jnp.where(z == at, items[at], send)
+    recent = [refs.pop(0)[...] for _ in range(lately)]
+    if sends and recent:
+        send = send + recent[-1]
+    if back:
+        kept = refs.pop(0)[...]
+        e = recent[0]
+        for at in range(1, len(recent)):
+            e = jnp.where(z == at + 1, recent[at], e)
+    del refs[:ties]
+    if ready:
+        refs.pop(0)[...] = mine
+    if sends:
+        refs.pop(0)[...] = send
+    if back:
+        refs.pop(0)[...] = e
+        refs.pop(0)[...] = jnp.where(y == 0, e + kept, e)
 
 
 def attn_body(per, first, last, place, al_k, al_o, q_k, q_o, g_k, g_o, n_k, n_o, e, r, other, *refs):
@@ -93,11 +128,11 @@
         stats[1][...] = cross
 
 
-def delta_body(per, chunks, parts, features, place, *refs):
+def delta_body(per, skip, chunks, parts, features, place, *refs):
     stats = refs[:parts]
     attn = refs[parts:parts + chunks]
-    q, g, n, d = refs[parts + chunks:parts + chunks + 4]
-    outs = refs[parts + chunks + 4:]
+    q, g, n = refs[parts + chunks:parts + chunks + 3]
+    outs = refs[parts + chunks + 3:]
     total = stats[0][...]
     for s in stats[1:]:
         total = total + s[...]
@@ -107,16 +142,16 @@
     slope = jnp.broadcast_to(slope, (DH, GROUP)).T
     for c in range(chunks):
         for j in range(per):
-            h = c * per + j
+            h = (skip + c) * per + j
             scaled = head(n, h).astype(F32) * head(g, h).astype(F32)
             x = (inverse * scaled - head(attn[c], j) * slope).astype(BF16)
-            d[:, h * DH:(h + 1) * DH] = x
-            outs[c][j] = dot(head(q, h), x, 0, 0)
-
-
-def grads_body(per, aliased, place, *refs):
+            outs[c][:, j * DH:(j + 1) * DH] = x
+            outs[chunks + c][j] = dot(head(q, h), x, 0, 0)
+
+
+def grads_body(per, ties, place, *refs):
     (q_k, q_o, k_k, k_o, v_k, v_o, s_k, s_o, d_k, d_o, sb_k, sb_o) = refs[:12]
-    qg_k, qg_o, kg_k, kg_o, vg_k, vg_o = refs[12:]
+    qg_k, qg_o, kg_k, kg_o, vg_k, vg_o = refs[12 + ties:]
     mask = causal()
     for j in range(per):
         at = slice(j * DH, (j + 1) * DH)
@@ -148,29 +183,71 @@
             pairs = [(count - 1 - a, count - 1 - b) for a, b in pairs]
         return lax.ppermute(array, "seq", pairs)
 
-    def along(part, reverse):
-        if long <= 4:
-            carry, send = None, part
-            for z in range(long - 1):
-                got = hop(send, lambda at: at == z, 1, reverse)
-                carry = got if carry is None else carry + got
-                send = carry + part
-            return jnp.zeros_like(part) if carry is None else carry
-        carry = hop(part, lambda at: True, 1, reverse)
-        far = 1
-        while far < long:
-            carry = carry + hop(carry, lambda at: True, far, reverse)
-            far *= 2
-        return carry
-
-    def scan(kept, sent, leads, reverse):
+    def shift(array, far, reverse):
+        return hop(array, lambda at: True, far, reverse)
+
+    def doubling(parts, reverse):
         out = []
-        for a, b in zip(kept, sent):
-            r = lax.ppermute(b, "seq", swap)
-            e = along(a + r, reverse)
-            other = lax.ppermute(jnp.where(leads, e + a, e), "seq", swap)
-            out.append((e, r, other))
+        for part in parts:
+            carry = shift(part, 1, reverse)
+            far = 1
+            while far < long:
+                carry = carry + shift(carry, far, reverse)
+                far *= 2
+            out.append(carry)
         return out
+
+    def scan(kept, sent, y, z, reverse, beside):
+        swapped = [lax.ppermute(b, "seq", swap) for b in sent]
+        if long > 4 or long < 2:
+            sums = [a + r for a, r in zip(kept, swapped)]
+            sums = doubling(sums, reverse) if long > 1 else [jnp.zeros_like(a) for a in sums]
+            others = [
+                lax.ppermute(jnp.where(y == 0, e + a, e), "seq", swap) for a, e in zip(kept, sums)
+            ]
+            return list(zip(sums, swapped, others)), [work(None) for work in beside]
+        chunks = len(kept)
+        shape = kept[0].shape
+        where = jnp.stack([y, z]).astype(jnp.int32)
+        whole = lambda i, s: (0, 0, 0)
+        parts, got, out, done, ties = [], [], [], [], []
+        for t in range(chunks + long - 1):
+            ready, sends, back = t < chunks, t < chunks + long - 2, t - (long - 1)
+            ins, outs = [], 0
+            if ready:
+                ins += [kept[t], swapped[t]]
+                outs += 1
+            older = []
+            if sends:
+                older = [parts[min(max(t - at, 0), chunks - 1)] if (t - at != t or not ready) and parts else None
+                         for at in range(long - 1)]
+                ins += [a for a in older if a is not None]
+                outs += 1
+            lately = got[max(back, 0):] if back >= 0 else got[-1:]
+            ins += lately
+            if back >= 0:
+                ins += [kept[back]]
+                outs += 2
+            here = functools.partial(step_body, ready, sends, back >= 0, tuple(a is not None for a in older), len(lately), len(ties))
+            result = list(call(
+                here, where, [(a, shape, whole) for a in ins] + [(a, None, None) for a in ties],
+                [(shape, F32, shape, whole)] * outs, flops=kept[0].size))
+            ties = []
+            if ready:
+                parts.append(result.pop(0))
+            if sends:
+                send = result.pop(0)
+                got.append(shift(send, 1, reverse))
+                if t > 0 and len(done) < len(beside):
+                    done.append(beside[len(done)](send))
+                    ties.append(done[-1][0])
+            if back >= 0:
+                e, turned = result
+                out.append((e, swapped[back], lax.ppermute(turned, "seq", swap)))
+                ties.append(out[-1][2])
+        while len(done) < len(beside):
+            done.append(beside[len(done)](None))
+        return out, done
 
     def shards(queries, keys, values, out_grad, norm_gain):
         tokens, width = queries.shape
@@ -179,7 +256,8 @@
         per = half // CHUNKS
         wide = half * DH
         narrow = per * DH
-        y = lax.axis_index("seq") % 2
+        at_seq = lax.axis_index("seq")
+        y, z = at_seq % 2, at_seq // 2
         place = y.astype(jnp.int32).reshape(1)
         turned = 1 - place
         gain = norm_gain.reshape(1, width)
@@ -202,29 +280,30 @@
         def at_o3(c):
             return lambda i, s: ((1 - s[0]) * CHUNKS + c, 0, 0)
 
-        def states(a, b, index):
+        def states(skip, width, index):
+            count = width // narrow - skip
             return call(
-                functools.partial(states_body, per), place,
-                [(a, (tokens, wide), index), (b, (tokens, wide), index)],
-                [((per, DH, DH), F32, (per, DH, DH), whole3)] * CHUNKS,
-                flops=half * mac * DH,
+                functools.partial(states_body, per, skip), place,
+                [(a, (tokens, width), index) for a in (keys, values)],
+                [((per, DH, DH), F32, (per, DH, DH), whole3)] * count,
+                flops=count * per * mac * DH, grant=61,
             )
 
-        sent = states(keys, values, sent_half)
-        kept = states(keys, values, kept_half)
-
-        group = 4
-        scores, attn_local = call(
-            functools.partial(local_body, group), place,
-            [(a, (tokens, group * DH), lambda i, s: (0, i)) for a in (queries, keys, values)],
-            [
-                ((heads, GROUP, GROUP), BF16, (group, GROUP, GROUP), lambda i, s: (i, 0, 0)),
-                ((tokens, width), F32, (tokens, group * DH), lambda i, s: (0, i)),
+        sent = states(0, narrow, at_o(0)) + states(1, wide, sent_half)
+
+        group = half // 2
+        strip = lambda i, s: (0, (2 * s[0] + i) % 4)
+        *kept, scores, attn_local = call(
+            functools.partial(local_body, per, CHUNKS, group), place,
+            [(a, (tokens, group * DH), strip) for a in (queries, keys, values)],
+            [((per, DH, DH), F32, (per, DH, DH), whole3)] * CHUNKS + [
+                ((heads, GROUP, GROUP), BF16, (group, GROUP, GROUP), lambda i, s: ((2 * s[0] + i) % 4, 0, 0)),
+                ((tokens, width), F32, (tokens, group * DH), strip),
             ],
-            grid=(heads // group,), flops=2 * heads * mac * GROUP,
+            grid=(4,), flops=heads * mac * (2 * GROUP + DH // 2),
         )
 
-        before = scan(kept, sent, y == 0, False)
+        before, _ = scan(kept, sent, y, z, False, [])
 
         block = (tokens, narrow)
         square = cross = None
@@ -257,34 +336,40 @@
         for step in range(1, parts):
             sums.append(lax.ppermute(mine, "head", [(i, (i + step) % parts) for i in range(parts)]))
 
-        def delta(which, index):
+        def delta(which, skip, width, index):
+            count = width // narrow - skip
             ins = [(a, (2, GROUP), whole2) for a in sums]
-            ins += [(attns[c][which], block, whole2) for c in range(CHUNKS)]
-            ins += [(queries, (tokens, wide), index), (out_grad, (tokens, wide), index), (gain, (1, wide), index)]
-            outs = [((tokens, wide), BF16, (tokens, wide), whole2)]
-            outs += [((per, DH, DH), F32, (per, DH, DH), whole3)] * CHUNKS
-            d, *g = call(
-                functools.partial(delta_body, per, CHUNKS, parts, float(parts * width)), place, ins, outs,
-                flops=half * mac * DH)
-            return d, g
-
-        d_o, sent = delta(1, sent_half)
-        d_k, kept = delta(0, kept_half)
-        after = scan(kept, sent, y == 1, True)
-
-        grads = []
-        for c in range(CHUNKS):
+            ins += [(attns[skip + c][which], block, whole2) for c in range(count)]
+            ins += [(queries, (tokens, width), index), (out_grad, (tokens, width), index), (gain, (1, width), index)]
+            outs = [(block, BF16, block, whole2)] * count
+            outs += [((per, DH, DH), F32, (per, DH, DH), whole3)] * count
+            result = call(
+                functools.partial(delta_body, per, skip, count, parts, float(parts * heads * DH)), place, ins, outs,
+                flops=count * per * mac * DH)
+            return result[:count], result[count:]
+
+        d_first, first_sent = delta(1, 0, narrow, at_o(0))
+        d_rest, rest_sent = delta(1, 1, wide, sent_half)
+        d_o, sent = d_first + d_rest, first_sent + rest_sent
+        d_k, kept = delta(0, 0, wide, kept_half)
+
+        def grads(c, tie):
             ins = []
             for a in (queries, keys, values):
                 ins += [(a, block, at_k(c)), (a, block, at_o(c))]
             ins += [(scores, (per, GROUP, GROUP), at_k3(c)), (scores, (per, GROUP, GROUP), at_o3(c))]
-            here = lambda i, s, c=c: (0, c)
-            ins += [(d_k, block, here), (d_o, block, here)]
+            ins += [(d_k[c], block, whole2), (d_o[c], block, whole2)]
             ins += [(a, (per, DH, DH), whole3) for a in priors[c]]
+            ties = 0 if tie is None else 1
+            if ties:
+                ins += [(tie, None, None)]
             outs = [(block, BF16, block, whole2)] * 2 + [(block, F32, block, whole2)] * 4
-            grads.append(call(
-                functools.partial(grads_body, per, c > 0), place, ins, outs,
-                flops=2 * per * mac * (4 * GROUP + DH)))
+            return call(
+                functools.partial(grads_body, per, ties), place, ins, outs,
+                flops=2 * per * mac * (4 * GROUP + DH))
+
+        after, grads = scan(
+            kept, sent, 1 - y, long - 1 - z, True, [functools.partial(grads, c) for c in range(CHUNKS)])
 
         kg = vg = qg = None
         for c in range(CHUNKS):
@@ -305,7 +390,7 @@
         if done[0] is not None:
             for n, a in enumerate(done):
                 aliases[len(ins) + 1] = n
-                ins.append((a, (8, 128), whole2))
+                ins.append((a, None, None))
         outs = [((tokens, width), BF16, block, mine)] * 3
 
         def body(place, qk, qo, kk, ko, vk, vo, k, v, e, r, other, *refs):

time: 112 us -> 145 us (1.29)
  waiting for transfers between devices: 19.7 us -> 44.3 us
  other arithmetic: 12.3 us -> 0.15 us
  Pallas kernels: 19.5 us -> 30.5 us
  local copies, waits for them, and re-layouts: 7.79 us -> 13.2 us
  starting transfers between devices: 50.5 us -> 54.6 us
    ppermute x24 -> x12, waiting for transfers between devices: 7.84 us -> 29.2 us  [hop(): return lax.ppermute(array, 'seq', pairs)]
    add x24 -> x0, other arithmetic: 12 us -> none  [the longest x16 9.95 us: along(): send = carry + part]
    pallas_call x17 -> x32, Pallas kernels: 19.5 us -> 30.5 us  [call(): pl.pallas_call(body, grid_spec=pltpu.PrefetchScalarGridSpec(num_scalar_pr...]
    unnamed x110 -> x66, local copies, waits for them, and re-layouts: 7.78 us -> 13.2 us
    ppermute x16, waiting for transfers between devices: 8.98 us -> 12.4 us  [the longest x8 12.3 us: scan(): out.append((e, swapped[back], lax.ppermute(turned, 'seq', swap)))]
    ppermute x24 -> x12, starting transfers between devices: 30.1 us -> 33 us  [hop(): return lax.ppermute(array, 'seq', pairs)]
  transfers between devices with their start and end apart: 43 -> 31, of which waited for: 13 -> 20; matrix products, arithmetic and copies ran while one was open for 11% -> 0% of each run, Pallas kernels for 14% -> 15%
where the time goes in v2:
time: 145 us; the launch traced here: 144 us
  starting transfers between devices  54.6 us (38%)
  waiting for transfers between devices  44.3 us (31%)
  Pallas kernels  30.5 us (21%)
  local copies, waits for them, and re-layouts  13.2 us (9%)
    ppermute x12, starting transfers between devices, hop(): return lax.ppermute(array, 'seq', pairs)  33 us
    pallas_call x32, Pallas kernels, call(): pl.pallas_call(body, grid_spec=pltpu.PrefetchScalarGridSpec(num_scalar_pr...  30.5 us
    ppermute x12, waiting for transfers between devices, hop(): return lax.ppermute(array, 'seq', pairs)  29.2 us
    unnamed x66, local copies, waits for them, and re-layouts  13.2 us
    ppermute x8, waiting for transfers between devices, scan(): out.append((e, swapped[back], lax.ppermute(turned, 'seq', swap)))  12.3 us
    ppermute x8, starting transfers between devices, scan(): out.append((e, swapped[back], lax.ppermute(turned, 'seq', swap)))  9.95 us
    ppermute x8, starting transfers between devices, scan(): swapped = [lax.ppermute(b, 'seq', swap) for b in sent]  9.95 us
  transfers between devices with their start and end apart: 31, of which 20 were waited for; matrix products, arithmetic and copies ran while one was open for 0% of the time, Pallas kernels for 15%

profile of v2, /device:TPU:0, one launch (start us, length us, event | category | flops | bytes accessed | tf_op | source)
XLA Modules:
  0.0 144.0 jit_solution(14614879048194141922)
XLA Ops:
  0.7 2.0 %shard_map.78 = f32[2,128,128]{2,1,0:T(8,128)} custom-call(s32[1]{0:T(128)} %bitcast.place, bf16[256,2048]{1,0:T(8,128)(2,1)} %k.9, bf16[256,2048]{1,0:T(8,128)(2,1)} %v.9), custom_call_target="tpu_custom_call" | custom-call | flops 16777216 | bytes 1048576 | tf_op jit(solution)/shard_map/pallas_call | solution.py:38
  2.7 3.0 %collective-permute-start.3 = (f32[2,128,128]{2,1,0:T(8,128)}, f32[2,128,128]{2,1,0:T(8,128)S(1)}, u32[]{:S(2)}, u32[]{:S(2)}) collective-permute-start(f32[2,128,128]{2,1,0:T(8,128)} %shard_map.78), channel_id=1, source_target_pairs={{0,4},{4,0},{8,12},{12,8},{16,20},{20,16},{24,28},{28,24},{1,5},{5... | collective-permute-start | bytes 393224 | tf_op jit(solution)/shard_map/ppermute | solution.py:201
  5.6 2.2 %shard_map.77 = (f32[2,128,128]{2,1,0:T(8,128)}, f32[2,128,128]{2,1,0:T(8,128)}, f32[2,128,128]{2,1,0:T(8,128)}) custom-call(s32[1]{0:T(128)} %bitcast.place, bf16[256,2048]{1,0:T(8,128)(2,1)} %k.9, bf16[256,2048]{1,0:T(8,128)(2,1)} %v.9), custom_call_target="tpu_custom_call" | custom-call | flops 50331648 | bytes 1048576 | tf_op jit(solution)/shard_map/pallas_call | solution.py:38
  9.1 3.8 %shard_map.76 = (f32[2,128,128]{2,1,0:T(8,128)S(1)}, f32[2,128,128]{2,1,0:T(8,128)S(1)}, f32[2,128,128]{2,1,0:T(8,128)S(1)}, f32[2,128,128]{2,1,0:T(8,128)S(1)},...) custom-call(s32[1]{0:T(128)} %bitcast.place, bf16[256,2048]{1,0:T(8,128)(2,1)S(1)} %copy-done, ...), custom_call_target="tpu_custom_call" | custom-call | flops 603979776 | bytes 1572864 | tf_op jit(solution)/shard_map/pallas_call | solution.py:38
  12.9 1.3 copy-done.4
  14.2 1.3 copy-done.6
  16.2 4.0 %collective-permute-start.4 = (f32[2,128,128]{2,1,0:T(8,128)S(1)}, f32[2,128,128]{2,1,0:T(8,128)S(1)}, u32[]{:S(2)}, u32[]{:S(2)}) collective-permute-start(f32[2,128,128]{2,1,0:T(8,128)S(1)} %get-tuple-element.133), channel_id=1, source_target_pairs={{0,8},{4,12},{8,16},{12,20},{16,24},{20,28},{1,9},{5,13},{9,17},{1... | collective-permute-start | bytes 393224 | tf_op jit(solution)/shard_map/ppermute | solution.py:184
  20.2 1.6 %collective-permute-start.1 = (f32[2,128,128]{2,1,0:T(8,128)S(1)}, f32[2,128,128]{2,1,0:T(8,128)S(1)}, u32[]{:S(2)}, u32[]{:S(2)}) collective-permute-start(f32[2,128,128]{2,1,0:T(8,128)S(1)} %copy-done.32), channel_id=1, source_target_pairs={{0,4},{4,0},{8,12},{12,8},{16,20},{20,16},{24,28},{28,24},{1,5},{5... | collective-permute-start | bytes 393224 | tf_op jit(solution)/shard_map/ppermute | solution.py:201
  23.3 4.4 %collective-permute-start.5 = (f32[2,128,128]{2,1,0:T(8,128)S(1)}, f32[2,128,128]{2,1,0:T(8,128)S(1)}, u32[]{:S(2)}, u32[]{:S(2)}) collective-permute-start(f32[2,128,128]{2,1,0:T(8,128)S(1)} %get-tuple-element.135), channel_id=1, source_target_pairs={{0,8},{4,12},{8,16},{12,20},{16,24},{20,28},{1,9},{5,13},{9,17},{1... | collective-permute-start | bytes 393224 | tf_op jit(solution)/shard_map/ppermute | solution.py:184
  27.6 1.6 %collective-permute-start = (f32[2,128,128]{2,1,0:T(8,128)S(1)}, f32[2,128,128]{2,1,0:T(8,128)S(1)}, u32[]{:S(2)}, u32[]{:S(2)}) collective-permute-start(f32[2,128,128]{2,1,0:T(8,128)S(1)} %copy-done.31), channel_id=1, source_target_pairs={{0,4},{4,0},{8,12},{12,8},{16,20},{20,16},{24,28},{28,24},{1,5},{5... | collective-permute-start | bytes 393224 | tf_op jit(solution)/shard_map/ppermute | solution.py:201
  30.7 4.5 %collective-permute-start.6 = (f32[2,128,128]{2,1,0:T(8,128)S(1)}, f32[2,128,128]{2,1,0:T(8,128)S(1)}, u32[]{:S(2)}, u32[]{:S(2)}) collective-permute-start(f32[2,128,128]{2,1,0:T(8,128)S(1)} %get-tuple-element.137), channel_id=1, source_target_pairs={{0,8},{4,12},{8,16},{12,20},{16,24},{20,28},{1,9},{5,13},{9,17},{1... | collective-permute-start | bytes 393224 | tf_op jit(solution)/shard_map/ppermute | solution.py:184
  35.2 2.5 %collective-permute-done.6.refs_6_.refs_4_.refs_3_ = f32[2,128,128]{2,1,0:T(8,128)S(1)} collective-permute-done((f32[2,128,128]{2,1,0:T(8,128)S(1)}, f32[2,128,128]{2,1,0:T(8,128)S(1)}, u32[]{:S(2)}, u32[]{:S(2)}) %collective-permute-start.6) | collective-permute-done | bytes 131104 | tf_op jit(solution)/shard_map/ppermute | solution.py:184
  38.3 4.4 %collective-permute-start.7 = (f32[2,128,128]{2,1,0:T(8,128)S(1)}, f32[2,128,128]{2,1,0:T(8,128)S(1)}, u32[]{:S(2)}, u32[]{:S(2)}) collective-permute-start(f32[2,128,128]{2,1,0:T(8,128)S(1)} %get-tuple-element.138), channel_id=1, source_target_pairs={{0,8},{4,12},{8,16},{12,20},{16,24},{20,28},{1,9},{5,13},{9,17},{1... | collective-permute-start | bytes 393224 | tf_op jit(solution)/shard_map/ppermute | solution.py:184
  42.7 1.6 %collective-permute-start.8 = (f32[2,128,128]{2,1,0:T(8,128)S(1)}, f32[2,128,128]{2,1,0:T(8,128)S(1)}, u32[]{:S(2)}, u32[]{:S(2)}) collective-permute-start(f32[2,128,128]{2,1,0:T(8,128)S(1)} %get-tuple-element.140), channel_id=1, source_target_pairs={{0,4},{4,0},{8,12},{12,8},{16,20},{20,16},{24,28},{28,24},{1,5},{5... | collective-permute-start | bytes 393224 | tf_op jit(solution)/shard_map/ppermute | solution.py:246
  45.2 2.5 %collective-permute-done.8.refs_7_.other = f32[2,128,128]{2,1,0:T(8,128)S(1)} collective-permute-done((f32[2,128,128]{2,1,0:T(8,128)S(1)}, f32[2,128,128]{2,1,0:T(8,128)S(1)}, u32[]{:S(2)}, u32[]{:S(2)}) %collective-permute-start.8) | collective-permute-done | bytes 131104 | tf_op jit(solution)/shard_map/ppermute | solution.py:246
  48.3 3.5 %collective-permute-start.9 = (f32[2,128,128]{2,1,0:T(8,128)S(1)}, f32[2,128,128]{2,1,0:T(8,128)S(1)}, u32[]{:S(2)}, u32[]{:S(2)}) collective-permute-start(f32[2,128,128]{2,1,0:T(8,128)S(1)} %get-tuple-element.141), channel_id=1, source_target_pairs={{0,8},{4,12},{8,16},{12,20},{16,24},{20,28},{1,9},{5,13},{9,17},{1... | collective-permute-start | bytes 393224 | tf_op jit(solution)/shard_map/ppermute | solution.py:184
  51.8 1.6 %collective-permute-start.10 = (f32[2,128,128]{2,1,0:T(8,128)S(1)}, f32[2,128,128]{2,1,0:T(8,128)S(1)}, u32[]{:S(2)}, u32[]{:S(2)}) collective-permute-start(f32[2,128,128]{2,1,0:T(8,128)S(1)} %get-tuple-element.142), channel_id=1, source_target_pairs={{0,4},{4,0},{8,12},{12,8},{16,20},{20,16},{24,28},{28,24},{1,5},{5... | collective-permute-start | bytes 393224 | tf_op jit(solution)/shard_map/ppermute | solution.py:246
  54.3 2.8 %collective-permute-done.10.refs_7_.other = f32[2,128,128]{2,1,0:T(8,128)S(1)} collective-permute-done((f32[2,128,128]{2,1,0:T(8,128)S(1)}, f32[2,128,128]{2,1,0:T(8,128)S(1)}, u32[]{:S(2)}, u32[]{:S(2)}) %collective-permute-start.10) | collective-permute-done | bytes 131104 | tf_op jit(solution)/shard_map/ppermute | solution.py:246
  57.7 4.6 %collective-permute-start.11 = (f32[2,128,128]{2,1,0:T(8,128)S(1)}, f32[2,128,128]{2,1,0:T(8,128)S(1)}, u32[]{:S(2)}, u32[]{:S(2)}) collective-permute-start(f32[2,128,128]{2,1,0:T(8,128)S(1)} %get-tuple-element.143), channel_id=1, source_target_pairs={{0,8},{4,12},{8,16},{12,20},{16,24},{20,28},{1,9},{5,13},{9,17},{1... | collective-permute-start | bytes 393224 | tf_op jit(solution)/shard_map/ppermute | solution.py:184
  62.3 1.6 %collective-permute-start.12 = (f32[2,128,128]{2,1,0:T(8,128)S(1)}, f32[2,128,128]{2,1,0:T(8,128)S(1)}, u32[]{:S(2)}, u32[]{:S(2)}) collective-permute-start(f32[2,128,128]{2,1,0:T(8,128)S(1)} %get-tuple-element.144), channel_id=1, source_target_pairs={{0,4},{4,0},{8,12},{12,8},{16,20},{20,16},{24,28},{28,24},{1,5},{5... | collective-permute-start | bytes 393224 | tf_op jit(solution)/shard_map/ppermute | solution.py:246
  64.8 2.5 %collective-permute-done.12.refs_4_.other = f32[2,128,128]{2,1,0:T(8,128)S(1)} collective-permute-done((f32[2,128,128]{2,1,0:T(8,128)S(1)}, f32[2,128,128]{2,1,0:T(8,128)S(1)}, u32[]{:S(2)}, u32[]{:S(2)}) %collective-permute-start.12) | collective-permute-done | bytes 131104 | tf_op jit(solution)/shard_map/ppermute | solution.py:246
  67.9 1.6 %collective-permute-start.13 = (f32[2,128,128]{2,1,0:T(8,128)S(1)}, f32[2,128,128]{2,1,0:T(8,128)S(1)}, u32[]{:S(2)}, u32[]{:S(2)}) collective-permute-start(f32[2,128,128]{2,1,0:T(8,128)S(1)} %get-tuple-element.146), channel_id=1, source_target_pairs={{0,4},{4,0},{8,12},{12,8},{16,20},{20,16},{24,28},{28,24},{1,5},{5... | collective-permute-start | bytes 393224 | tf_op jit(solution)/shard_map/ppermute | solution.py:246
  76.0 1.5 %collective-permute-start.15 = (f32[2,256]{1,0:T(2,128)S(1)}, f32[2,256]{1,0:T(2,128)S(1)}, u32[]{:S(2)}, u32[]{:S(2)}) collective-permute-start(f32[2,256]{1,0:T(2,128)S(1)} %get-tuple-element.156.refs_0_), channel_id=1, source_target_pairs={{0,2},{1,3},{2,0},{3,1},{4,6},{5,7},{6,4},{7,5},{8,10},{9,11},{10,... | collective-permute-start | bytes 6152 | tf_op jit(solution)/shard_map/ppermute | solution.py:337
  77.7 1.9 %collective-permute-done.15.refs_2_ = f32[2,256]{1,0:T(2,128)S(1)} collective-permute-done((f32[2,256]{1,0:T(2,128)S(1)}, f32[2,256]{1,0:T(2,128)S(1)}, u32[]{:S(2)}, u32[]{:S(2)}) %collective-permute-start.15) | collective-permute-done | bytes 2080 | tf_op jit(solution)/shard_map/ppermute | solution.py:337
  83.8 1.6 %collective-permute-start.19 = (f32[2,128,128]{2,1,0:T(8,128)S(1)}, f32[2,128,128]{2,1,0:T(8,128)S(1)}, u32[]{:S(2)}, u32[]{:S(2)}) collective-permute-start(f32[2,128,128]{2,1,0:T(8,128)S(1)} %get-tuple-element.173), channel_id=1, source_target_pairs={{0,4},{4,0},{8,12},{12,8},{16,20},{20,16},{24,28},{28,24},{1,5},{5... | collective-permute-start | bytes 393224 | tf_op jit(solution)/shard_map/ppermute | solution.py:201
  89.4 1.3 collective-permute-start.21
  91.6 4.7 %collective-permute-done.21.refs_4_ = f32[2,128,128]{2,1,0:T(8,128)S(1)} collective-permute-done((f32[2,128,128]{2,1,0:T(8,128)S(1)}, f32[2,128,128]{2,1,0:T(8,128)S(1)}, u32[]{:S(2)}, u32[]{:S(2)}) %collective-permute-start.21) | collective-permute-done | bytes 131104 | tf_op jit(solution)/shard_map/ppermute | solution.py:184
  96.9 1.3 collective-permute-start.22
  99.1 1.4 shard_map.95
  100.5 3.3 %collective-permute-done.22.refs_4_.refs_5_.refs_3_ = f32[2,128,128]{2,1,0:T(8,128)S(1)} collective-permute-done((f32[2,128,128]{2,1,0:T(8,128)S(1)}, f32[2,128,128]{2,1,0:T(8,128)S(1)}, u32[]{:S(2)}, u32[]{:S(2)}) %collective-permute-start.22) | collective-permute-done | bytes 131104 | tf_op jit(solution)/shard_map/ppermute | solution.py:184
  104.3 1.3 collective-permute-start.23
  105.6 1.4 shard_map.97
  107.0 4.1 %collective-permute-done.23.refs_6_.refs_4_.refs_3_ = f32[2,128,128]{2,1,0:T(8,128)S(1)} collective-permute-done((f32[2,128,128]{2,1,0:T(8,128)S(1)}, f32[2,128,128]{2,1,0:T(8,128)S(1)}, u32[]{:S(2)}, u32[]{:S(2)}) %collective-permute-start.23) | collective-permute-done | bytes 131104 | tf_op jit(solution)/shard_map/ppermute | solution.py:184
  112.6 1.3 collective-permute-start.24
  113.9 1.4 shard_map.99
  115.3 2.6 %collective-permute-done.25.refs_8_.other = f32[2,128,128]{2,1,0:T(8,128)S(1)} collective-permute-done((f32[2,128,128]{2,1,0:T(8,128)S(1)}, f32[2,128,128]{2,1,0:T(8,128)S(1)}, u32[]{:S(2)}, u32[]{:S(2)}) %collective-permute-start.25) | collective-permute-done | bytes 131104 | tf_op jit(solution)/shard_map/ppermute | solution.py:246
  117.9 2.5 %collective-permute-done.24.refs_5_.refs_4_.refs_0_ = f32[2,128,128]{2,1,0:T(8,128)S(1)} collective-permute-done((f32[2,128,128]{2,1,0:T(8,128)S(1)}, f32[2,128,128]{2,1,0:T(8,128)S(1)}, u32[]{:S(2)}, u32[]{:S(2)}) %collective-permute-start.24) | collective-permute-done | bytes 131104 | tf_op jit(solution)/shard_map/ppermute | solution.py:184
  121.0 1.6 %collective-permute-start.27 = (f32[2,128,128]{2,1,0:T(8,128)S(1)}, f32[2,128,128]{2,1,0:T(8,128)S(1)}, u32[]{:S(2)}, u32[]{:S(2)}) collective-permute-start(f32[2,128,128]{2,1,0:T(8,128)S(1)} %get-tuple-element.208), channel_id=1, source_target_pairs={{0,4},{4,0},{8,12},{12,8},{16,20},{20,16},{24,28},{28,24},{1,5},{5... | collective-permute-start | bytes 393224 | tf_op jit(solution)/shard_map/ppermute | solution.py:246
  122.7 1.3 collective-permute-start.26
  124.0 1.4 shard_map.101
  125.4 1.6 %collective-permute-done.27.refs_8_.other = f32[2,128,128]{2,1,0:T(8,128)S(1)} collective-permute-done((f32[2,128,128]{2,1,0:T(8,128)S(1)}, f32[2,128,128]{2,1,0:T(8,128)S(1)}, u32[]{:S(2)}, u32[]{:S(2)}) %collective-permute-start.27) | collective-permute-done | bytes 131104 | tf_op jit(solution)/shard_map/ppermute | solution.py:246
  127.0 2.6 %collective-permute-done.26.refs_5_.refs_1_ = f32[2,128,128]{2,1,0:T(8,128)S(1)} collective-permute-done((f32[2,128,128]{2,1,0:T(8,128)S(1)}, f32[2,128,128]{2,1,0:T(8,128)S(1)}, u32[]{:S(2)}, u32[]{:S(2)}) %collective-permute-start.26) | collective-permute-done | bytes 131104 | tf_op jit(solution)/shard_map/ppermute | solution.py:184
  130.1 1.3 collective-permute-start.28
  132.0 5.0 %collective-permute-done.28.refs_2_ = f32[2,128,128]{2,1,0:T(8,128)S(1)} collective-permute-done((f32[2,128,128]{2,1,0:T(8,128)S(1)}, f32[2,128,128]{2,1,0:T(8,128)S(1)}, u32[]{:S(2)}, u32[]{:S(2)}) %collective-permute-start.28) | collective-permute-done | bytes 131104 | tf_op jit(solution)/shard_map/ppermute | solution.py:184
  138.1 1.4 shard_map.104
  139.5 1.4 shard_map.105
  140.9 1.4 shard_map.106
  142.6 1.4 shard_map.107
  (115 shorter events, 32.3 us)
Async XLA Ops:
  0.6 7.2 %copy-start = (bf16[256,2048]{1,0:T(8,128)(2,1)S(1)}, bf16[256,2048]{1,0:T(8,128)(2,1)}, u32[]{:S(2)}) copy-start(bf16[256,2048]{1,0:T(8,128)(2,1)} %refs_1_.7) | copy-start | bytes 3145732
  0.7 7.2 %copy-start.1 = (bf16[256,2048]{1,0:T(8,128)(2,1)S(1)}, bf16[256,2048]{1,0:T(8,128)(2,1)}, u32[]{:S(2)}) copy-start(bf16[256,2048]{1,0:T(8,128)(2,1)} %k.9) | copy-start | bytes 3145732
  2.7 12.9 %collective-permute-start.3 = (f32[2,128,128]{2,1,0:T(8,128)}, f32[2,128,128]{2,1,0:T(8,128)S(1)}, u32[]{:S(2)}, u32[]{:S(2)}) collective-permute-start(f32[2,128,128]{2,1,0:T(8,128)} %shard_map.78), channel_id=1, source_target_pairs={{0,4},{4,0},{8,12},{12,8},{16,20},{20,16},{24,28},{28,24},{1,5},{5... | collective-permute-start | bytes 393224 | tf_op jit(solution)/shard_map/ppermute | solution.py:201
  7.8 14.0 %collective-permute-start.2 = (f32[2,128,128]{2,1,0:T(8,128)}, f32[2,128,128]{2,1,0:T(8,128)S(1)}, u32[]{:S(2)}, u32[]{:S(2)}) collective-permute-start(f32[2,128,128]{2,1,0:T(8,128)} %get-tuple-element.130), channel_id=1, source_target_pairs={{0,4},{4,0},{8,12},{12,8},{16,20},{20,16},{24,28},{28,24},{1,5},{5... | collective-permute-start | bytes 393224 | tf_op jit(solution)/shard_map/ppermute | solution.py:201
  9.1 11.1 %copy-start.32 = (f32[2,128,128]{2,1,0:T(8,128)S(1)}, f32[2,128,128]{2,1,0:T(8,128)}, u32[]{:S(2)}) copy-start(f32[2,128,128]{2,1,0:T(8,128)} %get-tuple-element.128) | copy-start | bytes 393220
  9.1 18.6 %copy-start.31 = (f32[2,128,128]{2,1,0:T(8,128)S(1)}, f32[2,128,128]{2,1,0:T(8,128)}, u32[]{:S(2)}) copy-start(f32[2,128,128]{2,1,0:T(8,128)} %get-tuple-element.126) | copy-start | bytes 393220
  16.2 6.5 %collective-permute-start.4 = (f32[2,128,128]{2,1,0:T(8,128)S(1)}, f32[2,128,128]{2,1,0:T(8,128)S(1)}, u32[]{:S(2)}, u32[]{:S(2)}) collective-permute-start(f32[2,128,128]{2,1,0:T(8,128)S(1)} %get-tuple-element.133), channel_id=1, source_target_pairs={{0,8},{4,12},{8,16},{12,20},{16,24},{20,28},{1,9},{5,13},{9,17},{1... | collective-permute-start | bytes 393224 | tf_op jit(solution)/shard_map/ppermute | solution.py:184
  20.2 9.0 %collective-permute-start.1 = (f32[2,128,128]{2,1,0:T(8,128)S(1)}, f32[2,128,128]{2,1,0:T(8,128)S(1)}, u32[]{:S(2)}, u32[]{:S(2)}) collective-permute-start(f32[2,128,128]{2,1,0:T(8,128)S(1)} %copy-done.32), channel_id=1, source_target_pairs={{0,4},{4,0},{8,12},{12,8},{16,20},{20,16},{24,28},{28,24},{1,5},{5... | collective-permute-start | bytes 393224 | tf_op jit(solution)/shard_map/ppermute | solution.py:201
  23.3 6.9 %collective-permute-start.5 = (f32[2,128,128]{2,1,0:T(8,128)S(1)}, f32[2,128,128]{2,1,0:T(8,128)S(1)}, u32[]{:S(2)}, u32[]{:S(2)}) collective-permute-start(f32[2,128,128]{2,1,0:T(8,128)S(1)} %get-tuple-element.135), channel_id=1, source_target_pairs={{0,8},{4,12},{8,16},{12,20},{16,24},{20,28},{1,9},{5,13},{9,17},{1... | collective-permute-start | bytes 393224 | tf_op jit(solution)/shard_map/ppermute | solution.py:184
  27.6 7.6 %collective-permute-start = (f32[2,128,128]{2,1,0:T(8,128)S(1)}, f32[2,128,128]{2,1,0:T(8,128)S(1)}, u32[]{:S(2)}, u32[]{:S(2)}) collective-permute-start(f32[2,128,128]{2,1,0:T(8,128)S(1)} %copy-done.31), channel_id=1, source_target_pairs={{0,4},{4,0},{8,12},{12,8},{16,20},{20,16},{24,28},{28,24},{1,5},{5... | collective-permute-start | bytes 393224 | tf_op jit(solution)/shard_map/ppermute | solution.py:201
  30.1 39.4 %copy-start.30 = (bf16[2048]{0:T(1024)(128)(2,1)S(1)}, bf16[2048]{0:T(1024)(128)(2,1)}, u32[]{:S(2)}) copy-start(bf16[2048]{0:T(1024)(128)(2,1)} %param.9) | copy-start | bytes 12292
  30.1 39.4 %copy-start.5 = (f32[256,2048]{1,0:T(8,128)S(1)}, f32[256,2048]{1,0:T(8,128)}, u32[]{:S(2)}) copy-start(f32[256,2048]{1,0:T(8,128)} %copy-done.4) | copy-start | bytes 6291460
  30.1 39.4 %copy-start.8 = (bf16[256,2048]{1,0:T(8,128)(2,1)S(1)}, bf16[256,2048]{1,0:T(8,128)(2,1)}, u32[]{:S(2)}) copy-start(bf16[256,2048]{1,0:T(8,128)(2,1)} %refs_6_.1) | copy-start | bytes 3145732
  30.7 7.0 %collective-permute-start.6 = (f32[2,128,128]{2,1,0:T(8,128)S(1)}, f32[2,128,128]{2,1,0:T(8,128)S(1)}, u32[]{:S(2)}, u32[]{:S(2)}) collective-permute-start(f32[2,128,128]{2,1,0:T(8,128)S(1)} %get-tuple-element.137), channel_id=1, source_target_pairs={{0,8},{4,12},{8,16},{12,20},{16,24},{20,28},{1,9},{5,13},{9,17},{1... | collective-permute-start | bytes 393224 | tf_op jit(solution)/shard_map/ppermute | solution.py:184
  38.3 6.9 %collective-permute-start.7 = (f32[2,128,128]{2,1,0:T(8,128)S(1)}, f32[2,128,128]{2,1,0:T(8,128)S(1)}, u32[]{:S(2)}, u32[]{:S(2)}) collective-permute-start(f32[2,128,128]{2,1,0:T(8,128)S(1)} %get-tuple-element.138), channel_id=1, source_target_pairs={{0,8},{4,12},{8,16},{12,20},{16,24},{20,28},{1,9},{5,13},{9,17},{1... | collective-permute-start | bytes 393224 | tf_op jit(solution)/shard_map/ppermute | solution.py:184
  42.7 5.0 %collective-permute-start.8 = (f32[2,128,128]{2,1,0:T(8,128)S(1)}, f32[2,128,128]{2,1,0:T(8,128)S(1)}, u32[]{:S(2)}, u32[]{:S(2)}) collective-permute-start(f32[2,128,128]{2,1,0:T(8,128)S(1)} %get-tuple-element.140), channel_id=1, source_target_pairs={{0,4},{4,0},{8,12},{12,8},{16,20},{20,16},{24,28},{28,24},{1,5},{5... | collective-permute-start | bytes 393224 | tf_op jit(solution)/shard_map/ppermute | solution.py:246
  48.3 6.0 %collective-permute-start.9 = (f32[2,128,128]{2,1,0:T(8,128)S(1)}, f32[2,128,128]{2,1,0:T(8,128)S(1)}, u32[]{:S(2)}, u32[]{:S(2)}) collective-permute-start(f32[2,128,128]{2,1,0:T(8,128)S(1)} %get-tuple-element.141), channel_id=1, source_target_pairs={{0,8},{4,12},{8,16},{12,20},{16,24},{20,28},{1,9},{5,13},{9,17},{1... | collective-permute-start | bytes 393224 | tf_op jit(solution)/shard_map/ppermute | solution.py:184
  51.8 5.3 %collective-permute-start.10 = (f32[2,128,128]{2,1,0:T(8,128)S(1)}, f32[2,128,128]{2,1,0:T(8,128)S(1)}, u32[]{:S(2)}, u32[]{:S(2)}) collective-permute-start(f32[2,128,128]{2,1,0:T(8,128)S(1)} %get-tuple-element.142), channel_id=1, source_target_pairs={{0,4},{4,0},{8,12},{12,8},{16,20},{20,16},{24,28},{28,24},{1,5},{5... | collective-permute-start | bytes 393224 | tf_op jit(solution)/shard_map/ppermute | solution.py:246
  57.7 7.1 %collective-permute-start.11 = (f32[2,128,128]{2,1,0:T(8,128)S(1)}, f32[2,128,128]{2,1,0:T(8,128)S(1)}, u32[]{:S(2)}, u32[]{:S(2)}) collective-permute-start(f32[2,128,128]{2,1,0:T(8,128)S(1)} %get-tuple-element.143), channel_id=1, source_target_pairs={{0,8},{4,12},{8,16},{12,20},{16,24},{20,28},{1,9},{5,13},{9,17},{1... | collective-permute-start | bytes 393224 | tf_op jit(solution)/shard_map/ppermute | solution.py:184
  62.3 5.0 %collective-permute-start.12 = (f32[2,128,128]{2,1,0:T(8,128)S(1)}, f32[2,128,128]{2,1,0:T(8,128)S(1)}, u32[]{:S(2)}, u32[]{:S(2)}) collective-permute-start(f32[2,128,128]{2,1,0:T(8,128)S(1)} %get-tuple-element.144), channel_id=1, source_target_pairs={{0,4},{4,0},{8,12},{12,8},{16,20},{20,16},{24,28},{28,24},{1,5},{5... | collective-permute-start | bytes 393224 | tf_op jit(solution)/shard_map/ppermute | solution.py:246
  67.9 7.5 %collective-permute-start.13 = (f32[2,128,128]{2,1,0:T(8,128)S(1)}, f32[2,128,128]{2,1,0:T(8,128)S(1)}, u32[]{:S(2)}, u32[]{:S(2)}) collective-permute-start(f32[2,128,128]{2,1,0:T(8,128)S(1)} %get-tuple-element.146), channel_id=1, source_target_pairs={{0,4},{4,0},{8,12},{12,8},{16,20},{20,16},{24,28},{28,24},{1,5},{5... | collective-permute-start | bytes 393224 | tf_op jit(solution)/shard_map/ppermute | solution.py:246
  76.0 5.5 %copy-start.16 = (f32[256,256]{1,0:T(8,128)}, f32[256,256]{1,0:T(8,128)S(1)}, u32[]{:S(2)}) copy-start(f32[256,256]{1,0:T(8,128)S(1)} %get-tuple-element.160.refs_7_) | copy-start | bytes 786436
  76.0 1.7 %collective-permute-start.16 = (f32[2,256]{1,0:T(2,128)S(1)}, f32[2,256]{1,0:T(2,128)S(1)}, u32[]{:S(2)}, u32[]{:S(2)}) collective-permute-start(f32[2,256]{1,0:T(2,128)S(1)} %get-tuple-element.156.refs_0_), channel_id=1, source_target_pairs={{0,3},{1,0},{2,1},{3,2},{4,7},{5,4},{6,5},{7,6},{8,11},{9,8},{10,9... | collective-permute-start | bytes 6152 | tf_op jit(solution)/shard_map/ppermute | solution.py:337
  76.0 3.6 %collective-permute-start.15 = (f32[2,256]{1,0:T(2,128)S(1)}, f32[2,256]{1,0:T(2,128)S(1)}, u32[]{:S(2)}, u32[]{:S(2)}) collective-permute-start(f32[2,256]{1,0:T(2,128)S(1)} %get-tuple-element.156.refs_0_), channel_id=1, source_target_pairs={{0,2},{1,3},{2,0},{3,1},{4,6},{5,7},{6,4},{7,5},{8,10},{9,11},{10,... | collective-permute-start | bytes 6152 | tf_op jit(solution)/shard_map/ppermute | solution.py:337
  77.5 3.0 %collective-permute-start.14 = (f32[2,256]{1,0:T(2,128)S(1)}, f32[2,256]{1,0:T(2,128)S(1)}, u32[]{:S(2)}, u32[]{:S(2)}) collective-permute-start(f32[2,256]{1,0:T(2,128)S(1)} %get-tuple-element.156.refs_0_), channel_id=1, source_target_pairs={{0,1},{1,2},{2,3},{3,0},{4,5},{5,6},{6,7},{7,4},{8,9},{9,10},{10,1... | collective-permute-start | bytes 6152 | tf_op jit(solution)/shard_map/ppermute | solution.py:337
  81.4 7.4 %collective-permute-start.20 = (f32[2,128,128]{2,1,0:T(8,128)}, f32[2,128,128]{2,1,0:T(8,128)S(1)}, u32[]{:S(2)}, u32[]{:S(2)}) collective-permute-start(f32[2,128,128]{2,1,0:T(8,128)} %get-tuple-element.176), channel_id=1, source_target_pairs={{0,4},{4,0},{8,12},{12,8},{16,20},{20,16},{24,28},{28,24},{1,5},{5... | collective-permute-start | bytes 393224 | tf_op jit(solution)/shard_map/ppermute | solution.py:201
  83.2 2.1 %copy-start.17 = (f32[256,256]{1,0:T(8,128)S(1)}, f32[256,256]{1,0:T(8,128)}, u32[]{:S(2)}) copy-start(f32[256,256]{1,0:T(8,128)} %copy-done.16) | copy-start | bytes 786436
  83.3 15.8 %copy-start.27 = (bf16[2,128,128]{2,1,0:T(8,128)(2,1)S(1)}, bf16[2,128,128]{2,1,0:T(8,128)(2,1)}, u32[]{:S(2)}) copy-start(bf16[2,128,128]{2,1,0:T(8,128)(2,1)} %copy-done.26) | copy-start | bytes 196612
  83.3 15.8 %copy-start.29 = (bf16[2,128,128]{2,1,0:T(8,128)(2,1)S(1)}, bf16[2,128,128]{2,1,0:T(8,128)(2,1)}, u32[]{:S(2)}) copy-start(bf16[2,128,128]{2,1,0:T(8,128)(2,1)} %copy-done.28) | copy-start | bytes 196612
  83.8 15.3 %copy-start.3 = (bf16[256,2048]{1,0:T(8,128)(2,1)S(1)}, bf16[256,2048]{1,0:T(8,128)(2,1)}, u32[]{:S(2)}) copy-start(bf16[256,2048]{1,0:T(8,128)(2,1)} %v.9) | copy-start | bytes 3145732
  83.8 15.2 %copy-start.7 = (bf16[16,256,256]{2,1,0:T(8,128)(2,1)S(1)}, bf16[16,256,256]{2,1,0:T(8,128)(2,1)}, u32[]{:S(2)}) copy-start(bf16[16,256,256]{2,1,0:T(8,128)(2,1)} %copy-done.6) | copy-start | bytes 6291460
  83.8 7.8 %collective-permute-start.19 = (f32[2,128,128]{2,1,0:T(8,128)S(1)}, f32[2,128,128]{2,1,0:T(8,128)S(1)}, u32[]{:S(2)}, u32[]{:S(2)}) collective-permute-start(f32[2,128,128]{2,1,0:T(8,128)S(1)} %get-tuple-element.173), channel_id=1, source_target_pairs={{0,4},{4,0},{8,12},{12,8},{16,20},{20,16},{24,28},{28,24},{1,5},{5... | collective-permute-start | bytes 393224 | tf_op jit(solution)/shard_map/ppermute | solution.py:201
  89.4 6.9 %collective-permute-start.21 = (f32[2,128,128]{2,1,0:T(8,128)S(1)}, f32[2,128,128]{2,1,0:T(8,128)S(1)}, u32[]{:S(2)}, u32[]{:S(2)}) collective-permute-start(f32[2,128,128]{2,1,0:T(8,128)S(1)} %get-tuple-element.178), channel_id=1, source_target_pairs={{28,20},{24,16},{20,12},{16,8},{12,4},{8,0},{29,21},{25,17},{21,13... | collective-permute-start | bytes 393224 | tf_op jit(solution)/shard_map/ppermute | solution.py:184
  90.7 9.7 %collective-permute-start.18 = (f32[2,128,128]{2,1,0:T(8,128)S(1)}, f32[2,128,128]{2,1,0:T(8,128)S(1)}, u32[]{:S(2)}, u32[]{:S(2)}) collective-permute-start(f32[2,128,128]{2,1,0:T(8,128)S(1)} %get-tuple-element.171), channel_id=1, source_target_pairs={{0,4},{4,0},{8,12},{12,8},{16,20},{20,16},{24,28},{28,24},{1,5},{5... | collective-permute-start | bytes 393224 | tf_op jit(solution)/shard_map/ppermute | solution.py:201
  96.9 6.9 %collective-permute-start.22 = (f32[2,128,128]{2,1,0:T(8,128)S(1)}, f32[2,128,128]{2,1,0:T(8,128)S(1)}, u32[]{:S(2)}, u32[]{:S(2)}) collective-permute-start(f32[2,128,128]{2,1,0:T(8,128)S(1)} %get-tuple-element.180.refs_12_), channel_id=1, source_target_pairs={{28,20},{24,16},{20,12},{16,8},{12,4},{8,0},{29,21},{25,17},{21,13... | collective-permute-start | bytes 393224 | tf_op jit(solution)/shard_map/ppermute | solution.py:184
  98.2 8.9 %collective-permute-start.17 = (f32[2,128,128]{2,1,0:T(8,128)S(1)}, f32[2,128,128]{2,1,0:T(8,128)S(1)}, u32[]{:S(2)}, u32[]{:S(2)}) collective-permute-start(f32[2,128,128]{2,1,0:T(8,128)S(1)} %get-tuple-element.169), channel_id=1, source_target_pairs={{0,4},{4,0},{8,12},{12,8},{16,20},{20,16},{24,28},{28,24},{1,5},{5... | collective-permute-start | bytes 393224 | tf_op jit(solution)/shard_map/ppermute | solution.py:201
  99.0 6.6 %copy-start.23 = (bf16[2,128,128]{2,1,0:T(8,128)(2,1)S(1)}, bf16[2,128,128]{2,1,0:T(8,128)(2,1)}, u32[]{:S(2)}) copy-start(bf16[2,128,128]{2,1,0:T(8,128)(2,1)} %copy-done.22) | copy-start | bytes 196612
  99.0 6.6 %copy-start.25 = (bf16[2,128,128]{2,1,0:T(8,128)(2,1)S(1)}, bf16[2,128,128]{2,1,0:T(8,128)(2,1)}, u32[]{:S(2)}) copy-start(bf16[2,128,128]{2,1,0:T(8,128)(2,1)} %copy-done.24) | copy-start | bytes 196612
  104.3 6.9 %collective-permute-start.23 = (f32[2,128,128]{2,1,0:T(8,128)S(1)}, f32[2,128,128]{2,1,0:T(8,128)S(1)}, u32[]{:S(2)}, u32[]{:S(2)}) collective-permute-start(f32[2,128,128]{2,1,0:T(8,128)S(1)} %get-tuple-element.187.refs_12_), channel_id=1, source_target_pairs={{28,20},{24,16},{20,12},{16,8},{12,4},{8,0},{29,21},{25,17},{21,13... | collective-permute-start | bytes 393224 | tf_op jit(solution)/shard_map/ppermute | solution.py:184
  105.6 8.3 %copy-start.19 = (bf16[2,128,128]{2,1,0:T(8,128)(2,1)S(1)}, bf16[2,128,128]{2,1,0:T(8,128)(2,1)}, u32[]{:S(2)}) copy-start(bf16[2,128,128]{2,1,0:T(8,128)(2,1)} %copy-done.18) | copy-start | bytes 196612
  105.6 8.3 %copy-start.21 = (bf16[2,128,128]{2,1,0:T(8,128)(2,1)S(1)}, bf16[2,128,128]{2,1,0:T(8,128)(2,1)}, u32[]{:S(2)}) copy-start(bf16[2,128,128]{2,1,0:T(8,128)(2,1)} %copy-done.20) | copy-start | bytes 196612
  111.8 6.2 %collective-permute-start.25 = (f32[2,128,128]{2,1,0:T(8,128)S(1)}, f32[2,128,128]{2,1,0:T(8,128)S(1)}, u32[]{:S(2)}, u32[]{:S(2)}) collective-permute-start(f32[2,128,128]{2,1,0:T(8,128)S(1)} %get-tuple-element.200), channel_id=1, source_target_pairs={{0,4},{4,0},{8,12},{12,8},{16,20},{20,16},{24,28},{28,24},{1,5},{5... | collective-permute-start | bytes 393224 | tf_op jit(solution)/shard_map/ppermute | solution.py:246
  112.6 7.8 %collective-permute-start.24 = (f32[2,128,128]{2,1,0:T(8,128)S(1)}, f32[2,128,128]{2,1,0:T(8,128)S(1)}, u32[]{:S(2)}, u32[]{:S(2)}) collective-permute-start(f32[2,128,128]{2,1,0:T(8,128)S(1)} %get-tuple-element.194.refs_12_), channel_id=1, source_target_pairs={{28,20},{24,16},{20,12},{16,8},{12,4},{8,0},{29,21},{25,17},{21,13... | collective-permute-start | bytes 393224 | tf_op jit(solution)/shard_map/ppermute | solution.py:184
  121.0 5.9 %collective-permute-start.27 = (f32[2,128,128]{2,1,0:T(8,128)S(1)}, f32[2,128,128]{2,1,0:T(8,128)S(1)}, u32[]{:S(2)}, u32[]{:S(2)}) collective-permute-start(f32[2,128,128]{2,1,0:T(8,128)S(1)} %get-tuple-element.208), channel_id=1, source_target_pairs={{0,4},{4,0},{8,12},{12,8},{16,20},{20,16},{24,28},{28,24},{1,5},{5... | collective-permute-start | bytes 393224 | tf_op jit(solution)/shard_map/ppermute | solution.py:246
  122.7 6.8 %collective-permute-start.26 = (f32[2,128,128]{2,1,0:T(8,128)S(1)}, f32[2,128,128]{2,1,0:T(8,128)S(1)}, u32[]{:S(2)}, u32[]{:S(2)}) collective-permute-start(f32[2,128,128]{2,1,0:T(8,128)S(1)} %get-tuple-element.201.refs_12_), channel_id=1, source_target_pairs={{28,20},{24,16},{20,12},{16,8},{12,4},{8,0},{29,21},{25,17},{21,13... | collective-permute-start | bytes 393224 | tf_op jit(solution)/shard_map/ppermute | solution.py:184
  130.1 6.9 %collective-permute-start.28 = (f32[2,128,128]{2,1,0:T(8,128)S(1)}, f32[2,128,128]{2,1,0:T(8,128)S(1)}, u32[]{:S(2)}, u32[]{:S(2)}) collective-permute-start(f32[2,128,128]{2,1,0:T(8,128)S(1)} %get-tuple-element.209), channel_id=1, source_target_pairs={{28,20},{24,16},{20,12},{16,8},{12,4},{8,0},{29,21},{25,17},{21,13... | collective-permute-start | bytes 393224 | tf_op jit(solution)/shard_map/ppermute | solution.py:184
  131.4 5.6 %collective-permute-start.29 = (f32[2,128,128]{2,1,0:T(8,128)S(1)}, f32[2,128,128]{2,1,0:T(8,128)S(1)}, u32[]{:S(2)}, u32[]{:S(2)}) collective-permute-start(f32[2,128,128]{2,1,0:T(8,128)S(1)} %get-tuple-element.210), channel_id=1, source_target_pairs={{0,4},{4,0},{8,12},{12,8},{16,20},{20,16},{24,28},{28,24},{1,5},{5... | collective-permute-start | bytes 393224 | tf_op jit(solution)/shard_map/ppermute | solution.py:246
  137.6 5.0 %collective-permute-start.30 = (f32[2,128,128]{2,1,0:T(8,128)S(1)}, f32[2,128,128]{2,1,0:T(8,128)S(1)}, u32[]{:S(2)}, u32[]{:S(2)}) collective-permute-start(f32[2,128,128]{2,1,0:T(8,128)S(1)} %get-tuple-element.212), channel_id=1, source_target_pairs={{0,4},{4,0},{8,12},{12,8},{16,20},{20,16},{24,28},{28,24},{1,5},{5... | collective-permute-start | bytes 393224 | tf_op jit(solution)/shard_map/ppermute | solution.py:246
  (16 other events, 13.8 us)

commit v3 on v1

--- a/solution.py
+++ b/solution.py
@@ -33,19 +33,19 @@
     return jnp.where(mask, scores, 0.0).astype(BF16)
 
 
-def call(body, place, ins, outs, grid=(1,), aliases=None, flops=0):
+def call(body, place, ins, outs, grid=(1,), aliases=None, flops=0, grant=6):
     size = sum(a.size * a.dtype.itemsize // 2 for a, _, _ in ins)
     return pl.pallas_call(
         body,
         grid_spec=pltpu.PrefetchScalarGridSpec(
             num_scalar_prefetch=1,
             grid=grid,
-            in_specs=[pl.BlockSpec(b, m) for _, b, m in ins],
+            in_specs=[pl.BlockSpec(b, m) if b else pl.BlockSpec(memory_space=pl.ANY) for _, b, m in ins],
             out_specs=[pl.BlockSpec(b, m) for _, _, b, m in outs],
         ),
         out_shape=[jax.ShapeDtypeStruct(s, d) for s, d, _, _ in outs],
         input_output_aliases=aliases or {},
-        compiler_params=pltpu.CompilerParams(vmem_limit_bytes=24 * 1024 * 1024),
+        compiler_params=pltpu.CompilerParams(vmem_limit_bytes=grant * 1024 * 1024),
         cost_estimate=pl.CostEstimate(flops=flops, bytes_accessed=size, transcendentals=0),
     )(place, *[a for a, _, _ in ins])
 
@@ -57,7 +57,14 @@
             out[j] = dot(head(a, h), head(b, h), 0, 0)
 
 
-def local_body(heads, place, q, k, v, scores, attn):
+def local_body(per, chunks, heads, place, q, k, v, *refs):
+    outs, scores, attn = refs[:chunks], refs[chunks], refs[chunks + 1]
+    for turn in range(2):
+        @pl.when(pl.program_id(0) == turn)
+        def _():
+            for j in range(heads):
+                h = turn * heads + j
+                outs[h // per][h % per] = dot(head(k, j), head(v, j), 0, 0)
     mask = causal()
     for j in range(heads):
         s = masked(dot(head(q, j), head(k, j), 1, 1), mask)
@@ -96,8 +103,8 @@
 def delta_body(per, chunks, parts, features, place, *refs):
     stats = refs[:parts]
     attn = refs[parts:parts + chunks]
-    q, g, n, d = refs[parts + chunks:parts + chunks + 4]
-    outs = refs[parts + chunks + 4:]
+    q, g, n = refs[parts + chunks:parts + chunks + 3]
+    outs = refs[parts + chunks + 3:]
     total = stats[0][...]
     for s in stats[1:]:
         total = total + s[...]
@@ -110,11 +117,11 @@
             h = c * per + j
             scaled = head(n, h).astype(F32) * head(g, h).astype(F32)
             x = (inverse * scaled - head(attn[c], j) * slope).astype(BF16)
-            d[:, h * DH:(h + 1) * DH] = x
-            outs[c][j] = dot(head(q, h), x, 0, 0)
-
-
-def grads_body(per, aliased, place, *refs):
+            outs[c][:, j * DH:(j + 1) * DH] = x
+            outs[chunks + c][j] = dot(head(q, h), x, 0, 0)
+
+
+def grads_body(per, place, *refs):
     (q_k, q_o, k_k, k_o, v_k, v_o, s_k, s_o, d_k, d_o, sb_k, sb_o) = refs[:12]
     qg_k, qg_o, kg_k, kg_o, vg_k, vg_o = refs[12:]
     mask = causal()
@@ -148,29 +155,54 @@
             pairs = [(count - 1 - a, count - 1 - b) for a, b in pairs]
         return lax.ppermute(array, "seq", pairs)
 
-    def along(part, reverse):
-        if long <= 4:
-            carry, send = None, part
-            for z in range(long - 1):
-                got = hop(send, lambda at: at == z, 1, reverse)
-                carry = got if carry is None else carry + got
-                send = carry + part
-            return jnp.zeros_like(part) if carry is None else carry
-        carry = hop(part, lambda at: True, 1, reverse)
-        far = 1
-        while far < long:
-            carry = carry + hop(carry, lambda at: True, far, reverse)
-            far *= 2
-        return carry
-
-    def scan(kept, sent, leads, reverse):
+    def shift(array, far, reverse):
+        return hop(array, lambda at: True, far, reverse)
+
+    def doubling(parts, reverse):
         out = []
-        for a, b in zip(kept, sent):
-            r = lax.ppermute(b, "seq", swap)
-            e = along(a + r, reverse)
-            other = lax.ppermute(jnp.where(leads, e + a, e), "seq", swap)
-            out.append((e, r, other))
+        for part in parts:
+            carry = shift(part, 1, reverse)
+            far = 1
+            while far < long:
+                carry = carry + shift(carry, far, reverse)
+                far *= 2
+            out.append(carry)
         return out
+
+    def scan(kept, sent, y, reverse, beside):
+        swapped = [lax.ppermute(b, "seq", swap) for b in sent]
+        if long > 4 or long < 2:
+            sums = [a + r for a, r in zip(kept, swapped)]
+            sums = doubling(sums, reverse) if long > 1 else [jnp.zeros_like(a) for a in sums]
+            others = [
+                lax.ppermute(jnp.where(y == 0, e + a, e), "seq", swap) for a, e in zip(kept, sums)
+            ]
+            return list(zip(sums, swapped, others)), [work() for work in beside]
+        chunks = len(kept)
+        order = sorted((2 * stage + c, -stage, c, stage) for stage in range(long) for c in range(chunks))
+        part, flight, carry, out, done = {}, dict(enumerate(swapped)), {}, {}, []
+        last = []
+        for turn, (_, _, c, stage) in enumerate(order):
+            if turn in (0, 3) and len(done) < len(beside):
+                done.append(beside[len(done)]())
+                last.append(done[-1][0])
+            got = flight[c]
+            if last:
+                got, *_ = lax.optimization_barrier((got, *last))
+            if stage == 0:
+                swapped[c] = got
+                part[c] = send = kept[c] + got
+            else:
+                carry[c] = got if stage == 1 else carry[c] + got
+                send = carry[c] + part[c]
+            if stage < long - 1:
+                flight[c] = hop(send, lambda at: at == stage, 1, reverse)
+                last = [send]
+            else:
+                send = jnp.where(y == 0, carry[c] + kept[c], carry[c])
+                out[c] = (carry[c], swapped[c], lax.ppermute(send, "seq", swap))
+                last = [send]
+        return [out[c] for c in range(chunks)], done + [work() for work in beside[len(done):]]
 
     def shards(queries, keys, values, out_grad, norm_gain):
         tokens, width = queries.shape
@@ -179,7 +211,8 @@
         per = half // CHUNKS
         wide = half * DH
         narrow = per * DH
-        y = lax.axis_index("seq") % 2
+        at_seq = lax.axis_index("seq")
+        y = at_seq % 2
         place = y.astype(jnp.int32).reshape(1)
         turned = 1 - place
         gain = norm_gain.reshape(1, width)
@@ -202,29 +235,26 @@
         def at_o3(c):
             return lambda i, s: ((1 - s[0]) * CHUNKS + c, 0, 0)
 
-        def states(a, b, index):
-            return call(
-                functools.partial(states_body, per), place,
-                [(a, (tokens, wide), index), (b, (tokens, wide), index)],
-                [((per, DH, DH), F32, (per, DH, DH), whole3)] * CHUNKS,
-                flops=half * mac * DH,
-            )
-
-        sent = states(keys, values, sent_half)
-        kept = states(keys, values, kept_half)
-
-        group = 4
-        scores, attn_local = call(
-            functools.partial(local_body, group), place,
-            [(a, (tokens, group * DH), lambda i, s: (0, i)) for a in (queries, keys, values)],
-            [
-                ((heads, GROUP, GROUP), BF16, (group, GROUP, GROUP), lambda i, s: (i, 0, 0)),
-                ((tokens, width), F32, (tokens, group * DH), lambda i, s: (0, i)),
+        sent = call(
+            functools.partial(states_body, per), place,
+            [(a, (tokens, wide), sent_half) for a in (keys, values)],
+            [((per, DH, DH), F32, (per, DH, DH), whole3)] * CHUNKS,
+            flops=half * mac * DH,
+        )
+
+        group = half // 2
+        strip = lambda i, s: (0, (2 * s[0] + i) % 4)
+        *kept, scores, attn_local = call(
+            functools.partial(local_body, per, CHUNKS, group), place,
+            [(a, (tokens, group * DH), strip) for a in (queries, keys, values)],
+            [((per, DH, DH), F32, (per, DH, DH), whole3)] * CHUNKS + [
+                ((heads, GROUP, GROUP), BF16, (group, GROUP, GROUP), lambda i, s: ((2 * s[0] + i) % 4, 0, 0)),
+                ((tokens, width), F32, (tokens, group * DH), strip),
             ],
-            grid=(heads // group,), flops=2 * heads * mac * GROUP,
+            grid=(4,), flops=heads * mac * (2 * GROUP + DH // 2),
         )
 
-        before = scan(kept, sent, y == 0, False)
+        before, _ = scan(kept, sent, y, False, [])
 
         block = (tokens, narrow)
         square = cross = None
@@ -254,37 +284,39 @@
                 square, cross = stats
 
         sums = [mine]
+        paired = parts & (parts - 1) == 0
         for step in range(1, parts):
-            sums.append(lax.ppermute(mine, "head", [(i, (i + step) % parts) for i in range(parts)]))
+            sums.append(lax.ppermute(
+                mine, "head", [(i, i ^ step if paired else (i + step) % parts) for i in range(parts)]))
 
         def delta(which, index):
             ins = [(a, (2, GROUP), whole2) for a in sums]
             ins += [(attns[c][which], block, whole2) for c in range(CHUNKS)]
             ins += [(queries, (tokens, wide), index), (out_grad, (tokens, wide), index), (gain, (1, wide), index)]
-            outs = [((tokens, wide), BF16, (tokens, wide), whole2)]
+            outs = [(block, BF16, block, whole2)] * CHUNKS
             outs += [((per, DH, DH), F32, (per, DH, DH), whole3)] * CHUNKS
-            d, *g = call(
-                functools.partial(delta_body, per, CHUNKS, parts, float(parts * width)), place, ins, outs,
+            result = call(
+                functools.partial(delta_body, per, CHUNKS, parts, float(parts * heads * DH)), place, ins, outs,
                 flops=half * mac * DH)
-            return d, g
+            return result[:CHUNKS], result[CHUNKS:]
 
         d_o, sent = delta(1, sent_half)
         d_k, kept = delta(0, kept_half)
-        after = scan(kept, sent, y == 1, True)
-
-        grads = []
-        for c in range(CHUNKS):
+
+        def grads(c):
             ins = []
             for a in (queries, keys, values):
                 ins += [(a, block, at_k(c)), (a, block, at_o(c))]
             ins += [(scores, (per, GROUP, GROUP), at_k3(c)), (scores, (per, GROUP, GROUP), at_o3(c))]
-            here = lambda i, s, c=c: (0, c)
-            ins += [(d_k, block, here), (d_o, block, here)]
+            ins += [(d_k[c], block, whole2), (d_o[c], block, whole2)]
             ins += [(a, (per, DH, DH), whole3) for a in priors[c]]
             outs = [(block, BF16, block, whole2)] * 2 + [(block, F32, block, whole2)] * 4
-            grads.append(call(
-                functools.partial(grads_body, per, c > 0), place, ins, outs,
-                flops=2 * per * mac * (4 * GROUP + DH)))
+            return call(
+                functools.partial(grads_body, per), place, ins, outs,
+                flops=2 * per * mac * (4 * GROUP + DH))
+
+        after, grads = scan(
+            kept, sent, 1 - y, True, [functools.partial(grads, c) for c in range(CHUNKS)])
 
         kg = vg = qg = None
         for c in range(CHUNKS):
@@ -305,7 +337,7 @@
         if done[0] is not None:
             for n, a in enumerate(done):
                 aliases[len(ins) + 1] = n
-                ins.append((a, (8, 128), whole2))
+                ins.append((a, None, None))
         outs = [((tokens, width), BF16, block, mine)] * 3
 
         def body(place, qk, qo, kk, ko, vk, vo, k, v, e, r, other, *refs):

time: 112 us -> 124 us (1.11)
  local copies, waits for them, and re-layouts: 7.79 us -> 21.5 us
  waiting for transfers between devices: 19.7 us -> 17.2 us
    unnamed x110 -> x142, local copies, waits for them, and re-layouts: 7.78 us -> 21.5 us
    ppermute x19, waiting for transfers between devices: 11.8 us -> 5.77 us  [the longest x8 3.99 us: scan(): out[c] = (carry[c], swapped[c], lax.ppermute(send, 'seq', swap))]
    ppermute x24, waiting for transfers between devices: 7.84 us -> 11.4 us  [hop(): return lax.ppermute(array, 'seq', pairs)]
    pallas_call x17 -> x16, Pallas kernels: 19.5 us -> 20.1 us  [call(): pl.pallas_call(body, grid_spec=pltpu.PrefetchScalarGridSpec(num_scalar_pr...]
  transfers between devices with their start and end apart: 43 -> 43, of which waited for: 13 -> 10; matrix products, arithmetic and copies ran while one was open for 11% -> 10% of each run, Pallas kernels for 14% -> 13%
where the time goes in v3:
time: 124 us; the launch traced here: 123 us
  starting transfers between devices  50.3 us (41%)
  local copies, waits for them, and re-layouts  21.5 us (17%)
  Pallas kernels  20.1 us (16%)
  waiting for transfers between devices  17.2 us (14%)
  other arithmetic  12 us (10%)
  between operations  1.7 us (1%)
    ppermute x24, starting transfers between devices, hop(): return lax.ppermute(array, 'seq', pairs)  29.4 us
    unnamed x142, local copies, waits for them, and re-layouts  21.5 us
    pallas_call x16, Pallas kernels, call(): pl.pallas_call(body, grid_spec=pltpu.PrefetchScalarGridSpec(num_scalar_pr...  20.1 us
    ppermute x24, waiting for transfers between devices, hop(): return lax.ppermute(array, 'seq', pairs)  11.4 us
    ppermute x8, starting transfers between devices, scan(): out[c] = (carry[c], swapped[c], lax.ppermute(send, 'seq', swap))  9.77 us
    ppermute x8, starting transfers between devices, scan(): swapped = [lax.ppermute(b, 'seq', swap) for b in sent]  9.21 us
    add x16, other arithmetic, scan(): send = carry[c] + part[c]  7.52 us
    add x8, other arithmetic, scan(): part[c] = send = kept[c] + got  4.23 us
  transfers between devices with their start and end apart: 43, of which 10 were waited for; matrix products, arithmetic and copies ran while one was open for 10% of the time, Pallas kernels for 13%

profile of v3, /device:TPU:0, one launch (start us, length us, event | category | flops | bytes accessed | tf_op | source)
XLA Modules:
  0.0 122.7 jit_solution(5083498280732172738)
XLA Ops:
  0.7 1.3 %copy-done.1 = bf16[256,2048]{1,0:T(8,128)(2,1)S(1)} copy-done((bf16[256,2048]{1,0:T(8,128)(2,1)S(1)}, bf16[256,2048]{1,0:T(8,128)(2,1)}, u32[]{:S(2)}) %copy-start.1) | copy-done | bytes 1048600
  2.0 1.2 copy-done.3
  3.2 1.0 shard_map.77
  4.2 3.0 %collective-permute-start.2 = (f32[2,128,128]{2,1,0:T(8,128)S(1)}, f32[2,128,128]{2,1,0:T(8,128)S(1)}, u32[]{:S(2)}, u32[]{:S(2)}) collective-permute-start(f32[2,128,128]{2,1,0:T(8,128)S(1)} %get-tuple-element.126), channel_id=1, source_target_pairs={{0,4},{4,0},{8,12},{12,8},{16,20},{20,16},{24,28},{28,24},{1,5},{5... | collective-permute-start | bytes 393224 | tf_op jit(solution)/shard_map/ppermute | solution.py:173
  7.2 3.8 %shard_map.76 = (f32[2,128,128]{2,1,0:T(8,128)S(1)}, f32[2,128,128]{2,1,0:T(8,128)S(1)}, f32[2,128,128]{2,1,0:T(8,128)S(1)}, f32[2,128,128]{2,1,0:T(8,128)S(1)},...) custom-call(s32[1]{0:T(128)} %bitcast.place, bf16[256,2048]{1,0:T(8,128)(2,1)S(1)} %copy-done, ...), custom_call_target="tpu_custom_call" | custom-call | flops 603979776 | bytes 1572864 | tf_op jit(solution)/shard_map/pallas_call | solution.py:38
  11.1 1.3 %copy-done.5 = bf16[16,256,256]{2,1,0:T(8,128)(2,1)} copy-done((bf16[16,256,256]{2,1,0:T(8,128)(2,1)}, bf16[16,256,256]{2,1,0:T(8,128)(2,1)S(1)}, u32[]{:S(2)}) %copy-start.5) | copy-done | bytes 2097176
  13.7 4.0 %collective-permute-start.5 = (f32[2,128,128]{2,1,0:T(8,128)S(1)}, f32[2,128,128]{2,1,0:T(8,128)S(1)}, u32[]{:S(2)}, u32[]{:S(2)}) collective-permute-start(f32[2,128,128]{2,1,0:T(8,128)S(1)} %add.149), channel_id=1, source_target_pairs={{0,8},{4,12},{1,9},{5,13},{2,10},{6,14},{3,11},{7,15}} | collective-permute-start | bytes 393224 | tf_op jit(solution)/shard_map/ppermute | solution.py:156
  17.7 1.6 %collective-permute-start.4 = (f32[2,128,128]{2,1,0:T(8,128)}, f32[2,128,128]{2,1,0:T(8,128)S(1)}, u32[]{:S(2)}, u32[]{:S(2)}) collective-permute-start(f32[2,128,128]{2,1,0:T(8,128)} %get-tuple-element.129), channel_id=1, source_target_pairs={{0,4},{4,0},{8,12},{12,8},{16,20},{20,16},{24,28},{28,24},{1,5},{5... | collective-permute-start | bytes 393224 | tf_op jit(solution)/shard_map/ppermute | solution.py:173
  20.0 1.9 %collective-permute-start.3 = (f32[2,128,128]{2,1,0:T(8,128)}, f32[2,128,128]{2,1,0:T(8,128)}, u32[]{:S(2)}, u32[]{:S(2)}) collective-permute-start(f32[2,128,128]{2,1,0:T(8,128)} %add.150), channel_id=1, source_target_pairs={{0,8},{4,12},{1,9},{5,13},{2,10},{6,14},{3,11},{7,15}} | collective-permute-start | bytes 393224 | tf_op jit(solution)/shard_map/ppermute | solution.py:156
  23.1 1.3 %collective-permute-start.9 = (f32[2,128,128]{2,1,0:T(8,128)}, f32[2,128,128]{2,1,0:T(8,128)}, u32[]{:S(2)}, u32[]{:S(2)}) collective-permute-start(f32[2,128,128]{2,1,0:T(8,128)} %add.151), channel_id=1, source_target_pairs={{8,16},{12,20},{9,17},{13,21},{10,18},{14,22},{11,19},{15,23}} | collective-permute-start | bytes 393224 | tf_op jit(solution)/shard_map/ppermute | solution.py:156
  25.4 3.0 %collective-permute-start.8 = (f32[2,128,128]{2,1,0:T(8,128)S(1)}, f32[2,128,128]{2,1,0:T(8,128)S(1)}, u32[]{:S(2)}, u32[]{:S(2)}) collective-permute-start(f32[2,128,128]{2,1,0:T(8,128)S(1)} %add.152), channel_id=1, source_target_pairs={{0,8},{4,12},{1,9},{5,13},{2,10},{6,14},{3,11},{7,15}} | collective-permute-start | bytes 393224 | tf_op jit(solution)/shard_map/ppermute | solution.py:156
  28.4 1.0 add.153
  31.0 1.9 %collective-permute-start.6 = (f32[2,128,128]{2,1,0:T(8,128)S(1)}, f32[2,128,128]{2,1,0:T(8,128)S(1)}, u32[]{:S(2)}, u32[]{:S(2)}) collective-permute-start(f32[2,128,128]{2,1,0:T(8,128)S(1)} %add.154), channel_id=1, source_target_pairs={{0,8},{4,12},{1,9},{5,13},{2,10},{6,14},{3,11},{7,15}} | collective-permute-start | bytes 393224 | tf_op jit(solution)/shard_map/ppermute | solution.py:156
  33.0 1.1 fusion.7
  35.7 1.0 fusion.6
  38.3 2.2 %collective-permute-start.19 = (f32[2,128,128]{2,1,0:T(8,128)S(1)}, f32[2,128,128]{2,1,0:T(8,128)S(1)}, u32[]{:S(2)}, u32[]{:S(2)}) collective-permute-start(f32[2,128,128]{2,1,0:T(8,128)S(1)} %get-tuple-element.261), channel_id=1, source_target_pairs={{0,4},{4,0},{8,12},{12,8},{16,20},{20,16},{24,28},{28,24},{1,5},{5... | collective-permute-start | bytes 393224 | tf_op jit(solution)/shard_map/ppermute | solution.py:203
  42.1 2.1 %collective-permute-start.17 = (f32[2,128,128]{2,1,0:T(8,128)S(1)}, f32[2,128,128]{2,1,0:T(8,128)S(1)}, u32[]{:S(2)}, u32[]{:S(2)}) collective-permute-start(f32[2,128,128]{2,1,0:T(8,128)S(1)} %get-tuple-element.253), channel_id=1, source_target_pairs={{0,4},{4,0},{8,12},{12,8},{16,20},{20,16},{24,28},{28,24},{1,5},{5... | collective-permute-start | bytes 393224 | tf_op jit(solution)/shard_map/ppermute | solution.py:203
  45.1 2.6 %collective-permute-done.18.other = f32[2,128,128]{2,1,0:T(8,128)S(1)} collective-permute-done((f32[2,128,128]{2,1,0:T(8,128)S(1)}, f32[2,128,128]{2,1,0:T(8,128)S(1)}, u32[]{:S(2)}, u32[]{:S(2)}) %collective-permute-start.18) | collective-permute-done | bytes 131104 | tf_op jit(solution)/shard_map/ppermute | solution.py:203
  52.7 1.5 %collective-permute-start.21 = (f32[2,256]{1,0:T(2,128)S(1)}, f32[2,256]{1,0:T(2,128)S(1)}, u32[]{:S(2)}, u32[]{:S(2)}) collective-permute-start(f32[2,256]{1,0:T(2,128)S(1)} %get-tuple-element.150.refs_0_), channel_id=1, source_target_pairs={{0,2},{1,3},{2,0},{3,1},{4,6},{5,7},{6,4},{7,5},{8,10},{9,11},{10,... | collective-permute-start | bytes 6152 | tf_op jit(solution)/shard_map/ppermute | solution.py:289
  54.6 1.1 collective-permute-done.22.refs_3_
  56.3 1.3 %shard_map.83 = (bf16[256,256]{1,0:T(8,128)(2,1)S(1)}, bf16[256,256]{1,0:T(8,128)(2,1)S(1)}, bf16[256,256]{1,0:T(8,128)(2,1)S(1)}, bf16[256,256]{1,0:T(8,128)(2,...) custom-call(s32[1]{0:T(128)} %bitcast.place, ...), custom_call_target="tpu_custom_call" | custom-call | flops 67108864 | bytes 1579008 | tf_op jit(solution)/shard_map/pallas_call | solution.py:38
  59.6 1.2 collective-permute-start.25
  64.2 1.4 %shard_map.85 = (bf16[256,256]{1,0:T(8,128)(2,1)S(1)}, bf16[256,256]{1,0:T(8,128)(2,1)S(1)}, f32[256,256]{1,0:T(8,128)S(1)}, f32[256,256]{1,0:T(8,128)S(1)}, f32...) custom-call(s32[1]{0:T(128)} %bitcast.place, bf16[256,2048]{1,0:T(8,128)(2,1)S(1)} %copy-done, bf16[256,2048]{1,0:T(8,128)(2,1)S(1)} %copy-done, ...), custom_call_target="tpu_custom_call" | custom-call | flops 301989888 | bytes 5439488 | tf_op jit(solution)/shard_map/pallas_call | solution.py:38
  70.4 1.2 %collective-permute-start.27 = (f32[2,128,128]{2,1,0:T(8,128)}, f32[2,128,128]{2,1,0:T(8,128)}, u32[]{:S(2)}, u32[]{:S(2)}) collective-permute-start(f32[2,128,128]{2,1,0:T(8,128)} %get-tuple-element.183), channel_id=1, source_target_pairs={{0,4},{4,0},{8,12},{12,8},{16,20},{20,16},{24,28},{28,24},{1,5},{5... | collective-permute-start | bytes 393224 | tf_op jit(solution)/shard_map/ppermute | solution.py:173
  72.4 1.3 %collective-permute-start.26 = (f32[2,128,128]{2,1,0:T(8,128)}, f32[2,128,128]{2,1,0:T(8,128)}, u32[]{:S(2)}, u32[]{:S(2)}) collective-permute-start(f32[2,128,128]{2,1,0:T(8,128)} %add.174), channel_id=1, source_target_pairs={{28,20},{24,16},{29,21},{25,17},{30,22},{26,18},{31,23},{27,19}} | collective-permute-start | bytes 393224 | tf_op jit(solution)/shard_map/ppermute | solution.py:156
  75.2 1.3 %collective-permute-start.32 = (f32[2,128,128]{2,1,0:T(8,128)}, f32[2,128,128]{2,1,0:T(8,128)}, u32[]{:S(2)}, u32[]{:S(2)}) collective-permute-start(f32[2,128,128]{2,1,0:T(8,128)} %add.175), channel_id=1, source_target_pairs={{20,12},{16,8},{21,13},{17,9},{22,14},{18,10},{23,15},{19,11}} | collective-permute-start | bytes 393224 | tf_op jit(solution)/shard_map/ppermute | solution.py:156
  76.5 1.6 %copy-done.7 = bf16[16,256,256]{2,1,0:T(8,128)(2,1)S(1)} copy-done((bf16[16,256,256]{2,1,0:T(8,128)(2,1)S(1)}, bf16[16,256,256]{2,1,0:T(8,128)(2,1)}, u32[]{:S(2)}) %copy-start.7) | copy-done | bytes 2097176
  81.6 1.4 %shard_map.86 = (bf16[256,256]{1,0:T(8,128)(2,1)S(1)}, bf16[256,256]{1,0:T(8,128)(2,1)S(1)}, f32[256,256]{1,0:T(8,128)S(1)}, f32[256,256]{1,0:T(8,128)S(1)}, f32...) custom-call(s32[1]{0:T(128)} %bitcast.place, bf16[256,2048]{1,0:T(8,128)(2,1)S(1)} %copy-done, bf16[256,2048]{1,0:T(8,128)(2,1)S(1)} %copy-done, ...), custom_call_target="tpu_custom_call" | custom-call | flops 301989888 | bytes 5439488 | tf_op jit(solution)/shard_map/pallas_call | solution.py:38
  83.0 1.0 add.176
  84.8 1.0 add.177
  88.2 1.3 %collective-permute-start.36 = (f32[2,128,128]{2,1,0:T(8,128)S(1)}, f32[2,128,128]{2,1,0:T(8,128)S(1)}, u32[]{:S(2)}, u32[]{:S(2)}) collective-permute-start(f32[2,128,128]{2,1,0:T(8,128)S(1)} %get-tuple-element.249), channel_id=1, source_target_pairs={{12,4},{8,0},{13,5},{9,1},{14,6},{10,2},{15,7},{11,3}} | collective-permute-start | bytes 393224 | tf_op jit(solution)/shard_map/ppermute | solution.py:156
  90.2 1.0 fusion.2
  91.3 1.4 %collective-permute-start.34 = (f32[2,128,128]{2,1,0:T(8,128)S(1)}, f32[2,128,128]{2,1,0:T(8,128)S(1)}, u32[]{:S(2)}, u32[]{:S(2)}) collective-permute-start(f32[2,128,128]{2,1,0:T(8,128)S(1)} %get-tuple-element.247), channel_id=1, source_target_pairs={{12,4},{8,0},{13,5},{9,1},{14,6},{10,2},{15,7},{11,3}} | collective-permute-start | bytes 393224 | tf_op jit(solution)/shard_map/ppermute | solution.py:156
  93.4 1.6 %collective-permute-done.36 = f32[2,128,128]{2,1,0:T(8,128)S(1)} collective-permute-done((f32[2,128,128]{2,1,0:T(8,128)S(1)}, f32[2,128,128]{2,1,0:T(8,128)S(1)}, u32[]{:S(2)}, u32[]{:S(2)}) %collective-permute-start.36) | collective-permute-done | bytes 131104 | tf_op jit(solution)/shard_map/ppermute | solution.py:156
  95.1 1.2 %collective-permute-start.42 = (f32[2,128,128]{2,1,0:T(8,128)S(1)}, f32[2,128,128]{2,1,0:T(8,128)S(1)}, u32[]{:S(2)}, u32[]{:S(2)}) collective-permute-start(f32[2,128,128]{2,1,0:T(8,128)S(1)} %get-tuple-element.245), channel_id=1, source_target_pairs={{0,4},{4,0},{8,12},{12,8},{16,20},{20,16},{24,28},{28,24},{1,5},{5... | collective-permute-start | bytes 393224 | tf_op jit(solution)/shard_map/ppermute | solution.py:203
  96.4 1.3 %collective-permute-start.38 = (f32[2,128,128]{2,1,0:T(8,128)S(1)}, f32[2,128,128]{2,1,0:T(8,128)S(1)}, u32[]{:S(2)}, u32[]{:S(2)}) collective-permute-start(f32[2,128,128]{2,1,0:T(8,128)S(1)} %get-tuple-element.243), channel_id=1, source_target_pairs={{12,4},{8,0},{13,5},{9,1},{14,6},{10,2},{15,7},{11,3}} | collective-permute-start | bytes 393224 | tf_op jit(solution)/shard_map/ppermute | solution.py:156
  97.7 6.3 %collective-permute-done.34 = f32[2,128,128]{2,1,0:T(8,128)S(1)} collective-permute-done((f32[2,128,128]{2,1,0:T(8,128)S(1)}, f32[2,128,128]{2,1,0:T(8,128)S(1)}, u32[]{:S(2)}, u32[]{:S(2)}) %collective-permute-start.34) | collective-permute-done | bytes 131104 | tf_op jit(solution)/shard_map/ppermute | solution.py:156
  104.1 1.5 %collective-permute-start.37 = (f32[2,128,128]{2,1,0:T(8,128)S(1)}, f32[2,128,128]{2,1,0:T(8,128)S(1)}, u32[]{:S(2)}, u32[]{:S(2)}) collective-permute-start(f32[2,128,128]{2,1,0:T(8,128)S(1)} %get-tuple-element.239), channel_id=1, source_target_pairs={{12,4},{8,0},{13,5},{9,1},{14,6},{10,2},{15,7},{11,3}} | collective-permute-start | bytes 393224 | tf_op jit(solution)/shard_map/ppermute | solution.py:156
  105.6 1.2 %collective-permute-done.38 = f32[2,128,128]{2,1,0:T(8,128)S(1)} collective-permute-done((f32[2,128,128]{2,1,0:T(8,128)S(1)}, f32[2,128,128]{2,1,0:T(8,128)S(1)}, u32[]{:S(2)}, u32[]{:S(2)}) %collective-permute-start.38) | collective-permute-done | bytes 131104 | tf_op jit(solution)/shard_map/ppermute | solution.py:156
  106.9 2.4 %collective-permute-start.40 = (f32[2,128,128]{2,1,0:T(8,128)S(1)}, f32[2,128,128]{2,1,0:T(8,128)S(1)}, u32[]{:S(2)}, u32[]{:S(2)}) collective-permute-start(f32[2,128,128]{2,1,0:T(8,128)S(1)} %get-tuple-element.237), channel_id=1, source_target_pairs={{0,4},{4,0},{8,12},{12,8},{16,20},{20,16},{24,28},{28,24},{1,5},{5... | collective-permute-start | bytes 393224 | tf_op jit(solution)/shard_map/ppermute | solution.py:203
  109.2 2.1 %collective-permute-done.37 = f32[2,128,128]{2,1,0:T(8,128)S(1)} collective-permute-done((f32[2,128,128]{2,1,0:T(8,128)S(1)}, f32[2,128,128]{2,1,0:T(8,128)S(1)}, u32[]{:S(2)}, u32[]{:S(2)}) %collective-permute-start.37) | collective-permute-done | bytes 131104 | tf_op jit(solution)/shard_map/ppermute | solution.py:156
  111.4 1.7 %collective-permute-start.39 = (f32[2,128,128]{2,1,0:T(8,128)S(1)}, f32[2,128,128]{2,1,0:T(8,128)S(1)}, u32[]{:S(2)}, u32[]{:S(2)}) collective-permute-start(f32[2,128,128]{2,1,0:T(8,128)S(1)} %get-tuple-element.235), channel_id=1, source_target_pairs={{0,4},{4,0},{8,12},{12,8},{16,20},{20,16},{24,28},{28,24},{1,5},{5... | collective-permute-start | bytes 393224 | tf_op jit(solution)/shard_map/ppermute | solution.py:203
  113.1 1.4 %shard_map.84 = (bf16[256,256]{1,0:T(8,128)(2,1)S(1)}, bf16[256,256]{1,0:T(8,128)(2,1)S(1)}, f32[256,256]{1,0:T(8,128)S(1)}, f32[256,256]{1,0:T(8,128)S(1)}, f32...) custom-call(s32[1]{0:T(128)} %bitcast.place, bf16[256,2048]{1,0:T(8,128)(2,1)S(1)} %copy-done, bf16[256,2048]{1,0:T(8,128)(2,1)S(1)} %copy-done, ...), custom_call_target="tpu_custom_call" | custom-call | flops 301989888 | bytes 5439488 | tf_op jit(solution)/shard_map/pallas_call | solution.py:38
  114.6 1.4 %shard_map.87 = (bf16[256,256]{1,0:T(8,128)(2,1)S(1)}, bf16[256,256]{1,0:T(8,128)(2,1)S(1)}, f32[256,256]{1,0:T(8,128)S(1)}, f32[256,256]{1,0:T(8,128)S(1)}, f32...) custom-call(s32[1]{0:T(128)} %bitcast.place, bf16[256,2048]{1,0:T(8,128)(2,1)S(1)} %copy-done, bf16[256,2048]{1,0:T(8,128)(2,1)S(1)} %copy-done, ...), custom_call_target="tpu_custom_call" | custom-call | flops 301989888 | bytes 5439488 | tf_op jit(solution)/shard_map/pallas_call | solution.py:38
  116.1 1.4 %shard_map.88 = (bf16[256,2048]{1,0:T(8,128)(2,1)}, bf16[256,2048]{1,0:T(8,128)(2,1)}, bf16[256,2048]{1,0:T(8,128)(2,1)}) custom-call(s32[1]{0:T(128)} %bitcast.place, bf16[256,256]{1,0:T(8,128)(2,1)S(1)} %copy-done.49, bf16[256,256]{1,0:T(8,128)(2,1)S(1)} %copy-done.51, f32[256,256]{1,0:T(8,128)S(1)} %copy-done.29, f32[256,256]{1,0:T(8,128)S(1)} %copy-done.31, ...), custom_call_target="tpu_custom_call" | custom-call | flops 67108864 | bytes 1900544 | tf_op jit(solution)/shard_map/pallas_call | solution.py:38
  117.6 1.4 %shard_map.89 = (bf16[256,2048]{1,0:T(8,128)(2,1)}, bf16[256,2048]{1,0:T(8,128)(2,1)}, bf16[256,2048]{1,0:T(8,128)(2,1)}) custom-call(s32[1]{0:T(128)} %bitcast.place, bf16[256,256]{1,0:T(8,128)(2,1)S(1)} %get-tuple-element.189.qk, bf16[256,256]{1,0:T(8,128)(2,1)S(1)} %get-tuple-element.213.qo, ...), custom_call_target="tpu_custom_call", output_to_operand_aliasing={{0}: (12, {}), {1}: (13, {}), {2}: (14, {})} | custom-call | flops 67108864 | bytes 3473408 | tf_op jit(solution)/shard_map/pallas_call | solution.py:38
  119.0 2.3 %shard_map.90 = (bf16[256,2048]{1,0:T(8,128)(2,1)}, bf16[256,2048]{1,0:T(8,128)(2,1)}, bf16[256,2048]{1,0:T(8,128)(2,1)}) custom-call(s32[1]{0:T(128)} %bitcast.place, bf16[256,256]{1,0:T(8,128)(2,1)S(1)} %get-tuple-element.207.qk, bf16[256,256]{1,0:T(8,128)(2,1)S(1)} %get-tuple-element.208.qo, ...), custom_call_target="tpu_custom_call", output_to_operand_aliasing={{0}: (12, {}), {1}: (13, {}), {2}: (14, {})} | custom-call | flops 67108864 | bytes 3473408 | tf_op jit(solution)/shard_map/pallas_call | solution.py:38
  121.3 1.4 %shard_map.91 = (bf16[256,2048]{1,0:T(8,128)(2,1)}, bf16[256,2048]{1,0:T(8,128)(2,1)}, bf16[256,2048]{1,0:T(8,128)(2,1)}) custom-call(s32[1]{0:T(128)} %bitcast.place, bf16[256,256]{1,0:T(8,128)(2,1)S(1)} %get-tuple-element.163.qk, bf16[256,256]{1,0:T(8,128)(2,1)S(1)} %get-tuple-element.164.qo, ...), custom_call_target="tpu_custom_call", output_to_operand_aliasing={{0}: (12, {}), {1}: (13, {}), {2}: (14, {})} | custom-call | flops 67108864 | bytes 3473408 | tf_op jit(solution)/shard_map/pallas_call | solution.py:38
  (229 shorter events, 37.9 us)
Async XLA Ops:
  4.2 9.5 %collective-permute-start.2 = (f32[2,128,128]{2,1,0:T(8,128)S(1)}, f32[2,128,128]{2,1,0:T(8,128)S(1)}, u32[]{:S(2)}, u32[]{:S(2)}) collective-permute-start(f32[2,128,128]{2,1,0:T(8,128)S(1)} %get-tuple-element.126), channel_id=1, source_target_pairs={{0,4},{4,0},{8,12},{12,8},{16,20},{20,16},{24,28},{28,24},{1,5},{5... | collective-permute-start | bytes 393224 | tf_op jit(solution)/shard_map/ppermute | solution.py:173
  7.2 12.1 %collective-permute-start.1 = (f32[2,128,128]{2,1,0:T(8,128)S(1)}, f32[2,128,128]{2,1,0:T(8,128)S(1)}, u32[]{:S(2)}, u32[]{:S(2)}) collective-permute-start(f32[2,128,128]{2,1,0:T(8,128)S(1)} %get-tuple-element.124), channel_id=1, source_target_pairs={{0,4},{4,0},{8,12},{12,8},{16,20},{20,16},{24,28},{28,24},{1,5},{5... | collective-permute-start | bytes 393224 | tf_op jit(solution)/shard_map/ppermute | solution.py:173
  13.7 8.7 %collective-permute-start.5 = (f32[2,128,128]{2,1,0:T(8,128)S(1)}, f32[2,128,128]{2,1,0:T(8,128)S(1)}, u32[]{:S(2)}, u32[]{:S(2)}) collective-permute-start(f32[2,128,128]{2,1,0:T(8,128)S(1)} %add.149), channel_id=1, source_target_pairs={{0,8},{4,12},{1,9},{5,13},{2,10},{6,14},{3,11},{7,15}} | collective-permute-start | bytes 393224 | tf_op jit(solution)/shard_map/ppermute | solution.py:156
  17.7 6.7 %collective-permute-start.4 = (f32[2,128,128]{2,1,0:T(8,128)}, f32[2,128,128]{2,1,0:T(8,128)S(1)}, u32[]{:S(2)}, u32[]{:S(2)}) collective-permute-start(f32[2,128,128]{2,1,0:T(8,128)} %get-tuple-element.129), channel_id=1, source_target_pairs={{0,4},{4,0},{8,12},{12,8},{16,20},{20,16},{24,28},{28,24},{1,5},{5... | collective-permute-start | bytes 393224 | tf_op jit(solution)/shard_map/ppermute | solution.py:173
  20.0 8.5 %collective-permute-start.3 = (f32[2,128,128]{2,1,0:T(8,128)}, f32[2,128,128]{2,1,0:T(8,128)}, u32[]{:S(2)}, u32[]{:S(2)}) collective-permute-start(f32[2,128,128]{2,1,0:T(8,128)} %add.150), channel_id=1, source_target_pairs={{0,8},{4,12},{1,9},{5,13},{2,10},{6,14},{3,11},{7,15}} | collective-permute-start | bytes 393224 | tf_op jit(solution)/shard_map/ppermute | solution.py:156
  21.9 8.2 %collective-permute-start = (f32[2,128,128]{2,1,0:T(8,128)}, f32[2,128,128]{2,1,0:T(8,128)S(1)}, u32[]{:S(2)}, u32[]{:S(2)}) collective-permute-start(f32[2,128,128]{2,1,0:T(8,128)} %get-tuple-element.122), channel_id=1, source_target_pairs={{0,4},{4,0},{8,12},{12,8},{16,20},{20,16},{24,28},{28,24},{1,5},{5... | collective-permute-start | bytes 393224 | tf_op jit(solution)/shard_map/ppermute | solution.py:173
  23.1 9.8 %collective-permute-start.9 = (f32[2,128,128]{2,1,0:T(8,128)}, f32[2,128,128]{2,1,0:T(8,128)}, u32[]{:S(2)}, u32[]{:S(2)}) collective-permute-start(f32[2,128,128]{2,1,0:T(8,128)} %add.151), channel_id=1, source_target_pairs={{8,16},{12,20},{9,17},{13,21},{10,18},{14,22},{11,19},{15,23}} | collective-permute-start | bytes 393224 | tf_op jit(solution)/shard_map/ppermute | solution.py:156
  25.4 9.4 %collective-permute-start.8 = (f32[2,128,128]{2,1,0:T(8,128)S(1)}, f32[2,128,128]{2,1,0:T(8,128)S(1)}, u32[]{:S(2)}, u32[]{:S(2)}) collective-permute-start(f32[2,128,128]{2,1,0:T(8,128)S(1)} %add.152), channel_id=1, source_target_pairs={{0,8},{4,12},{1,9},{5,13},{2,10},{6,14},{3,11},{7,15}} | collective-permute-start | bytes 393224 | tf_op jit(solution)/shard_map/ppermute | solution.py:156
  29.4 6.3 %collective-permute-start.7 = (f32[2,128,128]{2,1,0:T(8,128)S(1)}, f32[2,128,128]{2,1,0:T(8,128)S(1)}, u32[]{:S(2)}, u32[]{:S(2)}) collective-permute-start(f32[2,128,128]{2,1,0:T(8,128)S(1)} %add.153), channel_id=1, source_target_pairs={{8,16},{12,20},{9,17},{13,21},{10,18},{14,22},{11,19},{15,23}} | collective-permute-start | bytes 393224 | tf_op jit(solution)/shard_map/ppermute | solution.py:156
  31.0 6.5 %collective-permute-start.6 = (f32[2,128,128]{2,1,0:T(8,128)S(1)}, f32[2,128,128]{2,1,0:T(8,128)S(1)}, u32[]{:S(2)}, u32[]{:S(2)}) collective-permute-start(f32[2,128,128]{2,1,0:T(8,128)S(1)} %add.154), channel_id=1, source_target_pairs={{0,8},{4,12},{1,9},{5,13},{2,10},{6,14},{3,11},{7,15}} | collective-permute-start | bytes 393224 | tf_op jit(solution)/shard_map/ppermute | solution.py:156
  34.0 4.2 %collective-permute-start.13 = (f32[2,128,128]{2,1,0:T(8,128)S(1)}, f32[2,128,128]{2,1,0:T(8,128)S(1)}, u32[]{:S(2)}, u32[]{:S(2)}) collective-permute-start(f32[2,128,128]{2,1,0:T(8,128)S(1)} %get-tuple-element.265), channel_id=1, source_target_pairs={{16,24},{20,28},{17,25},{21,29},{18,26},{22,30},{19,27},{23,31}} | collective-permute-start | bytes 393224 | tf_op jit(solution)/shard_map/ppermute | solution.py:156
  34.9 5.6 %collective-permute-start.12 = (f32[2,128,128]{2,1,0:T(8,128)S(1)}, f32[2,128,128]{2,1,0:T(8,128)S(1)}, u32[]{:S(2)}, u32[]{:S(2)}) collective-permute-start(f32[2,128,128]{2,1,0:T(8,128)S(1)} %add.157), channel_id=1, source_target_pairs={{8,16},{12,20},{9,17},{13,21},{10,18},{14,22},{11,19},{15,23}} | collective-permute-start | bytes 393224 | tf_op jit(solution)/shard_map/ppermute | solution.py:156
  36.7 4.5 %collective-permute-start.11 = (f32[2,128,128]{2,1,0:T(8,128)S(1)}, f32[2,128,128]{2,1,0:T(8,128)S(1)}, u32[]{:S(2)}, u32[]{:S(2)}) collective-permute-start(f32[2,128,128]{2,1,0:T(8,128)S(1)} %get-tuple-element.263), channel_id=1, source_target_pairs={{16,24},{20,28},{17,25},{21,29},{18,26},{22,30},{19,27},{23,31}} | collective-permute-start | bytes 393224 | tf_op jit(solution)/shard_map/ppermute | solution.py:156
  37.6 3.8 %collective-permute-start.10 = (f32[2,128,128]{2,1,0:T(8,128)S(1)}, f32[2,128,128]{2,1,0:T(8,128)S(1)}, u32[]{:S(2)}, u32[]{:S(2)}) collective-permute-start(f32[2,128,128]{2,1,0:T(8,128)S(1)} %add.160), channel_id=1, source_target_pairs={{8,16},{12,20},{9,17},{13,21},{10,18},{14,22},{11,19},{15,23}} | collective-permute-start | bytes 393224 | tf_op jit(solution)/shard_map/ppermute | solution.py:156
  38.3 6.5 %collective-permute-start.19 = (f32[2,128,128]{2,1,0:T(8,128)S(1)}, f32[2,128,128]{2,1,0:T(8,128)S(1)}, u32[]{:S(2)}, u32[]{:S(2)}) collective-permute-start(f32[2,128,128]{2,1,0:T(8,128)S(1)} %get-tuple-element.261), channel_id=1, source_target_pairs={{0,4},{4,0},{8,12},{12,8},{16,20},{20,16},{24,28},{28,24},{1,5},{5... | collective-permute-start | bytes 393224 | tf_op jit(solution)/shard_map/ppermute | solution.py:203
  40.5 1.5 %collective-permute-start.15 = (f32[2,128,128]{2,1,0:T(8,128)S(1)}, f32[2,128,128]{2,1,0:T(8,128)S(1)}, u32[]{:S(2)}, u32[]{:S(2)}) collective-permute-start(f32[2,128,128]{2,1,0:T(8,128)S(1)} %get-tuple-element.259), channel_id=1, source_target_pairs={{16,24},{20,28},{17,25},{21,29},{18,26},{22,30},{19,27},{23,31}} | collective-permute-start | bytes 393224 | tf_op jit(solution)/shard_map/ppermute | solution.py:156
  41.3 6.5 %collective-permute-start.18 = (f32[2,128,128]{2,1,0:T(8,128)S(1)}, f32[2,128,128]{2,1,0:T(8,128)S(1)}, u32[]{:S(2)}, u32[]{:S(2)}) collective-permute-start(f32[2,128,128]{2,1,0:T(8,128)S(1)} %get-tuple-element.257), channel_id=1, source_target_pairs={{0,4},{4,0},{8,12},{12,8},{16,20},{20,16},{24,28},{28,24},{1,5},{5... | collective-permute-start | bytes 393224 | tf_op jit(solution)/shard_map/ppermute | solution.py:203
  41.4 2.8 %collective-permute-start.14 = (f32[2,128,128]{2,1,0:T(8,128)S(1)}, f32[2,128,128]{2,1,0:T(8,128)S(1)}, u32[]{:S(2)}, u32[]{:S(2)}) collective-permute-start(f32[2,128,128]{2,1,0:T(8,128)S(1)} %get-tuple-element.255), channel_id=1, source_target_pairs={{16,24},{20,28},{17,25},{21,29},{18,26},{22,30},{19,27},{23,31}} | collective-permute-start | bytes 393224 | tf_op jit(solution)/shard_map/ppermute | solution.py:156
  42.1 7.5 %collective-permute-start.17 = (f32[2,128,128]{2,1,0:T(8,128)S(1)}, f32[2,128,128]{2,1,0:T(8,128)S(1)}, u32[]{:S(2)}, u32[]{:S(2)}) collective-permute-start(f32[2,128,128]{2,1,0:T(8,128)S(1)} %get-tuple-element.253), channel_id=1, source_target_pairs={{0,4},{4,0},{8,12},{12,8},{16,20},{20,16},{24,28},{28,24},{1,5},{5... | collective-permute-start | bytes 393224 | tf_op jit(solution)/shard_map/ppermute | solution.py:203
  44.2 6.8 %collective-permute-start.16 = (f32[2,128,128]{2,1,0:T(8,128)S(1)}, f32[2,128,128]{2,1,0:T(8,128)S(1)}, u32[]{:S(2)}, u32[]{:S(2)}) collective-permute-start(f32[2,128,128]{2,1,0:T(8,128)S(1)} %get-tuple-element.251), channel_id=1, source_target_pairs={{0,4},{4,0},{8,12},{12,8},{16,20},{20,16},{24,28},{28,24},{1,5},{5... | collective-permute-start | bytes 393224 | tf_op jit(solution)/shard_map/ppermute | solution.py:203
  52.7 3.0 %collective-permute-start.22 = (f32[2,256]{1,0:T(2,128)S(1)}, f32[2,256]{1,0:T(2,128)S(1)}, u32[]{:S(2)}, u32[]{:S(2)}) collective-permute-start(f32[2,256]{1,0:T(2,128)S(1)} %get-tuple-element.150.refs_0_), channel_id=1, source_target_pairs={{0,3},{1,2},{2,1},{3,0},{4,7},{5,6},{6,5},{7,4},{8,11},{9,10},{10,... | collective-permute-start | bytes 6152 | tf_op jit(solution)/shard_map/ppermute | solution.py:289
  52.7 3.6 %collective-permute-start.21 = (f32[2,256]{1,0:T(2,128)S(1)}, f32[2,256]{1,0:T(2,128)S(1)}, u32[]{:S(2)}, u32[]{:S(2)}) collective-permute-start(f32[2,256]{1,0:T(2,128)S(1)} %get-tuple-element.150.refs_0_), channel_id=1, source_target_pairs={{0,2},{1,3},{2,0},{3,1},{4,6},{5,7},{6,4},{7,5},{8,10},{9,11},{10,... | collective-permute-start | bytes 6152 | tf_op jit(solution)/shard_map/ppermute | solution.py:289
  54.2 2.1 %collective-permute-start.20 = (f32[2,256]{1,0:T(2,128)S(1)}, f32[2,256]{1,0:T(2,128)S(1)}, u32[]{:S(2)}, u32[]{:S(2)}) collective-permute-start(f32[2,256]{1,0:T(2,128)S(1)} %get-tuple-element.150.refs_0_), channel_id=1, source_target_pairs={{0,1},{1,0},{2,3},{3,2},{4,5},{5,4},{6,7},{7,6},{8,9},{9,8},{10,11... | collective-permute-start | bytes 6152 | tf_op jit(solution)/shard_map/ppermute | solution.py:289
  59.6 10.2 %collective-permute-start.25 = (f32[2,128,128]{2,1,0:T(8,128)S(1)}, f32[2,128,128]{2,1,0:T(8,128)S(1)}, u32[]{:S(2)}, u32[]{:S(2)}) collective-permute-start(f32[2,128,128]{2,1,0:T(8,128)S(1)} %get-tuple-element.174), channel_id=1, source_target_pairs={{0,4},{4,0},{8,12},{12,8},{16,20},{20,16},{24,28},{28,24},{1,5},{5... | collective-permute-start | bytes 393224 | tf_op jit(solution)/shard_map/ppermute | solution.py:173
  60.7 10.9 %collective-permute-start.24 = (f32[2,128,128]{2,1,0:T(8,128)S(1)}, f32[2,128,128]{2,1,0:T(8,128)S(1)}, u32[]{:S(2)}, u32[]{:S(2)}) collective-permute-start(f32[2,128,128]{2,1,0:T(8,128)S(1)} %get-tuple-element.172), channel_id=1, source_target_pairs={{0,4},{4,0},{8,12},{12,8},{16,20},{20,16},{24,28},{28,24},{1,5},{5... | collective-permute-start | bytes 393224 | tf_op jit(solution)/shard_map/ppermute | solution.py:173
  69.8 4.8 %collective-permute-start.28 = (f32[2,128,128]{2,1,0:T(8,128)S(1)}, f32[2,128,128]{2,1,0:T(8,128)S(1)}, u32[]{:S(2)}, u32[]{:S(2)}) collective-permute-start(f32[2,128,128]{2,1,0:T(8,128)S(1)} %add.173), channel_id=1, source_target_pairs={{28,20},{24,16},{29,21},{25,17},{30,22},{26,18},{31,23},{27,19}} | collective-permute-start | bytes 393224 | tf_op jit(solution)/shard_map/ppermute | solution.py:156
  70.4 12.6 %collective-permute-start.27 = (f32[2,128,128]{2,1,0:T(8,128)}, f32[2,128,128]{2,1,0:T(8,128)}, u32[]{:S(2)}, u32[]{:S(2)}) collective-permute-start(f32[2,128,128]{2,1,0:T(8,128)} %get-tuple-element.183), channel_id=1, source_target_pairs={{0,4},{4,0},{8,12},{12,8},{16,20},{20,16},{24,28},{28,24},{1,5},{5... | collective-permute-start | bytes 393224 | tf_op jit(solution)/shard_map/ppermute | solution.py:173
  72.4 12.5 %collective-permute-start.26 = (f32[2,128,128]{2,1,0:T(8,128)}, f32[2,128,128]{2,1,0:T(8,128)}, u32[]{:S(2)}, u32[]{:S(2)}) collective-permute-start(f32[2,128,128]{2,1,0:T(8,128)} %add.174), channel_id=1, source_target_pairs={{28,20},{24,16},{29,21},{25,17},{30,22},{26,18},{31,23},{27,19}} | collective-permute-start | bytes 393224 | tf_op jit(solution)/shard_map/ppermute | solution.py:156
  73.7 12.8 %collective-permute-start.23 = (f32[2,128,128]{2,1,0:T(8,128)}, f32[2,128,128]{2,1,0:T(8,128)S(1)}, u32[]{:S(2)}, u32[]{:S(2)}) collective-permute-start(f32[2,128,128]{2,1,0:T(8,128)} %get-tuple-element.170), channel_id=1, source_target_pairs={{0,4},{4,0},{8,12},{12,8},{16,20},{20,16},{24,28},{28,24},{1,5},{5... | collective-permute-start | bytes 393224 | tf_op jit(solution)/shard_map/ppermute | solution.py:173
  75.2 12.0 %collective-permute-start.32 = (f32[2,128,128]{2,1,0:T(8,128)}, f32[2,128,128]{2,1,0:T(8,128)}, u32[]{:S(2)}, u32[]{:S(2)}) collective-permute-start(f32[2,128,128]{2,1,0:T(8,128)} %add.175), channel_id=1, source_target_pairs={{20,12},{16,8},{21,13},{17,9},{22,14},{18,10},{23,15},{19,11}} | collective-permute-start | bytes 393224 | tf_op jit(solution)/shard_map/ppermute | solution.py:156
  84.0 5.5 %collective-permute-start.31 = (f32[2,128,128]{2,1,0:T(8,128)S(1)}, f32[2,128,128]{2,1,0:T(8,128)S(1)}, u32[]{:S(2)}, u32[]{:S(2)}) collective-permute-start(f32[2,128,128]{2,1,0:T(8,128)S(1)} %add.176), channel_id=1, source_target_pairs={{28,20},{24,16},{29,21},{25,17},{30,22},{26,18},{31,23},{27,19}} | collective-permute-start | bytes 393224 | tf_op jit(solution)/shard_map/ppermute | solution.py:156
  85.8 4.4 %collective-permute-start.30 = (f32[2,128,128]{2,1,0:T(8,128)S(1)}, f32[2,128,128]{2,1,0:T(8,128)S(1)}, u32[]{:S(2)}, u32[]{:S(2)}) collective-permute-start(f32[2,128,128]{2,1,0:T(8,128)S(1)} %add.177), channel_id=1, source_target_pairs={{20,12},{16,8},{21,13},{17,9},{22,14},{18,10},{23,15},{19,11}} | collective-permute-start | bytes 393224 | tf_op jit(solution)/shard_map/ppermute | solution.py:156
  86.5 6.2 %collective-permute-start.29 = (f32[2,128,128]{2,1,0:T(8,128)S(1)}, f32[2,128,128]{2,1,0:T(8,128)S(1)}, u32[]{:S(2)}, u32[]{:S(2)}) collective-permute-start(f32[2,128,128]{2,1,0:T(8,128)S(1)} %add.178), channel_id=1, source_target_pairs={{28,20},{24,16},{29,21},{25,17},{30,22},{26,18},{31,23},{27,19}} | collective-permute-start | bytes 393224 | tf_op jit(solution)/shard_map/ppermute | solution.py:156
  88.2 6.9 %collective-permute-start.36 = (f32[2,128,128]{2,1,0:T(8,128)S(1)}, f32[2,128,128]{2,1,0:T(8,128)S(1)}, u32[]{:S(2)}, u32[]{:S(2)}) collective-permute-start(f32[2,128,128]{2,1,0:T(8,128)S(1)} %get-tuple-element.249), channel_id=1, source_target_pairs={{12,4},{8,0},{13,5},{9,1},{14,6},{10,2},{15,7},{11,3}} | collective-permute-start | bytes 393224 | tf_op jit(solution)/shard_map/ppermute | solution.py:156
  89.5 6.8 %collective-permute-start.35 = (f32[2,128,128]{2,1,0:T(8,128)S(1)}, f32[2,128,128]{2,1,0:T(8,128)S(1)}, u32[]{:S(2)}, u32[]{:S(2)}) collective-permute-start(f32[2,128,128]{2,1,0:T(8,128)S(1)} %add.181), channel_id=1, source_target_pairs={{20,12},{16,8},{21,13},{17,9},{22,14},{18,10},{23,15},{19,11}} | collective-permute-start | bytes 393224 | tf_op jit(solution)/shard_map/ppermute | solution.py:156
  91.2 21.9 %copy-start.8 = (bf16[16,256,256]{2,1,0:T(8,128)(2,1)S(1)}, bf16[16,256,256]{2,1,0:T(8,128)(2,1)}, u32[]{:S(2)}) copy-start(bf16[16,256,256]{2,1,0:T(8,128)(2,1)} %copy-done.5) | copy-start | bytes 6291460
  91.2 21.9 %copy-start.39 = (bf16[256,256]{1,0:T(8,128)(2,1)S(1)}, bf16[256,256]{1,0:T(8,128)(2,1)}, u32[]{:S(2)}) copy-start(bf16[256,256]{1,0:T(8,128)(2,1)} %copy-done.38) | copy-start | bytes 393220
  91.2 21.9 %copy-start.43 = (bf16[256,256]{1,0:T(8,128)(2,1)S(1)}, bf16[256,256]{1,0:T(8,128)(2,1)}, u32[]{:S(2)}) copy-start(bf16[256,256]{1,0:T(8,128)(2,1)} %copy-done.42) | copy-start | bytes 393220
  91.2 21.9 %copy-start.57 = (bf16[2,128,128]{2,1,0:T(8,128)(2,1)S(1)}, bf16[2,128,128]{2,1,0:T(8,128)(2,1)}, u32[]{:S(2)}) copy-start(bf16[2,128,128]{2,1,0:T(8,128)(2,1)} %copy-done.56) | copy-start | bytes 196612
  91.2 21.8 %copy-start.59 = (bf16[2,128,128]{2,1,0:T(8,128)(2,1)S(1)}, bf16[2,128,128]{2,1,0:T(8,128)(2,1)}, u32[]{:S(2)}) copy-start(bf16[2,128,128]{2,1,0:T(8,128)(2,1)} %copy-done.58) | copy-start | bytes 196612
  91.3 12.7 %collective-permute-start.34 = (f32[2,128,128]{2,1,0:T(8,128)S(1)}, f32[2,128,128]{2,1,0:T(8,128)S(1)}, u32[]{:S(2)}, u32[]{:S(2)}) collective-permute-start(f32[2,128,128]{2,1,0:T(8,128)S(1)} %get-tuple-element.247), channel_id=1, source_target_pairs={{12,4},{8,0},{13,5},{9,1},{14,6},{10,2},{15,7},{11,3}} | collective-permute-start | bytes 393224 | tf_op jit(solution)/shard_map/ppermute | solution.py:156
  92.7 11.4 %collective-permute-start.33 = (f32[2,128,128]{2,1,0:T(8,128)S(1)}, f32[2,128,128]{2,1,0:T(8,128)S(1)}, u32[]{:S(2)}, u32[]{:S(2)}) collective-permute-start(f32[2,128,128]{2,1,0:T(8,128)S(1)} %add.184), channel_id=1, source_target_pairs={{20,12},{16,8},{21,13},{17,9},{22,14},{18,10},{23,15},{19,11}} | collective-permute-start | bytes 393224 | tf_op jit(solution)/shard_map/ppermute | solution.py:156
  95.1 21.0 %collective-permute-start.42 = (f32[2,128,128]{2,1,0:T(8,128)S(1)}, f32[2,128,128]{2,1,0:T(8,128)S(1)}, u32[]{:S(2)}, u32[]{:S(2)}) collective-permute-start(f32[2,128,128]{2,1,0:T(8,128)S(1)} %get-tuple-element.245), channel_id=1, source_target_pairs={{0,4},{4,0},{8,12},{12,8},{16,20},{20,16},{24,28},{28,24},{1,5},{5... | collective-permute-start | bytes 393224 | tf_op jit(solution)/shard_map/ppermute | solution.py:203
  96.4 10.5 %collective-permute-start.38 = (f32[2,128,128]{2,1,0:T(8,128)S(1)}, f32[2,128,128]{2,1,0:T(8,128)S(1)}, u32[]{:S(2)}, u32[]{:S(2)}) collective-permute-start(f32[2,128,128]{2,1,0:T(8,128)S(1)} %get-tuple-element.243), channel_id=1, source_target_pairs={{12,4},{8,0},{13,5},{9,1},{14,6},{10,2},{15,7},{11,3}} | collective-permute-start | bytes 393224 | tf_op jit(solution)/shard_map/ppermute | solution.py:156
  104.0 13.6 %collective-permute-start.41 = (f32[2,128,128]{2,1,0:T(8,128)S(1)}, f32[2,128,128]{2,1,0:T(8,128)S(1)}, u32[]{:S(2)}, u32[]{:S(2)}) collective-permute-start(f32[2,128,128]{2,1,0:T(8,128)S(1)} %get-tuple-element.241), channel_id=1, source_target_pairs={{0,4},{4,0},{8,12},{12,8},{16,20},{20,16},{24,28},{28,24},{1,5},{5... | collective-permute-start | bytes 393224 | tf_op jit(solution)/shard_map/ppermute | solution.py:203
  104.1 7.3 %collective-permute-start.37 = (f32[2,128,128]{2,1,0:T(8,128)S(1)}, f32[2,128,128]{2,1,0:T(8,128)S(1)}, u32[]{:S(2)}, u32[]{:S(2)}) collective-permute-start(f32[2,128,128]{2,1,0:T(8,128)S(1)} %get-tuple-element.239), channel_id=1, source_target_pairs={{12,4},{8,0},{13,5},{9,1},{14,6},{10,2},{15,7},{11,3}} | collective-permute-start | bytes 393224 | tf_op jit(solution)/shard_map/ppermute | solution.py:156
  106.9 12.1 %collective-permute-start.40 = (f32[2,128,128]{2,1,0:T(8,128)S(1)}, f32[2,128,128]{2,1,0:T(8,128)S(1)}, u32[]{:S(2)}, u32[]{:S(2)}) collective-permute-start(f32[2,128,128]{2,1,0:T(8,128)S(1)} %get-tuple-element.237), channel_id=1, source_target_pairs={{0,4},{4,0},{8,12},{12,8},{16,20},{20,16},{24,28},{28,24},{1,5},{5... | collective-permute-start | bytes 393224 | tf_op jit(solution)/shard_map/ppermute | solution.py:203
  111.4 9.9 %collective-permute-start.39 = (f32[2,128,128]{2,1,0:T(8,128)S(1)}, f32[2,128,128]{2,1,0:T(8,128)S(1)}, u32[]{:S(2)}, u32[]{:S(2)}) collective-permute-start(f32[2,128,128]{2,1,0:T(8,128)S(1)} %get-tuple-element.235), channel_id=1, source_target_pairs={{0,4},{4,0},{8,12},{12,8},{16,20},{20,16},{24,28},{28,24},{1,5},{5... | collective-permute-start | bytes 393224 | tf_op jit(solution)/shard_map/ppermute | solution.py:203
  (66 other events, 236.8 us)

commit v4 on v3

--- a/solution.py
+++ b/solution.py
@@ -33,21 +33,27 @@
     return jnp.where(mask, scores, 0.0).astype(BF16)
 
 
+HBM, VMEM = pltpu.HBM, pltpu.VMEM
+
+
 def call(body, place, ins, outs, grid=(1,), aliases=None, flops=0, grant=6):
-    size = sum(a.size * a.dtype.itemsize // 2 for a, _, _ in ins)
+    ins = [(*item, None)[:4] for item in ins]
+    outs = [(*item, None)[:5] for item in outs]
+    arrays = [pltpu.with_memory_space_constraint(a, m) if m else a for a, _, _, m in ins]
+    size = sum(a.size * a.dtype.itemsize // 2 for a in arrays)
     return pl.pallas_call(
         body,
         grid_spec=pltpu.PrefetchScalarGridSpec(
             num_scalar_prefetch=1,
             grid=grid,
-            in_specs=[pl.BlockSpec(b, m) if b else pl.BlockSpec(memory_space=pl.ANY) for _, b, m in ins],
-            out_specs=[pl.BlockSpec(b, m) for _, _, b, m in outs],
+            in_specs=[pl.BlockSpec(b, m) if b else pl.BlockSpec(memory_space=pl.ANY) for _, b, m, _ in ins],
+            out_specs=[pl.BlockSpec(b, m) for _, _, b, m, _ in outs],
         ),
-        out_shape=[jax.ShapeDtypeStruct(s, d) for s, d, _, _ in outs],
+        out_shape=[(m or jax.ShapeDtypeStruct)(s, d) for s, d, _, _, m in outs],
         input_output_aliases=aliases or {},
         compiler_params=pltpu.CompilerParams(vmem_limit_bytes=grant * 1024 * 1024),
         cost_estimate=pl.CostEstimate(flops=flops, bytes_accessed=size, transcendentals=0),
-    )(place, *[a for a, _, _ in ins])
+    )(place, *arrays)
 
 
 def states_body(per, place, a, b, *outs):
@@ -237,8 +243,8 @@
 
         sent = call(
             functools.partial(states_body, per), place,
-            [(a, (tokens, wide), sent_half) for a in (keys, values)],
-            [((per, DH, DH), F32, (per, DH, DH), whole3)] * CHUNKS,
+            [(a, (tokens, wide), sent_half, HBM) for a in (keys, values)],
+            [((per, DH, DH), F32, (per, DH, DH), whole3, VMEM)] * CHUNKS,
             flops=half * mac * DH,
         )
 
@@ -246,10 +252,10 @@
         strip = lambda i, s: (0, (2 * s[0] + i) % 4)
         *kept, scores, attn_local = call(
             functools.partial(local_body, per, CHUNKS, group), place,
-            [(a, (tokens, group * DH), strip) for a in (queries, keys, values)],
-            [((per, DH, DH), F32, (per, DH, DH), whole3)] * CHUNKS + [
-                ((heads, GROUP, GROUP), BF16, (group, GROUP, GROUP), lambda i, s: ((2 * s[0] + i) % 4, 0, 0)),
-                ((tokens, width), F32, (tokens, group * DH), strip),
+            [(a, (tokens, group * DH), strip, HBM) for a in (queries, keys, values)],
+            [((per, DH, DH), F32, (per, DH, DH), whole3, VMEM)] * CHUNKS + [
+                ((heads, GROUP, GROUP), BF16, (group, GROUP, GROUP), lambda i, s: ((2 * s[0] + i) % 4, 0, 0), HBM),
+                ((tokens, width), F32, (tokens, group * DH), strip, HBM),
             ],
             grid=(4,), flops=heads * mac * (2 * GROUP + DH // 2),
         )
@@ -269,7 +275,7 @@
             ins += [(a, (per, DH, DH), whole3) for a in (e, r, other)]
             if not first:
                 ins += [(a, (GROUP, DH), whole2) for a in (square, cross)]
-            outs = [(block, F32, block, whole2)] * 2 + [((per, DH, DH), BF16, (per, DH, DH), whole3)] * 2
+            outs = [(block, F32, block, whole2, VMEM)] * 2 + [((per, DH, DH), BF16, (per, DH, DH), whole3, VMEM)] * 2
             if last:
                 outs += [((2, GROUP), F32, (2, GROUP), whole2)]
             else:
@@ -293,8 +299,8 @@
             ins = [(a, (2, GROUP), whole2) for a in sums]
             ins += [(attns[c][which], block, whole2) for c in range(CHUNKS)]
             ins += [(queries, (tokens, wide), index), (out_grad, (tokens, wide), index), (gain, (1, wide), index)]
-            outs = [(block, BF16, block, whole2)] * CHUNKS
-            outs += [((per, DH, DH), F32, (per, DH, DH), whole3)] * CHUNKS
+            outs = [(block, BF16, block, whole2, VMEM)] * CHUNKS
+            outs += [((per, DH, DH), F32, (per, DH, DH), whole3, VMEM)] * CHUNKS
             result = call(
                 functools.partial(delta_body, per, CHUNKS, parts, float(parts * heads * DH)), place, ins, outs,
                 flops=half * mac * DH)
@@ -305,12 +311,12 @@
 
         def grads(c):
             ins = []
-            for a in (queries, keys, values):
-                ins += [(a, block, at_k(c)), (a, block, at_o(c))]
-            ins += [(scores, (per, GROUP, GROUP), at_k3(c)), (scores, (per, GROUP, GROUP), at_o3(c))]
+            for a, m in ((queries, None), (keys, HBM), (values, HBM)):
+                ins += [(a, block, at_k(c), m), (a, block, at_o(c), m)]
+            ins += [(scores, (per, GROUP, GROUP), at(c), HBM) for at in (at_k3, at_o3)]
             ins += [(d_k[c], block, whole2), (d_o[c], block, whole2)]
             ins += [(a, (per, DH, DH), whole3) for a in priors[c]]
-            outs = [(block, BF16, block, whole2)] * 2 + [(block, F32, block, whole2)] * 4
+            outs = [(block, BF16, block, whole2, HBM)] * 2 + [(block, F32, block, whole2, HBM)] * 4
             return call(
                 functools.partial(grads_body, per), place, ins, outs,
                 flops=2 * per * mac * (4 * GROUP + DH))
@@ -330,15 +336,15 @@
         mine = lambda i, s: (0, jnp.where(i == 0, s[0], 1 - s[0]) * CHUNKS + c)
         whole2 = lambda i, s: (0, 0)
         whole3 = lambda i, s: (0, 0, 0)
-        ins = [(a, block, whole2) for a in (qg_k, qg_o, kl_k, kl_o, vl_k, vl_o)]
-        ins += [(a, block, mine) for a in (keys, values)]
+        ins = [(a, block, whole2, HBM) for a in (qg_k, qg_o, kl_k, kl_o, vl_k, vl_o)]
+        ins += [(a, block, mine, HBM) for a in (keys, values)]
         ins += [(a, (per, DH, DH), whole3) for a in (e, r, other)]
         aliases = {}
         if done[0] is not None:
             for n, a in enumerate(done):
                 aliases[len(ins) + 1] = n
-                ins.append((a, None, None))
-        outs = [((tokens, width), BF16, block, mine)] * 3
+                ins.append((a, None, None, HBM))
+        outs = [((tokens, width), BF16, block, mine, HBM)] * 3
 
         def body(place, qk, qo, kk, ko, vk, vo, k, v, e, r, other, *refs):
             kg, vg, qg = refs[-3:]

time: 124 us -> 115 us (0.927)
  local copies, waits for them, and re-layouts: 21.5 us -> 0.05 us
  Pallas kernels: 20.1 us -> 35.7 us
  waiting for transfers between devices: 17.2 us -> 24.9 us
  other arithmetic: 12 us -> 4.9 us
  starting transfers between devices: 50.3 us -> 47.6 us
    unnamed x142 -> x16, local copies, waits for them, and re-layouts: 21.5 us -> 0.04 us
    pallas_call x16, Pallas kernels: 20.1 us -> 35.7 us  [call(): pl.pallas_call(body, grid_spec=pltpu.PrefetchScalarGridSpec(num_scalar_pr...]
    ppermute x24, waiting for transfers between devices: 11.4 us -> 15.8 us  [hop(): return lax.ppermute(array, 'seq', pairs)]
    add x16, other arithmetic: 7.52 us -> 3.88 us  [scan(): send = carry[c] + part[c]]
    add x8, other arithmetic: 4.23 us -> 0.78 us  [scan(): part[c] = send = kept[c] + got]
    ppermute x8, waiting for transfers between devices: 0.02 us -> 1.92 us  [scan(): swapped = [lax.ppermute(b, 'seq', swap) for b in sent]]
    ppermute x24, starting transfers between devices: 29.4 us -> 27.6 us  [hop(): return lax.ppermute(array, 'seq', pairs)]
    ppermute x8, waiting for transfers between devices: 3.99 us -> 5.4 us  [scan(): out[c] = (carry[c], swapped[c], lax.ppermute(send, 'seq', swap))]
  transfers between devices with their start and end apart: 43 -> 43, of which waited for: 10 -> 13; matrix products, arithmetic and copies ran while one was open for 10% -> 4% of each run, Pallas kernels for 13% -> 26%
where the time goes in v4:
time: 115 us; the launch traced here: 114 us
  starting transfers between devices  47.6 us (41%)
  Pallas kernels  35.7 us (31%)
  waiting for transfers between devices  24.9 us (22%)
  other arithmetic  4.9 us (4%)
  between operations  1.26 us (1%)
    pallas_call x16, Pallas kernels, call(): pl.pallas_call(body, grid_spec=pltpu.PrefetchScalarGridSpec(num_scalar_pr...  35.7 us
    ppermute x24, starting transfers between devices, hop(): return lax.ppermute(array, 'seq', pairs)  27.6 us
    ppermute x24, waiting for transfers between devices, hop(): return lax.ppermute(array, 'seq', pairs)  15.8 us
    ppermute x8, starting transfers between devices, scan(): swapped = [lax.ppermute(b, 'seq', swap) for b in sent]  9.75 us
    ppermute x8, starting transfers between devices, scan(): out[c] = (carry[c], swapped[c], lax.ppermute(send, 'seq', swap))  8.38 us
    ppermute x8, waiting for transfers between devices, scan(): out[c] = (carry[c], swapped[c], lax.ppermute(send, 'seq', swap))  5.4 us
    add x16, other arithmetic, scan(): send = carry[c] + part[c]  3.88 us
  transfers between devices with their start and end apart: 43, of which 13 were waited for; matrix products, arithmetic and copies ran while one was open for 4% of the time, Pallas kernels for 26%

profile of v4, /device:TPU:0, one launch (start us, length us, event | category | flops | bytes accessed | tf_op | source)
XLA Modules:
  0.0 114.5 jit_solution(12206426195780297473)
XLA Ops:
  0.6 1.6 %shard_map.77 = (f32[2,128,128]{2,1,0:T(8,128)S(1)}, f32[2,128,128]{2,1,0:T(8,128)S(1)}, f32[2,128,128]{2,1,0:T(8,128)S(1)}, f32[2,128,128]{2,1,0:T(8,128)S(1)}) custom-call(s32[1]{0:T(128)} %bitcast.place, bf16[256,2048]{1,0:T(8,128)(2,1)} %k.9, bf16[256,2048]{1,0:T(8,128)(2,1)} %v.9), custom_call_target="tpu_custom_call" | custom-call | flops 67108864 | bytes 1048576 | tf_op jit(solution)/shard_map/pallas_call | solution.py:44
  2.2 3.0 %collective-permute-start.2 = (f32[2,128,128]{2,1,0:T(8,128)S(1)}, f32[2,128,128]{2,1,0:T(8,128)S(1)}, u32[]{:S(2)}, u32[]{:S(2)}) collective-permute-start(f32[2,128,128]{2,1,0:T(8,128)S(1)} %get-tuple-element.126), channel_id=1, source_target_pairs={{0,4},{4,0},{8,12},{12,8},{16,20},{20,16},{24,28},{28,24},{1,5},{5... | collective-permute-start | bytes 393224 | tf_op jit(solution)/shard_map/ppermute | solution.py:179
  5.3 6.0 %shard_map.76 = (f32[2,128,128]{2,1,0:T(8,128)S(1)}, f32[2,128,128]{2,1,0:T(8,128)S(1)}, f32[2,128,128]{2,1,0:T(8,128)S(1)}, f32[2,128,128]{2,1,0:T(8,128)S(1)},...) custom-call(s32[1]{0:T(128)} %bitcast.place, bf16[256,2048]{1,0:T(8,128)(2,1)} %refs_1_.7, bf16[256,2048]{1,0:T(8,128)(2,1)} %k.9, ...), custom_call_target="tpu_custom_call" | custom-call | flops 603979776 | bytes 1572864 | tf_op jit(solution)/shard_map/pallas_call | solution.py:44
  11.3 3.9 %collective-permute-start.5 = (f32[2,128,128]{2,1,0:T(8,128)S(1)}, f32[2,128,128]{2,1,0:T(8,128)S(1)}, u32[]{:S(2)}, u32[]{:S(2)}) collective-permute-start(f32[2,128,128]{2,1,0:T(8,128)S(1)} %add.149), channel_id=1, source_target_pairs={{0,8},{4,12},{1,9},{5,13},{2,10},{6,14},{3,11},{7,15}} | collective-permute-start | bytes 393224 | tf_op jit(solution)/shard_map/ppermute | solution.py:162
  15.3 1.7 %collective-permute-start.4 = (f32[2,128,128]{2,1,0:T(8,128)S(1)}, f32[2,128,128]{2,1,0:T(8,128)S(1)}, u32[]{:S(2)}, u32[]{:S(2)}) collective-permute-start(f32[2,128,128]{2,1,0:T(8,128)S(1)} %get-tuple-element.129), channel_id=1, source_target_pairs={{0,4},{4,0},{8,12},{12,8},{16,20},{20,16},{24,28},{28,24},{1,5},{5... | collective-permute-start | bytes 393224 | tf_op jit(solution)/shard_map/ppermute | solution.py:179
  16.9 1.3 %collective-permute-start.3 = (f32[2,128,128]{2,1,0:T(8,128)S(1)}, f32[2,128,128]{2,1,0:T(8,128)S(1)}, u32[]{:S(2)}, u32[]{:S(2)}) collective-permute-start(f32[2,128,128]{2,1,0:T(8,128)S(1)} %add.150), channel_id=1, source_target_pairs={{0,8},{4,12},{1,9},{5,13},{2,10},{6,14},{3,11},{7,15}} | collective-permute-start | bytes 393224 | tf_op jit(solution)/shard_map/ppermute | solution.py:162
  19.5 1.6 %collective-permute-done.4.r = f32[2,128,128]{2,1,0:T(8,128)S(1)} collective-permute-done((f32[2,128,128]{2,1,0:T(8,128)S(1)}, f32[2,128,128]{2,1,0:T(8,128)S(1)}, u32[]{:S(2)}, u32[]{:S(2)}) %collective-permute-start.4) | collective-permute-done | bytes 131104 | tf_op jit(solution)/shard_map/ppermute | solution.py:179
  21.0 2.8 %collective-permute-start.8 = (f32[2,128,128]{2,1,0:T(8,128)S(1)}, f32[2,128,128]{2,1,0:T(8,128)S(1)}, u32[]{:S(2)}, u32[]{:S(2)}) collective-permute-start(f32[2,128,128]{2,1,0:T(8,128)S(1)} %add.152), channel_id=1, source_target_pairs={{0,8},{4,12},{1,9},{5,13},{2,10},{6,14},{3,11},{7,15}} | collective-permute-start | bytes 393224 | tf_op jit(solution)/shard_map/ppermute | solution.py:162
  23.9 0.7 collective-permute-start.7
  24.6 1.9 %collective-permute-start.6 = (f32[2,128,128]{2,1,0:T(8,128)S(1)}, f32[2,128,128]{2,1,0:T(8,128)S(1)}, u32[]{:S(2)}, u32[]{:S(2)}) collective-permute-start(f32[2,128,128]{2,1,0:T(8,128)S(1)} %add.154), channel_id=1, source_target_pairs={{0,8},{4,12},{1,9},{5,13},{2,10},{6,14},{3,11},{7,15}} | collective-permute-start | bytes 393224 | tf_op jit(solution)/shard_map/ppermute | solution.py:162
  28.4 0.8 collective-permute-start.11
  29.2 0.8 collective-permute-start.10
  30.1 2.4 %collective-permute-start.19 = (f32[2,128,128]{2,1,0:T(8,128)S(1)}, f32[2,128,128]{2,1,0:T(8,128)S(1)}, u32[]{:S(2)}, u32[]{:S(2)}) collective-permute-start(f32[2,128,128]{2,1,0:T(8,128)S(1)} %get-tuple-element.261), channel_id=1, source_target_pairs={{0,4},{4,0},{8,12},{12,8},{16,20},{20,16},{24,28},{28,24},{1,5},{5... | collective-permute-start | bytes 393224 | tf_op jit(solution)/shard_map/ppermute | solution.py:209
  34.1 2.1 %collective-permute-start.17 = (f32[2,128,128]{2,1,0:T(8,128)S(1)}, f32[2,128,128]{2,1,0:T(8,128)S(1)}, u32[]{:S(2)}, u32[]{:S(2)}) collective-permute-start(f32[2,128,128]{2,1,0:T(8,128)S(1)} %get-tuple-element.253), channel_id=1, source_target_pairs={{0,4},{4,0},{8,12},{12,8},{16,20},{20,16},{24,28},{28,24},{1,5},{5... | collective-permute-start | bytes 393224 | tf_op jit(solution)/shard_map/ppermute | solution.py:209
  37.0 2.7 %collective-permute-done.18.other = f32[2,128,128]{2,1,0:T(8,128)S(1)} collective-permute-done((f32[2,128,128]{2,1,0:T(8,128)S(1)}, f32[2,128,128]{2,1,0:T(8,128)S(1)}, u32[]{:S(2)}, u32[]{:S(2)}) %collective-permute-start.18) | collective-permute-done | bytes 131104 | tf_op jit(solution)/shard_map/ppermute | solution.py:209
  40.0 1.2 %collective-permute-done.17.other = f32[2,128,128]{2,1,0:T(8,128)S(1)} collective-permute-done((f32[2,128,128]{2,1,0:T(8,128)S(1)}, f32[2,128,128]{2,1,0:T(8,128)S(1)}, u32[]{:S(2)}, u32[]{:S(2)}) %collective-permute-start.17) | collective-permute-done | bytes 131104 | tf_op jit(solution)/shard_map/ppermute | solution.py:209
  41.5 1.1 collective-permute-done.16.other
  43.1 1.5 %collective-permute-start.21 = (f32[2,256]{1,0:T(2,128)S(1)}, f32[2,256]{1,0:T(2,128)S(1)}, u32[]{:S(2)}, u32[]{:S(2)}) collective-permute-start(f32[2,256]{1,0:T(2,128)S(1)} %get-tuple-element.150.refs_0_), channel_id=1, source_target_pairs={{0,2},{1,3},{2,0},{3,1},{4,6},{5,7},{6,4},{7,5},{8,10},{9,11},{10,... | collective-permute-start | bytes 6152 | tf_op jit(solution)/shard_map/ppermute | solution.py:295
  44.9 1.1 %collective-permute-done.22.refs_3_ = f32[2,256]{1,0:T(2,128)S(1)} collective-permute-done((f32[2,256]{1,0:T(2,128)S(1)}, f32[2,256]{1,0:T(2,128)S(1)}, u32[]{:S(2)}, u32[]{:S(2)}) %collective-permute-start.22) | collective-permute-done | bytes 2080 | tf_op jit(solution)/shard_map/ppermute | solution.py:295
  47.4 1.2 %collective-permute-start.25 = (f32[2,128,128]{2,1,0:T(8,128)S(1)}, f32[2,128,128]{2,1,0:T(8,128)S(1)}, u32[]{:S(2)}, u32[]{:S(2)}) collective-permute-start(f32[2,128,128]{2,1,0:T(8,128)S(1)} %get-tuple-element.174), channel_id=1, source_target_pairs={{0,4},{4,0},{8,12},{12,8},{16,20},{20,16},{24,28},{28,24},{1,5},{5... | collective-permute-start | bytes 393224 | tf_op jit(solution)/shard_map/ppermute | solution.py:179
  48.6 0.9 collective-permute-start.24
  50.1 3.6 %shard_map.85 = (bf16[256,256]{1,0:T(8,128)(2,1)}, bf16[256,256]{1,0:T(8,128)(2,1)}, f32[256,256]{1,0:T(8,128)}, f32[256,256]{1,0:T(8,128)}, f32[256,256]{1,0:T(8,128)}, /*index=5*/f32[256,256]{1,0:T(8,128)}) custom-call(s32[1]{0:T(128)} %bitcast.place, bf16[256,2048]{1,0:T(8,128)(2,1)S(1)} %copy-done, bf16[256,2048]{1,0:T(8,128)(2,1)S(1)} %copy-done, ...), custom_call_target="tpu_custom_call" | custom-call | flops 301989888 | bytes 5439488 | tf_op jit(solution)/shard_map/pallas_call | solution.py:44
  54.5 1.2 %collective-permute-start.27 = (f32[2,128,128]{2,1,0:T(8,128)S(1)}, f32[2,128,128]{2,1,0:T(8,128)S(1)}, u32[]{:S(2)}, u32[]{:S(2)}) collective-permute-start(f32[2,128,128]{2,1,0:T(8,128)S(1)} %get-tuple-element.183), channel_id=1, source_target_pairs={{0,4},{4,0},{8,12},{12,8},{16,20},{20,16},{24,28},{28,24},{1,5},{5... | collective-permute-start | bytes 393224 | tf_op jit(solution)/shard_map/ppermute | solution.py:179
  56.0 0.7 add.174
  56.7 1.3 %collective-permute-start.26 = (f32[2,128,128]{2,1,0:T(8,128)}, f32[2,128,128]{2,1,0:T(8,128)}, u32[]{:S(2)}, u32[]{:S(2)}) collective-permute-start(f32[2,128,128]{2,1,0:T(8,128)} %add.174), channel_id=1, source_target_pairs={{28,20},{24,16},{29,21},{25,17},{30,22},{26,18},{31,23},{27,19}} | collective-permute-start | bytes 393224 | tf_op jit(solution)/shard_map/ppermute | solution.py:162
  58.0 1.2 %collective-permute-start.23 = (f32[2,128,128]{2,1,0:T(8,128)S(1)}, f32[2,128,128]{2,1,0:T(8,128)S(1)}, u32[]{:S(2)}, u32[]{:S(2)}) collective-permute-start(f32[2,128,128]{2,1,0:T(8,128)S(1)} %get-tuple-element.170), channel_id=1, source_target_pairs={{0,4},{4,0},{8,12},{12,8},{16,20},{20,16},{24,28},{28,24},{1,5},{5... | collective-permute-start | bytes 393224 | tf_op jit(solution)/shard_map/ppermute | solution.py:179
  59.2 0.7 add.175
  59.8 1.3 %collective-permute-start.32 = (f32[2,128,128]{2,1,0:T(8,128)}, f32[2,128,128]{2,1,0:T(8,128)}, u32[]{:S(2)}, u32[]{:S(2)}) collective-permute-start(f32[2,128,128]{2,1,0:T(8,128)} %add.175), channel_id=1, source_target_pairs={{20,12},{16,8},{21,13},{17,9},{22,14},{18,10},{23,15},{19,11}} | collective-permute-start | bytes 393224 | tf_op jit(solution)/shard_map/ppermute | solution.py:162
  61.2 3.7 %shard_map.86 = (bf16[256,256]{1,0:T(8,128)(2,1)}, bf16[256,256]{1,0:T(8,128)(2,1)}, f32[256,256]{1,0:T(8,128)}, f32[256,256]{1,0:T(8,128)}, f32[256,256]{1,0:T(8,128)}, /*index=5*/f32[256,256]{1,0:T(8,128)}) custom-call(s32[1]{0:T(128)} %bitcast.place, bf16[256,2048]{1,0:T(8,128)(2,1)S(1)} %copy-done, bf16[256,2048]{1,0:T(8,128)(2,1)S(1)} %copy-done, ...), custom_call_target="tpu_custom_call" | custom-call | flops 301989888 | bytes 5439488 | tf_op jit(solution)/shard_map/pallas_call | solution.py:44
  65.5 1.0 add.177
  67.9 0.9 fusion.3
  68.9 1.3 %collective-permute-start.36 = (f32[2,128,128]{2,1,0:T(8,128)S(1)}, f32[2,128,128]{2,1,0:T(8,128)S(1)}, u32[]{:S(2)}, u32[]{:S(2)}) collective-permute-start(f32[2,128,128]{2,1,0:T(8,128)S(1)} %get-tuple-element.249), channel_id=1, source_target_pairs={{12,4},{8,0},{13,5},{9,1},{14,6},{10,2},{15,7},{11,3}} | collective-permute-start | bytes 393224 | tf_op jit(solution)/shard_map/ppermute | solution.py:162
  70.9 1.0 fusion.2
  71.9 1.3 %collective-permute-start.34 = (f32[2,128,128]{2,1,0:T(8,128)S(1)}, f32[2,128,128]{2,1,0:T(8,128)S(1)}, u32[]{:S(2)}, u32[]{:S(2)}) collective-permute-start(f32[2,128,128]{2,1,0:T(8,128)S(1)} %get-tuple-element.247), channel_id=1, source_target_pairs={{12,4},{8,0},{13,5},{9,1},{14,6},{10,2},{15,7},{11,3}} | collective-permute-start | bytes 393224 | tf_op jit(solution)/shard_map/ppermute | solution.py:162
  73.9 4.7 %collective-permute-done.36 = f32[2,128,128]{2,1,0:T(8,128)S(1)} collective-permute-done((f32[2,128,128]{2,1,0:T(8,128)S(1)}, f32[2,128,128]{2,1,0:T(8,128)S(1)}, u32[]{:S(2)}, u32[]{:S(2)}) %collective-permute-start.36) | collective-permute-done | bytes 131104 | tf_op jit(solution)/shard_map/ppermute | solution.py:162
  79.2 1.3 %collective-permute-start.38 = (f32[2,128,128]{2,1,0:T(8,128)S(1)}, f32[2,128,128]{2,1,0:T(8,128)S(1)}, u32[]{:S(2)}, u32[]{:S(2)}) collective-permute-start(f32[2,128,128]{2,1,0:T(8,128)S(1)} %get-tuple-element.243), channel_id=1, source_target_pairs={{12,4},{8,0},{13,5},{9,1},{14,6},{10,2},{15,7},{11,3}} | collective-permute-start | bytes 393224 | tf_op jit(solution)/shard_map/ppermute | solution.py:162
  80.5 6.6 %collective-permute-done.34 = f32[2,128,128]{2,1,0:T(8,128)S(1)} collective-permute-done((f32[2,128,128]{2,1,0:T(8,128)S(1)}, f32[2,128,128]{2,1,0:T(8,128)S(1)}, u32[]{:S(2)}, u32[]{:S(2)}) %collective-permute-start.34) | collective-permute-done | bytes 131104 | tf_op jit(solution)/shard_map/ppermute | solution.py:162
  87.2 1.5 %collective-permute-start.37 = (f32[2,128,128]{2,1,0:T(8,128)S(1)}, f32[2,128,128]{2,1,0:T(8,128)S(1)}, u32[]{:S(2)}, u32[]{:S(2)}) collective-permute-start(f32[2,128,128]{2,1,0:T(8,128)S(1)} %get-tuple-element.239), channel_id=1, source_target_pairs={{12,4},{8,0},{13,5},{9,1},{14,6},{10,2},{15,7},{11,3}} | collective-permute-start | bytes 393224 | tf_op jit(solution)/shard_map/ppermute | solution.py:162
  88.6 1.9 %collective-permute-done.38 = f32[2,128,128]{2,1,0:T(8,128)S(1)} collective-permute-done((f32[2,128,128]{2,1,0:T(8,128)S(1)}, f32[2,128,128]{2,1,0:T(8,128)S(1)}, u32[]{:S(2)}, u32[]{:S(2)}) %collective-permute-start.38) | collective-permute-done | bytes 131104 | tf_op jit(solution)/shard_map/ppermute | solution.py:162
  90.5 1.7 %collective-permute-start.40 = (f32[2,128,128]{2,1,0:T(8,128)S(1)}, f32[2,128,128]{2,1,0:T(8,128)S(1)}, u32[]{:S(2)}, u32[]{:S(2)}) collective-permute-start(f32[2,128,128]{2,1,0:T(8,128)S(1)} %get-tuple-element.237), channel_id=1, source_target_pairs={{0,4},{4,0},{8,12},{12,8},{16,20},{20,16},{24,28},{28,24},{1,5},{5... | collective-permute-start | bytes 393224 | tf_op jit(solution)/shard_map/ppermute | solution.py:209
  92.3 2.3 %collective-permute-done.37 = f32[2,128,128]{2,1,0:T(8,128)S(1)} collective-permute-done((f32[2,128,128]{2,1,0:T(8,128)S(1)}, f32[2,128,128]{2,1,0:T(8,128)S(1)}, u32[]{:S(2)}, u32[]{:S(2)}) %collective-permute-start.37) | collective-permute-done | bytes 131104 | tf_op jit(solution)/shard_map/ppermute | solution.py:162
  94.6 1.5 %collective-permute-start.39 = (f32[2,128,128]{2,1,0:T(8,128)S(1)}, f32[2,128,128]{2,1,0:T(8,128)S(1)}, u32[]{:S(2)}, u32[]{:S(2)}) collective-permute-start(f32[2,128,128]{2,1,0:T(8,128)S(1)} %get-tuple-element.235), channel_id=1, source_target_pairs={{0,4},{4,0},{8,12},{12,8},{16,20},{20,16},{24,28},{28,24},{1,5},{5... | collective-permute-start | bytes 393224 | tf_op jit(solution)/shard_map/ppermute | solution.py:209
  96.1 3.6 %shard_map.84 = (bf16[256,256]{1,0:T(8,128)(2,1)}, bf16[256,256]{1,0:T(8,128)(2,1)}, f32[256,256]{1,0:T(8,128)}, f32[256,256]{1,0:T(8,128)}, f32[256,256]{1,0:T(8,128)}, /*index=5*/f32[256,256]{1,0:T(8,128)}) custom-call(s32[1]{0:T(128)} %bitcast.place, bf16[256,2048]{1,0:T(8,128)(2,1)S(1)} %copy-done, bf16[256,2048]{1,0:T(8,128)(2,1)S(1)} %copy-done, ...), custom_call_target="tpu_custom_call" | custom-call | flops 301989888 | bytes 5439488 | tf_op jit(solution)/shard_map/pallas_call | solution.py:44
  99.7 3.6 %shard_map.87 = (bf16[256,256]{1,0:T(8,128)(2,1)}, bf16[256,256]{1,0:T(8,128)(2,1)}, f32[256,256]{1,0:T(8,128)}, f32[256,256]{1,0:T(8,128)}, f32[256,256]{1,0:T(8,128)}, /*index=5*/f32[256,256]{1,0:T(8,128)}) custom-call(s32[1]{0:T(128)} %bitcast.place, bf16[256,2048]{1,0:T(8,128)(2,1)S(1)} %copy-done, bf16[256,2048]{1,0:T(8,128)(2,1)S(1)} %copy-done, ...), custom_call_target="tpu_custom_call" | custom-call | flops 301989888 | bytes 5439488 | tf_op jit(solution)/shard_map/pallas_call | solution.py:44
  103.3 2.8 %shard_map.88 = (bf16[256,2048]{1,0:T(8,128)(2,1)}, bf16[256,2048]{1,0:T(8,128)(2,1)}, bf16[256,2048]{1,0:T(8,128)(2,1)}) custom-call(s32[1]{0:T(128)} %bitcast.place, bf16[256,256]{1,0:T(8,128)(2,1)} %get-tuple-element.179.qk, bf16[256,256]{1,0:T(8,128)(2,1)} %get-tuple-element.218.qo, f32[256,256]{1,0:T(8,128)} %get-tuple-element.219.kk, ...), custom_call_target="tpu_custom_call" | custom-call | flops 67108864 | bytes 1900544 | tf_op jit(solution)/shard_map/pallas_call | solution.py:44
  106.0 2.8 %shard_map.89 = (bf16[256,2048]{1,0:T(8,128)(2,1)}, bf16[256,2048]{1,0:T(8,128)(2,1)}, bf16[256,2048]{1,0:T(8,128)(2,1)}) custom-call(s32[1]{0:T(128)} %bitcast.place, bf16[256,256]{1,0:T(8,128)(2,1)} %get-tuple-element.189.qk, bf16[256,256]{1,0:T(8,128)(2,1)} %get-tuple-element.213.qo, ...), custom_call_target="tpu_custom_call", output_to_operand_aliasing={{0}: (12, {}), {1}: (13, {}), {2}: (14, {})} | custom-call | flops 67108864 | bytes 3473408 | tf_op jit(solution)/shard_map/pallas_call | solution.py:44
  108.8 2.8 %shard_map.90 = (bf16[256,2048]{1,0:T(8,128)(2,1)}, bf16[256,2048]{1,0:T(8,128)(2,1)}, bf16[256,2048]{1,0:T(8,128)(2,1)}) custom-call(s32[1]{0:T(128)} %bitcast.place, bf16[256,256]{1,0:T(8,128)(2,1)} %get-tuple-element.207.qk, bf16[256,256]{1,0:T(8,128)(2,1)} %get-tuple-element.208.qo, ...), custom_call_target="tpu_custom_call", output_to_operand_aliasing={{0}: (12, {}), {1}: (13, {}), {2}: (14, {})} | custom-call | flops 67108864 | bytes 3473408 | tf_op jit(solution)/shard_map/pallas_call | solution.py:44
  111.7 2.8 %shard_map.91 = (bf16[256,2048]{1,0:T(8,128)(2,1)}, bf16[256,2048]{1,0:T(8,128)(2,1)}, bf16[256,2048]{1,0:T(8,128)(2,1)}) custom-call(s32[1]{0:T(128)} %bitcast.place, bf16[256,256]{1,0:T(8,128)(2,1)} %get-tuple-element.163.qk, bf16[256,256]{1,0:T(8,128)(2,1)} %get-tuple-element.164.qo, ...), custom_call_target="tpu_custom_call", output_to_operand_aliasing={{0}: (12, {}), {1}: (13, {}), {2}: (14, {})} | custom-call | flops 67108864 | bytes 3473408 | tf_op jit(solution)/shard_map/pallas_call | solution.py:44
  (103 shorter events, 14.0 us)
Async XLA Ops:
  2.2 9.1 %collective-permute-start.2 = (f32[2,128,128]{2,1,0:T(8,128)S(1)}, f32[2,128,128]{2,1,0:T(8,128)S(1)}, u32[]{:S(2)}, u32[]{:S(2)}) collective-permute-start(f32[2,128,128]{2,1,0:T(8,128)S(1)} %get-tuple-element.126), channel_id=1, source_target_pairs={{0,4},{4,0},{8,12},{12,8},{16,20},{20,16},{24,28},{28,24},{1,5},{5... | collective-permute-start | bytes 393224 | tf_op jit(solution)/shard_map/ppermute | solution.py:179
  5.2 11.7 %collective-permute-start.1 = (f32[2,128,128]{2,1,0:T(8,128)S(1)}, f32[2,128,128]{2,1,0:T(8,128)S(1)}, u32[]{:S(2)}, u32[]{:S(2)}) collective-permute-start(f32[2,128,128]{2,1,0:T(8,128)S(1)} %get-tuple-element.124), channel_id=1, source_target_pairs={{0,4},{4,0},{8,12},{12,8},{16,20},{20,16},{24,28},{28,24},{1,5},{5... | collective-permute-start | bytes 393224 | tf_op jit(solution)/shard_map/ppermute | solution.py:179
  11.3 7.4 %collective-permute-start.5 = (f32[2,128,128]{2,1,0:T(8,128)S(1)}, f32[2,128,128]{2,1,0:T(8,128)S(1)}, u32[]{:S(2)}, u32[]{:S(2)}) collective-permute-start(f32[2,128,128]{2,1,0:T(8,128)S(1)} %add.149), channel_id=1, source_target_pairs={{0,8},{4,12},{1,9},{5,13},{2,10},{6,14},{3,11},{7,15}} | collective-permute-start | bytes 393224 | tf_op jit(solution)/shard_map/ppermute | solution.py:162
  15.3 5.7 %collective-permute-start.4 = (f32[2,128,128]{2,1,0:T(8,128)S(1)}, f32[2,128,128]{2,1,0:T(8,128)S(1)}, u32[]{:S(2)}, u32[]{:S(2)}) collective-permute-start(f32[2,128,128]{2,1,0:T(8,128)S(1)} %get-tuple-element.129), channel_id=1, source_target_pairs={{0,4},{4,0},{8,12},{12,8},{16,20},{20,16},{24,28},{28,24},{1,5},{5... | collective-permute-start | bytes 393224 | tf_op jit(solution)/shard_map/ppermute | solution.py:179
  16.9 6.9 %collective-permute-start.3 = (f32[2,128,128]{2,1,0:T(8,128)S(1)}, f32[2,128,128]{2,1,0:T(8,128)S(1)}, u32[]{:S(2)}, u32[]{:S(2)}) collective-permute-start(f32[2,128,128]{2,1,0:T(8,128)S(1)} %add.150), channel_id=1, source_target_pairs={{0,8},{4,12},{1,9},{5,13},{2,10},{6,14},{3,11},{7,15}} | collective-permute-start | bytes 393224 | tf_op jit(solution)/shard_map/ppermute | solution.py:162
  18.3 6.3 %collective-permute-start = (f32[2,128,128]{2,1,0:T(8,128)S(1)}, f32[2,128,128]{2,1,0:T(8,128)S(1)}, u32[]{:S(2)}, u32[]{:S(2)}) collective-permute-start(f32[2,128,128]{2,1,0:T(8,128)S(1)} %get-tuple-element.122), channel_id=1, source_target_pairs={{0,4},{4,0},{8,12},{12,8},{16,20},{20,16},{24,28},{28,24},{1,5},{5... | collective-permute-start | bytes 393224 | tf_op jit(solution)/shard_map/ppermute | solution.py:179
  18.8 7.8 %collective-permute-start.9 = (f32[2,128,128]{2,1,0:T(8,128)S(1)}, f32[2,128,128]{2,1,0:T(8,128)S(1)}, u32[]{:S(2)}, u32[]{:S(2)}) collective-permute-start(f32[2,128,128]{2,1,0:T(8,128)S(1)} %add.151), channel_id=1, source_target_pairs={{8,16},{12,20},{9,17},{13,21},{10,18},{14,22},{11,19},{15,23}} | collective-permute-start | bytes 393224 | tf_op jit(solution)/shard_map/ppermute | solution.py:162
  21.0 6.6 %collective-permute-start.8 = (f32[2,128,128]{2,1,0:T(8,128)S(1)}, f32[2,128,128]{2,1,0:T(8,128)S(1)}, u32[]{:S(2)}, u32[]{:S(2)}) collective-permute-start(f32[2,128,128]{2,1,0:T(8,128)S(1)} %add.152), channel_id=1, source_target_pairs={{0,8},{4,12},{1,9},{5,13},{2,10},{6,14},{3,11},{7,15}} | collective-permute-start | bytes 393224 | tf_op jit(solution)/shard_map/ppermute | solution.py:162
  23.9 4.4 %collective-permute-start.7 = (f32[2,128,128]{2,1,0:T(8,128)S(1)}, f32[2,128,128]{2,1,0:T(8,128)S(1)}, u32[]{:S(2)}, u32[]{:S(2)}) collective-permute-start(f32[2,128,128]{2,1,0:T(8,128)S(1)} %add.153), channel_id=1, source_target_pairs={{8,16},{12,20},{9,17},{13,21},{10,18},{14,22},{11,19},{15,23}} | collective-permute-start | bytes 393224 | tf_op jit(solution)/shard_map/ppermute | solution.py:162
  24.6 4.6 %collective-permute-start.6 = (f32[2,128,128]{2,1,0:T(8,128)S(1)}, f32[2,128,128]{2,1,0:T(8,128)S(1)}, u32[]{:S(2)}, u32[]{:S(2)}) collective-permute-start(f32[2,128,128]{2,1,0:T(8,128)S(1)} %add.154), channel_id=1, source_target_pairs={{0,8},{4,12},{1,9},{5,13},{2,10},{6,14},{3,11},{7,15}} | collective-permute-start | bytes 393224 | tf_op jit(solution)/shard_map/ppermute | solution.py:162
  26.6 3.4 %collective-permute-start.13 = (f32[2,128,128]{2,1,0:T(8,128)S(1)}, f32[2,128,128]{2,1,0:T(8,128)S(1)}, u32[]{:S(2)}, u32[]{:S(2)}) collective-permute-start(f32[2,128,128]{2,1,0:T(8,128)S(1)} %get-tuple-element.265), channel_id=1, source_target_pairs={{16,24},{20,28},{17,25},{21,29},{18,26},{22,30},{19,27},{23,31}} | collective-permute-start | bytes 393224 | tf_op jit(solution)/shard_map/ppermute | solution.py:162
  27.6 4.9 %collective-permute-start.12 = (f32[2,128,128]{2,1,0:T(8,128)S(1)}, f32[2,128,128]{2,1,0:T(8,128)S(1)}, u32[]{:S(2)}, u32[]{:S(2)}) collective-permute-start(f32[2,128,128]{2,1,0:T(8,128)S(1)} %add.157), channel_id=1, source_target_pairs={{8,16},{12,20},{9,17},{13,21},{10,18},{14,22},{11,19},{15,23}} | collective-permute-start | bytes 393224 | tf_op jit(solution)/shard_map/ppermute | solution.py:162
  28.3 7.9 %copy-start.7 = (bf16[2048]{0:T(1024)(128)(2,1)S(1)}, bf16[2048]{0:T(1024)(128)(2,1)}, u32[]{:S(2)}) copy-start(bf16[2048]{0:T(1024)(128)(2,1)} %param.9) | copy-start | bytes 12292
  28.3 8.3 %copy-start = (bf16[256,2048]{1,0:T(8,128)(2,1)S(1)}, bf16[256,2048]{1,0:T(8,128)(2,1)}, u32[]{:S(2)}) copy-start(bf16[256,2048]{1,0:T(8,128)(2,1)} %refs_1_.7) | copy-start | bytes 3145732
  28.4 8.3 %copy-start.1 = (f32[256,2048]{1,0:T(8,128)S(1)}, f32[256,2048]{1,0:T(8,128)}, u32[]{:S(2)}) copy-start(f32[256,2048]{1,0:T(8,128)} %get-tuple-element.120.al_k.al_o) | copy-start | bytes 6291460
  28.4 8.3 %copy-start.2 = (bf16[256,2048]{1,0:T(8,128)(2,1)S(1)}, bf16[256,2048]{1,0:T(8,128)(2,1)}, u32[]{:S(2)}) copy-start(bf16[256,2048]{1,0:T(8,128)(2,1)} %refs_9_.3) | copy-start | bytes 3145732
  28.4 4.8 %collective-permute-start.11 = (f32[2,128,128]{2,1,0:T(8,128)S(1)}, f32[2,128,128]{2,1,0:T(8,128)S(1)}, u32[]{:S(2)}, u32[]{:S(2)}) collective-permute-start(f32[2,128,128]{2,1,0:T(8,128)S(1)} %get-tuple-element.263), channel_id=1, source_target_pairs={{16,24},{20,28},{17,25},{21,29},{18,26},{22,30},{19,27},{23,31}} | collective-permute-start | bytes 393224 | tf_op jit(solution)/shard_map/ppermute | solution.py:162
  29.2 4.1 %collective-permute-start.10 = (f32[2,128,128]{2,1,0:T(8,128)S(1)}, f32[2,128,128]{2,1,0:T(8,128)S(1)}, u32[]{:S(2)}, u32[]{:S(2)}) collective-permute-start(f32[2,128,128]{2,1,0:T(8,128)S(1)} %add.160), channel_id=1, source_target_pairs={{8,16},{12,20},{9,17},{13,21},{10,18},{14,22},{11,19},{15,23}} | collective-permute-start | bytes 393224 | tf_op jit(solution)/shard_map/ppermute | solution.py:162
  30.1 6.6 %collective-permute-start.19 = (f32[2,128,128]{2,1,0:T(8,128)S(1)}, f32[2,128,128]{2,1,0:T(8,128)S(1)}, u32[]{:S(2)}, u32[]{:S(2)}) collective-permute-start(f32[2,128,128]{2,1,0:T(8,128)S(1)} %get-tuple-element.261), channel_id=1, source_target_pairs={{0,4},{4,0},{8,12},{12,8},{16,20},{20,16},{24,28},{28,24},{1,5},{5... | collective-permute-start | bytes 393224 | tf_op jit(solution)/shard_map/ppermute | solution.py:209
  32.5 1.5 %collective-permute-start.15 = (f32[2,128,128]{2,1,0:T(8,128)S(1)}, f32[2,128,128]{2,1,0:T(8,128)S(1)}, u32[]{:S(2)}, u32[]{:S(2)}) collective-permute-start(f32[2,128,128]{2,1,0:T(8,128)S(1)} %get-tuple-element.259), channel_id=1, source_target_pairs={{16,24},{20,28},{17,25},{21,29},{18,26},{22,30},{19,27},{23,31}} | collective-permute-start | bytes 393224 | tf_op jit(solution)/shard_map/ppermute | solution.py:162
  33.2 6.5 %collective-permute-start.18 = (f32[2,128,128]{2,1,0:T(8,128)S(1)}, f32[2,128,128]{2,1,0:T(8,128)S(1)}, u32[]{:S(2)}, u32[]{:S(2)}) collective-permute-start(f32[2,128,128]{2,1,0:T(8,128)S(1)} %get-tuple-element.257), channel_id=1, source_target_pairs={{0,4},{4,0},{8,12},{12,8},{16,20},{20,16},{24,28},{28,24},{1,5},{5... | collective-permute-start | bytes 393224 | tf_op jit(solution)/shard_map/ppermute | solution.py:209
  33.3 2.8 %collective-permute-start.14 = (f32[2,128,128]{2,1,0:T(8,128)S(1)}, f32[2,128,128]{2,1,0:T(8,128)S(1)}, u32[]{:S(2)}, u32[]{:S(2)}) collective-permute-start(f32[2,128,128]{2,1,0:T(8,128)S(1)} %get-tuple-element.255), channel_id=1, source_target_pairs={{16,24},{20,28},{17,25},{21,29},{18,26},{22,30},{19,27},{23,31}} | collective-permute-start | bytes 393224 | tf_op jit(solution)/shard_map/ppermute | solution.py:162
  34.1 7.1 %collective-permute-start.17 = (f32[2,128,128]{2,1,0:T(8,128)S(1)}, f32[2,128,128]{2,1,0:T(8,128)S(1)}, u32[]{:S(2)}, u32[]{:S(2)}) collective-permute-start(f32[2,128,128]{2,1,0:T(8,128)S(1)} %get-tuple-element.253), channel_id=1, source_target_pairs={{0,4},{4,0},{8,12},{12,8},{16,20},{20,16},{24,28},{28,24},{1,5},{5... | collective-permute-start | bytes 393224 | tf_op jit(solution)/shard_map/ppermute | solution.py:209
  36.2 6.4 %collective-permute-start.16 = (f32[2,128,128]{2,1,0:T(8,128)S(1)}, f32[2,128,128]{2,1,0:T(8,128)S(1)}, u32[]{:S(2)}, u32[]{:S(2)}) collective-permute-start(f32[2,128,128]{2,1,0:T(8,128)S(1)} %get-tuple-element.251), channel_id=1, source_target_pairs={{0,4},{4,0},{8,12},{12,8},{16,20},{20,16},{24,28},{28,24},{1,5},{5... | collective-permute-start | bytes 393224 | tf_op jit(solution)/shard_map/ppermute | solution.py:209
  43.0 3.1 %collective-permute-start.22 = (f32[2,256]{1,0:T(2,128)S(1)}, f32[2,256]{1,0:T(2,128)S(1)}, u32[]{:S(2)}, u32[]{:S(2)}) collective-permute-start(f32[2,256]{1,0:T(2,128)S(1)} %get-tuple-element.150.refs_0_), channel_id=1, source_target_pairs={{0,3},{1,2},{2,1},{3,0},{4,7},{5,6},{6,5},{7,4},{8,11},{9,10},{10,... | collective-permute-start | bytes 6152 | tf_op jit(solution)/shard_map/ppermute | solution.py:295
  43.1 3.7 %collective-permute-start.21 = (f32[2,256]{1,0:T(2,128)S(1)}, f32[2,256]{1,0:T(2,128)S(1)}, u32[]{:S(2)}, u32[]{:S(2)}) collective-permute-start(f32[2,256]{1,0:T(2,128)S(1)} %get-tuple-element.150.refs_0_), channel_id=1, source_target_pairs={{0,2},{1,3},{2,0},{3,1},{4,6},{5,7},{6,4},{7,5},{8,10},{9,11},{10,... | collective-permute-start | bytes 6152 | tf_op jit(solution)/shard_map/ppermute | solution.py:295
  44.6 2.1 %collective-permute-start.20 = (f32[2,256]{1,0:T(2,128)S(1)}, f32[2,256]{1,0:T(2,128)S(1)}, u32[]{:S(2)}, u32[]{:S(2)}) collective-permute-start(f32[2,256]{1,0:T(2,128)S(1)} %get-tuple-element.150.refs_0_), channel_id=1, source_target_pairs={{0,1},{1,0},{2,3},{3,2},{4,5},{5,4},{6,7},{7,6},{8,9},{9,8},{10,11... | collective-permute-start | bytes 6152 | tf_op jit(solution)/shard_map/ppermute | solution.py:295
  47.4 6.4 %collective-permute-start.25 = (f32[2,128,128]{2,1,0:T(8,128)S(1)}, f32[2,128,128]{2,1,0:T(8,128)S(1)}, u32[]{:S(2)}, u32[]{:S(2)}) collective-permute-start(f32[2,128,128]{2,1,0:T(8,128)S(1)} %get-tuple-element.174), channel_id=1, source_target_pairs={{0,4},{4,0},{8,12},{12,8},{16,20},{20,16},{24,28},{28,24},{1,5},{5... | collective-permute-start | bytes 393224 | tf_op jit(solution)/shard_map/ppermute | solution.py:179
  48.6 7.4 %collective-permute-start.24 = (f32[2,128,128]{2,1,0:T(8,128)S(1)}, f32[2,128,128]{2,1,0:T(8,128)S(1)}, u32[]{:S(2)}, u32[]{:S(2)}) collective-permute-start(f32[2,128,128]{2,1,0:T(8,128)S(1)} %get-tuple-element.172), channel_id=1, source_target_pairs={{0,4},{4,0},{8,12},{12,8},{16,20},{20,16},{24,28},{28,24},{1,5},{5... | collective-permute-start | bytes 393224 | tf_op jit(solution)/shard_map/ppermute | solution.py:179
  53.8 5.4 %collective-permute-start.28 = (f32[2,128,128]{2,1,0:T(8,128)S(1)}, f32[2,128,128]{2,1,0:T(8,128)S(1)}, u32[]{:S(2)}, u32[]{:S(2)}) collective-permute-start(f32[2,128,128]{2,1,0:T(8,128)S(1)} %add.173), channel_id=1, source_target_pairs={{28,20},{24,16},{29,21},{25,17},{30,22},{26,18},{31,23},{27,19}} | collective-permute-start | bytes 393224 | tf_op jit(solution)/shard_map/ppermute | solution.py:162
  54.5 10.4 %collective-permute-start.27 = (f32[2,128,128]{2,1,0:T(8,128)S(1)}, f32[2,128,128]{2,1,0:T(8,128)S(1)}, u32[]{:S(2)}, u32[]{:S(2)}) collective-permute-start(f32[2,128,128]{2,1,0:T(8,128)S(1)} %get-tuple-element.183), channel_id=1, source_target_pairs={{0,4},{4,0},{8,12},{12,8},{16,20},{20,16},{24,28},{28,24},{1,5},{5... | collective-permute-start | bytes 393224 | tf_op jit(solution)/shard_map/ppermute | solution.py:179
  56.7 8.9 %collective-permute-start.26 = (f32[2,128,128]{2,1,0:T(8,128)}, f32[2,128,128]{2,1,0:T(8,128)}, u32[]{:S(2)}, u32[]{:S(2)}) collective-permute-start(f32[2,128,128]{2,1,0:T(8,128)} %add.174), channel_id=1, source_target_pairs={{28,20},{24,16},{29,21},{25,17},{30,22},{26,18},{31,23},{27,19}} | collective-permute-start | bytes 393224 | tf_op jit(solution)/shard_map/ppermute | solution.py:162
  58.0 9.2 %collective-permute-start.23 = (f32[2,128,128]{2,1,0:T(8,128)S(1)}, f32[2,128,128]{2,1,0:T(8,128)S(1)}, u32[]{:S(2)}, u32[]{:S(2)}) collective-permute-start(f32[2,128,128]{2,1,0:T(8,128)S(1)} %get-tuple-element.170), channel_id=1, source_target_pairs={{0,4},{4,0},{8,12},{12,8},{16,20},{20,16},{24,28},{28,24},{1,5},{5... | collective-permute-start | bytes 393224 | tf_op jit(solution)/shard_map/ppermute | solution.py:179
  59.8 8.1 %collective-permute-start.32 = (f32[2,128,128]{2,1,0:T(8,128)}, f32[2,128,128]{2,1,0:T(8,128)}, u32[]{:S(2)}, u32[]{:S(2)}) collective-permute-start(f32[2,128,128]{2,1,0:T(8,128)} %add.175), channel_id=1, source_target_pairs={{20,12},{16,8},{21,13},{17,9},{22,14},{18,10},{23,15},{19,11}} | collective-permute-start | bytes 393224 | tf_op jit(solution)/shard_map/ppermute | solution.py:162
  61.2 6.8 %copy-start.6 = (f32[2,128,128]{2,1,0:T(8,128)S(1)}, f32[2,128,128]{2,1,0:T(8,128)}, u32[]{:S(2)}) copy-start(f32[2,128,128]{2,1,0:T(8,128)} %copy-done.5) | copy-start | bytes 393220
  64.9 5.3 %collective-permute-start.31 = (f32[2,128,128]{2,1,0:T(8,128)S(1)}, f32[2,128,128]{2,1,0:T(8,128)S(1)}, u32[]{:S(2)}, u32[]{:S(2)}) collective-permute-start(f32[2,128,128]{2,1,0:T(8,128)S(1)} %add.176), channel_id=1, source_target_pairs={{28,20},{24,16},{29,21},{25,17},{30,22},{26,18},{31,23},{27,19}} | collective-permute-start | bytes 393224 | tf_op jit(solution)/shard_map/ppermute | solution.py:162
  66.5 4.4 %collective-permute-start.30 = (f32[2,128,128]{2,1,0:T(8,128)S(1)}, f32[2,128,128]{2,1,0:T(8,128)S(1)}, u32[]{:S(2)}, u32[]{:S(2)}) collective-permute-start(f32[2,128,128]{2,1,0:T(8,128)S(1)} %add.177), channel_id=1, source_target_pairs={{20,12},{16,8},{21,13},{17,9},{22,14},{18,10},{23,15},{19,11}} | collective-permute-start | bytes 393224 | tf_op jit(solution)/shard_map/ppermute | solution.py:162
  67.2 6.0 %collective-permute-start.29 = (f32[2,128,128]{2,1,0:T(8,128)S(1)}, f32[2,128,128]{2,1,0:T(8,128)S(1)}, u32[]{:S(2)}, u32[]{:S(2)}) collective-permute-start(f32[2,128,128]{2,1,0:T(8,128)S(1)} %add.178), channel_id=1, source_target_pairs={{28,20},{24,16},{29,21},{25,17},{30,22},{26,18},{31,23},{27,19}} | collective-permute-start | bytes 393224 | tf_op jit(solution)/shard_map/ppermute | solution.py:162
  68.9 9.8 %collective-permute-start.36 = (f32[2,128,128]{2,1,0:T(8,128)S(1)}, f32[2,128,128]{2,1,0:T(8,128)S(1)}, u32[]{:S(2)}, u32[]{:S(2)}) collective-permute-start(f32[2,128,128]{2,1,0:T(8,128)S(1)} %get-tuple-element.249), channel_id=1, source_target_pairs={{12,4},{8,0},{13,5},{9,1},{14,6},{10,2},{15,7},{11,3}} | collective-permute-start | bytes 393224 | tf_op jit(solution)/shard_map/ppermute | solution.py:162
  70.2 8.9 %collective-permute-start.35 = (f32[2,128,128]{2,1,0:T(8,128)S(1)}, f32[2,128,128]{2,1,0:T(8,128)S(1)}, u32[]{:S(2)}, u32[]{:S(2)}) collective-permute-start(f32[2,128,128]{2,1,0:T(8,128)S(1)} %add.181), channel_id=1, source_target_pairs={{20,12},{16,8},{21,13},{17,9},{22,14},{18,10},{23,15},{19,11}} | collective-permute-start | bytes 393224 | tf_op jit(solution)/shard_map/ppermute | solution.py:162
  71.9 15.1 %collective-permute-start.34 = (f32[2,128,128]{2,1,0:T(8,128)S(1)}, f32[2,128,128]{2,1,0:T(8,128)S(1)}, u32[]{:S(2)}, u32[]{:S(2)}) collective-permute-start(f32[2,128,128]{2,1,0:T(8,128)S(1)} %get-tuple-element.247), channel_id=1, source_target_pairs={{12,4},{8,0},{13,5},{9,1},{14,6},{10,2},{15,7},{11,3}} | collective-permute-start | bytes 393224 | tf_op jit(solution)/shard_map/ppermute | solution.py:162
  73.2 13.9 %collective-permute-start.33 = (f32[2,128,128]{2,1,0:T(8,128)S(1)}, f32[2,128,128]{2,1,0:T(8,128)S(1)}, u32[]{:S(2)}, u32[]{:S(2)}) collective-permute-start(f32[2,128,128]{2,1,0:T(8,128)S(1)} %add.184), channel_id=1, source_target_pairs={{20,12},{16,8},{21,13},{17,9},{22,14},{18,10},{23,15},{19,11}} | collective-permute-start | bytes 393224 | tf_op jit(solution)/shard_map/ppermute | solution.py:162
  78.7 24.6 %collective-permute-start.42 = (f32[2,128,128]{2,1,0:T(8,128)S(1)}, f32[2,128,128]{2,1,0:T(8,128)S(1)}, u32[]{:S(2)}, u32[]{:S(2)}) collective-permute-start(f32[2,128,128]{2,1,0:T(8,128)S(1)} %get-tuple-element.245), channel_id=1, source_target_pairs={{0,4},{4,0},{8,12},{12,8},{16,20},{20,16},{24,28},{28,24},{1,5},{5... | collective-permute-start | bytes 393224 | tf_op jit(solution)/shard_map/ppermute | solution.py:209
  79.2 11.3 %collective-permute-start.38 = (f32[2,128,128]{2,1,0:T(8,128)S(1)}, f32[2,128,128]{2,1,0:T(8,128)S(1)}, u32[]{:S(2)}, u32[]{:S(2)}) collective-permute-start(f32[2,128,128]{2,1,0:T(8,128)S(1)} %get-tuple-element.243), channel_id=1, source_target_pairs={{12,4},{8,0},{13,5},{9,1},{14,6},{10,2},{15,7},{11,3}} | collective-permute-start | bytes 393224 | tf_op jit(solution)/shard_map/ppermute | solution.py:162
  87.0 19.0 %collective-permute-start.41 = (f32[2,128,128]{2,1,0:T(8,128)S(1)}, f32[2,128,128]{2,1,0:T(8,128)S(1)}, u32[]{:S(2)}, u32[]{:S(2)}) collective-permute-start(f32[2,128,128]{2,1,0:T(8,128)S(1)} %get-tuple-element.241), channel_id=1, source_target_pairs={{0,4},{4,0},{8,12},{12,8},{16,20},{20,16},{24,28},{28,24},{1,5},{5... | collective-permute-start | bytes 393224 | tf_op jit(solution)/shard_map/ppermute | solution.py:209
  87.2 7.4 %collective-permute-start.37 = (f32[2,128,128]{2,1,0:T(8,128)S(1)}, f32[2,128,128]{2,1,0:T(8,128)S(1)}, u32[]{:S(2)}, u32[]{:S(2)}) collective-permute-start(f32[2,128,128]{2,1,0:T(8,128)S(1)} %get-tuple-element.239), channel_id=1, source_target_pairs={{12,4},{8,0},{13,5},{9,1},{14,6},{10,2},{15,7},{11,3}} | collective-permute-start | bytes 393224 | tf_op jit(solution)/shard_map/ppermute | solution.py:162
  90.5 18.3 %collective-permute-start.40 = (f32[2,128,128]{2,1,0:T(8,128)S(1)}, f32[2,128,128]{2,1,0:T(8,128)S(1)}, u32[]{:S(2)}, u32[]{:S(2)}) collective-permute-start(f32[2,128,128]{2,1,0:T(8,128)S(1)} %get-tuple-element.237), channel_id=1, source_target_pairs={{0,4},{4,0},{8,12},{12,8},{16,20},{20,16},{24,28},{28,24},{1,5},{5... | collective-permute-start | bytes 393224 | tf_op jit(solution)/shard_map/ppermute | solution.py:209
  94.6 17.0 %collective-permute-start.39 = (f32[2,128,128]{2,1,0:T(8,128)S(1)}, f32[2,128,128]{2,1,0:T(8,128)S(1)}, u32[]{:S(2)}, u32[]{:S(2)}) collective-permute-start(f32[2,128,128]{2,1,0:T(8,128)S(1)} %get-tuple-element.235), channel_id=1, source_target_pairs={{0,4},{4,0},{8,12},{12,8},{16,20},{20,16},{24,28},{28,24},{1,5},{5... | collective-permute-start | bytes 393224 | tf_op jit(solution)/shard_map/ppermute | solution.py:209
  (3 other events, 12.8 us)

commit v5 on v4

--- a/solution.py
+++ b/solution.py
@@ -23,10 +23,10 @@
     return ref[:, j * DH:(j + 1) * DH]
 
 
-def causal():
+def causal(turned=False):
     rows = lax.broadcasted_iota(jnp.int32, (GROUP, GROUP), 0)
     cols = lax.broadcasted_iota(jnp.int32, (GROUP, GROUP), 1)
-    return rows >= cols
+    return cols >= rows if turned else rows >= cols
 
 
 def masked(scores, mask):
@@ -64,7 +64,7 @@
 
 
 def local_body(per, chunks, heads, place, q, k, v, *refs):
-    outs, scores, attn = refs[:chunks], refs[chunks], refs[chunks + 1]
+    outs, attn = refs[:chunks], refs[chunks]
     for turn in range(2):
         @pl.when(pl.program_id(0) == turn)
         def _():
@@ -74,7 +74,6 @@
     mask = causal()
     for j in range(heads):
         s = masked(dot(head(q, j), head(k, j), 1, 1), mask)
-        scores[j] = s
         attn[:, j * DH:(j + 1) * DH] = dot(s, head(v, j), 1, 0)
 
 
@@ -82,11 +81,10 @@
     if not first:
         sq_in, cr_in, *refs = refs
     at_k, at_o, sb_k, sb_o, *stats = refs
-    second = place[0] == 1
     square = jnp.zeros((GROUP, DH), F32) if first else sq_in[...]
     cross = jnp.zeros((GROUP, DH), F32) if first else cr_in[...]
     for j in range(per):
-        kept = jnp.where(second, e[j] + r[j], e[j]).astype(BF16)
+        kept = (e[j] + r[j]).astype(BF16)
         sb_k[j] = kept
         sb_o[j] = other[j].astype(BF16)
         for al, q, g, n, sb, at in (
@@ -127,21 +125,32 @@
             outs[chunks + c][j] = dot(head(q, h), x, 0, 0)
 
 
-def grads_body(per, place, *refs):
-    (q_k, q_o, k_k, k_o, v_k, v_o, s_k, s_o, d_k, d_o, sb_k, sb_o) = refs[:12]
-    qg_k, qg_o, kg_k, kg_o, vg_k, vg_o = refs[12:]
+def query_body(per, place, k, v, d_k, d_o, sb_k, sb_o, *refs):
+    qg = refs[-1]
     mask = causal()
+    for turn, d, sb in ((0, d_k, sb_k), (1, d_o, sb_o)):
+        @pl.when(pl.program_id(0) == turn)
+        def _():
+            for j in range(per):
+                do = head(d, j)
+                ds = masked(dot(do, head(v, j), 1, 1), mask)
+                qg[:, j * DH:(j + 1) * DH] = (dot(ds, head(k, j), 1, 0) + dot(do, sb[j], 1, 1)).astype(BF16)
+
+
+def final_body(per, terms, place, q, k, v, d, *refs):
+    later_in, kg, vg = refs[:terms], refs[-2], refs[-1]
+    mask = causal(turned=True)
     for j in range(per):
         at = slice(j * DH, (j + 1) * DH)
-        for q, k, v, s, d, sb, qg, kg, vg in (
-            (q_k, k_k, v_k, s_k, d_k, sb_k, qg_k, kg_k, vg_k),
-            (q_o, k_o, v_o, s_o, d_o, sb_o, qg_o, kg_o, vg_o),
-        ):
-            do = head(d, j)
-            ds = masked(dot(do, head(v, j), 1, 1), mask)
-            qg[:, at] = (dot(ds, head(k, j), 1, 0) + dot(do, sb[j], 1, 1)).astype(BF16)
-            kg[:, at] = dot(ds, head(q, j), 0, 0)
-            vg[:, at] = dot(s[j], do, 0, 0)
+        later = later_in[0][j]
+        for term in later_in[1:]:
+            later = later + term[j]
+        later = later.astype(BF16)
+        qj, kj, vj, do = head(q, j), head(k, j), head(v, j), head(d, j)
+        ds = masked(dot(vj, do, 1, 1), mask)
+        st = masked(dot(kj, qj, 1, 1), mask)
+        kg[:, at] = (dot(ds, qj, 1, 0) + dot(vj, later, 1, 1)).astype(BF16)
+        vg[:, at] = (dot(st, do, 1, 0) + dot(kj, later, 1, 0)).astype(BF16)
 
 
 def solution(mesh):
@@ -175,40 +184,46 @@
             out.append(carry)
         return out
 
-    def scan(kept, sent, y, reverse, beside):
-        swapped = [lax.ppermute(b, "seq", swap) for b in sent]
+    def scan(kept, sent, y, reverse, ready):
+        own = [None] * len(kept)
         if long > 4 or long < 2:
+            swapped = [lax.ppermute(b, "seq", swap) for b in sent]
+            own = [jnp.where(y == 0, 0.0, r) for r in swapped]
             sums = [a + r for a, r in zip(kept, swapped)]
             sums = doubling(sums, reverse) if long > 1 else [jnp.zeros_like(a) for a in sums]
             others = [
                 lax.ppermute(jnp.where(y == 0, e + a, e), "seq", swap) for a, e in zip(kept, sums)
             ]
-            return list(zip(sums, swapped, others)), [work() for work in beside]
+            return list(zip(sums, own, others))
         chunks = len(kept)
         order = sorted((2 * stage + c, -stage, c, stage) for stage in range(long) for c in range(chunks))
-        part, flight, carry, out, done = {}, dict(enumerate(swapped)), {}, {}, []
-        last = []
-        for turn, (_, _, c, stage) in enumerate(order):
-            if turn in (0, 3) and len(done) < len(beside):
-                done.append(beside[len(done)]())
-                last.append(done[-1][0])
-            got = flight[c]
-            if last:
-                got, *_ = lax.optimization_barrier((got, *last))
+        part, flight, carry, out = {}, {}, {}, {}
+        last = ready
+
+        def swap_after(c, *things):
+            if c < chunks:
+                part_sent, *_ = lax.optimization_barrier((sent[c], *things))
+                flight[c] = lax.ppermute(part_sent, "seq", swap)
+
+        swap_after(0)
+        swap_after(1)
+        swap_after(2, *ready)
+        for _, _, c, stage in order:
+            got, *_ = lax.optimization_barrier((flight[c], *last))
             if stage == 0:
-                swapped[c] = got
+                own[c] = jnp.where(y == 0, 0.0, got)
                 part[c] = send = kept[c] + got
+                swap_after(c + 3, send)
             else:
                 carry[c] = got if stage == 1 else carry[c] + got
                 send = carry[c] + part[c]
             if stage < long - 1:
                 flight[c] = hop(send, lambda at: at == stage, 1, reverse)
-                last = [send]
             else:
                 send = jnp.where(y == 0, carry[c] + kept[c], carry[c])
-                out[c] = (carry[c], swapped[c], lax.ppermute(send, "seq", swap))
-                last = [send]
-        return [out[c] for c in range(chunks)], done + [work() for work in beside[len(done):]]
+                out[c] = (carry[c], own[c], lax.ppermute(send, "seq", swap))
+            last = [send]
+        return [out[c] for c in range(chunks)]
 
     def shards(queries, keys, values, out_grad, norm_gain):
         tokens, width = queries.shape
@@ -235,12 +250,6 @@
         def at_o(c):
             return lambda i, s: (0, (1 - s[0]) * CHUNKS + c)
 
-        def at_k3(c):
-            return lambda i, s: (s[0] * CHUNKS + c, 0, 0)
-
-        def at_o3(c):
-            return lambda i, s: ((1 - s[0]) * CHUNKS + c, 0, 0)
-
         sent = call(
             functools.partial(states_body, per), place,
             [(a, (tokens, wide), sent_half, HBM) for a in (keys, values)],
@@ -250,17 +259,16 @@
 
         group = half // 2
         strip = lambda i, s: (0, (2 * s[0] + i) % 4)
-        *kept, scores, attn_local = call(
+        *kept, attn_local = call(
             functools.partial(local_body, per, CHUNKS, group), place,
             [(a, (tokens, group * DH), strip, HBM) for a in (queries, keys, values)],
             [((per, DH, DH), F32, (per, DH, DH), whole3, VMEM)] * CHUNKS + [
-                ((heads, GROUP, GROUP), BF16, (group, GROUP, GROUP), lambda i, s: ((2 * s[0] + i) % 4, 0, 0), HBM),
-                ((tokens, width), F32, (tokens, group * DH), strip, HBM),
+                ((tokens, width), F32, (tokens, group * DH), strip, VMEM),
             ],
             grid=(4,), flops=heads * mac * (2 * GROUP + DH // 2),
         )
 
-        before, _ = scan(kept, sent, y, False, [])
+        before = scan(kept, sent, y, False, [attn_local])
 
         block = (tokens, narrow)
         square = cross = None
@@ -309,64 +317,41 @@
         d_o, sent = delta(1, sent_half)
         d_k, kept = delta(0, kept_half)
 
-        def grads(c):
-            ins = []
-            for a, m in ((queries, None), (keys, HBM), (values, HBM)):
-                ins += [(a, block, at_k(c), m), (a, block, at_o(c), m)]
-            ins += [(scores, (per, GROUP, GROUP), at(c), HBM) for at in (at_k3, at_o3)]
-            ins += [(d_k[c], block, whole2), (d_o[c], block, whole2)]
-            ins += [(a, (per, DH, DH), whole3) for a in priors[c]]
-            outs = [(block, BF16, block, whole2, HBM)] * 2 + [(block, F32, block, whole2, HBM)] * 4
-            return call(
-                functools.partial(grads_body, per), place, ins, outs,
-                flops=2 * per * mac * (4 * GROUP + DH))
-
-        after, grads = scan(
-            kept, sent, 1 - y, True, [functools.partial(grads, c) for c in range(CHUNKS)])
-
-        kg = vg = qg = None
+        def mine(c):
+            return lambda i, s: (0, jnp.where(i == 0, s[0], 1 - s[0]) * CHUNKS + c)
+
+        state3 = (per, DH, DH)
+        qg = None
         for c in range(CHUNKS):
-            e, r, other = after[c]
-            kg, vg, qg = finish(c, per, narrow, tokens, width, place, keys, values, grads[c], e, r, other, kg, vg, qg)
-        return qg, kg, vg
-
-    def finish(c, per, narrow, tokens, width, place, keys, values, grads, e, r, other, *done):
-        qg_k, qg_o, kl_k, kl_o, vl_k, vl_o = grads
-        block = (tokens, narrow)
-        mine = lambda i, s: (0, jnp.where(i == 0, s[0], 1 - s[0]) * CHUNKS + c)
-        whole2 = lambda i, s: (0, 0)
-        whole3 = lambda i, s: (0, 0, 0)
-        ins = [(a, block, whole2, HBM) for a in (qg_k, qg_o, kl_k, kl_o, vl_k, vl_o)]
-        ins += [(a, block, mine, HBM) for a in (keys, values)]
-        ins += [(a, (per, DH, DH), whole3) for a in (e, r, other)]
-        aliases = {}
-        if done[0] is not None:
-            for n, a in enumerate(done):
-                aliases[len(ins) + 1] = n
-                ins.append((a, None, None, HBM))
-        outs = [((tokens, width), BF16, block, mine, HBM)] * 3
-
-        def body(place, qk, qo, kk, ko, vk, vo, k, v, e, r, other, *refs):
-            kg, vg, qg = refs[-3:]
-            mine = pl.program_id(0) == 0
-
-            def one(q_in, k_in, v_in, state):
-                qg[...] = q_in[...]
-                for j in range(per):
-                    at = slice(j * DH, (j + 1) * DH)
-                    later = state(j).astype(BF16)
-                    kg[:, at] = (k_in[:, at] + dot(v[:, at], later, 1, 1)).astype(BF16)
-                    vg[:, at] = (v_in[:, at] + dot(k[:, at], later, 1, 0)).astype(BF16)
-
-            @pl.when(mine)
-            def _():
-                one(qk, kk, vk, lambda j: jnp.where(place[0] == 0, e[j] + r[j], e[j]))
-
-            @pl.when(jnp.logical_not(mine))
-            def _():
-                one(qo, ko, vo, lambda j: other[j])
-
-        return call(body, place, ins, outs, grid=(2,), aliases=aliases, flops=4 * per * 2 * GROUP * DH * DH)
+            ins = [(a, block, mine(c)) for a in (keys, values)]
+            ins += [(a, block, whole2) for a in (d_k[c], d_o[c])]
+            ins += [(a, state3, whole3) for a in priors[c]]
+            aliases = {}
+            if c > 0:
+                aliases[len(ins) + 1] = 0
+                ins.append((qg, None, None, HBM))
+            qg, = call(
+                functools.partial(query_body, per), place, ins, [((tokens, width), BF16, block, mine(c), HBM)],
+                grid=(2,), aliases=aliases, flops=2 * per * mac * (2 * GROUP + DH))
+
+        after = scan(kept, sent, 1 - y, True, [qg])
+
+        grads = None
+        turns = [(c, 0) for c in range(CHUNKS)] + [(c, 1) for c in range(CHUNKS)]
+        for c, which in turns:
+            index, d = ((at_k(c), d_k[c]), (at_o(c), d_o[c]))[which]
+            states = after[c][2:] if which else after[c][:2]
+            ins = [(a, block, index) for a in (queries, keys, values)]
+            ins += [(d, block, whole2)] + [(a, state3, whole3) for a in states]
+            aliases = {}
+            if grads is not None:
+                aliases = {len(ins) + 1: 0, len(ins) + 2: 1}
+                ins += [(a, None, None, HBM) for a in grads]
+            grads = call(
+                functools.partial(final_body, per, len(states)), place, ins,
+                [((tokens, width), BF16, block, index, HBM)] * 2,
+                aliases=aliases, flops=per * mac * (4 * GROUP + 2 * DH))
+        return qg, grads[0], grads[1]
 
     return jax.shard_map(
         shards,

time: 115 us -> 121 us (1.052)
  local copies, waits for them, and re-layouts: 0.05 us -> 15.5 us
  Pallas kernels: 35.7 us -> 26.3 us
  starting transfers between devices: 47.6 us -> 48.9 us
    unnamed x16 -> x84, local copies, waits for them, and re-layouts: 0.04 us -> 15.5 us
    pallas_call x16 -> x20, Pallas kernels: 35.7 us -> 26.3 us  [call(): pl.pallas_call(body, grid_spec=pltpu.PrefetchScalarGridSpec(num_scalar_pr...]
    ppermute x16, waiting for transfers between devices: 7.32 us -> 2.1 us  [the longest x8 1.49 us: swap_after(): flight[c] = lax.ppermute(part_sent, 'seq', swap)]
    ppermute x24, waiting for transfers between devices: 15.8 us -> 20.4 us  [hop(): return lax.ppermute(array, 'seq', pairs)]
    add x16, other arithmetic: 3.88 us -> 0.33 us  [scan(): send = carry[c] + part[c]]
    select_n x0 -> x8, other arithmetic: none -> 2.89 us  [scan(): own[c] = jnp.where(y == 0, 0.0, got)]
  transfers between devices with their start and end apart: 43 -> 43, of which waited for: 13 -> 11; matrix products, arithmetic and copies ran while one was open for 4% -> 4% of each run, Pallas kernels for 26% -> 18%
where the time goes in v5:
time: 121 us
  starting transfers between devices  48.9 us (40%)
  Pallas kernels  26.3 us (22%)
  waiting for transfers between devices  24.3 us (20%)
  local copies, waits for them, and re-layouts  15.5 us (13%)
  other arithmetic  4.34 us (4%)
  between operations  1.37 us (1%)
    ppermute x24, starting transfers between devices, hop(): return lax.ppermute(array, 'seq', pairs)  27.9 us
    pallas_call x20, Pallas kernels, call(): pl.pallas_call(body, grid_spec=pltpu.PrefetchScalarGridSpec(num_scalar_pr...  26.3 us
    ppermute x24, waiting for transfers between devices, hop(): return lax.ppermute(array, 'seq', pairs)  20.4 us
    unnamed x84, local copies, waits for them, and re-layouts  15.5 us
    ppermute x8, starting transfers between devices, swap_after(): flight[c] = lax.ppermute(part_sent, 'seq', swap)  9.9 us
    ppermute x8, starting transfers between devices, scan(): out[c] = (carry[c], own[c], lax.ppermute(send, 'seq', swap))  9.13 us
    select_n x8, other arithmetic, scan(): own[c] = jnp.where(y == 0, 0.0, got)  2.89 us
  transfers between devices with their start and end apart: 43, of which 11 were waited for; matrix products, arithmetic and copies ran while one was open for 4% of the time, Pallas kernels for 18%

profile of v5, /device:TPU:0, one launch (start us, length us, event | category | flops | bytes accessed | tf_op | source)
XLA Modules:
  0.0 120.6 jit_solution(10004393649844568564)
XLA Ops:
  0.6 1.6 %shard_map.77 = (f32[2,128,128]{2,1,0:T(8,128)S(1)}, f32[2,128,128]{2,1,0:T(8,128)S(1)}, f32[2,128,128]{2,1,0:T(8,128)S(1)}, f32[2,128,128]{2,1,0:T(8,128)S(1)}) custom-call(s32[1]{0:T(128)} %bitcast.place, bf16[256,2048]{1,0:T(8,128)(2,1)} %k.25, bf16[256,2048]{1,0:T(8,128)(2,1)} %v.25), custom_call_target="tpu_custom_call" | custom-call | flops 67108864 | bytes 1048576 | tf_op jit(solution)/shard_map/pallas_call | solution.py:44
  2.2 3.0 %collective-permute-start = (f32[2,128,128]{2,1,0:T(8,128)S(1)}, f32[2,128,128]{2,1,0:T(8,128)S(1)}, u32[]{:S(2)}, u32[]{:S(2)}) collective-permute-start(f32[2,128,128]{2,1,0:T(8,128)S(1)} %get-tuple-element.107), channel_id=1, source_target_pairs={{0,4},{4,0},{8,12},{12,8},{16,20},{20,16},{24,28},{28,24},{1,5},{5... | collective-permute-start | bytes 393224 | tf_op jit(solution)/shard_map/ppermute | solution.py:206
  5.3 5.0 %shard_map.76 = (f32[2,128,128]{2,1,0:T(8,128)S(1)}, f32[2,128,128]{2,1,0:T(8,128)S(1)}, f32[2,128,128]{2,1,0:T(8,128)S(1)}, f32[2,128,128]{2,1,0:T(8,128)S(1)}, f32[256,2048]{1,0:T(8,128)S(1)}) custom-call(s32[1]{0:T(128)} %bitcast.place, bf16[256,2048]{1,0:T(8,128)(2,1)} %q.17, bf16[256,2048]{1,0:T(8,128)(2,1)} %k.25, bf16[256,2048]{1,0:T(8,128)(2,1)} %v.25), custom_call_target="tpu_custom_call" | custom-call | flops 603979776 | bytes 1572864 | tf_op jit(solution)/shard_map/pallas_call | solution.py:44
  10.3 2.0 %collective-permute-start.4 = (f32[2,128,128]{2,1,0:T(8,128)S(1)}, f32[2,128,128]{2,1,0:T(8,128)}, u32[]{:S(2)}, u32[]{:S(2)}) collective-permute-start(f32[2,128,128]{2,1,0:T(8,128)S(1)} %get-tuple-element.115), channel_id=1, source_target_pairs={{0,4},{4,0},{8,12},{12,8},{16,20},{20,16},{24,28},{28,24},{1,5},{5... | collective-permute-start | bytes 393224 | tf_op jit(solution)/shard_map/ppermute | solution.py:206
  12.3 3.5 %collective-permute-start.5 = (f32[2,128,128]{2,1,0:T(8,128)S(1)}, f32[2,128,128]{2,1,0:T(8,128)S(1)}, u32[]{:S(2)}, u32[]{:S(2)}) collective-permute-start(f32[2,128,128]{2,1,0:T(8,128)S(1)} %get-tuple-element.244), channel_id=1, source_target_pairs={{0,8},{4,12},{1,9},{5,13},{2,10},{6,14},{3,11},{7,15}} | collective-permute-start | bytes 393224 | tf_op jit(solution)/shard_map/ppermute | solution.py:171
  15.9 0.9 broadcast_select_fusion.5
  16.8 1.3 %collective-permute-start.3 = (f32[2,128,128]{2,1,0:T(8,128)S(1)}, f32[2,128,128]{2,1,0:T(8,128)S(1)}, u32[]{:S(2)}, u32[]{:S(2)}) collective-permute-start(f32[2,128,128]{2,1,0:T(8,128)S(1)} %get-tuple-element.246), channel_id=1, source_target_pairs={{0,8},{4,12},{1,9},{5,13},{2,10},{6,14},{3,11},{7,15}} | collective-permute-start | bytes 393224 | tf_op jit(solution)/shard_map/ppermute | solution.py:171
  20.1 0.9 broadcast_select_fusion.6
  21.1 5.0 %collective-permute-start.8 = (f32[2,128,128]{2,1,0:T(8,128)S(1)}, f32[2,128,128]{2,1,0:T(8,128)S(1)}, u32[]{:S(2)}, u32[]{:S(2)}) collective-permute-start(f32[2,128,128]{2,1,0:T(8,128)S(1)} %get-tuple-element.248), channel_id=1, source_target_pairs={{0,8},{4,12},{1,9},{5,13},{2,10},{6,14},{3,11},{7,15}} | collective-permute-start | bytes 393224 | tf_op jit(solution)/shard_map/ppermute | solution.py:171
  26.8 1.9 %collective-permute-start.6 = (f32[2,128,128]{2,1,0:T(8,128)S(1)}, f32[2,128,128]{2,1,0:T(8,128)S(1)}, u32[]{:S(2)}, u32[]{:S(2)}) collective-permute-start(f32[2,128,128]{2,1,0:T(8,128)S(1)} %get-tuple-element.250), channel_id=1, source_target_pairs={{0,8},{4,12},{1,9},{5,13},{2,10},{6,14},{3,11},{7,15}} | collective-permute-start | bytes 393224 | tf_op jit(solution)/shard_map/ppermute | solution.py:171
  30.3 0.8 collective-permute-start.11
  32.0 0.9 add_select_fusion.7
  34.3 1.6 %collective-permute-start.18 = (f32[2,128,128]{2,1,0:T(8,128)S(1)}, f32[2,128,128]{2,1,0:T(8,128)S(1)}, u32[]{:S(2)}, u32[]{:S(2)}) collective-permute-start(f32[2,128,128]{2,1,0:T(8,128)S(1)} %get-tuple-element.225), channel_id=1, source_target_pairs={{0,4},{4,0},{8,12},{12,8},{16,20},{20,16},{24,28},{28,24},{1,5},{5... | collective-permute-start | bytes 393224 | tf_op jit(solution)/shard_map/ppermute | solution.py:224
  37.2 1.6 %collective-permute-start.16 = (f32[2,128,128]{2,1,0:T(8,128)S(1)}, f32[2,128,128]{2,1,0:T(8,128)S(1)}, u32[]{:S(2)}, u32[]{:S(2)}) collective-permute-start(f32[2,128,128]{2,1,0:T(8,128)S(1)} %get-tuple-element.219), channel_id=1, source_target_pairs={{0,4},{4,0},{8,12},{12,8},{16,20},{20,16},{24,28},{28,24},{1,5},{5... | collective-permute-start | bytes 393224 | tf_op jit(solution)/shard_map/ppermute | solution.py:224
  45.8 1.6 %collective-permute-start.21 = (f32[2,256]{1,0:T(2,128)S(1)}, f32[2,256]{1,0:T(2,128)S(1)}, u32[]{:S(2)}, u32[]{:S(2)}) collective-permute-start(f32[2,256]{1,0:T(2,128)S(1)} %get-tuple-element.136.refs_0_), channel_id=1, source_target_pairs={{0,2},{1,3},{2,0},{3,1},{4,6},{5,7},{6,4},{7,5},{8,10},{9,11},{10,... | collective-permute-start | bytes 6152 | tf_op jit(solution)/shard_map/ppermute | solution.py:303
  47.6 1.1 collective-permute-done.22.refs_3_
  49.4 1.1 shard_map.83
  55.0 1.5 %collective-permute-start.25 = (f32[2,128,128]{2,1,0:T(8,128)}, f32[2,128,128]{2,1,0:T(8,128)S(1)}, u32[]{:S(2)}, u32[]{:S(2)}) collective-permute-start(f32[2,128,128]{2,1,0:T(8,128)} %copy-done.40), channel_id=1, source_target_pairs={{0,4},{4,0},{8,12},{12,8},{16,20},{20,16},{24,28},{28,24},{1,5},{5... | collective-permute-start | bytes 393224 | tf_op jit(solution)/shard_map/ppermute | solution.py:206
  56.5 1.2 %copy-done.4 = bf16[256,2048]{1,0:T(8,128)(2,1)S(1)} copy-done((bf16[256,2048]{1,0:T(8,128)(2,1)S(1)}, bf16[256,2048]{1,0:T(8,128)(2,1)}, u32[]{:S(2)}) %copy-start.4) | copy-done | bytes 1048600
  57.7 0.9 copy-done.9
  58.7 0.9 copy-done.11
  59.6 0.9 copy-done.13
  60.6 0.9 copy-done.15
  63.8 1.6 %shard_map.84.refs_0_ = bf16[256,2048]{1,0:T(8,128)(2,1)} custom-call(s32[1]{0:T(128)} %bitcast.place, bf16[256,2048]{1,0:T(8,128)(2,1)S(1)} %copy-done.1, bf16[256,2048]{1,0:T(8,128)(2,1)S(1)} %copy-done.2, bf16[256,256]{1,0:T(8,128)(2,1)S(1)} %get-tuple-element.157.d_k.d, bf16[256,256]{1,0:T(8,128)(2,1)S(1)} %copy-done.7, ...), custom_call_target="tpu_custom_call" | custom-call | flops 167772160 | bytes 1245184 | tf_op jit(solution)/shard_map/pallas_call | solution.py:44
  65.4 1.7 %shard_map.85.refs_0_ = bf16[256,2048]{1,0:T(8,128)(2,1)} custom-call(s32[1]{0:T(128)} %bitcast.place, bf16[256,2048]{1,0:T(8,128)(2,1)S(1)} %copy-done.1, bf16[256,2048]{1,0:T(8,128)(2,1)S(1)} %copy-done.2, bf16[256,256]{1,0:T(8,128)(2,1)S(1)} %get-tuple-element.153.d_k.d, ...), custom_call_target="tpu_custom_call", output_to_operand_aliasing={{}: (7, {})} | custom-call | flops 167772160 | bytes 1769472 | tf_op jit(solution)/shard_map/pallas_call | solution.py:44
  67.1 1.7 %shard_map.86.refs_0_ = bf16[256,2048]{1,0:T(8,128)(2,1)} custom-call(s32[1]{0:T(128)} %bitcast.place, bf16[256,2048]{1,0:T(8,128)(2,1)S(1)} %copy-done.1, bf16[256,2048]{1,0:T(8,128)(2,1)S(1)} %copy-done.2, bf16[256,256]{1,0:T(8,128)(2,1)S(1)} %get-tuple-element.149.d_k.d, ...), custom_call_target="tpu_custom_call", output_to_operand_aliasing={{}: (7, {})} | custom-call | flops 167772160 | bytes 1769472 | tf_op jit(solution)/shard_map/pallas_call | solution.py:44
  68.8 1.7 %shard_map.87 = bf16[256,2048]{1,0:T(8,128)(2,1)} custom-call(s32[1]{0:T(128)} %bitcast.place, bf16[256,2048]{1,0:T(8,128)(2,1)S(1)} %copy-done.1, bf16[256,2048]{1,0:T(8,128)(2,1)S(1)} %copy-done.2, bf16[256,256]{1,0:T(8,128)(2,1)S(1)} %get-tuple-element.141.d_k.d, bf16[256,256]{1,0:T(8,128)(2,1)S(1)} %get-tuple-element.146.d_o.d, ...), custom_call_target="tpu_custom_call", output_to_operand_aliasing={{}: (7, {})} | custom-call | flops 167772160 | bytes 1769472 | tf_op jit(solution)/shard_map/pallas_call | solution.py:44
  71.0 0.9 broadcast_select_fusion
  73.3 1.5 %collective-permute-start.24 = (f32[2,128,128]{2,1,0:T(8,128)S(1)}, f32[2,128,128]{2,1,0:T(8,128)S(1)}, u32[]{:S(2)}, u32[]{:S(2)}) collective-permute-start(f32[2,128,128]{2,1,0:T(8,128)S(1)} %copy-done.37), channel_id=1, source_target_pairs={{0,4},{4,0},{8,12},{12,8},{16,20},{20,16},{24,28},{28,24},{1,5},{5... | collective-permute-start | bytes 393224 | tf_op jit(solution)/shard_map/ppermute | solution.py:206
  77.2 1.3 %collective-permute-done.24 = f32[2,128,128]{2,1,0:T(8,128)S(1)} collective-permute-done((f32[2,128,128]{2,1,0:T(8,128)S(1)}, f32[2,128,128]{2,1,0:T(8,128)S(1)}, u32[]{:S(2)}, u32[]{:S(2)}) %collective-permute-start.24) | collective-permute-done | bytes 131104 | tf_op jit(solution)/shard_map/ppermute | solution.py:206
  79.2 1.3 %collective-permute-start.36 = (f32[2,128,128]{2,1,0:T(8,128)S(1)}, f32[2,128,128]{2,1,0:T(8,128)S(1)}, u32[]{:S(2)}, u32[]{:S(2)}) collective-permute-start(f32[2,128,128]{2,1,0:T(8,128)S(1)} %get-tuple-element.217), channel_id=1, source_target_pairs={{12,4},{8,0},{13,5},{9,1},{14,6},{10,2},{15,7},{11,3}} | collective-permute-start | bytes 393224 | tf_op jit(solution)/shard_map/ppermute | solution.py:171
  81.3 1.3 %collective-permute-start.34 = (f32[2,128,128]{2,1,0:T(8,128)S(1)}, f32[2,128,128]{2,1,0:T(8,128)S(1)}, u32[]{:S(2)}, u32[]{:S(2)}) collective-permute-start(f32[2,128,128]{2,1,0:T(8,128)S(1)} %get-tuple-element.215), channel_id=1, source_target_pairs={{12,4},{8,0},{13,5},{9,1},{14,6},{10,2},{15,7},{11,3}} | collective-permute-start | bytes 393224 | tf_op jit(solution)/shard_map/ppermute | solution.py:171
  83.3 14.5 %collective-permute-done.36 = f32[2,128,128]{2,1,0:T(8,128)S(1)} collective-permute-done((f32[2,128,128]{2,1,0:T(8,128)S(1)}, f32[2,128,128]{2,1,0:T(8,128)S(1)}, u32[]{:S(2)}, u32[]{:S(2)}) %collective-permute-start.36) | collective-permute-done | bytes 131104 | tf_op jit(solution)/shard_map/ppermute | solution.py:171
  97.8 1.6 %collective-permute-start.42 = (f32[2,128,128]{2,1,0:T(8,128)S(1)}, f32[2,128,128]{2,1,0:T(8,128)S(1)}, u32[]{:S(2)}, u32[]{:S(2)}) collective-permute-start(f32[2,128,128]{2,1,0:T(8,128)S(1)} %get-tuple-element.213), channel_id=1, source_target_pairs={{0,4},{4,0},{8,12},{12,8},{16,20},{20,16},{24,28},{28,24},{1,5},{5... | collective-permute-start | bytes 393224 | tf_op jit(solution)/shard_map/ppermute | solution.py:224
  99.5 1.3 %collective-permute-start.38 = (f32[2,128,128]{2,1,0:T(8,128)S(1)}, f32[2,128,128]{2,1,0:T(8,128)S(1)}, u32[]{:S(2)}, u32[]{:S(2)}) collective-permute-start(f32[2,128,128]{2,1,0:T(8,128)S(1)} %get-tuple-element.211), channel_id=1, source_target_pairs={{12,4},{8,0},{13,5},{9,1},{14,6},{10,2},{15,7},{11,3}} | collective-permute-start | bytes 393224 | tf_op jit(solution)/shard_map/ppermute | solution.py:171
  101.4 1.6 %collective-permute-start.41 = (f32[2,128,128]{2,1,0:T(8,128)S(1)}, f32[2,128,128]{2,1,0:T(8,128)S(1)}, u32[]{:S(2)}, u32[]{:S(2)}) collective-permute-start(f32[2,128,128]{2,1,0:T(8,128)S(1)} %get-tuple-element.209), channel_id=1, source_target_pairs={{0,4},{4,0},{8,12},{12,8},{16,20},{20,16},{24,28},{28,24},{1,5},{5... | collective-permute-start | bytes 393224 | tf_op jit(solution)/shard_map/ppermute | solution.py:224
  103.0 1.5 %collective-permute-start.37 = (f32[2,128,128]{2,1,0:T(8,128)S(1)}, f32[2,128,128]{2,1,0:T(8,128)S(1)}, u32[]{:S(2)}, u32[]{:S(2)}) collective-permute-start(f32[2,128,128]{2,1,0:T(8,128)S(1)} %get-tuple-element.207), channel_id=1, source_target_pairs={{12,4},{8,0},{13,5},{9,1},{14,6},{10,2},{15,7},{11,3}} | collective-permute-start | bytes 393224 | tf_op jit(solution)/shard_map/ppermute | solution.py:171
  104.4 1.9 %collective-permute-done.38 = f32[2,128,128]{2,1,0:T(8,128)S(1)} collective-permute-done((f32[2,128,128]{2,1,0:T(8,128)S(1)}, f32[2,128,128]{2,1,0:T(8,128)S(1)}, u32[]{:S(2)}, u32[]{:S(2)}) %collective-permute-start.38) | collective-permute-done | bytes 131104 | tf_op jit(solution)/shard_map/ppermute | solution.py:171
  106.4 1.0 collective-permute-start.40
  107.4 2.4 %collective-permute-done.37 = f32[2,128,128]{2,1,0:T(8,128)S(1)} collective-permute-done((f32[2,128,128]{2,1,0:T(8,128)S(1)}, f32[2,128,128]{2,1,0:T(8,128)S(1)}, u32[]{:S(2)}, u32[]{:S(2)}) %collective-permute-start.37) | collective-permute-done | bytes 131104 | tf_op jit(solution)/shard_map/ppermute | solution.py:171
  110.5 1.3 %shard_map.88 = (bf16[256,2048]{1,0:T(8,128)(2,1)}, bf16[256,2048]{1,0:T(8,128)(2,1)}) custom-call(s32[1]{0:T(128)} %bitcast.place, bf16[256,2048]{1,0:T(8,128)(2,1)S(1)} %copy-done, bf16[256,2048]{1,0:T(8,128)(2,1)S(1)} %copy-done.1, bf16[256,2048]{1,0:T(8,128)(2,1)S(1)} %copy-done.2, bf16[256,256]{1,0:T(8,128)(2,1)S(1)} %get-tuple-element.157.d_k.d, ...), custom_call_target="tpu_custom_call" | custom-call | flops 167772160 | bytes 1769472 | tf_op jit(solution)/shard_map/pallas_call | solution.py:44
  111.7 1.3 %shard_map.89 = (bf16[256,2048]{1,0:T(8,128)(2,1)}, bf16[256,2048]{1,0:T(8,128)(2,1)}) custom-call(s32[1]{0:T(128)} %bitcast.place, bf16[256,2048]{1,0:T(8,128)(2,1)S(1)} %copy-done, bf16[256,2048]{1,0:T(8,128)(2,1)S(1)} %copy-done.1, bf16[256,2048]{1,0:T(8,128)(2,1)S(1)} %copy-done.2, ...), custom_call_target="tpu_custom_call", output_to_operand_aliasing={{0}: (7, {}), {1}: (8, {})} | custom-call | flops 167772160 | bytes 2818048 | tf_op jit(solution)/shard_map/pallas_call | solution.py:44
  113.0 1.3 %shard_map.90 = (bf16[256,2048]{1,0:T(8,128)(2,1)}, bf16[256,2048]{1,0:T(8,128)(2,1)}) custom-call(s32[1]{0:T(128)} %bitcast.place, bf16[256,2048]{1,0:T(8,128)(2,1)S(1)} %copy-done, bf16[256,2048]{1,0:T(8,128)(2,1)S(1)} %copy-done.1, bf16[256,2048]{1,0:T(8,128)(2,1)S(1)} %copy-done.2, ...), custom_call_target="tpu_custom_call", output_to_operand_aliasing={{0}: (7, {}), {1}: (8, {})} | custom-call | flops 167772160 | bytes 2818048 | tf_op jit(solution)/shard_map/pallas_call | solution.py:44
  114.2 1.3 %shard_map.91 = (bf16[256,2048]{1,0:T(8,128)(2,1)}, bf16[256,2048]{1,0:T(8,128)(2,1)}) custom-call(s32[1]{0:T(128)} %bitcast.place, bf16[256,2048]{1,0:T(8,128)(2,1)S(1)} %copy-done, bf16[256,2048]{1,0:T(8,128)(2,1)S(1)} %copy-done.1, bf16[256,2048]{1,0:T(8,128)(2,1)S(1)} %copy-done.2, ...), custom_call_target="tpu_custom_call", output_to_operand_aliasing={{0}: (7, {}), {1}: (8, {})} | custom-call | flops 167772160 | bytes 2818048 | tf_op jit(solution)/shard_map/pallas_call | solution.py:44
  115.5 1.3 %shard_map.92 = (bf16[256,2048]{1,0:T(8,128)(2,1)}, bf16[256,2048]{1,0:T(8,128)(2,1)}) custom-call(s32[1]{0:T(128)} %bitcast.place, bf16[256,2048]{1,0:T(8,128)(2,1)S(1)} %copy-done, bf16[256,2048]{1,0:T(8,128)(2,1)S(1)} %copy-done.1, bf16[256,2048]{1,0:T(8,128)(2,1)S(1)} %copy-done.2, ...), custom_call_target="tpu_custom_call", output_to_operand_aliasing={{0}: (6, {}), {1}: (7, {})} | custom-call | flops 167772160 | bytes 2752512 | tf_op jit(solution)/shard_map/pallas_call | solution.py:44
  116.8 1.3 %shard_map.93 = (bf16[256,2048]{1,0:T(8,128)(2,1)}, bf16[256,2048]{1,0:T(8,128)(2,1)}) custom-call(s32[1]{0:T(128)} %bitcast.place, bf16[256,2048]{1,0:T(8,128)(2,1)S(1)} %copy-done, bf16[256,2048]{1,0:T(8,128)(2,1)S(1)} %copy-done.1, bf16[256,2048]{1,0:T(8,128)(2,1)S(1)} %copy-done.2, ...), custom_call_target="tpu_custom_call", output_to_operand_aliasing={{0}: (6, {}), {1}: (7, {})} | custom-call | flops 167772160 | bytes 2752512 | tf_op jit(solution)/shard_map/pallas_call | solution.py:44
  118.0 1.3 %shard_map.94 = (bf16[256,2048]{1,0:T(8,128)(2,1)}, bf16[256,2048]{1,0:T(8,128)(2,1)}) custom-call(s32[1]{0:T(128)} %bitcast.place, bf16[256,2048]{1,0:T(8,128)(2,1)S(1)} %copy-done, bf16[256,2048]{1,0:T(8,128)(2,1)S(1)} %copy-done.1, bf16[256,2048]{1,0:T(8,128)(2,1)S(1)} %copy-done.2, ...), custom_call_target="tpu_custom_call", output_to_operand_aliasing={{0}: (6, {}), {1}: (7, {})} | custom-call | flops 167772160 | bytes 2752512 | tf_op jit(solution)/shard_map/pallas_call | solution.py:44
  119.3 1.3 %shard_map.95 = (bf16[256,2048]{1,0:T(8,128)(2,1)}, bf16[256,2048]{1,0:T(8,128)(2,1)}) custom-call(s32[1]{0:T(128)} %bitcast.place, bf16[256,2048]{1,0:T(8,128)(2,1)S(1)} %copy-done, bf16[256,2048]{1,0:T(8,128)(2,1)S(1)} %copy-done.1, bf16[256,2048]{1,0:T(8,128)(2,1)S(1)} %copy-done.2, ...), custom_call_target="tpu_custom_call", output_to_operand_aliasing={{0}: (6, {}), {1}: (7, {})} | custom-call | flops 167772160 | bytes 2752512 | tf_op jit(solution)/shard_map/pallas_call | solution.py:44
  (175 shorter events, 29.9 us)
Async XLA Ops:
  2.2 10.1 %collective-permute-start = (f32[2,128,128]{2,1,0:T(8,128)S(1)}, f32[2,128,128]{2,1,0:T(8,128)S(1)}, u32[]{:S(2)}, u32[]{:S(2)}) collective-permute-start(f32[2,128,128]{2,1,0:T(8,128)S(1)} %get-tuple-element.107), channel_id=1, source_target_pairs={{0,4},{4,0},{8,12},{12,8},{16,20},{20,16},{24,28},{28,24},{1,5},{5... | collective-permute-start | bytes 393224 | tf_op jit(solution)/shard_map/ppermute | solution.py:206
  5.2 10.6 %collective-permute-start.2 = (f32[2,128,128]{2,1,0:T(8,128)S(1)}, f32[2,128,128]{2,1,0:T(8,128)}, u32[]{:S(2)}, u32[]{:S(2)}) collective-permute-start(f32[2,128,128]{2,1,0:T(8,128)S(1)} %get-tuple-element.111), channel_id=1, source_target_pairs={{0,4},{4,0},{8,12},{12,8},{16,20},{20,16},{24,28},{28,24},{1,5},{5... | collective-permute-start | bytes 393224 | tf_op jit(solution)/shard_map/ppermute | solution.py:206
  10.3 20.0 %copy-start.5 = (f32[2,128,128]{2,1,0:T(8,128)}, f32[2,128,128]{2,1,0:T(8,128)S(1)}, u32[]{:S(2)}) copy-start(f32[2,128,128]{2,1,0:T(8,128)S(1)} %get-tuple-element.106) | copy-start | bytes 393220
  10.3 9.8 %collective-permute-start.4 = (f32[2,128,128]{2,1,0:T(8,128)S(1)}, f32[2,128,128]{2,1,0:T(8,128)}, u32[]{:S(2)}, u32[]{:S(2)}) collective-permute-start(f32[2,128,128]{2,1,0:T(8,128)S(1)} %get-tuple-element.115), channel_id=1, source_target_pairs={{0,4},{4,0},{8,12},{12,8},{16,20},{20,16},{24,28},{28,24},{1,5},{5... | collective-permute-start | bytes 393224 | tf_op jit(solution)/shard_map/ppermute | solution.py:206
  12.3 7.1 %collective-permute-start.5 = (f32[2,128,128]{2,1,0:T(8,128)S(1)}, f32[2,128,128]{2,1,0:T(8,128)S(1)}, u32[]{:S(2)}, u32[]{:S(2)}) collective-permute-start(f32[2,128,128]{2,1,0:T(8,128)S(1)} %get-tuple-element.244), channel_id=1, source_target_pairs={{0,8},{4,12},{1,9},{5,13},{2,10},{6,14},{3,11},{7,15}} | collective-permute-start | bytes 393224 | tf_op jit(solution)/shard_map/ppermute | solution.py:171
  16.8 9.3 %collective-permute-start.3 = (f32[2,128,128]{2,1,0:T(8,128)S(1)}, f32[2,128,128]{2,1,0:T(8,128)S(1)}, u32[]{:S(2)}, u32[]{:S(2)}) collective-permute-start(f32[2,128,128]{2,1,0:T(8,128)S(1)} %get-tuple-element.246), channel_id=1, source_target_pairs={{0,8},{4,12},{1,9},{5,13},{2,10},{6,14},{3,11},{7,15}} | collective-permute-start | bytes 393224 | tf_op jit(solution)/shard_map/ppermute | solution.py:171
  18.1 8.7 %collective-permute-start.1 = (f32[2,128,128]{2,1,0:T(8,128)S(1)}, f32[2,128,128]{2,1,0:T(8,128)S(1)}, u32[]{:S(2)}, u32[]{:S(2)}) collective-permute-start(f32[2,128,128]{2,1,0:T(8,128)S(1)} %get-tuple-element.109), channel_id=1, source_target_pairs={{0,4},{4,0},{8,12},{12,8},{16,20},{20,16},{24,28},{28,24},{1,5},{5... | collective-permute-start | bytes 393224 | tf_op jit(solution)/shard_map/ppermute | solution.py:206
  19.5 9.3 %collective-permute-start.9 = (f32[2,128,128]{2,1,0:T(8,128)S(1)}, f32[2,128,128]{2,1,0:T(8,128)S(1)}, u32[]{:S(2)}, u32[]{:S(2)}) collective-permute-start(f32[2,128,128]{2,1,0:T(8,128)S(1)} %add.151), channel_id=1, source_target_pairs={{8,16},{12,20},{9,17},{13,21},{10,18},{14,22},{11,19},{15,23}} | collective-permute-start | bytes 393224 | tf_op jit(solution)/shard_map/ppermute | solution.py:171
  21.1 8.4 %collective-permute-start.8 = (f32[2,128,128]{2,1,0:T(8,128)S(1)}, f32[2,128,128]{2,1,0:T(8,128)S(1)}, u32[]{:S(2)}, u32[]{:S(2)}) collective-permute-start(f32[2,128,128]{2,1,0:T(8,128)S(1)} %get-tuple-element.248), channel_id=1, source_target_pairs={{0,8},{4,12},{1,9},{5,13},{2,10},{6,14},{3,11},{7,15}} | collective-permute-start | bytes 393224 | tf_op jit(solution)/shard_map/ppermute | solution.py:171
  26.1 4.1 %collective-permute-start.7 = (f32[2,128,128]{2,1,0:T(8,128)S(1)}, f32[2,128,128]{2,1,0:T(8,128)S(1)}, u32[]{:S(2)}, u32[]{:S(2)}) collective-permute-start(f32[2,128,128]{2,1,0:T(8,128)S(1)} %add.153), channel_id=1, source_target_pairs={{8,16},{12,20},{9,17},{13,21},{10,18},{14,22},{11,19},{15,23}} | collective-permute-start | bytes 393224 | tf_op jit(solution)/shard_map/ppermute | solution.py:171
  26.8 4.4 %collective-permute-start.6 = (f32[2,128,128]{2,1,0:T(8,128)S(1)}, f32[2,128,128]{2,1,0:T(8,128)S(1)}, u32[]{:S(2)}, u32[]{:S(2)}) collective-permute-start(f32[2,128,128]{2,1,0:T(8,128)S(1)} %get-tuple-element.250), channel_id=1, source_target_pairs={{0,8},{4,12},{1,9},{5,13},{2,10},{6,14},{3,11},{7,15}} | collective-permute-start | bytes 393224 | tf_op jit(solution)/shard_map/ppermute | solution.py:171
  28.8 3.2 %collective-permute-start.13 = (f32[2,128,128]{2,1,0:T(8,128)S(1)}, f32[2,128,128]{2,1,0:T(8,128)S(1)}, u32[]{:S(2)}, u32[]{:S(2)}) collective-permute-start(f32[2,128,128]{2,1,0:T(8,128)S(1)} %get-tuple-element.233), channel_id=1, source_target_pairs={{16,24},{20,28},{17,25},{21,29},{18,26},{22,30},{19,27},{23,31}} | collective-permute-start | bytes 393224 | tf_op jit(solution)/shard_map/ppermute | solution.py:171
  29.5 4.0 %collective-permute-start.12 = (f32[2,128,128]{2,1,0:T(8,128)S(1)}, f32[2,128,128]{2,1,0:T(8,128)S(1)}, u32[]{:S(2)}, u32[]{:S(2)}) collective-permute-start(f32[2,128,128]{2,1,0:T(8,128)S(1)} %add.157), channel_id=1, source_target_pairs={{8,16},{12,20},{9,17},{13,21},{10,18},{14,22},{11,19},{15,23}} | collective-permute-start | bytes 393224 | tf_op jit(solution)/shard_map/ppermute | solution.py:171
  30.3 9.1 %copy-start = (bf16[256,2048]{1,0:T(8,128)(2,1)S(1)}, bf16[256,2048]{1,0:T(8,128)(2,1)}, u32[]{:S(2)}) copy-start(bf16[256,2048]{1,0:T(8,128)(2,1)} %q.17) | copy-start | bytes 3145732
  30.3 9.1 %copy-start.3 = (bf16[256,2048]{1,0:T(8,128)(2,1)S(1)}, bf16[256,2048]{1,0:T(8,128)(2,1)}, u32[]{:S(2)}) copy-start(bf16[256,2048]{1,0:T(8,128)(2,1)} %refs_9_.3) | copy-start | bytes 3145732
  30.3 3.9 %collective-permute-start.11 = (f32[2,128,128]{2,1,0:T(8,128)S(1)}, f32[2,128,128]{2,1,0:T(8,128)S(1)}, u32[]{:S(2)}, u32[]{:S(2)}) collective-permute-start(f32[2,128,128]{2,1,0:T(8,128)S(1)} %get-tuple-element.231), channel_id=1, source_target_pairs={{16,24},{20,28},{17,25},{21,29},{18,26},{22,30},{19,27},{23,31}} | collective-permute-start | bytes 393224 | tf_op jit(solution)/shard_map/ppermute | solution.py:171
  31.3 4.5 %collective-permute-start.10 = (f32[2,128,128]{2,1,0:T(8,128)S(1)}, f32[2,128,128]{2,1,0:T(8,128)S(1)}, u32[]{:S(2)}, u32[]{:S(2)}) collective-permute-start(f32[2,128,128]{2,1,0:T(8,128)S(1)} %add.160), channel_id=1, source_target_pairs={{8,16},{12,20},{9,17},{13,21},{10,18},{14,22},{11,19},{15,23}} | collective-permute-start | bytes 393224 | tf_op jit(solution)/shard_map/ppermute | solution.py:171
  32.9 6.5 %collective-permute-start.19 = (f32[2,128,128]{2,1,0:T(8,128)S(1)}, f32[2,128,128]{2,1,0:T(8,128)S(1)}, u32[]{:S(2)}, u32[]{:S(2)}) collective-permute-start(f32[2,128,128]{2,1,0:T(8,128)S(1)} %get-tuple-element.229), channel_id=1, source_target_pairs={{0,4},{4,0},{8,12},{12,8},{16,20},{20,16},{24,28},{28,24},{1,5},{5... | collective-permute-start | bytes 393224 | tf_op jit(solution)/shard_map/ppermute | solution.py:224
  33.5 3.0 %collective-permute-start.15 = (f32[2,128,128]{2,1,0:T(8,128)S(1)}, f32[2,128,128]{2,1,0:T(8,128)S(1)}, u32[]{:S(2)}, u32[]{:S(2)}) collective-permute-start(f32[2,128,128]{2,1,0:T(8,128)S(1)} %get-tuple-element.227), channel_id=1, source_target_pairs={{16,24},{20,28},{17,25},{21,29},{18,26},{22,30},{19,27},{23,31}} | collective-permute-start | bytes 393224 | tf_op jit(solution)/shard_map/ppermute | solution.py:171
  34.3 7.4 %collective-permute-start.18 = (f32[2,128,128]{2,1,0:T(8,128)S(1)}, f32[2,128,128]{2,1,0:T(8,128)S(1)}, u32[]{:S(2)}, u32[]{:S(2)}) collective-permute-start(f32[2,128,128]{2,1,0:T(8,128)S(1)} %get-tuple-element.225), channel_id=1, source_target_pairs={{0,4},{4,0},{8,12},{12,8},{16,20},{20,16},{24,28},{28,24},{1,5},{5... | collective-permute-start | bytes 393224 | tf_op jit(solution)/shard_map/ppermute | solution.py:224
  35.9 1.3 %collective-permute-start.14 = (f32[2,128,128]{2,1,0:T(8,128)S(1)}, f32[2,128,128]{2,1,0:T(8,128)S(1)}, u32[]{:S(2)}, u32[]{:S(2)}) collective-permute-start(f32[2,128,128]{2,1,0:T(8,128)S(1)} %get-tuple-element.223), channel_id=1, source_target_pairs={{16,24},{20,28},{17,25},{21,29},{18,26},{22,30},{19,27},{23,31}} | collective-permute-start | bytes 393224 | tf_op jit(solution)/shard_map/ppermute | solution.py:171
  36.6 6.1 %collective-permute-start.17 = (f32[2,128,128]{2,1,0:T(8,128)S(1)}, f32[2,128,128]{2,1,0:T(8,128)S(1)}, u32[]{:S(2)}, u32[]{:S(2)}) collective-permute-start(f32[2,128,128]{2,1,0:T(8,128)S(1)} %get-tuple-element.221), channel_id=1, source_target_pairs={{0,4},{4,0},{8,12},{12,8},{16,20},{20,16},{24,28},{28,24},{1,5},{5... | collective-permute-start | bytes 393224 | tf_op jit(solution)/shard_map/ppermute | solution.py:224
  37.2 8.1 %collective-permute-start.16 = (f32[2,128,128]{2,1,0:T(8,128)S(1)}, f32[2,128,128]{2,1,0:T(8,128)S(1)}, u32[]{:S(2)}, u32[]{:S(2)}) collective-permute-start(f32[2,128,128]{2,1,0:T(8,128)S(1)} %get-tuple-element.219), channel_id=1, source_target_pairs={{0,4},{4,0},{8,12},{12,8},{16,20},{20,16},{24,28},{28,24},{1,5},{5... | collective-permute-start | bytes 393224 | tf_op jit(solution)/shard_map/ppermute | solution.py:224
  45.7 3.1 %collective-permute-start.22 = (f32[2,256]{1,0:T(2,128)S(1)}, f32[2,256]{1,0:T(2,128)S(1)}, u32[]{:S(2)}, u32[]{:S(2)}) collective-permute-start(f32[2,256]{1,0:T(2,128)S(1)} %get-tuple-element.136.refs_0_), channel_id=1, source_target_pairs={{0,3},{1,2},{2,1},{3,0},{4,7},{5,6},{6,5},{7,4},{8,11},{9,10},{10,... | collective-permute-start | bytes 6152 | tf_op jit(solution)/shard_map/ppermute | solution.py:303
  45.8 3.7 %collective-permute-start.21 = (f32[2,256]{1,0:T(2,128)S(1)}, f32[2,256]{1,0:T(2,128)S(1)}, u32[]{:S(2)}, u32[]{:S(2)}) collective-permute-start(f32[2,256]{1,0:T(2,128)S(1)} %get-tuple-element.136.refs_0_), channel_id=1, source_target_pairs={{0,2},{1,3},{2,0},{3,1},{4,6},{5,7},{6,4},{7,5},{8,10},{9,11},{10,... | collective-permute-start | bytes 6152 | tf_op jit(solution)/shard_map/ppermute | solution.py:303
  47.3 2.1 %collective-permute-start.20 = (f32[2,256]{1,0:T(2,128)S(1)}, f32[2,256]{1,0:T(2,128)S(1)}, u32[]{:S(2)}, u32[]{:S(2)}) collective-permute-start(f32[2,256]{1,0:T(2,128)S(1)} %get-tuple-element.136.refs_0_), channel_id=1, source_target_pairs={{0,1},{1,0},{2,3},{3,2},{4,5},{5,4},{6,7},{7,6},{8,9},{9,8},{10,11... | collective-permute-start | bytes 6152 | tf_op jit(solution)/shard_map/ppermute | solution.py:303
  54.4 9.1 %copy-start.1 = (bf16[256,2048]{1,0:T(8,128)(2,1)S(1)}, bf16[256,2048]{1,0:T(8,128)(2,1)}, u32[]{:S(2)}) copy-start(bf16[256,2048]{1,0:T(8,128)(2,1)} %k.25) | copy-start | bytes 3145732
  54.4 9.1 %copy-start.2 = (bf16[256,2048]{1,0:T(8,128)(2,1)S(1)}, bf16[256,2048]{1,0:T(8,128)(2,1)}, u32[]{:S(2)}) copy-start(bf16[256,2048]{1,0:T(8,128)(2,1)} %v.25) | copy-start | bytes 3145732
  54.4 16.6 %collective-permute-start.23 = (f32[2,128,128]{2,1,0:T(8,128)}, f32[2,128,128]{2,1,0:T(8,128)}, u32[]{:S(2)}, u32[]{:S(2)}) collective-permute-start(f32[2,128,128]{2,1,0:T(8,128)} %get-tuple-element.164), channel_id=1, source_target_pairs={{0,4},{4,0},{8,12},{12,8},{16,20},{20,16},{24,28},{28,24},{1,5},{5... | collective-permute-start | bytes 393224 | tf_op jit(solution)/shard_map/ppermute | solution.py:206
  55.0 17.6 %collective-permute-start.25 = (f32[2,128,128]{2,1,0:T(8,128)}, f32[2,128,128]{2,1,0:T(8,128)S(1)}, u32[]{:S(2)}, u32[]{:S(2)}) collective-permute-start(f32[2,128,128]{2,1,0:T(8,128)} %copy-done.40), channel_id=1, source_target_pairs={{0,4},{4,0},{8,12},{12,8},{16,20},{20,16},{24,28},{28,24},{1,5},{5... | collective-permute-start | bytes 393224 | tf_op jit(solution)/shard_map/ppermute | solution.py:206
  70.5 5.3 %collective-permute-start.27 = (f32[2,128,128]{2,1,0:T(8,128)S(1)}, f32[2,128,128]{2,1,0:T(8,128)S(1)}, u32[]{:S(2)}, u32[]{:S(2)}) collective-permute-start(f32[2,128,128]{2,1,0:T(8,128)S(1)} %copy-done.39), channel_id=1, source_target_pairs={{0,4},{4,0},{8,12},{12,8},{16,20},{20,16},{24,28},{28,24},{1,5},{5... | collective-permute-start | bytes 393224 | tf_op jit(solution)/shard_map/ppermute | solution.py:206
  71.9 3.0 %collective-permute-start.28 = (f32[2,128,128]{2,1,0:T(8,128)S(1)}, f32[2,128,128]{2,1,0:T(8,128)S(1)}, u32[]{:S(2)}, u32[]{:S(2)}) collective-permute-start(f32[2,128,128]{2,1,0:T(8,128)S(1)} %get-tuple-element.236), channel_id=1, source_target_pairs={{28,20},{24,16},{29,21},{25,17},{30,22},{26,18},{31,23},{27,19}} | collective-permute-start | bytes 393224 | tf_op jit(solution)/shard_map/ppermute | solution.py:171
  72.6 3.8 %collective-permute-start.26 = (f32[2,128,128]{2,1,0:T(8,128)S(1)}, f32[2,128,128]{2,1,0:T(8,128)S(1)}, u32[]{:S(2)}, u32[]{:S(2)}) collective-permute-start(f32[2,128,128]{2,1,0:T(8,128)S(1)} %get-tuple-element.238), channel_id=1, source_target_pairs={{28,20},{24,16},{29,21},{25,17},{30,22},{26,18},{31,23},{27,19}} | collective-permute-start | bytes 393224 | tf_op jit(solution)/shard_map/ppermute | solution.py:171
  73.3 5.1 %collective-permute-start.24 = (f32[2,128,128]{2,1,0:T(8,128)S(1)}, f32[2,128,128]{2,1,0:T(8,128)S(1)}, u32[]{:S(2)}, u32[]{:S(2)}) collective-permute-start(f32[2,128,128]{2,1,0:T(8,128)S(1)} %copy-done.37), channel_id=1, source_target_pairs={{0,4},{4,0},{8,12},{12,8},{16,20},{20,16},{24,28},{28,24},{1,5},{5... | collective-permute-start | bytes 393224 | tf_op jit(solution)/shard_map/ppermute | solution.py:206
  74.9 4.3 %collective-permute-start.32 = (f32[2,128,128]{2,1,0:T(8,128)S(1)}, f32[2,128,128]{2,1,0:T(8,128)S(1)}, u32[]{:S(2)}, u32[]{:S(2)}) collective-permute-start(f32[2,128,128]{2,1,0:T(8,128)S(1)} %add.175), channel_id=1, source_target_pairs={{20,12},{16,8},{21,13},{17,9},{22,14},{18,10},{23,15},{19,11}} | collective-permute-start | bytes 393224 | tf_op jit(solution)/shard_map/ppermute | solution.py:171
  75.8 4.7 %collective-permute-start.31 = (f32[2,128,128]{2,1,0:T(8,128)S(1)}, f32[2,128,128]{2,1,0:T(8,128)S(1)}, u32[]{:S(2)}, u32[]{:S(2)}) collective-permute-start(f32[2,128,128]{2,1,0:T(8,128)S(1)} %get-tuple-element.240), channel_id=1, source_target_pairs={{28,20},{24,16},{29,21},{25,17},{30,22},{26,18},{31,23},{27,19}} | collective-permute-start | bytes 393224 | tf_op jit(solution)/shard_map/ppermute | solution.py:171
  76.5 4.7 %collective-permute-start.30 = (f32[2,128,128]{2,1,0:T(8,128)S(1)}, f32[2,128,128]{2,1,0:T(8,128)S(1)}, u32[]{:S(2)}, u32[]{:S(2)}) collective-permute-start(f32[2,128,128]{2,1,0:T(8,128)S(1)} %add.177), channel_id=1, source_target_pairs={{20,12},{16,8},{21,13},{17,9},{22,14},{18,10},{23,15},{19,11}} | collective-permute-start | bytes 393224 | tf_op jit(solution)/shard_map/ppermute | solution.py:171
  78.5 4.1 %collective-permute-start.29 = (f32[2,128,128]{2,1,0:T(8,128)S(1)}, f32[2,128,128]{2,1,0:T(8,128)S(1)}, u32[]{:S(2)}, u32[]{:S(2)}) collective-permute-start(f32[2,128,128]{2,1,0:T(8,128)S(1)} %get-tuple-element.242), channel_id=1, source_target_pairs={{28,20},{24,16},{29,21},{25,17},{30,22},{26,18},{31,23},{27,19}} | collective-permute-start | bytes 393224 | tf_op jit(solution)/shard_map/ppermute | solution.py:171
  79.2 18.6 %collective-permute-start.36 = (f32[2,128,128]{2,1,0:T(8,128)S(1)}, f32[2,128,128]{2,1,0:T(8,128)S(1)}, u32[]{:S(2)}, u32[]{:S(2)}) collective-permute-start(f32[2,128,128]{2,1,0:T(8,128)S(1)} %get-tuple-element.217), channel_id=1, source_target_pairs={{12,4},{8,0},{13,5},{9,1},{14,6},{10,2},{15,7},{11,3}} | collective-permute-start | bytes 393224 | tf_op jit(solution)/shard_map/ppermute | solution.py:171
  80.6 18.9 %collective-permute-start.35 = (f32[2,128,128]{2,1,0:T(8,128)S(1)}, f32[2,128,128]{2,1,0:T(8,128)S(1)}, u32[]{:S(2)}, u32[]{:S(2)}) collective-permute-start(f32[2,128,128]{2,1,0:T(8,128)S(1)} %add.181), channel_id=1, source_target_pairs={{20,12},{16,8},{21,13},{17,9},{22,14},{18,10},{23,15},{19,11}} | collective-permute-start | bytes 393224 | tf_op jit(solution)/shard_map/ppermute | solution.py:171
  81.3 20.0 %collective-permute-start.34 = (f32[2,128,128]{2,1,0:T(8,128)S(1)}, f32[2,128,128]{2,1,0:T(8,128)S(1)}, u32[]{:S(2)}, u32[]{:S(2)}) collective-permute-start(f32[2,128,128]{2,1,0:T(8,128)S(1)} %get-tuple-element.215), channel_id=1, source_target_pairs={{12,4},{8,0},{13,5},{9,1},{14,6},{10,2},{15,7},{11,3}} | collective-permute-start | bytes 393224 | tf_op jit(solution)/shard_map/ppermute | solution.py:171
  82.6 20.3 %collective-permute-start.33 = (f32[2,128,128]{2,1,0:T(8,128)S(1)}, f32[2,128,128]{2,1,0:T(8,128)S(1)}, u32[]{:S(2)}, u32[]{:S(2)}) collective-permute-start(f32[2,128,128]{2,1,0:T(8,128)S(1)} %add.184), channel_id=1, source_target_pairs={{20,12},{16,8},{21,13},{17,9},{22,14},{18,10},{23,15},{19,11}} | collective-permute-start | bytes 393224 | tf_op jit(solution)/shard_map/ppermute | solution.py:171
  97.8 17.7 %collective-permute-start.42 = (f32[2,128,128]{2,1,0:T(8,128)S(1)}, f32[2,128,128]{2,1,0:T(8,128)S(1)}, u32[]{:S(2)}, u32[]{:S(2)}) collective-permute-start(f32[2,128,128]{2,1,0:T(8,128)S(1)} %get-tuple-element.213), channel_id=1, source_target_pairs={{0,4},{4,0},{8,12},{12,8},{16,20},{20,16},{24,28},{28,24},{1,5},{5... | collective-permute-start | bytes 393224 | tf_op jit(solution)/shard_map/ppermute | solution.py:224
  99.5 6.9 %collective-permute-start.38 = (f32[2,128,128]{2,1,0:T(8,128)S(1)}, f32[2,128,128]{2,1,0:T(8,128)S(1)}, u32[]{:S(2)}, u32[]{:S(2)}) collective-permute-start(f32[2,128,128]{2,1,0:T(8,128)S(1)} %get-tuple-element.211), channel_id=1, source_target_pairs={{12,4},{8,0},{13,5},{9,1},{14,6},{10,2},{15,7},{11,3}} | collective-permute-start | bytes 393224 | tf_op jit(solution)/shard_map/ppermute | solution.py:171
  101.4 15.4 %collective-permute-start.41 = (f32[2,128,128]{2,1,0:T(8,128)S(1)}, f32[2,128,128]{2,1,0:T(8,128)S(1)}, u32[]{:S(2)}, u32[]{:S(2)}) collective-permute-start(f32[2,128,128]{2,1,0:T(8,128)S(1)} %get-tuple-element.209), channel_id=1, source_target_pairs={{0,4},{4,0},{8,12},{12,8},{16,20},{20,16},{24,28},{28,24},{1,5},{5... | collective-permute-start | bytes 393224 | tf_op jit(solution)/shard_map/ppermute | solution.py:224
  103.0 6.9 %collective-permute-start.37 = (f32[2,128,128]{2,1,0:T(8,128)S(1)}, f32[2,128,128]{2,1,0:T(8,128)S(1)}, u32[]{:S(2)}, u32[]{:S(2)}) collective-permute-start(f32[2,128,128]{2,1,0:T(8,128)S(1)} %get-tuple-element.207), channel_id=1, source_target_pairs={{12,4},{8,0},{13,5},{9,1},{14,6},{10,2},{15,7},{11,3}} | collective-permute-start | bytes 393224 | tf_op jit(solution)/shard_map/ppermute | solution.py:171
  106.4 11.7 %collective-permute-start.40 = (f32[2,128,128]{2,1,0:T(8,128)S(1)}, f32[2,128,128]{2,1,0:T(8,128)S(1)}, u32[]{:S(2)}, u32[]{:S(2)}) collective-permute-start(f32[2,128,128]{2,1,0:T(8,128)S(1)} %get-tuple-element.205), channel_id=1, source_target_pairs={{0,4},{4,0},{8,12},{12,8},{16,20},{20,16},{24,28},{28,24},{1,5},{5... | collective-permute-start | bytes 393224 | tf_op jit(solution)/shard_map/ppermute | solution.py:224
  109.8 9.5 %collective-permute-start.39 = (f32[2,128,128]{2,1,0:T(8,128)S(1)}, f32[2,128,128]{2,1,0:T(8,128)S(1)}, u32[]{:S(2)}, u32[]{:S(2)}) collective-permute-start(f32[2,128,128]{2,1,0:T(8,128)S(1)} %get-tuple-element.203), channel_id=1, source_target_pairs={{0,4},{4,0},{8,12},{12,8},{16,20},{20,16},{24,28},{28,24},{1,5},{5... | collective-permute-start | bytes 393224 | tf_op jit(solution)/shard_map/ppermute | solution.py:224
  (37 other events, 66.4 us)

commit v6 on v5

--- a/solution.py
+++ b/solution.py
@@ -36,11 +36,10 @@
 HBM, VMEM = pltpu.HBM, pltpu.VMEM
 
 
-def call(body, place, ins, outs, grid=(1,), aliases=None, flops=0, grant=6):
+def call(body, place, ins, outs, grid=(1,), aliases=None, grant=6):
     ins = [(*item, None)[:4] for item in ins]
     outs = [(*item, None)[:5] for item in outs]
     arrays = [pltpu.with_memory_space_constraint(a, m) if m else a for a, _, _, m in ins]
-    size = sum(a.size * a.dtype.itemsize // 2 for a in arrays)
     return pl.pallas_call(
         body,
         grid_spec=pltpu.PrefetchScalarGridSpec(
@@ -52,7 +51,7 @@
         out_shape=[(m or jax.ShapeDtypeStruct)(s, d) for s, d, _, _, m in outs],
         input_output_aliases=aliases or {},
         compiler_params=pltpu.CompilerParams(vmem_limit_bytes=grant * 1024 * 1024),
-        cost_estimate=pl.CostEstimate(flops=flops, bytes_accessed=size, transcendentals=0),
+        cost_estimate=pl.CostEstimate(flops=1024, bytes_accessed=1024, transcendentals=0),
     )(place, *arrays)
 
 
@@ -125,10 +124,12 @@
             outs[chunks + c][j] = dot(head(q, h), x, 0, 0)
 
 
-def query_body(per, place, k, v, d_k, d_o, sb_k, sb_o, *refs):
+def query_body(per, chunks, place, k, v, *refs):
     qg = refs[-1]
     mask = causal()
-    for turn, d, sb in ((0, d_k, sb_k), (1, d_o, sb_o)):
+    for turn in range(2 * chunks):
+        d, sb = refs[turn], refs[2 * chunks + turn]
+
         @pl.when(pl.program_id(0) == turn)
         def _():
             for j in range(per):
@@ -184,7 +185,7 @@
             out.append(carry)
         return out
 
-    def scan(kept, sent, y, reverse, ready):
+    def scan(kept, sent, y, reverse, ready, beside):
         own = [None] * len(kept)
         if long > 4 or long < 2:
             swapped = [lax.ppermute(b, "seq", swap) for b in sent]
@@ -209,6 +210,8 @@
         swap_after(1)
         swap_after(2, *ready)
         for _, _, c, stage in order:
+            if (stage, c) in beside:
+                last = last + [beside[stage, c](out)]
             got, *_ = lax.optimization_barrier((flight[c], *last))
             if stage == 0:
                 own[c] = jnp.where(y == 0, 0.0, got)
@@ -237,7 +240,6 @@
         place = y.astype(jnp.int32).reshape(1)
         turned = 1 - place
         gain = norm_gain.reshape(1, width)
-        mac = 2 * GROUP * DH
 
         kept_half = lambda i, s: (0, s[0])
         sent_half = lambda i, s: (0, 1 - s[0])
@@ -254,7 +256,6 @@
             functools.partial(states_body, per), place,
             [(a, (tokens, wide), sent_half, HBM) for a in (keys, values)],
             [((per, DH, DH), F32, (per, DH, DH), whole3, VMEM)] * CHUNKS,
-            flops=half * mac * DH,
         )
 
         group = half // 2
@@ -263,12 +264,12 @@
             functools.partial(local_body, per, CHUNKS, group), place,
             [(a, (tokens, group * DH), strip, HBM) for a in (queries, keys, values)],
             [((per, DH, DH), F32, (per, DH, DH), whole3, VMEM)] * CHUNKS + [
-                ((tokens, width), F32, (tokens, group * DH), strip, VMEM),
+                ((tokens, width), F32, (tokens, group * DH), strip, HBM),
             ],
-            grid=(4,), flops=heads * mac * (2 * GROUP + DH // 2),
+            grid=(4,),
         )
 
-        before = scan(kept, sent, y, False, [attn_local])
+        before = scan(kept, sent, y, False, [attn_local], {})
 
         block = (tokens, narrow)
         square = cross = None
@@ -289,7 +290,7 @@
             else:
                 outs += [((GROUP, DH), F32, (GROUP, DH), whole2)] * 2
             a_k, a_o, s_k, s_o, *stats = call(
-                functools.partial(attn_body, per, first, last), place, ins, outs, flops=2 * per * mac * DH)
+                functools.partial(attn_body, per, first, last), place, ins, outs)
             attns.append((a_k, a_o))
             priors.append((s_k, s_o))
             if last:
@@ -310,48 +311,62 @@
             outs = [(block, BF16, block, whole2, VMEM)] * CHUNKS
             outs += [((per, DH, DH), F32, (per, DH, DH), whole3, VMEM)] * CHUNKS
             result = call(
-                functools.partial(delta_body, per, CHUNKS, parts, float(parts * heads * DH)), place, ins, outs,
-                flops=half * mac * DH)
+                functools.partial(delta_body, per, CHUNKS, parts, float(parts * heads * DH)), place, ins, outs)
             return result[:CHUNKS], result[CHUNKS:]
 
         d_o, sent = delta(1, sent_half)
         d_k, kept = delta(0, kept_half)
 
         def mine(c):
-            return lambda i, s: (0, jnp.where(i == 0, s[0], 1 - s[0]) * CHUNKS + c)
+            return lambda i, s: (0, jnp.where(i % 2 == 0, s[0], 1 - s[0]) * CHUNKS + c + i // 2)
 
         state3 = (per, DH, DH)
-        qg = None
-        for c in range(CHUNKS):
-            ins = [(a, block, mine(c)) for a in (keys, values)]
-            ins += [(a, block, whole2) for a in (d_k[c], d_o[c])]
-            ins += [(a, state3, whole3) for a in priors[c]]
+        made = {"query": [], "rest": []}
+
+        def query(c, count):
+            ins = [(a, block, mine(c), HBM) for a in (keys, values)]
+            some = range(c, c + count)
+            ins += [(a, block, whole2) for i in some for a in (d_k[i], d_o[i])]
+            ins += [(a, state3, whole3) for i in some for a in priors[i]]
             aliases = {}
-            if c > 0:
+            if made["query"]:
                 aliases[len(ins) + 1] = 0
-                ins.append((qg, None, None, HBM))
-            qg, = call(
-                functools.partial(query_body, per), place, ins, [((tokens, width), BF16, block, mine(c), HBM)],
-                grid=(2,), aliases=aliases, flops=2 * per * mac * (2 * GROUP + DH))
-
-        after = scan(kept, sent, 1 - y, True, [qg])
-
-        grads = None
-        turns = [(c, 0) for c in range(CHUNKS)] + [(c, 1) for c in range(CHUNKS)]
-        for c, which in turns:
+                ins += [(a, None, None, HBM) for a in made["query"]]
+            made["query"] = call(
+                functools.partial(query_body, per, count), place, ins,
+                [((tokens, width), BF16, block, mine(c), HBM)], grid=(2 * count,), aliases=aliases)
+            return made["query"][0]
+
+        def rest(c, which, after):
             index, d = ((at_k(c), d_k[c]), (at_o(c), d_o[c]))[which]
             states = after[c][2:] if which else after[c][:2]
-            ins = [(a, block, index) for a in (queries, keys, values)]
+            ins = [(a, block, index, HBM) for a in (queries, keys, values)]
             ins += [(d, block, whole2)] + [(a, state3, whole3) for a in states]
             aliases = {}
-            if grads is not None:
+            if made["rest"]:
                 aliases = {len(ins) + 1: 0, len(ins) + 2: 1}
-                ins += [(a, None, None, HBM) for a in grads]
-            grads = call(
+                ins += [(a, None, None, HBM) for a in made["rest"]]
+            made["rest"] = call(
                 functools.partial(final_body, per, len(states)), place, ins,
                 [((tokens, width), BF16, block, index, HBM)] * 2,
-                aliases=aliases, flops=per * mac * (4 * GROUP + 2 * DH))
-        return qg, grads[0], grads[1]
+                aliases=aliases)
+            return made["rest"][0]
+
+        tail = long - 1
+        beside = {
+            (1, 0): lambda out: query(2, 1),
+            (2, 0): lambda out: query(3, 1),
+            (tail, CHUNKS - 2): lambda out: rest(0, 0, out),
+            (tail, CHUNKS - 1): lambda out: rest(1, 0, out),
+        } if 2 < long <= 4 else {}
+        after = scan(kept, sent, 1 - y, True, [query(0, 2)], beside)
+        if not beside:
+            query(2, 2)
+        for c in range(2 if beside else 0, CHUNKS):
+            rest(c, 0, after)
+        for c in range(CHUNKS):
+            rest(c, 1, after)
+        return made["query"][0], made["rest"][0], made["rest"][1]
 
     return jax.shard_map(
         shards,

time: 121 us -> 116 us (0.959)
  Pallas kernels: 26.3 us -> 38.3 us
  local copies, waits for them, and re-layouts: 15.5 us -> 5.19 us
  waiting for transfers between devices: 24.3 us -> 19.9 us
  other arithmetic: 4.34 us -> 1.71 us
    pallas_call x20 -> x19, Pallas kernels: 26.3 us -> 38.3 us  [call(): pl.pallas_call(body, grid_spec=pltpu.PrefetchScalarGridSpec(num_scalar_pr...]
    unnamed x84 -> x56, local copies, waits for them, and re-layouts: 15.5 us -> 5.18 us
    ppermute x24, waiting for transfers between devices: 20.4 us -> 11 us  [hop(): return lax.ppermute(array, 'seq', pairs)]
    ppermute x8, waiting for transfers between devices: 0.61 us -> 3.51 us  [scan(): out[c] = (carry[c], own[c], lax.ppermute(send, 'seq', swap))]
    select_n x8, other arithmetic: 2.89 us -> 1.07 us  [scan(): own[c] = jnp.where(y == 0, 0.0, got)]
    ppermute x8, waiting for transfers between devices: 1.49 us -> 2.76 us  [swap_after(): flight[c] = lax.ppermute(part_sent, 'seq', swap)]
  transfers between devices with their start and end apart: 43 -> 43, of which waited for: 11 -> 11; matrix products, arithmetic and copies ran while one was open for 4% -> 1% of each run, Pallas kernels for 18% -> 29%
where the time goes in v6:
time: 116 us; the launch traced here: 115 us
  starting transfers between devices  48.6 us (42%)
  Pallas kernels  38.3 us (33%)
  waiting for transfers between devices  19.9 us (17%)
  local copies, waits for them, and re-layouts  5.19 us (4%)
  other arithmetic  1.71 us (1%)
  between operations  1.32 us (1%)
    pallas_call x19, Pallas kernels, call(): pl.pallas_call(body, grid_spec=pltpu.PrefetchScalarGridSpec(num_scalar_pr...  38.3 us
    ppermute x24, starting transfers between devices, hop(): return lax.ppermute(array, 'seq', pairs)  28 us
    ppermute x24, waiting for transfers between devices, hop(): return lax.ppermute(array, 'seq', pairs)  11 us
    ppermute x8, starting transfers between devices, swap_after(): flight[c] = lax.ppermute(part_sent, 'seq', swap)  9.67 us
    ppermute x8, starting transfers between devices, scan(): out[c] = (carry[c], own[c], lax.ppermute(send, 'seq', swap))  8.94 us
    unnamed x56, local copies, waits for them, and re-layouts  5.18 us
    ppermute x8, waiting for transfers between devices, scan(): out[c] = (carry[c], own[c], lax.ppermute(send, 'seq', swap))  3.51 us
    ppermute x8, waiting for transfers between devices, swap_after(): flight[c] = lax.ppermute(part_sent, 'seq', swap)  2.76 us
  transfers between devices with their start and end apart: 43, of which 11 were waited for; matrix products, arithmetic and copies ran while one was open for 1% of the time, Pallas kernels for 29%

profile of v6, /device:TPU:0, one launch (start us, length us, event | category | flops | bytes accessed | tf_op | source)
XLA Modules:
  0.0 115.1 jit_solution(14124656902313597446)
XLA Ops:
  0.6 1.6 %shard_map.77 = (f32[2,128,128]{2,1,0:T(8,128)S(1)}, f32[2,128,128]{2,1,0:T(8,128)S(1)}, f32[2,128,128]{2,1,0:T(8,128)S(1)}, f32[2,128,128]{2,1,0:T(8,128)S(1)}) custom-call(s32[1]{0:T(128)} %bitcast.place, bf16[256,2048]{1,0:T(8,128)(2,1)} %k.23, bf16[256,2048]{1,0:T(8,128)(2,1)} %v.23), custom_call_target="tpu_custom_call" | custom-call | flops 1024 | bytes 1024 | tf_op jit(solution)/shard_map/pallas_call | solution.py:43
  2.2 3.0 %collective-permute-start = (f32[2,128,128]{2,1,0:T(8,128)S(1)}, f32[2,128,128]{2,1,0:T(8,128)S(1)}, u32[]{:S(2)}, u32[]{:S(2)}) collective-permute-start(f32[2,128,128]{2,1,0:T(8,128)S(1)} %get-tuple-element.107), channel_id=1, source_target_pairs={{0,4},{4,0},{8,12},{12,8},{16,20},{20,16},{24,28},{28,24},{1,5},{5... | collective-permute-start | bytes 393224 | tf_op jit(solution)/shard_map/ppermute | solution.py:207
  5.3 5.9 %shard_map.76 = (f32[2,128,128]{2,1,0:T(8,128)S(1)}, f32[2,128,128]{2,1,0:T(8,128)S(1)}, f32[2,128,128]{2,1,0:T(8,128)S(1)}, f32[2,128,128]{2,1,0:T(8,128)S(1)}, f32[256,2048]{1,0:T(8,128)}) custom-call(s32[1]{0:T(128)} %bitcast.place, bf16[256,2048]{1,0:T(8,128)(2,1)} %q.17, bf16[256,2048]{1,0:T(8,128)(2,1)} %k.23, bf16[256,2048]{1,0:T(8,128)(2,1)} %v.23), custom_call_target="tpu_custom_call" | custom-call | flops 1024 | bytes 1024 | tf_op jit(solution)/shard_map/pallas_call | solution.py:43
  11.2 2.0 %collective-permute-start.4 = (f32[2,128,128]{2,1,0:T(8,128)S(1)}, f32[2,128,128]{2,1,0:T(8,128)S(1)}, u32[]{:S(2)}, u32[]{:S(2)}) collective-permute-start(f32[2,128,128]{2,1,0:T(8,128)S(1)} %get-tuple-element.115), channel_id=1, source_target_pairs={{0,4},{4,0},{8,12},{12,8},{16,20},{20,16},{24,28},{28,24},{1,5},{5... | collective-permute-start | bytes 393224 | tf_op jit(solution)/shard_map/ppermute | solution.py:207
  13.2 3.5 %collective-permute-start.5 = (f32[2,128,128]{2,1,0:T(8,128)S(1)}, f32[2,128,128]{2,1,0:T(8,128)S(1)}, u32[]{:S(2)}, u32[]{:S(2)}) collective-permute-start(f32[2,128,128]{2,1,0:T(8,128)S(1)} %get-tuple-element.244), channel_id=1, source_target_pairs={{0,8},{4,12},{1,9},{5,13},{2,10},{6,14},{3,11},{7,15}} | collective-permute-start | bytes 393224 | tf_op jit(solution)/shard_map/ppermute | solution.py:172
  17.3 1.3 %collective-permute-start.3 = (f32[2,128,128]{2,1,0:T(8,128)S(1)}, f32[2,128,128]{2,1,0:T(8,128)S(1)}, u32[]{:S(2)}, u32[]{:S(2)}) collective-permute-start(f32[2,128,128]{2,1,0:T(8,128)S(1)} %get-tuple-element.246), channel_id=1, source_target_pairs={{0,8},{4,12},{1,9},{5,13},{2,10},{6,14},{3,11},{7,15}} | collective-permute-start | bytes 393224 | tf_op jit(solution)/shard_map/ppermute | solution.py:172
  18.6 1.6 %collective-permute-done.5 = f32[2,128,128]{2,1,0:T(8,128)S(1)} collective-permute-done((f32[2,128,128]{2,1,0:T(8,128)S(1)}, f32[2,128,128]{2,1,0:T(8,128)S(1)}, u32[]{:S(2)}, u32[]{:S(2)}) %collective-permute-start.5) | collective-permute-done | bytes 131104 | tf_op jit(solution)/shard_map/ppermute | solution.py:172
  20.9 5.0 %collective-permute-start.8 = (f32[2,128,128]{2,1,0:T(8,128)S(1)}, f32[2,128,128]{2,1,0:T(8,128)S(1)}, u32[]{:S(2)}, u32[]{:S(2)}) collective-permute-start(f32[2,128,128]{2,1,0:T(8,128)S(1)} %get-tuple-element.248), channel_id=1, source_target_pairs={{0,8},{4,12},{1,9},{5,13},{2,10},{6,14},{3,11},{7,15}} | collective-permute-start | bytes 393224 | tf_op jit(solution)/shard_map/ppermute | solution.py:172
  26.7 1.9 %collective-permute-start.6 = (f32[2,128,128]{2,1,0:T(8,128)S(1)}, f32[2,128,128]{2,1,0:T(8,128)S(1)}, u32[]{:S(2)}, u32[]{:S(2)}) collective-permute-start(f32[2,128,128]{2,1,0:T(8,128)S(1)} %get-tuple-element.250), channel_id=1, source_target_pairs={{0,8},{4,12},{1,9},{5,13},{2,10},{6,14},{3,11},{7,15}} | collective-permute-start | bytes 393224 | tf_op jit(solution)/shard_map/ppermute | solution.py:172
  30.2 0.8 collective-permute-start.11
  31.1 0.8 collective-permute-start.10
  33.0 1.9 %collective-permute-start.18 = (f32[2,128,128]{2,1,0:T(8,128)S(1)}, f32[2,128,128]{2,1,0:T(8,128)S(1)}, u32[]{:S(2)}, u32[]{:S(2)}) collective-permute-start(f32[2,128,128]{2,1,0:T(8,128)S(1)} %get-tuple-element.225), channel_id=1, source_target_pairs={{0,4},{4,0},{8,12},{12,8},{16,20},{20,16},{24,28},{28,24},{1,5},{5... | collective-permute-start | bytes 393224 | tf_op jit(solution)/shard_map/ppermute | solution.py:227
  36.0 1.9 %collective-permute-start.16 = (f32[2,128,128]{2,1,0:T(8,128)S(1)}, f32[2,128,128]{2,1,0:T(8,128)S(1)}, u32[]{:S(2)}, u32[]{:S(2)}) collective-permute-start(f32[2,128,128]{2,1,0:T(8,128)S(1)} %get-tuple-element.219), channel_id=1, source_target_pairs={{0,4},{4,0},{8,12},{12,8},{16,20},{20,16},{24,28},{28,24},{1,5},{5... | collective-permute-start | bytes 393224 | tf_op jit(solution)/shard_map/ppermute | solution.py:227
  39.4 0.7 collective-permute-done.18.other
  40.5 1.1 collective-permute-done.17.other
  41.9 1.1 collective-permute-done.16.other
  43.5 1.6 %collective-permute-start.21 = (f32[2,256]{1,0:T(2,128)S(1)}, f32[2,256]{1,0:T(2,128)S(1)}, u32[]{:S(2)}, u32[]{:S(2)}) collective-permute-start(f32[2,256]{1,0:T(2,128)S(1)} %get-tuple-element.136.refs_0_), channel_id=1, source_target_pairs={{0,2},{1,3},{2,0},{3,1},{4,6},{5,7},{6,4},{7,5},{8,10},{9,11},{10,... | collective-permute-start | bytes 6152 | tf_op jit(solution)/shard_map/ppermute | solution.py:304
  45.4 1.8 %collective-permute-done.21.refs_2_ = f32[2,256]{1,0:T(2,128)S(1)} collective-permute-done((f32[2,256]{1,0:T(2,128)S(1)}, f32[2,256]{1,0:T(2,128)S(1)}, u32[]{:S(2)}, u32[]{:S(2)}) %collective-permute-start.21) | collective-permute-done | bytes 2080 | tf_op jit(solution)/shard_map/ppermute | solution.py:304
  47.2 0.9 collective-permute-done.22.refs_3_
  48.1 1.2 %shard_map.83 = (bf16[256,256]{1,0:T(8,128)(2,1)S(1)}, bf16[256,256]{1,0:T(8,128)(2,1)S(1)}, bf16[256,256]{1,0:T(8,128)(2,1)S(1)}, bf16[256,256]{1,0:T(8,128)(2,...) custom-call(s32[1]{0:T(128)} %bitcast.place, ...), custom_call_target="tpu_custom_call" | custom-call | flops 1024 | bytes 1024 | tf_op jit(solution)/shard_map/pallas_call | solution.py:43
  51.2 1.2 %collective-permute-start.23 = (f32[2,128,128]{2,1,0:T(8,128)}, f32[2,128,128]{2,1,0:T(8,128)}, u32[]{:S(2)}, u32[]{:S(2)}) collective-permute-start(f32[2,128,128]{2,1,0:T(8,128)} %get-tuple-element.164), channel_id=1, source_target_pairs={{0,4},{4,0},{8,12},{12,8},{16,20},{20,16},{24,28},{28,24},{1,5},{5... | collective-permute-start | bytes 393224 | tf_op jit(solution)/shard_map/ppermute | solution.py:207
  52.4 0.9 copy-done.4
  54.0 0.7 copy-done.20
  55.6 4.2 %shard_map.84.refs_4_ = bf16[256,2048]{1,0:T(8,128)(2,1)} custom-call(s32[1]{0:T(128)} %bitcast.place, bf16[256,2048]{1,0:T(8,128)(2,1)} %k.23, bf16[256,2048]{1,0:T(8,128)(2,1)} %v.23, bf16[256,256]{1,0:T(8,128)(2,1)S(1)} %get-tuple-element.153.refs_0_.d, bf16[256,256]{1,0:T(8,128)(2,1)S(1)} %get-tuple-element.154.refs_1_.d, ...), custom_call_target="tpu_custom_call" | custom-call | flops 1024 | bytes 1024 | tf_op jit(solution)/shard_map/pallas_call | solution.py:43
  59.8 0.9 collective-permute-start.25
  60.7 1.2 %collective-permute-start.27 = (f32[2,128,128]{2,1,0:T(8,128)S(1)}, f32[2,128,128]{2,1,0:T(8,128)S(1)}, u32[]{:S(2)}, u32[]{:S(2)}) collective-permute-start(f32[2,128,128]{2,1,0:T(8,128)S(1)} %copy-done.24), channel_id=1, source_target_pairs={{0,4},{4,0},{8,12},{12,8},{16,20},{20,16},{24,28},{28,24},{1,5},{5... | collective-permute-start | bytes 393224 | tf_op jit(solution)/shard_map/ppermute | solution.py:207
  61.8 0.9 broadcast_select_fusion.3
  63.4 2.7 %collective-permute-done.25 = f32[2,128,128]{2,1,0:T(8,128)S(1)} collective-permute-done((f32[2,128,128]{2,1,0:T(8,128)S(1)}, f32[2,128,128]{2,1,0:T(8,128)S(1)}, u32[]{:S(2)}, u32[]{:S(2)}) %collective-permute-start.25) | collective-permute-done | bytes 131104 | tf_op jit(solution)/shard_map/ppermute | solution.py:207
  66.2 0.9 collective-permute-start.24
  67.8 2.6 %shard_map.85.refs_4_ = bf16[256,2048]{1,0:T(8,128)(2,1)} custom-call(s32[1]{0:T(128)} %bitcast.place, bf16[256,2048]{1,0:T(8,128)(2,1)} %k.23, bf16[256,2048]{1,0:T(8,128)(2,1)} %v.23, bf16[256,256]{1,0:T(8,128)(2,1)S(1)} %get-tuple-element.149.refs_0_.d, bf16[256,256]{1,0:T(8,128)(2,1)S(1)} %get-tuple-element.150.refs_1_.d, ...), custom_call_target="tpu_custom_call", output_to_operand_aliasing={{}: (7, {})} | custom-call | flops 1024 | bytes 1024 | tf_op jit(solution)/shard_map/pallas_call | solution.py:43
  73.2 2.6 %shard_map.86 = bf16[256,2048]{1,0:T(8,128)(2,1)} custom-call(s32[1]{0:T(128)} %bitcast.place, bf16[256,2048]{1,0:T(8,128)(2,1)} %k.23, bf16[256,2048]{1,0:T(8,128)(2,1)} %v.23, bf16[256,256]{1,0:T(8,128)(2,1)S(1)} %get-tuple-element.141.refs_0_.d, bf16[256,256]{1,0:T(8,128)(2,1)S(1)} %get-tuple-element.146.refs_1_.d, ...), custom_call_target="tpu_custom_call", output_to_operand_aliasing={{}: (7, {})} | custom-call | flops 1024 | bytes 1024 | tf_op jit(solution)/shard_map/pallas_call | solution.py:43
  75.8 1.3 %collective-permute-start.36 = (f32[2,128,128]{2,1,0:T(8,128)S(1)}, f32[2,128,128]{2,1,0:T(8,128)S(1)}, u32[]{:S(2)}, u32[]{:S(2)}) collective-permute-start(f32[2,128,128]{2,1,0:T(8,128)S(1)} %get-tuple-element.217), channel_id=1, source_target_pairs={{12,4},{8,0},{13,5},{9,1},{14,6},{10,2},{15,7},{11,3}} | collective-permute-start | bytes 393224 | tf_op jit(solution)/shard_map/ppermute | solution.py:172
  77.8 1.3 %collective-permute-start.34 = (f32[2,128,128]{2,1,0:T(8,128)S(1)}, f32[2,128,128]{2,1,0:T(8,128)S(1)}, u32[]{:S(2)}, u32[]{:S(2)}) collective-permute-start(f32[2,128,128]{2,1,0:T(8,128)S(1)} %get-tuple-element.215), channel_id=1, source_target_pairs={{12,4},{8,0},{13,5},{9,1},{14,6},{10,2},{15,7},{11,3}} | collective-permute-start | bytes 393224 | tf_op jit(solution)/shard_map/ppermute | solution.py:172
  79.9 8.6 %collective-permute-done.36 = f32[2,128,128]{2,1,0:T(8,128)S(1)} collective-permute-done((f32[2,128,128]{2,1,0:T(8,128)S(1)}, f32[2,128,128]{2,1,0:T(8,128)S(1)}, u32[]{:S(2)}, u32[]{:S(2)}) %collective-permute-start.36) | collective-permute-done | bytes 131104 | tf_op jit(solution)/shard_map/ppermute | solution.py:172
  88.5 1.3 %collective-permute-start.42 = (f32[2,128,128]{2,1,0:T(8,128)S(1)}, f32[2,128,128]{2,1,0:T(8,128)S(1)}, u32[]{:S(2)}, u32[]{:S(2)}) collective-permute-start(f32[2,128,128]{2,1,0:T(8,128)S(1)} %get-tuple-element.213), channel_id=1, source_target_pairs={{0,4},{4,0},{8,12},{12,8},{16,20},{20,16},{24,28},{28,24},{1,5},{5... | collective-permute-start | bytes 393224 | tf_op jit(solution)/shard_map/ppermute | solution.py:227
  89.9 1.3 %collective-permute-start.38 = (f32[2,128,128]{2,1,0:T(8,128)S(1)}, f32[2,128,128]{2,1,0:T(8,128)S(1)}, u32[]{:S(2)}, u32[]{:S(2)}) collective-permute-start(f32[2,128,128]{2,1,0:T(8,128)S(1)} %get-tuple-element.211), channel_id=1, source_target_pairs={{12,4},{8,0},{13,5},{9,1},{14,6},{10,2},{15,7},{11,3}} | collective-permute-start | bytes 393224 | tf_op jit(solution)/shard_map/ppermute | solution.py:172
  91.2 1.2 %collective-permute-start.41 = (f32[2,128,128]{2,1,0:T(8,128)S(1)}, f32[2,128,128]{2,1,0:T(8,128)S(1)}, u32[]{:S(2)}, u32[]{:S(2)}) collective-permute-start(f32[2,128,128]{2,1,0:T(8,128)S(1)} %get-tuple-element.209), channel_id=1, source_target_pairs={{0,4},{4,0},{8,12},{12,8},{16,20},{20,16},{24,28},{28,24},{1,5},{5... | collective-permute-start | bytes 393224 | tf_op jit(solution)/shard_map/ppermute | solution.py:227
  92.4 1.5 %collective-permute-start.37 = (f32[2,128,128]{2,1,0:T(8,128)S(1)}, f32[2,128,128]{2,1,0:T(8,128)S(1)}, u32[]{:S(2)}, u32[]{:S(2)}) collective-permute-start(f32[2,128,128]{2,1,0:T(8,128)S(1)} %get-tuple-element.207), channel_id=1, source_target_pairs={{12,4},{8,0},{13,5},{9,1},{14,6},{10,2},{15,7},{11,3}} | collective-permute-start | bytes 393224 | tf_op jit(solution)/shard_map/ppermute | solution.py:172
  93.9 2.3 %shard_map.87 = (bf16[256,2048]{1,0:T(8,128)(2,1)}, bf16[256,2048]{1,0:T(8,128)(2,1)}) custom-call(s32[1]{0:T(128)} %bitcast.place, bf16[256,2048]{1,0:T(8,128)(2,1)} %q.17, bf16[256,2048]{1,0:T(8,128)(2,1)} %k.23, bf16[256,2048]{1,0:T(8,128)(2,1)} %v.23, bf16[256,256]{1,0:T(8,128)(2,1)S(1)} %get-tuple-element.153.refs_0_.d, ...), custom_call_target="tpu_custom_call" | custom-call | flops 1024 | bytes 1024 | tf_op jit(solution)/shard_map/pallas_call | solution.py:43
  96.7 1.0 collective-permute-start.40
  97.8 2.3 %shard_map.88 = (bf16[256,2048]{1,0:T(8,128)(2,1)}, bf16[256,2048]{1,0:T(8,128)(2,1)}) custom-call(s32[1]{0:T(128)} %bitcast.place, bf16[256,2048]{1,0:T(8,128)(2,1)} %q.17, bf16[256,2048]{1,0:T(8,128)(2,1)} %k.23, bf16[256,2048]{1,0:T(8,128)(2,1)} %v.23, ...), custom_call_target="tpu_custom_call", output_to_operand_aliasing={{0}: (7, {}), {1}: (8, {})} | custom-call | flops 1024 | bytes 1024 | tf_op jit(solution)/shard_map/pallas_call | solution.py:43
  100.1 1.1 collective-permute-start.39
  101.2 2.3 %shard_map.89 = (bf16[256,2048]{1,0:T(8,128)(2,1)}, bf16[256,2048]{1,0:T(8,128)(2,1)}) custom-call(s32[1]{0:T(128)} %bitcast.place, bf16[256,2048]{1,0:T(8,128)(2,1)} %q.17, bf16[256,2048]{1,0:T(8,128)(2,1)} %k.23, bf16[256,2048]{1,0:T(8,128)(2,1)} %v.23, ...), custom_call_target="tpu_custom_call", output_to_operand_aliasing={{0}: (7, {}), {1}: (8, {})} | custom-call | flops 1024 | bytes 1024 | tf_op jit(solution)/shard_map/pallas_call | solution.py:43
  103.5 2.3 %shard_map.90 = (bf16[256,2048]{1,0:T(8,128)(2,1)}, bf16[256,2048]{1,0:T(8,128)(2,1)}) custom-call(s32[1]{0:T(128)} %bitcast.place, bf16[256,2048]{1,0:T(8,128)(2,1)} %q.17, bf16[256,2048]{1,0:T(8,128)(2,1)} %k.23, bf16[256,2048]{1,0:T(8,128)(2,1)} %v.23, ...), custom_call_target="tpu_custom_call", output_to_operand_aliasing={{0}: (7, {}), {1}: (8, {})} | custom-call | flops 1024 | bytes 1024 | tf_op jit(solution)/shard_map/pallas_call | solution.py:43
  105.8 2.3 %shard_map.91 = (bf16[256,2048]{1,0:T(8,128)(2,1)}, bf16[256,2048]{1,0:T(8,128)(2,1)}) custom-call(s32[1]{0:T(128)} %bitcast.place, bf16[256,2048]{1,0:T(8,128)(2,1)} %q.17, bf16[256,2048]{1,0:T(8,128)(2,1)} %k.23, bf16[256,2048]{1,0:T(8,128)(2,1)} %v.23, ...), custom_call_target="tpu_custom_call", output_to_operand_aliasing={{0}: (6, {}), {1}: (7, {})} | custom-call | flops 1024 | bytes 1024 | tf_op jit(solution)/shard_map/pallas_call | solution.py:43
  108.2 2.3 %shard_map.92 = (bf16[256,2048]{1,0:T(8,128)(2,1)}, bf16[256,2048]{1,0:T(8,128)(2,1)}) custom-call(s32[1]{0:T(128)} %bitcast.place, bf16[256,2048]{1,0:T(8,128)(2,1)} %q.17, bf16[256,2048]{1,0:T(8,128)(2,1)} %k.23, bf16[256,2048]{1,0:T(8,128)(2,1)} %v.23, ...), custom_call_target="tpu_custom_call", output_to_operand_aliasing={{0}: (6, {}), {1}: (7, {})} | custom-call | flops 1024 | bytes 1024 | tf_op jit(solution)/shard_map/pallas_call | solution.py:43
  110.5 2.3 %shard_map.93 = (bf16[256,2048]{1,0:T(8,128)(2,1)}, bf16[256,2048]{1,0:T(8,128)(2,1)}) custom-call(s32[1]{0:T(128)} %bitcast.place, bf16[256,2048]{1,0:T(8,128)(2,1)} %q.17, bf16[256,2048]{1,0:T(8,128)(2,1)} %k.23, bf16[256,2048]{1,0:T(8,128)(2,1)} %v.23, ...), custom_call_target="tpu_custom_call", output_to_operand_aliasing={{0}: (6, {}), {1}: (7, {})} | custom-call | flops 1024 | bytes 1024 | tf_op jit(solution)/shard_map/pallas_call | solution.py:43
  112.8 2.3 %shard_map.94 = (bf16[256,2048]{1,0:T(8,128)(2,1)}, bf16[256,2048]{1,0:T(8,128)(2,1)}) custom-call(s32[1]{0:T(128)} %bitcast.place, bf16[256,2048]{1,0:T(8,128)(2,1)} %q.17, bf16[256,2048]{1,0:T(8,128)(2,1)} %k.23, bf16[256,2048]{1,0:T(8,128)(2,1)} %v.23, ...), custom_call_target="tpu_custom_call", output_to_operand_aliasing={{0}: (6, {}), {1}: (7, {})} | custom-call | flops 1024 | bytes 1024 | tf_op jit(solution)/shard_map/pallas_call | solution.py:43
  (146 shorter events, 18.6 us)
Async XLA Ops:
  2.2 11.0 %collective-permute-start = (f32[2,128,128]{2,1,0:T(8,128)S(1)}, f32[2,128,128]{2,1,0:T(8,128)S(1)}, u32[]{:S(2)}, u32[]{:S(2)}) collective-permute-start(f32[2,128,128]{2,1,0:T(8,128)S(1)} %get-tuple-element.107), channel_id=1, source_target_pairs={{0,4},{4,0},{8,12},{12,8},{16,20},{20,16},{24,28},{28,24},{1,5},{5... | collective-permute-start | bytes 393224 | tf_op jit(solution)/shard_map/ppermute | solution.py:207
  5.2 12.0 %collective-permute-start.2 = (f32[2,128,128]{2,1,0:T(8,128)S(1)}, f32[2,128,128]{2,1,0:T(8,128)S(1)}, u32[]{:S(2)}, u32[]{:S(2)}) collective-permute-start(f32[2,128,128]{2,1,0:T(8,128)S(1)} %get-tuple-element.111), channel_id=1, source_target_pairs={{0,4},{4,0},{8,12},{12,8},{16,20},{20,16},{24,28},{28,24},{1,5},{5... | collective-permute-start | bytes 393224 | tf_op jit(solution)/shard_map/ppermute | solution.py:207
  11.2 9.7 %collective-permute-start.4 = (f32[2,128,128]{2,1,0:T(8,128)S(1)}, f32[2,128,128]{2,1,0:T(8,128)S(1)}, u32[]{:S(2)}, u32[]{:S(2)}) collective-permute-start(f32[2,128,128]{2,1,0:T(8,128)S(1)} %get-tuple-element.115), channel_id=1, source_target_pairs={{0,4},{4,0},{8,12},{12,8},{16,20},{20,16},{24,28},{28,24},{1,5},{5... | collective-permute-start | bytes 393224 | tf_op jit(solution)/shard_map/ppermute | solution.py:207
  13.2 7.0 %collective-permute-start.5 = (f32[2,128,128]{2,1,0:T(8,128)S(1)}, f32[2,128,128]{2,1,0:T(8,128)S(1)}, u32[]{:S(2)}, u32[]{:S(2)}) collective-permute-start(f32[2,128,128]{2,1,0:T(8,128)S(1)} %get-tuple-element.244), channel_id=1, source_target_pairs={{0,8},{4,12},{1,9},{5,13},{2,10},{6,14},{3,11},{7,15}} | collective-permute-start | bytes 393224 | tf_op jit(solution)/shard_map/ppermute | solution.py:172
  16.7 10.0 %collective-permute-start.1 = (f32[2,128,128]{2,1,0:T(8,128)S(1)}, f32[2,128,128]{2,1,0:T(8,128)S(1)}, u32[]{:S(2)}, u32[]{:S(2)}) collective-permute-start(f32[2,128,128]{2,1,0:T(8,128)S(1)} %get-tuple-element.109), channel_id=1, source_target_pairs={{0,4},{4,0},{8,12},{12,8},{16,20},{20,16},{24,28},{28,24},{1,5},{5... | collective-permute-start | bytes 393224 | tf_op jit(solution)/shard_map/ppermute | solution.py:207
  17.3 8.7 %collective-permute-start.3 = (f32[2,128,128]{2,1,0:T(8,128)S(1)}, f32[2,128,128]{2,1,0:T(8,128)S(1)}, u32[]{:S(2)}, u32[]{:S(2)}) collective-permute-start(f32[2,128,128]{2,1,0:T(8,128)S(1)} %get-tuple-element.246), channel_id=1, source_target_pairs={{0,8},{4,12},{1,9},{5,13},{2,10},{6,14},{3,11},{7,15}} | collective-permute-start | bytes 393224 | tf_op jit(solution)/shard_map/ppermute | solution.py:172
  20.2 8.4 %collective-permute-start.9 = (f32[2,128,128]{2,1,0:T(8,128)S(1)}, f32[2,128,128]{2,1,0:T(8,128)S(1)}, u32[]{:S(2)}, u32[]{:S(2)}) collective-permute-start(f32[2,128,128]{2,1,0:T(8,128)S(1)} %add.151), channel_id=1, source_target_pairs={{8,16},{12,20},{9,17},{13,21},{10,18},{14,22},{11,19},{15,23}} | collective-permute-start | bytes 393224 | tf_op jit(solution)/shard_map/ppermute | solution.py:172
  20.9 8.4 %collective-permute-start.8 = (f32[2,128,128]{2,1,0:T(8,128)S(1)}, f32[2,128,128]{2,1,0:T(8,128)S(1)}, u32[]{:S(2)}, u32[]{:S(2)}) collective-permute-start(f32[2,128,128]{2,1,0:T(8,128)S(1)} %get-tuple-element.248), channel_id=1, source_target_pairs={{0,8},{4,12},{1,9},{5,13},{2,10},{6,14},{3,11},{7,15}} | collective-permute-start | bytes 393224 | tf_op jit(solution)/shard_map/ppermute | solution.py:172
  26.0 4.1 %collective-permute-start.7 = (f32[2,128,128]{2,1,0:T(8,128)S(1)}, f32[2,128,128]{2,1,0:T(8,128)S(1)}, u32[]{:S(2)}, u32[]{:S(2)}) collective-permute-start(f32[2,128,128]{2,1,0:T(8,128)S(1)} %add.153), channel_id=1, source_target_pairs={{8,16},{12,20},{9,17},{13,21},{10,18},{14,22},{11,19},{15,23}} | collective-permute-start | bytes 393224 | tf_op jit(solution)/shard_map/ppermute | solution.py:172
  26.7 4.4 %collective-permute-start.6 = (f32[2,128,128]{2,1,0:T(8,128)S(1)}, f32[2,128,128]{2,1,0:T(8,128)S(1)}, u32[]{:S(2)}, u32[]{:S(2)}) collective-permute-start(f32[2,128,128]{2,1,0:T(8,128)S(1)} %get-tuple-element.250), channel_id=1, source_target_pairs={{0,8},{4,12},{1,9},{5,13},{2,10},{6,14},{3,11},{7,15}} | collective-permute-start | bytes 393224 | tf_op jit(solution)/shard_map/ppermute | solution.py:172
  28.7 3.3 %collective-permute-start.13 = (f32[2,128,128]{2,1,0:T(8,128)S(1)}, f32[2,128,128]{2,1,0:T(8,128)S(1)}, u32[]{:S(2)}, u32[]{:S(2)}) collective-permute-start(f32[2,128,128]{2,1,0:T(8,128)S(1)} %get-tuple-element.233), channel_id=1, source_target_pairs={{16,24},{20,28},{17,25},{21,29},{18,26},{22,30},{19,27},{23,31}} | collective-permute-start | bytes 393224 | tf_op jit(solution)/shard_map/ppermute | solution.py:172
  29.4 2.9 %collective-permute-start.12 = (f32[2,128,128]{2,1,0:T(8,128)S(1)}, f32[2,128,128]{2,1,0:T(8,128)S(1)}, u32[]{:S(2)}, u32[]{:S(2)}) collective-permute-start(f32[2,128,128]{2,1,0:T(8,128)S(1)} %add.157), channel_id=1, source_target_pairs={{8,16},{12,20},{9,17},{13,21},{10,18},{14,22},{11,19},{15,23}} | collective-permute-start | bytes 393224 | tf_op jit(solution)/shard_map/ppermute | solution.py:172
  30.1 8.4 %copy-start = (bf16[256,2048]{1,0:T(8,128)(2,1)S(1)}, bf16[256,2048]{1,0:T(8,128)(2,1)}, u32[]{:S(2)}) copy-start(bf16[256,2048]{1,0:T(8,128)(2,1)} %q.17) | copy-start | bytes 3145732
  30.1 8.4 %copy-start.1 = (f32[256,2048]{1,0:T(8,128)S(1)}, f32[256,2048]{1,0:T(8,128)}, u32[]{:S(2)}) copy-start(f32[256,2048]{1,0:T(8,128)} %get-tuple-element.103.al_k.al_o) | copy-start | bytes 6291460
  30.2 2.8 %collective-permute-start.11 = (f32[2,128,128]{2,1,0:T(8,128)S(1)}, f32[2,128,128]{2,1,0:T(8,128)S(1)}, u32[]{:S(2)}, u32[]{:S(2)}) collective-permute-start(f32[2,128,128]{2,1,0:T(8,128)S(1)} %get-tuple-element.231), channel_id=1, source_target_pairs={{16,24},{20,28},{17,25},{21,29},{18,26},{22,30},{19,27},{23,31}} | collective-permute-start | bytes 393224 | tf_op jit(solution)/shard_map/ppermute | solution.py:172
  31.1 3.8 %collective-permute-start.10 = (f32[2,128,128]{2,1,0:T(8,128)S(1)}, f32[2,128,128]{2,1,0:T(8,128)S(1)}, u32[]{:S(2)}, u32[]{:S(2)}) collective-permute-start(f32[2,128,128]{2,1,0:T(8,128)S(1)} %add.160), channel_id=1, source_target_pairs={{8,16},{12,20},{9,17},{13,21},{10,18},{14,22},{11,19},{15,23}} | collective-permute-start | bytes 393224 | tf_op jit(solution)/shard_map/ppermute | solution.py:172
  32.0 6.5 %collective-permute-start.19 = (f32[2,128,128]{2,1,0:T(8,128)S(1)}, f32[2,128,128]{2,1,0:T(8,128)S(1)}, u32[]{:S(2)}, u32[]{:S(2)}) collective-permute-start(f32[2,128,128]{2,1,0:T(8,128)S(1)} %get-tuple-element.229), channel_id=1, source_target_pairs={{0,4},{4,0},{8,12},{12,8},{16,20},{20,16},{24,28},{28,24},{1,5},{5... | collective-permute-start | bytes 393224 | tf_op jit(solution)/shard_map/ppermute | solution.py:227
  32.3 3.3 %collective-permute-start.15 = (f32[2,128,128]{2,1,0:T(8,128)S(1)}, f32[2,128,128]{2,1,0:T(8,128)S(1)}, u32[]{:S(2)}, u32[]{:S(2)}) collective-permute-start(f32[2,128,128]{2,1,0:T(8,128)S(1)} %get-tuple-element.227), channel_id=1, source_target_pairs={{16,24},{20,28},{17,25},{21,29},{18,26},{22,30},{19,27},{23,31}} | collective-permute-start | bytes 393224 | tf_op jit(solution)/shard_map/ppermute | solution.py:172
  33.0 7.1 %collective-permute-start.18 = (f32[2,128,128]{2,1,0:T(8,128)S(1)}, f32[2,128,128]{2,1,0:T(8,128)S(1)}, u32[]{:S(2)}, u32[]{:S(2)}) collective-permute-start(f32[2,128,128]{2,1,0:T(8,128)S(1)} %get-tuple-element.225), channel_id=1, source_target_pairs={{0,4},{4,0},{8,12},{12,8},{16,20},{20,16},{24,28},{28,24},{1,5},{5... | collective-permute-start | bytes 393224 | tf_op jit(solution)/shard_map/ppermute | solution.py:227
  34.9 1.0 collective-permute-start.14
  35.7 5.9 %collective-permute-start.17 = (f32[2,128,128]{2,1,0:T(8,128)S(1)}, f32[2,128,128]{2,1,0:T(8,128)S(1)}, u32[]{:S(2)}, u32[]{:S(2)}) collective-permute-start(f32[2,128,128]{2,1,0:T(8,128)S(1)} %get-tuple-element.221), channel_id=1, source_target_pairs={{0,4},{4,0},{8,12},{12,8},{16,20},{20,16},{24,28},{28,24},{1,5},{5... | collective-permute-start | bytes 393224 | tf_op jit(solution)/shard_map/ppermute | solution.py:227
  36.0 7.0 %collective-permute-start.16 = (f32[2,128,128]{2,1,0:T(8,128)S(1)}, f32[2,128,128]{2,1,0:T(8,128)S(1)}, u32[]{:S(2)}, u32[]{:S(2)}) collective-permute-start(f32[2,128,128]{2,1,0:T(8,128)S(1)} %get-tuple-element.219), channel_id=1, source_target_pairs={{0,4},{4,0},{8,12},{12,8},{16,20},{20,16},{24,28},{28,24},{1,5},{5... | collective-permute-start | bytes 393224 | tf_op jit(solution)/shard_map/ppermute | solution.py:227
  43.4 1.9 %collective-permute-start.20 = (f32[2,256]{1,0:T(2,128)S(1)}, f32[2,256]{1,0:T(2,128)S(1)}, u32[]{:S(2)}, u32[]{:S(2)}) collective-permute-start(f32[2,256]{1,0:T(2,128)S(1)} %get-tuple-element.136.refs_0_), channel_id=1, source_target_pairs={{0,1},{1,0},{2,3},{3,2},{4,5},{5,4},{6,7},{7,6},{8,9},{9,8},{10,11... | collective-permute-start | bytes 6152 | tf_op jit(solution)/shard_map/ppermute | solution.py:304
  43.5 3.7 %collective-permute-start.21 = (f32[2,256]{1,0:T(2,128)S(1)}, f32[2,256]{1,0:T(2,128)S(1)}, u32[]{:S(2)}, u32[]{:S(2)}) collective-permute-start(f32[2,256]{1,0:T(2,128)S(1)} %get-tuple-element.136.refs_0_), channel_id=1, source_target_pairs={{0,2},{1,3},{2,0},{3,1},{4,6},{5,7},{6,4},{7,5},{8,10},{9,11},{10,... | collective-permute-start | bytes 6152 | tf_op jit(solution)/shard_map/ppermute | solution.py:304
  45.0 3.0 %collective-permute-start.22 = (f32[2,256]{1,0:T(2,128)S(1)}, f32[2,256]{1,0:T(2,128)S(1)}, u32[]{:S(2)}, u32[]{:S(2)}) collective-permute-start(f32[2,256]{1,0:T(2,128)S(1)} %get-tuple-element.136.refs_0_), channel_id=1, source_target_pairs={{0,3},{1,2},{2,1},{3,0},{4,7},{5,6},{6,5},{7,4},{8,11},{9,10},{10,... | collective-permute-start | bytes 6152 | tf_op jit(solution)/shard_map/ppermute | solution.py:304
  51.2 10.6 %collective-permute-start.23 = (f32[2,128,128]{2,1,0:T(8,128)}, f32[2,128,128]{2,1,0:T(8,128)}, u32[]{:S(2)}, u32[]{:S(2)}) collective-permute-start(f32[2,128,128]{2,1,0:T(8,128)} %get-tuple-element.164), channel_id=1, source_target_pairs={{0,4},{4,0},{8,12},{12,8},{16,20},{20,16},{24,28},{28,24},{1,5},{5... | collective-permute-start | bytes 393224 | tf_op jit(solution)/shard_map/ppermute | solution.py:207
  55.6 10.6 %copy-start.22 = (f32[2,128,128]{2,1,0:T(8,128)S(1)}, f32[2,128,128]{2,1,0:T(8,128)}, u32[]{:S(2)}) copy-start(f32[2,128,128]{2,1,0:T(8,128)} %copy-done.21) | copy-start | bytes 393220
  55.6 12.2 %copy-start.6 = (bf16[2,128,128]{2,1,0:T(8,128)(2,1)S(1)}, bf16[2,128,128]{2,1,0:T(8,128)(2,1)}, u32[]{:S(2)}) copy-start(bf16[2,128,128]{2,1,0:T(8,128)(2,1)} %copy-done.5) | copy-start | bytes 196612
  55.6 12.2 %copy-start.8 = (bf16[2,128,128]{2,1,0:T(8,128)(2,1)S(1)}, bf16[2,128,128]{2,1,0:T(8,128)(2,1)}, u32[]{:S(2)}) copy-start(bf16[2,128,128]{2,1,0:T(8,128)(2,1)} %copy-done.7) | copy-start | bytes 196612
  59.8 6.4 %collective-permute-start.25 = (f32[2,128,128]{2,1,0:T(8,128)S(1)}, f32[2,128,128]{2,1,0:T(8,128)S(1)}, u32[]{:S(2)}, u32[]{:S(2)}) collective-permute-start(f32[2,128,128]{2,1,0:T(8,128)S(1)} %copy-done.26), channel_id=1, source_target_pairs={{0,4},{4,0},{8,12},{12,8},{16,20},{20,16},{24,28},{28,24},{1,5},{5... | collective-permute-start | bytes 393224 | tf_op jit(solution)/shard_map/ppermute | solution.py:207
  60.7 10.4 %collective-permute-start.27 = (f32[2,128,128]{2,1,0:T(8,128)S(1)}, f32[2,128,128]{2,1,0:T(8,128)S(1)}, u32[]{:S(2)}, u32[]{:S(2)}) collective-permute-start(f32[2,128,128]{2,1,0:T(8,128)S(1)} %copy-done.24), channel_id=1, source_target_pairs={{0,4},{4,0},{8,12},{12,8},{16,20},{20,16},{24,28},{28,24},{1,5},{5... | collective-permute-start | bytes 393224 | tf_op jit(solution)/shard_map/ppermute | solution.py:207
  62.8 7.6 %collective-permute-start.28 = (f32[2,128,128]{2,1,0:T(8,128)S(1)}, f32[2,128,128]{2,1,0:T(8,128)S(1)}, u32[]{:S(2)}, u32[]{:S(2)}) collective-permute-start(f32[2,128,128]{2,1,0:T(8,128)S(1)} %get-tuple-element.242), channel_id=1, source_target_pairs={{28,20},{24,16},{29,21},{25,17},{30,22},{26,18},{31,23},{27,19}} | collective-permute-start | bytes 393224 | tf_op jit(solution)/shard_map/ppermute | solution.py:172
  66.2 6.3 %collective-permute-start.24 = (f32[2,128,128]{2,1,0:T(8,128)S(1)}, f32[2,128,128]{2,1,0:T(8,128)S(1)}, u32[]{:S(2)}, u32[]{:S(2)}) collective-permute-start(f32[2,128,128]{2,1,0:T(8,128)S(1)} %copy-done.22), channel_id=1, source_target_pairs={{0,4},{4,0},{8,12},{12,8},{16,20},{20,16},{24,28},{28,24},{1,5},{5... | collective-permute-start | bytes 393224 | tf_op jit(solution)/shard_map/ppermute | solution.py:207
  67.1 4.7 %collective-permute-start.26 = (f32[2,128,128]{2,1,0:T(8,128)S(1)}, f32[2,128,128]{2,1,0:T(8,128)S(1)}, u32[]{:S(2)}, u32[]{:S(2)}) collective-permute-start(f32[2,128,128]{2,1,0:T(8,128)S(1)} %get-tuple-element.240), channel_id=1, source_target_pairs={{28,20},{24,16},{29,21},{25,17},{30,22},{26,18},{31,23},{27,19}} | collective-permute-start | bytes 393224 | tf_op jit(solution)/shard_map/ppermute | solution.py:172
  70.4 5.4 %collective-permute-start.32 = (f32[2,128,128]{2,1,0:T(8,128)S(1)}, f32[2,128,128]{2,1,0:T(8,128)S(1)}, u32[]{:S(2)}, u32[]{:S(2)}) collective-permute-start(f32[2,128,128]{2,1,0:T(8,128)S(1)} %add.175), channel_id=1, source_target_pairs={{20,12},{16,8},{21,13},{17,9},{22,14},{18,10},{23,15},{19,11}} | collective-permute-start | bytes 393224 | tf_op jit(solution)/shard_map/ppermute | solution.py:172
  71.1 6.0 %collective-permute-start.31 = (f32[2,128,128]{2,1,0:T(8,128)S(1)}, f32[2,128,128]{2,1,0:T(8,128)S(1)}, u32[]{:S(2)}, u32[]{:S(2)}) collective-permute-start(f32[2,128,128]{2,1,0:T(8,128)S(1)} %get-tuple-element.236), channel_id=1, source_target_pairs={{28,20},{24,16},{29,21},{25,17},{30,22},{26,18},{31,23},{27,19}} | collective-permute-start | bytes 393224 | tf_op jit(solution)/shard_map/ppermute | solution.py:172
  71.8 6.0 %collective-permute-start.30 = (f32[2,128,128]{2,1,0:T(8,128)S(1)}, f32[2,128,128]{2,1,0:T(8,128)S(1)}, u32[]{:S(2)}, u32[]{:S(2)}) collective-permute-start(f32[2,128,128]{2,1,0:T(8,128)S(1)} %add.177), channel_id=1, source_target_pairs={{20,12},{16,8},{21,13},{17,9},{22,14},{18,10},{23,15},{19,11}} | collective-permute-start | bytes 393224 | tf_op jit(solution)/shard_map/ppermute | solution.py:172
  72.5 6.6 %collective-permute-start.29 = (f32[2,128,128]{2,1,0:T(8,128)S(1)}, f32[2,128,128]{2,1,0:T(8,128)S(1)}, u32[]{:S(2)}, u32[]{:S(2)}) collective-permute-start(f32[2,128,128]{2,1,0:T(8,128)S(1)} %get-tuple-element.238), channel_id=1, source_target_pairs={{28,20},{24,16},{29,21},{25,17},{30,22},{26,18},{31,23},{27,19}} | collective-permute-start | bytes 393224 | tf_op jit(solution)/shard_map/ppermute | solution.py:172
  75.8 12.7 %collective-permute-start.36 = (f32[2,128,128]{2,1,0:T(8,128)S(1)}, f32[2,128,128]{2,1,0:T(8,128)S(1)}, u32[]{:S(2)}, u32[]{:S(2)}) collective-permute-start(f32[2,128,128]{2,1,0:T(8,128)S(1)} %get-tuple-element.217), channel_id=1, source_target_pairs={{12,4},{8,0},{13,5},{9,1},{14,6},{10,2},{15,7},{11,3}} | collective-permute-start | bytes 393224 | tf_op jit(solution)/shard_map/ppermute | solution.py:172
  77.1 12.7 %collective-permute-start.35 = (f32[2,128,128]{2,1,0:T(8,128)S(1)}, f32[2,128,128]{2,1,0:T(8,128)S(1)}, u32[]{:S(2)}, u32[]{:S(2)}) collective-permute-start(f32[2,128,128]{2,1,0:T(8,128)S(1)} %add.181), channel_id=1, source_target_pairs={{20,12},{16,8},{21,13},{17,9},{22,14},{18,10},{23,15},{19,11}} | collective-permute-start | bytes 393224 | tf_op jit(solution)/shard_map/ppermute | solution.py:172
  77.8 13.3 %collective-permute-start.34 = (f32[2,128,128]{2,1,0:T(8,128)S(1)}, f32[2,128,128]{2,1,0:T(8,128)S(1)}, u32[]{:S(2)}, u32[]{:S(2)}) collective-permute-start(f32[2,128,128]{2,1,0:T(8,128)S(1)} %get-tuple-element.215), channel_id=1, source_target_pairs={{12,4},{8,0},{13,5},{9,1},{14,6},{10,2},{15,7},{11,3}} | collective-permute-start | bytes 393224 | tf_op jit(solution)/shard_map/ppermute | solution.py:172
  79.2 13.2 %collective-permute-start.33 = (f32[2,128,128]{2,1,0:T(8,128)S(1)}, f32[2,128,128]{2,1,0:T(8,128)S(1)}, u32[]{:S(2)}, u32[]{:S(2)}) collective-permute-start(f32[2,128,128]{2,1,0:T(8,128)S(1)} %add.184), channel_id=1, source_target_pairs={{20,12},{16,8},{21,13},{17,9},{22,14},{18,10},{23,15},{19,11}} | collective-permute-start | bytes 393224 | tf_op jit(solution)/shard_map/ppermute | solution.py:172
  88.5 17.3 %collective-permute-start.42 = (f32[2,128,128]{2,1,0:T(8,128)S(1)}, f32[2,128,128]{2,1,0:T(8,128)S(1)}, u32[]{:S(2)}, u32[]{:S(2)}) collective-permute-start(f32[2,128,128]{2,1,0:T(8,128)S(1)} %get-tuple-element.213), channel_id=1, source_target_pairs={{0,4},{4,0},{8,12},{12,8},{16,20},{20,16},{24,28},{28,24},{1,5},{5... | collective-permute-start | bytes 393224 | tf_op jit(solution)/shard_map/ppermute | solution.py:227
  89.9 6.9 %collective-permute-start.38 = (f32[2,128,128]{2,1,0:T(8,128)S(1)}, f32[2,128,128]{2,1,0:T(8,128)S(1)}, u32[]{:S(2)}, u32[]{:S(2)}) collective-permute-start(f32[2,128,128]{2,1,0:T(8,128)S(1)} %get-tuple-element.211), channel_id=1, source_target_pairs={{12,4},{8,0},{13,5},{9,1},{14,6},{10,2},{15,7},{11,3}} | collective-permute-start | bytes 393224 | tf_op jit(solution)/shard_map/ppermute | solution.py:172
  91.2 17.0 %collective-permute-start.41 = (f32[2,128,128]{2,1,0:T(8,128)S(1)}, f32[2,128,128]{2,1,0:T(8,128)S(1)}, u32[]{:S(2)}, u32[]{:S(2)}) collective-permute-start(f32[2,128,128]{2,1,0:T(8,128)S(1)} %get-tuple-element.209), channel_id=1, source_target_pairs={{0,4},{4,0},{8,12},{12,8},{16,20},{20,16},{24,28},{28,24},{1,5},{5... | collective-permute-start | bytes 393224 | tf_op jit(solution)/shard_map/ppermute | solution.py:227
  92.4 7.7 %collective-permute-start.37 = (f32[2,128,128]{2,1,0:T(8,128)S(1)}, f32[2,128,128]{2,1,0:T(8,128)S(1)}, u32[]{:S(2)}, u32[]{:S(2)}) collective-permute-start(f32[2,128,128]{2,1,0:T(8,128)S(1)} %get-tuple-element.207), channel_id=1, source_target_pairs={{12,4},{8,0},{13,5},{9,1},{14,6},{10,2},{15,7},{11,3}} | collective-permute-start | bytes 393224 | tf_op jit(solution)/shard_map/ppermute | solution.py:172
  96.7 13.7 %collective-permute-start.40 = (f32[2,128,128]{2,1,0:T(8,128)S(1)}, f32[2,128,128]{2,1,0:T(8,128)S(1)}, u32[]{:S(2)}, u32[]{:S(2)}) collective-permute-start(f32[2,128,128]{2,1,0:T(8,128)S(1)} %get-tuple-element.205), channel_id=1, source_target_pairs={{0,4},{4,0},{8,12},{12,8},{16,20},{20,16},{24,28},{28,24},{1,5},{5... | collective-permute-start | bytes 393224 | tf_op jit(solution)/shard_map/ppermute | solution.py:227
  100.1 12.6 %collective-permute-start.39 = (f32[2,128,128]{2,1,0:T(8,128)S(1)}, f32[2,128,128]{2,1,0:T(8,128)S(1)}, u32[]{:S(2)}, u32[]{:S(2)}) collective-permute-start(f32[2,128,128]{2,1,0:T(8,128)S(1)} %get-tuple-element.203), channel_id=1, source_target_pairs={{0,4},{4,0},{8,12},{12,8},{16,20},{20,16},{24,28},{28,24},{1,5},{5... | collective-permute-start | bytes 393224 | tf_op jit(solution)/shard_map/ppermute | solution.py:227
  (23 other events, 54.2 us)

commit v7 on v6

--- a/solution.py
+++ b/solution.py
@@ -36,7 +36,7 @@
 HBM, VMEM = pltpu.HBM, pltpu.VMEM
 
 
-def call(body, place, ins, outs, grid=(1,), aliases=None, grant=6):
+def call(body, place, ins, outs, grid=(1,), aliases=None, grant=8):
     ins = [(*item, None)[:4] for item in ins]
     outs = [(*item, None)[:5] for item in outs]
     arrays = [pltpu.with_memory_space_constraint(a, m) if m else a for a, _, _, m in ins]
@@ -77,8 +77,9 @@
 
 
 def attn_body(per, first, last, place, al_k, al_o, q_k, q_o, g_k, g_o, n_k, n_o, e, r, other, *refs):
+    one, two, *refs = refs
     if not first:
-        sq_in, cr_in, *refs = refs
+        sq_in, cr_in = one, two
     at_k, at_o, sb_k, sb_o, *stats = refs
     square = jnp.zeros((GROUP, DH), F32) if first else sq_in[...]
     cross = jnp.zeros((GROUP, DH), F32) if first else cr_in[...]
@@ -185,15 +186,15 @@
             out.append(carry)
         return out
 
-    def scan(kept, sent, y, reverse, ready, beside):
+    def scan(kept, sent, leads, reverse, ready, beside):
         own = [None] * len(kept)
         if long > 4 or long < 2:
             swapped = [lax.ppermute(b, "seq", swap) for b in sent]
-            own = [jnp.where(y == 0, 0.0, r) for r in swapped]
+            own = [jnp.where(leads, 0.0, r) for r in swapped]
             sums = [a + r for a, r in zip(kept, swapped)]
             sums = doubling(sums, reverse) if long > 1 else [jnp.zeros_like(a) for a in sums]
             others = [
-                lax.ppermute(jnp.where(y == 0, e + a, e), "seq", swap) for a, e in zip(kept, sums)
+                lax.ppermute(jnp.where(leads, e + a, e), "seq", swap) for a, e in zip(kept, sums)
             ]
             return list(zip(sums, own, others))
         chunks = len(kept)
@@ -214,7 +215,7 @@
                 last = last + [beside[stage, c](out)]
             got, *_ = lax.optimization_barrier((flight[c], *last))
             if stage == 0:
-                own[c] = jnp.where(y == 0, 0.0, got)
+                own[c] = jnp.where(leads, 0.0, got)
                 part[c] = send = kept[c] + got
                 swap_after(c + 3, send)
             else:
@@ -223,7 +224,7 @@
             if stage < long - 1:
                 flight[c] = hop(send, lambda at: at == stage, 1, reverse)
             else:
-                send = jnp.where(y == 0, carry[c] + kept[c], carry[c])
+                send = jnp.where(leads, carry[c] + kept[c], carry[c])
                 out[c] = (carry[c], own[c], lax.ppermute(send, "seq", swap))
             last = [send]
         return [out[c] for c in range(chunks)]
@@ -237,8 +238,7 @@
         narrow = per * DH
         at_seq = lax.axis_index("seq")
         y = at_seq % 2
-        place = y.astype(jnp.int32).reshape(1)
-        turned = 1 - place
+        place, leads, ends = lax.optimization_barrier((y.astype(jnp.int32).reshape(1), y == 0, y == 1))
         gain = norm_gain.reshape(1, width)
 
         kept_half = lambda i, s: (0, s[0])
@@ -264,12 +264,13 @@
             functools.partial(local_body, per, CHUNKS, group), place,
             [(a, (tokens, group * DH), strip, HBM) for a in (queries, keys, values)],
             [((per, DH, DH), F32, (per, DH, DH), whole3, VMEM)] * CHUNKS + [
-                ((tokens, width), F32, (tokens, group * DH), strip, HBM),
+                ((tokens, width), F32, (tokens, group * DH), strip, VMEM),
             ],
             grid=(4,),
         )
-
-        before = scan(kept, sent, y, False, [attn_local], {})
+        tail = long - 1
+        spread = 2 < long <= 4
+        before = scan(kept, sent, leads, False, [attn_local], {})
 
         block = (tokens, narrow)
         square = cross = None
@@ -282,7 +283,9 @@
                 ins += [(a, block, at_k(c)), (a, block, at_o(c))]
             ins += [(gain, (1, narrow), at_k(c)), (gain, (1, narrow), at_o(c))]
             ins += [(a, (per, DH, DH), whole3) for a in (e, r, other)]
-            if not first:
+            if first:
+                ins += [(a, None, None, VMEM) for a in (keys, values)]
+            else:
                 ins += [(a, (GROUP, DH), whole2) for a in (square, cross)]
             outs = [(block, F32, block, whole2, VMEM)] * 2 + [((per, DH, DH), BF16, (per, DH, DH), whole3, VMEM)] * 2
             if last:
@@ -324,7 +327,7 @@
         made = {"query": [], "rest": []}
 
         def query(c, count):
-            ins = [(a, block, mine(c), HBM) for a in (keys, values)]
+            ins = [(a, block, mine(c)) for a in (keys, values)]
             some = range(c, c + count)
             ins += [(a, block, whole2) for i in some for a in (d_k[i], d_o[i])]
             ins += [(a, state3, whole3) for i in some for a in priors[i]]
@@ -340,7 +343,7 @@
         def rest(c, which, after):
             index, d = ((at_k(c), d_k[c]), (at_o(c), d_o[c]))[which]
             states = after[c][2:] if which else after[c][:2]
-            ins = [(a, block, index, HBM) for a in (queries, keys, values)]
+            ins = [(a, block, index) for a in (queries, keys, values)]
             ins += [(d, block, whole2)] + [(a, state3, whole3) for a in states]
             aliases = {}
             if made["rest"]:
@@ -352,14 +355,13 @@
                 aliases=aliases)
             return made["rest"][0]
 
-        tail = long - 1
         beside = {
             (1, 0): lambda out: query(2, 1),
             (2, 0): lambda out: query(3, 1),
             (tail, CHUNKS - 2): lambda out: rest(0, 0, out),
             (tail, CHUNKS - 1): lambda out: rest(1, 0, out),
-        } if 2 < long <= 4 else {}
-        after = scan(kept, sent, 1 - y, True, [query(0, 2)], beside)
+        } if spread else {}
+        after = scan(kept, sent, ends, True, [query(0, 2)], beside)
         if not beside:
             query(2, 2)
         for c in range(2 if beside else 0, CHUNKS):

time: 116 us -> 102 us (0.88)
  Pallas kernels: 38.3 us -> 25.5 us
  waiting for transfers between devices: 19.9 us -> 25.1 us
  local copies, waits for them, and re-layouts: 5.19 us -> 0.04 us
    pallas_call x19, Pallas kernels: 38.3 us -> 25.5 us  [call(): pl.pallas_call(body, grid_spec=pltpu.PrefetchScalarGridSpec(num_scalar_pr...]
    unnamed x56 -> x10, local copies, waits for them, and re-layouts: 5.18 us -> 0.03 us
    ppermute x24, waiting for transfers between devices: 11 us -> 14.6 us  [hop(): return lax.ppermute(array, 'seq', pairs)]
  transfers between devices with their start and end apart: 43 -> 43, of which waited for: 11 -> 13; matrix products, arithmetic and copies ran while one was open for 1% -> 1% of each run, Pallas kernels for 29% -> 21%
where the time goes in v7:
time: 102 us; the launch traced here: 101 us
  starting transfers between devices  48.7 us (48%)
  Pallas kernels  25.5 us (25%)
  waiting for transfers between devices  25.1 us (25%)
  between operations  1.25 us (1%)
    ppermute x24, starting transfers between devices, hop(): return lax.ppermute(array, 'seq', pairs)  28 us
    pallas_call x19, Pallas kernels, call(): pl.pallas_call(body, grid_spec=pltpu.PrefetchScalarGridSpec(num_scalar_pr...  25.5 us
    ppermute x24, waiting for transfers between devices, hop(): return lax.ppermute(array, 'seq', pairs)  14.6 us
    ppermute x8, starting transfers between devices, swap_after(): flight[c] = lax.ppermute(part_sent, 'seq', swap)  9.8 us
    ppermute x8, starting transfers between devices, scan(): out[c] = (carry[c], own[c], lax.ppermute(send, 'seq', swap))  8.96 us
    ppermute x8, waiting for transfers between devices, scan(): out[c] = (carry[c], own[c], lax.ppermute(send, 'seq', swap))  4.16 us
    ppermute x8, waiting for transfers between devices, swap_after(): flight[c] = lax.ppermute(part_sent, 'seq', swap)  3.67 us
    ppermute x3, waiting for transfers between devices, shards(): lax.ppermute(mine, 'head', [(i, i ^ step if paired else (i + step) % part...  2.7 us
  transfers between devices with their start and end apart: 43, of which 13 were waited for; matrix products, arithmetic and copies ran while one was open for 1% of the time, Pallas kernels for 21%

profile of v7, /device:TPU:0, one launch (start us, length us, event | category | flops | bytes accessed | tf_op | source)
XLA Modules:
  0.0 101.4 jit_solution(8798027681246986311)
XLA Ops:
  0.6 1.6 %shard_map.77 = (f32[2,128,128]{2,1,0:T(8,128)S(1)}, f32[2,128,128]{2,1,0:T(8,128)S(1)}, f32[2,128,128]{2,1,0:T(8,128)S(1)}, f32[2,128,128]{2,1,0:T(8,128)S(1)}) custom-call(s32[1]{0:T(128)} %bitcast.place, bf16[256,2048]{1,0:T(8,128)(2,1)} %k.23, bf16[256,2048]{1,0:T(8,128)(2,1)} %v.23), custom_call_target="tpu_custom_call" | custom-call | flops 1024 | bytes 1024 | tf_op jit(solution)/shard_map/pallas_call | solution.py:43
  2.2 3.0 %collective-permute-start = (f32[2,128,128]{2,1,0:T(8,128)S(1)}, f32[2,128,128]{2,1,0:T(8,128)S(1)}, u32[]{:S(2)}, u32[]{:S(2)}) collective-permute-start(f32[2,128,128]{2,1,0:T(8,128)S(1)} %get-tuple-element.111), channel_id=1, source_target_pairs={{0,4},{4,0},{8,12},{12,8},{16,20},{20,16},{24,28},{28,24},{1,5},{5... | collective-permute-start | bytes 393224 | tf_op jit(solution)/shard_map/ppermute | solution.py:208
  5.3 5.0 %shard_map.76 = (f32[2,128,128]{2,1,0:T(8,128)S(1)}, f32[2,128,128]{2,1,0:T(8,128)S(1)}, f32[2,128,128]{2,1,0:T(8,128)S(1)}, f32[2,128,128]{2,1,0:T(8,128)S(1)}, f32[256,2048]{1,0:T(8,128)S(1)}) custom-call(s32[1]{0:T(128)} %bitcast.place, bf16[256,2048]{1,0:T(8,128)(2,1)} %q.17, bf16[256,2048]{1,0:T(8,128)(2,1)} %k.23, bf16[256,2048]{1,0:T(8,128)(2,1)} %v.23), custom_call_target="tpu_custom_call" | custom-call | flops 1024 | bytes 1024 | tf_op jit(solution)/shard_map/pallas_call | solution.py:43
  10.3 2.0 %collective-permute-start.4 = (f32[2,128,128]{2,1,0:T(8,128)S(1)}, f32[2,128,128]{2,1,0:T(8,128)S(1)}, u32[]{:S(2)}, u32[]{:S(2)}) collective-permute-start(f32[2,128,128]{2,1,0:T(8,128)S(1)} %get-tuple-element.119), channel_id=1, source_target_pairs={{0,4},{4,0},{8,12},{12,8},{16,20},{20,16},{24,28},{28,24},{1,5},{5... | collective-permute-start | bytes 393224 | tf_op jit(solution)/shard_map/ppermute | solution.py:208
  12.3 3.5 %collective-permute-start.5 = (f32[2,128,128]{2,1,0:T(8,128)S(1)}, f32[2,128,128]{2,1,0:T(8,128)S(1)}, u32[]{:S(2)}, u32[]{:S(2)}) collective-permute-start(f32[2,128,128]{2,1,0:T(8,128)S(1)} %get-tuple-element.250), channel_id=1, source_target_pairs={{0,8},{4,12},{1,9},{5,13},{2,10},{6,14},{3,11},{7,15}} | collective-permute-start | bytes 393224 | tf_op jit(solution)/shard_map/ppermute | solution.py:173
  16.4 1.3 %collective-permute-start.3 = (f32[2,128,128]{2,1,0:T(8,128)S(1)}, f32[2,128,128]{2,1,0:T(8,128)S(1)}, u32[]{:S(2)}, u32[]{:S(2)}) collective-permute-start(f32[2,128,128]{2,1,0:T(8,128)S(1)} %get-tuple-element.252), channel_id=1, source_target_pairs={{0,8},{4,12},{1,9},{5,13},{2,10},{6,14},{3,11},{7,15}} | collective-permute-start | bytes 393224 | tf_op jit(solution)/shard_map/ppermute | solution.py:173
  17.7 1.6 %collective-permute-done.5 = f32[2,128,128]{2,1,0:T(8,128)S(1)} collective-permute-done((f32[2,128,128]{2,1,0:T(8,128)S(1)}, f32[2,128,128]{2,1,0:T(8,128)S(1)}, u32[]{:S(2)}, u32[]{:S(2)}) %collective-permute-start.5) | collective-permute-done | bytes 131104 | tf_op jit(solution)/shard_map/ppermute | solution.py:173
  19.4 0.7 collective-permute-start.9
  20.1 5.0 %collective-permute-start.8 = (f32[2,128,128]{2,1,0:T(8,128)S(1)}, f32[2,128,128]{2,1,0:T(8,128)S(1)}, u32[]{:S(2)}, u32[]{:S(2)}) collective-permute-start(f32[2,128,128]{2,1,0:T(8,128)S(1)} %get-tuple-element.254), channel_id=1, source_target_pairs={{0,8},{4,12},{1,9},{5,13},{2,10},{6,14},{3,11},{7,15}} | collective-permute-start | bytes 393224 | tf_op jit(solution)/shard_map/ppermute | solution.py:173
  25.1 0.7 collective-permute-start.7
  25.9 1.9 %collective-permute-start.6 = (f32[2,128,128]{2,1,0:T(8,128)S(1)}, f32[2,128,128]{2,1,0:T(8,128)S(1)}, u32[]{:S(2)}, u32[]{:S(2)}) collective-permute-start(f32[2,128,128]{2,1,0:T(8,128)S(1)} %get-tuple-element.256), channel_id=1, source_target_pairs={{0,8},{4,12},{1,9},{5,13},{2,10},{6,14},{3,11},{7,15}} | collective-permute-start | bytes 393224 | tf_op jit(solution)/shard_map/ppermute | solution.py:173
  29.3 0.8 collective-permute-start.11
  30.3 0.8 collective-permute-start.10
  32.2 1.9 %collective-permute-start.18 = (f32[2,128,128]{2,1,0:T(8,128)S(1)}, f32[2,128,128]{2,1,0:T(8,128)S(1)}, u32[]{:S(2)}, u32[]{:S(2)}) collective-permute-start(f32[2,128,128]{2,1,0:T(8,128)S(1)} %get-tuple-element.231), channel_id=1, source_target_pairs={{0,4},{4,0},{8,12},{12,8},{16,20},{20,16},{24,28},{28,24},{1,5},{5... | collective-permute-start | bytes 393224 | tf_op jit(solution)/shard_map/ppermute | solution.py:228
  35.2 1.9 %collective-permute-start.16 = (f32[2,128,128]{2,1,0:T(8,128)S(1)}, f32[2,128,128]{2,1,0:T(8,128)S(1)}, u32[]{:S(2)}, u32[]{:S(2)}) collective-permute-start(f32[2,128,128]{2,1,0:T(8,128)S(1)} %get-tuple-element.225), channel_id=1, source_target_pairs={{0,4},{4,0},{8,12},{12,8},{16,20},{20,16},{24,28},{28,24},{1,5},{5... | collective-permute-start | bytes 393224 | tf_op jit(solution)/shard_map/ppermute | solution.py:228
  37.9 1.4 %collective-permute-done.18.other = f32[2,128,128]{2,1,0:T(8,128)S(1)} collective-permute-done((f32[2,128,128]{2,1,0:T(8,128)S(1)}, f32[2,128,128]{2,1,0:T(8,128)S(1)}, u32[]{:S(2)}, u32[]{:S(2)}) %collective-permute-start.18) | collective-permute-done | bytes 131104 | tf_op jit(solution)/shard_map/ppermute | solution.py:228
  39.6 1.1 %collective-permute-done.17.other = f32[2,128,128]{2,1,0:T(8,128)S(1)} collective-permute-done((f32[2,128,128]{2,1,0:T(8,128)S(1)}, f32[2,128,128]{2,1,0:T(8,128)S(1)}, u32[]{:S(2)}, u32[]{:S(2)}) %collective-permute-start.17) | collective-permute-done | bytes 131104 | tf_op jit(solution)/shard_map/ppermute | solution.py:228
  41.0 1.1 %collective-permute-done.16.other = f32[2,128,128]{2,1,0:T(8,128)S(1)} collective-permute-done((f32[2,128,128]{2,1,0:T(8,128)S(1)}, f32[2,128,128]{2,1,0:T(8,128)S(1)}, u32[]{:S(2)}, u32[]{:S(2)}) %collective-permute-start.16) | collective-permute-done | bytes 131104 | tf_op jit(solution)/shard_map/ppermute | solution.py:228
  42.6 1.5 %collective-permute-start.21 = (f32[2,256]{1,0:T(2,128)S(1)}, f32[2,256]{1,0:T(2,128)S(1)}, u32[]{:S(2)}, u32[]{:S(2)}) collective-permute-start(f32[2,256]{1,0:T(2,128)S(1)} %get-tuple-element.141.refs_0_), channel_id=1, source_target_pairs={{0,2},{1,3},{2,0},{3,1},{4,6},{5,7},{6,4},{7,5},{8,10},{9,11},{10,... | collective-permute-start | bytes 6152 | tf_op jit(solution)/shard_map/ppermute | solution.py:307
  44.5 1.8 %collective-permute-done.21.refs_2_ = f32[2,256]{1,0:T(2,128)S(1)} collective-permute-done((f32[2,256]{1,0:T(2,128)S(1)}, f32[2,256]{1,0:T(2,128)S(1)}, u32[]{:S(2)}, u32[]{:S(2)}) %collective-permute-start.21) | collective-permute-done | bytes 2080 | tf_op jit(solution)/shard_map/ppermute | solution.py:307
  46.3 0.9 collective-permute-done.22.refs_3_
  47.8 1.2 %collective-permute-start.23 = (f32[2,128,128]{2,1,0:T(8,128)S(1)}, f32[2,128,128]{2,1,0:T(8,128)S(1)}, u32[]{:S(2)}, u32[]{:S(2)}) collective-permute-start(f32[2,128,128]{2,1,0:T(8,128)S(1)} %get-tuple-element.170), channel_id=1, source_target_pairs={{0,4},{4,0},{8,12},{12,8},{16,20},{20,16},{24,28},{28,24},{1,5},{5... | collective-permute-start | bytes 393224 | tf_op jit(solution)/shard_map/ppermute | solution.py:208
  49.7 2.9 %shard_map.84.refs_4_ = bf16[256,2048]{1,0:T(8,128)(2,1)} custom-call(s32[1]{0:T(128)} %bitcast.place, bf16[256,2048]{1,0:T(8,128)(2,1)S(1)} %copy-done.1, bf16[256,2048]{1,0:T(8,128)(2,1)S(1)} %copy-done.2, bf16[256,256]{1,0:T(8,128)(2,1)S(1)} %get-tuple-element.158.refs_0_.d, bf16[256,256]{1,0:T(8,128)(2,1)S(1)} %get-tuple-element.159.refs_1_.d, ...), custom_call_target="tpu_custom_call" | custom-call | flops 1024 | bytes 1024 | tf_op jit(solution)/shard_map/pallas_call | solution.py:43
  52.6 0.9 collective-permute-start.25
  53.4 1.2 %collective-permute-start.27 = (f32[2,128,128]{2,1,0:T(8,128)S(1)}, f32[2,128,128]{2,1,0:T(8,128)S(1)}, u32[]{:S(2)}, u32[]{:S(2)}) collective-permute-start(f32[2,128,128]{2,1,0:T(8,128)S(1)} %get-tuple-element.178), channel_id=1, source_target_pairs={{0,4},{4,0},{8,12},{12,8},{16,20},{20,16},{24,28},{28,24},{1,5},{5... | collective-permute-start | bytes 393224 | tf_op jit(solution)/shard_map/ppermute | solution.py:208
  55.3 3.7 %collective-permute-done.25 = f32[2,128,128]{2,1,0:T(8,128)S(1)} collective-permute-done((f32[2,128,128]{2,1,0:T(8,128)S(1)}, f32[2,128,128]{2,1,0:T(8,128)S(1)}, u32[]{:S(2)}, u32[]{:S(2)}) %collective-permute-start.25) | collective-permute-done | bytes 131104 | tf_op jit(solution)/shard_map/ppermute | solution.py:208
  58.9 0.9 collective-permute-start.24
  60.5 1.7 %shard_map.85.refs_4_ = bf16[256,2048]{1,0:T(8,128)(2,1)} custom-call(s32[1]{0:T(128)} %bitcast.place, bf16[256,2048]{1,0:T(8,128)(2,1)S(1)} %copy-done.1, bf16[256,2048]{1,0:T(8,128)(2,1)S(1)} %copy-done.2, bf16[256,256]{1,0:T(8,128)(2,1)S(1)} %get-tuple-element.154.refs_0_.d, ...), custom_call_target="tpu_custom_call", output_to_operand_aliasing={{}: (7, {})} | custom-call | flops 1024 | bytes 1024 | tf_op jit(solution)/shard_map/pallas_call | solution.py:43
  65.1 1.7 %shard_map.86 = bf16[256,2048]{1,0:T(8,128)(2,1)} custom-call(s32[1]{0:T(128)} %bitcast.place, bf16[256,2048]{1,0:T(8,128)(2,1)S(1)} %copy-done.1, bf16[256,2048]{1,0:T(8,128)(2,1)S(1)} %copy-done.2, bf16[256,256]{1,0:T(8,128)(2,1)S(1)} %get-tuple-element.146.refs_0_.d, ...), custom_call_target="tpu_custom_call", output_to_operand_aliasing={{}: (7, {})} | custom-call | flops 1024 | bytes 1024 | tf_op jit(solution)/shard_map/pallas_call | solution.py:43
  66.8 1.3 %collective-permute-start.36 = (f32[2,128,128]{2,1,0:T(8,128)S(1)}, f32[2,128,128]{2,1,0:T(8,128)S(1)}, u32[]{:S(2)}, u32[]{:S(2)}) collective-permute-start(f32[2,128,128]{2,1,0:T(8,128)S(1)} %get-tuple-element.223), channel_id=1, source_target_pairs={{12,4},{8,0},{13,5},{9,1},{14,6},{10,2},{15,7},{11,3}} | collective-permute-start | bytes 393224 | tf_op jit(solution)/shard_map/ppermute | solution.py:173
  68.9 1.3 %collective-permute-start.34 = (f32[2,128,128]{2,1,0:T(8,128)S(1)}, f32[2,128,128]{2,1,0:T(8,128)S(1)}, u32[]{:S(2)}, u32[]{:S(2)}) collective-permute-start(f32[2,128,128]{2,1,0:T(8,128)S(1)} %get-tuple-element.221), channel_id=1, source_target_pairs={{12,4},{8,0},{13,5},{9,1},{14,6},{10,2},{15,7},{11,3}} | collective-permute-start | bytes 393224 | tf_op jit(solution)/shard_map/ppermute | solution.py:173
  70.9 10.0 %collective-permute-done.36 = f32[2,128,128]{2,1,0:T(8,128)S(1)} collective-permute-done((f32[2,128,128]{2,1,0:T(8,128)S(1)}, f32[2,128,128]{2,1,0:T(8,128)S(1)}, u32[]{:S(2)}, u32[]{:S(2)}) %collective-permute-start.36) | collective-permute-done | bytes 131104 | tf_op jit(solution)/shard_map/ppermute | solution.py:173
  80.9 1.5 %collective-permute-start.42 = (f32[2,128,128]{2,1,0:T(8,128)S(1)}, f32[2,128,128]{2,1,0:T(8,128)S(1)}, u32[]{:S(2)}, u32[]{:S(2)}) collective-permute-start(f32[2,128,128]{2,1,0:T(8,128)S(1)} %get-tuple-element.219), channel_id=1, source_target_pairs={{0,4},{4,0},{8,12},{12,8},{16,20},{20,16},{24,28},{28,24},{1,5},{5... | collective-permute-start | bytes 393224 | tf_op jit(solution)/shard_map/ppermute | solution.py:228
  82.4 1.3 %collective-permute-start.38 = (f32[2,128,128]{2,1,0:T(8,128)S(1)}, f32[2,128,128]{2,1,0:T(8,128)S(1)}, u32[]{:S(2)}, u32[]{:S(2)}) collective-permute-start(f32[2,128,128]{2,1,0:T(8,128)S(1)} %get-tuple-element.217), channel_id=1, source_target_pairs={{12,4},{8,0},{13,5},{9,1},{14,6},{10,2},{15,7},{11,3}} | collective-permute-start | bytes 393224 | tf_op jit(solution)/shard_map/ppermute | solution.py:173
  83.7 1.0 collective-permute-done.34
  84.7 1.3 %collective-permute-start.41 = (f32[2,128,128]{2,1,0:T(8,128)S(1)}, f32[2,128,128]{2,1,0:T(8,128)S(1)}, u32[]{:S(2)}, u32[]{:S(2)}) collective-permute-start(f32[2,128,128]{2,1,0:T(8,128)S(1)} %get-tuple-element.215), channel_id=1, source_target_pairs={{0,4},{4,0},{8,12},{12,8},{16,20},{20,16},{24,28},{28,24},{1,5},{5... | collective-permute-start | bytes 393224 | tf_op jit(solution)/shard_map/ppermute | solution.py:228
  86.0 1.5 %collective-permute-start.37 = (f32[2,128,128]{2,1,0:T(8,128)S(1)}, f32[2,128,128]{2,1,0:T(8,128)S(1)}, u32[]{:S(2)}, u32[]{:S(2)}) collective-permute-start(f32[2,128,128]{2,1,0:T(8,128)S(1)} %get-tuple-element.213), channel_id=1, source_target_pairs={{12,4},{8,0},{13,5},{9,1},{14,6},{10,2},{15,7},{11,3}} | collective-permute-start | bytes 393224 | tf_op jit(solution)/shard_map/ppermute | solution.py:173
  87.5 1.3 %shard_map.87 = (bf16[256,2048]{1,0:T(8,128)(2,1)}, bf16[256,2048]{1,0:T(8,128)(2,1)}) custom-call(s32[1]{0:T(128)} %bitcast.place, bf16[256,2048]{1,0:T(8,128)(2,1)S(1)} %copy-done, bf16[256,2048]{1,0:T(8,128)(2,1)S(1)} %copy-done.1, bf16[256,2048]{1,0:T(8,128)(2,1)S(1)} %copy-done.2, bf16[256,256]{1,0:T(8,128)(2,1)S(1)} %get-tuple-element.158.refs_0_.d, ...), custom_call_target="tpu_custom_call" | custom-call | flops 1024 | bytes 1024 | tf_op jit(solution)/shard_map/pallas_call | solution.py:43
  89.3 1.0 %collective-permute-start.40 = (f32[2,128,128]{2,1,0:T(8,128)S(1)}, f32[2,128,128]{2,1,0:T(8,128)S(1)}, u32[]{:S(2)}, u32[]{:S(2)}) collective-permute-start(f32[2,128,128]{2,1,0:T(8,128)S(1)} %get-tuple-element.211), channel_id=1, source_target_pairs={{0,4},{4,0},{8,12},{12,8},{16,20},{20,16},{24,28},{28,24},{1,5},{5... | collective-permute-start | bytes 393224 | tf_op jit(solution)/shard_map/ppermute | solution.py:228
  90.3 1.3 %shard_map.88 = (bf16[256,2048]{1,0:T(8,128)(2,1)}, bf16[256,2048]{1,0:T(8,128)(2,1)}) custom-call(s32[1]{0:T(128)} %bitcast.place, bf16[256,2048]{1,0:T(8,128)(2,1)S(1)} %copy-done, bf16[256,2048]{1,0:T(8,128)(2,1)S(1)} %copy-done.1, bf16[256,2048]{1,0:T(8,128)(2,1)S(1)} %copy-done.2, ...), custom_call_target="tpu_custom_call", output_to_operand_aliasing={{0}: (7, {}), {1}: (8, {})} | custom-call | flops 1024 | bytes 1024 | tf_op jit(solution)/shard_map/pallas_call | solution.py:43
  91.5 1.4 %collective-permute-done.37 = f32[2,128,128]{2,1,0:T(8,128)S(1)} collective-permute-done((f32[2,128,128]{2,1,0:T(8,128)S(1)}, f32[2,128,128]{2,1,0:T(8,128)S(1)}, u32[]{:S(2)}, u32[]{:S(2)}) %collective-permute-start.37) | collective-permute-done | bytes 131104 | tf_op jit(solution)/shard_map/ppermute | solution.py:173
  92.9 0.9 collective-permute-start.39
  93.8 1.3 %shard_map.89 = (bf16[256,2048]{1,0:T(8,128)(2,1)}, bf16[256,2048]{1,0:T(8,128)(2,1)}) custom-call(s32[1]{0:T(128)} %bitcast.place, bf16[256,2048]{1,0:T(8,128)(2,1)S(1)} %copy-done, bf16[256,2048]{1,0:T(8,128)(2,1)S(1)} %copy-done.1, bf16[256,2048]{1,0:T(8,128)(2,1)S(1)} %copy-done.2, ...), custom_call_target="tpu_custom_call", output_to_operand_aliasing={{0}: (7, {}), {1}: (8, {})} | custom-call | flops 1024 | bytes 1024 | tf_op jit(solution)/shard_map/pallas_call | solution.py:43
  95.1 1.3 %shard_map.90 = (bf16[256,2048]{1,0:T(8,128)(2,1)}, bf16[256,2048]{1,0:T(8,128)(2,1)}) custom-call(s32[1]{0:T(128)} %bitcast.place, bf16[256,2048]{1,0:T(8,128)(2,1)S(1)} %copy-done, bf16[256,2048]{1,0:T(8,128)(2,1)S(1)} %copy-done.1, bf16[256,2048]{1,0:T(8,128)(2,1)S(1)} %copy-done.2, ...), custom_call_target="tpu_custom_call", output_to_operand_aliasing={{0}: (7, {}), {1}: (8, {})} | custom-call | flops 1024 | bytes 1024 | tf_op jit(solution)/shard_map/pallas_call | solution.py:43
  96.3 1.3 %shard_map.91 = (bf16[256,2048]{1,0:T(8,128)(2,1)}, bf16[256,2048]{1,0:T(8,128)(2,1)}) custom-call(s32[1]{0:T(128)} %bitcast.place, bf16[256,2048]{1,0:T(8,128)(2,1)S(1)} %copy-done, bf16[256,2048]{1,0:T(8,128)(2,1)S(1)} %copy-done.1, bf16[256,2048]{1,0:T(8,128)(2,1)S(1)} %copy-done.2, ...), custom_call_target="tpu_custom_call", output_to_operand_aliasing={{0}: (6, {}), {1}: (7, {})} | custom-call | flops 1024 | bytes 1024 | tf_op jit(solution)/shard_map/pallas_call | solution.py:43
  97.6 1.3 %shard_map.92 = (bf16[256,2048]{1,0:T(8,128)(2,1)}, bf16[256,2048]{1,0:T(8,128)(2,1)}) custom-call(s32[1]{0:T(128)} %bitcast.place, bf16[256,2048]{1,0:T(8,128)(2,1)S(1)} %copy-done, bf16[256,2048]{1,0:T(8,128)(2,1)S(1)} %copy-done.1, bf16[256,2048]{1,0:T(8,128)(2,1)S(1)} %copy-done.2, ...), custom_call_target="tpu_custom_call", output_to_operand_aliasing={{0}: (6, {}), {1}: (7, {})} | custom-call | flops 1024 | bytes 1024 | tf_op jit(solution)/shard_map/pallas_call | solution.py:43
  98.8 1.3 %shard_map.93 = (bf16[256,2048]{1,0:T(8,128)(2,1)}, bf16[256,2048]{1,0:T(8,128)(2,1)}) custom-call(s32[1]{0:T(128)} %bitcast.place, bf16[256,2048]{1,0:T(8,128)(2,1)S(1)} %copy-done, bf16[256,2048]{1,0:T(8,128)(2,1)S(1)} %copy-done.1, bf16[256,2048]{1,0:T(8,128)(2,1)S(1)} %copy-done.2, ...), custom_call_target="tpu_custom_call", output_to_operand_aliasing={{0}: (6, {}), {1}: (7, {})} | custom-call | flops 1024 | bytes 1024 | tf_op jit(solution)/shard_map/pallas_call | solution.py:43
  100.1 1.3 %shard_map.94 = (bf16[256,2048]{1,0:T(8,128)(2,1)}, bf16[256,2048]{1,0:T(8,128)(2,1)}) custom-call(s32[1]{0:T(128)} %bitcast.place, bf16[256,2048]{1,0:T(8,128)(2,1)S(1)} %copy-done, bf16[256,2048]{1,0:T(8,128)(2,1)S(1)} %copy-done.1, bf16[256,2048]{1,0:T(8,128)(2,1)S(1)} %copy-done.2, ...), custom_call_target="tpu_custom_call", output_to_operand_aliasing={{0}: (6, {}), {1}: (7, {})} | custom-call | flops 1024 | bytes 1024 | tf_op jit(solution)/shard_map/pallas_call | solution.py:43
  (100 shorter events, 14.3 us)
Async XLA Ops:
  2.2 10.1 %collective-permute-start = (f32[2,128,128]{2,1,0:T(8,128)S(1)}, f32[2,128,128]{2,1,0:T(8,128)S(1)}, u32[]{:S(2)}, u32[]{:S(2)}) collective-permute-start(f32[2,128,128]{2,1,0:T(8,128)S(1)} %get-tuple-element.111), channel_id=1, source_target_pairs={{0,4},{4,0},{8,12},{12,8},{16,20},{20,16},{24,28},{28,24},{1,5},{5... | collective-permute-start | bytes 393224 | tf_op jit(solution)/shard_map/ppermute | solution.py:208
  5.2 11.2 %collective-permute-start.2 = (f32[2,128,128]{2,1,0:T(8,128)S(1)}, f32[2,128,128]{2,1,0:T(8,128)S(1)}, u32[]{:S(2)}, u32[]{:S(2)}) collective-permute-start(f32[2,128,128]{2,1,0:T(8,128)S(1)} %get-tuple-element.115), channel_id=1, source_target_pairs={{0,4},{4,0},{8,12},{12,8},{16,20},{20,16},{24,28},{28,24},{1,5},{5... | collective-permute-start | bytes 393224 | tf_op jit(solution)/shard_map/ppermute | solution.py:208
  10.3 9.8 %collective-permute-start.4 = (f32[2,128,128]{2,1,0:T(8,128)S(1)}, f32[2,128,128]{2,1,0:T(8,128)S(1)}, u32[]{:S(2)}, u32[]{:S(2)}) collective-permute-start(f32[2,128,128]{2,1,0:T(8,128)S(1)} %get-tuple-element.119), channel_id=1, source_target_pairs={{0,4},{4,0},{8,12},{12,8},{16,20},{20,16},{24,28},{28,24},{1,5},{5... | collective-permute-start | bytes 393224 | tf_op jit(solution)/shard_map/ppermute | solution.py:208
  12.3 7.0 %collective-permute-start.5 = (f32[2,128,128]{2,1,0:T(8,128)S(1)}, f32[2,128,128]{2,1,0:T(8,128)S(1)}, u32[]{:S(2)}, u32[]{:S(2)}) collective-permute-start(f32[2,128,128]{2,1,0:T(8,128)S(1)} %get-tuple-element.250), channel_id=1, source_target_pairs={{0,8},{4,12},{1,9},{5,13},{2,10},{6,14},{3,11},{7,15}} | collective-permute-start | bytes 393224 | tf_op jit(solution)/shard_map/ppermute | solution.py:173
  15.8 10.0 %collective-permute-start.1 = (f32[2,128,128]{2,1,0:T(8,128)S(1)}, f32[2,128,128]{2,1,0:T(8,128)S(1)}, u32[]{:S(2)}, u32[]{:S(2)}) collective-permute-start(f32[2,128,128]{2,1,0:T(8,128)S(1)} %get-tuple-element.113), channel_id=1, source_target_pairs={{0,4},{4,0},{8,12},{12,8},{16,20},{20,16},{24,28},{28,24},{1,5},{5... | collective-permute-start | bytes 393224 | tf_op jit(solution)/shard_map/ppermute | solution.py:208
  16.4 8.7 %collective-permute-start.3 = (f32[2,128,128]{2,1,0:T(8,128)S(1)}, f32[2,128,128]{2,1,0:T(8,128)S(1)}, u32[]{:S(2)}, u32[]{:S(2)}) collective-permute-start(f32[2,128,128]{2,1,0:T(8,128)S(1)} %get-tuple-element.252), channel_id=1, source_target_pairs={{0,8},{4,12},{1,9},{5,13},{2,10},{6,14},{3,11},{7,15}} | collective-permute-start | bytes 393224 | tf_op jit(solution)/shard_map/ppermute | solution.py:173
  19.4 8.4 %collective-permute-start.9 = (f32[2,128,128]{2,1,0:T(8,128)S(1)}, f32[2,128,128]{2,1,0:T(8,128)S(1)}, u32[]{:S(2)}, u32[]{:S(2)}) collective-permute-start(f32[2,128,128]{2,1,0:T(8,128)S(1)} %add.151), channel_id=1, source_target_pairs={{8,16},{12,20},{9,17},{13,21},{10,18},{14,22},{11,19},{15,23}} | collective-permute-start | bytes 393224 | tf_op jit(solution)/shard_map/ppermute | solution.py:173
  20.1 8.4 %collective-permute-start.8 = (f32[2,128,128]{2,1,0:T(8,128)S(1)}, f32[2,128,128]{2,1,0:T(8,128)S(1)}, u32[]{:S(2)}, u32[]{:S(2)}) collective-permute-start(f32[2,128,128]{2,1,0:T(8,128)S(1)} %get-tuple-element.254), channel_id=1, source_target_pairs={{0,8},{4,12},{1,9},{5,13},{2,10},{6,14},{3,11},{7,15}} | collective-permute-start | bytes 393224 | tf_op jit(solution)/shard_map/ppermute | solution.py:173
  25.1 4.1 %collective-permute-start.7 = (f32[2,128,128]{2,1,0:T(8,128)S(1)}, f32[2,128,128]{2,1,0:T(8,128)S(1)}, u32[]{:S(2)}, u32[]{:S(2)}) collective-permute-start(f32[2,128,128]{2,1,0:T(8,128)S(1)} %add.153), channel_id=1, source_target_pairs={{8,16},{12,20},{9,17},{13,21},{10,18},{14,22},{11,19},{15,23}} | collective-permute-start | bytes 393224 | tf_op jit(solution)/shard_map/ppermute | solution.py:173
  25.9 4.4 %collective-permute-start.6 = (f32[2,128,128]{2,1,0:T(8,128)S(1)}, f32[2,128,128]{2,1,0:T(8,128)S(1)}, u32[]{:S(2)}, u32[]{:S(2)}) collective-permute-start(f32[2,128,128]{2,1,0:T(8,128)S(1)} %get-tuple-element.256), channel_id=1, source_target_pairs={{0,8},{4,12},{1,9},{5,13},{2,10},{6,14},{3,11},{7,15}} | collective-permute-start | bytes 393224 | tf_op jit(solution)/shard_map/ppermute | solution.py:173
  27.8 3.3 %collective-permute-start.13 = (f32[2,128,128]{2,1,0:T(8,128)S(1)}, f32[2,128,128]{2,1,0:T(8,128)S(1)}, u32[]{:S(2)}, u32[]{:S(2)}) collective-permute-start(f32[2,128,128]{2,1,0:T(8,128)S(1)} %get-tuple-element.239), channel_id=1, source_target_pairs={{16,24},{20,28},{17,25},{21,29},{18,26},{22,30},{19,27},{23,31}} | collective-permute-start | bytes 393224 | tf_op jit(solution)/shard_map/ppermute | solution.py:173
  28.6 2.9 %collective-permute-start.12 = (f32[2,128,128]{2,1,0:T(8,128)S(1)}, f32[2,128,128]{2,1,0:T(8,128)S(1)}, u32[]{:S(2)}, u32[]{:S(2)}) collective-permute-start(f32[2,128,128]{2,1,0:T(8,128)S(1)} %add.157), channel_id=1, source_target_pairs={{8,16},{12,20},{9,17},{13,21},{10,18},{14,22},{11,19},{15,23}} | collective-permute-start | bytes 393224 | tf_op jit(solution)/shard_map/ppermute | solution.py:173
  29.3 7.7 %copy-start.4 = (bf16[2048]{0:T(1024)(128)(2,1)S(1)}, bf16[2048]{0:T(1024)(128)(2,1)}, u32[]{:S(2)}) copy-start(bf16[2048]{0:T(1024)(128)(2,1)} %param.9) | copy-start | bytes 12292
  29.3 8.3 %copy-start = (bf16[256,2048]{1,0:T(8,128)(2,1)S(1)}, bf16[256,2048]{1,0:T(8,128)(2,1)}, u32[]{:S(2)}) copy-start(bf16[256,2048]{1,0:T(8,128)(2,1)} %q.17) | copy-start | bytes 3145732
  29.3 8.3 %copy-start.1 = (bf16[256,2048]{1,0:T(8,128)(2,1)S(1)}, bf16[256,2048]{1,0:T(8,128)(2,1)}, u32[]{:S(2)}) copy-start(bf16[256,2048]{1,0:T(8,128)(2,1)} %k.23) | copy-start | bytes 3145732
  29.3 8.3 %copy-start.2 = (bf16[256,2048]{1,0:T(8,128)(2,1)S(1)}, bf16[256,2048]{1,0:T(8,128)(2,1)}, u32[]{:S(2)}) copy-start(bf16[256,2048]{1,0:T(8,128)(2,1)} %v.23) | copy-start | bytes 3145732
  29.3 8.3 %copy-start.3 = (bf16[256,2048]{1,0:T(8,128)(2,1)S(1)}, bf16[256,2048]{1,0:T(8,128)(2,1)}, u32[]{:S(2)}) copy-start(bf16[256,2048]{1,0:T(8,128)(2,1)} %refs_9_.3) | copy-start | bytes 3145732
  29.3 2.8 %collective-permute-start.11 = (f32[2,128,128]{2,1,0:T(8,128)S(1)}, f32[2,128,128]{2,1,0:T(8,128)S(1)}, u32[]{:S(2)}, u32[]{:S(2)}) collective-permute-start(f32[2,128,128]{2,1,0:T(8,128)S(1)} %get-tuple-element.237), channel_id=1, source_target_pairs={{16,24},{20,28},{17,25},{21,29},{18,26},{22,30},{19,27},{23,31}} | collective-permute-start | bytes 393224 | tf_op jit(solution)/shard_map/ppermute | solution.py:173
  30.3 3.8 %collective-permute-start.10 = (f32[2,128,128]{2,1,0:T(8,128)S(1)}, f32[2,128,128]{2,1,0:T(8,128)S(1)}, u32[]{:S(2)}, u32[]{:S(2)}) collective-permute-start(f32[2,128,128]{2,1,0:T(8,128)S(1)} %add.160), channel_id=1, source_target_pairs={{8,16},{12,20},{9,17},{13,21},{10,18},{14,22},{11,19},{15,23}} | collective-permute-start | bytes 393224 | tf_op jit(solution)/shard_map/ppermute | solution.py:173
  31.2 6.4 %collective-permute-start.19 = (f32[2,128,128]{2,1,0:T(8,128)S(1)}, f32[2,128,128]{2,1,0:T(8,128)S(1)}, u32[]{:S(2)}, u32[]{:S(2)}) collective-permute-start(f32[2,128,128]{2,1,0:T(8,128)S(1)} %get-tuple-element.235), channel_id=1, source_target_pairs={{0,4},{4,0},{8,12},{12,8},{16,20},{20,16},{24,28},{28,24},{1,5},{5... | collective-permute-start | bytes 393224 | tf_op jit(solution)/shard_map/ppermute | solution.py:228
  31.5 3.3 %collective-permute-start.15 = (f32[2,128,128]{2,1,0:T(8,128)S(1)}, f32[2,128,128]{2,1,0:T(8,128)S(1)}, u32[]{:S(2)}, u32[]{:S(2)}) collective-permute-start(f32[2,128,128]{2,1,0:T(8,128)S(1)} %get-tuple-element.233), channel_id=1, source_target_pairs={{16,24},{20,28},{17,25},{21,29},{18,26},{22,30},{19,27},{23,31}} | collective-permute-start | bytes 393224 | tf_op jit(solution)/shard_map/ppermute | solution.py:173
  32.2 7.1 %collective-permute-start.18 = (f32[2,128,128]{2,1,0:T(8,128)S(1)}, f32[2,128,128]{2,1,0:T(8,128)S(1)}, u32[]{:S(2)}, u32[]{:S(2)}) collective-permute-start(f32[2,128,128]{2,1,0:T(8,128)S(1)} %get-tuple-element.231), channel_id=1, source_target_pairs={{0,4},{4,0},{8,12},{12,8},{16,20},{20,16},{24,28},{28,24},{1,5},{5... | collective-permute-start | bytes 393224 | tf_op jit(solution)/shard_map/ppermute | solution.py:228
  34.1 1.0 %collective-permute-start.14 = (f32[2,128,128]{2,1,0:T(8,128)S(1)}, f32[2,128,128]{2,1,0:T(8,128)S(1)}, u32[]{:S(2)}, u32[]{:S(2)}) collective-permute-start(f32[2,128,128]{2,1,0:T(8,128)S(1)} %get-tuple-element.229), channel_id=1, source_target_pairs={{16,24},{20,28},{17,25},{21,29},{18,26},{22,30},{19,27},{23,31}} | collective-permute-start | bytes 393224 | tf_op jit(solution)/shard_map/ppermute | solution.py:173
  34.8 5.9 %collective-permute-start.17 = (f32[2,128,128]{2,1,0:T(8,128)S(1)}, f32[2,128,128]{2,1,0:T(8,128)S(1)}, u32[]{:S(2)}, u32[]{:S(2)}) collective-permute-start(f32[2,128,128]{2,1,0:T(8,128)S(1)} %get-tuple-element.227), channel_id=1, source_target_pairs={{0,4},{4,0},{8,12},{12,8},{16,20},{20,16},{24,28},{28,24},{1,5},{5... | collective-permute-start | bytes 393224 | tf_op jit(solution)/shard_map/ppermute | solution.py:228
  35.2 6.9 %collective-permute-start.16 = (f32[2,128,128]{2,1,0:T(8,128)S(1)}, f32[2,128,128]{2,1,0:T(8,128)S(1)}, u32[]{:S(2)}, u32[]{:S(2)}) collective-permute-start(f32[2,128,128]{2,1,0:T(8,128)S(1)} %get-tuple-element.225), channel_id=1, source_target_pairs={{0,4},{4,0},{8,12},{12,8},{16,20},{20,16},{24,28},{28,24},{1,5},{5... | collective-permute-start | bytes 393224 | tf_op jit(solution)/shard_map/ppermute | solution.py:228
  42.5 1.9 %collective-permute-start.20 = (f32[2,256]{1,0:T(2,128)S(1)}, f32[2,256]{1,0:T(2,128)S(1)}, u32[]{:S(2)}, u32[]{:S(2)}) collective-permute-start(f32[2,256]{1,0:T(2,128)S(1)} %get-tuple-element.141.refs_0_), channel_id=1, source_target_pairs={{0,1},{1,0},{2,3},{3,2},{4,5},{5,4},{6,7},{7,6},{8,9},{9,8},{10,11... | collective-permute-start | bytes 6152 | tf_op jit(solution)/shard_map/ppermute | solution.py:307
  42.6 3.7 %collective-permute-start.21 = (f32[2,256]{1,0:T(2,128)S(1)}, f32[2,256]{1,0:T(2,128)S(1)}, u32[]{:S(2)}, u32[]{:S(2)}) collective-permute-start(f32[2,256]{1,0:T(2,128)S(1)} %get-tuple-element.141.refs_0_), channel_id=1, source_target_pairs={{0,2},{1,3},{2,0},{3,1},{4,6},{5,7},{6,4},{7,5},{8,10},{9,11},{10,... | collective-permute-start | bytes 6152 | tf_op jit(solution)/shard_map/ppermute | solution.py:307
  44.2 3.0 %collective-permute-start.22 = (f32[2,256]{1,0:T(2,128)S(1)}, f32[2,256]{1,0:T(2,128)S(1)}, u32[]{:S(2)}, u32[]{:S(2)}) collective-permute-start(f32[2,256]{1,0:T(2,128)S(1)} %get-tuple-element.141.refs_0_), channel_id=1, source_target_pairs={{0,3},{1,2},{2,1},{3,0},{4,7},{5,6},{6,5},{7,4},{8,11},{9,10},{10,... | collective-permute-start | bytes 6152 | tf_op jit(solution)/shard_map/ppermute | solution.py:307
  47.8 6.7 %collective-permute-start.23 = (f32[2,128,128]{2,1,0:T(8,128)S(1)}, f32[2,128,128]{2,1,0:T(8,128)S(1)}, u32[]{:S(2)}, u32[]{:S(2)}) collective-permute-start(f32[2,128,128]{2,1,0:T(8,128)S(1)} %get-tuple-element.170), channel_id=1, source_target_pairs={{0,4},{4,0},{8,12},{12,8},{16,20},{20,16},{24,28},{28,24},{1,5},{5... | collective-permute-start | bytes 393224 | tf_op jit(solution)/shard_map/ppermute | solution.py:208
  52.6 6.4 %collective-permute-start.25 = (f32[2,128,128]{2,1,0:T(8,128)S(1)}, f32[2,128,128]{2,1,0:T(8,128)S(1)}, u32[]{:S(2)}, u32[]{:S(2)}) collective-permute-start(f32[2,128,128]{2,1,0:T(8,128)S(1)} %get-tuple-element.174), channel_id=1, source_target_pairs={{0,4},{4,0},{8,12},{12,8},{16,20},{20,16},{24,28},{28,24},{1,5},{5... | collective-permute-start | bytes 393224 | tf_op jit(solution)/shard_map/ppermute | solution.py:208
  53.4 9.5 %collective-permute-start.27 = (f32[2,128,128]{2,1,0:T(8,128)S(1)}, f32[2,128,128]{2,1,0:T(8,128)S(1)}, u32[]{:S(2)}, u32[]{:S(2)}) collective-permute-start(f32[2,128,128]{2,1,0:T(8,128)S(1)} %get-tuple-element.178), channel_id=1, source_target_pairs={{0,4},{4,0},{8,12},{12,8},{16,20},{20,16},{24,28},{28,24},{1,5},{5... | collective-permute-start | bytes 393224 | tf_op jit(solution)/shard_map/ppermute | solution.py:208
  54.6 7.6 %collective-permute-start.28 = (f32[2,128,128]{2,1,0:T(8,128)S(1)}, f32[2,128,128]{2,1,0:T(8,128)S(1)}, u32[]{:S(2)}, u32[]{:S(2)}) collective-permute-start(f32[2,128,128]{2,1,0:T(8,128)S(1)} %get-tuple-element.248), channel_id=1, source_target_pairs={{28,20},{24,16},{29,21},{25,17},{30,22},{26,18},{31,23},{27,19}} | collective-permute-start | bytes 393224 | tf_op jit(solution)/shard_map/ppermute | solution.py:173
  58.9 5.4 %collective-permute-start.24 = (f32[2,128,128]{2,1,0:T(8,128)S(1)}, f32[2,128,128]{2,1,0:T(8,128)S(1)}, u32[]{:S(2)}, u32[]{:S(2)}) collective-permute-start(f32[2,128,128]{2,1,0:T(8,128)S(1)} %get-tuple-element.172), channel_id=1, source_target_pairs={{0,4},{4,0},{8,12},{12,8},{16,20},{20,16},{24,28},{28,24},{1,5},{5... | collective-permute-start | bytes 393224 | tf_op jit(solution)/shard_map/ppermute | solution.py:208
  59.8 3.8 %collective-permute-start.26 = (f32[2,128,128]{2,1,0:T(8,128)S(1)}, f32[2,128,128]{2,1,0:T(8,128)S(1)}, u32[]{:S(2)}, u32[]{:S(2)}) collective-permute-start(f32[2,128,128]{2,1,0:T(8,128)S(1)} %get-tuple-element.246), channel_id=1, source_target_pairs={{28,20},{24,16},{29,21},{25,17},{30,22},{26,18},{31,23},{27,19}} | collective-permute-start | bytes 393224 | tf_op jit(solution)/shard_map/ppermute | solution.py:173
  62.2 4.5 %collective-permute-start.32 = (f32[2,128,128]{2,1,0:T(8,128)S(1)}, f32[2,128,128]{2,1,0:T(8,128)S(1)}, u32[]{:S(2)}, u32[]{:S(2)}) collective-permute-start(f32[2,128,128]{2,1,0:T(8,128)S(1)} %add.175), channel_id=1, source_target_pairs={{20,12},{16,8},{21,13},{17,9},{22,14},{18,10},{23,15},{19,11}} | collective-permute-start | bytes 393224 | tf_op jit(solution)/shard_map/ppermute | solution.py:173
  63.0 5.1 %collective-permute-start.31 = (f32[2,128,128]{2,1,0:T(8,128)S(1)}, f32[2,128,128]{2,1,0:T(8,128)S(1)}, u32[]{:S(2)}, u32[]{:S(2)}) collective-permute-start(f32[2,128,128]{2,1,0:T(8,128)S(1)} %get-tuple-element.242), channel_id=1, source_target_pairs={{28,20},{24,16},{29,21},{25,17},{30,22},{26,18},{31,23},{27,19}} | collective-permute-start | bytes 393224 | tf_op jit(solution)/shard_map/ppermute | solution.py:173
  63.7 5.1 %collective-permute-start.30 = (f32[2,128,128]{2,1,0:T(8,128)S(1)}, f32[2,128,128]{2,1,0:T(8,128)S(1)}, u32[]{:S(2)}, u32[]{:S(2)}) collective-permute-start(f32[2,128,128]{2,1,0:T(8,128)S(1)} %add.177), channel_id=1, source_target_pairs={{20,12},{16,8},{21,13},{17,9},{22,14},{18,10},{23,15},{19,11}} | collective-permute-start | bytes 393224 | tf_op jit(solution)/shard_map/ppermute | solution.py:173
  64.4 5.8 %collective-permute-start.29 = (f32[2,128,128]{2,1,0:T(8,128)S(1)}, f32[2,128,128]{2,1,0:T(8,128)S(1)}, u32[]{:S(2)}, u32[]{:S(2)}) collective-permute-start(f32[2,128,128]{2,1,0:T(8,128)S(1)} %get-tuple-element.244), channel_id=1, source_target_pairs={{28,20},{24,16},{29,21},{25,17},{30,22},{26,18},{31,23},{27,19}} | collective-permute-start | bytes 393224 | tf_op jit(solution)/shard_map/ppermute | solution.py:173
  66.8 14.0 %collective-permute-start.36 = (f32[2,128,128]{2,1,0:T(8,128)S(1)}, f32[2,128,128]{2,1,0:T(8,128)S(1)}, u32[]{:S(2)}, u32[]{:S(2)}) collective-permute-start(f32[2,128,128]{2,1,0:T(8,128)S(1)} %get-tuple-element.223), channel_id=1, source_target_pairs={{12,4},{8,0},{13,5},{9,1},{14,6},{10,2},{15,7},{11,3}} | collective-permute-start | bytes 393224 | tf_op jit(solution)/shard_map/ppermute | solution.py:173
  68.1 14.2 %collective-permute-start.35 = (f32[2,128,128]{2,1,0:T(8,128)S(1)}, f32[2,128,128]{2,1,0:T(8,128)S(1)}, u32[]{:S(2)}, u32[]{:S(2)}) collective-permute-start(f32[2,128,128]{2,1,0:T(8,128)S(1)} %add.181), channel_id=1, source_target_pairs={{20,12},{16,8},{21,13},{17,9},{22,14},{18,10},{23,15},{19,11}} | collective-permute-start | bytes 393224 | tf_op jit(solution)/shard_map/ppermute | solution.py:173
  68.9 15.8 %collective-permute-start.34 = (f32[2,128,128]{2,1,0:T(8,128)S(1)}, f32[2,128,128]{2,1,0:T(8,128)S(1)}, u32[]{:S(2)}, u32[]{:S(2)}) collective-permute-start(f32[2,128,128]{2,1,0:T(8,128)S(1)} %get-tuple-element.221), channel_id=1, source_target_pairs={{12,4},{8,0},{13,5},{9,1},{14,6},{10,2},{15,7},{11,3}} | collective-permute-start | bytes 393224 | tf_op jit(solution)/shard_map/ppermute | solution.py:173
  70.2 15.8 %collective-permute-start.33 = (f32[2,128,128]{2,1,0:T(8,128)S(1)}, f32[2,128,128]{2,1,0:T(8,128)S(1)}, u32[]{:S(2)}, u32[]{:S(2)}) collective-permute-start(f32[2,128,128]{2,1,0:T(8,128)S(1)} %add.184), channel_id=1, source_target_pairs={{20,12},{16,8},{21,13},{17,9},{22,14},{18,10},{23,15},{19,11}} | collective-permute-start | bytes 393224 | tf_op jit(solution)/shard_map/ppermute | solution.py:173
  80.9 15.5 %collective-permute-start.42 = (f32[2,128,128]{2,1,0:T(8,128)S(1)}, f32[2,128,128]{2,1,0:T(8,128)S(1)}, u32[]{:S(2)}, u32[]{:S(2)}) collective-permute-start(f32[2,128,128]{2,1,0:T(8,128)S(1)} %get-tuple-element.219), channel_id=1, source_target_pairs={{0,4},{4,0},{8,12},{12,8},{16,20},{20,16},{24,28},{28,24},{1,5},{5... | collective-permute-start | bytes 393224 | tf_op jit(solution)/shard_map/ppermute | solution.py:228
  82.4 6.9 %collective-permute-start.38 = (f32[2,128,128]{2,1,0:T(8,128)S(1)}, f32[2,128,128]{2,1,0:T(8,128)S(1)}, u32[]{:S(2)}, u32[]{:S(2)}) collective-permute-start(f32[2,128,128]{2,1,0:T(8,128)S(1)} %get-tuple-element.217), channel_id=1, source_target_pairs={{12,4},{8,0},{13,5},{9,1},{14,6},{10,2},{15,7},{11,3}} | collective-permute-start | bytes 393224 | tf_op jit(solution)/shard_map/ppermute | solution.py:173
  84.7 12.9 %collective-permute-start.41 = (f32[2,128,128]{2,1,0:T(8,128)S(1)}, f32[2,128,128]{2,1,0:T(8,128)S(1)}, u32[]{:S(2)}, u32[]{:S(2)}) collective-permute-start(f32[2,128,128]{2,1,0:T(8,128)S(1)} %get-tuple-element.215), channel_id=1, source_target_pairs={{0,4},{4,0},{8,12},{12,8},{16,20},{20,16},{24,28},{28,24},{1,5},{5... | collective-permute-start | bytes 393224 | tf_op jit(solution)/shard_map/ppermute | solution.py:228
  86.0 6.9 %collective-permute-start.37 = (f32[2,128,128]{2,1,0:T(8,128)S(1)}, f32[2,128,128]{2,1,0:T(8,128)S(1)}, u32[]{:S(2)}, u32[]{:S(2)}) collective-permute-start(f32[2,128,128]{2,1,0:T(8,128)S(1)} %get-tuple-element.213), channel_id=1, source_target_pairs={{12,4},{8,0},{13,5},{9,1},{14,6},{10,2},{15,7},{11,3}} | collective-permute-start | bytes 393224 | tf_op jit(solution)/shard_map/ppermute | solution.py:173
  89.3 9.6 %collective-permute-start.40 = (f32[2,128,128]{2,1,0:T(8,128)S(1)}, f32[2,128,128]{2,1,0:T(8,128)S(1)}, u32[]{:S(2)}, u32[]{:S(2)}) collective-permute-start(f32[2,128,128]{2,1,0:T(8,128)S(1)} %get-tuple-element.211), channel_id=1, source_target_pairs={{0,4},{4,0},{8,12},{12,8},{16,20},{20,16},{24,28},{28,24},{1,5},{5... | collective-permute-start | bytes 393224 | tf_op jit(solution)/shard_map/ppermute | solution.py:228
  92.9 7.2 %collective-permute-start.39 = (f32[2,128,128]{2,1,0:T(8,128)S(1)}, f32[2,128,128]{2,1,0:T(8,128)S(1)}, u32[]{:S(2)}, u32[]{:S(2)}) collective-permute-start(f32[2,128,128]{2,1,0:T(8,128)S(1)} %get-tuple-element.209), channel_id=1, source_target_pairs={{0,4},{4,0},{8,12},{12,8},{16,20},{20,16},{24,28},{28,24},{1,5},{5... | collective-permute-start | bytes 393224 | tf_op jit(solution)/shard_map/ppermute | solution.py:228

commit v8 on v7

--- a/solution.py
+++ b/solution.py
@@ -71,8 +71,9 @@
                 h = turn * heads + j
                 outs[h // per][h % per] = dot(head(k, j), head(v, j), 0, 0)
     mask = causal()
-    for j in range(heads):
-        s = masked(dot(head(q, j), head(k, j), 1, 1), mask)
+    scores = [dot(head(q, j), head(k, j), 1, 1) for j in range(heads)]
+    scores = [masked(s, mask) for s in scores]
+    for j, s in enumerate(scores):
         attn[:, j * DH:(j + 1) * DH] = dot(s, head(v, j), 1, 0)
 
 
@@ -133,26 +134,36 @@
 
         @pl.when(pl.program_id(0) == turn)
         def _():
-            for j in range(per):
-                do = head(d, j)
-                ds = masked(dot(do, head(v, j), 1, 1), mask)
-                qg[:, j * DH:(j + 1) * DH] = (dot(ds, head(k, j), 1, 0) + dot(do, sb[j], 1, 1)).astype(BF16)
-
-
-def final_body(per, terms, place, q, k, v, d, *refs):
-    later_in, kg, vg = refs[:terms], refs[-2], refs[-1]
+            first = [dot(head(d, j), head(v, j), 1, 1) for j in range(per)]
+            prior = [dot(head(d, j), sb[j], 1, 1) for j in range(per)]
+            first = [masked(s, mask) for s in first]
+            for j, s in enumerate(first):
+                qg[:, j * DH:(j + 1) * DH] = (dot(s, head(k, j), 1, 0) + prior[j]).astype(BF16)
+
+
+def final_body(per, chunks, terms, place, q, k, v, *refs):
+    ds, later_in, kg, vg = refs[:chunks], refs[chunks:chunks + chunks * terms], refs[-2], refs[-1]
     mask = causal(turned=True)
-    for j in range(per):
-        at = slice(j * DH, (j + 1) * DH)
-        later = later_in[0][j]
-        for term in later_in[1:]:
-            later = later + term[j]
-        later = later.astype(BF16)
-        qj, kj, vj, do = head(q, j), head(k, j), head(v, j), head(d, j)
-        ds = masked(dot(vj, do, 1, 1), mask)
-        st = masked(dot(kj, qj, 1, 1), mask)
-        kg[:, at] = (dot(ds, qj, 1, 0) + dot(vj, later, 1, 1)).astype(BF16)
-        vg[:, at] = (dot(st, do, 1, 0) + dot(kj, later, 1, 0)).astype(BF16)
+    heads = range(chunks * per)
+
+    def later(h):
+        state = later_in[h // per * terms][h % per]
+        for n in range(1, terms):
+            state = state + later_in[h // per * terms + n][h % per]
+        return state.astype(BF16)
+
+    outer = [head(ds[h // per], h % per) for h in heads]
+    grad = [dot(head(v, h), outer[h], 1, 1) for h in heads]
+    score = [dot(head(k, h), head(q, h), 1, 1) for h in heads]
+    states = [later(h) for h in heads]
+    kg_part = [dot(head(v, h), states[h], 1, 1) for h in heads]
+    vg_part = [dot(head(k, h), states[h], 1, 0) for h in heads]
+    grad = [masked(x, mask) for x in grad]
+    score = [masked(x, mask) for x in score]
+    for h in heads:
+        at = slice(h * DH, (h + 1) * DH)
+        kg[:, at] = (dot(grad[h], head(q, h), 1, 0) + kg_part[h]).astype(BF16)
+        vg[:, at] = (dot(score[h], outer[h], 1, 0) + vg_part[h]).astype(BF16)
 
 
 def solution(mesh):
@@ -340,32 +351,35 @@
                 [((tokens, width), BF16, block, mine(c), HBM)], grid=(2 * count,), aliases=aliases)
             return made["query"][0]
 
-        def rest(c, which, after):
-            index, d = ((at_k(c), d_k[c]), (at_o(c), d_o[c]))[which]
-            states = after[c][2:] if which else after[c][:2]
-            ins = [(a, block, index) for a in (queries, keys, values)]
-            ins += [(d, block, whole2)] + [(a, state3, whole3) for a in states]
+        def rest(c, which, after, count=1):
+            steps = CHUNKS // count
+            index = lambda i, s: (0, (1 - s[0] if which else s[0]) * steps + c // count)
+            wider = (tokens, narrow * count)
+            some = range(c, c + count)
+            states = [a for i in some for a in (after[i][2:] if which else after[i][:2])]
+            ins = [(a, wider, index) for a in (queries, keys, values)]
+            ins += [((d_o if which else d_k)[i], block, whole2) for i in some]
+            ins += [(a, state3, whole3) for a in states]
             aliases = {}
             if made["rest"]:
                 aliases = {len(ins) + 1: 0, len(ins) + 2: 1}
                 ins += [(a, None, None, HBM) for a in made["rest"]]
             made["rest"] = call(
-                functools.partial(final_body, per, len(states)), place, ins,
-                [((tokens, width), BF16, block, index, HBM)] * 2,
-                aliases=aliases)
+                functools.partial(final_body, per, count, len(states) // count), place, ins,
+                [((tokens, width), BF16, wider, index, HBM)] * 2, aliases=aliases)
             return made["rest"][0]
 
         beside = {
-            (1, 0): lambda out: query(2, 1),
-            (2, 0): lambda out: query(3, 1),
-            (tail, CHUNKS - 2): lambda out: rest(0, 0, out),
-            (tail, CHUNKS - 1): lambda out: rest(1, 0, out),
+            (tail, 0): lambda out: query(1, 1),
+            (tail, 1): lambda out: query(2, 1),
+            (tail, CHUNKS - 2): lambda out: query(3, 1),
+            (tail, CHUNKS - 1): lambda out: rest(0, 0, out, 2),
         } if spread else {}
-        after = scan(kept, sent, ends, True, [query(0, 2)], beside)
-        if not beside:
-            query(2, 2)
-        for c in range(2 if beside else 0, CHUNKS):
-            rest(c, 0, after)
+        after = scan(kept, sent, ends, True, [query(0, 1)], beside)
+        if not spread:
+            query(1, 3)
+            rest(0, 0, after, 2)
+        rest(2, 0, after, 2)
         for c in range(CHUNKS):
             rest(c, 1, after)
         return made["query"][0], made["rest"][0], made["rest"][1]

time: 102 us -> 99.9 us (0.979)
  Pallas kernels: 25.5 us -> 23.2 us
    pallas_call x19 -> x18, Pallas kernels: 25.5 us -> 23.2 us  [call(): pl.pallas_call(body, grid_spec=pltpu.PrefetchScalarGridSpec(num_scalar_pr...]
  transfers between devices with their start and end apart: 43 -> 43, of which waited for: 13 -> 13; matrix products, arithmetic and copies ran while one was open for 1% -> 1% of each run, Pallas kernels for 21% -> 19%
where the time goes in v8:
time: 99.9 us; the launch traced here: 99.4 us
  starting transfers between devices  49.2 us (49%)
  waiting for transfers between devices  25 us (25%)
  Pallas kernels  23.2 us (23%)
  between operations  1.23 us (1%)
    ppermute x24, starting transfers between devices, hop(): return lax.ppermute(array, 'seq', pairs)  28 us
    pallas_call x18, Pallas kernels, call(): pl.pallas_call(body, grid_spec=pltpu.PrefetchScalarGridSpec(num_scalar_pr...  23.2 us
    ppermute x24, waiting for transfers between devices, hop(): return lax.ppermute(array, 'seq', pairs)  15 us
    ppermute x8, starting transfers between devices, swap_after(): flight[c] = lax.ppermute(part_sent, 'seq', swap)  10.2 us
    ppermute x8, starting transfers between devices, scan(): out[c] = (carry[c], own[c], lax.ppermute(send, 'seq', swap))  9.07 us
    ppermute x8, waiting for transfers between devices, scan(): out[c] = (carry[c], own[c], lax.ppermute(send, 'seq', swap))  4.16 us
    ppermute x8, waiting for transfers between devices, swap_after(): flight[c] = lax.ppermute(part_sent, 'seq', swap)  3.14 us
    ppermute x3, waiting for transfers between devices, shards(): lax.ppermute(mine, 'head', [(i, i ^ step if paired else (i + step) % part...  2.7 us
  transfers between devices with their start and end apart: 43, of which 13 were waited for; matrix products, arithmetic and copies ran while one was open for 1% of the time, Pallas kernels for 19%

profile of v8, /device:TPU:0, one launch (start us, length us, event | category | flops | bytes accessed | tf_op | source)
XLA Modules:
  0.0 99.4 jit_solution(13523780283320047206)
XLA Ops:
  0.6 1.6 %shard_map.77 = (f32[2,128,128]{2,1,0:T(8,128)S(1)}, f32[2,128,128]{2,1,0:T(8,128)S(1)}, f32[2,128,128]{2,1,0:T(8,128)S(1)}, f32[2,128,128]{2,1,0:T(8,128)S(1)}) custom-call(s32[1]{0:T(128)} %bitcast.place, bf16[256,2048]{1,0:T(8,128)(2,1)} %k.21, bf16[256,2048]{1,0:T(8,128)(2,1)} %v.21), custom_call_target="tpu_custom_call" | custom-call | flops 1024 | bytes 1024 | tf_op jit(solution)/shard_map/pallas_call | solution.py:43
  2.2 3.0 %collective-permute-start = (f32[2,128,128]{2,1,0:T(8,128)S(1)}, f32[2,128,128]{2,1,0:T(8,128)S(1)}, u32[]{:S(2)}, u32[]{:S(2)}) collective-permute-start(f32[2,128,128]{2,1,0:T(8,128)S(1)} %get-tuple-element.107), channel_id=1, source_target_pairs={{0,4},{4,0},{8,12},{12,8},{16,20},{20,16},{24,28},{28,24},{1,5},{5... | collective-permute-start | bytes 393224 | tf_op jit(solution)/shard_map/ppermute | solution.py:219
  5.3 4.3 %shard_map.76 = (f32[2,128,128]{2,1,0:T(8,128)S(1)}, f32[2,128,128]{2,1,0:T(8,128)S(1)}, f32[2,128,128]{2,1,0:T(8,128)S(1)}, f32[2,128,128]{2,1,0:T(8,128)S(1)}, f32[256,2048]{1,0:T(8,128)S(1)}) custom-call(s32[1]{0:T(128)} %bitcast.place, bf16[256,2048]{1,0:T(8,128)(2,1)} %q.13, bf16[256,2048]{1,0:T(8,128)(2,1)} %k.21, bf16[256,2048]{1,0:T(8,128)(2,1)} %v.21), custom_call_target="tpu_custom_call" | custom-call | flops 1024 | bytes 1024 | tf_op jit(solution)/shard_map/pallas_call | solution.py:43
  9.7 2.0 %collective-permute-start.4 = (f32[2,128,128]{2,1,0:T(8,128)S(1)}, f32[2,128,128]{2,1,0:T(8,128)S(1)}, u32[]{:S(2)}, u32[]{:S(2)}) collective-permute-start(f32[2,128,128]{2,1,0:T(8,128)S(1)} %get-tuple-element.115), channel_id=1, source_target_pairs={{0,4},{4,0},{8,12},{12,8},{16,20},{20,16},{24,28},{28,24},{1,5},{5... | collective-permute-start | bytes 393224 | tf_op jit(solution)/shard_map/ppermute | solution.py:219
  11.7 3.5 %collective-permute-start.5 = (f32[2,128,128]{2,1,0:T(8,128)S(1)}, f32[2,128,128]{2,1,0:T(8,128)S(1)}, u32[]{:S(2)}, u32[]{:S(2)}) collective-permute-start(f32[2,128,128]{2,1,0:T(8,128)S(1)} %get-tuple-element.242), channel_id=1, source_target_pairs={{0,8},{4,12},{1,9},{5,13},{2,10},{6,14},{3,11},{7,15}} | collective-permute-start | bytes 393224 | tf_op jit(solution)/shard_map/ppermute | solution.py:184
  15.8 1.3 %collective-permute-start.3 = (f32[2,128,128]{2,1,0:T(8,128)S(1)}, f32[2,128,128]{2,1,0:T(8,128)S(1)}, u32[]{:S(2)}, u32[]{:S(2)}) collective-permute-start(f32[2,128,128]{2,1,0:T(8,128)S(1)} %get-tuple-element.244), channel_id=1, source_target_pairs={{0,8},{4,12},{1,9},{5,13},{2,10},{6,14},{3,11},{7,15}} | collective-permute-start | bytes 393224 | tf_op jit(solution)/shard_map/ppermute | solution.py:184
  17.1 1.6 %collective-permute-done.5 = f32[2,128,128]{2,1,0:T(8,128)S(1)} collective-permute-done((f32[2,128,128]{2,1,0:T(8,128)S(1)}, f32[2,128,128]{2,1,0:T(8,128)S(1)}, u32[]{:S(2)}, u32[]{:S(2)}) %collective-permute-start.5) | collective-permute-done | bytes 131104 | tf_op jit(solution)/shard_map/ppermute | solution.py:184
  19.5 5.0 %collective-permute-start.8 = (f32[2,128,128]{2,1,0:T(8,128)S(1)}, f32[2,128,128]{2,1,0:T(8,128)S(1)}, u32[]{:S(2)}, u32[]{:S(2)}) collective-permute-start(f32[2,128,128]{2,1,0:T(8,128)S(1)} %get-tuple-element.246), channel_id=1, source_target_pairs={{0,8},{4,12},{1,9},{5,13},{2,10},{6,14},{3,11},{7,15}} | collective-permute-start | bytes 393224 | tf_op jit(solution)/shard_map/ppermute | solution.py:184
  25.2 1.9 %collective-permute-start.6 = (f32[2,128,128]{2,1,0:T(8,128)S(1)}, f32[2,128,128]{2,1,0:T(8,128)S(1)}, u32[]{:S(2)}, u32[]{:S(2)}) collective-permute-start(f32[2,128,128]{2,1,0:T(8,128)S(1)} %get-tuple-element.248), channel_id=1, source_target_pairs={{0,8},{4,12},{1,9},{5,13},{2,10},{6,14},{3,11},{7,15}} | collective-permute-start | bytes 393224 | tf_op jit(solution)/shard_map/ppermute | solution.py:184
  28.7 0.8 collective-permute-start.11
  29.7 0.8 collective-permute-start.10
  30.9 0.7 collective-permute-start.15
  31.6 1.9 %collective-permute-start.18 = (f32[2,128,128]{2,1,0:T(8,128)S(1)}, f32[2,128,128]{2,1,0:T(8,128)S(1)}, u32[]{:S(2)}, u32[]{:S(2)}) collective-permute-start(f32[2,128,128]{2,1,0:T(8,128)S(1)} %get-tuple-element.223), channel_id=1, source_target_pairs={{0,4},{4,0},{8,12},{12,8},{16,20},{20,16},{24,28},{28,24},{1,5},{5... | collective-permute-start | bytes 393224 | tf_op jit(solution)/shard_map/ppermute | solution.py:239
  34.5 1.9 %collective-permute-start.16 = (f32[2,128,128]{2,1,0:T(8,128)S(1)}, f32[2,128,128]{2,1,0:T(8,128)S(1)}, u32[]{:S(2)}, u32[]{:S(2)}) collective-permute-start(f32[2,128,128]{2,1,0:T(8,128)S(1)} %get-tuple-element.217), channel_id=1, source_target_pairs={{0,4},{4,0},{8,12},{12,8},{16,20},{20,16},{24,28},{28,24},{1,5},{5... | collective-permute-start | bytes 393224 | tf_op jit(solution)/shard_map/ppermute | solution.py:239
  37.4 1.3 %collective-permute-done.18.other = f32[2,128,128]{2,1,0:T(8,128)S(1)} collective-permute-done((f32[2,128,128]{2,1,0:T(8,128)S(1)}, f32[2,128,128]{2,1,0:T(8,128)S(1)}, u32[]{:S(2)}, u32[]{:S(2)}) %collective-permute-start.18) | collective-permute-done | bytes 131104 | tf_op jit(solution)/shard_map/ppermute | solution.py:239
  39.0 1.1 %collective-permute-done.17.other = f32[2,128,128]{2,1,0:T(8,128)S(1)} collective-permute-done((f32[2,128,128]{2,1,0:T(8,128)S(1)}, f32[2,128,128]{2,1,0:T(8,128)S(1)}, u32[]{:S(2)}, u32[]{:S(2)}) %collective-permute-start.17) | collective-permute-done | bytes 131104 | tf_op jit(solution)/shard_map/ppermute | solution.py:239
  40.4 1.1 %collective-permute-done.16.other = f32[2,128,128]{2,1,0:T(8,128)S(1)} collective-permute-done((f32[2,128,128]{2,1,0:T(8,128)S(1)}, f32[2,128,128]{2,1,0:T(8,128)S(1)}, u32[]{:S(2)}, u32[]{:S(2)}) %collective-permute-start.16) | collective-permute-done | bytes 131104 | tf_op jit(solution)/shard_map/ppermute | solution.py:239
  42.0 1.5 %collective-permute-start.21 = (f32[2,256]{1,0:T(2,128)S(1)}, f32[2,256]{1,0:T(2,128)S(1)}, u32[]{:S(2)}, u32[]{:S(2)}) collective-permute-start(f32[2,256]{1,0:T(2,128)S(1)} %get-tuple-element.137.refs_0_), channel_id=1, source_target_pairs={{0,2},{1,3},{2,0},{3,1},{4,6},{5,7},{6,4},{7,5},{8,10},{9,11},{10,... | collective-permute-start | bytes 6152 | tf_op jit(solution)/shard_map/ppermute | solution.py:318
  43.9 1.8 %collective-permute-done.21.refs_2_ = f32[2,256]{1,0:T(2,128)S(1)} collective-permute-done((f32[2,256]{1,0:T(2,128)S(1)}, f32[2,256]{1,0:T(2,128)S(1)}, u32[]{:S(2)}, u32[]{:S(2)}) %collective-permute-start.21) | collective-permute-done | bytes 2080 | tf_op jit(solution)/shard_map/ppermute | solution.py:318
  45.6 0.9 collective-permute-done.22.refs_3_
  47.2 1.2 %collective-permute-start.23 = (f32[2,128,128]{2,1,0:T(8,128)S(1)}, f32[2,128,128]{2,1,0:T(8,128)S(1)}, u32[]{:S(2)}, u32[]{:S(2)}) collective-permute-start(f32[2,128,128]{2,1,0:T(8,128)S(1)} %get-tuple-element.166), channel_id=1, source_target_pairs={{0,4},{4,0},{8,12},{12,8},{16,20},{20,16},{24,28},{28,24},{1,5},{5... | collective-permute-start | bytes 393224 | tf_op jit(solution)/shard_map/ppermute | solution.py:219
  48.4 0.9 collective-permute-start.25
  49.9 1.6 %shard_map.84.refs_4_ = bf16[256,2048]{1,0:T(8,128)(2,1)} custom-call(s32[1]{0:T(128)} %bitcast.place, bf16[256,2048]{1,0:T(8,128)(2,1)S(1)} %copy-done.1, bf16[256,2048]{1,0:T(8,128)(2,1)S(1)} %copy-done.2, bf16[256,256]{1,0:T(8,128)(2,1)S(1)} %get-tuple-element.158.refs_0_, bf16[256,256]{1,0:T(8,128)(2,1)S(1)} %get-tuple-element.159.refs_1_.refs_0_, ...), custom_call_target="tpu_custom_call" | custom-call | flops 1024 | bytes 1024 | tf_op jit(solution)/shard_map/pallas_call | solution.py:43
  51.5 1.2 %collective-permute-start.27 = (f32[2,128,128]{2,1,0:T(8,128)S(1)}, f32[2,128,128]{2,1,0:T(8,128)S(1)}, u32[]{:S(2)}, u32[]{:S(2)}) collective-permute-start(f32[2,128,128]{2,1,0:T(8,128)S(1)} %get-tuple-element.174), channel_id=1, source_target_pairs={{0,4},{4,0},{8,12},{12,8},{16,20},{20,16},{24,28},{28,24},{1,5},{5... | collective-permute-start | bytes 393224 | tf_op jit(solution)/shard_map/ppermute | solution.py:219
  52.7 0.9 collective-permute-done.23
  54.3 2.1 %collective-permute-done.25 = f32[2,128,128]{2,1,0:T(8,128)S(1)} collective-permute-done((f32[2,128,128]{2,1,0:T(8,128)S(1)}, f32[2,128,128]{2,1,0:T(8,128)S(1)}, u32[]{:S(2)}, u32[]{:S(2)}) %collective-permute-start.25) | collective-permute-done | bytes 131104 | tf_op jit(solution)/shard_map/ppermute | solution.py:219
  56.4 0.7 collective-permute-start.26
  57.1 1.2 %collective-permute-start.24 = (f32[2,128,128]{2,1,0:T(8,128)S(1)}, f32[2,128,128]{2,1,0:T(8,128)S(1)}, u32[]{:S(2)}, u32[]{:S(2)}) collective-permute-start(f32[2,128,128]{2,1,0:T(8,128)S(1)} %get-tuple-element.168), channel_id=1, source_target_pairs={{0,4},{4,0},{8,12},{12,8},{16,20},{20,16},{24,28},{28,24},{1,5},{5... | collective-permute-start | bytes 393224 | tf_op jit(solution)/shard_map/ppermute | solution.py:219
  58.3 1.6 %shard_map.85.refs_4_ = bf16[256,2048]{1,0:T(8,128)(2,1)} custom-call(s32[1]{0:T(128)} %bitcast.place, bf16[256,2048]{1,0:T(8,128)(2,1)S(1)} %copy-done.1, bf16[256,2048]{1,0:T(8,128)(2,1)S(1)} %copy-done.2, bf16[256,256]{1,0:T(8,128)(2,1)S(1)} %get-tuple-element.154.refs_0_.refs_1_, ...), custom_call_target="tpu_custom_call", output_to_operand_aliasing={{}: (7, {})} | custom-call | flops 1024 | bytes 1024 | tf_op jit(solution)/shard_map/pallas_call | solution.py:43
  60.6 0.7 collective-permute-start.31
  62.9 1.3 %collective-permute-start.36 = (f32[2,128,128]{2,1,0:T(8,128)S(1)}, f32[2,128,128]{2,1,0:T(8,128)S(1)}, u32[]{:S(2)}, u32[]{:S(2)}) collective-permute-start(f32[2,128,128]{2,1,0:T(8,128)S(1)} %get-tuple-element.215), channel_id=1, source_target_pairs={{12,4},{8,0},{13,5},{9,1},{14,6},{10,2},{15,7},{11,3}} | collective-permute-start | bytes 393224 | tf_op jit(solution)/shard_map/ppermute | solution.py:184
  65.0 1.3 %collective-permute-start.34 = (f32[2,128,128]{2,1,0:T(8,128)S(1)}, f32[2,128,128]{2,1,0:T(8,128)S(1)}, u32[]{:S(2)}, u32[]{:S(2)}) collective-permute-start(f32[2,128,128]{2,1,0:T(8,128)S(1)} %get-tuple-element.213), channel_id=1, source_target_pairs={{12,4},{8,0},{13,5},{9,1},{14,6},{10,2},{15,7},{11,3}} | collective-permute-start | bytes 393224 | tf_op jit(solution)/shard_map/ppermute | solution.py:184
  67.0 12.2 %collective-permute-done.36 = f32[2,128,128]{2,1,0:T(8,128)S(1)} collective-permute-done((f32[2,128,128]{2,1,0:T(8,128)S(1)}, f32[2,128,128]{2,1,0:T(8,128)S(1)}, u32[]{:S(2)}, u32[]{:S(2)}) %collective-permute-start.36) | collective-permute-done | bytes 131104 | tf_op jit(solution)/shard_map/ppermute | solution.py:184
  79.2 1.5 %collective-permute-start.42 = (f32[2,128,128]{2,1,0:T(8,128)S(1)}, f32[2,128,128]{2,1,0:T(8,128)S(1)}, u32[]{:S(2)}, u32[]{:S(2)}) collective-permute-start(f32[2,128,128]{2,1,0:T(8,128)S(1)} %get-tuple-element.211), channel_id=1, source_target_pairs={{0,4},{4,0},{8,12},{12,8},{16,20},{20,16},{24,28},{28,24},{1,5},{5... | collective-permute-start | bytes 393224 | tf_op jit(solution)/shard_map/ppermute | solution.py:239
  80.7 1.3 %collective-permute-start.38 = (f32[2,128,128]{2,1,0:T(8,128)S(1)}, f32[2,128,128]{2,1,0:T(8,128)S(1)}, u32[]{:S(2)}, u32[]{:S(2)}) collective-permute-start(f32[2,128,128]{2,1,0:T(8,128)S(1)} %get-tuple-element.209), channel_id=1, source_target_pairs={{12,4},{8,0},{13,5},{9,1},{14,6},{10,2},{15,7},{11,3}} | collective-permute-start | bytes 393224 | tf_op jit(solution)/shard_map/ppermute | solution.py:184
  82.0 1.6 %shard_map.86.refs_4_ = bf16[256,2048]{1,0:T(8,128)(2,1)} custom-call(s32[1]{0:T(128)} %bitcast.place, bf16[256,2048]{1,0:T(8,128)(2,1)S(1)} %copy-done.1, bf16[256,2048]{1,0:T(8,128)(2,1)S(1)} %copy-done.2, bf16[256,256]{1,0:T(8,128)(2,1)S(1)} %get-tuple-element.150.refs_0_, ...), custom_call_target="tpu_custom_call", output_to_operand_aliasing={{}: (7, {})} | custom-call | flops 1024 | bytes 1024 | tf_op jit(solution)/shard_map/pallas_call | solution.py:43
  83.7 0.7 collective-permute-start.41
  84.4 1.5 %collective-permute-start.37 = (f32[2,128,128]{2,1,0:T(8,128)S(1)}, f32[2,128,128]{2,1,0:T(8,128)S(1)}, u32[]{:S(2)}, u32[]{:S(2)}) collective-permute-start(f32[2,128,128]{2,1,0:T(8,128)S(1)} %get-tuple-element.205), channel_id=1, source_target_pairs={{12,4},{8,0},{13,5},{9,1},{14,6},{10,2},{15,7},{11,3}} | collective-permute-start | bytes 393224 | tf_op jit(solution)/shard_map/ppermute | solution.py:184
  85.9 1.6 %shard_map.87 = bf16[256,2048]{1,0:T(8,128)(2,1)} custom-call(s32[1]{0:T(128)} %bitcast.place, bf16[256,2048]{1,0:T(8,128)(2,1)S(1)} %copy-done.1, bf16[256,2048]{1,0:T(8,128)(2,1)S(1)} %copy-done.2, bf16[256,256]{1,0:T(8,128)(2,1)S(1)} %get-tuple-element.142.refs_0_.refs_1_, ...), custom_call_target="tpu_custom_call", output_to_operand_aliasing={{}: (7, {})} | custom-call | flops 1024 | bytes 1024 | tf_op jit(solution)/shard_map/pallas_call | solution.py:43
  87.5 1.7 %shard_map.88 = (bf16[256,2048]{1,0:T(8,128)(2,1)}, bf16[256,2048]{1,0:T(8,128)(2,1)}) custom-call(s32[1]{0:T(128)} %bitcast.place, bf16[256,2048]{1,0:T(8,128)(2,1)S(1)} %copy-done, bf16[256,2048]{1,0:T(8,128)(2,1)S(1)} %copy-done.1, bf16[256,2048]{1,0:T(8,128)(2,1)S(1)} %copy-done.2, bf16[256,256]{1,0:T(8,128)(2,1)S(1)} %get-tuple-element.158.refs_0_, ...), custom_call_target="tpu_custom_call" | custom-call | flops 1024 | bytes 1024 | tf_op jit(solution)/shard_map/pallas_call | solution.py:43
  89.2 1.5 %collective-permute-start.40 = (f32[2,128,128]{2,1,0:T(8,128)S(1)}, f32[2,128,128]{2,1,0:T(8,128)S(1)}, u32[]{:S(2)}, u32[]{:S(2)}) collective-permute-start(f32[2,128,128]{2,1,0:T(8,128)S(1)} %get-tuple-element.203), channel_id=1, source_target_pairs={{0,4},{4,0},{8,12},{12,8},{16,20},{20,16},{24,28},{28,24},{1,5},{5... | collective-permute-start | bytes 393224 | tf_op jit(solution)/shard_map/ppermute | solution.py:239
  90.7 0.9 collective-permute-done.37
  91.6 1.1 %collective-permute-start.39 = (f32[2,128,128]{2,1,0:T(8,128)S(1)}, f32[2,128,128]{2,1,0:T(8,128)S(1)}, u32[]{:S(2)}, u32[]{:S(2)}) collective-permute-start(f32[2,128,128]{2,1,0:T(8,128)S(1)} %get-tuple-element.201), channel_id=1, source_target_pairs={{0,4},{4,0},{8,12},{12,8},{16,20},{20,16},{24,28},{28,24},{1,5},{5... | collective-permute-start | bytes 393224 | tf_op jit(solution)/shard_map/ppermute | solution.py:239
  92.8 1.7 %shard_map.89 = (bf16[256,2048]{1,0:T(8,128)(2,1)}, bf16[256,2048]{1,0:T(8,128)(2,1)}) custom-call(s32[1]{0:T(128)} %bitcast.place, bf16[256,2048]{1,0:T(8,128)(2,1)S(1)} %copy-done, bf16[256,2048]{1,0:T(8,128)(2,1)S(1)} %copy-done.1, bf16[256,2048]{1,0:T(8,128)(2,1)S(1)} %copy-done.2, ...), custom_call_target="tpu_custom_call", output_to_operand_aliasing={{0}: (10, {}), {1}: (11, {})} | custom-call | flops 1024 | bytes 1024 | tf_op jit(solution)/shard_map/pallas_call | solution.py:43
  94.4 1.2 %shard_map.90 = (bf16[256,2048]{1,0:T(8,128)(2,1)}, bf16[256,2048]{1,0:T(8,128)(2,1)}) custom-call(s32[1]{0:T(128)} %bitcast.place, bf16[256,2048]{1,0:T(8,128)(2,1)S(1)} %copy-done, bf16[256,2048]{1,0:T(8,128)(2,1)S(1)} %copy-done.1, bf16[256,2048]{1,0:T(8,128)(2,1)S(1)} %copy-done.2, ...), custom_call_target="tpu_custom_call", output_to_operand_aliasing={{0}: (6, {}), {1}: (7, {})} | custom-call | flops 1024 | bytes 1024 | tf_op jit(solution)/shard_map/pallas_call | solution.py:43
  95.7 1.2 %shard_map.91 = (bf16[256,2048]{1,0:T(8,128)(2,1)}, bf16[256,2048]{1,0:T(8,128)(2,1)}) custom-call(s32[1]{0:T(128)} %bitcast.place, bf16[256,2048]{1,0:T(8,128)(2,1)S(1)} %copy-done, bf16[256,2048]{1,0:T(8,128)(2,1)S(1)} %copy-done.1, bf16[256,2048]{1,0:T(8,128)(2,1)S(1)} %copy-done.2, ...), custom_call_target="tpu_custom_call", output_to_operand_aliasing={{0}: (6, {}), {1}: (7, {})} | custom-call | flops 1024 | bytes 1024 | tf_op jit(solution)/shard_map/pallas_call | solution.py:43
  96.9 1.2 %shard_map.92 = (bf16[256,2048]{1,0:T(8,128)(2,1)}, bf16[256,2048]{1,0:T(8,128)(2,1)}) custom-call(s32[1]{0:T(128)} %bitcast.place, bf16[256,2048]{1,0:T(8,128)(2,1)S(1)} %copy-done, bf16[256,2048]{1,0:T(8,128)(2,1)S(1)} %copy-done.1, bf16[256,2048]{1,0:T(8,128)(2,1)S(1)} %copy-done.2, ...), custom_call_target="tpu_custom_call", output_to_operand_aliasing={{0}: (6, {}), {1}: (7, {})} | custom-call | flops 1024 | bytes 1024 | tf_op jit(solution)/shard_map/pallas_call | solution.py:43
  98.2 1.2 %shard_map.93 = (bf16[256,2048]{1,0:T(8,128)(2,1)}, bf16[256,2048]{1,0:T(8,128)(2,1)}) custom-call(s32[1]{0:T(128)} %bitcast.place, bf16[256,2048]{1,0:T(8,128)(2,1)S(1)} %copy-done, bf16[256,2048]{1,0:T(8,128)(2,1)S(1)} %copy-done.1, bf16[256,2048]{1,0:T(8,128)(2,1)S(1)} %copy-done.2, ...), custom_call_target="tpu_custom_call", output_to_operand_aliasing={{0}: (6, {}), {1}: (7, {})} | custom-call | flops 1024 | bytes 1024 | tf_op jit(solution)/shard_map/pallas_call | solution.py:43
  (99 shorter events, 13.4 us)
Async XLA Ops:
  2.2 9.5 %collective-permute-start = (f32[2,128,128]{2,1,0:T(8,128)S(1)}, f32[2,128,128]{2,1,0:T(8,128)S(1)}, u32[]{:S(2)}, u32[]{:S(2)}) collective-permute-start(f32[2,128,128]{2,1,0:T(8,128)S(1)} %get-tuple-element.107), channel_id=1, source_target_pairs={{0,4},{4,0},{8,12},{12,8},{16,20},{20,16},{24,28},{28,24},{1,5},{5... | collective-permute-start | bytes 393224 | tf_op jit(solution)/shard_map/ppermute | solution.py:219
  5.2 10.5 %collective-permute-start.2 = (f32[2,128,128]{2,1,0:T(8,128)S(1)}, f32[2,128,128]{2,1,0:T(8,128)S(1)}, u32[]{:S(2)}, u32[]{:S(2)}) collective-permute-start(f32[2,128,128]{2,1,0:T(8,128)S(1)} %get-tuple-element.111), channel_id=1, source_target_pairs={{0,4},{4,0},{8,12},{12,8},{16,20},{20,16},{24,28},{28,24},{1,5},{5... | collective-permute-start | bytes 393224 | tf_op jit(solution)/shard_map/ppermute | solution.py:219
  9.7 9.8 %collective-permute-start.4 = (f32[2,128,128]{2,1,0:T(8,128)S(1)}, f32[2,128,128]{2,1,0:T(8,128)S(1)}, u32[]{:S(2)}, u32[]{:S(2)}) collective-permute-start(f32[2,128,128]{2,1,0:T(8,128)S(1)} %get-tuple-element.115), channel_id=1, source_target_pairs={{0,4},{4,0},{8,12},{12,8},{16,20},{20,16},{24,28},{28,24},{1,5},{5... | collective-permute-start | bytes 393224 | tf_op jit(solution)/shard_map/ppermute | solution.py:219
  11.7 7.0 %collective-permute-start.5 = (f32[2,128,128]{2,1,0:T(8,128)S(1)}, f32[2,128,128]{2,1,0:T(8,128)S(1)}, u32[]{:S(2)}, u32[]{:S(2)}) collective-permute-start(f32[2,128,128]{2,1,0:T(8,128)S(1)} %get-tuple-element.242), channel_id=1, source_target_pairs={{0,8},{4,12},{1,9},{5,13},{2,10},{6,14},{3,11},{7,15}} | collective-permute-start | bytes 393224 | tf_op jit(solution)/shard_map/ppermute | solution.py:184
  15.2 10.0 %collective-permute-start.1 = (f32[2,128,128]{2,1,0:T(8,128)S(1)}, f32[2,128,128]{2,1,0:T(8,128)S(1)}, u32[]{:S(2)}, u32[]{:S(2)}) collective-permute-start(f32[2,128,128]{2,1,0:T(8,128)S(1)} %get-tuple-element.109), channel_id=1, source_target_pairs={{0,4},{4,0},{8,12},{12,8},{16,20},{20,16},{24,28},{28,24},{1,5},{5... | collective-permute-start | bytes 393224 | tf_op jit(solution)/shard_map/ppermute | solution.py:219
  15.8 8.7 %collective-permute-start.3 = (f32[2,128,128]{2,1,0:T(8,128)S(1)}, f32[2,128,128]{2,1,0:T(8,128)S(1)}, u32[]{:S(2)}, u32[]{:S(2)}) collective-permute-start(f32[2,128,128]{2,1,0:T(8,128)S(1)} %get-tuple-element.244), channel_id=1, source_target_pairs={{0,8},{4,12},{1,9},{5,13},{2,10},{6,14},{3,11},{7,15}} | collective-permute-start | bytes 393224 | tf_op jit(solution)/shard_map/ppermute | solution.py:184
  18.7 8.4 %collective-permute-start.9 = (f32[2,128,128]{2,1,0:T(8,128)S(1)}, f32[2,128,128]{2,1,0:T(8,128)S(1)}, u32[]{:S(2)}, u32[]{:S(2)}) collective-permute-start(f32[2,128,128]{2,1,0:T(8,128)S(1)} %add.151), channel_id=1, source_target_pairs={{8,16},{12,20},{9,17},{13,21},{10,18},{14,22},{11,19},{15,23}} | collective-permute-start | bytes 393224 | tf_op jit(solution)/shard_map/ppermute | solution.py:184
  19.5 8.4 %collective-permute-start.8 = (f32[2,128,128]{2,1,0:T(8,128)S(1)}, f32[2,128,128]{2,1,0:T(8,128)S(1)}, u32[]{:S(2)}, u32[]{:S(2)}) collective-permute-start(f32[2,128,128]{2,1,0:T(8,128)S(1)} %get-tuple-element.246), channel_id=1, source_target_pairs={{0,8},{4,12},{1,9},{5,13},{2,10},{6,14},{3,11},{7,15}} | collective-permute-start | bytes 393224 | tf_op jit(solution)/shard_map/ppermute | solution.py:184
  24.5 4.1 %collective-permute-start.7 = (f32[2,128,128]{2,1,0:T(8,128)S(1)}, f32[2,128,128]{2,1,0:T(8,128)S(1)}, u32[]{:S(2)}, u32[]{:S(2)}) collective-permute-start(f32[2,128,128]{2,1,0:T(8,128)S(1)} %add.153), channel_id=1, source_target_pairs={{8,16},{12,20},{9,17},{13,21},{10,18},{14,22},{11,19},{15,23}} | collective-permute-start | bytes 393224 | tf_op jit(solution)/shard_map/ppermute | solution.py:184
  25.2 4.4 %collective-permute-start.6 = (f32[2,128,128]{2,1,0:T(8,128)S(1)}, f32[2,128,128]{2,1,0:T(8,128)S(1)}, u32[]{:S(2)}, u32[]{:S(2)}) collective-permute-start(f32[2,128,128]{2,1,0:T(8,128)S(1)} %get-tuple-element.248), channel_id=1, source_target_pairs={{0,8},{4,12},{1,9},{5,13},{2,10},{6,14},{3,11},{7,15}} | collective-permute-start | bytes 393224 | tf_op jit(solution)/shard_map/ppermute | solution.py:184
  27.2 3.3 %collective-permute-start.13 = (f32[2,128,128]{2,1,0:T(8,128)S(1)}, f32[2,128,128]{2,1,0:T(8,128)S(1)}, u32[]{:S(2)}, u32[]{:S(2)}) collective-permute-start(f32[2,128,128]{2,1,0:T(8,128)S(1)} %get-tuple-element.231), channel_id=1, source_target_pairs={{16,24},{20,28},{17,25},{21,29},{18,26},{22,30},{19,27},{23,31}} | collective-permute-start | bytes 393224 | tf_op jit(solution)/shard_map/ppermute | solution.py:184
  27.9 2.9 %collective-permute-start.12 = (f32[2,128,128]{2,1,0:T(8,128)S(1)}, f32[2,128,128]{2,1,0:T(8,128)S(1)}, u32[]{:S(2)}, u32[]{:S(2)}) collective-permute-start(f32[2,128,128]{2,1,0:T(8,128)S(1)} %add.157), channel_id=1, source_target_pairs={{8,16},{12,20},{9,17},{13,21},{10,18},{14,22},{11,19},{15,23}} | collective-permute-start | bytes 393224 | tf_op jit(solution)/shard_map/ppermute | solution.py:184
  28.6 7.8 %copy-start.4 = (bf16[2048]{0:T(1024)(128)(2,1)S(1)}, bf16[2048]{0:T(1024)(128)(2,1)}, u32[]{:S(2)}) copy-start(bf16[2048]{0:T(1024)(128)(2,1)} %param.9) | copy-start | bytes 12292
  28.7 8.4 %copy-start = (bf16[256,2048]{1,0:T(8,128)(2,1)S(1)}, bf16[256,2048]{1,0:T(8,128)(2,1)}, u32[]{:S(2)}) copy-start(bf16[256,2048]{1,0:T(8,128)(2,1)} %q.13) | copy-start | bytes 3145732
  28.7 8.4 %copy-start.1 = (bf16[256,2048]{1,0:T(8,128)(2,1)S(1)}, bf16[256,2048]{1,0:T(8,128)(2,1)}, u32[]{:S(2)}) copy-start(bf16[256,2048]{1,0:T(8,128)(2,1)} %k.21) | copy-start | bytes 3145732
  28.7 8.4 %copy-start.2 = (bf16[256,2048]{1,0:T(8,128)(2,1)S(1)}, bf16[256,2048]{1,0:T(8,128)(2,1)}, u32[]{:S(2)}) copy-start(bf16[256,2048]{1,0:T(8,128)(2,1)} %v.21) | copy-start | bytes 3145732
  28.7 8.4 %copy-start.3 = (bf16[256,2048]{1,0:T(8,128)(2,1)S(1)}, bf16[256,2048]{1,0:T(8,128)(2,1)}, u32[]{:S(2)}) copy-start(bf16[256,2048]{1,0:T(8,128)(2,1)} %refs_9_.3) | copy-start | bytes 3145732
  28.7 2.8 %collective-permute-start.11 = (f32[2,128,128]{2,1,0:T(8,128)S(1)}, f32[2,128,128]{2,1,0:T(8,128)S(1)}, u32[]{:S(2)}, u32[]{:S(2)}) collective-permute-start(f32[2,128,128]{2,1,0:T(8,128)S(1)} %get-tuple-element.229), channel_id=1, source_target_pairs={{16,24},{20,28},{17,25},{21,29},{18,26},{22,30},{19,27},{23,31}} | collective-permute-start | bytes 393224 | tf_op jit(solution)/shard_map/ppermute | solution.py:184
  29.7 3.8 %collective-permute-start.10 = (f32[2,128,128]{2,1,0:T(8,128)S(1)}, f32[2,128,128]{2,1,0:T(8,128)S(1)}, u32[]{:S(2)}, u32[]{:S(2)}) collective-permute-start(f32[2,128,128]{2,1,0:T(8,128)S(1)} %add.160), channel_id=1, source_target_pairs={{8,16},{12,20},{9,17},{13,21},{10,18},{14,22},{11,19},{15,23}} | collective-permute-start | bytes 393224 | tf_op jit(solution)/shard_map/ppermute | solution.py:184
  30.5 6.5 %collective-permute-start.19 = (f32[2,128,128]{2,1,0:T(8,128)S(1)}, f32[2,128,128]{2,1,0:T(8,128)S(1)}, u32[]{:S(2)}, u32[]{:S(2)}) collective-permute-start(f32[2,128,128]{2,1,0:T(8,128)S(1)} %get-tuple-element.227), channel_id=1, source_target_pairs={{0,4},{4,0},{8,12},{12,8},{16,20},{20,16},{24,28},{28,24},{1,5},{5... | collective-permute-start | bytes 393224 | tf_op jit(solution)/shard_map/ppermute | solution.py:239
  30.9 3.3 %collective-permute-start.15 = (f32[2,128,128]{2,1,0:T(8,128)S(1)}, f32[2,128,128]{2,1,0:T(8,128)S(1)}, u32[]{:S(2)}, u32[]{:S(2)}) collective-permute-start(f32[2,128,128]{2,1,0:T(8,128)S(1)} %get-tuple-element.225), channel_id=1, source_target_pairs={{16,24},{20,28},{17,25},{21,29},{18,26},{22,30},{19,27},{23,31}} | collective-permute-start | bytes 393224 | tf_op jit(solution)/shard_map/ppermute | solution.py:184
  31.6 7.1 %collective-permute-start.18 = (f32[2,128,128]{2,1,0:T(8,128)S(1)}, f32[2,128,128]{2,1,0:T(8,128)S(1)}, u32[]{:S(2)}, u32[]{:S(2)}) collective-permute-start(f32[2,128,128]{2,1,0:T(8,128)S(1)} %get-tuple-element.223), channel_id=1, source_target_pairs={{0,4},{4,0},{8,12},{12,8},{16,20},{20,16},{24,28},{28,24},{1,5},{5... | collective-permute-start | bytes 393224 | tf_op jit(solution)/shard_map/ppermute | solution.py:239
  33.5 1.0 %collective-permute-start.14 = (f32[2,128,128]{2,1,0:T(8,128)S(1)}, f32[2,128,128]{2,1,0:T(8,128)S(1)}, u32[]{:S(2)}, u32[]{:S(2)}) collective-permute-start(f32[2,128,128]{2,1,0:T(8,128)S(1)} %get-tuple-element.221), channel_id=1, source_target_pairs={{16,24},{20,28},{17,25},{21,29},{18,26},{22,30},{19,27},{23,31}} | collective-permute-start | bytes 393224 | tf_op jit(solution)/shard_map/ppermute | solution.py:184
  34.2 5.9 %collective-permute-start.17 = (f32[2,128,128]{2,1,0:T(8,128)S(1)}, f32[2,128,128]{2,1,0:T(8,128)S(1)}, u32[]{:S(2)}, u32[]{:S(2)}) collective-permute-start(f32[2,128,128]{2,1,0:T(8,128)S(1)} %get-tuple-element.219), channel_id=1, source_target_pairs={{0,4},{4,0},{8,12},{12,8},{16,20},{20,16},{24,28},{28,24},{1,5},{5... | collective-permute-start | bytes 393224 | tf_op jit(solution)/shard_map/ppermute | solution.py:239
  34.5 7.0 %collective-permute-start.16 = (f32[2,128,128]{2,1,0:T(8,128)S(1)}, f32[2,128,128]{2,1,0:T(8,128)S(1)}, u32[]{:S(2)}, u32[]{:S(2)}) collective-permute-start(f32[2,128,128]{2,1,0:T(8,128)S(1)} %get-tuple-element.217), channel_id=1, source_target_pairs={{0,4},{4,0},{8,12},{12,8},{16,20},{20,16},{24,28},{28,24},{1,5},{5... | collective-permute-start | bytes 393224 | tf_op jit(solution)/shard_map/ppermute | solution.py:239
  41.9 1.9 %collective-permute-start.20 = (f32[2,256]{1,0:T(2,128)S(1)}, f32[2,256]{1,0:T(2,128)S(1)}, u32[]{:S(2)}, u32[]{:S(2)}) collective-permute-start(f32[2,256]{1,0:T(2,128)S(1)} %get-tuple-element.137.refs_0_), channel_id=1, source_target_pairs={{0,1},{1,0},{2,3},{3,2},{4,5},{5,4},{6,7},{7,6},{8,9},{9,8},{10,11... | collective-permute-start | bytes 6152 | tf_op jit(solution)/shard_map/ppermute | solution.py:318
  42.0 3.7 %collective-permute-start.21 = (f32[2,256]{1,0:T(2,128)S(1)}, f32[2,256]{1,0:T(2,128)S(1)}, u32[]{:S(2)}, u32[]{:S(2)}) collective-permute-start(f32[2,256]{1,0:T(2,128)S(1)} %get-tuple-element.137.refs_0_), channel_id=1, source_target_pairs={{0,2},{1,3},{2,0},{3,1},{4,6},{5,7},{6,4},{7,5},{8,10},{9,11},{10,... | collective-permute-start | bytes 6152 | tf_op jit(solution)/shard_map/ppermute | solution.py:318
  43.5 3.0 %collective-permute-start.22 = (f32[2,256]{1,0:T(2,128)S(1)}, f32[2,256]{1,0:T(2,128)S(1)}, u32[]{:S(2)}, u32[]{:S(2)}) collective-permute-start(f32[2,256]{1,0:T(2,128)S(1)} %get-tuple-element.137.refs_0_), channel_id=1, source_target_pairs={{0,3},{1,2},{2,1},{3,0},{4,7},{5,6},{6,5},{7,4},{8,11},{9,10},{10,... | collective-permute-start | bytes 6152 | tf_op jit(solution)/shard_map/ppermute | solution.py:318
  47.2 6.4 %collective-permute-start.23 = (f32[2,128,128]{2,1,0:T(8,128)S(1)}, f32[2,128,128]{2,1,0:T(8,128)S(1)}, u32[]{:S(2)}, u32[]{:S(2)}) collective-permute-start(f32[2,128,128]{2,1,0:T(8,128)S(1)} %get-tuple-element.166), channel_id=1, source_target_pairs={{0,4},{4,0},{8,12},{12,8},{16,20},{20,16},{24,28},{28,24},{1,5},{5... | collective-permute-start | bytes 393224 | tf_op jit(solution)/shard_map/ppermute | solution.py:219
  48.4 8.0 %collective-permute-start.25 = (f32[2,128,128]{2,1,0:T(8,128)S(1)}, f32[2,128,128]{2,1,0:T(8,128)S(1)}, u32[]{:S(2)}, u32[]{:S(2)}) collective-permute-start(f32[2,128,128]{2,1,0:T(8,128)S(1)} %get-tuple-element.170), channel_id=1, source_target_pairs={{0,4},{4,0},{8,12},{12,8},{16,20},{20,16},{24,28},{28,24},{1,5},{5... | collective-permute-start | bytes 393224 | tf_op jit(solution)/shard_map/ppermute | solution.py:219
  51.5 9.1 %collective-permute-start.27 = (f32[2,128,128]{2,1,0:T(8,128)S(1)}, f32[2,128,128]{2,1,0:T(8,128)S(1)}, u32[]{:S(2)}, u32[]{:S(2)}) collective-permute-start(f32[2,128,128]{2,1,0:T(8,128)S(1)} %get-tuple-element.174), channel_id=1, source_target_pairs={{0,4},{4,0},{8,12},{12,8},{16,20},{20,16},{24,28},{28,24},{1,5},{5... | collective-permute-start | bytes 393224 | tf_op jit(solution)/shard_map/ppermute | solution.py:219
  53.6 6.3 %collective-permute-start.28 = (f32[2,128,128]{2,1,0:T(8,128)S(1)}, f32[2,128,128]{2,1,0:T(8,128)S(1)}, u32[]{:S(2)}, u32[]{:S(2)}) collective-permute-start(f32[2,128,128]{2,1,0:T(8,128)S(1)} %get-tuple-element.240), channel_id=1, source_target_pairs={{28,20},{24,16},{29,21},{25,17},{30,22},{26,18},{31,23},{27,19}} | collective-permute-start | bytes 393224 | tf_op jit(solution)/shard_map/ppermute | solution.py:184
  56.4 4.9 %collective-permute-start.26 = (f32[2,128,128]{2,1,0:T(8,128)S(1)}, f32[2,128,128]{2,1,0:T(8,128)S(1)}, u32[]{:S(2)}, u32[]{:S(2)}) collective-permute-start(f32[2,128,128]{2,1,0:T(8,128)S(1)} %get-tuple-element.238), channel_id=1, source_target_pairs={{28,20},{24,16},{29,21},{25,17},{30,22},{26,18},{31,23},{27,19}} | collective-permute-start | bytes 393224 | tf_op jit(solution)/shard_map/ppermute | solution.py:184
  57.1 5.0 %collective-permute-start.24 = (f32[2,128,128]{2,1,0:T(8,128)S(1)}, f32[2,128,128]{2,1,0:T(8,128)S(1)}, u32[]{:S(2)}, u32[]{:S(2)}) collective-permute-start(f32[2,128,128]{2,1,0:T(8,128)S(1)} %get-tuple-element.168), channel_id=1, source_target_pairs={{0,4},{4,0},{8,12},{12,8},{16,20},{20,16},{24,28},{28,24},{1,5},{5... | collective-permute-start | bytes 393224 | tf_op jit(solution)/shard_map/ppermute | solution.py:219
  59.9 2.9 %collective-permute-start.32 = (f32[2,128,128]{2,1,0:T(8,128)S(1)}, f32[2,128,128]{2,1,0:T(8,128)S(1)}, u32[]{:S(2)}, u32[]{:S(2)}) collective-permute-start(f32[2,128,128]{2,1,0:T(8,128)S(1)} %add.175), channel_id=1, source_target_pairs={{20,12},{16,8},{21,13},{17,9},{22,14},{18,10},{23,15},{19,11}} | collective-permute-start | bytes 393224 | tf_op jit(solution)/shard_map/ppermute | solution.py:184
  60.6 3.6 %collective-permute-start.31 = (f32[2,128,128]{2,1,0:T(8,128)S(1)}, f32[2,128,128]{2,1,0:T(8,128)S(1)}, u32[]{:S(2)}, u32[]{:S(2)}) collective-permute-start(f32[2,128,128]{2,1,0:T(8,128)S(1)} %get-tuple-element.236), channel_id=1, source_target_pairs={{28,20},{24,16},{29,21},{25,17},{30,22},{26,18},{31,23},{27,19}} | collective-permute-start | bytes 393224 | tf_op jit(solution)/shard_map/ppermute | solution.py:184
  61.4 3.6 %collective-permute-start.30 = (f32[2,128,128]{2,1,0:T(8,128)S(1)}, f32[2,128,128]{2,1,0:T(8,128)S(1)}, u32[]{:S(2)}, u32[]{:S(2)}) collective-permute-start(f32[2,128,128]{2,1,0:T(8,128)S(1)} %add.177), channel_id=1, source_target_pairs={{20,12},{16,8},{21,13},{17,9},{22,14},{18,10},{23,15},{19,11}} | collective-permute-start | bytes 393224 | tf_op jit(solution)/shard_map/ppermute | solution.py:184
  62.2 4.1 %collective-permute-start.29 = (f32[2,128,128]{2,1,0:T(8,128)S(1)}, f32[2,128,128]{2,1,0:T(8,128)S(1)}, u32[]{:S(2)}, u32[]{:S(2)}) collective-permute-start(f32[2,128,128]{2,1,0:T(8,128)S(1)} %get-tuple-element.234), channel_id=1, source_target_pairs={{28,20},{24,16},{29,21},{25,17},{30,22},{26,18},{31,23},{27,19}} | collective-permute-start | bytes 393224 | tf_op jit(solution)/shard_map/ppermute | solution.py:184
  62.9 16.3 %collective-permute-start.36 = (f32[2,128,128]{2,1,0:T(8,128)S(1)}, f32[2,128,128]{2,1,0:T(8,128)S(1)}, u32[]{:S(2)}, u32[]{:S(2)}) collective-permute-start(f32[2,128,128]{2,1,0:T(8,128)S(1)} %get-tuple-element.215), channel_id=1, source_target_pairs={{12,4},{8,0},{13,5},{9,1},{14,6},{10,2},{15,7},{11,3}} | collective-permute-start | bytes 393224 | tf_op jit(solution)/shard_map/ppermute | solution.py:184
  64.2 16.5 %collective-permute-start.35 = (f32[2,128,128]{2,1,0:T(8,128)S(1)}, f32[2,128,128]{2,1,0:T(8,128)S(1)}, u32[]{:S(2)}, u32[]{:S(2)}) collective-permute-start(f32[2,128,128]{2,1,0:T(8,128)S(1)} %add.181), channel_id=1, source_target_pairs={{20,12},{16,8},{21,13},{17,9},{22,14},{18,10},{23,15},{19,11}} | collective-permute-start | bytes 393224 | tf_op jit(solution)/shard_map/ppermute | solution.py:184
  65.0 18.7 %collective-permute-start.34 = (f32[2,128,128]{2,1,0:T(8,128)S(1)}, f32[2,128,128]{2,1,0:T(8,128)S(1)}, u32[]{:S(2)}, u32[]{:S(2)}) collective-permute-start(f32[2,128,128]{2,1,0:T(8,128)S(1)} %get-tuple-element.213), channel_id=1, source_target_pairs={{12,4},{8,0},{13,5},{9,1},{14,6},{10,2},{15,7},{11,3}} | collective-permute-start | bytes 393224 | tf_op jit(solution)/shard_map/ppermute | solution.py:184
  66.3 18.1 %collective-permute-start.33 = (f32[2,128,128]{2,1,0:T(8,128)S(1)}, f32[2,128,128]{2,1,0:T(8,128)S(1)}, u32[]{:S(2)}, u32[]{:S(2)}) collective-permute-start(f32[2,128,128]{2,1,0:T(8,128)S(1)} %add.184), channel_id=1, source_target_pairs={{20,12},{16,8},{21,13},{17,9},{22,14},{18,10},{23,15},{19,11}} | collective-permute-start | bytes 393224 | tf_op jit(solution)/shard_map/ppermute | solution.py:184
  79.2 15.2 %collective-permute-start.42 = (f32[2,128,128]{2,1,0:T(8,128)S(1)}, f32[2,128,128]{2,1,0:T(8,128)S(1)}, u32[]{:S(2)}, u32[]{:S(2)}) collective-permute-start(f32[2,128,128]{2,1,0:T(8,128)S(1)} %get-tuple-element.211), channel_id=1, source_target_pairs={{0,4},{4,0},{8,12},{12,8},{16,20},{20,16},{24,28},{28,24},{1,5},{5... | collective-permute-start | bytes 393224 | tf_op jit(solution)/shard_map/ppermute | solution.py:239
  80.7 8.4 %collective-permute-start.38 = (f32[2,128,128]{2,1,0:T(8,128)S(1)}, f32[2,128,128]{2,1,0:T(8,128)S(1)}, u32[]{:S(2)}, u32[]{:S(2)}) collective-permute-start(f32[2,128,128]{2,1,0:T(8,128)S(1)} %get-tuple-element.209), channel_id=1, source_target_pairs={{12,4},{8,0},{13,5},{9,1},{14,6},{10,2},{15,7},{11,3}} | collective-permute-start | bytes 393224 | tf_op jit(solution)/shard_map/ppermute | solution.py:184
  83.7 12.0 %collective-permute-start.41 = (f32[2,128,128]{2,1,0:T(8,128)S(1)}, f32[2,128,128]{2,1,0:T(8,128)S(1)}, u32[]{:S(2)}, u32[]{:S(2)}) collective-permute-start(f32[2,128,128]{2,1,0:T(8,128)S(1)} %get-tuple-element.207), channel_id=1, source_target_pairs={{0,4},{4,0},{8,12},{12,8},{16,20},{20,16},{24,28},{28,24},{1,5},{5... | collective-permute-start | bytes 393224 | tf_op jit(solution)/shard_map/ppermute | solution.py:239
  84.4 7.2 %collective-permute-start.37 = (f32[2,128,128]{2,1,0:T(8,128)S(1)}, f32[2,128,128]{2,1,0:T(8,128)S(1)}, u32[]{:S(2)}, u32[]{:S(2)}) collective-permute-start(f32[2,128,128]{2,1,0:T(8,128)S(1)} %get-tuple-element.205), channel_id=1, source_target_pairs={{12,4},{8,0},{13,5},{9,1},{14,6},{10,2},{15,7},{11,3}} | collective-permute-start | bytes 393224 | tf_op jit(solution)/shard_map/ppermute | solution.py:184
  89.2 7.7 %collective-permute-start.40 = (f32[2,128,128]{2,1,0:T(8,128)S(1)}, f32[2,128,128]{2,1,0:T(8,128)S(1)}, u32[]{:S(2)}, u32[]{:S(2)}) collective-permute-start(f32[2,128,128]{2,1,0:T(8,128)S(1)} %get-tuple-element.203), channel_id=1, source_target_pairs={{0,4},{4,0},{8,12},{12,8},{16,20},{20,16},{24,28},{28,24},{1,5},{5... | collective-permute-start | bytes 393224 | tf_op jit(solution)/shard_map/ppermute | solution.py:239
  91.6 6.5 %collective-permute-start.39 = (f32[2,128,128]{2,1,0:T(8,128)S(1)}, f32[2,128,128]{2,1,0:T(8,128)S(1)}, u32[]{:S(2)}, u32[]{:S(2)}) collective-permute-start(f32[2,128,128]{2,1,0:T(8,128)S(1)} %get-tuple-element.201), channel_id=1, source_target_pairs={{0,4},{4,0},{8,12},{12,8},{16,20},{20,16},{24,28},{28,24},{1,5},{5... | collective-permute-start | bytes 393224 | tf_op jit(solution)/shard_map/ppermute | solution.py:239

commit v9 on v8

--- a/solution.py
+++ b/solution.py
@@ -209,7 +209,7 @@
             ]
             return list(zip(sums, own, others))
         chunks = len(kept)
-        order = sorted((2 * stage + c, -stage, c, stage) for stage in range(long) for c in range(chunks))
+        order = sorted((2 * stage + c, stage, c) for stage in range(long) for c in range(chunks))
         part, flight, carry, out = {}, {}, {}, {}
         last = ready
 
@@ -220,8 +220,8 @@
 
         swap_after(0)
         swap_after(1)
-        swap_after(2, *ready)
-        for _, _, c, stage in order:
+        swap_after(2)
+        for _, stage, c in order:
             if (stage, c) in beside:
                 last = last + [beside[stage, c](out)]
             got, *_ = lax.optimization_barrier((flight[c], *last))
@@ -252,8 +252,6 @@
         place, leads, ends = lax.optimization_barrier((y.astype(jnp.int32).reshape(1), y == 0, y == 1))
         gain = norm_gain.reshape(1, width)
 
-        kept_half = lambda i, s: (0, s[0])
-        sent_half = lambda i, s: (0, 1 - s[0])
         whole2 = lambda i, s: (0, 0)
         whole3 = lambda i, s: (0, 0, 0)
 
@@ -263,11 +261,14 @@
         def at_o(c):
             return lambda i, s: (0, (1 - s[0]) * CHUNKS + c)
 
-        sent = call(
-            functools.partial(states_body, per), place,
-            [(a, (tokens, wide), sent_half, HBM) for a in (keys, values)],
-            [((per, DH, DH), F32, (per, DH, DH), whole3, VMEM)] * CHUNKS,
-        )
+        some = CHUNKS // 2
+        sent = []
+        for n in range(2):
+            sent += call(
+                functools.partial(states_body, per), place,
+                [(a, (tokens, wide // 2), lambda i, s: (0, 2 * (1 - s[0]) + n), HBM) for a in (keys, values)],
+                [((per, DH, DH), F32, (per, DH, DH), whole3, VMEM)] * some,
+            )
 
         group = half // 2
         strip = lambda i, s: (0, (2 * s[0] + i) % 4)
@@ -318,18 +319,22 @@
             sums.append(lax.ppermute(
                 mine, "head", [(i, i ^ step if paired else (i + step) % parts) for i in range(parts)]))
 
-        def delta(which, index):
+        def delta(which, first, count):
+            span = count * narrow
+            index = lambda i, s: (0, (1 - s[0] if which else s[0]) * (CHUNKS // count) + first // count)
             ins = [(a, (2, GROUP), whole2) for a in sums]
-            ins += [(attns[c][which], block, whole2) for c in range(CHUNKS)]
-            ins += [(queries, (tokens, wide), index), (out_grad, (tokens, wide), index), (gain, (1, wide), index)]
-            outs = [(block, BF16, block, whole2, VMEM)] * CHUNKS
-            outs += [((per, DH, DH), F32, (per, DH, DH), whole3, VMEM)] * CHUNKS
+            ins += [(attns[c][which], block, whole2) for c in range(first, first + count)]
+            ins += [(queries, (tokens, span), index), (out_grad, (tokens, span), index), (gain, (1, span), index)]
+            outs = [(block, BF16, block, whole2, VMEM)] * count
+            outs += [((per, DH, DH), F32, (per, DH, DH), whole3, VMEM)] * count
             result = call(
-                functools.partial(delta_body, per, CHUNKS, parts, float(parts * heads * DH)), place, ins, outs)
-            return result[:CHUNKS], result[CHUNKS:]
-
-        d_o, sent = delta(1, sent_half)
-        d_k, kept = delta(0, kept_half)
+                functools.partial(delta_body, per, count, parts, float(parts * heads * DH)), place, ins, outs)
+            return result[:count], result[count:]
+
+        d_one, sent_one = delta(1, 0, some)
+        d_two, sent_two = delta(1, some, some)
+        d_o, sent = d_one + d_two, sent_one + sent_two
+        d_k, kept = delta(0, 0, CHUNKS)
 
         def mine(c):
             return lambda i, s: (0, jnp.where(i % 2 == 0, s[0], 1 - s[0]) * CHUNKS + c + i // 2)
@@ -370,9 +375,9 @@
             return made["rest"][0]
 
         beside = {
-            (tail, 0): lambda out: query(1, 1),
-            (tail, 1): lambda out: query(2, 1),
-            (tail, CHUNKS - 2): lambda out: query(3, 1),
+            (2, 0): lambda out: query(1, 1),
+            (tail, 0): lambda out: query(2, 1),
+            (tail, 1): lambda out: query(3, 1),
             (tail, CHUNKS - 1): lambda out: rest(0, 0, out, 2),
         } if spread else {}
         after = scan(kept, sent, ends, True, [query(0, 1)], beside)

time: 99.9 us -> 97.9 us (0.980)
  waiting for transfers between devices: 25 us -> 22.8 us
  Pallas kernels: 23.2 us -> 24.4 us
  starting transfers between devices: 49.2 us -> 48.1 us
    ppermute x24, waiting for transfers between devices: 15 us -> 9.2 us  [hop(): return lax.ppermute(array, 'seq', pairs)]
    ppermute x8, waiting for transfers between devices: 3.14 us -> 5.92 us  [swap_after(): flight[c] = lax.ppermute(part_sent, 'seq', swap)]
    pallas_call x18 -> x20, Pallas kernels: 23.2 us -> 24.4 us  [call(): pl.pallas_call(body, grid_spec=pltpu.PrefetchScalarGridSpec(num_scalar_pr...]
    ppermute x24, starting transfers between devices: 28 us -> 26.9 us  [hop(): return lax.ppermute(array, 'seq', pairs)]
  transfers between devices with their start and end apart: 43 -> 43, of which waited for: 13 -> 14; matrix products, arithmetic and copies ran while one was open for 1% -> 1% of each run, Pallas kernels for 19% -> 22%
where the time goes in v9:
time: 97.9 us; the launch traced here: 97.4 us
  starting transfers between devices  48.1 us (49%)
  Pallas kernels  24.4 us (25%)
  waiting for transfers between devices  22.8 us (23%)
  between operations  1.28 us (1%)
    ppermute x24, starting transfers between devices, hop(): return lax.ppermute(array, 'seq', pairs)  26.9 us
    pallas_call x20, Pallas kernels, call(): pl.pallas_call(body, grid_spec=pltpu.PrefetchScalarGridSpec(num_scalar_pr...  24.4 us
    ppermute x8, starting transfers between devices, swap_after(): flight[c] = lax.ppermute(part_sent, 'seq', swap)  10.2 us
    ppermute x24, waiting for transfers between devices, hop(): return lax.ppermute(array, 'seq', pairs)  9.2 us
    ppermute x8, starting transfers between devices, scan(): out[c] = (carry[c], own[c], lax.ppermute(send, 'seq', swap))  9.11 us
    ppermute x8, waiting for transfers between devices, swap_after(): flight[c] = lax.ppermute(part_sent, 'seq', swap)  5.92 us
    ppermute x8, waiting for transfers between devices, scan(): out[c] = (carry[c], own[c], lax.ppermute(send, 'seq', swap))  4.92 us
    ppermute x3, waiting for transfers between devices, shards(): lax.ppermute(mine, 'head', [(i, i ^ step if paired else (i + step) % part...  2.71 us
  transfers between devices with their start and end apart: 43, of which 14 were waited for; matrix products, arithmetic and copies ran while one was open for 1% of the time, Pallas kernels for 22%

profile of v9, /device:TPU:0, one launch (start us, length us, event | category | flops | bytes accessed | tf_op | source)
XLA Modules:
  0.0 97.4 jit_solution(6024461657909148879)
XLA Ops:
  0.6 1.3 %shard_map.78 = (f32[2,128,128]{2,1,0:T(8,128)S(1)}, f32[2,128,128]{2,1,0:T(8,128)S(1)}) custom-call(s32[1]{0:T(128)} %bitcast.place, bf16[256,2048]{1,0:T(8,128)(2,1)} %k.21, bf16[256,2048]{1,0:T(8,128)(2,1)} %v.21), custom_call_target="tpu_custom_call" | custom-call | flops 1024 | bytes 1024 | tf_op jit(solution)/shard_map/pallas_call | solution.py:43
  2.0 3.0 %collective-permute-start = (f32[2,128,128]{2,1,0:T(8,128)S(1)}, f32[2,128,128]{2,1,0:T(8,128)S(1)}, u32[]{:S(2)}, u32[]{:S(2)}) collective-permute-start(f32[2,128,128]{2,1,0:T(8,128)S(1)} %get-tuple-element.105), channel_id=1, source_target_pairs={{0,4},{4,0},{8,12},{12,8},{16,20},{20,16},{24,28},{28,24},{1,5},{5... | collective-permute-start | bytes 393224 | tf_op jit(solution)/shard_map/ppermute | solution.py:219
  5.0 1.3 %shard_map.77 = (f32[2,128,128]{2,1,0:T(8,128)S(1)}, f32[2,128,128]{2,1,0:T(8,128)S(1)}) custom-call(s32[1]{0:T(128)} %bitcast.place, bf16[256,2048]{1,0:T(8,128)(2,1)} %k.21, bf16[256,2048]{1,0:T(8,128)(2,1)} %v.21), custom_call_target="tpu_custom_call" | custom-call | flops 1024 | bytes 1024 | tf_op jit(solution)/shard_map/pallas_call | solution.py:43
  6.4 2.0 %collective-permute-start.4 = (f32[2,128,128]{2,1,0:T(8,128)S(1)}, f32[2,128,128]{2,1,0:T(8,128)S(1)}, u32[]{:S(2)}, u32[]{:S(2)}) collective-permute-start(f32[2,128,128]{2,1,0:T(8,128)S(1)} %get-tuple-element.111), channel_id=1, source_target_pairs={{0,4},{4,0},{8,12},{12,8},{16,20},{20,16},{24,28},{28,24},{1,5},{5... | collective-permute-start | bytes 393224 | tf_op jit(solution)/shard_map/ppermute | solution.py:219
  8.4 4.3 %shard_map.76 = (f32[2,128,128]{2,1,0:T(8,128)S(1)}, f32[2,128,128]{2,1,0:T(8,128)S(1)}, f32[2,128,128]{2,1,0:T(8,128)S(1)}, f32[2,128,128]{2,1,0:T(8,128)S(1)}, f32[256,2048]{1,0:T(8,128)S(1)}) custom-call(s32[1]{0:T(128)} %bitcast.place, bf16[256,2048]{1,0:T(8,128)(2,1)} %q.13, bf16[256,2048]{1,0:T(8,128)(2,1)} %k.21, bf16[256,2048]{1,0:T(8,128)(2,1)} %v.21), custom_call_target="tpu_custom_call" | custom-call | flops 1024 | bytes 1024 | tf_op jit(solution)/shard_map/pallas_call | solution.py:43
  12.8 3.5 %collective-permute-start.2 = (f32[2,128,128]{2,1,0:T(8,128)S(1)}, f32[2,128,128]{2,1,0:T(8,128)S(1)}, u32[]{:S(2)}, u32[]{:S(2)}) collective-permute-start(f32[2,128,128]{2,1,0:T(8,128)S(1)} %get-tuple-element.238), channel_id=1, source_target_pairs={{0,8},{4,12},{1,9},{5,13},{2,10},{6,14},{3,11},{7,15}} | collective-permute-start | bytes 393224 | tf_op jit(solution)/shard_map/ppermute | solution.py:184
  16.9 1.3 %collective-permute-start.8 = (f32[2,128,128]{2,1,0:T(8,128)S(1)}, f32[2,128,128]{2,1,0:T(8,128)S(1)}, u32[]{:S(2)}, u32[]{:S(2)}) collective-permute-start(f32[2,128,128]{2,1,0:T(8,128)S(1)} %get-tuple-element.240), channel_id=1, source_target_pairs={{0,8},{4,12},{1,9},{5,13},{2,10},{6,14},{3,11},{7,15}} | collective-permute-start | bytes 393224 | tf_op jit(solution)/shard_map/ppermute | solution.py:184
  18.2 1.3 %collective-permute-start.7 = (f32[2,128,128]{2,1,0:T(8,128)S(1)}, f32[2,128,128]{2,1,0:T(8,128)S(1)}, u32[]{:S(2)}, u32[]{:S(2)}) collective-permute-start(f32[2,128,128]{2,1,0:T(8,128)S(1)} %get-tuple-element.242), channel_id=1, source_target_pairs={{0,8},{4,12},{1,9},{5,13},{2,10},{6,14},{3,11},{7,15}} | collective-permute-start | bytes 393224 | tf_op jit(solution)/shard_map/ppermute | solution.py:184
  21.3 4.5 %collective-permute-start.5 = (f32[2,128,128]{2,1,0:T(8,128)S(1)}, f32[2,128,128]{2,1,0:T(8,128)S(1)}, u32[]{:S(2)}, u32[]{:S(2)}) collective-permute-start(f32[2,128,128]{2,1,0:T(8,128)S(1)} %get-tuple-element.244), channel_id=1, source_target_pairs={{0,8},{4,12},{1,9},{5,13},{2,10},{6,14},{3,11},{7,15}} | collective-permute-start | bytes 393224 | tf_op jit(solution)/shard_map/ppermute | solution.py:184
  29.1 0.8 collective-permute-start.15
  30.0 0.8 collective-permute-start.14
  31.7 2.1 %collective-permute-start.18 = (f32[2,128,128]{2,1,0:T(8,128)S(1)}, f32[2,128,128]{2,1,0:T(8,128)S(1)}, u32[]{:S(2)}, u32[]{:S(2)}) collective-permute-start(f32[2,128,128]{2,1,0:T(8,128)S(1)} %get-tuple-element.217), channel_id=1, source_target_pairs={{0,4},{4,0},{8,12},{12,8},{16,20},{20,16},{24,28},{28,24},{1,5},{5... | collective-permute-start | bytes 393224 | tf_op jit(solution)/shard_map/ppermute | solution.py:239
  33.9 2.1 %collective-permute-start.16 = (f32[2,128,128]{2,1,0:T(8,128)S(1)}, f32[2,128,128]{2,1,0:T(8,128)S(1)}, u32[]{:S(2)}, u32[]{:S(2)}) collective-permute-start(f32[2,128,128]{2,1,0:T(8,128)S(1)} %get-tuple-element.213), channel_id=1, source_target_pairs={{0,4},{4,0},{8,12},{12,8},{16,20},{20,16},{24,28},{28,24},{1,5},{5... | collective-permute-start | bytes 393224 | tf_op jit(solution)/shard_map/ppermute | solution.py:239
  36.0 1.4 %collective-permute-done.19.other = f32[2,128,128]{2,1,0:T(8,128)S(1)} collective-permute-done((f32[2,128,128]{2,1,0:T(8,128)S(1)}, f32[2,128,128]{2,1,0:T(8,128)S(1)}, u32[]{:S(2)}, u32[]{:S(2)}) %collective-permute-start.19) | collective-permute-done | bytes 131104 | tf_op jit(solution)/shard_map/ppermute | solution.py:239
  37.6 1.4 %collective-permute-done.18.other = f32[2,128,128]{2,1,0:T(8,128)S(1)} collective-permute-done((f32[2,128,128]{2,1,0:T(8,128)S(1)}, f32[2,128,128]{2,1,0:T(8,128)S(1)}, u32[]{:S(2)}, u32[]{:S(2)}) %collective-permute-start.18) | collective-permute-done | bytes 131104 | tf_op jit(solution)/shard_map/ppermute | solution.py:239
  39.3 1.1 %collective-permute-done.17.other = f32[2,128,128]{2,1,0:T(8,128)S(1)} collective-permute-done((f32[2,128,128]{2,1,0:T(8,128)S(1)}, f32[2,128,128]{2,1,0:T(8,128)S(1)}, u32[]{:S(2)}, u32[]{:S(2)}) %collective-permute-start.17) | collective-permute-done | bytes 131104 | tf_op jit(solution)/shard_map/ppermute | solution.py:239
  40.7 1.1 %collective-permute-done.16.other = f32[2,128,128]{2,1,0:T(8,128)S(1)} collective-permute-done((f32[2,128,128]{2,1,0:T(8,128)S(1)}, f32[2,128,128]{2,1,0:T(8,128)S(1)}, u32[]{:S(2)}, u32[]{:S(2)}) %collective-permute-start.16) | collective-permute-done | bytes 131104 | tf_op jit(solution)/shard_map/ppermute | solution.py:239
  42.3 1.6 %collective-permute-start.21 = (f32[2,256]{1,0:T(2,128)S(1)}, f32[2,256]{1,0:T(2,128)S(1)}, u32[]{:S(2)}, u32[]{:S(2)}) collective-permute-start(f32[2,256]{1,0:T(2,128)S(1)} %get-tuple-element.134.refs_0_), channel_id=1, source_target_pairs={{0,2},{1,3},{2,0},{3,1},{4,6},{5,7},{6,4},{7,5},{8,10},{9,11},{10,... | collective-permute-start | bytes 6152 | tf_op jit(solution)/shard_map/ppermute | solution.py:319
  44.2 1.8 %collective-permute-done.21.refs_2_ = f32[2,256]{1,0:T(2,128)S(1)} collective-permute-done((f32[2,256]{1,0:T(2,128)S(1)}, f32[2,256]{1,0:T(2,128)S(1)}, u32[]{:S(2)}, u32[]{:S(2)}) %collective-permute-start.21) | collective-permute-done | bytes 2080 | tf_op jit(solution)/shard_map/ppermute | solution.py:319
  46.0 0.9 collective-permute-done.22.refs_3_
  47.3 1.2 %collective-permute-start.23 = (f32[2,128,128]{2,1,0:T(8,128)S(1)}, f32[2,128,128]{2,1,0:T(8,128)S(1)}, u32[]{:S(2)}, u32[]{:S(2)}) collective-permute-start(f32[2,128,128]{2,1,0:T(8,128)S(1)} %get-tuple-element.163), channel_id=1, source_target_pairs={{0,4},{4,0},{8,12},{12,8},{16,20},{20,16},{24,28},{28,24},{1,5},{5... | collective-permute-start | bytes 393224 | tf_op jit(solution)/shard_map/ppermute | solution.py:219
  48.9 0.9 collective-permute-start.26
  49.9 1.2 %collective-permute-start.27 = (f32[2,128,128]{2,1,0:T(8,128)S(1)}, f32[2,128,128]{2,1,0:T(8,128)S(1)}, u32[]{:S(2)}, u32[]{:S(2)}) collective-permute-start(f32[2,128,128]{2,1,0:T(8,128)S(1)} %get-tuple-element.169), channel_id=1, source_target_pairs={{0,4},{4,0},{8,12},{12,8},{16,20},{20,16},{24,28},{28,24},{1,5},{5... | collective-permute-start | bytes 393224 | tf_op jit(solution)/shard_map/ppermute | solution.py:219
  51.7 1.6 %shard_map.86.refs_4_ = bf16[256,2048]{1,0:T(8,128)(2,1)} custom-call(s32[1]{0:T(128)} %bitcast.place, bf16[256,2048]{1,0:T(8,128)(2,1)S(1)} %copy-done.1, bf16[256,2048]{1,0:T(8,128)(2,1)S(1)} %copy-done.2, bf16[256,256]{1,0:T(8,128)(2,1)S(1)} %get-tuple-element.155.refs_0_, bf16[256,256]{1,0:T(8,128)(2,1)S(1)} %get-tuple-element.156.refs_1_.refs_0_, ...), custom_call_target="tpu_custom_call" | custom-call | flops 1024 | bytes 1024 | tf_op jit(solution)/shard_map/pallas_call | solution.py:43
  54.4 4.1 %collective-permute-done.27 = f32[2,128,128]{2,1,0:T(8,128)S(1)} collective-permute-done((f32[2,128,128]{2,1,0:T(8,128)S(1)}, f32[2,128,128]{2,1,0:T(8,128)S(1)}, u32[]{:S(2)}, u32[]{:S(2)}) %collective-permute-start.27) | collective-permute-done | bytes 131104 | tf_op jit(solution)/shard_map/ppermute | solution.py:219
  59.3 1.2 %collective-permute-start.24 = (f32[2,128,128]{2,1,0:T(8,128)S(1)}, f32[2,128,128]{2,1,0:T(8,128)S(1)}, u32[]{:S(2)}, u32[]{:S(2)}) collective-permute-start(f32[2,128,128]{2,1,0:T(8,128)S(1)} %get-tuple-element.165), channel_id=1, source_target_pairs={{0,4},{4,0},{8,12},{12,8},{16,20},{20,16},{24,28},{28,24},{1,5},{5... | collective-permute-start | bytes 393224 | tf_op jit(solution)/shard_map/ppermute | solution.py:219
  60.5 0.7 collective-permute-start.30
  61.2 1.6 %shard_map.87.refs_4_ = bf16[256,2048]{1,0:T(8,128)(2,1)} custom-call(s32[1]{0:T(128)} %bitcast.place, bf16[256,2048]{1,0:T(8,128)(2,1)S(1)} %copy-done.1, bf16[256,2048]{1,0:T(8,128)(2,1)S(1)} %copy-done.2, bf16[256,256]{1,0:T(8,128)(2,1)S(1)} %get-tuple-element.149.refs_0_.refs_1_, ...), custom_call_target="tpu_custom_call", output_to_operand_aliasing={{}: (7, {})} | custom-call | flops 1024 | bytes 1024 | tf_op jit(solution)/shard_map/pallas_call | solution.py:43
  62.8 0.7 collective-permute-start.29
  63.5 0.8 collective-permute-done.24
  66.5 1.3 %collective-permute-start.33 = (f32[2,128,128]{2,1,0:T(8,128)S(1)}, f32[2,128,128]{2,1,0:T(8,128)S(1)}, u32[]{:S(2)}, u32[]{:S(2)}) collective-permute-start(f32[2,128,128]{2,1,0:T(8,128)S(1)} %get-tuple-element.211), channel_id=1, source_target_pairs={{12,4},{8,0},{13,5},{9,1},{14,6},{10,2},{15,7},{11,3}} | collective-permute-start | bytes 393224 | tf_op jit(solution)/shard_map/ppermute | solution.py:184
  68.5 1.3 %collective-permute-start.38 = (f32[2,128,128]{2,1,0:T(8,128)S(1)}, f32[2,128,128]{2,1,0:T(8,128)S(1)}, u32[]{:S(2)}, u32[]{:S(2)}) collective-permute-start(f32[2,128,128]{2,1,0:T(8,128)S(1)} %get-tuple-element.209), channel_id=1, source_target_pairs={{12,4},{8,0},{13,5},{9,1},{14,6},{10,2},{15,7},{11,3}} | collective-permute-start | bytes 393224 | tf_op jit(solution)/shard_map/ppermute | solution.py:184
  69.9 1.3 %collective-permute-start.37 = (f32[2,128,128]{2,1,0:T(8,128)S(1)}, f32[2,128,128]{2,1,0:T(8,128)S(1)}, u32[]{:S(2)}, u32[]{:S(2)}) collective-permute-start(f32[2,128,128]{2,1,0:T(8,128)S(1)} %get-tuple-element.207), channel_id=1, source_target_pairs={{12,4},{8,0},{13,5},{9,1},{14,6},{10,2},{15,7},{11,3}} | collective-permute-start | bytes 393224 | tf_op jit(solution)/shard_map/ppermute | solution.py:184
  71.2 1.6 %shard_map.88.refs_4_ = bf16[256,2048]{1,0:T(8,128)(2,1)} custom-call(s32[1]{0:T(128)} %bitcast.place, bf16[256,2048]{1,0:T(8,128)(2,1)S(1)} %copy-done.1, bf16[256,2048]{1,0:T(8,128)(2,1)S(1)} %copy-done.2, bf16[256,256]{1,0:T(8,128)(2,1)S(1)} %get-tuple-element.145.refs_0_, ...), custom_call_target="tpu_custom_call", output_to_operand_aliasing={{}: (7, {})} | custom-call | flops 1024 | bytes 1024 | tf_op jit(solution)/shard_map/pallas_call | solution.py:43
  72.8 7.3 %collective-permute-done.33 = f32[2,128,128]{2,1,0:T(8,128)S(1)} collective-permute-done((f32[2,128,128]{2,1,0:T(8,128)S(1)}, f32[2,128,128]{2,1,0:T(8,128)S(1)}, u32[]{:S(2)}, u32[]{:S(2)}) %collective-permute-start.33) | collective-permute-done | bytes 131104 | tf_op jit(solution)/shard_map/ppermute | solution.py:184
  80.1 1.1 %collective-permute-start.42 = (f32[2,128,128]{2,1,0:T(8,128)S(1)}, f32[2,128,128]{2,1,0:T(8,128)S(1)}, u32[]{:S(2)}, u32[]{:S(2)}) collective-permute-start(f32[2,128,128]{2,1,0:T(8,128)S(1)} %get-tuple-element.205), channel_id=1, source_target_pairs={{0,4},{4,0},{8,12},{12,8},{16,20},{20,16},{24,28},{28,24},{1,5},{5... | collective-permute-start | bytes 393224 | tf_op jit(solution)/shard_map/ppermute | solution.py:239
  81.2 1.5 %collective-permute-start.36 = (f32[2,128,128]{2,1,0:T(8,128)S(1)}, f32[2,128,128]{2,1,0:T(8,128)S(1)}, u32[]{:S(2)}, u32[]{:S(2)}) collective-permute-start(f32[2,128,128]{2,1,0:T(8,128)S(1)} %get-tuple-element.203), channel_id=1, source_target_pairs={{12,4},{8,0},{13,5},{9,1},{14,6},{10,2},{15,7},{11,3}} | collective-permute-start | bytes 393224 | tf_op jit(solution)/shard_map/ppermute | solution.py:184
  82.7 1.6 %shard_map.89 = bf16[256,2048]{1,0:T(8,128)(2,1)} custom-call(s32[1]{0:T(128)} %bitcast.place, bf16[256,2048]{1,0:T(8,128)(2,1)S(1)} %copy-done.1, bf16[256,2048]{1,0:T(8,128)(2,1)S(1)} %copy-done.2, bf16[256,256]{1,0:T(8,128)(2,1)S(1)} %get-tuple-element.139.refs_0_.refs_1_, ...), custom_call_target="tpu_custom_call", output_to_operand_aliasing={{}: (7, {})} | custom-call | flops 1024 | bytes 1024 | tf_op jit(solution)/shard_map/pallas_call | solution.py:43
  84.4 1.0 %collective-permute-start.41 = (f32[2,128,128]{2,1,0:T(8,128)S(1)}, f32[2,128,128]{2,1,0:T(8,128)S(1)}, u32[]{:S(2)}, u32[]{:S(2)}) collective-permute-start(f32[2,128,128]{2,1,0:T(8,128)S(1)} %get-tuple-element.201), channel_id=1, source_target_pairs={{0,4},{4,0},{8,12},{12,8},{16,20},{20,16},{24,28},{28,24},{1,5},{5... | collective-permute-start | bytes 393224 | tf_op jit(solution)/shard_map/ppermute | solution.py:239
  85.4 1.0 %collective-permute-done.37 = f32[2,128,128]{2,1,0:T(8,128)S(1)} collective-permute-done((f32[2,128,128]{2,1,0:T(8,128)S(1)}, f32[2,128,128]{2,1,0:T(8,128)S(1)}, u32[]{:S(2)}, u32[]{:S(2)}) %collective-permute-start.37) | collective-permute-done | bytes 131104 | tf_op jit(solution)/shard_map/ppermute | solution.py:184
  86.4 1.8 %collective-permute-start.40 = (f32[2,128,128]{2,1,0:T(8,128)S(1)}, f32[2,128,128]{2,1,0:T(8,128)S(1)}, u32[]{:S(2)}, u32[]{:S(2)}) collective-permute-start(f32[2,128,128]{2,1,0:T(8,128)S(1)} %get-tuple-element.199), channel_id=1, source_target_pairs={{0,4},{4,0},{8,12},{12,8},{16,20},{20,16},{24,28},{28,24},{1,5},{5... | collective-permute-start | bytes 393224 | tf_op jit(solution)/shard_map/ppermute | solution.py:239
  88.2 1.7 %shard_map.90 = (bf16[256,2048]{1,0:T(8,128)(2,1)}, bf16[256,2048]{1,0:T(8,128)(2,1)}) custom-call(s32[1]{0:T(128)} %bitcast.place, bf16[256,2048]{1,0:T(8,128)(2,1)S(1)} %copy-done, bf16[256,2048]{1,0:T(8,128)(2,1)S(1)} %copy-done.1, bf16[256,2048]{1,0:T(8,128)(2,1)S(1)} %copy-done.2, bf16[256,256]{1,0:T(8,128)(2,1)S(1)} %get-tuple-element.155.refs_0_, ...), custom_call_target="tpu_custom_call" | custom-call | flops 1024 | bytes 1024 | tf_op jit(solution)/shard_map/pallas_call | solution.py:43
  89.9 0.9 collective-permute-start.39
  90.8 1.7 %shard_map.91 = (bf16[256,2048]{1,0:T(8,128)(2,1)}, bf16[256,2048]{1,0:T(8,128)(2,1)}) custom-call(s32[1]{0:T(128)} %bitcast.place, bf16[256,2048]{1,0:T(8,128)(2,1)S(1)} %copy-done, bf16[256,2048]{1,0:T(8,128)(2,1)S(1)} %copy-done.1, bf16[256,2048]{1,0:T(8,128)(2,1)S(1)} %copy-done.2, ...), custom_call_target="tpu_custom_call", output_to_operand_aliasing={{0}: (10, {}), {1}: (11, {})} | custom-call | flops 1024 | bytes 1024 | tf_op jit(solution)/shard_map/pallas_call | solution.py:43
  92.4 1.2 %shard_map.92 = (bf16[256,2048]{1,0:T(8,128)(2,1)}, bf16[256,2048]{1,0:T(8,128)(2,1)}) custom-call(s32[1]{0:T(128)} %bitcast.place, bf16[256,2048]{1,0:T(8,128)(2,1)S(1)} %copy-done, bf16[256,2048]{1,0:T(8,128)(2,1)S(1)} %copy-done.1, bf16[256,2048]{1,0:T(8,128)(2,1)S(1)} %copy-done.2, ...), custom_call_target="tpu_custom_call", output_to_operand_aliasing={{0}: (6, {}), {1}: (7, {})} | custom-call | flops 1024 | bytes 1024 | tf_op jit(solution)/shard_map/pallas_call | solution.py:43
  93.7 1.2 %shard_map.93 = (bf16[256,2048]{1,0:T(8,128)(2,1)}, bf16[256,2048]{1,0:T(8,128)(2,1)}) custom-call(s32[1]{0:T(128)} %bitcast.place, bf16[256,2048]{1,0:T(8,128)(2,1)S(1)} %copy-done, bf16[256,2048]{1,0:T(8,128)(2,1)S(1)} %copy-done.1, bf16[256,2048]{1,0:T(8,128)(2,1)S(1)} %copy-done.2, ...), custom_call_target="tpu_custom_call", output_to_operand_aliasing={{0}: (6, {}), {1}: (7, {})} | custom-call | flops 1024 | bytes 1024 | tf_op jit(solution)/shard_map/pallas_call | solution.py:43
  94.9 1.2 %shard_map.94 = (bf16[256,2048]{1,0:T(8,128)(2,1)}, bf16[256,2048]{1,0:T(8,128)(2,1)}) custom-call(s32[1]{0:T(128)} %bitcast.place, bf16[256,2048]{1,0:T(8,128)(2,1)S(1)} %copy-done, bf16[256,2048]{1,0:T(8,128)(2,1)S(1)} %copy-done.1, bf16[256,2048]{1,0:T(8,128)(2,1)S(1)} %copy-done.2, ...), custom_call_target="tpu_custom_call", output_to_operand_aliasing={{0}: (6, {}), {1}: (7, {})} | custom-call | flops 1024 | bytes 1024 | tf_op jit(solution)/shard_map/pallas_call | solution.py:43
  96.2 1.2 %shard_map.95 = (bf16[256,2048]{1,0:T(8,128)(2,1)}, bf16[256,2048]{1,0:T(8,128)(2,1)}) custom-call(s32[1]{0:T(128)} %bitcast.place, bf16[256,2048]{1,0:T(8,128)(2,1)S(1)} %copy-done, bf16[256,2048]{1,0:T(8,128)(2,1)S(1)} %copy-done.1, bf16[256,2048]{1,0:T(8,128)(2,1)S(1)} %copy-done.2, ...), custom_call_target="tpu_custom_call", output_to_operand_aliasing={{0}: (6, {}), {1}: (7, {})} | custom-call | flops 1024 | bytes 1024 | tf_op jit(solution)/shard_map/pallas_call | solution.py:43
  (101 shorter events, 14.7 us)
Async XLA Ops:
  2.0 10.8 %collective-permute-start = (f32[2,128,128]{2,1,0:T(8,128)S(1)}, f32[2,128,128]{2,1,0:T(8,128)S(1)}, u32[]{:S(2)}, u32[]{:S(2)}) collective-permute-start(f32[2,128,128]{2,1,0:T(8,128)S(1)} %get-tuple-element.105), channel_id=1, source_target_pairs={{0,4},{4,0},{8,12},{12,8},{16,20},{20,16},{24,28},{28,24},{1,5},{5... | collective-permute-start | bytes 393224 | tf_op jit(solution)/shard_map/ppermute | solution.py:219
  6.3 11.9 %collective-permute-start.3 = (f32[2,128,128]{2,1,0:T(8,128)S(1)}, f32[2,128,128]{2,1,0:T(8,128)S(1)}, u32[]{:S(2)}, u32[]{:S(2)}) collective-permute-start(f32[2,128,128]{2,1,0:T(8,128)S(1)} %get-tuple-element.109), channel_id=1, source_target_pairs={{0,4},{4,0},{8,12},{12,8},{16,20},{20,16},{24,28},{28,24},{1,5},{5... | collective-permute-start | bytes 393224 | tf_op jit(solution)/shard_map/ppermute | solution.py:219
  6.4 10.5 %collective-permute-start.4 = (f32[2,128,128]{2,1,0:T(8,128)S(1)}, f32[2,128,128]{2,1,0:T(8,128)S(1)}, u32[]{:S(2)}, u32[]{:S(2)}) collective-permute-start(f32[2,128,128]{2,1,0:T(8,128)S(1)} %get-tuple-element.111), channel_id=1, source_target_pairs={{0,4},{4,0},{8,12},{12,8},{16,20},{20,16},{24,28},{28,24},{1,5},{5... | collective-permute-start | bytes 393224 | tf_op jit(solution)/shard_map/ppermute | solution.py:219
  12.8 7.3 %collective-permute-start.2 = (f32[2,128,128]{2,1,0:T(8,128)S(1)}, f32[2,128,128]{2,1,0:T(8,128)S(1)}, u32[]{:S(2)}, u32[]{:S(2)}) collective-permute-start(f32[2,128,128]{2,1,0:T(8,128)S(1)} %get-tuple-element.238), channel_id=1, source_target_pairs={{0,8},{4,12},{1,9},{5,13},{2,10},{6,14},{3,11},{7,15}} | collective-permute-start | bytes 393224 | tf_op jit(solution)/shard_map/ppermute | solution.py:184
  16.3 5.0 %collective-permute-start.1 = (f32[2,128,128]{2,1,0:T(8,128)S(1)}, f32[2,128,128]{2,1,0:T(8,128)S(1)}, u32[]{:S(2)}, u32[]{:S(2)}) collective-permute-start(f32[2,128,128]{2,1,0:T(8,128)S(1)} %get-tuple-element.107), channel_id=1, source_target_pairs={{0,4},{4,0},{8,12},{12,8},{16,20},{20,16},{24,28},{28,24},{1,5},{5... | collective-permute-start | bytes 393224 | tf_op jit(solution)/shard_map/ppermute | solution.py:219
  16.9 9.0 %collective-permute-start.8 = (f32[2,128,128]{2,1,0:T(8,128)S(1)}, f32[2,128,128]{2,1,0:T(8,128)S(1)}, u32[]{:S(2)}, u32[]{:S(2)}) collective-permute-start(f32[2,128,128]{2,1,0:T(8,128)S(1)} %get-tuple-element.240), channel_id=1, source_target_pairs={{0,8},{4,12},{1,9},{5,13},{2,10},{6,14},{3,11},{7,15}} | collective-permute-start | bytes 393224 | tf_op jit(solution)/shard_map/ppermute | solution.py:184
  18.2 8.3 %collective-permute-start.7 = (f32[2,128,128]{2,1,0:T(8,128)S(1)}, f32[2,128,128]{2,1,0:T(8,128)S(1)}, u32[]{:S(2)}, u32[]{:S(2)}) collective-permute-start(f32[2,128,128]{2,1,0:T(8,128)S(1)} %get-tuple-element.242), channel_id=1, source_target_pairs={{0,8},{4,12},{1,9},{5,13},{2,10},{6,14},{3,11},{7,15}} | collective-permute-start | bytes 393224 | tf_op jit(solution)/shard_map/ppermute | solution.py:184
  20.1 7.2 %collective-permute-start.6 = (f32[2,128,128]{2,1,0:T(8,128)S(1)}, f32[2,128,128]{2,1,0:T(8,128)S(1)}, u32[]{:S(2)}, u32[]{:S(2)}) collective-permute-start(f32[2,128,128]{2,1,0:T(8,128)S(1)} %add.152), channel_id=1, source_target_pairs={{8,16},{12,20},{9,17},{13,21},{10,18},{14,22},{11,19},{15,23}} | collective-permute-start | bytes 393224 | tf_op jit(solution)/shard_map/ppermute | solution.py:184
  21.3 7.0 %collective-permute-start.5 = (f32[2,128,128]{2,1,0:T(8,128)S(1)}, f32[2,128,128]{2,1,0:T(8,128)S(1)}, u32[]{:S(2)}, u32[]{:S(2)}) collective-permute-start(f32[2,128,128]{2,1,0:T(8,128)S(1)} %get-tuple-element.244), channel_id=1, source_target_pairs={{0,8},{4,12},{1,9},{5,13},{2,10},{6,14},{3,11},{7,15}} | collective-permute-start | bytes 393224 | tf_op jit(solution)/shard_map/ppermute | solution.py:184
  25.8 3.2 %collective-permute-start.12 = (f32[2,128,128]{2,1,0:T(8,128)S(1)}, f32[2,128,128]{2,1,0:T(8,128)S(1)}, u32[]{:S(2)}, u32[]{:S(2)}) collective-permute-start(f32[2,128,128]{2,1,0:T(8,128)S(1)} %add.154), channel_id=1, source_target_pairs={{8,16},{12,20},{9,17},{13,21},{10,18},{14,22},{11,19},{15,23}} | collective-permute-start | bytes 393224 | tf_op jit(solution)/shard_map/ppermute | solution.py:184
  26.6 3.4 %collective-permute-start.11 = (f32[2,128,128]{2,1,0:T(8,128)S(1)}, f32[2,128,128]{2,1,0:T(8,128)S(1)}, u32[]{:S(2)}, u32[]{:S(2)}) collective-permute-start(f32[2,128,128]{2,1,0:T(8,128)S(1)} %add.155), channel_id=1, source_target_pairs={{8,16},{12,20},{9,17},{13,21},{10,18},{14,22},{11,19},{15,23}} | collective-permute-start | bytes 393224 | tf_op jit(solution)/shard_map/ppermute | solution.py:184
  27.3 3.5 %collective-permute-start.10 = (f32[2,128,128]{2,1,0:T(8,128)S(1)}, f32[2,128,128]{2,1,0:T(8,128)S(1)}, u32[]{:S(2)}, u32[]{:S(2)}) collective-permute-start(f32[2,128,128]{2,1,0:T(8,128)S(1)} %get-tuple-element.227), channel_id=1, source_target_pairs={{16,24},{20,28},{17,25},{21,29},{18,26},{22,30},{19,27},{23,31}} | collective-permute-start | bytes 393224 | tf_op jit(solution)/shard_map/ppermute | solution.py:184
  28.3 2.6 %collective-permute-start.9 = (f32[2,128,128]{2,1,0:T(8,128)S(1)}, f32[2,128,128]{2,1,0:T(8,128)S(1)}, u32[]{:S(2)}, u32[]{:S(2)}) collective-permute-start(f32[2,128,128]{2,1,0:T(8,128)S(1)} %add.158), channel_id=1, source_target_pairs={{8,16},{12,20},{9,17},{13,21},{10,18},{14,22},{11,19},{15,23}} | collective-permute-start | bytes 393224 | tf_op jit(solution)/shard_map/ppermute | solution.py:184
  29.0 8.3 %copy-start.3 = (bf16[256,2048]{1,0:T(8,128)(2,1)S(1)}, bf16[256,2048]{1,0:T(8,128)(2,1)}, u32[]{:S(2)}) copy-start(bf16[256,2048]{1,0:T(8,128)(2,1)} %refs_7_.3) | copy-start | bytes 3145732
  29.1 6.9 %copy-start.4 = (bf16[2048]{0:T(1024)(128)(2,1)S(1)}, bf16[2048]{0:T(1024)(128)(2,1)}, u32[]{:S(2)}) copy-start(bf16[2048]{0:T(1024)(128)(2,1)} %param.9) | copy-start | bytes 12292
  29.1 8.2 %copy-start = (bf16[256,2048]{1,0:T(8,128)(2,1)S(1)}, bf16[256,2048]{1,0:T(8,128)(2,1)}, u32[]{:S(2)}) copy-start(bf16[256,2048]{1,0:T(8,128)(2,1)} %q.13) | copy-start | bytes 3145732
  29.1 8.2 %copy-start.1 = (bf16[256,2048]{1,0:T(8,128)(2,1)S(1)}, bf16[256,2048]{1,0:T(8,128)(2,1)}, u32[]{:S(2)}) copy-start(bf16[256,2048]{1,0:T(8,128)(2,1)} %k.21) | copy-start | bytes 3145732
  29.1 8.2 %copy-start.2 = (bf16[256,2048]{1,0:T(8,128)(2,1)S(1)}, bf16[256,2048]{1,0:T(8,128)(2,1)}, u32[]{:S(2)}) copy-start(bf16[256,2048]{1,0:T(8,128)(2,1)} %v.21) | copy-start | bytes 3145732
  29.1 2.5 %collective-permute-start.15 = (f32[2,128,128]{2,1,0:T(8,128)S(1)}, f32[2,128,128]{2,1,0:T(8,128)S(1)}, u32[]{:S(2)}, u32[]{:S(2)}) collective-permute-start(f32[2,128,128]{2,1,0:T(8,128)S(1)} %get-tuple-element.225), channel_id=1, source_target_pairs={{16,24},{20,28},{17,25},{21,29},{18,26},{22,30},{19,27},{23,31}} | collective-permute-start | bytes 393224 | tf_op jit(solution)/shard_map/ppermute | solution.py:184
  30.0 3.8 %collective-permute-start.14 = (f32[2,128,128]{2,1,0:T(8,128)S(1)}, f32[2,128,128]{2,1,0:T(8,128)S(1)}, u32[]{:S(2)}, u32[]{:S(2)}) collective-permute-start(f32[2,128,128]{2,1,0:T(8,128)S(1)} %get-tuple-element.223), channel_id=1, source_target_pairs={{16,24},{20,28},{17,25},{21,29},{18,26},{22,30},{19,27},{23,31}} | collective-permute-start | bytes 393224 | tf_op jit(solution)/shard_map/ppermute | solution.py:184
  30.8 6.5 %collective-permute-start.19 = (f32[2,128,128]{2,1,0:T(8,128)S(1)}, f32[2,128,128]{2,1,0:T(8,128)S(1)}, u32[]{:S(2)}, u32[]{:S(2)}) collective-permute-start(f32[2,128,128]{2,1,0:T(8,128)S(1)} %get-tuple-element.221), channel_id=1, source_target_pairs={{0,4},{4,0},{8,12},{12,8},{16,20},{20,16},{24,28},{28,24},{1,5},{5... | collective-permute-start | bytes 393224 | tf_op jit(solution)/shard_map/ppermute | solution.py:239
  30.9 2.9 %collective-permute-start.13 = (f32[2,128,128]{2,1,0:T(8,128)S(1)}, f32[2,128,128]{2,1,0:T(8,128)S(1)}, u32[]{:S(2)}, u32[]{:S(2)}) collective-permute-start(f32[2,128,128]{2,1,0:T(8,128)S(1)} %get-tuple-element.219), channel_id=1, source_target_pairs={{16,24},{20,28},{17,25},{21,29},{18,26},{22,30},{19,27},{23,31}} | collective-permute-start | bytes 393224 | tf_op jit(solution)/shard_map/ppermute | solution.py:184
  31.7 7.3 %collective-permute-start.18 = (f32[2,128,128]{2,1,0:T(8,128)S(1)}, f32[2,128,128]{2,1,0:T(8,128)S(1)}, u32[]{:S(2)}, u32[]{:S(2)}) collective-permute-start(f32[2,128,128]{2,1,0:T(8,128)S(1)} %get-tuple-element.217), channel_id=1, source_target_pairs={{0,4},{4,0},{8,12},{12,8},{16,20},{20,16},{24,28},{28,24},{1,5},{5... | collective-permute-start | bytes 393224 | tf_op jit(solution)/shard_map/ppermute | solution.py:239
  33.8 6.6 %collective-permute-start.17 = (f32[2,128,128]{2,1,0:T(8,128)S(1)}, f32[2,128,128]{2,1,0:T(8,128)S(1)}, u32[]{:S(2)}, u32[]{:S(2)}) collective-permute-start(f32[2,128,128]{2,1,0:T(8,128)S(1)} %get-tuple-element.215), channel_id=1, source_target_pairs={{0,4},{4,0},{8,12},{12,8},{16,20},{20,16},{24,28},{28,24},{1,5},{5... | collective-permute-start | bytes 393224 | tf_op jit(solution)/shard_map/ppermute | solution.py:239
  33.9 7.9 %collective-permute-start.16 = (f32[2,128,128]{2,1,0:T(8,128)S(1)}, f32[2,128,128]{2,1,0:T(8,128)S(1)}, u32[]{:S(2)}, u32[]{:S(2)}) collective-permute-start(f32[2,128,128]{2,1,0:T(8,128)S(1)} %get-tuple-element.213), channel_id=1, source_target_pairs={{0,4},{4,0},{8,12},{12,8},{16,20},{20,16},{24,28},{28,24},{1,5},{5... | collective-permute-start | bytes 393224 | tf_op jit(solution)/shard_map/ppermute | solution.py:239
  42.2 1.9 %collective-permute-start.20 = (f32[2,256]{1,0:T(2,128)S(1)}, f32[2,256]{1,0:T(2,128)S(1)}, u32[]{:S(2)}, u32[]{:S(2)}) collective-permute-start(f32[2,256]{1,0:T(2,128)S(1)} %get-tuple-element.134.refs_0_), channel_id=1, source_target_pairs={{0,1},{1,0},{2,3},{3,2},{4,5},{5,4},{6,7},{7,6},{8,9},{9,8},{10,11... | collective-permute-start | bytes 6152 | tf_op jit(solution)/shard_map/ppermute | solution.py:319
  42.3 3.7 %collective-permute-start.21 = (f32[2,256]{1,0:T(2,128)S(1)}, f32[2,256]{1,0:T(2,128)S(1)}, u32[]{:S(2)}, u32[]{:S(2)}) collective-permute-start(f32[2,256]{1,0:T(2,128)S(1)} %get-tuple-element.134.refs_0_), channel_id=1, source_target_pairs={{0,2},{1,3},{2,0},{3,1},{4,6},{5,7},{6,4},{7,5},{8,10},{9,11},{10,... | collective-permute-start | bytes 6152 | tf_op jit(solution)/shard_map/ppermute | solution.py:319
  43.9 3.0 %collective-permute-start.22 = (f32[2,256]{1,0:T(2,128)S(1)}, f32[2,256]{1,0:T(2,128)S(1)}, u32[]{:S(2)}, u32[]{:S(2)}) collective-permute-start(f32[2,256]{1,0:T(2,128)S(1)} %get-tuple-element.134.refs_0_), channel_id=1, source_target_pairs={{0,3},{1,2},{2,1},{3,0},{4,7},{5,6},{6,5},{7,4},{8,11},{9,10},{10,... | collective-permute-start | bytes 6152 | tf_op jit(solution)/shard_map/ppermute | solution.py:319
  47.3 6.4 %collective-permute-start.23 = (f32[2,128,128]{2,1,0:T(8,128)S(1)}, f32[2,128,128]{2,1,0:T(8,128)S(1)}, u32[]{:S(2)}, u32[]{:S(2)}) collective-permute-start(f32[2,128,128]{2,1,0:T(8,128)S(1)} %get-tuple-element.163), channel_id=1, source_target_pairs={{0,4},{4,0},{8,12},{12,8},{16,20},{20,16},{24,28},{28,24},{1,5},{5... | collective-permute-start | bytes 393224 | tf_op jit(solution)/shard_map/ppermute | solution.py:219
  48.9 10.3 %collective-permute-start.26 = (f32[2,128,128]{2,1,0:T(8,128)S(1)}, f32[2,128,128]{2,1,0:T(8,128)S(1)}, u32[]{:S(2)}, u32[]{:S(2)}) collective-permute-start(f32[2,128,128]{2,1,0:T(8,128)S(1)} %get-tuple-element.167), channel_id=1, source_target_pairs={{0,4},{4,0},{8,12},{12,8},{16,20},{20,16},{24,28},{28,24},{1,5},{5... | collective-permute-start | bytes 393224 | tf_op jit(solution)/shard_map/ppermute | solution.py:219
  49.9 8.7 %collective-permute-start.27 = (f32[2,128,128]{2,1,0:T(8,128)S(1)}, f32[2,128,128]{2,1,0:T(8,128)S(1)}, u32[]{:S(2)}, u32[]{:S(2)}) collective-permute-start(f32[2,128,128]{2,1,0:T(8,128)S(1)} %get-tuple-element.169), channel_id=1, source_target_pairs={{0,4},{4,0},{8,12},{12,8},{16,20},{20,16},{24,28},{28,24},{1,5},{5... | collective-permute-start | bytes 393224 | tf_op jit(solution)/shard_map/ppermute | solution.py:219
  53.7 9.1 %collective-permute-start.25 = (f32[2,128,128]{2,1,0:T(8,128)S(1)}, f32[2,128,128]{2,1,0:T(8,128)S(1)}, u32[]{:S(2)}, u32[]{:S(2)}) collective-permute-start(f32[2,128,128]{2,1,0:T(8,128)S(1)} %get-tuple-element.236), channel_id=1, source_target_pairs={{28,20},{24,16},{29,21},{25,17},{30,22},{26,18},{31,23},{27,19}} | collective-permute-start | bytes 393224 | tf_op jit(solution)/shard_map/ppermute | solution.py:184
  58.6 6.4 %collective-permute-start.31 = (f32[2,128,128]{2,1,0:T(8,128)S(1)}, f32[2,128,128]{2,1,0:T(8,128)S(1)}, u32[]{:S(2)}, u32[]{:S(2)}) collective-permute-start(f32[2,128,128]{2,1,0:T(8,128)S(1)} %get-tuple-element.234), channel_id=1, source_target_pairs={{28,20},{24,16},{29,21},{25,17},{30,22},{26,18},{31,23},{27,19}} | collective-permute-start | bytes 393224 | tf_op jit(solution)/shard_map/ppermute | solution.py:184
  59.3 5.0 %collective-permute-start.24 = (f32[2,128,128]{2,1,0:T(8,128)S(1)}, f32[2,128,128]{2,1,0:T(8,128)S(1)}, u32[]{:S(2)}, u32[]{:S(2)}) collective-permute-start(f32[2,128,128]{2,1,0:T(8,128)S(1)} %get-tuple-element.165), channel_id=1, source_target_pairs={{0,4},{4,0},{8,12},{12,8},{16,20},{20,16},{24,28},{28,24},{1,5},{5... | collective-permute-start | bytes 393224 | tf_op jit(solution)/shard_map/ppermute | solution.py:219
  60.5 5.2 %collective-permute-start.30 = (f32[2,128,128]{2,1,0:T(8,128)S(1)}, f32[2,128,128]{2,1,0:T(8,128)S(1)}, u32[]{:S(2)}, u32[]{:S(2)}) collective-permute-start(f32[2,128,128]{2,1,0:T(8,128)S(1)} %get-tuple-element.232), channel_id=1, source_target_pairs={{28,20},{24,16},{29,21},{25,17},{30,22},{26,18},{31,23},{27,19}} | collective-permute-start | bytes 393224 | tf_op jit(solution)/shard_map/ppermute | solution.py:184
  62.8 3.6 %collective-permute-start.29 = (f32[2,128,128]{2,1,0:T(8,128)S(1)}, f32[2,128,128]{2,1,0:T(8,128)S(1)}, u32[]{:S(2)}, u32[]{:S(2)}) collective-permute-start(f32[2,128,128]{2,1,0:T(8,128)S(1)} %add.176), channel_id=1, source_target_pairs={{20,12},{16,8},{21,13},{17,9},{22,14},{18,10},{23,15},{19,11}} | collective-permute-start | bytes 393224 | tf_op jit(solution)/shard_map/ppermute | solution.py:184
  64.3 3.4 %collective-permute-start.28 = (f32[2,128,128]{2,1,0:T(8,128)S(1)}, f32[2,128,128]{2,1,0:T(8,128)S(1)}, u32[]{:S(2)}, u32[]{:S(2)}) collective-permute-start(f32[2,128,128]{2,1,0:T(8,128)S(1)} %get-tuple-element.230), channel_id=1, source_target_pairs={{28,20},{24,16},{29,21},{25,17},{30,22},{26,18},{31,23},{27,19}} | collective-permute-start | bytes 393224 | tf_op jit(solution)/shard_map/ppermute | solution.py:184
  65.0 3.4 %collective-permute-start.35 = (f32[2,128,128]{2,1,0:T(8,128)S(1)}, f32[2,128,128]{2,1,0:T(8,128)S(1)}, u32[]{:S(2)}, u32[]{:S(2)}) collective-permute-start(f32[2,128,128]{2,1,0:T(8,128)S(1)} %add.178), channel_id=1, source_target_pairs={{20,12},{16,8},{21,13},{17,9},{22,14},{18,10},{23,15},{19,11}} | collective-permute-start | bytes 393224 | tf_op jit(solution)/shard_map/ppermute | solution.py:184
  65.7 4.1 %collective-permute-start.34 = (f32[2,128,128]{2,1,0:T(8,128)S(1)}, f32[2,128,128]{2,1,0:T(8,128)S(1)}, u32[]{:S(2)}, u32[]{:S(2)}) collective-permute-start(f32[2,128,128]{2,1,0:T(8,128)S(1)} %add.179), channel_id=1, source_target_pairs={{20,12},{16,8},{21,13},{17,9},{22,14},{18,10},{23,15},{19,11}} | collective-permute-start | bytes 393224 | tf_op jit(solution)/shard_map/ppermute | solution.py:184
  66.5 13.6 %collective-permute-start.33 = (f32[2,128,128]{2,1,0:T(8,128)S(1)}, f32[2,128,128]{2,1,0:T(8,128)S(1)}, u32[]{:S(2)}, u32[]{:S(2)}) collective-permute-start(f32[2,128,128]{2,1,0:T(8,128)S(1)} %get-tuple-element.211), channel_id=1, source_target_pairs={{12,4},{8,0},{13,5},{9,1},{14,6},{10,2},{15,7},{11,3}} | collective-permute-start | bytes 393224 | tf_op jit(solution)/shard_map/ppermute | solution.py:184
  67.8 13.4 %collective-permute-start.32 = (f32[2,128,128]{2,1,0:T(8,128)S(1)}, f32[2,128,128]{2,1,0:T(8,128)S(1)}, u32[]{:S(2)}, u32[]{:S(2)}) collective-permute-start(f32[2,128,128]{2,1,0:T(8,128)S(1)} %add.182), channel_id=1, source_target_pairs={{20,12},{16,8},{21,13},{17,9},{22,14},{18,10},{23,15},{19,11}} | collective-permute-start | bytes 393224 | tf_op jit(solution)/shard_map/ppermute | solution.py:184
  68.5 15.8 %collective-permute-start.38 = (f32[2,128,128]{2,1,0:T(8,128)S(1)}, f32[2,128,128]{2,1,0:T(8,128)S(1)}, u32[]{:S(2)}, u32[]{:S(2)}) collective-permute-start(f32[2,128,128]{2,1,0:T(8,128)S(1)} %get-tuple-element.209), channel_id=1, source_target_pairs={{12,4},{8,0},{13,5},{9,1},{14,6},{10,2},{15,7},{11,3}} | collective-permute-start | bytes 393224 | tf_op jit(solution)/shard_map/ppermute | solution.py:184
  69.9 16.5 %collective-permute-start.37 = (f32[2,128,128]{2,1,0:T(8,128)S(1)}, f32[2,128,128]{2,1,0:T(8,128)S(1)}, u32[]{:S(2)}, u32[]{:S(2)}) collective-permute-start(f32[2,128,128]{2,1,0:T(8,128)S(1)} %get-tuple-element.207), channel_id=1, source_target_pairs={{12,4},{8,0},{13,5},{9,1},{14,6},{10,2},{15,7},{11,3}} | collective-permute-start | bytes 393224 | tf_op jit(solution)/shard_map/ppermute | solution.py:184
  80.1 12.4 %collective-permute-start.42 = (f32[2,128,128]{2,1,0:T(8,128)S(1)}, f32[2,128,128]{2,1,0:T(8,128)S(1)}, u32[]{:S(2)}, u32[]{:S(2)}) collective-permute-start(f32[2,128,128]{2,1,0:T(8,128)S(1)} %get-tuple-element.205), channel_id=1, source_target_pairs={{0,4},{4,0},{8,12},{12,8},{16,20},{20,16},{24,28},{28,24},{1,5},{5... | collective-permute-start | bytes 393224 | tf_op jit(solution)/shard_map/ppermute | solution.py:239
  81.2 8.6 %collective-permute-start.36 = (f32[2,128,128]{2,1,0:T(8,128)S(1)}, f32[2,128,128]{2,1,0:T(8,128)S(1)}, u32[]{:S(2)}, u32[]{:S(2)}) collective-permute-start(f32[2,128,128]{2,1,0:T(8,128)S(1)} %get-tuple-element.203), channel_id=1, source_target_pairs={{12,4},{8,0},{13,5},{9,1},{14,6},{10,2},{15,7},{11,3}} | collective-permute-start | bytes 393224 | tf_op jit(solution)/shard_map/ppermute | solution.py:184
  84.4 9.3 %collective-permute-start.41 = (f32[2,128,128]{2,1,0:T(8,128)S(1)}, f32[2,128,128]{2,1,0:T(8,128)S(1)}, u32[]{:S(2)}, u32[]{:S(2)}) collective-permute-start(f32[2,128,128]{2,1,0:T(8,128)S(1)} %get-tuple-element.201), channel_id=1, source_target_pairs={{0,4},{4,0},{8,12},{12,8},{16,20},{20,16},{24,28},{28,24},{1,5},{5... | collective-permute-start | bytes 393224 | tf_op jit(solution)/shard_map/ppermute | solution.py:239
  86.4 8.5 %collective-permute-start.40 = (f32[2,128,128]{2,1,0:T(8,128)S(1)}, f32[2,128,128]{2,1,0:T(8,128)S(1)}, u32[]{:S(2)}, u32[]{:S(2)}) collective-permute-start(f32[2,128,128]{2,1,0:T(8,128)S(1)} %get-tuple-element.199), channel_id=1, source_target_pairs={{0,4},{4,0},{8,12},{12,8},{16,20},{20,16},{24,28},{28,24},{1,5},{5... | collective-permute-start | bytes 393224 | tf_op jit(solution)/shard_map/ppermute | solution.py:239
  89.9 6.3 %collective-permute-start.39 = (f32[2,128,128]{2,1,0:T(8,128)S(1)}, f32[2,128,128]{2,1,0:T(8,128)S(1)}, u32[]{:S(2)}, u32[]{:S(2)}) collective-permute-start(f32[2,128,128]{2,1,0:T(8,128)S(1)} %get-tuple-element.197), channel_id=1, source_target_pairs={{0,4},{4,0},{8,12},{12,8},{16,20},{20,16},{24,28},{28,24},{1,5},{5... | collective-permute-start | bytes 393224 | tf_op jit(solution)/shard_map/ppermute | solution.py:239

commit v10 on v9

--- a/solution.py
+++ b/solution.py
@@ -210,7 +210,7 @@
             return list(zip(sums, own, others))
         chunks = len(kept)
         order = sorted((2 * stage + c, stage, c) for stage in range(long) for c in range(chunks))
-        part, flight, carry, out = {}, {}, {}, {}
+        part, flight, carry, out, sends = {}, {}, {}, {}, {}
         last = ready
 
         def swap_after(c, *things):
@@ -223,7 +223,7 @@
         swap_after(2)
         for _, stage, c in order:
             if (stage, c) in beside:
-                last = last + [beside[stage, c](out)]
+                last = last + [beside[stage, c](out, sends)]
             got, *_ = lax.optimization_barrier((flight[c], *last))
             if stage == 0:
                 own[c] = jnp.where(leads, 0.0, got)
@@ -238,6 +238,7 @@
                 send = jnp.where(leads, carry[c] + kept[c], carry[c])
                 out[c] = (carry[c], own[c], lax.ppermute(send, "seq", swap))
             last = [send]
+            sends[stage, c] = send
         return [out[c] for c in range(chunks)]
 
     def shards(queries, keys, values, out_grad, norm_gain):
@@ -342,10 +343,13 @@
         state3 = (per, DH, DH)
         made = {"query": [], "rest": []}
 
-        def query(c, count):
+        def query(c, count, tie=None):
             ins = [(a, block, mine(c)) for a in (keys, values)]
             some = range(c, c + count)
-            ins += [(a, block, whole2) for i in some for a in (d_k[i], d_o[i])]
+            grads = [a for i in some for a in (d_k[i], d_o[i])]
+            if tie is not None:
+                grads[0], _ = lax.optimization_barrier((grads[0], tie))
+            ins += [(a, block, whole2) for a in grads]
             ins += [(a, state3, whole3) for i in some for a in priors[i]]
             aliases = {}
             if made["query"]:
@@ -375,18 +379,21 @@
             return made["rest"][0]
 
         beside = {
-            (2, 0): lambda out: query(1, 1),
-            (tail, 0): lambda out: query(2, 1),
-            (tail, 1): lambda out: query(3, 1),
-            (tail, CHUNKS - 1): lambda out: rest(0, 0, out, 2),
+            (2, 0): lambda out, sends: query(0, 2, sends[1, 1]),
+            (tail, 0): lambda out, sends: query(2, 1, sends[2, 1]),
+            (tail, 1): lambda out, sends: query(3, 1),
+            (tail, 2): lambda out, sends: rest(0, 0, out, 2),
+            (tail, 3): lambda out, sends: rest(2, 0, out),
         } if spread else {}
-        after = scan(kept, sent, ends, True, [query(0, 1)], beside)
+        after = scan(kept, sent, ends, True, [], beside)
         if not spread:
-            query(1, 3)
+            query(0, CHUNKS)
             rest(0, 0, after, 2)
-        rest(2, 0, after, 2)
-        for c in range(CHUNKS):
-            rest(c, 1, after)
+            rest(2, 0, after)
+        rest(3, 0, after)
+        rest(0, 1, after, 2)
+        rest(2, 1, after)
+        rest(3, 1, after)
         return made["query"][0], made["rest"][0], made["rest"][1]
 
     return jax.shard_map(

time: 97.9 us -> 93.7 us (0.957)
  waiting for transfers between devices: 22.8 us -> 20.5 us
  starting transfers between devices: 48.1 us -> 46.5 us
    ppermute x24, waiting for transfers between devices: 9.2 us -> 6.4 us  [hop(): return lax.ppermute(array, 'seq', pairs)]
    ppermute x8, waiting for transfers between devices: 5.92 us -> 7.57 us  [swap_after(): flight[c] = lax.ppermute(part_sent, 'seq', swap)]
    ppermute x24, starting transfers between devices: 26.9 us -> 25.7 us  [hop(): return lax.ppermute(array, 'seq', pairs)]
    pallas_call x20 -> x19, Pallas kernels: 24.4 us -> 23.9 us  [call(): pl.pallas_call(body, grid_spec=pltpu.PrefetchScalarGridSpec(num_scalar_pr...]
where the time goes in v10:
time: 93.7 us; the launch traced here: 92.9 us
  starting transfers between devices  46.5 us (50%)
  Pallas kernels  23.9 us (26%)
  waiting for transfers between devices  20.5 us (22%)
  between operations  1.27 us (1%)
    ppermute x24, starting transfers between devices, hop(): return lax.ppermute(array, 'seq', pairs)  25.7 us
    pallas_call x19, Pallas kernels, call(): pl.pallas_call(body, grid_spec=pltpu.PrefetchScalarGridSpec(num_scalar_pr...  23.9 us
    ppermute x8, starting transfers between devices, swap_after(): flight[c] = lax.ppermute(part_sent, 'seq', swap)  10.3 us
    ppermute x8, starting transfers between devices, scan(): out[c] = (carry[c], own[c], lax.ppermute(send, 'seq', swap))  8.62 us
    ppermute x8, waiting for transfers between devices, swap_after(): flight[c] = lax.ppermute(part_sent, 'seq', swap)  7.57 us
    ppermute x24, waiting for transfers between devices, hop(): return lax.ppermute(array, 'seq', pairs)  6.4 us
    ppermute x8, waiting for transfers between devices, scan(): out[c] = (carry[c], own[c], lax.ppermute(send, 'seq', swap))  4.74 us
    ppermute x3, starting transfers between devices, shards(): lax.ppermute(mine, 'head', [(i, i ^ step if paired else (i + step) % part...  1.92 us
  transfers between devices with their start and end apart: 43, of which 14 were waited for; matrix products, arithmetic and copies ran while one was open for 1% of the time, Pallas kernels for 22%

profile of v10, /device:TPU:0, one launch (start us, length us, event | category | flops | bytes accessed | tf_op | source)
XLA Modules:
  0.0 92.9 jit_solution(4817025519278616741)
XLA Ops:
  0.6 1.3 %shard_map.78 = (f32[2,128,128]{2,1,0:T(8,128)S(1)}, f32[2,128,128]{2,1,0:T(8,128)S(1)}) custom-call(s32[1]{0:T(128)} %bitcast.place, bf16[256,2048]{1,0:T(8,128)(2,1)} %k.19, bf16[256,2048]{1,0:T(8,128)(2,1)} %v.19), custom_call_target="tpu_custom_call" | custom-call | flops 1024 | bytes 1024 | tf_op jit(solution)/shard_map/pallas_call | solution.py:43
  2.0 3.0 %collective-permute-start = (f32[2,128,128]{2,1,0:T(8,128)S(1)}, f32[2,128,128]{2,1,0:T(8,128)S(1)}, u32[]{:S(2)}, u32[]{:S(2)}) collective-permute-start(f32[2,128,128]{2,1,0:T(8,128)S(1)} %get-tuple-element.106), channel_id=1, source_target_pairs={{0,4},{4,0},{8,12},{12,8},{16,20},{20,16},{24,28},{28,24},{1,5},{5... | collective-permute-start | bytes 393224 | tf_op jit(solution)/shard_map/ppermute | solution.py:219
  5.1 1.3 %shard_map.77 = (f32[2,128,128]{2,1,0:T(8,128)S(1)}, f32[2,128,128]{2,1,0:T(8,128)S(1)}) custom-call(s32[1]{0:T(128)} %bitcast.place, bf16[256,2048]{1,0:T(8,128)(2,1)} %k.19, bf16[256,2048]{1,0:T(8,128)(2,1)} %v.19), custom_call_target="tpu_custom_call" | custom-call | flops 1024 | bytes 1024 | tf_op jit(solution)/shard_map/pallas_call | solution.py:43
  6.4 2.0 %collective-permute-start.3 = (f32[2,128,128]{2,1,0:T(8,128)S(1)}, f32[2,128,128]{2,1,0:T(8,128)S(1)}, u32[]{:S(2)}, u32[]{:S(2)}) collective-permute-start(f32[2,128,128]{2,1,0:T(8,128)S(1)} %get-tuple-element.110), channel_id=1, source_target_pairs={{0,4},{4,0},{8,12},{12,8},{16,20},{20,16},{24,28},{28,24},{1,5},{5... | collective-permute-start | bytes 393224 | tf_op jit(solution)/shard_map/ppermute | solution.py:219
  8.4 4.3 %shard_map.76 = (f32[2,128,128]{2,1,0:T(8,128)S(1)}, f32[2,128,128]{2,1,0:T(8,128)S(1)}, f32[2,128,128]{2,1,0:T(8,128)S(1)}, f32[2,128,128]{2,1,0:T(8,128)S(1)}, f32[256,2048]{1,0:T(8,128)S(1)}) custom-call(s32[1]{0:T(128)} %bitcast.place, bf16[256,2048]{1,0:T(8,128)(2,1)} %q.13, bf16[256,2048]{1,0:T(8,128)(2,1)} %k.19, bf16[256,2048]{1,0:T(8,128)(2,1)} %v.19), custom_call_target="tpu_custom_call" | custom-call | flops 1024 | bytes 1024 | tf_op jit(solution)/shard_map/pallas_call | solution.py:43
  12.8 3.5 %collective-permute-start.2 = (f32[2,128,128]{2,1,0:T(8,128)S(1)}, f32[2,128,128]{2,1,0:T(8,128)S(1)}, u32[]{:S(2)}, u32[]{:S(2)}) collective-permute-start(f32[2,128,128]{2,1,0:T(8,128)S(1)} %get-tuple-element.240), channel_id=1, source_target_pairs={{0,8},{4,12},{1,9},{5,13},{2,10},{6,14},{3,11},{7,15}} | collective-permute-start | bytes 393224 | tf_op jit(solution)/shard_map/ppermute | solution.py:184
  16.3 1.3 %collective-permute-start.8 = (f32[2,128,128]{2,1,0:T(8,128)S(1)}, f32[2,128,128]{2,1,0:T(8,128)S(1)}, u32[]{:S(2)}, u32[]{:S(2)}) collective-permute-start(f32[2,128,128]{2,1,0:T(8,128)S(1)} %get-tuple-element.242), channel_id=1, source_target_pairs={{0,8},{4,12},{1,9},{5,13},{2,10},{6,14},{3,11},{7,15}} | collective-permute-start | bytes 393224 | tf_op jit(solution)/shard_map/ppermute | solution.py:184
  18.2 1.3 %collective-permute-start.7 = (f32[2,128,128]{2,1,0:T(8,128)S(1)}, f32[2,128,128]{2,1,0:T(8,128)S(1)}, u32[]{:S(2)}, u32[]{:S(2)}) collective-permute-start(f32[2,128,128]{2,1,0:T(8,128)S(1)} %get-tuple-element.244), channel_id=1, source_target_pairs={{0,8},{4,12},{1,9},{5,13},{2,10},{6,14},{3,11},{7,15}} | collective-permute-start | bytes 393224 | tf_op jit(solution)/shard_map/ppermute | solution.py:184
  20.9 1.8 %collective-permute-done.1 = f32[2,128,128]{2,1,0:T(8,128)S(1)} collective-permute-done((f32[2,128,128]{2,1,0:T(8,128)S(1)}, f32[2,128,128]{2,1,0:T(8,128)S(1)}, u32[]{:S(2)}, u32[]{:S(2)}) %collective-permute-start.1) | collective-permute-done | bytes 131104 | tf_op jit(solution)/shard_map/ppermute | solution.py:219
  22.7 3.3 %collective-permute-start.5 = (f32[2,128,128]{2,1,0:T(8,128)S(1)}, f32[2,128,128]{2,1,0:T(8,128)S(1)}, u32[]{:S(2)}, u32[]{:S(2)}) collective-permute-start(f32[2,128,128]{2,1,0:T(8,128)S(1)} %get-tuple-element.246), channel_id=1, source_target_pairs={{0,8},{4,12},{1,9},{5,13},{2,10},{6,14},{3,11},{7,15}} | collective-permute-start | bytes 393224 | tf_op jit(solution)/shard_map/ppermute | solution.py:184
  26.7 0.7 collective-permute-start.11
  29.3 0.8 collective-permute-start.15
  30.1 0.8 collective-permute-start.14
  31.8 2.1 %collective-permute-start.18 = (f32[2,128,128]{2,1,0:T(8,128)S(1)}, f32[2,128,128]{2,1,0:T(8,128)S(1)}, u32[]{:S(2)}, u32[]{:S(2)}) collective-permute-start(f32[2,128,128]{2,1,0:T(8,128)S(1)} %get-tuple-element.219), channel_id=1, source_target_pairs={{0,4},{4,0},{8,12},{12,8},{16,20},{20,16},{24,28},{28,24},{1,5},{5... | collective-permute-start | bytes 393224 | tf_op jit(solution)/shard_map/ppermute | solution.py:239
  34.0 2.1 %collective-permute-start.16 = (f32[2,128,128]{2,1,0:T(8,128)S(1)}, f32[2,128,128]{2,1,0:T(8,128)S(1)}, u32[]{:S(2)}, u32[]{:S(2)}) collective-permute-start(f32[2,128,128]{2,1,0:T(8,128)S(1)} %get-tuple-element.215), channel_id=1, source_target_pairs={{0,4},{4,0},{8,12},{12,8},{16,20},{20,16},{24,28},{28,24},{1,5},{5... | collective-permute-start | bytes 393224 | tf_op jit(solution)/shard_map/ppermute | solution.py:239
  36.1 1.4 %collective-permute-done.19.other = f32[2,128,128]{2,1,0:T(8,128)S(1)} collective-permute-done((f32[2,128,128]{2,1,0:T(8,128)S(1)}, f32[2,128,128]{2,1,0:T(8,128)S(1)}, u32[]{:S(2)}, u32[]{:S(2)}) %collective-permute-start.19) | collective-permute-done | bytes 131104 | tf_op jit(solution)/shard_map/ppermute | solution.py:239
  37.8 1.2 %collective-permute-done.18.other = f32[2,128,128]{2,1,0:T(8,128)S(1)} collective-permute-done((f32[2,128,128]{2,1,0:T(8,128)S(1)}, f32[2,128,128]{2,1,0:T(8,128)S(1)}, u32[]{:S(2)}, u32[]{:S(2)}) %collective-permute-start.18) | collective-permute-done | bytes 131104 | tf_op jit(solution)/shard_map/ppermute | solution.py:239
  39.3 1.1 %collective-permute-done.17.other = f32[2,128,128]{2,1,0:T(8,128)S(1)} collective-permute-done((f32[2,128,128]{2,1,0:T(8,128)S(1)}, f32[2,128,128]{2,1,0:T(8,128)S(1)}, u32[]{:S(2)}, u32[]{:S(2)}) %collective-permute-start.17) | collective-permute-done | bytes 131104 | tf_op jit(solution)/shard_map/ppermute | solution.py:239
  40.7 1.1 %collective-permute-done.16.other = f32[2,128,128]{2,1,0:T(8,128)S(1)} collective-permute-done((f32[2,128,128]{2,1,0:T(8,128)S(1)}, f32[2,128,128]{2,1,0:T(8,128)S(1)}, u32[]{:S(2)}, u32[]{:S(2)}) %collective-permute-start.16) | collective-permute-done | bytes 131104 | tf_op jit(solution)/shard_map/ppermute | solution.py:239
  42.3 1.5 %collective-permute-start.21 = (f32[2,256]{1,0:T(2,128)S(1)}, f32[2,256]{1,0:T(2,128)S(1)}, u32[]{:S(2)}, u32[]{:S(2)}) collective-permute-start(f32[2,256]{1,0:T(2,128)S(1)} %get-tuple-element.135.refs_0_), channel_id=1, source_target_pairs={{0,2},{1,3},{2,0},{3,1},{4,6},{5,7},{6,4},{7,5},{8,10},{9,11},{10,... | collective-permute-start | bytes 6152 | tf_op jit(solution)/shard_map/ppermute | solution.py:320
  44.1 1.1 %collective-permute-done.22.refs_3_ = f32[2,256]{1,0:T(2,128)S(1)} collective-permute-done((f32[2,256]{1,0:T(2,128)S(1)}, f32[2,256]{1,0:T(2,128)S(1)}, u32[]{:S(2)}, u32[]{:S(2)}) %collective-permute-start.22) | collective-permute-done | bytes 2080 | tf_op jit(solution)/shard_map/ppermute | solution.py:320
  46.3 1.2 %collective-permute-start.24 = (f32[2,128,128]{2,1,0:T(8,128)S(1)}, f32[2,128,128]{2,1,0:T(8,128)S(1)}, u32[]{:S(2)}, u32[]{:S(2)}) collective-permute-start(f32[2,128,128]{2,1,0:T(8,128)S(1)} %get-tuple-element.152), channel_id=1, source_target_pairs={{0,4},{4,0},{8,12},{12,8},{16,20},{20,16},{24,28},{28,24},{1,5},{5... | collective-permute-start | bytes 393224 | tf_op jit(solution)/shard_map/ppermute | solution.py:219
  48.0 0.9 collective-permute-start.23
  48.9 1.2 %collective-permute-start.28 = (f32[2,128,128]{2,1,0:T(8,128)S(1)}, f32[2,128,128]{2,1,0:T(8,128)S(1)}, u32[]{:S(2)}, u32[]{:S(2)}) collective-permute-start(f32[2,128,128]{2,1,0:T(8,128)S(1)} %get-tuple-element.158), channel_id=1, source_target_pairs={{0,4},{4,0},{8,12},{12,8},{16,20},{20,16},{24,28},{28,24},{1,5},{5... | collective-permute-start | bytes 393224 | tf_op jit(solution)/shard_map/ppermute | solution.py:219
  50.8 2.0 %collective-permute-done.24 = f32[2,128,128]{2,1,0:T(8,128)S(1)} collective-permute-done((f32[2,128,128]{2,1,0:T(8,128)S(1)}, f32[2,128,128]{2,1,0:T(8,128)S(1)}, u32[]{:S(2)}, u32[]{:S(2)}) %collective-permute-start.24) | collective-permute-done | bytes 131104 | tf_op jit(solution)/shard_map/ppermute | solution.py:219
  53.4 1.2 %collective-permute-start.26 = (f32[2,128,128]{2,1,0:T(8,128)S(1)}, f32[2,128,128]{2,1,0:T(8,128)S(1)}, u32[]{:S(2)}, u32[]{:S(2)}) collective-permute-start(f32[2,128,128]{2,1,0:T(8,128)S(1)} %get-tuple-element.156), channel_id=1, source_target_pairs={{0,4},{4,0},{8,12},{12,8},{16,20},{20,16},{24,28},{28,24},{1,5},{5... | collective-permute-start | bytes 393224 | tf_op jit(solution)/shard_map/ppermute | solution.py:219
  54.7 0.9 collective-permute-done.23
  56.3 2.1 %collective-permute-done.28 = f32[2,128,128]{2,1,0:T(8,128)S(1)} collective-permute-done((f32[2,128,128]{2,1,0:T(8,128)S(1)}, f32[2,128,128]{2,1,0:T(8,128)S(1)}, u32[]{:S(2)}, u32[]{:S(2)}) %collective-permute-start.28) | collective-permute-done | bytes 131104 | tf_op jit(solution)/shard_map/ppermute | solution.py:219
  58.4 0.7 collective-permute-start.32
  59.8 0.8 collective-permute-done.26
  62.7 2.7 %shard_map.86.refs_4_ = bf16[256,2048]{1,0:T(8,128)(2,1)} custom-call(s32[1]{0:T(128)} %bitcast.place, bf16[256,2048]{1,0:T(8,128)(2,1)S(1)} %copy-done.1, bf16[256,2048]{1,0:T(8,128)(2,1)S(1)} %copy-done.2, bf16[256,256]{1,0:T(8,128)(2,1)S(1)} %get-tuple-element.165.refs_0_, bf16[256,256]{1,0:T(8,128)(2,1)S(1)} %get-tuple-element.166.refs_1_.refs_0_, ...), custom_call_target="tpu_custom_call" | custom-call | flops 1024 | bytes 1024 | tf_op jit(solution)/shard_map/pallas_call | solution.py:43
  65.5 1.3 %collective-permute-start.34 = (f32[2,128,128]{2,1,0:T(8,128)S(1)}, f32[2,128,128]{2,1,0:T(8,128)S(1)}, u32[]{:S(2)}, u32[]{:S(2)}) collective-permute-start(f32[2,128,128]{2,1,0:T(8,128)S(1)} %get-tuple-element.213), channel_id=1, source_target_pairs={{12,4},{8,0},{13,5},{9,1},{14,6},{10,2},{15,7},{11,3}} | collective-permute-start | bytes 393224 | tf_op jit(solution)/shard_map/ppermute | solution.py:184
  67.5 1.3 %collective-permute-start.38 = (f32[2,128,128]{2,1,0:T(8,128)S(1)}, f32[2,128,128]{2,1,0:T(8,128)S(1)}, u32[]{:S(2)}, u32[]{:S(2)}) collective-permute-start(f32[2,128,128]{2,1,0:T(8,128)S(1)} %get-tuple-element.211), channel_id=1, source_target_pairs={{12,4},{8,0},{13,5},{9,1},{14,6},{10,2},{15,7},{11,3}} | collective-permute-start | bytes 393224 | tf_op jit(solution)/shard_map/ppermute | solution.py:184
  68.9 1.3 %collective-permute-start.37 = (f32[2,128,128]{2,1,0:T(8,128)S(1)}, f32[2,128,128]{2,1,0:T(8,128)S(1)}, u32[]{:S(2)}, u32[]{:S(2)}) collective-permute-start(f32[2,128,128]{2,1,0:T(8,128)S(1)} %get-tuple-element.209), channel_id=1, source_target_pairs={{12,4},{8,0},{13,5},{9,1},{14,6},{10,2},{15,7},{11,3}} | collective-permute-start | bytes 393224 | tf_op jit(solution)/shard_map/ppermute | solution.py:184
  70.2 1.6 %shard_map.87.refs_4_ = bf16[256,2048]{1,0:T(8,128)(2,1)} custom-call(s32[1]{0:T(128)} %bitcast.place, bf16[256,2048]{1,0:T(8,128)(2,1)S(1)} %copy-done.1, bf16[256,2048]{1,0:T(8,128)(2,1)S(1)} %copy-done.2, bf16[256,256]{1,0:T(8,128)(2,1)S(1)} %get-tuple-element.176.refs_0_, ...), custom_call_target="tpu_custom_call", output_to_operand_aliasing={{}: (7, {})} | custom-call | flops 1024 | bytes 1024 | tf_op jit(solution)/shard_map/pallas_call | solution.py:43
  71.8 5.3 %collective-permute-done.34 = f32[2,128,128]{2,1,0:T(8,128)S(1)} collective-permute-done((f32[2,128,128]{2,1,0:T(8,128)S(1)}, f32[2,128,128]{2,1,0:T(8,128)S(1)}, u32[]{:S(2)}, u32[]{:S(2)}) %collective-permute-start.34) | collective-permute-done | bytes 131104 | tf_op jit(solution)/shard_map/ppermute | solution.py:184
  77.1 1.1 %collective-permute-start.41 = (f32[2,128,128]{2,1,0:T(8,128)S(1)}, f32[2,128,128]{2,1,0:T(8,128)S(1)}, u32[]{:S(2)}, u32[]{:S(2)}) collective-permute-start(f32[2,128,128]{2,1,0:T(8,128)S(1)} %get-tuple-element.207), channel_id=1, source_target_pairs={{0,4},{4,0},{8,12},{12,8},{16,20},{20,16},{24,28},{28,24},{1,5},{5... | collective-permute-start | bytes 393224 | tf_op jit(solution)/shard_map/ppermute | solution.py:239
  78.3 1.5 %collective-permute-start.36 = (f32[2,128,128]{2,1,0:T(8,128)S(1)}, f32[2,128,128]{2,1,0:T(8,128)S(1)}, u32[]{:S(2)}, u32[]{:S(2)}) collective-permute-start(f32[2,128,128]{2,1,0:T(8,128)S(1)} %get-tuple-element.205), channel_id=1, source_target_pairs={{12,4},{8,0},{13,5},{9,1},{14,6},{10,2},{15,7},{11,3}} | collective-permute-start | bytes 393224 | tf_op jit(solution)/shard_map/ppermute | solution.py:184
  79.7 1.6 %shard_map.88 = bf16[256,2048]{1,0:T(8,128)(2,1)} custom-call(s32[1]{0:T(128)} %bitcast.place, bf16[256,2048]{1,0:T(8,128)(2,1)S(1)} %copy-done.1, bf16[256,2048]{1,0:T(8,128)(2,1)S(1)} %copy-done.2, bf16[256,256]{1,0:T(8,128)(2,1)S(1)} %get-tuple-element.140.refs_0_, ...), custom_call_target="tpu_custom_call", output_to_operand_aliasing={{}: (7, {})} | custom-call | flops 1024 | bytes 1024 | tf_op jit(solution)/shard_map/pallas_call | solution.py:43
  81.4 1.1 %collective-permute-start.42 = (f32[2,128,128]{2,1,0:T(8,128)S(1)}, f32[2,128,128]{2,1,0:T(8,128)S(1)}, u32[]{:S(2)}, u32[]{:S(2)}) collective-permute-start(f32[2,128,128]{2,1,0:T(8,128)S(1)} %get-tuple-element.203), channel_id=1, source_target_pairs={{0,4},{4,0},{8,12},{12,8},{16,20},{20,16},{24,28},{28,24},{1,5},{5... | collective-permute-start | bytes 393224 | tf_op jit(solution)/shard_map/ppermute | solution.py:239
  82.4 1.7 %shard_map.89 = (bf16[256,2048]{1,0:T(8,128)(2,1)}, bf16[256,2048]{1,0:T(8,128)(2,1)}) custom-call(s32[1]{0:T(128)} %bitcast.place, bf16[256,2048]{1,0:T(8,128)(2,1)S(1)} %copy-done, bf16[256,2048]{1,0:T(8,128)(2,1)S(1)} %copy-done.1, bf16[256,2048]{1,0:T(8,128)(2,1)S(1)} %copy-done.2, bf16[256,256]{1,0:T(8,128)(2,1)S(1)} %get-tuple-element.165.refs_0_, ...), custom_call_target="tpu_custom_call" | custom-call | flops 1024 | bytes 1024 | tf_op jit(solution)/shard_map/pallas_call | solution.py:43
  84.1 1.1 %collective-permute-start.40 = (f32[2,128,128]{2,1,0:T(8,128)S(1)}, f32[2,128,128]{2,1,0:T(8,128)S(1)}, u32[]{:S(2)}, u32[]{:S(2)}) collective-permute-start(f32[2,128,128]{2,1,0:T(8,128)S(1)} %get-tuple-element.201), channel_id=1, source_target_pairs={{0,4},{4,0},{8,12},{12,8},{16,20},{20,16},{24,28},{28,24},{1,5},{5... | collective-permute-start | bytes 393224 | tf_op jit(solution)/shard_map/ppermute | solution.py:239
  85.2 1.2 %shard_map.90 = (bf16[256,2048]{1,0:T(8,128)(2,1)}, bf16[256,2048]{1,0:T(8,128)(2,1)}) custom-call(s32[1]{0:T(128)} %bitcast.place, bf16[256,2048]{1,0:T(8,128)(2,1)S(1)} %copy-done, bf16[256,2048]{1,0:T(8,128)(2,1)S(1)} %copy-done.1, bf16[256,2048]{1,0:T(8,128)(2,1)S(1)} %copy-done.2, ...), custom_call_target="tpu_custom_call", output_to_operand_aliasing={{0}: (7, {}), {1}: (8, {})} | custom-call | flops 1024 | bytes 1024 | tf_op jit(solution)/shard_map/pallas_call | solution.py:43
  86.5 1.1 %collective-permute-start.39 = (f32[2,128,128]{2,1,0:T(8,128)S(1)}, f32[2,128,128]{2,1,0:T(8,128)S(1)}, u32[]{:S(2)}, u32[]{:S(2)}) collective-permute-start(f32[2,128,128]{2,1,0:T(8,128)S(1)} %get-tuple-element.199), channel_id=1, source_target_pairs={{0,4},{4,0},{8,12},{12,8},{16,20},{20,16},{24,28},{28,24},{1,5},{5... | collective-permute-start | bytes 393224 | tf_op jit(solution)/shard_map/ppermute | solution.py:239
  87.6 1.2 %shard_map.91 = (bf16[256,2048]{1,0:T(8,128)(2,1)}, bf16[256,2048]{1,0:T(8,128)(2,1)}) custom-call(s32[1]{0:T(128)} %bitcast.place, bf16[256,2048]{1,0:T(8,128)(2,1)S(1)} %copy-done, bf16[256,2048]{1,0:T(8,128)(2,1)S(1)} %copy-done.1, bf16[256,2048]{1,0:T(8,128)(2,1)S(1)} %copy-done.2, ...), custom_call_target="tpu_custom_call", output_to_operand_aliasing={{0}: (7, {}), {1}: (8, {})} | custom-call | flops 1024 | bytes 1024 | tf_op jit(solution)/shard_map/pallas_call | solution.py:43
  88.8 1.7 %shard_map.92 = (bf16[256,2048]{1,0:T(8,128)(2,1)}, bf16[256,2048]{1,0:T(8,128)(2,1)}) custom-call(s32[1]{0:T(128)} %bitcast.place, bf16[256,2048]{1,0:T(8,128)(2,1)S(1)} %copy-done, bf16[256,2048]{1,0:T(8,128)(2,1)S(1)} %copy-done.1, bf16[256,2048]{1,0:T(8,128)(2,1)S(1)} %copy-done.2, ...), custom_call_target="tpu_custom_call", output_to_operand_aliasing={{0}: (8, {}), {1}: (9, {})} | custom-call | flops 1024 | bytes 1024 | tf_op jit(solution)/shard_map/pallas_call | solution.py:43
  90.5 1.2 %shard_map.93 = (bf16[256,2048]{1,0:T(8,128)(2,1)}, bf16[256,2048]{1,0:T(8,128)(2,1)}) custom-call(s32[1]{0:T(128)} %bitcast.place, bf16[256,2048]{1,0:T(8,128)(2,1)S(1)} %copy-done, bf16[256,2048]{1,0:T(8,128)(2,1)S(1)} %copy-done.1, bf16[256,2048]{1,0:T(8,128)(2,1)S(1)} %copy-done.2, ...), custom_call_target="tpu_custom_call", output_to_operand_aliasing={{0}: (6, {}), {1}: (7, {})} | custom-call | flops 1024 | bytes 1024 | tf_op jit(solution)/shard_map/pallas_call | solution.py:43
  91.7 1.2 %shard_map.94 = (bf16[256,2048]{1,0:T(8,128)(2,1)}, bf16[256,2048]{1,0:T(8,128)(2,1)}) custom-call(s32[1]{0:T(128)} %bitcast.place, bf16[256,2048]{1,0:T(8,128)(2,1)S(1)} %copy-done, bf16[256,2048]{1,0:T(8,128)(2,1)S(1)} %copy-done.1, bf16[256,2048]{1,0:T(8,128)(2,1)S(1)} %copy-done.2, ...), custom_call_target="tpu_custom_call", output_to_operand_aliasing={{0}: (6, {}), {1}: (7, {})} | custom-call | flops 1024 | bytes 1024 | tf_op jit(solution)/shard_map/pallas_call | solution.py:43
  (100 shorter events, 14.6 us)
Async XLA Ops:
  2.0 10.8 %collective-permute-start = (f32[2,128,128]{2,1,0:T(8,128)S(1)}, f32[2,128,128]{2,1,0:T(8,128)S(1)}, u32[]{:S(2)}, u32[]{:S(2)}) collective-permute-start(f32[2,128,128]{2,1,0:T(8,128)S(1)} %get-tuple-element.106), channel_id=1, source_target_pairs={{0,4},{4,0},{8,12},{12,8},{16,20},{20,16},{24,28},{28,24},{1,5},{5... | collective-permute-start | bytes 393224 | tf_op jit(solution)/shard_map/ppermute | solution.py:219
  5.0 11.3 %collective-permute-start.4 = (f32[2,128,128]{2,1,0:T(8,128)S(1)}, f32[2,128,128]{2,1,0:T(8,128)S(1)}, u32[]{:S(2)}, u32[]{:S(2)}) collective-permute-start(f32[2,128,128]{2,1,0:T(8,128)S(1)} %get-tuple-element.112), channel_id=1, source_target_pairs={{0,4},{4,0},{8,12},{12,8},{16,20},{20,16},{24,28},{28,24},{1,5},{5... | collective-permute-start | bytes 393224 | tf_op jit(solution)/shard_map/ppermute | solution.py:219
  6.4 11.3 %collective-permute-start.3 = (f32[2,128,128]{2,1,0:T(8,128)S(1)}, f32[2,128,128]{2,1,0:T(8,128)S(1)}, u32[]{:S(2)}, u32[]{:S(2)}) collective-permute-start(f32[2,128,128]{2,1,0:T(8,128)S(1)} %get-tuple-element.110), channel_id=1, source_target_pairs={{0,4},{4,0},{8,12},{12,8},{16,20},{20,16},{24,28},{28,24},{1,5},{5... | collective-permute-start | bytes 393224 | tf_op jit(solution)/shard_map/ppermute | solution.py:219
  12.8 7.4 %collective-permute-start.2 = (f32[2,128,128]{2,1,0:T(8,128)S(1)}, f32[2,128,128]{2,1,0:T(8,128)S(1)}, u32[]{:S(2)}, u32[]{:S(2)}) collective-permute-start(f32[2,128,128]{2,1,0:T(8,128)S(1)} %get-tuple-element.240), channel_id=1, source_target_pairs={{0,8},{4,12},{1,9},{5,13},{2,10},{6,14},{3,11},{7,15}} | collective-permute-start | bytes 393224 | tf_op jit(solution)/shard_map/ppermute | solution.py:184
  16.3 9.7 %collective-permute-start.8 = (f32[2,128,128]{2,1,0:T(8,128)S(1)}, f32[2,128,128]{2,1,0:T(8,128)S(1)}, u32[]{:S(2)}, u32[]{:S(2)}) collective-permute-start(f32[2,128,128]{2,1,0:T(8,128)S(1)} %get-tuple-element.242), channel_id=1, source_target_pairs={{0,8},{4,12},{1,9},{5,13},{2,10},{6,14},{3,11},{7,15}} | collective-permute-start | bytes 393224 | tf_op jit(solution)/shard_map/ppermute | solution.py:184
  17.6 5.0 %collective-permute-start.1 = (f32[2,128,128]{2,1,0:T(8,128)S(1)}, f32[2,128,128]{2,1,0:T(8,128)S(1)}, u32[]{:S(2)}, u32[]{:S(2)}) collective-permute-start(f32[2,128,128]{2,1,0:T(8,128)S(1)} %get-tuple-element.108), channel_id=1, source_target_pairs={{0,4},{4,0},{8,12},{12,8},{16,20},{20,16},{24,28},{28,24},{1,5},{5... | collective-permute-start | bytes 393224 | tf_op jit(solution)/shard_map/ppermute | solution.py:219
  18.2 8.5 %collective-permute-start.7 = (f32[2,128,128]{2,1,0:T(8,128)S(1)}, f32[2,128,128]{2,1,0:T(8,128)S(1)}, u32[]{:S(2)}, u32[]{:S(2)}) collective-permute-start(f32[2,128,128]{2,1,0:T(8,128)S(1)} %get-tuple-element.244), channel_id=1, source_target_pairs={{0,8},{4,12},{1,9},{5,13},{2,10},{6,14},{3,11},{7,15}} | collective-permute-start | bytes 393224 | tf_op jit(solution)/shard_map/ppermute | solution.py:184
  20.2 7.2 %collective-permute-start.6 = (f32[2,128,128]{2,1,0:T(8,128)S(1)}, f32[2,128,128]{2,1,0:T(8,128)S(1)}, u32[]{:S(2)}, u32[]{:S(2)}) collective-permute-start(f32[2,128,128]{2,1,0:T(8,128)S(1)} %add.152), channel_id=1, source_target_pairs={{8,16},{12,20},{9,17},{13,21},{10,18},{14,22},{11,19},{15,23}} | collective-permute-start | bytes 393224 | tf_op jit(solution)/shard_map/ppermute | solution.py:184
  22.7 5.8 %collective-permute-start.5 = (f32[2,128,128]{2,1,0:T(8,128)S(1)}, f32[2,128,128]{2,1,0:T(8,128)S(1)}, u32[]{:S(2)}, u32[]{:S(2)}) collective-permute-start(f32[2,128,128]{2,1,0:T(8,128)S(1)} %get-tuple-element.246), channel_id=1, source_target_pairs={{0,8},{4,12},{1,9},{5,13},{2,10},{6,14},{3,11},{7,15}} | collective-permute-start | bytes 393224 | tf_op jit(solution)/shard_map/ppermute | solution.py:184
  26.0 3.2 %collective-permute-start.12 = (f32[2,128,128]{2,1,0:T(8,128)S(1)}, f32[2,128,128]{2,1,0:T(8,128)S(1)}, u32[]{:S(2)}, u32[]{:S(2)}) collective-permute-start(f32[2,128,128]{2,1,0:T(8,128)S(1)} %add.154), channel_id=1, source_target_pairs={{8,16},{12,20},{9,17},{13,21},{10,18},{14,22},{11,19},{15,23}} | collective-permute-start | bytes 393224 | tf_op jit(solution)/shard_map/ppermute | solution.py:184
  26.7 3.4 %collective-permute-start.11 = (f32[2,128,128]{2,1,0:T(8,128)S(1)}, f32[2,128,128]{2,1,0:T(8,128)S(1)}, u32[]{:S(2)}, u32[]{:S(2)}) collective-permute-start(f32[2,128,128]{2,1,0:T(8,128)S(1)} %add.155), channel_id=1, source_target_pairs={{8,16},{12,20},{9,17},{13,21},{10,18},{14,22},{11,19},{15,23}} | collective-permute-start | bytes 393224 | tf_op jit(solution)/shard_map/ppermute | solution.py:184
  27.4 3.5 %collective-permute-start.10 = (f32[2,128,128]{2,1,0:T(8,128)S(1)}, f32[2,128,128]{2,1,0:T(8,128)S(1)}, u32[]{:S(2)}, u32[]{:S(2)}) collective-permute-start(f32[2,128,128]{2,1,0:T(8,128)S(1)} %get-tuple-element.229), channel_id=1, source_target_pairs={{16,24},{20,28},{17,25},{21,29},{18,26},{22,30},{19,27},{23,31}} | collective-permute-start | bytes 393224 | tf_op jit(solution)/shard_map/ppermute | solution.py:184
  28.5 2.6 %collective-permute-start.9 = (f32[2,128,128]{2,1,0:T(8,128)S(1)}, f32[2,128,128]{2,1,0:T(8,128)S(1)}, u32[]{:S(2)}, u32[]{:S(2)}) collective-permute-start(f32[2,128,128]{2,1,0:T(8,128)S(1)} %add.158), channel_id=1, source_target_pairs={{8,16},{12,20},{9,17},{13,21},{10,18},{14,22},{11,19},{15,23}} | collective-permute-start | bytes 393224 | tf_op jit(solution)/shard_map/ppermute | solution.py:184
  29.2 8.3 %copy-start.3 = (bf16[256,2048]{1,0:T(8,128)(2,1)S(1)}, bf16[256,2048]{1,0:T(8,128)(2,1)}, u32[]{:S(2)}) copy-start(bf16[256,2048]{1,0:T(8,128)(2,1)} %refs_7_.3) | copy-start | bytes 3145732
  29.2 6.9 %copy-start.4 = (bf16[2048]{0:T(1024)(128)(2,1)S(1)}, bf16[2048]{0:T(1024)(128)(2,1)}, u32[]{:S(2)}) copy-start(bf16[2048]{0:T(1024)(128)(2,1)} %param.9) | copy-start | bytes 12292
  29.2 8.2 %copy-start = (bf16[256,2048]{1,0:T(8,128)(2,1)S(1)}, bf16[256,2048]{1,0:T(8,128)(2,1)}, u32[]{:S(2)}) copy-start(bf16[256,2048]{1,0:T(8,128)(2,1)} %q.13) | copy-start | bytes 3145732
  29.2 8.2 %copy-start.1 = (bf16[256,2048]{1,0:T(8,128)(2,1)S(1)}, bf16[256,2048]{1,0:T(8,128)(2,1)}, u32[]{:S(2)}) copy-start(bf16[256,2048]{1,0:T(8,128)(2,1)} %k.19) | copy-start | bytes 3145732
  29.2 8.2 %copy-start.2 = (bf16[256,2048]{1,0:T(8,128)(2,1)S(1)}, bf16[256,2048]{1,0:T(8,128)(2,1)}, u32[]{:S(2)}) copy-start(bf16[256,2048]{1,0:T(8,128)(2,1)} %v.19) | copy-start | bytes 3145732
  29.3 2.5 %collective-permute-start.15 = (f32[2,128,128]{2,1,0:T(8,128)S(1)}, f32[2,128,128]{2,1,0:T(8,128)S(1)}, u32[]{:S(2)}, u32[]{:S(2)}) collective-permute-start(f32[2,128,128]{2,1,0:T(8,128)S(1)} %get-tuple-element.227), channel_id=1, source_target_pairs={{16,24},{20,28},{17,25},{21,29},{18,26},{22,30},{19,27},{23,31}} | collective-permute-start | bytes 393224 | tf_op jit(solution)/shard_map/ppermute | solution.py:184
  30.1 3.8 %collective-permute-start.14 = (f32[2,128,128]{2,1,0:T(8,128)S(1)}, f32[2,128,128]{2,1,0:T(8,128)S(1)}, u32[]{:S(2)}, u32[]{:S(2)}) collective-permute-start(f32[2,128,128]{2,1,0:T(8,128)S(1)} %get-tuple-element.225), channel_id=1, source_target_pairs={{16,24},{20,28},{17,25},{21,29},{18,26},{22,30},{19,27},{23,31}} | collective-permute-start | bytes 393224 | tf_op jit(solution)/shard_map/ppermute | solution.py:184
  31.0 6.5 %collective-permute-start.19 = (f32[2,128,128]{2,1,0:T(8,128)S(1)}, f32[2,128,128]{2,1,0:T(8,128)S(1)}, u32[]{:S(2)}, u32[]{:S(2)}) collective-permute-start(f32[2,128,128]{2,1,0:T(8,128)S(1)} %get-tuple-element.223), channel_id=1, source_target_pairs={{0,4},{4,0},{8,12},{12,8},{16,20},{20,16},{24,28},{28,24},{1,5},{5... | collective-permute-start | bytes 393224 | tf_op jit(solution)/shard_map/ppermute | solution.py:239
  31.1 2.9 %collective-permute-start.13 = (f32[2,128,128]{2,1,0:T(8,128)S(1)}, f32[2,128,128]{2,1,0:T(8,128)S(1)}, u32[]{:S(2)}, u32[]{:S(2)}) collective-permute-start(f32[2,128,128]{2,1,0:T(8,128)S(1)} %get-tuple-element.221), channel_id=1, source_target_pairs={{16,24},{20,28},{17,25},{21,29},{18,26},{22,30},{19,27},{23,31}} | collective-permute-start | bytes 393224 | tf_op jit(solution)/shard_map/ppermute | solution.py:184
  31.8 7.2 %collective-permute-start.18 = (f32[2,128,128]{2,1,0:T(8,128)S(1)}, f32[2,128,128]{2,1,0:T(8,128)S(1)}, u32[]{:S(2)}, u32[]{:S(2)}) collective-permute-start(f32[2,128,128]{2,1,0:T(8,128)S(1)} %get-tuple-element.219), channel_id=1, source_target_pairs={{0,4},{4,0},{8,12},{12,8},{16,20},{20,16},{24,28},{28,24},{1,5},{5... | collective-permute-start | bytes 393224 | tf_op jit(solution)/shard_map/ppermute | solution.py:239
  33.9 6.5 %collective-permute-start.17 = (f32[2,128,128]{2,1,0:T(8,128)S(1)}, f32[2,128,128]{2,1,0:T(8,128)S(1)}, u32[]{:S(2)}, u32[]{:S(2)}) collective-permute-start(f32[2,128,128]{2,1,0:T(8,128)S(1)} %get-tuple-element.217), channel_id=1, source_target_pairs={{0,4},{4,0},{8,12},{12,8},{16,20},{20,16},{24,28},{28,24},{1,5},{5... | collective-permute-start | bytes 393224 | tf_op jit(solution)/shard_map/ppermute | solution.py:239
  34.0 7.7 %collective-permute-start.16 = (f32[2,128,128]{2,1,0:T(8,128)S(1)}, f32[2,128,128]{2,1,0:T(8,128)S(1)}, u32[]{:S(2)}, u32[]{:S(2)}) collective-permute-start(f32[2,128,128]{2,1,0:T(8,128)S(1)} %get-tuple-element.215), channel_id=1, source_target_pairs={{0,4},{4,0},{8,12},{12,8},{16,20},{20,16},{24,28},{28,24},{1,5},{5... | collective-permute-start | bytes 393224 | tf_op jit(solution)/shard_map/ppermute | solution.py:239
  42.2 3.1 %collective-permute-start.22 = (f32[2,256]{1,0:T(2,128)S(1)}, f32[2,256]{1,0:T(2,128)S(1)}, u32[]{:S(2)}, u32[]{:S(2)}) collective-permute-start(f32[2,256]{1,0:T(2,128)S(1)} %get-tuple-element.135.refs_0_), channel_id=1, source_target_pairs={{0,3},{1,2},{2,1},{3,0},{4,7},{5,6},{6,5},{7,4},{8,11},{9,10},{10,... | collective-permute-start | bytes 6152 | tf_op jit(solution)/shard_map/ppermute | solution.py:320
  42.3 3.7 %collective-permute-start.21 = (f32[2,256]{1,0:T(2,128)S(1)}, f32[2,256]{1,0:T(2,128)S(1)}, u32[]{:S(2)}, u32[]{:S(2)}) collective-permute-start(f32[2,256]{1,0:T(2,128)S(1)} %get-tuple-element.135.refs_0_), channel_id=1, source_target_pairs={{0,2},{1,3},{2,0},{3,1},{4,6},{5,7},{6,4},{7,5},{8,10},{9,11},{10,... | collective-permute-start | bytes 6152 | tf_op jit(solution)/shard_map/ppermute | solution.py:320
  43.8 2.1 %collective-permute-start.20 = (f32[2,256]{1,0:T(2,128)S(1)}, f32[2,256]{1,0:T(2,128)S(1)}, u32[]{:S(2)}, u32[]{:S(2)}) collective-permute-start(f32[2,256]{1,0:T(2,128)S(1)} %get-tuple-element.135.refs_0_), channel_id=1, source_target_pairs={{0,1},{1,0},{2,3},{3,2},{4,5},{5,4},{6,7},{7,6},{8,9},{9,8},{10,11... | collective-permute-start | bytes 6152 | tf_op jit(solution)/shard_map/ppermute | solution.py:320
  46.3 6.4 %collective-permute-start.24 = (f32[2,128,128]{2,1,0:T(8,128)S(1)}, f32[2,128,128]{2,1,0:T(8,128)S(1)}, u32[]{:S(2)}, u32[]{:S(2)}) collective-permute-start(f32[2,128,128]{2,1,0:T(8,128)S(1)} %get-tuple-element.152), channel_id=1, source_target_pairs={{0,4},{4,0},{8,12},{12,8},{16,20},{20,16},{24,28},{28,24},{1,5},{5... | collective-permute-start | bytes 393224 | tf_op jit(solution)/shard_map/ppermute | solution.py:219
  48.0 7.5 %collective-permute-start.23 = (f32[2,128,128]{2,1,0:T(8,128)S(1)}, f32[2,128,128]{2,1,0:T(8,128)S(1)}, u32[]{:S(2)}, u32[]{:S(2)}) collective-permute-start(f32[2,128,128]{2,1,0:T(8,128)S(1)} %get-tuple-element.150), channel_id=1, source_target_pairs={{0,4},{4,0},{8,12},{12,8},{16,20},{20,16},{24,28},{28,24},{1,5},{5... | collective-permute-start | bytes 393224 | tf_op jit(solution)/shard_map/ppermute | solution.py:219
  48.9 9.4 %collective-permute-start.28 = (f32[2,128,128]{2,1,0:T(8,128)S(1)}, f32[2,128,128]{2,1,0:T(8,128)S(1)}, u32[]{:S(2)}, u32[]{:S(2)}) collective-permute-start(f32[2,128,128]{2,1,0:T(8,128)S(1)} %get-tuple-element.158), channel_id=1, source_target_pairs={{0,4},{4,0},{8,12},{12,8},{16,20},{20,16},{24,28},{28,24},{1,5},{5... | collective-permute-start | bytes 393224 | tf_op jit(solution)/shard_map/ppermute | solution.py:219
  52.8 6.3 %collective-permute-start.27 = (f32[2,128,128]{2,1,0:T(8,128)S(1)}, f32[2,128,128]{2,1,0:T(8,128)S(1)}, u32[]{:S(2)}, u32[]{:S(2)}) collective-permute-start(f32[2,128,128]{2,1,0:T(8,128)S(1)} %get-tuple-element.238), channel_id=1, source_target_pairs={{28,20},{24,16},{29,21},{25,17},{30,22},{26,18},{31,23},{27,19}} | collective-permute-start | bytes 393224 | tf_op jit(solution)/shard_map/ppermute | solution.py:184
  53.4 7.2 %collective-permute-start.26 = (f32[2,128,128]{2,1,0:T(8,128)S(1)}, f32[2,128,128]{2,1,0:T(8,128)S(1)}, u32[]{:S(2)}, u32[]{:S(2)}) collective-permute-start(f32[2,128,128]{2,1,0:T(8,128)S(1)} %get-tuple-element.156), channel_id=1, source_target_pairs={{0,4},{4,0},{8,12},{12,8},{16,20},{20,16},{24,28},{28,24},{1,5},{5... | collective-permute-start | bytes 393224 | tf_op jit(solution)/shard_map/ppermute | solution.py:219
  55.6 5.7 %collective-permute-start.25 = (f32[2,128,128]{2,1,0:T(8,128)S(1)}, f32[2,128,128]{2,1,0:T(8,128)S(1)}, u32[]{:S(2)}, u32[]{:S(2)}) collective-permute-start(f32[2,128,128]{2,1,0:T(8,128)S(1)} %get-tuple-element.236), channel_id=1, source_target_pairs={{28,20},{24,16},{29,21},{25,17},{30,22},{26,18},{31,23},{27,19}} | collective-permute-start | bytes 393224 | tf_op jit(solution)/shard_map/ppermute | solution.py:184
  58.4 3.6 %collective-permute-start.32 = (f32[2,128,128]{2,1,0:T(8,128)S(1)}, f32[2,128,128]{2,1,0:T(8,128)S(1)}, u32[]{:S(2)}, u32[]{:S(2)}) collective-permute-start(f32[2,128,128]{2,1,0:T(8,128)S(1)} %get-tuple-element.234), channel_id=1, source_target_pairs={{28,20},{24,16},{29,21},{25,17},{30,22},{26,18},{31,23},{27,19}} | collective-permute-start | bytes 393224 | tf_op jit(solution)/shard_map/ppermute | solution.py:184
  59.1 6.3 %collective-permute-start.31 = (f32[2,128,128]{2,1,0:T(8,128)S(1)}, f32[2,128,128]{2,1,0:T(8,128)S(1)}, u32[]{:S(2)}, u32[]{:S(2)}) collective-permute-start(f32[2,128,128]{2,1,0:T(8,128)S(1)} %add.176), channel_id=1, source_target_pairs={{20,12},{16,8},{21,13},{17,9},{22,14},{18,10},{23,15},{19,11}} | collective-permute-start | bytes 393224 | tf_op jit(solution)/shard_map/ppermute | solution.py:184
  60.6 6.1 %collective-permute-start.30 = (f32[2,128,128]{2,1,0:T(8,128)S(1)}, f32[2,128,128]{2,1,0:T(8,128)S(1)}, u32[]{:S(2)}, u32[]{:S(2)}) collective-permute-start(f32[2,128,128]{2,1,0:T(8,128)S(1)} %get-tuple-element.232), channel_id=1, source_target_pairs={{28,20},{24,16},{29,21},{25,17},{30,22},{26,18},{31,23},{27,19}} | collective-permute-start | bytes 393224 | tf_op jit(solution)/shard_map/ppermute | solution.py:184
  61.3 6.1 %collective-permute-start.29 = (f32[2,128,128]{2,1,0:T(8,128)S(1)}, f32[2,128,128]{2,1,0:T(8,128)S(1)}, u32[]{:S(2)}, u32[]{:S(2)}) collective-permute-start(f32[2,128,128]{2,1,0:T(8,128)S(1)} %add.178), channel_id=1, source_target_pairs={{20,12},{16,8},{21,13},{17,9},{22,14},{18,10},{23,15},{19,11}} | collective-permute-start | bytes 393224 | tf_op jit(solution)/shard_map/ppermute | solution.py:184
  62.1 6.8 %collective-permute-start.35 = (f32[2,128,128]{2,1,0:T(8,128)S(1)}, f32[2,128,128]{2,1,0:T(8,128)S(1)}, u32[]{:S(2)}, u32[]{:S(2)}) collective-permute-start(f32[2,128,128]{2,1,0:T(8,128)S(1)} %add.179), channel_id=1, source_target_pairs={{20,12},{16,8},{21,13},{17,9},{22,14},{18,10},{23,15},{19,11}} | collective-permute-start | bytes 393224 | tf_op jit(solution)/shard_map/ppermute | solution.py:184
  65.5 11.6 %collective-permute-start.34 = (f32[2,128,128]{2,1,0:T(8,128)S(1)}, f32[2,128,128]{2,1,0:T(8,128)S(1)}, u32[]{:S(2)}, u32[]{:S(2)}) collective-permute-start(f32[2,128,128]{2,1,0:T(8,128)S(1)} %get-tuple-element.213), channel_id=1, source_target_pairs={{12,4},{8,0},{13,5},{9,1},{14,6},{10,2},{15,7},{11,3}} | collective-permute-start | bytes 393224 | tf_op jit(solution)/shard_map/ppermute | solution.py:184
  66.8 11.4 %collective-permute-start.33 = (f32[2,128,128]{2,1,0:T(8,128)S(1)}, f32[2,128,128]{2,1,0:T(8,128)S(1)}, u32[]{:S(2)}, u32[]{:S(2)}) collective-permute-start(f32[2,128,128]{2,1,0:T(8,128)S(1)} %add.182), channel_id=1, source_target_pairs={{20,12},{16,8},{21,13},{17,9},{22,14},{18,10},{23,15},{19,11}} | collective-permute-start | bytes 393224 | tf_op jit(solution)/shard_map/ppermute | solution.py:184
  67.5 13.8 %collective-permute-start.38 = (f32[2,128,128]{2,1,0:T(8,128)S(1)}, f32[2,128,128]{2,1,0:T(8,128)S(1)}, u32[]{:S(2)}, u32[]{:S(2)}) collective-permute-start(f32[2,128,128]{2,1,0:T(8,128)S(1)} %get-tuple-element.211), channel_id=1, source_target_pairs={{12,4},{8,0},{13,5},{9,1},{14,6},{10,2},{15,7},{11,3}} | collective-permute-start | bytes 393224 | tf_op jit(solution)/shard_map/ppermute | solution.py:184
  68.9 15.2 %collective-permute-start.37 = (f32[2,128,128]{2,1,0:T(8,128)S(1)}, f32[2,128,128]{2,1,0:T(8,128)S(1)}, u32[]{:S(2)}, u32[]{:S(2)}) collective-permute-start(f32[2,128,128]{2,1,0:T(8,128)S(1)} %get-tuple-element.209), channel_id=1, source_target_pairs={{12,4},{8,0},{13,5},{9,1},{14,6},{10,2},{15,7},{11,3}} | collective-permute-start | bytes 393224 | tf_op jit(solution)/shard_map/ppermute | solution.py:184
  77.1 11.7 %collective-permute-start.41 = (f32[2,128,128]{2,1,0:T(8,128)S(1)}, f32[2,128,128]{2,1,0:T(8,128)S(1)}, u32[]{:S(2)}, u32[]{:S(2)}) collective-permute-start(f32[2,128,128]{2,1,0:T(8,128)S(1)} %get-tuple-element.207), channel_id=1, source_target_pairs={{0,4},{4,0},{8,12},{12,8},{16,20},{20,16},{24,28},{28,24},{1,5},{5... | collective-permute-start | bytes 393224 | tf_op jit(solution)/shard_map/ppermute | solution.py:239
  78.3 8.2 %collective-permute-start.36 = (f32[2,128,128]{2,1,0:T(8,128)S(1)}, f32[2,128,128]{2,1,0:T(8,128)S(1)}, u32[]{:S(2)}, u32[]{:S(2)}) collective-permute-start(f32[2,128,128]{2,1,0:T(8,128)S(1)} %get-tuple-element.205), channel_id=1, source_target_pairs={{12,4},{8,0},{13,5},{9,1},{14,6},{10,2},{15,7},{11,3}} | collective-permute-start | bytes 393224 | tf_op jit(solution)/shard_map/ppermute | solution.py:184
  81.4 7.4 %collective-permute-start.42 = (f32[2,128,128]{2,1,0:T(8,128)S(1)}, f32[2,128,128]{2,1,0:T(8,128)S(1)}, u32[]{:S(2)}, u32[]{:S(2)}) collective-permute-start(f32[2,128,128]{2,1,0:T(8,128)S(1)} %get-tuple-element.203), channel_id=1, source_target_pairs={{0,4},{4,0},{8,12},{12,8},{16,20},{20,16},{24,28},{28,24},{1,5},{5... | collective-permute-start | bytes 393224 | tf_op jit(solution)/shard_map/ppermute | solution.py:239
  84.1 6.3 %collective-permute-start.40 = (f32[2,128,128]{2,1,0:T(8,128)S(1)}, f32[2,128,128]{2,1,0:T(8,128)S(1)}, u32[]{:S(2)}, u32[]{:S(2)}) collective-permute-start(f32[2,128,128]{2,1,0:T(8,128)S(1)} %get-tuple-element.201), channel_id=1, source_target_pairs={{0,4},{4,0},{8,12},{12,8},{16,20},{20,16},{24,28},{28,24},{1,5},{5... | collective-permute-start | bytes 393224 | tf_op jit(solution)/shard_map/ppermute | solution.py:239
  86.5 5.2 %collective-permute-start.39 = (f32[2,128,128]{2,1,0:T(8,128)S(1)}, f32[2,128,128]{2,1,0:T(8,128)S(1)}, u32[]{:S(2)}, u32[]{:S(2)}) collective-permute-start(f32[2,128,128]{2,1,0:T(8,128)S(1)} %get-tuple-element.199), channel_id=1, source_target_pairs={{0,4},{4,0},{8,12},{12,8},{16,20},{20,16},{24,28},{28,24},{1,5},{5... | collective-permute-start | bytes 393224 | tf_op jit(solution)/shard_map/ppermute | solution.py:239

commit v11 on v10

--- a/solution.py
+++ b/solution.py
@@ -63,8 +63,8 @@
 
 
 def local_body(per, chunks, heads, place, q, k, v, *refs):
-    outs, attn = refs[:chunks], refs[chunks]
-    for turn in range(2):
+    outs, attn = refs[-1 - chunks:-1], refs[-1]
+    for turn in range(chunks * per // heads):
         @pl.when(pl.program_id(0) == turn)
         def _():
             for j in range(heads):
@@ -126,25 +126,31 @@
             outs[chunks + c][j] = dot(head(q, h), x, 0, 0)
 
 
-def query_body(per, chunks, place, k, v, *refs):
+def column(ref, base, h):
+    return ref[:, pl.ds(pl.multiple_of(base + h * DH, DH), DH)]
+
+
+def query_body(per, half, first, chunks, place, k, v, *refs):
     qg = refs[-1]
     mask = causal()
     for turn in range(2 * chunks):
         d, sb = refs[turn], refs[2 * chunks + turn]
+        base = (1 - place[0] if turn % 2 else place[0]) * half * DH + (first + turn // 2) * per * DH
 
         @pl.when(pl.program_id(0) == turn)
         def _():
-            first = [dot(head(d, j), head(v, j), 1, 1) for j in range(per)]
+            scores = [dot(head(d, j), column(v, base, j), 1, 1) for j in range(per)]
             prior = [dot(head(d, j), sb[j], 1, 1) for j in range(per)]
-            first = [masked(s, mask) for s in first]
-            for j, s in enumerate(first):
-                qg[:, j * DH:(j + 1) * DH] = (dot(s, head(k, j), 1, 0) + prior[j]).astype(BF16)
-
-
-def final_body(per, chunks, terms, place, q, k, v, *refs):
+            scores = [masked(s, mask) for s in scores]
+            for j, s in enumerate(scores):
+                qg[:, j * DH:(j + 1) * DH] = (dot(s, column(k, base, j), 1, 0) + prior[j]).astype(BF16)
+
+
+def final_body(per, half, first, other, chunks, terms, place, q, k, v, *refs):
     ds, later_in, kg, vg = refs[:chunks], refs[chunks:chunks + chunks * terms], refs[-2], refs[-1]
     mask = causal(turned=True)
     heads = range(chunks * per)
+    base = (1 - place[0] if other else place[0]) * half * DH + first * per * DH
 
     def later(h):
         state = later_in[h // per * terms][h % per]
@@ -153,16 +159,17 @@
         return state.astype(BF16)
 
     outer = [head(ds[h // per], h % per) for h in heads]
-    grad = [dot(head(v, h), outer[h], 1, 1) for h in heads]
-    score = [dot(head(k, h), head(q, h), 1, 1) for h in heads]
+    qs, ks, vs = ([column(a, base, h) for h in heads] for a in (q, k, v))
+    grad = [dot(vs[h], outer[h], 1, 1) for h in heads]
+    score = [dot(ks[h], qs[h], 1, 1) for h in heads]
     states = [later(h) for h in heads]
-    kg_part = [dot(head(v, h), states[h], 1, 1) for h in heads]
-    vg_part = [dot(head(k, h), states[h], 1, 0) for h in heads]
+    kg_part = [dot(vs[h], states[h], 1, 1) for h in heads]
+    vg_part = [dot(ks[h], states[h], 1, 0) for h in heads]
     grad = [masked(x, mask) for x in grad]
     score = [masked(x, mask) for x in score]
     for h in heads:
         at = slice(h * DH, (h + 1) * DH)
-        kg[:, at] = (dot(grad[h], head(q, h), 1, 0) + kg_part[h]).astype(BF16)
+        kg[:, at] = (dot(grad[h], qs[h], 1, 0) + kg_part[h]).astype(BF16)
         vg[:, at] = (dot(score[h], outer[h], 1, 0) + vg_part[h]).astype(BF16)
 
 
@@ -272,18 +279,24 @@
             )
 
         group = half // 2
-        strip = lambda i, s: (0, (2 * s[0] + i) % 4)
-        *kept, attn_local = call(
-            functools.partial(local_body, per, CHUNKS, group), place,
-            [(a, (tokens, group * DH), strip, HBM) for a in (queries, keys, values)],
-            [((per, DH, DH), F32, (per, DH, DH), whole3, VMEM)] * CHUNKS + [
-                ((tokens, width), F32, (tokens, group * DH), strip, VMEM),
-            ],
-            grid=(4,),
-        )
+
+        def local(which, chunks, memory, ties):
+            strip = lambda i, s: (0, 2 * (1 - s[0] if which else s[0]) + i)
+            return call(
+                functools.partial(local_body, per, chunks, group), place,
+                [(a, (tokens, group * DH), strip, memory) for a in (queries, keys, values)]
+                + [(a, None, None) for a in ties],
+                [((per, DH, DH), F32, (per, DH, DH), whole3, VMEM)] * chunks + [
+                    ((tokens, wide), F32, (tokens, group * DH), lambda i, s: (0, i), VMEM),
+                ],
+                grid=(2,),
+            )
+
+        *kept, local_kept = local(0, CHUNKS, HBM, [])
         tail = long - 1
         spread = 2 < long <= 4
-        before = scan(kept, sent, leads, False, [attn_local], {})
+        before = scan(kept, sent, leads, False, [local_kept], {})
+        local_other, = local(1, 0, VMEM, [before[CHUNKS - 1][0]])
 
         block = (tokens, narrow)
         square = cross = None
@@ -292,7 +305,9 @@
             e, r, other = before[c]
             first, last = c == 0, c == CHUNKS - 1
             ins = []
-            for a in (attn_local, queries, out_grad):
+            here = lambda i, s: (0, c)
+            ins += [(local_kept, block, here), (local_other, block, here)]
+            for a in (queries, out_grad):
                 ins += [(a, block, at_k(c)), (a, block, at_o(c))]
             ins += [(gain, (1, narrow), at_k(c)), (gain, (1, narrow), at_o(c))]
             ins += [(a, (per, DH, DH), whole3) for a in (e, r, other)]
@@ -344,7 +359,7 @@
         made = {"query": [], "rest": []}
 
         def query(c, count, tie=None):
-            ins = [(a, block, mine(c)) for a in (keys, values)]
+            ins = [(a, (tokens, width), whole2) for a in (keys, values)]
             some = range(c, c + count)
             grads = [a for i in some for a in (d_k[i], d_o[i])]
             if tie is not None:
@@ -356,7 +371,7 @@
                 aliases[len(ins) + 1] = 0
                 ins += [(a, None, None, HBM) for a in made["query"]]
             made["query"] = call(
-                functools.partial(query_body, per, count), place, ins,
+                functools.partial(query_body, per, half, c, count), place, ins,
                 [((tokens, width), BF16, block, mine(c), HBM)], grid=(2 * count,), aliases=aliases)
             return made["query"][0]
 
@@ -366,7 +381,7 @@
             wider = (tokens, narrow * count)
             some = range(c, c + count)
             states = [a for i in some for a in (after[i][2:] if which else after[i][:2])]
-            ins = [(a, wider, index) for a in (queries, keys, values)]
+            ins = [(a, (tokens, width), whole2) for a in (queries, keys, values)]
             ins += [((d_o if which else d_k)[i], block, whole2) for i in some]
             ins += [(a, state3, whole3) for a in states]
             aliases = {}
@@ -374,7 +389,7 @@
                 aliases = {len(ins) + 1: 0, len(ins) + 2: 1}
                 ins += [(a, None, None, HBM) for a in made["rest"]]
             made["rest"] = call(
-                functools.partial(final_body, per, count, len(states) // count), place, ins,
+                functools.partial(final_body, per, half, c, which, count, len(states) // count), place, ins,
                 [((tokens, width), BF16, wider, index, HBM)] * 2, aliases=aliases)
             return made["rest"][0]
 

time: 93.7 us -> 92.7 us (0.989)
    ppermute x8, starting transfers between devices: 10.3 us -> 11.6 us  [swap_after(): flight[c] = lax.ppermute(part_sent, 'seq', swap)]
    pallas_call x19 -> x20, Pallas kernels: 23.9 us -> 23 us  [call(): pl.pallas_call(body, grid_spec=pltpu.PrefetchScalarGridSpec(num_scalar_pr...]
  transfers between devices with their start and end apart: 43 -> 43, of which waited for: 14 -> 13; matrix products, arithmetic and copies ran while one was open for 1% -> 1% of each run, Pallas kernels for 22% -> 21%
where the time goes in v11:
time: 92.7 us; the launch traced here: 92 us
  starting transfers between devices  47.3 us (51%)
  Pallas kernels  23 us (25%)
  waiting for transfers between devices  19.6 us (21%)
  between operations  1.29 us (1%)
    ppermute x24, starting transfers between devices, hop(): return lax.ppermute(array, 'seq', pairs)  25.2 us
    pallas_call x20, Pallas kernels, call(): pl.pallas_call(body, grid_spec=pltpu.PrefetchScalarGridSpec(num_scalar_pr...  23 us
    ppermute x8, starting transfers between devices, swap_after(): flight[c] = lax.ppermute(part_sent, 'seq', swap)  11.6 us
    ppermute x8, starting transfers between devices, scan(): out[c] = (carry[c], own[c], lax.ppermute(send, 'seq', swap))  8.62 us
    ppermute x8, waiting for transfers between devices, swap_after(): flight[c] = lax.ppermute(part_sent, 'seq', swap)  6.69 us
    ppermute x24, waiting for transfers between devices, hop(): return lax.ppermute(array, 'seq', pairs)  6.67 us
    ppermute x8, waiting for transfers between devices, scan(): out[c] = (carry[c], own[c], lax.ppermute(send, 'seq', swap))  4.42 us
    ppermute x3, starting transfers between devices, shards(): lax.ppermute(mine, 'head', [(i, i ^ step if paired else (i + step) % part...  1.92 us
  transfers between devices with their start and end apart: 43, of which 13 were waited for; matrix products, arithmetic and copies ran while one was open for 1% of the time, Pallas kernels for 21%

profile of v11, /device:TPU:0, one launch (start us, length us, event | category | flops | bytes accessed | tf_op | source)
XLA Modules:
  0.0 92.0 jit_solution(17080001151009575055)
XLA Ops:
  0.6 1.3 %shard_map.78 = (f32[2,128,128]{2,1,0:T(8,128)S(1)}, f32[2,128,128]{2,1,0:T(8,128)S(1)}) custom-call(s32[1]{0:T(128)} %bitcast.place, bf16[256,2048]{1,0:T(8,128)(2,1)} %k.21, bf16[256,2048]{1,0:T(8,128)(2,1)} %v.21), custom_call_target="tpu_custom_call" | custom-call | flops 1024 | bytes 1024 | tf_op jit(solution)/shard_map/pallas_call | solution.py:43
  2.0 3.0 %collective-permute-start = (f32[2,128,128]{2,1,0:T(8,128)S(1)}, f32[2,128,128]{2,1,0:T(8,128)S(1)}, u32[]{:S(2)}, u32[]{:S(2)}) collective-permute-start(f32[2,128,128]{2,1,0:T(8,128)S(1)} %get-tuple-element.106), channel_id=1, source_target_pairs={{0,4},{4,0},{8,12},{12,8},{16,20},{20,16},{24,28},{28,24},{1,5},{5... | collective-permute-start | bytes 393224 | tf_op jit(solution)/shard_map/ppermute | solution.py:226
  5.1 1.3 %shard_map.77 = (f32[2,128,128]{2,1,0:T(8,128)S(1)}, f32[2,128,128]{2,1,0:T(8,128)S(1)}) custom-call(s32[1]{0:T(128)} %bitcast.place, bf16[256,2048]{1,0:T(8,128)(2,1)} %k.21, bf16[256,2048]{1,0:T(8,128)(2,1)} %v.21), custom_call_target="tpu_custom_call" | custom-call | flops 1024 | bytes 1024 | tf_op jit(solution)/shard_map/pallas_call | solution.py:43
  6.4 2.0 %collective-permute-start.3 = (f32[2,128,128]{2,1,0:T(8,128)S(1)}, f32[2,128,128]{2,1,0:T(8,128)S(1)}, u32[]{:S(2)}, u32[]{:S(2)}) collective-permute-start(f32[2,128,128]{2,1,0:T(8,128)S(1)} %get-tuple-element.110), channel_id=1, source_target_pairs={{0,4},{4,0},{8,12},{12,8},{16,20},{20,16},{24,28},{28,24},{1,5},{5... | collective-permute-start | bytes 393224 | tf_op jit(solution)/shard_map/ppermute | solution.py:226
  8.4 2.6 %shard_map.76 = (f32[2,128,128]{2,1,0:T(8,128)S(1)}, f32[2,128,128]{2,1,0:T(8,128)S(1)}, f32[2,128,128]{2,1,0:T(8,128)S(1)}, f32[2,128,128]{2,1,0:T(8,128)S(1)}, f32[256,1024]{1,0:T(8,128)S(1)}) custom-call(s32[1]{0:T(128)} %bitcast.place, bf16[256,2048]{1,0:T(8,128)(2,1)} %q.15, bf16[256,2048]{1,0:T(8,128)(2,1)} %k.21, bf16[256,2048]{1,0:T(8,128)(2,1)} %v.21), custom_call_target="tpu_custom_call" | custom-call | flops 1024 | bytes 1024 | tf_op jit(solution)/shard_map/pallas_call | solution.py:43
  11.1 3.5 %collective-permute-start.2 = (f32[2,128,128]{2,1,0:T(8,128)S(1)}, f32[2,128,128]{2,1,0:T(8,128)S(1)}, u32[]{:S(2)}, u32[]{:S(2)}) collective-permute-start(f32[2,128,128]{2,1,0:T(8,128)S(1)} %get-tuple-element.240), channel_id=1, source_target_pairs={{0,8},{4,12},{1,9},{5,13},{2,10},{6,14},{3,11},{7,15}} | collective-permute-start | bytes 393224 | tf_op jit(solution)/shard_map/ppermute | solution.py:191
  14.6 1.6 %collective-permute-start.8 = (f32[2,128,128]{2,1,0:T(8,128)S(1)}, f32[2,128,128]{2,1,0:T(8,128)S(1)}, u32[]{:S(2)}, u32[]{:S(2)}) collective-permute-start(f32[2,128,128]{2,1,0:T(8,128)S(1)} %get-tuple-element.242), channel_id=1, source_target_pairs={{0,8},{4,12},{1,9},{5,13},{2,10},{6,14},{3,11},{7,15}} | collective-permute-start | bytes 393224 | tf_op jit(solution)/shard_map/ppermute | solution.py:191
  16.2 1.6 %collective-permute-start.1 = (f32[2,128,128]{2,1,0:T(8,128)S(1)}, f32[2,128,128]{2,1,0:T(8,128)S(1)}, u32[]{:S(2)}, u32[]{:S(2)}) collective-permute-start(f32[2,128,128]{2,1,0:T(8,128)S(1)} %get-tuple-element.108), channel_id=1, source_target_pairs={{0,4},{4,0},{8,12},{12,8},{16,20},{20,16},{24,28},{28,24},{1,5},{5... | collective-permute-start | bytes 393224 | tf_op jit(solution)/shard_map/ppermute | solution.py:226
  17.8 1.6 %collective-permute-start.7 = (f32[2,128,128]{2,1,0:T(8,128)S(1)}, f32[2,128,128]{2,1,0:T(8,128)S(1)}, u32[]{:S(2)}, u32[]{:S(2)}) collective-permute-start(f32[2,128,128]{2,1,0:T(8,128)S(1)} %get-tuple-element.244), channel_id=1, source_target_pairs={{0,8},{4,12},{1,9},{5,13},{2,10},{6,14},{3,11},{7,15}} | collective-permute-start | bytes 393224 | tf_op jit(solution)/shard_map/ppermute | solution.py:191
  20.1 1.2 %collective-permute-done.1 = f32[2,128,128]{2,1,0:T(8,128)S(1)} collective-permute-done((f32[2,128,128]{2,1,0:T(8,128)S(1)}, f32[2,128,128]{2,1,0:T(8,128)S(1)}, u32[]{:S(2)}, u32[]{:S(2)}) %collective-permute-start.1) | collective-permute-done | bytes 131104 | tf_op jit(solution)/shard_map/ppermute | solution.py:226
  21.2 2.4 %collective-permute-start.5 = (f32[2,128,128]{2,1,0:T(8,128)S(1)}, f32[2,128,128]{2,1,0:T(8,128)S(1)}, u32[]{:S(2)}, u32[]{:S(2)}) collective-permute-start(f32[2,128,128]{2,1,0:T(8,128)S(1)} %get-tuple-element.246), channel_id=1, source_target_pairs={{0,8},{4,12},{1,9},{5,13},{2,10},{6,14},{3,11},{7,15}} | collective-permute-start | bytes 393224 | tf_op jit(solution)/shard_map/ppermute | solution.py:191
  28.3 0.8 collective-permute-start.19
  29.1 0.8 collective-permute-start.13
  30.0 1.4 %collective-permute-start.18 = (f32[2,128,128]{2,1,0:T(8,128)S(1)}, f32[2,128,128]{2,1,0:T(8,128)S(1)}, u32[]{:S(2)}, u32[]{:S(2)}) collective-permute-start(f32[2,128,128]{2,1,0:T(8,128)S(1)} %get-tuple-element.219), channel_id=1, source_target_pairs={{0,4},{4,0},{8,12},{12,8},{16,20},{20,16},{24,28},{28,24},{1,5},{5... | collective-permute-start | bytes 393224 | tf_op jit(solution)/shard_map/ppermute | solution.py:246
  31.4 0.8 collective-permute-start.17
  32.2 1.4 %collective-permute-start.16 = (f32[2,128,128]{2,1,0:T(8,128)S(1)}, f32[2,128,128]{2,1,0:T(8,128)S(1)}, u32[]{:S(2)}, u32[]{:S(2)}) collective-permute-start(f32[2,128,128]{2,1,0:T(8,128)S(1)} %get-tuple-element.215), channel_id=1, source_target_pairs={{0,4},{4,0},{8,12},{12,8},{16,20},{20,16},{24,28},{28,24},{1,5},{5... | collective-permute-start | bytes 393224 | tf_op jit(solution)/shard_map/ppermute | solution.py:246
  33.7 1.1 %shard_map.79.al_o = f32[256,1024]{1,0:T(8,128)S(1)} custom-call(s32[1]{0:T(128)} %bitcast.place, bf16[256,2048]{1,0:T(8,128)(2,1)S(1)} %copy-done, bf16[256,2048]{1,0:T(8,128)(2,1)S(1)} %copy-done.1, bf16[256,2048]{1,0:T(8,128)(2,1)S(1)} %copy-done.2, f32[2,128,128]{2,1,0:T(8,128)S(1)} %get-tuple-element.216.refs_0_.e), custom_call_target="tpu_custom_call" | custom-call | flops 1024 | bytes 1024 | tf_op jit(solution)/shard_map/pallas_call | solution.py:43
  35.2 2.0 %collective-permute-done.18.other = f32[2,128,128]{2,1,0:T(8,128)S(1)} collective-permute-done((f32[2,128,128]{2,1,0:T(8,128)S(1)}, f32[2,128,128]{2,1,0:T(8,128)S(1)}, u32[]{:S(2)}, u32[]{:S(2)}) %collective-permute-start.18) | collective-permute-done | bytes 131104 | tf_op jit(solution)/shard_map/ppermute | solution.py:246
  37.5 1.1 %collective-permute-done.17.other = f32[2,128,128]{2,1,0:T(8,128)S(1)} collective-permute-done((f32[2,128,128]{2,1,0:T(8,128)S(1)}, f32[2,128,128]{2,1,0:T(8,128)S(1)}, u32[]{:S(2)}, u32[]{:S(2)}) %collective-permute-start.17) | collective-permute-done | bytes 131104 | tf_op jit(solution)/shard_map/ppermute | solution.py:246
  38.9 1.1 %collective-permute-done.16.other = f32[2,128,128]{2,1,0:T(8,128)S(1)} collective-permute-done((f32[2,128,128]{2,1,0:T(8,128)S(1)}, f32[2,128,128]{2,1,0:T(8,128)S(1)}, u32[]{:S(2)}, u32[]{:S(2)}) %collective-permute-start.16) | collective-permute-done | bytes 131104 | tf_op jit(solution)/shard_map/ppermute | solution.py:246
  40.5 1.6 %collective-permute-start.21 = (f32[2,256]{1,0:T(2,128)S(1)}, f32[2,256]{1,0:T(2,128)S(1)}, u32[]{:S(2)}, u32[]{:S(2)}) collective-permute-start(f32[2,256]{1,0:T(2,128)S(1)} %get-tuple-element.135.refs_0_), channel_id=1, source_target_pairs={{0,2},{1,3},{2,0},{3,1},{4,6},{5,7},{6,4},{7,5},{8,10},{9,11},{10,... | collective-permute-start | bytes 6152 | tf_op jit(solution)/shard_map/ppermute | solution.py:335
  42.3 1.1 %collective-permute-done.22.refs_3_ = f32[2,256]{1,0:T(2,128)S(1)} collective-permute-done((f32[2,256]{1,0:T(2,128)S(1)}, f32[2,256]{1,0:T(2,128)S(1)}, u32[]{:S(2)}, u32[]{:S(2)}) %collective-permute-start.22) | collective-permute-done | bytes 2080 | tf_op jit(solution)/shard_map/ppermute | solution.py:335
  44.5 1.4 %collective-permute-start.24 = (f32[2,128,128]{2,1,0:T(8,128)S(1)}, f32[2,128,128]{2,1,0:T(8,128)S(1)}, u32[]{:S(2)}, u32[]{:S(2)}) collective-permute-start(f32[2,128,128]{2,1,0:T(8,128)S(1)} %get-tuple-element.152), channel_id=1, source_target_pairs={{0,4},{4,0},{8,12},{12,8},{16,20},{20,16},{24,28},{28,24},{1,5},{5... | collective-permute-start | bytes 393224 | tf_op jit(solution)/shard_map/ppermute | solution.py:226
  46.4 0.8 collective-permute-start.23
  47.1 1.3 %collective-permute-start.28 = (f32[2,128,128]{2,1,0:T(8,128)S(1)}, f32[2,128,128]{2,1,0:T(8,128)S(1)}, u32[]{:S(2)}, u32[]{:S(2)}) collective-permute-start(f32[2,128,128]{2,1,0:T(8,128)S(1)} %get-tuple-element.158), channel_id=1, source_target_pairs={{0,4},{4,0},{8,12},{12,8},{16,20},{20,16},{24,28},{28,24},{1,5},{5... | collective-permute-start | bytes 393224 | tf_op jit(solution)/shard_map/ppermute | solution.py:226
  49.1 1.8 %collective-permute-done.24 = f32[2,128,128]{2,1,0:T(8,128)S(1)} collective-permute-done((f32[2,128,128]{2,1,0:T(8,128)S(1)}, f32[2,128,128]{2,1,0:T(8,128)S(1)}, u32[]{:S(2)}, u32[]{:S(2)}) %collective-permute-start.24) | collective-permute-done | bytes 131104 | tf_op jit(solution)/shard_map/ppermute | solution.py:226
  51.6 1.4 %collective-permute-start.26 = (f32[2,128,128]{2,1,0:T(8,128)S(1)}, f32[2,128,128]{2,1,0:T(8,128)S(1)}, u32[]{:S(2)}, u32[]{:S(2)}) collective-permute-start(f32[2,128,128]{2,1,0:T(8,128)S(1)} %get-tuple-element.156), channel_id=1, source_target_pairs={{0,4},{4,0},{8,12},{12,8},{16,20},{20,16},{24,28},{28,24},{1,5},{5... | collective-permute-start | bytes 393224 | tf_op jit(solution)/shard_map/ppermute | solution.py:226
  53.0 0.7 collective-permute-done.23
  54.4 2.1 %collective-permute-done.28 = f32[2,128,128]{2,1,0:T(8,128)S(1)} collective-permute-done((f32[2,128,128]{2,1,0:T(8,128)S(1)}, f32[2,128,128]{2,1,0:T(8,128)S(1)}, u32[]{:S(2)}, u32[]{:S(2)}) %collective-permute-start.28) | collective-permute-done | bytes 131104 | tf_op jit(solution)/shard_map/ppermute | solution.py:226
  58.0 0.8 collective-permute-done.26
  60.9 2.6 %shard_map.87.refs_4_ = bf16[256,2048]{1,0:T(8,128)(2,1)} custom-call(s32[1]{0:T(128)} %bitcast.place, bf16[256,2048]{1,0:T(8,128)(2,1)S(1)} %copy-done.1, bf16[256,2048]{1,0:T(8,128)(2,1)S(1)} %copy-done.2, bf16[256,256]{1,0:T(8,128)(2,1)S(1)} %get-tuple-element.165.refs_0_, bf16[256,256]{1,0:T(8,128)(2,1)S(1)} %get-tuple-element.166.refs_1_.refs_0_, ...), custom_call_target="tpu_custom_call" | custom-call | flops 1024 | bytes 1024 | tf_op jit(solution)/shard_map/pallas_call | solution.py:43
  63.6 1.3 %collective-permute-start.34 = (f32[2,128,128]{2,1,0:T(8,128)S(1)}, f32[2,128,128]{2,1,0:T(8,128)S(1)}, u32[]{:S(2)}, u32[]{:S(2)}) collective-permute-start(f32[2,128,128]{2,1,0:T(8,128)S(1)} %get-tuple-element.213), channel_id=1, source_target_pairs={{12,4},{8,0},{13,5},{9,1},{14,6},{10,2},{15,7},{11,3}} | collective-permute-start | bytes 393224 | tf_op jit(solution)/shard_map/ppermute | solution.py:191
  65.6 1.3 %collective-permute-start.38 = (f32[2,128,128]{2,1,0:T(8,128)S(1)}, f32[2,128,128]{2,1,0:T(8,128)S(1)}, u32[]{:S(2)}, u32[]{:S(2)}) collective-permute-start(f32[2,128,128]{2,1,0:T(8,128)S(1)} %get-tuple-element.211), channel_id=1, source_target_pairs={{12,4},{8,0},{13,5},{9,1},{14,6},{10,2},{15,7},{11,3}} | collective-permute-start | bytes 393224 | tf_op jit(solution)/shard_map/ppermute | solution.py:191
  67.0 1.3 %collective-permute-start.37 = (f32[2,128,128]{2,1,0:T(8,128)S(1)}, f32[2,128,128]{2,1,0:T(8,128)S(1)}, u32[]{:S(2)}, u32[]{:S(2)}) collective-permute-start(f32[2,128,128]{2,1,0:T(8,128)S(1)} %get-tuple-element.209), channel_id=1, source_target_pairs={{12,4},{8,0},{13,5},{9,1},{14,6},{10,2},{15,7},{11,3}} | collective-permute-start | bytes 393224 | tf_op jit(solution)/shard_map/ppermute | solution.py:191
  68.3 1.5 %shard_map.88.refs_4_ = bf16[256,2048]{1,0:T(8,128)(2,1)} custom-call(s32[1]{0:T(128)} %bitcast.place, bf16[256,2048]{1,0:T(8,128)(2,1)S(1)} %copy-done.1, bf16[256,2048]{1,0:T(8,128)(2,1)S(1)} %copy-done.2, bf16[256,256]{1,0:T(8,128)(2,1)S(1)} %get-tuple-element.176.refs_0_, ...), custom_call_target="tpu_custom_call", output_to_operand_aliasing={{}: (7, {})} | custom-call | flops 1024 | bytes 1024 | tf_op jit(solution)/shard_map/pallas_call | solution.py:43
  69.8 6.3 %collective-permute-done.34 = f32[2,128,128]{2,1,0:T(8,128)S(1)} collective-permute-done((f32[2,128,128]{2,1,0:T(8,128)S(1)}, f32[2,128,128]{2,1,0:T(8,128)S(1)}, u32[]{:S(2)}, u32[]{:S(2)}) %collective-permute-start.34) | collective-permute-done | bytes 131104 | tf_op jit(solution)/shard_map/ppermute | solution.py:191
  76.1 1.4 %collective-permute-start.41 = (f32[2,128,128]{2,1,0:T(8,128)S(1)}, f32[2,128,128]{2,1,0:T(8,128)S(1)}, u32[]{:S(2)}, u32[]{:S(2)}) collective-permute-start(f32[2,128,128]{2,1,0:T(8,128)S(1)} %get-tuple-element.207), channel_id=1, source_target_pairs={{0,4},{4,0},{8,12},{12,8},{16,20},{20,16},{24,28},{28,24},{1,5},{5... | collective-permute-start | bytes 393224 | tf_op jit(solution)/shard_map/ppermute | solution.py:246
  77.6 1.5 %collective-permute-start.36 = (f32[2,128,128]{2,1,0:T(8,128)S(1)}, f32[2,128,128]{2,1,0:T(8,128)S(1)}, u32[]{:S(2)}, u32[]{:S(2)}) collective-permute-start(f32[2,128,128]{2,1,0:T(8,128)S(1)} %get-tuple-element.205), channel_id=1, source_target_pairs={{12,4},{8,0},{13,5},{9,1},{14,6},{10,2},{15,7},{11,3}} | collective-permute-start | bytes 393224 | tf_op jit(solution)/shard_map/ppermute | solution.py:191
  79.1 1.5 %shard_map.89 = bf16[256,2048]{1,0:T(8,128)(2,1)} custom-call(s32[1]{0:T(128)} %bitcast.place, bf16[256,2048]{1,0:T(8,128)(2,1)S(1)} %copy-done.1, bf16[256,2048]{1,0:T(8,128)(2,1)S(1)} %copy-done.2, bf16[256,256]{1,0:T(8,128)(2,1)S(1)} %get-tuple-element.140.refs_0_, ...), custom_call_target="tpu_custom_call", output_to_operand_aliasing={{}: (7, {})} | custom-call | flops 1024 | bytes 1024 | tf_op jit(solution)/shard_map/pallas_call | solution.py:43
  80.6 0.7 collective-permute-start.42
  81.3 1.7 %shard_map.90 = (bf16[256,2048]{1,0:T(8,128)(2,1)}, bf16[256,2048]{1,0:T(8,128)(2,1)}) custom-call(s32[1]{0:T(128)} %bitcast.place, bf16[256,2048]{1,0:T(8,128)(2,1)S(1)} %copy-done, bf16[256,2048]{1,0:T(8,128)(2,1)S(1)} %copy-done.1, bf16[256,2048]{1,0:T(8,128)(2,1)S(1)} %copy-done.2, bf16[256,256]{1,0:T(8,128)(2,1)S(1)} %get-tuple-element.165.refs_0_, ...), custom_call_target="tpu_custom_call" | custom-call | flops 1024 | bytes 1024 | tf_op jit(solution)/shard_map/pallas_call | solution.py:43
  83.0 1.5 %collective-permute-start.40 = (f32[2,128,128]{2,1,0:T(8,128)S(1)}, f32[2,128,128]{2,1,0:T(8,128)S(1)}, u32[]{:S(2)}, u32[]{:S(2)}) collective-permute-start(f32[2,128,128]{2,1,0:T(8,128)S(1)} %get-tuple-element.201), channel_id=1, source_target_pairs={{0,4},{4,0},{8,12},{12,8},{16,20},{20,16},{24,28},{28,24},{1,5},{5... | collective-permute-start | bytes 393224 | tf_op jit(solution)/shard_map/ppermute | solution.py:246
  84.5 1.2 %shard_map.91 = (bf16[256,2048]{1,0:T(8,128)(2,1)}, bf16[256,2048]{1,0:T(8,128)(2,1)}) custom-call(s32[1]{0:T(128)} %bitcast.place, bf16[256,2048]{1,0:T(8,128)(2,1)S(1)} %copy-done, bf16[256,2048]{1,0:T(8,128)(2,1)S(1)} %copy-done.1, bf16[256,2048]{1,0:T(8,128)(2,1)S(1)} %copy-done.2, ...), custom_call_target="tpu_custom_call", output_to_operand_aliasing={{0}: (7, {}), {1}: (8, {})} | custom-call | flops 1024 | bytes 1024 | tf_op jit(solution)/shard_map/pallas_call | solution.py:43
  85.8 0.7 collective-permute-start.39
  86.5 1.2 %shard_map.92 = (bf16[256,2048]{1,0:T(8,128)(2,1)}, bf16[256,2048]{1,0:T(8,128)(2,1)}) custom-call(s32[1]{0:T(128)} %bitcast.place, bf16[256,2048]{1,0:T(8,128)(2,1)S(1)} %copy-done, bf16[256,2048]{1,0:T(8,128)(2,1)S(1)} %copy-done.1, bf16[256,2048]{1,0:T(8,128)(2,1)S(1)} %copy-done.2, ...), custom_call_target="tpu_custom_call", output_to_operand_aliasing={{0}: (7, {}), {1}: (8, {})} | custom-call | flops 1024 | bytes 1024 | tf_op jit(solution)/shard_map/pallas_call | solution.py:43
  87.7 1.7 %shard_map.93 = (bf16[256,2048]{1,0:T(8,128)(2,1)}, bf16[256,2048]{1,0:T(8,128)(2,1)}) custom-call(s32[1]{0:T(128)} %bitcast.place, bf16[256,2048]{1,0:T(8,128)(2,1)S(1)} %copy-done, bf16[256,2048]{1,0:T(8,128)(2,1)S(1)} %copy-done.1, bf16[256,2048]{1,0:T(8,128)(2,1)S(1)} %copy-done.2, ...), custom_call_target="tpu_custom_call", output_to_operand_aliasing={{0}: (8, {}), {1}: (9, {})} | custom-call | flops 1024 | bytes 1024 | tf_op jit(solution)/shard_map/pallas_call | solution.py:43
  89.4 1.2 %shard_map.94 = (bf16[256,2048]{1,0:T(8,128)(2,1)}, bf16[256,2048]{1,0:T(8,128)(2,1)}) custom-call(s32[1]{0:T(128)} %bitcast.place, bf16[256,2048]{1,0:T(8,128)(2,1)S(1)} %copy-done, bf16[256,2048]{1,0:T(8,128)(2,1)S(1)} %copy-done.1, bf16[256,2048]{1,0:T(8,128)(2,1)S(1)} %copy-done.2, ...), custom_call_target="tpu_custom_call", output_to_operand_aliasing={{0}: (6, {}), {1}: (7, {})} | custom-call | flops 1024 | bytes 1024 | tf_op jit(solution)/shard_map/pallas_call | solution.py:43
  90.8 1.2 %shard_map.95 = (bf16[256,2048]{1,0:T(8,128)(2,1)}, bf16[256,2048]{1,0:T(8,128)(2,1)}) custom-call(s32[1]{0:T(128)} %bitcast.place, bf16[256,2048]{1,0:T(8,128)(2,1)S(1)} %copy-done, bf16[256,2048]{1,0:T(8,128)(2,1)S(1)} %copy-done.1, bf16[256,2048]{1,0:T(8,128)(2,1)S(1)} %copy-done.2, ...), custom_call_target="tpu_custom_call", output_to_operand_aliasing={{0}: (6, {}), {1}: (7, {})} | custom-call | flops 1024 | bytes 1024 | tf_op jit(solution)/shard_map/pallas_call | solution.py:43
  (101 shorter events, 15.4 us)
Async XLA Ops:
  2.0 9.1 %collective-permute-start = (f32[2,128,128]{2,1,0:T(8,128)S(1)}, f32[2,128,128]{2,1,0:T(8,128)S(1)}, u32[]{:S(2)}, u32[]{:S(2)}) collective-permute-start(f32[2,128,128]{2,1,0:T(8,128)S(1)} %get-tuple-element.106), channel_id=1, source_target_pairs={{0,4},{4,0},{8,12},{12,8},{16,20},{20,16},{24,28},{28,24},{1,5},{5... | collective-permute-start | bytes 393224 | tf_op jit(solution)/shard_map/ppermute | solution.py:226
  5.0 9.6 %collective-permute-start.4 = (f32[2,128,128]{2,1,0:T(8,128)S(1)}, f32[2,128,128]{2,1,0:T(8,128)S(1)}, u32[]{:S(2)}, u32[]{:S(2)}) collective-permute-start(f32[2,128,128]{2,1,0:T(8,128)S(1)} %get-tuple-element.112), channel_id=1, source_target_pairs={{0,4},{4,0},{8,12},{12,8},{16,20},{20,16},{24,28},{28,24},{1,5},{5... | collective-permute-start | bytes 393224 | tf_op jit(solution)/shard_map/ppermute | solution.py:226
  6.4 9.8 %collective-permute-start.3 = (f32[2,128,128]{2,1,0:T(8,128)S(1)}, f32[2,128,128]{2,1,0:T(8,128)S(1)}, u32[]{:S(2)}, u32[]{:S(2)}) collective-permute-start(f32[2,128,128]{2,1,0:T(8,128)S(1)} %get-tuple-element.110), channel_id=1, source_target_pairs={{0,4},{4,0},{8,12},{12,8},{16,20},{20,16},{24,28},{28,24},{1,5},{5... | collective-permute-start | bytes 393224 | tf_op jit(solution)/shard_map/ppermute | solution.py:226
  11.1 8.3 %collective-permute-start.2 = (f32[2,128,128]{2,1,0:T(8,128)S(1)}, f32[2,128,128]{2,1,0:T(8,128)S(1)}, u32[]{:S(2)}, u32[]{:S(2)}) collective-permute-start(f32[2,128,128]{2,1,0:T(8,128)S(1)} %get-tuple-element.240), channel_id=1, source_target_pairs={{0,8},{4,12},{1,9},{5,13},{2,10},{6,14},{3,11},{7,15}} | collective-permute-start | bytes 393224 | tf_op jit(solution)/shard_map/ppermute | solution.py:191
  14.6 9.0 %collective-permute-start.8 = (f32[2,128,128]{2,1,0:T(8,128)S(1)}, f32[2,128,128]{2,1,0:T(8,128)S(1)}, u32[]{:S(2)}, u32[]{:S(2)}) collective-permute-start(f32[2,128,128]{2,1,0:T(8,128)S(1)} %get-tuple-element.242), channel_id=1, source_target_pairs={{0,8},{4,12},{1,9},{5,13},{2,10},{6,14},{3,11},{7,15}} | collective-permute-start | bytes 393224 | tf_op jit(solution)/shard_map/ppermute | solution.py:191
  16.2 5.0 %collective-permute-start.1 = (f32[2,128,128]{2,1,0:T(8,128)S(1)}, f32[2,128,128]{2,1,0:T(8,128)S(1)}, u32[]{:S(2)}, u32[]{:S(2)}) collective-permute-start(f32[2,128,128]{2,1,0:T(8,128)S(1)} %get-tuple-element.108), channel_id=1, source_target_pairs={{0,4},{4,0},{8,12},{12,8},{16,20},{20,16},{24,28},{28,24},{1,5},{5... | collective-permute-start | bytes 393224 | tf_op jit(solution)/shard_map/ppermute | solution.py:226
  17.8 6.5 %collective-permute-start.7 = (f32[2,128,128]{2,1,0:T(8,128)S(1)}, f32[2,128,128]{2,1,0:T(8,128)S(1)}, u32[]{:S(2)}, u32[]{:S(2)}) collective-permute-start(f32[2,128,128]{2,1,0:T(8,128)S(1)} %get-tuple-element.244), channel_id=1, source_target_pairs={{0,8},{4,12},{1,9},{5,13},{2,10},{6,14},{3,11},{7,15}} | collective-permute-start | bytes 393224 | tf_op jit(solution)/shard_map/ppermute | solution.py:191
  19.4 5.7 %collective-permute-start.6 = (f32[2,128,128]{2,1,0:T(8,128)S(1)}, f32[2,128,128]{2,1,0:T(8,128)S(1)}, u32[]{:S(2)}, u32[]{:S(2)}) collective-permute-start(f32[2,128,128]{2,1,0:T(8,128)S(1)} %add.152), channel_id=1, source_target_pairs={{8,16},{12,20},{9,17},{13,21},{10,18},{14,22},{11,19},{15,23}} | collective-permute-start | bytes 393224 | tf_op jit(solution)/shard_map/ppermute | solution.py:191
  21.2 4.9 %collective-permute-start.5 = (f32[2,128,128]{2,1,0:T(8,128)S(1)}, f32[2,128,128]{2,1,0:T(8,128)S(1)}, u32[]{:S(2)}, u32[]{:S(2)}) collective-permute-start(f32[2,128,128]{2,1,0:T(8,128)S(1)} %get-tuple-element.246), channel_id=1, source_target_pairs={{0,8},{4,12},{1,9},{5,13},{2,10},{6,14},{3,11},{7,15}} | collective-permute-start | bytes 393224 | tf_op jit(solution)/shard_map/ppermute | solution.py:191
  23.7 3.2 %collective-permute-start.12 = (f32[2,128,128]{2,1,0:T(8,128)S(1)}, f32[2,128,128]{2,1,0:T(8,128)S(1)}, u32[]{:S(2)}, u32[]{:S(2)}) collective-permute-start(f32[2,128,128]{2,1,0:T(8,128)S(1)} %add.154), channel_id=1, source_target_pairs={{8,16},{12,20},{9,17},{13,21},{10,18},{14,22},{11,19},{15,23}} | collective-permute-start | bytes 393224 | tf_op jit(solution)/shard_map/ppermute | solution.py:191
  24.4 3.2 %collective-permute-start.11 = (f32[2,128,128]{2,1,0:T(8,128)S(1)}, f32[2,128,128]{2,1,0:T(8,128)S(1)}, u32[]{:S(2)}, u32[]{:S(2)}) collective-permute-start(f32[2,128,128]{2,1,0:T(8,128)S(1)} %add.155), channel_id=1, source_target_pairs={{8,16},{12,20},{9,17},{13,21},{10,18},{14,22},{11,19},{15,23}} | collective-permute-start | bytes 393224 | tf_op jit(solution)/shard_map/ppermute | solution.py:191
  25.1 3.2 %collective-permute-start.10 = (f32[2,128,128]{2,1,0:T(8,128)S(1)}, f32[2,128,128]{2,1,0:T(8,128)S(1)}, u32[]{:S(2)}, u32[]{:S(2)}) collective-permute-start(f32[2,128,128]{2,1,0:T(8,128)S(1)} %get-tuple-element.229), channel_id=1, source_target_pairs={{16,24},{20,28},{17,25},{21,29},{18,26},{22,30},{19,27},{23,31}} | collective-permute-start | bytes 393224 | tf_op jit(solution)/shard_map/ppermute | solution.py:191
  26.1 2.9 %collective-permute-start.9 = (f32[2,128,128]{2,1,0:T(8,128)S(1)}, f32[2,128,128]{2,1,0:T(8,128)S(1)}, u32[]{:S(2)}, u32[]{:S(2)}) collective-permute-start(f32[2,128,128]{2,1,0:T(8,128)S(1)} %add.158), channel_id=1, source_target_pairs={{8,16},{12,20},{9,17},{13,21},{10,18},{14,22},{11,19},{15,23}} | collective-permute-start | bytes 393224 | tf_op jit(solution)/shard_map/ppermute | solution.py:191
  26.9 3.1 %collective-permute-start.15 = (f32[2,128,128]{2,1,0:T(8,128)S(1)}, f32[2,128,128]{2,1,0:T(8,128)S(1)}, u32[]{:S(2)}, u32[]{:S(2)}) collective-permute-start(f32[2,128,128]{2,1,0:T(8,128)S(1)} %get-tuple-element.227), channel_id=1, source_target_pairs={{16,24},{20,28},{17,25},{21,29},{18,26},{22,30},{19,27},{23,31}} | collective-permute-start | bytes 393224 | tf_op jit(solution)/shard_map/ppermute | solution.py:191
  27.6 3.8 %collective-permute-start.14 = (f32[2,128,128]{2,1,0:T(8,128)S(1)}, f32[2,128,128]{2,1,0:T(8,128)S(1)}, u32[]{:S(2)}, u32[]{:S(2)}) collective-permute-start(f32[2,128,128]{2,1,0:T(8,128)S(1)} %get-tuple-element.225), channel_id=1, source_target_pairs={{16,24},{20,28},{17,25},{21,29},{18,26},{22,30},{19,27},{23,31}} | collective-permute-start | bytes 393224 | tf_op jit(solution)/shard_map/ppermute | solution.py:191
  28.3 5.3 %copy-start.2 = (bf16[256,2048]{1,0:T(8,128)(2,1)S(1)}, bf16[256,2048]{1,0:T(8,128)(2,1)}, u32[]{:S(2)}) copy-start(bf16[256,2048]{1,0:T(8,128)(2,1)} %v.21) | copy-start | bytes 3145732
  28.3 6.5 %collective-permute-start.19 = (f32[2,128,128]{2,1,0:T(8,128)S(1)}, f32[2,128,128]{2,1,0:T(8,128)S(1)}, u32[]{:S(2)}, u32[]{:S(2)}) collective-permute-start(f32[2,128,128]{2,1,0:T(8,128)S(1)} %get-tuple-element.223), channel_id=1, source_target_pairs={{0,4},{4,0},{8,12},{12,8},{16,20},{20,16},{24,28},{28,24},{1,5},{5... | collective-permute-start | bytes 393224 | tf_op jit(solution)/shard_map/ppermute | solution.py:246
  29.1 4.5 %copy-start.1 = (bf16[256,2048]{1,0:T(8,128)(2,1)S(1)}, bf16[256,2048]{1,0:T(8,128)(2,1)}, u32[]{:S(2)}) copy-start(bf16[256,2048]{1,0:T(8,128)(2,1)} %k.21) | copy-start | bytes 3145732
  29.1 4.5 %copy-start = (bf16[256,2048]{1,0:T(8,128)(2,1)S(1)}, bf16[256,2048]{1,0:T(8,128)(2,1)}, u32[]{:S(2)}) copy-start(bf16[256,2048]{1,0:T(8,128)(2,1)} %q.15) | copy-start | bytes 3145732
  29.1 3.0 %collective-permute-start.13 = (f32[2,128,128]{2,1,0:T(8,128)S(1)}, f32[2,128,128]{2,1,0:T(8,128)S(1)}, u32[]{:S(2)}, u32[]{:S(2)}) collective-permute-start(f32[2,128,128]{2,1,0:T(8,128)S(1)} %get-tuple-element.221), channel_id=1, source_target_pairs={{16,24},{20,28},{17,25},{21,29},{18,26},{22,30},{19,27},{23,31}} | collective-permute-start | bytes 393224 | tf_op jit(solution)/shard_map/ppermute | solution.py:191
  30.0 7.2 %collective-permute-start.18 = (f32[2,128,128]{2,1,0:T(8,128)S(1)}, f32[2,128,128]{2,1,0:T(8,128)S(1)}, u32[]{:S(2)}, u32[]{:S(2)}) collective-permute-start(f32[2,128,128]{2,1,0:T(8,128)S(1)} %get-tuple-element.219), channel_id=1, source_target_pairs={{0,4},{4,0},{8,12},{12,8},{16,20},{20,16},{24,28},{28,24},{1,5},{5... | collective-permute-start | bytes 393224 | tf_op jit(solution)/shard_map/ppermute | solution.py:246
  31.4 7.2 %collective-permute-start.17 = (f32[2,128,128]{2,1,0:T(8,128)S(1)}, f32[2,128,128]{2,1,0:T(8,128)S(1)}, u32[]{:S(2)}, u32[]{:S(2)}) collective-permute-start(f32[2,128,128]{2,1,0:T(8,128)S(1)} %get-tuple-element.217), channel_id=1, source_target_pairs={{0,4},{4,0},{8,12},{12,8},{16,20},{20,16},{24,28},{28,24},{1,5},{5... | collective-permute-start | bytes 393224 | tf_op jit(solution)/shard_map/ppermute | solution.py:246
  32.2 1.4 %copy-start.4 = (bf16[2048]{0:T(1024)(128)(2,1)S(1)}, bf16[2048]{0:T(1024)(128)(2,1)}, u32[]{:S(2)}) copy-start(bf16[2048]{0:T(1024)(128)(2,1)} %param.9) | copy-start | bytes 12292
  32.2 7.8 %collective-permute-start.16 = (f32[2,128,128]{2,1,0:T(8,128)S(1)}, f32[2,128,128]{2,1,0:T(8,128)S(1)}, u32[]{:S(2)}, u32[]{:S(2)}) collective-permute-start(f32[2,128,128]{2,1,0:T(8,128)S(1)} %get-tuple-element.215), channel_id=1, source_target_pairs={{0,4},{4,0},{8,12},{12,8},{16,20},{20,16},{24,28},{28,24},{1,5},{5... | collective-permute-start | bytes 393224 | tf_op jit(solution)/shard_map/ppermute | solution.py:246
  33.6 1.2 %copy-start.3 = (bf16[256,2048]{1,0:T(8,128)(2,1)S(1)}, bf16[256,2048]{1,0:T(8,128)(2,1)}, u32[]{:S(2)}) copy-start(bf16[256,2048]{1,0:T(8,128)(2,1)} %refs_7_.3) | copy-start | bytes 3145732
  40.4 3.1 %collective-permute-start.22 = (f32[2,256]{1,0:T(2,128)S(1)}, f32[2,256]{1,0:T(2,128)S(1)}, u32[]{:S(2)}, u32[]{:S(2)}) collective-permute-start(f32[2,256]{1,0:T(2,128)S(1)} %get-tuple-element.135.refs_0_), channel_id=1, source_target_pairs={{0,3},{1,2},{2,1},{3,0},{4,7},{5,6},{6,5},{7,4},{8,11},{9,10},{10,... | collective-permute-start | bytes 6152 | tf_op jit(solution)/shard_map/ppermute | solution.py:335
  40.5 3.7 %collective-permute-start.21 = (f32[2,256]{1,0:T(2,128)S(1)}, f32[2,256]{1,0:T(2,128)S(1)}, u32[]{:S(2)}, u32[]{:S(2)}) collective-permute-start(f32[2,256]{1,0:T(2,128)S(1)} %get-tuple-element.135.refs_0_), channel_id=1, source_target_pairs={{0,2},{1,3},{2,0},{3,1},{4,6},{5,7},{6,4},{7,5},{8,10},{9,11},{10,... | collective-permute-start | bytes 6152 | tf_op jit(solution)/shard_map/ppermute | solution.py:335
  42.0 2.1 %collective-permute-start.20 = (f32[2,256]{1,0:T(2,128)S(1)}, f32[2,256]{1,0:T(2,128)S(1)}, u32[]{:S(2)}, u32[]{:S(2)}) collective-permute-start(f32[2,256]{1,0:T(2,128)S(1)} %get-tuple-element.135.refs_0_), channel_id=1, source_target_pairs={{0,1},{1,0},{2,3},{3,2},{4,5},{5,4},{6,7},{7,6},{8,9},{9,8},{10,11... | collective-permute-start | bytes 6152 | tf_op jit(solution)/shard_map/ppermute | solution.py:335
  44.5 6.4 %collective-permute-start.24 = (f32[2,128,128]{2,1,0:T(8,128)S(1)}, f32[2,128,128]{2,1,0:T(8,128)S(1)}, u32[]{:S(2)}, u32[]{:S(2)}) collective-permute-start(f32[2,128,128]{2,1,0:T(8,128)S(1)} %get-tuple-element.152), channel_id=1, source_target_pairs={{0,4},{4,0},{8,12},{12,8},{16,20},{20,16},{24,28},{28,24},{1,5},{5... | collective-permute-start | bytes 393224 | tf_op jit(solution)/shard_map/ppermute | solution.py:226
  46.4 7.4 %collective-permute-start.23 = (f32[2,128,128]{2,1,0:T(8,128)S(1)}, f32[2,128,128]{2,1,0:T(8,128)S(1)}, u32[]{:S(2)}, u32[]{:S(2)}) collective-permute-start(f32[2,128,128]{2,1,0:T(8,128)S(1)} %get-tuple-element.150), channel_id=1, source_target_pairs={{0,4},{4,0},{8,12},{12,8},{16,20},{20,16},{24,28},{28,24},{1,5},{5... | collective-permute-start | bytes 393224 | tf_op jit(solution)/shard_map/ppermute | solution.py:226
  47.1 9.4 %collective-permute-start.28 = (f32[2,128,128]{2,1,0:T(8,128)S(1)}, f32[2,128,128]{2,1,0:T(8,128)S(1)}, u32[]{:S(2)}, u32[]{:S(2)}) collective-permute-start(f32[2,128,128]{2,1,0:T(8,128)S(1)} %get-tuple-element.158), channel_id=1, source_target_pairs={{0,4},{4,0},{8,12},{12,8},{16,20},{20,16},{24,28},{28,24},{1,5},{5... | collective-permute-start | bytes 393224 | tf_op jit(solution)/shard_map/ppermute | solution.py:226
  51.0 6.3 %collective-permute-start.27 = (f32[2,128,128]{2,1,0:T(8,128)S(1)}, f32[2,128,128]{2,1,0:T(8,128)S(1)}, u32[]{:S(2)}, u32[]{:S(2)}) collective-permute-start(f32[2,128,128]{2,1,0:T(8,128)S(1)} %get-tuple-element.238), channel_id=1, source_target_pairs={{28,20},{24,16},{29,21},{25,17},{30,22},{26,18},{31,23},{27,19}} | collective-permute-start | bytes 393224 | tf_op jit(solution)/shard_map/ppermute | solution.py:191
  51.6 7.2 %collective-permute-start.26 = (f32[2,128,128]{2,1,0:T(8,128)S(1)}, f32[2,128,128]{2,1,0:T(8,128)S(1)}, u32[]{:S(2)}, u32[]{:S(2)}) collective-permute-start(f32[2,128,128]{2,1,0:T(8,128)S(1)} %get-tuple-element.156), channel_id=1, source_target_pairs={{0,4},{4,0},{8,12},{12,8},{16,20},{20,16},{24,28},{28,24},{1,5},{5... | collective-permute-start | bytes 393224 | tf_op jit(solution)/shard_map/ppermute | solution.py:226
  53.8 5.8 %collective-permute-start.25 = (f32[2,128,128]{2,1,0:T(8,128)S(1)}, f32[2,128,128]{2,1,0:T(8,128)S(1)}, u32[]{:S(2)}, u32[]{:S(2)}) collective-permute-start(f32[2,128,128]{2,1,0:T(8,128)S(1)} %get-tuple-element.236), channel_id=1, source_target_pairs={{28,20},{24,16},{29,21},{25,17},{30,22},{26,18},{31,23},{27,19}} | collective-permute-start | bytes 393224 | tf_op jit(solution)/shard_map/ppermute | solution.py:191
  56.6 3.7 %collective-permute-start.32 = (f32[2,128,128]{2,1,0:T(8,128)S(1)}, f32[2,128,128]{2,1,0:T(8,128)S(1)}, u32[]{:S(2)}, u32[]{:S(2)}) collective-permute-start(f32[2,128,128]{2,1,0:T(8,128)S(1)} %get-tuple-element.234), channel_id=1, source_target_pairs={{28,20},{24,16},{29,21},{25,17},{30,22},{26,18},{31,23},{27,19}} | collective-permute-start | bytes 393224 | tf_op jit(solution)/shard_map/ppermute | solution.py:191
  57.3 6.2 %collective-permute-start.31 = (f32[2,128,128]{2,1,0:T(8,128)S(1)}, f32[2,128,128]{2,1,0:T(8,128)S(1)}, u32[]{:S(2)}, u32[]{:S(2)}) collective-permute-start(f32[2,128,128]{2,1,0:T(8,128)S(1)} %add.176), channel_id=1, source_target_pairs={{20,12},{16,8},{21,13},{17,9},{22,14},{18,10},{23,15},{19,11}} | collective-permute-start | bytes 393224 | tf_op jit(solution)/shard_map/ppermute | solution.py:191
  58.8 6.0 %collective-permute-start.30 = (f32[2,128,128]{2,1,0:T(8,128)S(1)}, f32[2,128,128]{2,1,0:T(8,128)S(1)}, u32[]{:S(2)}, u32[]{:S(2)}) collective-permute-start(f32[2,128,128]{2,1,0:T(8,128)S(1)} %get-tuple-element.232), channel_id=1, source_target_pairs={{28,20},{24,16},{29,21},{25,17},{30,22},{26,18},{31,23},{27,19}} | collective-permute-start | bytes 393224 | tf_op jit(solution)/shard_map/ppermute | solution.py:191
  59.6 6.0 %collective-permute-start.29 = (f32[2,128,128]{2,1,0:T(8,128)S(1)}, f32[2,128,128]{2,1,0:T(8,128)S(1)}, u32[]{:S(2)}, u32[]{:S(2)}) collective-permute-start(f32[2,128,128]{2,1,0:T(8,128)S(1)} %add.178), channel_id=1, source_target_pairs={{20,12},{16,8},{21,13},{17,9},{22,14},{18,10},{23,15},{19,11}} | collective-permute-start | bytes 393224 | tf_op jit(solution)/shard_map/ppermute | solution.py:191
  60.3 6.7 %collective-permute-start.35 = (f32[2,128,128]{2,1,0:T(8,128)S(1)}, f32[2,128,128]{2,1,0:T(8,128)S(1)}, u32[]{:S(2)}, u32[]{:S(2)}) collective-permute-start(f32[2,128,128]{2,1,0:T(8,128)S(1)} %add.179), channel_id=1, source_target_pairs={{20,12},{16,8},{21,13},{17,9},{22,14},{18,10},{23,15},{19,11}} | collective-permute-start | bytes 393224 | tf_op jit(solution)/shard_map/ppermute | solution.py:191
  63.6 12.5 %collective-permute-start.34 = (f32[2,128,128]{2,1,0:T(8,128)S(1)}, f32[2,128,128]{2,1,0:T(8,128)S(1)}, u32[]{:S(2)}, u32[]{:S(2)}) collective-permute-start(f32[2,128,128]{2,1,0:T(8,128)S(1)} %get-tuple-element.213), channel_id=1, source_target_pairs={{12,4},{8,0},{13,5},{9,1},{14,6},{10,2},{15,7},{11,3}} | collective-permute-start | bytes 393224 | tf_op jit(solution)/shard_map/ppermute | solution.py:191
  64.9 12.6 %collective-permute-start.33 = (f32[2,128,128]{2,1,0:T(8,128)S(1)}, f32[2,128,128]{2,1,0:T(8,128)S(1)}, u32[]{:S(2)}, u32[]{:S(2)}) collective-permute-start(f32[2,128,128]{2,1,0:T(8,128)S(1)} %add.182), channel_id=1, source_target_pairs={{20,12},{16,8},{21,13},{17,9},{22,14},{18,10},{23,15},{19,11}} | collective-permute-start | bytes 393224 | tf_op jit(solution)/shard_map/ppermute | solution.py:191
  65.6 15.0 %collective-permute-start.38 = (f32[2,128,128]{2,1,0:T(8,128)S(1)}, f32[2,128,128]{2,1,0:T(8,128)S(1)}, u32[]{:S(2)}, u32[]{:S(2)}) collective-permute-start(f32[2,128,128]{2,1,0:T(8,128)S(1)} %get-tuple-element.211), channel_id=1, source_target_pairs={{12,4},{8,0},{13,5},{9,1},{14,6},{10,2},{15,7},{11,3}} | collective-permute-start | bytes 393224 | tf_op jit(solution)/shard_map/ppermute | solution.py:191
  67.0 16.0 %collective-permute-start.37 = (f32[2,128,128]{2,1,0:T(8,128)S(1)}, f32[2,128,128]{2,1,0:T(8,128)S(1)}, u32[]{:S(2)}, u32[]{:S(2)}) collective-permute-start(f32[2,128,128]{2,1,0:T(8,128)S(1)} %get-tuple-element.209), channel_id=1, source_target_pairs={{12,4},{8,0},{13,5},{9,1},{14,6},{10,2},{15,7},{11,3}} | collective-permute-start | bytes 393224 | tf_op jit(solution)/shard_map/ppermute | solution.py:191
  76.1 11.6 %collective-permute-start.41 = (f32[2,128,128]{2,1,0:T(8,128)S(1)}, f32[2,128,128]{2,1,0:T(8,128)S(1)}, u32[]{:S(2)}, u32[]{:S(2)}) collective-permute-start(f32[2,128,128]{2,1,0:T(8,128)S(1)} %get-tuple-element.207), channel_id=1, source_target_pairs={{0,4},{4,0},{8,12},{12,8},{16,20},{20,16},{24,28},{28,24},{1,5},{5... | collective-permute-start | bytes 393224 | tf_op jit(solution)/shard_map/ppermute | solution.py:246
  77.6 8.1 %collective-permute-start.36 = (f32[2,128,128]{2,1,0:T(8,128)S(1)}, f32[2,128,128]{2,1,0:T(8,128)S(1)}, u32[]{:S(2)}, u32[]{:S(2)}) collective-permute-start(f32[2,128,128]{2,1,0:T(8,128)S(1)} %get-tuple-element.205), channel_id=1, source_target_pairs={{12,4},{8,0},{13,5},{9,1},{14,6},{10,2},{15,7},{11,3}} | collective-permute-start | bytes 393224 | tf_op jit(solution)/shard_map/ppermute | solution.py:191
  80.6 7.1 %collective-permute-start.42 = (f32[2,128,128]{2,1,0:T(8,128)S(1)}, f32[2,128,128]{2,1,0:T(8,128)S(1)}, u32[]{:S(2)}, u32[]{:S(2)}) collective-permute-start(f32[2,128,128]{2,1,0:T(8,128)S(1)} %get-tuple-element.203), channel_id=1, source_target_pairs={{0,4},{4,0},{8,12},{12,8},{16,20},{20,16},{24,28},{28,24},{1,5},{5... | collective-permute-start | bytes 393224 | tf_op jit(solution)/shard_map/ppermute | solution.py:246
  83.0 6.3 %collective-permute-start.40 = (f32[2,128,128]{2,1,0:T(8,128)S(1)}, f32[2,128,128]{2,1,0:T(8,128)S(1)}, u32[]{:S(2)}, u32[]{:S(2)}) collective-permute-start(f32[2,128,128]{2,1,0:T(8,128)S(1)} %get-tuple-element.201), channel_id=1, source_target_pairs={{0,4},{4,0},{8,12},{12,8},{16,20},{20,16},{24,28},{28,24},{1,5},{5... | collective-permute-start | bytes 393224 | tf_op jit(solution)/shard_map/ppermute | solution.py:246
  85.8 5.0 %collective-permute-start.39 = (f32[2,128,128]{2,1,0:T(8,128)S(1)}, f32[2,128,128]{2,1,0:T(8,128)S(1)}, u32[]{:S(2)}, u32[]{:S(2)}) collective-permute-start(f32[2,128,128]{2,1,0:T(8,128)S(1)} %get-tuple-element.199), channel_id=1, source_target_pairs={{0,4},{4,0},{8,12},{12,8},{16,20},{20,16},{24,28},{28,24},{1,5},{5... | collective-permute-start | bytes 393224 | tf_op jit(solution)/shard_map/ppermute | solution.py:246

commit v12 on v11

--- a/solution.py
+++ b/solution.py
@@ -130,47 +130,46 @@
     return ref[:, pl.ds(pl.multiple_of(base + h * DH, DH), DH)]
 
 
-def query_body(per, half, first, chunks, place, k, v, *refs):
+def query_body(per, half, chunks, place, k, v, *refs):
     qg = refs[-1]
     mask = causal()
     for turn in range(2 * chunks):
         d, sb = refs[turn], refs[2 * chunks + turn]
-        base = (1 - place[0] if turn % 2 else place[0]) * half * DH + (first + turn // 2) * per * DH
+        base = (1 - place[0] if turn % 2 else place[0]) * half * DH + turn // 2 * per * DH
+        scores = [dot(head(d, j), column(v, base, j), 1, 1) for j in range(per)]
+        prior = [dot(head(d, j), sb[j], 1, 1) for j in range(per)]
+        scores = [masked(s, mask) for s in scores]
+        for j, s in enumerate(scores):
+            qg[:, pl.ds(pl.multiple_of(base + j * DH, DH), DH)] = (
+                dot(s, column(k, base, j), 1, 0) + prior[j]).astype(BF16)
+
+
+def final_body(per, half, units, place, q, k, v, *refs):
+    count = len(units)
+    kg, vg = refs[-2], refs[-1]
+    mask = causal(turned=True)
+    used = count
+    for turn, (c, other, terms) in enumerate(units):
+        d, later_in = refs[turn], refs[used:used + terms]
+        used += terms
+        base = (1 - place[0] if other else place[0]) * half * DH + c * per * DH
 
         @pl.when(pl.program_id(0) == turn)
         def _():
-            scores = [dot(head(d, j), column(v, base, j), 1, 1) for j in range(per)]
-            prior = [dot(head(d, j), sb[j], 1, 1) for j in range(per)]
-            scores = [masked(s, mask) for s in scores]
-            for j, s in enumerate(scores):
-                qg[:, j * DH:(j + 1) * DH] = (dot(s, column(k, base, j), 1, 0) + prior[j]).astype(BF16)
-
-
-def final_body(per, half, first, other, chunks, terms, place, q, k, v, *refs):
-    ds, later_in, kg, vg = refs[:chunks], refs[chunks:chunks + chunks * terms], refs[-2], refs[-1]
-    mask = causal(turned=True)
-    heads = range(chunks * per)
-    base = (1 - place[0] if other else place[0]) * half * DH + first * per * DH
-
-    def later(h):
-        state = later_in[h // per * terms][h % per]
-        for n in range(1, terms):
-            state = state + later_in[h // per * terms + n][h % per]
-        return state.astype(BF16)
-
-    outer = [head(ds[h // per], h % per) for h in heads]
-    qs, ks, vs = ([column(a, base, h) for h in heads] for a in (q, k, v))
-    grad = [dot(vs[h], outer[h], 1, 1) for h in heads]
-    score = [dot(ks[h], qs[h], 1, 1) for h in heads]
-    states = [later(h) for h in heads]
-    kg_part = [dot(vs[h], states[h], 1, 1) for h in heads]
-    vg_part = [dot(ks[h], states[h], 1, 0) for h in heads]
-    grad = [masked(x, mask) for x in grad]
-    score = [masked(x, mask) for x in score]
-    for h in heads:
-        at = slice(h * DH, (h + 1) * DH)
-        kg[:, at] = (dot(grad[h], qs[h], 1, 0) + kg_part[h]).astype(BF16)
-        vg[:, at] = (dot(score[h], outer[h], 1, 0) + vg_part[h]).astype(BF16)
+            heads = range(per)
+            states = [sum((t[h] for t in later_in[1:]), later_in[0][h]).astype(BF16) for h in heads]
+            outer = [head(d, h) for h in heads]
+            qs, ks, vs = ([column(a, base, h) for h in heads] for a in (q, k, v))
+            grad = [dot(vs[h], outer[h], 1, 1) for h in heads]
+            score = [dot(ks[h], qs[h], 1, 1) for h in heads]
+            kg_part = [dot(vs[h], states[h], 1, 1) for h in heads]
+            vg_part = [dot(ks[h], states[h], 1, 0) for h in heads]
+            grad = [masked(x, mask) for x in grad]
+            score = [masked(x, mask) for x in score]
+            for h in heads:
+                at = slice(h * DH, (h + 1) * DH)
+                kg[:, at] = (dot(grad[h], qs[h], 1, 0) + kg_part[h]).astype(BF16)
+                vg[:, at] = (dot(score[h], outer[h], 1, 0) + vg_part[h]).astype(BF16)
 
 
 def solution(mesh):
@@ -293,7 +292,6 @@
             )
 
         *kept, local_kept = local(0, CHUNKS, HBM, [])
-        tail = long - 1
         spread = 2 < long <= 4
         before = scan(kept, sent, leads, False, [local_kept], {})
         local_other, = local(1, 0, VMEM, [before[CHUNKS - 1][0]])
@@ -352,64 +350,51 @@
         d_o, sent = d_one + d_two, sent_one + sent_two
         d_k, kept = delta(0, 0, CHUNKS)
 
-        def mine(c):
-            return lambda i, s: (0, jnp.where(i % 2 == 0, s[0], 1 - s[0]) * CHUNKS + c + i // 2)
-
         state3 = (per, DH, DH)
-        made = {"query": [], "rest": []}
-
-        def query(c, count, tie=None):
+
+        def query(tie=None):
             ins = [(a, (tokens, width), whole2) for a in (keys, values)]
-            some = range(c, c + count)
-            grads = [a for i in some for a in (d_k[i], d_o[i])]
+            grads = [a for i in range(CHUNKS) for a in (d_k[i], d_o[i])]
             if tie is not None:
                 grads[0], _ = lax.optimization_barrier((grads[0], tie))
             ins += [(a, block, whole2) for a in grads]
-            ins += [(a, state3, whole3) for i in some for a in priors[i]]
+            ins += [(a, state3, whole3) for i in range(CHUNKS) for a in priors[i]]
+            made = call(
+                functools.partial(query_body, per, half, CHUNKS), place, ins,
+                [((tokens, width), BF16, (tokens, width), whole2, VMEM)])
+            query_made.extend(made)
+            return made[0]
+
+        def rest(units, after, made):
+            states = [after[c][2:] if other else after[c][:2] for c, other in units]
+
+            def index(i, s):
+                at = 0
+                for n, (c, other) in enumerate(units):
+                    at = jnp.where(i == n, (1 - s[0] if other else s[0]) * CHUNKS + c, at)
+                return (0, at)
+
+            ins = [(a, (tokens, width), whole2) for a in (queries, keys, values)]
+            ins += [((d_o if other else d_k)[c], block, whole2) for c, other in units]
+            ins += [(a, state3, whole3) for some in states for a in some]
             aliases = {}
-            if made["query"]:
-                aliases[len(ins) + 1] = 0
-                ins += [(a, None, None, HBM) for a in made["query"]]
-            made["query"] = call(
-                functools.partial(query_body, per, half, c, count), place, ins,
-                [((tokens, width), BF16, block, mine(c), HBM)], grid=(2 * count,), aliases=aliases)
-            return made["query"][0]
-
-        def rest(c, which, after, count=1):
-            steps = CHUNKS // count
-            index = lambda i, s: (0, (1 - s[0] if which else s[0]) * steps + c // count)
-            wider = (tokens, narrow * count)
-            some = range(c, c + count)
-            states = [a for i in some for a in (after[i][2:] if which else after[i][:2])]
-            ins = [(a, (tokens, width), whole2) for a in (queries, keys, values)]
-            ins += [((d_o if which else d_k)[i], block, whole2) for i in some]
-            ins += [(a, state3, whole3) for a in states]
-            aliases = {}
-            if made["rest"]:
+            if made:
                 aliases = {len(ins) + 1: 0, len(ins) + 2: 1}
-                ins += [(a, None, None, HBM) for a in made["rest"]]
-            made["rest"] = call(
-                functools.partial(final_body, per, half, c, which, count, len(states) // count), place, ins,
-                [((tokens, width), BF16, wider, index, HBM)] * 2, aliases=aliases)
-            return made["rest"][0]
-
-        beside = {
-            (2, 0): lambda out, sends: query(0, 2, sends[1, 1]),
-            (tail, 0): lambda out, sends: query(2, 1, sends[2, 1]),
-            (tail, 1): lambda out, sends: query(3, 1),
-            (tail, 2): lambda out, sends: rest(0, 0, out, 2),
-            (tail, 3): lambda out, sends: rest(2, 0, out),
-        } if spread else {}
+                ins += [(a, None, None, HBM) for a in made]
+            kinds = [(c, other, len(some)) for (c, other), some in zip(units, states)]
+            return call(
+                functools.partial(final_body, per, half, kinds), place, ins,
+                [((tokens, width), BF16, block, index, HBM)] * 2, grid=(len(units),), aliases=aliases)
+
+        query_made = []
+        beside = {(2, 0): lambda out, sends: query(sends[1, 1])} if spread else {}
         after = scan(kept, sent, ends, True, [], beside)
         if not spread:
-            query(0, CHUNKS)
-            rest(0, 0, after, 2)
-            rest(2, 0, after)
-        rest(3, 0, after)
-        rest(0, 1, after, 2)
-        rest(2, 1, after)
-        rest(3, 1, after)
-        return made["query"][0], made["rest"][0], made["rest"][1]
+            query()
+        made = rest([(c, 0) for c in range(CHUNKS)] + [(c, 1) for c in range(CHUNKS - 2)], after, [])
+        for c in range(CHUNKS - 2, CHUNKS):
+            made = rest([(c, 1)], after, made)
+        return query_made[0], made[0], made[1]
 
     return jax.shard_map(
         shards,

time: 92.7 us -> 96.4 us (1.040)
  waiting for transfers between devices: 19.6 us -> 27 us
  Pallas kernels: 23 us -> 17.9 us
  local copies, waits for them, and re-layouts: 0.08 us -> 1.05 us
    ppermute x24, waiting for transfers between devices: 6.67 us -> 14.3 us  [hop(): return lax.ppermute(array, 'seq', pairs)]
    pallas_call x20 -> x15, Pallas kernels: 23 us -> 17.9 us  [call(): pl.pallas_call(body, grid_spec=pltpu.PrefetchScalarGridSpec(num_scalar_pr...]
    unnamed x10 -> x11, local copies, waits for them, and re-layouts: 0.08 us -> 1.05 us
  transfers between devices with their start and end apart: 43 -> 43, of which waited for: 13 -> 14; matrix products, arithmetic and copies ran while one was open for 1% -> 2% of each run, Pallas kernels for 21% -> 15%
where the time goes in v12:
time: 96.4 us; the launch traced here: 95.8 us
  starting transfers between devices  47.8 us (50%)
  waiting for transfers between devices  27 us (28%)
  Pallas kernels  17.9 us (19%)
  between operations  1.32 us (1%)
  local copies, waits for them, and re-layouts  1.05 us (1%)
    ppermute x24, starting transfers between devices, hop(): return lax.ppermute(array, 'seq', pairs)  25.2 us
    pallas_call x15, Pallas kernels, call(): pl.pallas_call(body, grid_spec=pltpu.PrefetchScalarGridSpec(num_scalar_pr...  17.9 us
    ppermute x24, waiting for transfers between devices, hop(): return lax.ppermute(array, 'seq', pairs)  14.3 us
    ppermute x8, starting transfers between devices, swap_after(): flight[c] = lax.ppermute(part_sent, 'seq', swap)  11.6 us
    ppermute x8, starting transfers between devices, scan(): out[c] = (carry[c], own[c], lax.ppermute(send, 'seq', swap))  9.18 us
    ppermute x8, waiting for transfers between devices, swap_after(): flight[c] = lax.ppermute(part_sent, 'seq', swap)  6.68 us
    ppermute x8, waiting for transfers between devices, scan(): out[c] = (carry[c], own[c], lax.ppermute(send, 'seq', swap))  4.22 us
  transfers between devices with their start and end apart: 43, of which 14 were waited for; matrix products, arithmetic and copies ran while one was open for 2% of the time, Pallas kernels for 15%

profile of v12, /device:TPU:0, one launch (start us, length us, event | category | flops | bytes accessed | tf_op | source)
XLA Modules:
  0.0 95.8 jit_solution(14520571092207522732)
XLA Ops:
  0.6 1.3 %shard_map.78 = (f32[2,128,128]{2,1,0:T(8,128)S(1)}, f32[2,128,128]{2,1,0:T(8,128)S(1)}) custom-call(s32[1]{0:T(128)} %bitcast.place, bf16[256,2048]{1,0:T(8,128)(2,1)} %k.11, bf16[256,2048]{1,0:T(8,128)(2,1)} %v.11), custom_call_target="tpu_custom_call" | custom-call | flops 1024 | bytes 1024 | tf_op jit(solution)/shard_map/pallas_call | solution.py:43
  2.0 3.0 %collective-permute-start = (f32[2,128,128]{2,1,0:T(8,128)S(1)}, f32[2,128,128]{2,1,0:T(8,128)S(1)}, u32[]{:S(2)}, u32[]{:S(2)}) collective-permute-start(f32[2,128,128]{2,1,0:T(8,128)S(1)} %get-tuple-element.99), channel_id=1, source_target_pairs={{0,4},{4,0},{8,12},{12,8},{16,20},{20,16},{24,28},{28,24},{1,5},{5... | collective-permute-start | bytes 393224 | tf_op jit(solution)/shard_map/ppermute | solution.py:225
  5.1 1.3 %shard_map.77 = (f32[2,128,128]{2,1,0:T(8,128)S(1)}, f32[2,128,128]{2,1,0:T(8,128)S(1)}) custom-call(s32[1]{0:T(128)} %bitcast.place, bf16[256,2048]{1,0:T(8,128)(2,1)} %k.11, bf16[256,2048]{1,0:T(8,128)(2,1)} %v.11), custom_call_target="tpu_custom_call" | custom-call | flops 1024 | bytes 1024 | tf_op jit(solution)/shard_map/pallas_call | solution.py:43
  6.4 2.0 %collective-permute-start.3 = (f32[2,128,128]{2,1,0:T(8,128)S(1)}, f32[2,128,128]{2,1,0:T(8,128)S(1)}, u32[]{:S(2)}, u32[]{:S(2)}) collective-permute-start(f32[2,128,128]{2,1,0:T(8,128)S(1)} %get-tuple-element.103), channel_id=1, source_target_pairs={{0,4},{4,0},{8,12},{12,8},{16,20},{20,16},{24,28},{28,24},{1,5},{5... | collective-permute-start | bytes 393224 | tf_op jit(solution)/shard_map/ppermute | solution.py:225
  8.4 2.6 %shard_map.76 = (f32[2,128,128]{2,1,0:T(8,128)S(1)}, f32[2,128,128]{2,1,0:T(8,128)S(1)}, f32[2,128,128]{2,1,0:T(8,128)S(1)}, f32[2,128,128]{2,1,0:T(8,128)S(1)}, f32[256,1024]{1,0:T(8,128)S(1)}) custom-call(s32[1]{0:T(128)} %bitcast.place, bf16[256,2048]{1,0:T(8,128)(2,1)} %q.9, bf16[256,2048]{1,0:T(8,128)(2,1)} %k.11, bf16[256,2048]{1,0:T(8,128)(2,1)} %v.11), custom_call_target="tpu_custom_call" | custom-call | flops 1024 | bytes 1024 | tf_op jit(solution)/shard_map/pallas_call | solution.py:43
  11.1 3.5 %collective-permute-start.2 = (f32[2,128,128]{2,1,0:T(8,128)S(1)}, f32[2,128,128]{2,1,0:T(8,128)S(1)}, u32[]{:S(2)}, u32[]{:S(2)}) collective-permute-start(f32[2,128,128]{2,1,0:T(8,128)S(1)} %get-tuple-element.226), channel_id=1, source_target_pairs={{0,8},{4,12},{1,9},{5,13},{2,10},{6,14},{3,11},{7,15}} | collective-permute-start | bytes 393224 | tf_op jit(solution)/shard_map/ppermute | solution.py:190
  14.6 1.6 %collective-permute-start.8 = (f32[2,128,128]{2,1,0:T(8,128)S(1)}, f32[2,128,128]{2,1,0:T(8,128)S(1)}, u32[]{:S(2)}, u32[]{:S(2)}) collective-permute-start(f32[2,128,128]{2,1,0:T(8,128)S(1)} %get-tuple-element.228), channel_id=1, source_target_pairs={{0,8},{4,12},{1,9},{5,13},{2,10},{6,14},{3,11},{7,15}} | collective-permute-start | bytes 393224 | tf_op jit(solution)/shard_map/ppermute | solution.py:190
  16.2 1.6 %collective-permute-start.1 = (f32[2,128,128]{2,1,0:T(8,128)S(1)}, f32[2,128,128]{2,1,0:T(8,128)S(1)}, u32[]{:S(2)}, u32[]{:S(2)}) collective-permute-start(f32[2,128,128]{2,1,0:T(8,128)S(1)} %get-tuple-element.101), channel_id=1, source_target_pairs={{0,4},{4,0},{8,12},{12,8},{16,20},{20,16},{24,28},{28,24},{1,5},{5... | collective-permute-start | bytes 393224 | tf_op jit(solution)/shard_map/ppermute | solution.py:225
  17.8 1.6 %collective-permute-start.7 = (f32[2,128,128]{2,1,0:T(8,128)S(1)}, f32[2,128,128]{2,1,0:T(8,128)S(1)}, u32[]{:S(2)}, u32[]{:S(2)}) collective-permute-start(f32[2,128,128]{2,1,0:T(8,128)S(1)} %get-tuple-element.230), channel_id=1, source_target_pairs={{0,8},{4,12},{1,9},{5,13},{2,10},{6,14},{3,11},{7,15}} | collective-permute-start | bytes 393224 | tf_op jit(solution)/shard_map/ppermute | solution.py:190
  20.1 1.2 %collective-permute-done.1 = f32[2,128,128]{2,1,0:T(8,128)S(1)} collective-permute-done((f32[2,128,128]{2,1,0:T(8,128)S(1)}, f32[2,128,128]{2,1,0:T(8,128)S(1)}, u32[]{:S(2)}, u32[]{:S(2)}) %collective-permute-start.1) | collective-permute-done | bytes 131104 | tf_op jit(solution)/shard_map/ppermute | solution.py:225
  21.2 2.4 %collective-permute-start.5 = (f32[2,128,128]{2,1,0:T(8,128)S(1)}, f32[2,128,128]{2,1,0:T(8,128)S(1)}, u32[]{:S(2)}, u32[]{:S(2)}) collective-permute-start(f32[2,128,128]{2,1,0:T(8,128)S(1)} %get-tuple-element.232), channel_id=1, source_target_pairs={{0,8},{4,12},{1,9},{5,13},{2,10},{6,14},{3,11},{7,15}} | collective-permute-start | bytes 393224 | tf_op jit(solution)/shard_map/ppermute | solution.py:190
  24.4 0.7 collective-permute-start.11
  27.6 0.7 collective-permute-start.14
  28.3 0.8 collective-permute-start.19
  29.1 0.8 collective-permute-start.13
  30.0 1.4 %collective-permute-start.18 = (f32[2,128,128]{2,1,0:T(8,128)S(1)}, f32[2,128,128]{2,1,0:T(8,128)S(1)}, u32[]{:S(2)}, u32[]{:S(2)}) collective-permute-start(f32[2,128,128]{2,1,0:T(8,128)S(1)} %get-tuple-element.205), channel_id=1, source_target_pairs={{0,4},{4,0},{8,12},{12,8},{16,20},{20,16},{24,28},{28,24},{1,5},{5... | collective-permute-start | bytes 393224 | tf_op jit(solution)/shard_map/ppermute | solution.py:245
  31.4 0.8 collective-permute-start.17
  32.2 1.4 %collective-permute-start.16 = (f32[2,128,128]{2,1,0:T(8,128)S(1)}, f32[2,128,128]{2,1,0:T(8,128)S(1)}, u32[]{:S(2)}, u32[]{:S(2)}) collective-permute-start(f32[2,128,128]{2,1,0:T(8,128)S(1)} %get-tuple-element.201), channel_id=1, source_target_pairs={{0,4},{4,0},{8,12},{12,8},{16,20},{20,16},{24,28},{28,24},{1,5},{5... | collective-permute-start | bytes 393224 | tf_op jit(solution)/shard_map/ppermute | solution.py:245
  33.7 1.1 %shard_map.79.al_o = f32[256,1024]{1,0:T(8,128)S(1)} custom-call(s32[1]{0:T(128)} %bitcast.place, bf16[256,2048]{1,0:T(8,128)(2,1)S(1)} %copy-done, bf16[256,2048]{1,0:T(8,128)(2,1)S(1)} %copy-done.2, bf16[256,2048]{1,0:T(8,128)(2,1)S(1)} %copy-done.3, f32[2,128,128]{2,1,0:T(8,128)S(1)} %get-tuple-element.202.refs_0_.e), custom_call_target="tpu_custom_call" | custom-call | flops 1024 | bytes 1024 | tf_op jit(solution)/shard_map/pallas_call | solution.py:43
  35.2 2.0 %collective-permute-done.18.other = f32[2,128,128]{2,1,0:T(8,128)S(1)} collective-permute-done((f32[2,128,128]{2,1,0:T(8,128)S(1)}, f32[2,128,128]{2,1,0:T(8,128)S(1)}, u32[]{:S(2)}, u32[]{:S(2)}) %collective-permute-start.18) | collective-permute-done | bytes 131104 | tf_op jit(solution)/shard_map/ppermute | solution.py:245
  37.5 1.1 %collective-permute-done.17.other = f32[2,128,128]{2,1,0:T(8,128)S(1)} collective-permute-done((f32[2,128,128]{2,1,0:T(8,128)S(1)}, f32[2,128,128]{2,1,0:T(8,128)S(1)}, u32[]{:S(2)}, u32[]{:S(2)}) %collective-permute-start.17) | collective-permute-done | bytes 131104 | tf_op jit(solution)/shard_map/ppermute | solution.py:245
  38.9 1.1 %collective-permute-done.16.other = f32[2,128,128]{2,1,0:T(8,128)S(1)} collective-permute-done((f32[2,128,128]{2,1,0:T(8,128)S(1)}, f32[2,128,128]{2,1,0:T(8,128)S(1)}, u32[]{:S(2)}, u32[]{:S(2)}) %collective-permute-start.16) | collective-permute-done | bytes 131104 | tf_op jit(solution)/shard_map/ppermute | solution.py:245
  40.5 1.6 %collective-permute-start.21 = (f32[2,256]{1,0:T(2,128)S(1)}, f32[2,256]{1,0:T(2,128)S(1)}, u32[]{:S(2)}, u32[]{:S(2)}) collective-permute-start(f32[2,256]{1,0:T(2,128)S(1)} %get-tuple-element.128.refs_0_), channel_id=1, source_target_pairs={{0,2},{1,3},{2,0},{3,1},{4,6},{5,7},{6,4},{7,5},{8,10},{9,11},{10,... | collective-permute-start | bytes 6152 | tf_op jit(solution)/shard_map/ppermute | solution.py:333
  42.3 1.1 %collective-permute-done.22.refs_3_ = f32[2,256]{1,0:T(2,128)S(1)} collective-permute-done((f32[2,256]{1,0:T(2,128)S(1)}, f32[2,256]{1,0:T(2,128)S(1)}, u32[]{:S(2)}, u32[]{:S(2)}) %collective-permute-start.22) | collective-permute-done | bytes 2080 | tf_op jit(solution)/shard_map/ppermute | solution.py:333
  44.5 1.4 %collective-permute-start.24 = (f32[2,128,128]{2,1,0:T(8,128)S(1)}, f32[2,128,128]{2,1,0:T(8,128)S(1)}, u32[]{:S(2)}, u32[]{:S(2)}) collective-permute-start(f32[2,128,128]{2,1,0:T(8,128)S(1)} %get-tuple-element.139), channel_id=1, source_target_pairs={{0,4},{4,0},{8,12},{12,8},{16,20},{20,16},{24,28},{28,24},{1,5},{5... | collective-permute-start | bytes 393224 | tf_op jit(solution)/shard_map/ppermute | solution.py:225
  46.4 0.8 collective-permute-start.28
  47.1 1.3 %collective-permute-start.23 = (f32[2,128,128]{2,1,0:T(8,128)S(1)}, f32[2,128,128]{2,1,0:T(8,128)S(1)}, u32[]{:S(2)}, u32[]{:S(2)}) collective-permute-start(f32[2,128,128]{2,1,0:T(8,128)S(1)} %get-tuple-element.137), channel_id=1, source_target_pairs={{0,4},{4,0},{8,12},{12,8},{16,20},{20,16},{24,28},{28,24},{1,5},{5... | collective-permute-start | bytes 393224 | tf_op jit(solution)/shard_map/ppermute | solution.py:225
  49.1 1.8 %collective-permute-done.24 = f32[2,128,128]{2,1,0:T(8,128)S(1)} collective-permute-done((f32[2,128,128]{2,1,0:T(8,128)S(1)}, f32[2,128,128]{2,1,0:T(8,128)S(1)}, u32[]{:S(2)}, u32[]{:S(2)}) %collective-permute-start.24) | collective-permute-done | bytes 131104 | tf_op jit(solution)/shard_map/ppermute | solution.py:225
  51.6 1.4 %collective-permute-start.26 = (f32[2,128,128]{2,1,0:T(8,128)S(1)}, f32[2,128,128]{2,1,0:T(8,128)S(1)}, u32[]{:S(2)}, u32[]{:S(2)}) collective-permute-start(f32[2,128,128]{2,1,0:T(8,128)S(1)} %get-tuple-element.145), channel_id=1, source_target_pairs={{0,4},{4,0},{8,12},{12,8},{16,20},{20,16},{24,28},{28,24},{1,5},{5... | collective-permute-start | bytes 393224 | tf_op jit(solution)/shard_map/ppermute | solution.py:225
  53.0 3.5 %collective-permute-done.23 = f32[2,128,128]{2,1,0:T(8,128)S(1)} collective-permute-done((f32[2,128,128]{2,1,0:T(8,128)S(1)}, f32[2,128,128]{2,1,0:T(8,128)S(1)}, u32[]{:S(2)}, u32[]{:S(2)}) %collective-permute-start.23) | collective-permute-done | bytes 131104 | tf_op jit(solution)/shard_map/ppermute | solution.py:225
  56.6 0.7 collective-permute-start.25
  57.3 0.7 collective-permute-start.31
  60.9 1.8 %shard_map.87 = bf16[256,2048]{1,0:T(8,128)(2,1)S(1)} custom-call(s32[1]{0:T(128)} %bitcast.place, bf16[256,2048]{1,0:T(8,128)(2,1)S(1)} %copy-done.2, bf16[256,2048]{1,0:T(8,128)(2,1)S(1)} %copy-done.3, bf16[256,256]{1,0:T(8,128)(2,1)S(1)} %get-tuple-element.152.refs_0_, bf16[256,256]{1,0:T(8,128)(2,1)S(1)} %get-tuple-element.153.refs_1_.refs_4_, ...), custom_call_target="tpu_custom_call" | custom-call | flops 1024 | bytes 1024 | tf_op jit(solution)/shard_map/pallas_call | solution.py:43
  62.8 1.3 %collective-permute-start.33 = (f32[2,128,128]{2,1,0:T(8,128)S(1)}, f32[2,128,128]{2,1,0:T(8,128)S(1)}, u32[]{:S(2)}, u32[]{:S(2)}) collective-permute-start(f32[2,128,128]{2,1,0:T(8,128)S(1)} %get-tuple-element.199), channel_id=1, source_target_pairs={{12,4},{8,0},{13,5},{9,1},{14,6},{10,2},{15,7},{11,3}} | collective-permute-start | bytes 393224 | tf_op jit(solution)/shard_map/ppermute | solution.py:190
  64.9 1.3 %collective-permute-start.38 = (f32[2,128,128]{2,1,0:T(8,128)S(1)}, f32[2,128,128]{2,1,0:T(8,128)S(1)}, u32[]{:S(2)}, u32[]{:S(2)}) collective-permute-start(f32[2,128,128]{2,1,0:T(8,128)S(1)} %get-tuple-element.197), channel_id=1, source_target_pairs={{12,4},{8,0},{13,5},{9,1},{14,6},{10,2},{15,7},{11,3}} | collective-permute-start | bytes 393224 | tf_op jit(solution)/shard_map/ppermute | solution.py:190
  66.2 1.3 %collective-permute-start.37 = (f32[2,128,128]{2,1,0:T(8,128)S(1)}, f32[2,128,128]{2,1,0:T(8,128)S(1)}, u32[]{:S(2)}, u32[]{:S(2)}) collective-permute-start(f32[2,128,128]{2,1,0:T(8,128)S(1)} %get-tuple-element.195), channel_id=1, source_target_pairs={{12,4},{8,0},{13,5},{9,1},{14,6},{10,2},{15,7},{11,3}} | collective-permute-start | bytes 393224 | tf_op jit(solution)/shard_map/ppermute | solution.py:190
  67.5 8.3 %collective-permute-done.33 = f32[2,128,128]{2,1,0:T(8,128)S(1)} collective-permute-done((f32[2,128,128]{2,1,0:T(8,128)S(1)}, f32[2,128,128]{2,1,0:T(8,128)S(1)}, u32[]{:S(2)}, u32[]{:S(2)}) %collective-permute-start.33) | collective-permute-done | bytes 131104 | tf_op jit(solution)/shard_map/ppermute | solution.py:190
  75.9 1.2 %collective-permute-start.41 = (f32[2,128,128]{2,1,0:T(8,128)S(1)}, f32[2,128,128]{2,1,0:T(8,128)S(1)}, u32[]{:S(2)}, u32[]{:S(2)}) collective-permute-start(f32[2,128,128]{2,1,0:T(8,128)S(1)} %get-tuple-element.193), channel_id=1, source_target_pairs={{0,4},{4,0},{8,12},{12,8},{16,20},{20,16},{24,28},{28,24},{1,5},{5... | collective-permute-start | bytes 393224 | tf_op jit(solution)/shard_map/ppermute | solution.py:245
  77.1 1.5 %collective-permute-start.36 = (f32[2,128,128]{2,1,0:T(8,128)S(1)}, f32[2,128,128]{2,1,0:T(8,128)S(1)}, u32[]{:S(2)}, u32[]{:S(2)}) collective-permute-start(f32[2,128,128]{2,1,0:T(8,128)S(1)} %get-tuple-element.191), channel_id=1, source_target_pairs={{12,4},{8,0},{13,5},{9,1},{14,6},{10,2},{15,7},{11,3}} | collective-permute-start | bytes 393224 | tf_op jit(solution)/shard_map/ppermute | solution.py:190
  78.6 1.6 %collective-permute-done.38 = f32[2,128,128]{2,1,0:T(8,128)S(1)} collective-permute-done((f32[2,128,128]{2,1,0:T(8,128)S(1)}, f32[2,128,128]{2,1,0:T(8,128)S(1)}, u32[]{:S(2)}, u32[]{:S(2)}) %collective-permute-start.38) | collective-permute-done | bytes 131104 | tf_op jit(solution)/shard_map/ppermute | solution.py:190
  80.2 1.2 %collective-permute-start.42 = (f32[2,128,128]{2,1,0:T(8,128)S(1)}, f32[2,128,128]{2,1,0:T(8,128)S(1)}, u32[]{:S(2)}, u32[]{:S(2)}) collective-permute-start(f32[2,128,128]{2,1,0:T(8,128)S(1)} %get-tuple-element.189), channel_id=1, source_target_pairs={{0,4},{4,0},{8,12},{12,8},{16,20},{20,16},{24,28},{28,24},{1,5},{5... | collective-permute-start | bytes 393224 | tf_op jit(solution)/shard_map/ppermute | solution.py:245
  81.4 3.4 %collective-permute-done.37 = f32[2,128,128]{2,1,0:T(8,128)S(1)} collective-permute-done((f32[2,128,128]{2,1,0:T(8,128)S(1)}, f32[2,128,128]{2,1,0:T(8,128)S(1)}, u32[]{:S(2)}, u32[]{:S(2)}) %collective-permute-start.37) | collective-permute-done | bytes 131104 | tf_op jit(solution)/shard_map/ppermute | solution.py:190
  84.8 1.2 %collective-permute-start.40 = (f32[2,128,128]{2,1,0:T(8,128)S(1)}, f32[2,128,128]{2,1,0:T(8,128)S(1)}, u32[]{:S(2)}, u32[]{:S(2)}) collective-permute-start(f32[2,128,128]{2,1,0:T(8,128)S(1)} %get-tuple-element.187), channel_id=1, source_target_pairs={{0,4},{4,0},{8,12},{12,8},{16,20},{20,16},{24,28},{28,24},{1,5},{5... | collective-permute-start | bytes 393224 | tf_op jit(solution)/shard_map/ppermute | solution.py:245
  86.7 1.2 %collective-permute-start.39 = (f32[2,128,128]{2,1,0:T(8,128)S(1)}, f32[2,128,128]{2,1,0:T(8,128)S(1)}, u32[]{:S(2)}, u32[]{:S(2)}) collective-permute-start(f32[2,128,128]{2,1,0:T(8,128)S(1)} %get-tuple-element.185), channel_id=1, source_target_pairs={{0,4},{4,0},{8,12},{12,8},{16,20},{20,16},{24,28},{28,24},{1,5},{5... | collective-permute-start | bytes 393224 | tf_op jit(solution)/shard_map/ppermute | solution.py:245
  87.9 1.0 %copy.16 = bf16[256,2048]{1,0:T(8,128)(2,1)} copy(bf16[256,2048]{1,0:T(8,128)(2,1)S(1)} %shard_map.87) | data formatting | bytes 2097152
  88.9 4.5 %shard_map.88 = (bf16[256,2048]{1,0:T(8,128)(2,1)}, bf16[256,2048]{1,0:T(8,128)(2,1)}) custom-call(s32[1]{0:T(128)} %bitcast.place, bf16[256,2048]{1,0:T(8,128)(2,1)S(1)} %copy-done, bf16[256,2048]{1,0:T(8,128)(2,1)S(1)} %copy-done.2, bf16[256,2048]{1,0:T(8,128)(2,1)S(1)} %copy-done.3, bf16[256,256]{1,0:T(8,128)(2,1)S(1)} %get-tuple-element.152.refs_0_, ...), custom_call_target="tpu_custom_call" | custom-call | flops 1024 | bytes 1024 | tf_op jit(solution)/shard_map/pallas_call | solution.py:43
  93.4 1.2 %shard_map.89 = (bf16[256,2048]{1,0:T(8,128)(2,1)}, bf16[256,2048]{1,0:T(8,128)(2,1)}) custom-call(s32[1]{0:T(128)} %bitcast.place, bf16[256,2048]{1,0:T(8,128)(2,1)S(1)} %copy-done, bf16[256,2048]{1,0:T(8,128)(2,1)S(1)} %copy-done.2, bf16[256,2048]{1,0:T(8,128)(2,1)S(1)} %copy-done.3, ...), custom_call_target="tpu_custom_call", output_to_operand_aliasing={{0}: (6, {}), {1}: (7, {})} | custom-call | flops 1024 | bytes 1024 | tf_op jit(solution)/shard_map/pallas_call | solution.py:43
  94.6 1.2 %shard_map.90 = (bf16[256,2048]{1,0:T(8,128)(2,1)}, bf16[256,2048]{1,0:T(8,128)(2,1)}) custom-call(s32[1]{0:T(128)} %bitcast.place, bf16[256,2048]{1,0:T(8,128)(2,1)S(1)} %copy-done, bf16[256,2048]{1,0:T(8,128)(2,1)S(1)} %copy-done.2, bf16[256,2048]{1,0:T(8,128)(2,1)S(1)} %copy-done.3, ...), custom_call_target="tpu_custom_call", output_to_operand_aliasing={{0}: (6, {}), {1}: (7, {})} | custom-call | flops 1024 | bytes 1024 | tf_op jit(solution)/shard_map/pallas_call | solution.py:43
  (97 shorter events, 13.2 us)
Async XLA Ops:
  2.0 9.1 %collective-permute-start = (f32[2,128,128]{2,1,0:T(8,128)S(1)}, f32[2,128,128]{2,1,0:T(8,128)S(1)}, u32[]{:S(2)}, u32[]{:S(2)}) collective-permute-start(f32[2,128,128]{2,1,0:T(8,128)S(1)} %get-tuple-element.99), channel_id=1, source_target_pairs={{0,4},{4,0},{8,12},{12,8},{16,20},{20,16},{24,28},{28,24},{1,5},{5... | collective-permute-start | bytes 393224 | tf_op jit(solution)/shard_map/ppermute | solution.py:225
  5.0 9.6 %collective-permute-start.4 = (f32[2,128,128]{2,1,0:T(8,128)S(1)}, f32[2,128,128]{2,1,0:T(8,128)S(1)}, u32[]{:S(2)}, u32[]{:S(2)}) collective-permute-start(f32[2,128,128]{2,1,0:T(8,128)S(1)} %get-tuple-element.105), channel_id=1, source_target_pairs={{0,4},{4,0},{8,12},{12,8},{16,20},{20,16},{24,28},{28,24},{1,5},{5... | collective-permute-start | bytes 393224 | tf_op jit(solution)/shard_map/ppermute | solution.py:225
  6.4 9.8 %collective-permute-start.3 = (f32[2,128,128]{2,1,0:T(8,128)S(1)}, f32[2,128,128]{2,1,0:T(8,128)S(1)}, u32[]{:S(2)}, u32[]{:S(2)}) collective-permute-start(f32[2,128,128]{2,1,0:T(8,128)S(1)} %get-tuple-element.103), channel_id=1, source_target_pairs={{0,4},{4,0},{8,12},{12,8},{16,20},{20,16},{24,28},{28,24},{1,5},{5... | collective-permute-start | bytes 393224 | tf_op jit(solution)/shard_map/ppermute | solution.py:225
  11.1 8.3 %collective-permute-start.2 = (f32[2,128,128]{2,1,0:T(8,128)S(1)}, f32[2,128,128]{2,1,0:T(8,128)S(1)}, u32[]{:S(2)}, u32[]{:S(2)}) collective-permute-start(f32[2,128,128]{2,1,0:T(8,128)S(1)} %get-tuple-element.226), channel_id=1, source_target_pairs={{0,8},{4,12},{1,9},{5,13},{2,10},{6,14},{3,11},{7,15}} | collective-permute-start | bytes 393224 | tf_op jit(solution)/shard_map/ppermute | solution.py:190
  14.6 9.0 %collective-permute-start.8 = (f32[2,128,128]{2,1,0:T(8,128)S(1)}, f32[2,128,128]{2,1,0:T(8,128)S(1)}, u32[]{:S(2)}, u32[]{:S(2)}) collective-permute-start(f32[2,128,128]{2,1,0:T(8,128)S(1)} %get-tuple-element.228), channel_id=1, source_target_pairs={{0,8},{4,12},{1,9},{5,13},{2,10},{6,14},{3,11},{7,15}} | collective-permute-start | bytes 393224 | tf_op jit(solution)/shard_map/ppermute | solution.py:190
  16.2 5.0 %collective-permute-start.1 = (f32[2,128,128]{2,1,0:T(8,128)S(1)}, f32[2,128,128]{2,1,0:T(8,128)S(1)}, u32[]{:S(2)}, u32[]{:S(2)}) collective-permute-start(f32[2,128,128]{2,1,0:T(8,128)S(1)} %get-tuple-element.101), channel_id=1, source_target_pairs={{0,4},{4,0},{8,12},{12,8},{16,20},{20,16},{24,28},{28,24},{1,5},{5... | collective-permute-start | bytes 393224 | tf_op jit(solution)/shard_map/ppermute | solution.py:225
  17.8 6.5 %collective-permute-start.7 = (f32[2,128,128]{2,1,0:T(8,128)S(1)}, f32[2,128,128]{2,1,0:T(8,128)S(1)}, u32[]{:S(2)}, u32[]{:S(2)}) collective-permute-start(f32[2,128,128]{2,1,0:T(8,128)S(1)} %get-tuple-element.230), channel_id=1, source_target_pairs={{0,8},{4,12},{1,9},{5,13},{2,10},{6,14},{3,11},{7,15}} | collective-permute-start | bytes 393224 | tf_op jit(solution)/shard_map/ppermute | solution.py:190
  19.4 5.7 %collective-permute-start.6 = (f32[2,128,128]{2,1,0:T(8,128)S(1)}, f32[2,128,128]{2,1,0:T(8,128)S(1)}, u32[]{:S(2)}, u32[]{:S(2)}) collective-permute-start(f32[2,128,128]{2,1,0:T(8,128)S(1)} %add.152), channel_id=1, source_target_pairs={{8,16},{12,20},{9,17},{13,21},{10,18},{14,22},{11,19},{15,23}} | collective-permute-start | bytes 393224 | tf_op jit(solution)/shard_map/ppermute | solution.py:190
  21.2 4.9 %collective-permute-start.5 = (f32[2,128,128]{2,1,0:T(8,128)S(1)}, f32[2,128,128]{2,1,0:T(8,128)S(1)}, u32[]{:S(2)}, u32[]{:S(2)}) collective-permute-start(f32[2,128,128]{2,1,0:T(8,128)S(1)} %get-tuple-element.232), channel_id=1, source_target_pairs={{0,8},{4,12},{1,9},{5,13},{2,10},{6,14},{3,11},{7,15}} | collective-permute-start | bytes 393224 | tf_op jit(solution)/shard_map/ppermute | solution.py:190
  23.7 3.2 %collective-permute-start.12 = (f32[2,128,128]{2,1,0:T(8,128)S(1)}, f32[2,128,128]{2,1,0:T(8,128)S(1)}, u32[]{:S(2)}, u32[]{:S(2)}) collective-permute-start(f32[2,128,128]{2,1,0:T(8,128)S(1)} %add.154), channel_id=1, source_target_pairs={{8,16},{12,20},{9,17},{13,21},{10,18},{14,22},{11,19},{15,23}} | collective-permute-start | bytes 393224 | tf_op jit(solution)/shard_map/ppermute | solution.py:190
  24.4 3.2 %collective-permute-start.11 = (f32[2,128,128]{2,1,0:T(8,128)S(1)}, f32[2,128,128]{2,1,0:T(8,128)S(1)}, u32[]{:S(2)}, u32[]{:S(2)}) collective-permute-start(f32[2,128,128]{2,1,0:T(8,128)S(1)} %add.155), channel_id=1, source_target_pairs={{8,16},{12,20},{9,17},{13,21},{10,18},{14,22},{11,19},{15,23}} | collective-permute-start | bytes 393224 | tf_op jit(solution)/shard_map/ppermute | solution.py:190
  25.1 3.2 %collective-permute-start.10 = (f32[2,128,128]{2,1,0:T(8,128)S(1)}, f32[2,128,128]{2,1,0:T(8,128)S(1)}, u32[]{:S(2)}, u32[]{:S(2)}) collective-permute-start(f32[2,128,128]{2,1,0:T(8,128)S(1)} %get-tuple-element.215), channel_id=1, source_target_pairs={{16,24},{20,28},{17,25},{21,29},{18,26},{22,30},{19,27},{23,31}} | collective-permute-start | bytes 393224 | tf_op jit(solution)/shard_map/ppermute | solution.py:190
  26.1 2.9 %collective-permute-start.9 = (f32[2,128,128]{2,1,0:T(8,128)S(1)}, f32[2,128,128]{2,1,0:T(8,128)S(1)}, u32[]{:S(2)}, u32[]{:S(2)}) collective-permute-start(f32[2,128,128]{2,1,0:T(8,128)S(1)} %add.158), channel_id=1, source_target_pairs={{8,16},{12,20},{9,17},{13,21},{10,18},{14,22},{11,19},{15,23}} | collective-permute-start | bytes 393224 | tf_op jit(solution)/shard_map/ppermute | solution.py:190
  26.9 3.1 %collective-permute-start.15 = (f32[2,128,128]{2,1,0:T(8,128)S(1)}, f32[2,128,128]{2,1,0:T(8,128)S(1)}, u32[]{:S(2)}, u32[]{:S(2)}) collective-permute-start(f32[2,128,128]{2,1,0:T(8,128)S(1)} %get-tuple-element.213), channel_id=1, source_target_pairs={{16,24},{20,28},{17,25},{21,29},{18,26},{22,30},{19,27},{23,31}} | collective-permute-start | bytes 393224 | tf_op jit(solution)/shard_map/ppermute | solution.py:190
  27.6 3.8 %collective-permute-start.14 = (f32[2,128,128]{2,1,0:T(8,128)S(1)}, f32[2,128,128]{2,1,0:T(8,128)S(1)}, u32[]{:S(2)}, u32[]{:S(2)}) collective-permute-start(f32[2,128,128]{2,1,0:T(8,128)S(1)} %get-tuple-element.211), channel_id=1, source_target_pairs={{16,24},{20,28},{17,25},{21,29},{18,26},{22,30},{19,27},{23,31}} | collective-permute-start | bytes 393224 | tf_op jit(solution)/shard_map/ppermute | solution.py:190
  28.3 5.3 %copy-start.3 = (bf16[256,2048]{1,0:T(8,128)(2,1)S(1)}, bf16[256,2048]{1,0:T(8,128)(2,1)}, u32[]{:S(2)}) copy-start(bf16[256,2048]{1,0:T(8,128)(2,1)} %v.11) | copy-start | bytes 3145732
  28.3 6.5 %collective-permute-start.19 = (f32[2,128,128]{2,1,0:T(8,128)S(1)}, f32[2,128,128]{2,1,0:T(8,128)S(1)}, u32[]{:S(2)}, u32[]{:S(2)}) collective-permute-start(f32[2,128,128]{2,1,0:T(8,128)S(1)} %get-tuple-element.209), channel_id=1, source_target_pairs={{0,4},{4,0},{8,12},{12,8},{16,20},{20,16},{24,28},{28,24},{1,5},{5... | collective-permute-start | bytes 393224 | tf_op jit(solution)/shard_map/ppermute | solution.py:245
  29.1 4.5 %copy-start.2 = (bf16[256,2048]{1,0:T(8,128)(2,1)S(1)}, bf16[256,2048]{1,0:T(8,128)(2,1)}, u32[]{:S(2)}) copy-start(bf16[256,2048]{1,0:T(8,128)(2,1)} %k.11) | copy-start | bytes 3145732
  29.1 4.5 %copy-start = (bf16[256,2048]{1,0:T(8,128)(2,1)S(1)}, bf16[256,2048]{1,0:T(8,128)(2,1)}, u32[]{:S(2)}) copy-start(bf16[256,2048]{1,0:T(8,128)(2,1)} %q.9) | copy-start | bytes 3145732
  29.1 3.0 %collective-permute-start.13 = (f32[2,128,128]{2,1,0:T(8,128)S(1)}, f32[2,128,128]{2,1,0:T(8,128)S(1)}, u32[]{:S(2)}, u32[]{:S(2)}) collective-permute-start(f32[2,128,128]{2,1,0:T(8,128)S(1)} %get-tuple-element.207), channel_id=1, source_target_pairs={{16,24},{20,28},{17,25},{21,29},{18,26},{22,30},{19,27},{23,31}} | collective-permute-start | bytes 393224 | tf_op jit(solution)/shard_map/ppermute | solution.py:190
  30.0 7.2 %collective-permute-start.18 = (f32[2,128,128]{2,1,0:T(8,128)S(1)}, f32[2,128,128]{2,1,0:T(8,128)S(1)}, u32[]{:S(2)}, u32[]{:S(2)}) collective-permute-start(f32[2,128,128]{2,1,0:T(8,128)S(1)} %get-tuple-element.205), channel_id=1, source_target_pairs={{0,4},{4,0},{8,12},{12,8},{16,20},{20,16},{24,28},{28,24},{1,5},{5... | collective-permute-start | bytes 393224 | tf_op jit(solution)/shard_map/ppermute | solution.py:245
  31.4 7.2 %collective-permute-start.17 = (f32[2,128,128]{2,1,0:T(8,128)S(1)}, f32[2,128,128]{2,1,0:T(8,128)S(1)}, u32[]{:S(2)}, u32[]{:S(2)}) collective-permute-start(f32[2,128,128]{2,1,0:T(8,128)S(1)} %get-tuple-element.203), channel_id=1, source_target_pairs={{0,4},{4,0},{8,12},{12,8},{16,20},{20,16},{24,28},{28,24},{1,5},{5... | collective-permute-start | bytes 393224 | tf_op jit(solution)/shard_map/ppermute | solution.py:245
  32.2 1.4 %copy-start.4 = (bf16[2048]{0:T(1024)(128)(2,1)S(1)}, bf16[2048]{0:T(1024)(128)(2,1)}, u32[]{:S(2)}) copy-start(bf16[2048]{0:T(1024)(128)(2,1)} %param.9) | copy-start | bytes 12292
  32.2 7.8 %collective-permute-start.16 = (f32[2,128,128]{2,1,0:T(8,128)S(1)}, f32[2,128,128]{2,1,0:T(8,128)S(1)}, u32[]{:S(2)}, u32[]{:S(2)}) collective-permute-start(f32[2,128,128]{2,1,0:T(8,128)S(1)} %get-tuple-element.201), channel_id=1, source_target_pairs={{0,4},{4,0},{8,12},{12,8},{16,20},{20,16},{24,28},{28,24},{1,5},{5... | collective-permute-start | bytes 393224 | tf_op jit(solution)/shard_map/ppermute | solution.py:245
  33.6 1.2 %copy-start.1 = (bf16[256,2048]{1,0:T(8,128)(2,1)S(1)}, bf16[256,2048]{1,0:T(8,128)(2,1)}, u32[]{:S(2)}) copy-start(bf16[256,2048]{1,0:T(8,128)(2,1)} %refs_7_.3) | copy-start | bytes 3145732
  40.4 3.1 %collective-permute-start.22 = (f32[2,256]{1,0:T(2,128)S(1)}, f32[2,256]{1,0:T(2,128)S(1)}, u32[]{:S(2)}, u32[]{:S(2)}) collective-permute-start(f32[2,256]{1,0:T(2,128)S(1)} %get-tuple-element.128.refs_0_), channel_id=1, source_target_pairs={{0,3},{1,2},{2,1},{3,0},{4,7},{5,6},{6,5},{7,4},{8,11},{9,10},{10,... | collective-permute-start | bytes 6152 | tf_op jit(solution)/shard_map/ppermute | solution.py:333
  40.5 3.7 %collective-permute-start.21 = (f32[2,256]{1,0:T(2,128)S(1)}, f32[2,256]{1,0:T(2,128)S(1)}, u32[]{:S(2)}, u32[]{:S(2)}) collective-permute-start(f32[2,256]{1,0:T(2,128)S(1)} %get-tuple-element.128.refs_0_), channel_id=1, source_target_pairs={{0,2},{1,3},{2,0},{3,1},{4,6},{5,7},{6,4},{7,5},{8,10},{9,11},{10,... | collective-permute-start | bytes 6152 | tf_op jit(solution)/shard_map/ppermute | solution.py:333
  42.0 2.1 %collective-permute-start.20 = (f32[2,256]{1,0:T(2,128)S(1)}, f32[2,256]{1,0:T(2,128)S(1)}, u32[]{:S(2)}, u32[]{:S(2)}) collective-permute-start(f32[2,256]{1,0:T(2,128)S(1)} %get-tuple-element.128.refs_0_), channel_id=1, source_target_pairs={{0,1},{1,0},{2,3},{3,2},{4,5},{5,4},{6,7},{7,6},{8,9},{9,8},{10,11... | collective-permute-start | bytes 6152 | tf_op jit(solution)/shard_map/ppermute | solution.py:333
  44.5 6.4 %collective-permute-start.24 = (f32[2,128,128]{2,1,0:T(8,128)S(1)}, f32[2,128,128]{2,1,0:T(8,128)S(1)}, u32[]{:S(2)}, u32[]{:S(2)}) collective-permute-start(f32[2,128,128]{2,1,0:T(8,128)S(1)} %get-tuple-element.139), channel_id=1, source_target_pairs={{0,4},{4,0},{8,12},{12,8},{16,20},{20,16},{24,28},{28,24},{1,5},{5... | collective-permute-start | bytes 393224 | tf_op jit(solution)/shard_map/ppermute | solution.py:225
  46.4 10.9 %collective-permute-start.28 = (f32[2,128,128]{2,1,0:T(8,128)S(1)}, f32[2,128,128]{2,1,0:T(8,128)S(1)}, u32[]{:S(2)}, u32[]{:S(2)}) collective-permute-start(f32[2,128,128]{2,1,0:T(8,128)S(1)} %get-tuple-element.147), channel_id=1, source_target_pairs={{0,4},{4,0},{8,12},{12,8},{16,20},{20,16},{24,28},{28,24},{1,5},{5... | collective-permute-start | bytes 393224 | tf_op jit(solution)/shard_map/ppermute | solution.py:225
  47.1 9.4 %collective-permute-start.23 = (f32[2,128,128]{2,1,0:T(8,128)S(1)}, f32[2,128,128]{2,1,0:T(8,128)S(1)}, u32[]{:S(2)}, u32[]{:S(2)}) collective-permute-start(f32[2,128,128]{2,1,0:T(8,128)S(1)} %get-tuple-element.137), channel_id=1, source_target_pairs={{0,4},{4,0},{8,12},{12,8},{16,20},{20,16},{24,28},{28,24},{1,5},{5... | collective-permute-start | bytes 393224 | tf_op jit(solution)/shard_map/ppermute | solution.py:225
  51.0 7.0 %collective-permute-start.27 = (f32[2,128,128]{2,1,0:T(8,128)S(1)}, f32[2,128,128]{2,1,0:T(8,128)S(1)}, u32[]{:S(2)}, u32[]{:S(2)}) collective-permute-start(f32[2,128,128]{2,1,0:T(8,128)S(1)} %get-tuple-element.224), channel_id=1, source_target_pairs={{28,20},{24,16},{29,21},{25,17},{30,22},{26,18},{31,23},{27,19}} | collective-permute-start | bytes 393224 | tf_op jit(solution)/shard_map/ppermute | solution.py:190
  51.6 7.2 %collective-permute-start.26 = (f32[2,128,128]{2,1,0:T(8,128)S(1)}, f32[2,128,128]{2,1,0:T(8,128)S(1)}, u32[]{:S(2)}, u32[]{:S(2)}) collective-permute-start(f32[2,128,128]{2,1,0:T(8,128)S(1)} %get-tuple-element.145), channel_id=1, source_target_pairs={{0,4},{4,0},{8,12},{12,8},{16,20},{20,16},{24,28},{28,24},{1,5},{5... | collective-permute-start | bytes 393224 | tf_op jit(solution)/shard_map/ppermute | solution.py:225
  56.6 2.9 %collective-permute-start.25 = (f32[2,128,128]{2,1,0:T(8,128)S(1)}, f32[2,128,128]{2,1,0:T(8,128)S(1)}, u32[]{:S(2)}, u32[]{:S(2)}) collective-permute-start(f32[2,128,128]{2,1,0:T(8,128)S(1)} %get-tuple-element.222), channel_id=1, source_target_pairs={{28,20},{24,16},{29,21},{25,17},{30,22},{26,18},{31,23},{27,19}} | collective-permute-start | bytes 393224 | tf_op jit(solution)/shard_map/ppermute | solution.py:190
  57.3 2.9 %collective-permute-start.31 = (f32[2,128,128]{2,1,0:T(8,128)S(1)}, f32[2,128,128]{2,1,0:T(8,128)S(1)}, u32[]{:S(2)}, u32[]{:S(2)}) collective-permute-start(f32[2,128,128]{2,1,0:T(8,128)S(1)} %get-tuple-element.220), channel_id=1, source_target_pairs={{28,20},{24,16},{29,21},{25,17},{30,22},{26,18},{31,23},{27,19}} | collective-permute-start | bytes 393224 | tf_op jit(solution)/shard_map/ppermute | solution.py:190
  58.0 4.8 %collective-permute-start.30 = (f32[2,128,128]{2,1,0:T(8,128)S(1)}, f32[2,128,128]{2,1,0:T(8,128)S(1)}, u32[]{:S(2)}, u32[]{:S(2)}) collective-permute-start(f32[2,128,128]{2,1,0:T(8,128)S(1)} %add.176), channel_id=1, source_target_pairs={{20,12},{16,8},{21,13},{17,9},{22,14},{18,10},{23,15},{19,11}} | collective-permute-start | bytes 393224 | tf_op jit(solution)/shard_map/ppermute | solution.py:190
  58.8 5.3 %collective-permute-start.29 = (f32[2,128,128]{2,1,0:T(8,128)S(1)}, f32[2,128,128]{2,1,0:T(8,128)S(1)}, u32[]{:S(2)}, u32[]{:S(2)}) collective-permute-start(f32[2,128,128]{2,1,0:T(8,128)S(1)} %get-tuple-element.218), channel_id=1, source_target_pairs={{28,20},{24,16},{29,21},{25,17},{30,22},{26,18},{31,23},{27,19}} | collective-permute-start | bytes 393224 | tf_op jit(solution)/shard_map/ppermute | solution.py:190
  59.6 5.3 %collective-permute-start.35 = (f32[2,128,128]{2,1,0:T(8,128)S(1)}, f32[2,128,128]{2,1,0:T(8,128)S(1)}, u32[]{:S(2)}, u32[]{:S(2)}) collective-permute-start(f32[2,128,128]{2,1,0:T(8,128)S(1)} %add.178), channel_id=1, source_target_pairs={{20,12},{16,8},{21,13},{17,9},{22,14},{18,10},{23,15},{19,11}} | collective-permute-start | bytes 393224 | tf_op jit(solution)/shard_map/ppermute | solution.py:190
  60.3 5.9 %collective-permute-start.34 = (f32[2,128,128]{2,1,0:T(8,128)S(1)}, f32[2,128,128]{2,1,0:T(8,128)S(1)}, u32[]{:S(2)}, u32[]{:S(2)}) collective-permute-start(f32[2,128,128]{2,1,0:T(8,128)S(1)} %add.179), channel_id=1, source_target_pairs={{20,12},{16,8},{21,13},{17,9},{22,14},{18,10},{23,15},{19,11}} | collective-permute-start | bytes 393224 | tf_op jit(solution)/shard_map/ppermute | solution.py:190
  62.8 13.0 %collective-permute-start.33 = (f32[2,128,128]{2,1,0:T(8,128)S(1)}, f32[2,128,128]{2,1,0:T(8,128)S(1)}, u32[]{:S(2)}, u32[]{:S(2)}) collective-permute-start(f32[2,128,128]{2,1,0:T(8,128)S(1)} %get-tuple-element.199), channel_id=1, source_target_pairs={{12,4},{8,0},{13,5},{9,1},{14,6},{10,2},{15,7},{11,3}} | collective-permute-start | bytes 393224 | tf_op jit(solution)/shard_map/ppermute | solution.py:190
  64.2 12.9 %collective-permute-start.32 = (f32[2,128,128]{2,1,0:T(8,128)S(1)}, f32[2,128,128]{2,1,0:T(8,128)S(1)}, u32[]{:S(2)}, u32[]{:S(2)}) collective-permute-start(f32[2,128,128]{2,1,0:T(8,128)S(1)} %add.182), channel_id=1, source_target_pairs={{20,12},{16,8},{21,13},{17,9},{22,14},{18,10},{23,15},{19,11}} | collective-permute-start | bytes 393224 | tf_op jit(solution)/shard_map/ppermute | solution.py:190
  64.9 15.3 %collective-permute-start.38 = (f32[2,128,128]{2,1,0:T(8,128)S(1)}, f32[2,128,128]{2,1,0:T(8,128)S(1)}, u32[]{:S(2)}, u32[]{:S(2)}) collective-permute-start(f32[2,128,128]{2,1,0:T(8,128)S(1)} %get-tuple-element.197), channel_id=1, source_target_pairs={{12,4},{8,0},{13,5},{9,1},{14,6},{10,2},{15,7},{11,3}} | collective-permute-start | bytes 393224 | tf_op jit(solution)/shard_map/ppermute | solution.py:190
  66.2 18.6 %collective-permute-start.37 = (f32[2,128,128]{2,1,0:T(8,128)S(1)}, f32[2,128,128]{2,1,0:T(8,128)S(1)}, u32[]{:S(2)}, u32[]{:S(2)}) collective-permute-start(f32[2,128,128]{2,1,0:T(8,128)S(1)} %get-tuple-element.195), channel_id=1, source_target_pairs={{12,4},{8,0},{13,5},{9,1},{14,6},{10,2},{15,7},{11,3}} | collective-permute-start | bytes 393224 | tf_op jit(solution)/shard_map/ppermute | solution.py:190
  75.9 13.0 %collective-permute-start.41 = (f32[2,128,128]{2,1,0:T(8,128)S(1)}, f32[2,128,128]{2,1,0:T(8,128)S(1)}, u32[]{:S(2)}, u32[]{:S(2)}) collective-permute-start(f32[2,128,128]{2,1,0:T(8,128)S(1)} %get-tuple-element.193), channel_id=1, source_target_pairs={{0,4},{4,0},{8,12},{12,8},{16,20},{20,16},{24,28},{28,24},{1,5},{5... | collective-permute-start | bytes 393224 | tf_op jit(solution)/shard_map/ppermute | solution.py:245
  77.1 9.6 %collective-permute-start.36 = (f32[2,128,128]{2,1,0:T(8,128)S(1)}, f32[2,128,128]{2,1,0:T(8,128)S(1)}, u32[]{:S(2)}, u32[]{:S(2)}) collective-permute-start(f32[2,128,128]{2,1,0:T(8,128)S(1)} %get-tuple-element.191), channel_id=1, source_target_pairs={{12,4},{8,0},{13,5},{9,1},{14,6},{10,2},{15,7},{11,3}} | collective-permute-start | bytes 393224 | tf_op jit(solution)/shard_map/ppermute | solution.py:190
  80.2 8.7 %collective-permute-start.42 = (f32[2,128,128]{2,1,0:T(8,128)S(1)}, f32[2,128,128]{2,1,0:T(8,128)S(1)}, u32[]{:S(2)}, u32[]{:S(2)}) collective-permute-start(f32[2,128,128]{2,1,0:T(8,128)S(1)} %get-tuple-element.189), channel_id=1, source_target_pairs={{0,4},{4,0},{8,12},{12,8},{16,20},{20,16},{24,28},{28,24},{1,5},{5... | collective-permute-start | bytes 393224 | tf_op jit(solution)/shard_map/ppermute | solution.py:245
  84.8 8.5 %collective-permute-start.40 = (f32[2,128,128]{2,1,0:T(8,128)S(1)}, f32[2,128,128]{2,1,0:T(8,128)S(1)}, u32[]{:S(2)}, u32[]{:S(2)}) collective-permute-start(f32[2,128,128]{2,1,0:T(8,128)S(1)} %get-tuple-element.187), channel_id=1, source_target_pairs={{0,4},{4,0},{8,12},{12,8},{16,20},{20,16},{24,28},{28,24},{1,5},{5... | collective-permute-start | bytes 393224 | tf_op jit(solution)/shard_map/ppermute | solution.py:245
  86.7 7.9 %collective-permute-start.39 = (f32[2,128,128]{2,1,0:T(8,128)S(1)}, f32[2,128,128]{2,1,0:T(8,128)S(1)}, u32[]{:S(2)}, u32[]{:S(2)}) collective-permute-start(f32[2,128,128]{2,1,0:T(8,128)S(1)} %get-tuple-element.185), channel_id=1, source_target_pairs={{0,4},{4,0},{8,12},{12,8},{16,20},{20,16},{24,28},{28,24},{1,5},{5... | collective-permute-start | bytes 393224 | tf_op jit(solution)/shard_map/ppermute | solution.py:245

commit v13 on v12

--- a/solution.py
+++ b/solution.py
@@ -387,12 +387,27 @@
                 [((tokens, width), BF16, block, index, HBM)] * 2, grid=(len(units),), aliases=aliases)
 
         query_made = []
-        beside = {(2, 0): lambda out, sends: query(sends[1, 1])} if spread else {}
+        made = []
+
+        def one(c):
+            def work(out, sends):
+                made[:] = rest([(c, 0)], out, made)
+                return made[0]
+            return work
+
+        beside = {
+            (2, 0): lambda out, sends: query(sends[1, 2]),
+            (long - 1, 1): one(0),
+            (long - 1, 2): one(1),
+            (long - 1, 3): one(2),
+        } if spread else {}
         after = scan(kept, sent, ends, True, [], beside)
         if not spread:
             query()
-        made = rest([(c, 0) for c in range(CHUNKS)] + [(c, 1) for c in range(CHUNKS - 2)], after, [])
-        for c in range(CHUNKS - 2, CHUNKS):
+        for c in range(3 if spread else 0, CHUNKS):
+            one(c)(after, None)
+        made = rest([(0, 1), (1, 1)], after, made)
+        for c in range(2, CHUNKS):
             made = rest([(c, 1)], after, made)
         return query_made[0], made[0], made[1]
 

time: 96.4 us -> 92.7 us (0.962)
  waiting for transfers between devices: 27 us -> 21.6 us
  Pallas kernels: 17.9 us -> 20.2 us
    ppermute x24, waiting for transfers between devices: 14.3 us -> 8.88 us  [hop(): return lax.ppermute(array, 'seq', pairs)]
    pallas_call x15 -> x19, Pallas kernels: 17.9 us -> 20.2 us  [call(): pl.pallas_call(body, grid_spec=pltpu.PrefetchScalarGridSpec(num_scalar_pr...]
  transfers between devices with their start and end apart: 43 -> 43, of which waited for: 14 -> 12; matrix products, arithmetic and copies ran while one was open for 2% -> 2% of each run, Pallas kernels for 15% -> 18%
where the time goes in v13:
time: 92.7 us; the launch traced here: 92.2 us
  starting transfers between devices  47.3 us (51%)
  waiting for transfers between devices  21.6 us (23%)
  Pallas kernels  20.2 us (22%)
  between operations  1.31 us (1%)
  local copies, waits for them, and re-layouts  1.05 us (1%)
    ppermute x24, starting transfers between devices, hop(): return lax.ppermute(array, 'seq', pairs)  25.2 us
    pallas_call x19, Pallas kernels, call(): pl.pallas_call(body, grid_spec=pltpu.PrefetchScalarGridSpec(num_scalar_pr...  20.2 us
    ppermute x8, starting transfers between devices, swap_after(): flight[c] = lax.ppermute(part_sent, 'seq', swap)  11.6 us
    ppermute x24, waiting for transfers between devices, hop(): return lax.ppermute(array, 'seq', pairs)  8.88 us
    ppermute x8, starting transfers between devices, scan(): out[c] = (carry[c], own[c], lax.ppermute(send, 'seq', swap))  8.63 us
    ppermute x8, waiting for transfers between devices, swap_after(): flight[c] = lax.ppermute(part_sent, 'seq', swap)  6.7 us
    ppermute x8, waiting for transfers between devices, scan(): out[c] = (carry[c], own[c], lax.ppermute(send, 'seq', swap))  4.22 us
    ppermute x3, starting transfers between devices, shards(): lax.ppermute(mine, 'head', [(i, i ^ step if paired else (i + step) % part...  1.92 us
  transfers between devices with their start and end apart: 43, of which 12 were waited for; matrix products, arithmetic and copies ran while one was open for 2% of the time, Pallas kernels for 18%

profile of v13, /device:TPU:0, one launch (start us, length us, event | category | flops | bytes accessed | tf_op | source)
XLA Modules:
  0.0 92.2 jit_solution(12790252082632335731)
XLA Ops:
  0.6 1.3 %shard_map.78 = (f32[2,128,128]{2,1,0:T(8,128)S(1)}, f32[2,128,128]{2,1,0:T(8,128)S(1)}) custom-call(s32[1]{0:T(128)} %bitcast.place, bf16[256,2048]{1,0:T(8,128)(2,1)} %k.19, bf16[256,2048]{1,0:T(8,128)(2,1)} %v.19), custom_call_target="tpu_custom_call" | custom-call | flops 1024 | bytes 1024 | tf_op jit(solution)/shard_map/pallas_call | solution.py:43
  2.0 3.0 %collective-permute-start = (f32[2,128,128]{2,1,0:T(8,128)S(1)}, f32[2,128,128]{2,1,0:T(8,128)S(1)}, u32[]{:S(2)}, u32[]{:S(2)}) collective-permute-start(f32[2,128,128]{2,1,0:T(8,128)S(1)} %get-tuple-element.107), channel_id=1, source_target_pairs={{0,4},{4,0},{8,12},{12,8},{16,20},{20,16},{24,28},{28,24},{1,5},{5... | collective-permute-start | bytes 393224 | tf_op jit(solution)/shard_map/ppermute | solution.py:225
  5.1 1.3 %shard_map.77 = (f32[2,128,128]{2,1,0:T(8,128)S(1)}, f32[2,128,128]{2,1,0:T(8,128)S(1)}) custom-call(s32[1]{0:T(128)} %bitcast.place, bf16[256,2048]{1,0:T(8,128)(2,1)} %k.19, bf16[256,2048]{1,0:T(8,128)(2,1)} %v.19), custom_call_target="tpu_custom_call" | custom-call | flops 1024 | bytes 1024 | tf_op jit(solution)/shard_map/pallas_call | solution.py:43
  6.4 2.0 %collective-permute-start.3 = (f32[2,128,128]{2,1,0:T(8,128)S(1)}, f32[2,128,128]{2,1,0:T(8,128)S(1)}, u32[]{:S(2)}, u32[]{:S(2)}) collective-permute-start(f32[2,128,128]{2,1,0:T(8,128)S(1)} %get-tuple-element.111), channel_id=1, source_target_pairs={{0,4},{4,0},{8,12},{12,8},{16,20},{20,16},{24,28},{28,24},{1,5},{5... | collective-permute-start | bytes 393224 | tf_op jit(solution)/shard_map/ppermute | solution.py:225
  8.4 2.6 %shard_map.76 = (f32[2,128,128]{2,1,0:T(8,128)S(1)}, f32[2,128,128]{2,1,0:T(8,128)S(1)}, f32[2,128,128]{2,1,0:T(8,128)S(1)}, f32[2,128,128]{2,1,0:T(8,128)S(1)}, f32[256,1024]{1,0:T(8,128)S(1)}) custom-call(s32[1]{0:T(128)} %bitcast.place, bf16[256,2048]{1,0:T(8,128)(2,1)} %q.17, bf16[256,2048]{1,0:T(8,128)(2,1)} %k.19, bf16[256,2048]{1,0:T(8,128)(2,1)} %v.19), custom_call_target="tpu_custom_call" | custom-call | flops 1024 | bytes 1024 | tf_op jit(solution)/shard_map/pallas_call | solution.py:43
  11.1 3.5 %collective-permute-start.2 = (f32[2,128,128]{2,1,0:T(8,128)S(1)}, f32[2,128,128]{2,1,0:T(8,128)S(1)}, u32[]{:S(2)}, u32[]{:S(2)}) collective-permute-start(f32[2,128,128]{2,1,0:T(8,128)S(1)} %get-tuple-element.242), channel_id=1, source_target_pairs={{0,8},{4,12},{1,9},{5,13},{2,10},{6,14},{3,11},{7,15}} | collective-permute-start | bytes 393224 | tf_op jit(solution)/shard_map/ppermute | solution.py:190
  14.6 1.6 %collective-permute-start.8 = (f32[2,128,128]{2,1,0:T(8,128)S(1)}, f32[2,128,128]{2,1,0:T(8,128)S(1)}, u32[]{:S(2)}, u32[]{:S(2)}) collective-permute-start(f32[2,128,128]{2,1,0:T(8,128)S(1)} %get-tuple-element.244), channel_id=1, source_target_pairs={{0,8},{4,12},{1,9},{5,13},{2,10},{6,14},{3,11},{7,15}} | collective-permute-start | bytes 393224 | tf_op jit(solution)/shard_map/ppermute | solution.py:190
  16.2 1.6 %collective-permute-start.1 = (f32[2,128,128]{2,1,0:T(8,128)S(1)}, f32[2,128,128]{2,1,0:T(8,128)S(1)}, u32[]{:S(2)}, u32[]{:S(2)}) collective-permute-start(f32[2,128,128]{2,1,0:T(8,128)S(1)} %get-tuple-element.109), channel_id=1, source_target_pairs={{0,4},{4,0},{8,12},{12,8},{16,20},{20,16},{24,28},{28,24},{1,5},{5... | collective-permute-start | bytes 393224 | tf_op jit(solution)/shard_map/ppermute | solution.py:225
  17.8 1.6 %collective-permute-start.7 = (f32[2,128,128]{2,1,0:T(8,128)S(1)}, f32[2,128,128]{2,1,0:T(8,128)S(1)}, u32[]{:S(2)}, u32[]{:S(2)}) collective-permute-start(f32[2,128,128]{2,1,0:T(8,128)S(1)} %get-tuple-element.246), channel_id=1, source_target_pairs={{0,8},{4,12},{1,9},{5,13},{2,10},{6,14},{3,11},{7,15}} | collective-permute-start | bytes 393224 | tf_op jit(solution)/shard_map/ppermute | solution.py:190
  20.1 1.2 %collective-permute-done.1 = f32[2,128,128]{2,1,0:T(8,128)S(1)} collective-permute-done((f32[2,128,128]{2,1,0:T(8,128)S(1)}, f32[2,128,128]{2,1,0:T(8,128)S(1)}, u32[]{:S(2)}, u32[]{:S(2)}) %collective-permute-start.1) | collective-permute-done | bytes 131104 | tf_op jit(solution)/shard_map/ppermute | solution.py:225
  21.2 2.4 %collective-permute-start.5 = (f32[2,128,128]{2,1,0:T(8,128)S(1)}, f32[2,128,128]{2,1,0:T(8,128)S(1)}, u32[]{:S(2)}, u32[]{:S(2)}) collective-permute-start(f32[2,128,128]{2,1,0:T(8,128)S(1)} %get-tuple-element.248), channel_id=1, source_target_pairs={{0,8},{4,12},{1,9},{5,13},{2,10},{6,14},{3,11},{7,15}} | collective-permute-start | bytes 393224 | tf_op jit(solution)/shard_map/ppermute | solution.py:190
  28.3 0.8 collective-permute-start.19
  29.1 0.8 collective-permute-start.13
  30.0 1.4 %collective-permute-start.18 = (f32[2,128,128]{2,1,0:T(8,128)S(1)}, f32[2,128,128]{2,1,0:T(8,128)S(1)}, u32[]{:S(2)}, u32[]{:S(2)}) collective-permute-start(f32[2,128,128]{2,1,0:T(8,128)S(1)} %get-tuple-element.221), channel_id=1, source_target_pairs={{0,4},{4,0},{8,12},{12,8},{16,20},{20,16},{24,28},{28,24},{1,5},{5... | collective-permute-start | bytes 393224 | tf_op jit(solution)/shard_map/ppermute | solution.py:245
  31.4 0.8 collective-permute-start.17
  32.2 1.4 %collective-permute-start.16 = (f32[2,128,128]{2,1,0:T(8,128)S(1)}, f32[2,128,128]{2,1,0:T(8,128)S(1)}, u32[]{:S(2)}, u32[]{:S(2)}) collective-permute-start(f32[2,128,128]{2,1,0:T(8,128)S(1)} %get-tuple-element.217), channel_id=1, source_target_pairs={{0,4},{4,0},{8,12},{12,8},{16,20},{20,16},{24,28},{28,24},{1,5},{5... | collective-permute-start | bytes 393224 | tf_op jit(solution)/shard_map/ppermute | solution.py:245
  33.7 1.1 %shard_map.79.al_o = f32[256,1024]{1,0:T(8,128)S(1)} custom-call(s32[1]{0:T(128)} %bitcast.place, bf16[256,2048]{1,0:T(8,128)(2,1)S(1)} %copy-done, bf16[256,2048]{1,0:T(8,128)(2,1)S(1)} %copy-done.1, bf16[256,2048]{1,0:T(8,128)(2,1)S(1)} %copy-done.2, f32[2,128,128]{2,1,0:T(8,128)S(1)} %get-tuple-element.218.refs_0_.e), custom_call_target="tpu_custom_call" | custom-call | flops 1024 | bytes 1024 | tf_op jit(solution)/shard_map/pallas_call | solution.py:43
  35.2 2.0 %collective-permute-done.18.other = f32[2,128,128]{2,1,0:T(8,128)S(1)} collective-permute-done((f32[2,128,128]{2,1,0:T(8,128)S(1)}, f32[2,128,128]{2,1,0:T(8,128)S(1)}, u32[]{:S(2)}, u32[]{:S(2)}) %collective-permute-start.18) | collective-permute-done | bytes 131104 | tf_op jit(solution)/shard_map/ppermute | solution.py:245
  37.5 1.1 %collective-permute-done.17.other = f32[2,128,128]{2,1,0:T(8,128)S(1)} collective-permute-done((f32[2,128,128]{2,1,0:T(8,128)S(1)}, f32[2,128,128]{2,1,0:T(8,128)S(1)}, u32[]{:S(2)}, u32[]{:S(2)}) %collective-permute-start.17) | collective-permute-done | bytes 131104 | tf_op jit(solution)/shard_map/ppermute | solution.py:245
  38.9 1.1 %collective-permute-done.16.other = f32[2,128,128]{2,1,0:T(8,128)S(1)} collective-permute-done((f32[2,128,128]{2,1,0:T(8,128)S(1)}, f32[2,128,128]{2,1,0:T(8,128)S(1)}, u32[]{:S(2)}, u32[]{:S(2)}) %collective-permute-start.16) | collective-permute-done | bytes 131104 | tf_op jit(solution)/shard_map/ppermute | solution.py:245
  40.5 1.6 %collective-permute-start.21 = (f32[2,256]{1,0:T(2,128)S(1)}, f32[2,256]{1,0:T(2,128)S(1)}, u32[]{:S(2)}, u32[]{:S(2)}) collective-permute-start(f32[2,256]{1,0:T(2,128)S(1)} %get-tuple-element.136.refs_0_), channel_id=1, source_target_pairs={{0,2},{1,3},{2,0},{3,1},{4,6},{5,7},{6,4},{7,5},{8,10},{9,11},{10,... | collective-permute-start | bytes 6152 | tf_op jit(solution)/shard_map/ppermute | solution.py:333
  42.3 1.1 %collective-permute-done.22.refs_3_ = f32[2,256]{1,0:T(2,128)S(1)} collective-permute-done((f32[2,256]{1,0:T(2,128)S(1)}, f32[2,256]{1,0:T(2,128)S(1)}, u32[]{:S(2)}, u32[]{:S(2)}) %collective-permute-start.22) | collective-permute-done | bytes 2080 | tf_op jit(solution)/shard_map/ppermute | solution.py:333
  44.5 1.4 %collective-permute-start.25 = (f32[2,128,128]{2,1,0:T(8,128)S(1)}, f32[2,128,128]{2,1,0:T(8,128)S(1)}, u32[]{:S(2)}, u32[]{:S(2)}) collective-permute-start(f32[2,128,128]{2,1,0:T(8,128)S(1)} %get-tuple-element.151), channel_id=1, source_target_pairs={{0,4},{4,0},{8,12},{12,8},{16,20},{20,16},{24,28},{28,24},{1,5},{5... | collective-permute-start | bytes 393224 | tf_op jit(solution)/shard_map/ppermute | solution.py:225
  46.4 0.8 collective-permute-start.24
  47.1 1.3 %collective-permute-start.23 = (f32[2,128,128]{2,1,0:T(8,128)S(1)}, f32[2,128,128]{2,1,0:T(8,128)S(1)}, u32[]{:S(2)}, u32[]{:S(2)}) collective-permute-start(f32[2,128,128]{2,1,0:T(8,128)S(1)} %get-tuple-element.145), channel_id=1, source_target_pairs={{0,4},{4,0},{8,12},{12,8},{16,20},{20,16},{24,28},{28,24},{1,5},{5... | collective-permute-start | bytes 393224 | tf_op jit(solution)/shard_map/ppermute | solution.py:225
  49.1 1.8 %collective-permute-done.25 = f32[2,128,128]{2,1,0:T(8,128)S(1)} collective-permute-done((f32[2,128,128]{2,1,0:T(8,128)S(1)}, f32[2,128,128]{2,1,0:T(8,128)S(1)}, u32[]{:S(2)}, u32[]{:S(2)}) %collective-permute-start.25) | collective-permute-done | bytes 131104 | tf_op jit(solution)/shard_map/ppermute | solution.py:225
  51.6 1.4 %collective-permute-start.28 = (f32[2,128,128]{2,1,0:T(8,128)S(1)}, f32[2,128,128]{2,1,0:T(8,128)S(1)}, u32[]{:S(2)}, u32[]{:S(2)}) collective-permute-start(f32[2,128,128]{2,1,0:T(8,128)S(1)} %get-tuple-element.156), channel_id=1, source_target_pairs={{0,4},{4,0},{8,12},{12,8},{16,20},{20,16},{24,28},{28,24},{1,5},{5... | collective-permute-start | bytes 393224 | tf_op jit(solution)/shard_map/ppermute | solution.py:225
  53.0 0.7 collective-permute-done.24
  54.4 2.1 %collective-permute-done.23 = f32[2,128,128]{2,1,0:T(8,128)S(1)} collective-permute-done((f32[2,128,128]{2,1,0:T(8,128)S(1)}, f32[2,128,128]{2,1,0:T(8,128)S(1)}, u32[]{:S(2)}, u32[]{:S(2)}) %collective-permute-start.23) | collective-permute-done | bytes 131104 | tf_op jit(solution)/shard_map/ppermute | solution.py:225
  58.0 0.8 collective-permute-done.28
  60.9 1.8 %shard_map.87 = bf16[256,2048]{1,0:T(8,128)(2,1)S(1)} custom-call(s32[1]{0:T(128)} %bitcast.place, bf16[256,2048]{1,0:T(8,128)(2,1)S(1)} %copy-done.1, bf16[256,2048]{1,0:T(8,128)(2,1)S(1)} %copy-done.2, bf16[256,256]{1,0:T(8,128)(2,1)S(1)} %get-tuple-element.161.refs_0_, bf16[256,256]{1,0:T(8,128)(2,1)S(1)} %get-tuple-element.162.refs_1_.refs_0_, ...), custom_call_target="tpu_custom_call" | custom-call | flops 1024 | bytes 1024 | tf_op jit(solution)/shard_map/pallas_call | solution.py:43
  62.8 1.3 %collective-permute-start.33 = (f32[2,128,128]{2,1,0:T(8,128)S(1)}, f32[2,128,128]{2,1,0:T(8,128)S(1)}, u32[]{:S(2)}, u32[]{:S(2)}) collective-permute-start(f32[2,128,128]{2,1,0:T(8,128)S(1)} %get-tuple-element.215), channel_id=1, source_target_pairs={{12,4},{8,0},{13,5},{9,1},{14,6},{10,2},{15,7},{11,3}} | collective-permute-start | bytes 393224 | tf_op jit(solution)/shard_map/ppermute | solution.py:190
  64.9 1.3 %collective-permute-start.38 = (f32[2,128,128]{2,1,0:T(8,128)S(1)}, f32[2,128,128]{2,1,0:T(8,128)S(1)}, u32[]{:S(2)}, u32[]{:S(2)}) collective-permute-start(f32[2,128,128]{2,1,0:T(8,128)S(1)} %get-tuple-element.213), channel_id=1, source_target_pairs={{12,4},{8,0},{13,5},{9,1},{14,6},{10,2},{15,7},{11,3}} | collective-permute-start | bytes 393224 | tf_op jit(solution)/shard_map/ppermute | solution.py:190
  66.2 1.3 %collective-permute-start.37 = (f32[2,128,128]{2,1,0:T(8,128)S(1)}, f32[2,128,128]{2,1,0:T(8,128)S(1)}, u32[]{:S(2)}, u32[]{:S(2)}) collective-permute-start(f32[2,128,128]{2,1,0:T(8,128)S(1)} %get-tuple-element.211), channel_id=1, source_target_pairs={{12,4},{8,0},{13,5},{9,1},{14,6},{10,2},{15,7},{11,3}} | collective-permute-start | bytes 393224 | tf_op jit(solution)/shard_map/ppermute | solution.py:190
  67.5 8.5 %collective-permute-done.33 = f32[2,128,128]{2,1,0:T(8,128)S(1)} collective-permute-done((f32[2,128,128]{2,1,0:T(8,128)S(1)}, f32[2,128,128]{2,1,0:T(8,128)S(1)}, u32[]{:S(2)}, u32[]{:S(2)}) %collective-permute-start.33) | collective-permute-done | bytes 131104 | tf_op jit(solution)/shard_map/ppermute | solution.py:190
  76.0 1.2 %collective-permute-start.41 = (f32[2,128,128]{2,1,0:T(8,128)S(1)}, f32[2,128,128]{2,1,0:T(8,128)S(1)}, u32[]{:S(2)}, u32[]{:S(2)}) collective-permute-start(f32[2,128,128]{2,1,0:T(8,128)S(1)} %get-tuple-element.209), channel_id=1, source_target_pairs={{0,4},{4,0},{8,12},{12,8},{16,20},{20,16},{24,28},{28,24},{1,5},{5... | collective-permute-start | bytes 393224 | tf_op jit(solution)/shard_map/ppermute | solution.py:245
  77.3 1.5 %collective-permute-start.36 = (f32[2,128,128]{2,1,0:T(8,128)S(1)}, f32[2,128,128]{2,1,0:T(8,128)S(1)}, u32[]{:S(2)}, u32[]{:S(2)}) collective-permute-start(f32[2,128,128]{2,1,0:T(8,128)S(1)} %get-tuple-element.207), channel_id=1, source_target_pairs={{12,4},{8,0},{13,5},{9,1},{14,6},{10,2},{15,7},{11,3}} | collective-permute-start | bytes 393224 | tf_op jit(solution)/shard_map/ppermute | solution.py:190
  78.8 1.2 %shard_map.88 = (bf16[256,2048]{1,0:T(8,128)(2,1)}, bf16[256,2048]{1,0:T(8,128)(2,1)}) custom-call(s32[1]{0:T(128)} %bitcast.place, bf16[256,2048]{1,0:T(8,128)(2,1)S(1)} %copy-done, bf16[256,2048]{1,0:T(8,128)(2,1)S(1)} %copy-done.1, bf16[256,2048]{1,0:T(8,128)(2,1)S(1)} %copy-done.2, bf16[256,256]{1,0:T(8,128)(2,1)S(1)} %get-tuple-element.161.refs_0_, ...), custom_call_target="tpu_custom_call" | custom-call | flops 1024 | bytes 1024 | tf_op jit(solution)/shard_map/pallas_call | solution.py:43
  80.0 0.9 %collective-permute-start.42 = (f32[2,128,128]{2,1,0:T(8,128)S(1)}, f32[2,128,128]{2,1,0:T(8,128)S(1)}, u32[]{:S(2)}, u32[]{:S(2)}) collective-permute-start(f32[2,128,128]{2,1,0:T(8,128)S(1)} %get-tuple-element.205), channel_id=1, source_target_pairs={{0,4},{4,0},{8,12},{12,8},{16,20},{20,16},{24,28},{28,24},{1,5},{5... | collective-permute-start | bytes 393224 | tf_op jit(solution)/shard_map/ppermute | solution.py:245
  81.0 1.2 %shard_map.89 = (bf16[256,2048]{1,0:T(8,128)(2,1)}, bf16[256,2048]{1,0:T(8,128)(2,1)}) custom-call(s32[1]{0:T(128)} %bitcast.place, bf16[256,2048]{1,0:T(8,128)(2,1)S(1)} %copy-done, bf16[256,2048]{1,0:T(8,128)(2,1)S(1)} %copy-done.1, bf16[256,2048]{1,0:T(8,128)(2,1)S(1)} %copy-done.2, ...), custom_call_target="tpu_custom_call", output_to_operand_aliasing={{0}: (7, {}), {1}: (8, {})} | custom-call | flops 1024 | bytes 1024 | tf_op jit(solution)/shard_map/pallas_call | solution.py:43
  82.2 1.2 %collective-permute-start.40 = (f32[2,128,128]{2,1,0:T(8,128)S(1)}, f32[2,128,128]{2,1,0:T(8,128)S(1)}, u32[]{:S(2)}, u32[]{:S(2)}) collective-permute-start(f32[2,128,128]{2,1,0:T(8,128)S(1)} %get-tuple-element.203), channel_id=1, source_target_pairs={{0,4},{4,0},{8,12},{12,8},{16,20},{20,16},{24,28},{28,24},{1,5},{5... | collective-permute-start | bytes 393224 | tf_op jit(solution)/shard_map/ppermute | solution.py:245
  83.5 1.2 %shard_map.90 = (bf16[256,2048]{1,0:T(8,128)(2,1)}, bf16[256,2048]{1,0:T(8,128)(2,1)}) custom-call(s32[1]{0:T(128)} %bitcast.place, bf16[256,2048]{1,0:T(8,128)(2,1)S(1)} %copy-done, bf16[256,2048]{1,0:T(8,128)(2,1)S(1)} %copy-done.1, bf16[256,2048]{1,0:T(8,128)(2,1)S(1)} %copy-done.2, ...), custom_call_target="tpu_custom_call", output_to_operand_aliasing={{0}: (7, {}), {1}: (8, {})} | custom-call | flops 1024 | bytes 1024 | tf_op jit(solution)/shard_map/pallas_call | solution.py:43
  84.7 0.9 %collective-permute-start.39 = (f32[2,128,128]{2,1,0:T(8,128)S(1)}, f32[2,128,128]{2,1,0:T(8,128)S(1)}, u32[]{:S(2)}, u32[]{:S(2)}) collective-permute-start(f32[2,128,128]{2,1,0:T(8,128)S(1)} %get-tuple-element.201), channel_id=1, source_target_pairs={{0,4},{4,0},{8,12},{12,8},{16,20},{20,16},{24,28},{28,24},{1,5},{5... | collective-permute-start | bytes 393224 | tf_op jit(solution)/shard_map/ppermute | solution.py:245
  85.6 1.0 %copy.32 = bf16[256,2048]{1,0:T(8,128)(2,1)} copy(bf16[256,2048]{1,0:T(8,128)(2,1)S(1)} %shard_map.87) | data formatting | bytes 2097152
  86.6 1.2 %shard_map.91 = (bf16[256,2048]{1,0:T(8,128)(2,1)}, bf16[256,2048]{1,0:T(8,128)(2,1)}) custom-call(s32[1]{0:T(128)} %bitcast.place, bf16[256,2048]{1,0:T(8,128)(2,1)S(1)} %copy-done, bf16[256,2048]{1,0:T(8,128)(2,1)S(1)} %copy-done.1, bf16[256,2048]{1,0:T(8,128)(2,1)S(1)} %copy-done.2, ...), custom_call_target="tpu_custom_call", output_to_operand_aliasing={{0}: (7, {}), {1}: (8, {})} | custom-call | flops 1024 | bytes 1024 | tf_op jit(solution)/shard_map/pallas_call | solution.py:43
  87.8 1.9 %shard_map.92 = (bf16[256,2048]{1,0:T(8,128)(2,1)}, bf16[256,2048]{1,0:T(8,128)(2,1)}) custom-call(s32[1]{0:T(128)} %bitcast.place, bf16[256,2048]{1,0:T(8,128)(2,1)S(1)} %copy-done, bf16[256,2048]{1,0:T(8,128)(2,1)S(1)} %copy-done.1, bf16[256,2048]{1,0:T(8,128)(2,1)S(1)} %copy-done.2, ...), custom_call_target="tpu_custom_call", output_to_operand_aliasing={{0}: (8, {}), {1}: (9, {})} | custom-call | flops 1024 | bytes 1024 | tf_op jit(solution)/shard_map/pallas_call | solution.py:43
  89.7 1.2 %shard_map.93 = (bf16[256,2048]{1,0:T(8,128)(2,1)}, bf16[256,2048]{1,0:T(8,128)(2,1)}) custom-call(s32[1]{0:T(128)} %bitcast.place, bf16[256,2048]{1,0:T(8,128)(2,1)S(1)} %copy-done, bf16[256,2048]{1,0:T(8,128)(2,1)S(1)} %copy-done.1, bf16[256,2048]{1,0:T(8,128)(2,1)S(1)} %copy-done.2, ...), custom_call_target="tpu_custom_call", output_to_operand_aliasing={{0}: (6, {}), {1}: (7, {})} | custom-call | flops 1024 | bytes 1024 | tf_op jit(solution)/shard_map/pallas_call | solution.py:43
  90.9 1.2 %shard_map.94 = (bf16[256,2048]{1,0:T(8,128)(2,1)}, bf16[256,2048]{1,0:T(8,128)(2,1)}) custom-call(s32[1]{0:T(128)} %bitcast.place, bf16[256,2048]{1,0:T(8,128)(2,1)S(1)} %copy-done, bf16[256,2048]{1,0:T(8,128)(2,1)S(1)} %copy-done.1, bf16[256,2048]{1,0:T(8,128)(2,1)S(1)} %copy-done.2, ...), custom_call_target="tpu_custom_call", output_to_operand_aliasing={{0}: (6, {}), {1}: (7, {})} | custom-call | flops 1024 | bytes 1024 | tf_op jit(solution)/shard_map/pallas_call | solution.py:43
  (101 shorter events, 15.2 us)
Async XLA Ops:
  2.0 9.1 %collective-permute-start = (f32[2,128,128]{2,1,0:T(8,128)S(1)}, f32[2,128,128]{2,1,0:T(8,128)S(1)}, u32[]{:S(2)}, u32[]{:S(2)}) collective-permute-start(f32[2,128,128]{2,1,0:T(8,128)S(1)} %get-tuple-element.107), channel_id=1, source_target_pairs={{0,4},{4,0},{8,12},{12,8},{16,20},{20,16},{24,28},{28,24},{1,5},{5... | collective-permute-start | bytes 393224 | tf_op jit(solution)/shard_map/ppermute | solution.py:225
  5.0 9.6 %collective-permute-start.4 = (f32[2,128,128]{2,1,0:T(8,128)S(1)}, f32[2,128,128]{2,1,0:T(8,128)S(1)}, u32[]{:S(2)}, u32[]{:S(2)}) collective-permute-start(f32[2,128,128]{2,1,0:T(8,128)S(1)} %get-tuple-element.113), channel_id=1, source_target_pairs={{0,4},{4,0},{8,12},{12,8},{16,20},{20,16},{24,28},{28,24},{1,5},{5... | collective-permute-start | bytes 393224 | tf_op jit(solution)/shard_map/ppermute | solution.py:225
  6.4 9.8 %collective-permute-start.3 = (f32[2,128,128]{2,1,0:T(8,128)S(1)}, f32[2,128,128]{2,1,0:T(8,128)S(1)}, u32[]{:S(2)}, u32[]{:S(2)}) collective-permute-start(f32[2,128,128]{2,1,0:T(8,128)S(1)} %get-tuple-element.111), channel_id=1, source_target_pairs={{0,4},{4,0},{8,12},{12,8},{16,20},{20,16},{24,28},{28,24},{1,5},{5... | collective-permute-start | bytes 393224 | tf_op jit(solution)/shard_map/ppermute | solution.py:225
  11.1 8.3 %collective-permute-start.2 = (f32[2,128,128]{2,1,0:T(8,128)S(1)}, f32[2,128,128]{2,1,0:T(8,128)S(1)}, u32[]{:S(2)}, u32[]{:S(2)}) collective-permute-start(f32[2,128,128]{2,1,0:T(8,128)S(1)} %get-tuple-element.242), channel_id=1, source_target_pairs={{0,8},{4,12},{1,9},{5,13},{2,10},{6,14},{3,11},{7,15}} | collective-permute-start | bytes 393224 | tf_op jit(solution)/shard_map/ppermute | solution.py:190
  14.6 9.0 %collective-permute-start.8 = (f32[2,128,128]{2,1,0:T(8,128)S(1)}, f32[2,128,128]{2,1,0:T(8,128)S(1)}, u32[]{:S(2)}, u32[]{:S(2)}) collective-permute-start(f32[2,128,128]{2,1,0:T(8,128)S(1)} %get-tuple-element.244), channel_id=1, source_target_pairs={{0,8},{4,12},{1,9},{5,13},{2,10},{6,14},{3,11},{7,15}} | collective-permute-start | bytes 393224 | tf_op jit(solution)/shard_map/ppermute | solution.py:190
  16.2 5.0 %collective-permute-start.1 = (f32[2,128,128]{2,1,0:T(8,128)S(1)}, f32[2,128,128]{2,1,0:T(8,128)S(1)}, u32[]{:S(2)}, u32[]{:S(2)}) collective-permute-start(f32[2,128,128]{2,1,0:T(8,128)S(1)} %get-tuple-element.109), channel_id=1, source_target_pairs={{0,4},{4,0},{8,12},{12,8},{16,20},{20,16},{24,28},{28,24},{1,5},{5... | collective-permute-start | bytes 393224 | tf_op jit(solution)/shard_map/ppermute | solution.py:225
  17.8 6.5 %collective-permute-start.7 = (f32[2,128,128]{2,1,0:T(8,128)S(1)}, f32[2,128,128]{2,1,0:T(8,128)S(1)}, u32[]{:S(2)}, u32[]{:S(2)}) collective-permute-start(f32[2,128,128]{2,1,0:T(8,128)S(1)} %get-tuple-element.246), channel_id=1, source_target_pairs={{0,8},{4,12},{1,9},{5,13},{2,10},{6,14},{3,11},{7,15}} | collective-permute-start | bytes 393224 | tf_op jit(solution)/shard_map/ppermute | solution.py:190
  19.4 5.7 %collective-permute-start.6 = (f32[2,128,128]{2,1,0:T(8,128)S(1)}, f32[2,128,128]{2,1,0:T(8,128)S(1)}, u32[]{:S(2)}, u32[]{:S(2)}) collective-permute-start(f32[2,128,128]{2,1,0:T(8,128)S(1)} %add.152), channel_id=1, source_target_pairs={{8,16},{12,20},{9,17},{13,21},{10,18},{14,22},{11,19},{15,23}} | collective-permute-start | bytes 393224 | tf_op jit(solution)/shard_map/ppermute | solution.py:190
  21.2 4.9 %collective-permute-start.5 = (f32[2,128,128]{2,1,0:T(8,128)S(1)}, f32[2,128,128]{2,1,0:T(8,128)S(1)}, u32[]{:S(2)}, u32[]{:S(2)}) collective-permute-start(f32[2,128,128]{2,1,0:T(8,128)S(1)} %get-tuple-element.248), channel_id=1, source_target_pairs={{0,8},{4,12},{1,9},{5,13},{2,10},{6,14},{3,11},{7,15}} | collective-permute-start | bytes 393224 | tf_op jit(solution)/shard_map/ppermute | solution.py:190
  23.7 3.2 %collective-permute-start.12 = (f32[2,128,128]{2,1,0:T(8,128)S(1)}, f32[2,128,128]{2,1,0:T(8,128)S(1)}, u32[]{:S(2)}, u32[]{:S(2)}) collective-permute-start(f32[2,128,128]{2,1,0:T(8,128)S(1)} %add.154), channel_id=1, source_target_pairs={{8,16},{12,20},{9,17},{13,21},{10,18},{14,22},{11,19},{15,23}} | collective-permute-start | bytes 393224 | tf_op jit(solution)/shard_map/ppermute | solution.py:190
  24.4 3.2 %collective-permute-start.11 = (f32[2,128,128]{2,1,0:T(8,128)S(1)}, f32[2,128,128]{2,1,0:T(8,128)S(1)}, u32[]{:S(2)}, u32[]{:S(2)}) collective-permute-start(f32[2,128,128]{2,1,0:T(8,128)S(1)} %add.155), channel_id=1, source_target_pairs={{8,16},{12,20},{9,17},{13,21},{10,18},{14,22},{11,19},{15,23}} | collective-permute-start | bytes 393224 | tf_op jit(solution)/shard_map/ppermute | solution.py:190
  25.1 3.2 %collective-permute-start.10 = (f32[2,128,128]{2,1,0:T(8,128)S(1)}, f32[2,128,128]{2,1,0:T(8,128)S(1)}, u32[]{:S(2)}, u32[]{:S(2)}) collective-permute-start(f32[2,128,128]{2,1,0:T(8,128)S(1)} %get-tuple-element.231), channel_id=1, source_target_pairs={{16,24},{20,28},{17,25},{21,29},{18,26},{22,30},{19,27},{23,31}} | collective-permute-start | bytes 393224 | tf_op jit(solution)/shard_map/ppermute | solution.py:190
  26.1 2.9 %collective-permute-start.9 = (f32[2,128,128]{2,1,0:T(8,128)S(1)}, f32[2,128,128]{2,1,0:T(8,128)S(1)}, u32[]{:S(2)}, u32[]{:S(2)}) collective-permute-start(f32[2,128,128]{2,1,0:T(8,128)S(1)} %add.158), channel_id=1, source_target_pairs={{8,16},{12,20},{9,17},{13,21},{10,18},{14,22},{11,19},{15,23}} | collective-permute-start | bytes 393224 | tf_op jit(solution)/shard_map/ppermute | solution.py:190
  26.9 3.1 %collective-permute-start.15 = (f32[2,128,128]{2,1,0:T(8,128)S(1)}, f32[2,128,128]{2,1,0:T(8,128)S(1)}, u32[]{:S(2)}, u32[]{:S(2)}) collective-permute-start(f32[2,128,128]{2,1,0:T(8,128)S(1)} %get-tuple-element.229), channel_id=1, source_target_pairs={{16,24},{20,28},{17,25},{21,29},{18,26},{22,30},{19,27},{23,31}} | collective-permute-start | bytes 393224 | tf_op jit(solution)/shard_map/ppermute | solution.py:190
  27.6 3.8 %collective-permute-start.14 = (f32[2,128,128]{2,1,0:T(8,128)S(1)}, f32[2,128,128]{2,1,0:T(8,128)S(1)}, u32[]{:S(2)}, u32[]{:S(2)}) collective-permute-start(f32[2,128,128]{2,1,0:T(8,128)S(1)} %get-tuple-element.227), channel_id=1, source_target_pairs={{16,24},{20,28},{17,25},{21,29},{18,26},{22,30},{19,27},{23,31}} | collective-permute-start | bytes 393224 | tf_op jit(solution)/shard_map/ppermute | solution.py:190
  28.3 5.3 %copy-start.2 = (bf16[256,2048]{1,0:T(8,128)(2,1)S(1)}, bf16[256,2048]{1,0:T(8,128)(2,1)}, u32[]{:S(2)}) copy-start(bf16[256,2048]{1,0:T(8,128)(2,1)} %v.19) | copy-start | bytes 3145732
  28.3 6.5 %collective-permute-start.19 = (f32[2,128,128]{2,1,0:T(8,128)S(1)}, f32[2,128,128]{2,1,0:T(8,128)S(1)}, u32[]{:S(2)}, u32[]{:S(2)}) collective-permute-start(f32[2,128,128]{2,1,0:T(8,128)S(1)} %get-tuple-element.225), channel_id=1, source_target_pairs={{0,4},{4,0},{8,12},{12,8},{16,20},{20,16},{24,28},{28,24},{1,5},{5... | collective-permute-start | bytes 393224 | tf_op jit(solution)/shard_map/ppermute | solution.py:245
  29.1 4.5 %copy-start.1 = (bf16[256,2048]{1,0:T(8,128)(2,1)S(1)}, bf16[256,2048]{1,0:T(8,128)(2,1)}, u32[]{:S(2)}) copy-start(bf16[256,2048]{1,0:T(8,128)(2,1)} %k.19) | copy-start | bytes 3145732
  29.1 4.5 %copy-start = (bf16[256,2048]{1,0:T(8,128)(2,1)S(1)}, bf16[256,2048]{1,0:T(8,128)(2,1)}, u32[]{:S(2)}) copy-start(bf16[256,2048]{1,0:T(8,128)(2,1)} %q.17) | copy-start | bytes 3145732
  29.1 3.0 %collective-permute-start.13 = (f32[2,128,128]{2,1,0:T(8,128)S(1)}, f32[2,128,128]{2,1,0:T(8,128)S(1)}, u32[]{:S(2)}, u32[]{:S(2)}) collective-permute-start(f32[2,128,128]{2,1,0:T(8,128)S(1)} %get-tuple-element.223), channel_id=1, source_target_pairs={{16,24},{20,28},{17,25},{21,29},{18,26},{22,30},{19,27},{23,31}} | collective-permute-start | bytes 393224 | tf_op jit(solution)/shard_map/ppermute | solution.py:190
  30.0 7.2 %collective-permute-start.18 = (f32[2,128,128]{2,1,0:T(8,128)S(1)}, f32[2,128,128]{2,1,0:T(8,128)S(1)}, u32[]{:S(2)}, u32[]{:S(2)}) collective-permute-start(f32[2,128,128]{2,1,0:T(8,128)S(1)} %get-tuple-element.221), channel_id=1, source_target_pairs={{0,4},{4,0},{8,12},{12,8},{16,20},{20,16},{24,28},{28,24},{1,5},{5... | collective-permute-start | bytes 393224 | tf_op jit(solution)/shard_map/ppermute | solution.py:245
  31.4 7.2 %collective-permute-start.17 = (f32[2,128,128]{2,1,0:T(8,128)S(1)}, f32[2,128,128]{2,1,0:T(8,128)S(1)}, u32[]{:S(2)}, u32[]{:S(2)}) collective-permute-start(f32[2,128,128]{2,1,0:T(8,128)S(1)} %get-tuple-element.219), channel_id=1, source_target_pairs={{0,4},{4,0},{8,12},{12,8},{16,20},{20,16},{24,28},{28,24},{1,5},{5... | collective-permute-start | bytes 393224 | tf_op jit(solution)/shard_map/ppermute | solution.py:245
  32.2 1.4 %copy-start.4 = (bf16[2048]{0:T(1024)(128)(2,1)S(1)}, bf16[2048]{0:T(1024)(128)(2,1)}, u32[]{:S(2)}) copy-start(bf16[2048]{0:T(1024)(128)(2,1)} %param.9) | copy-start | bytes 12292
  32.2 7.8 %collective-permute-start.16 = (f32[2,128,128]{2,1,0:T(8,128)S(1)}, f32[2,128,128]{2,1,0:T(8,128)S(1)}, u32[]{:S(2)}, u32[]{:S(2)}) collective-permute-start(f32[2,128,128]{2,1,0:T(8,128)S(1)} %get-tuple-element.217), channel_id=1, source_target_pairs={{0,4},{4,0},{8,12},{12,8},{16,20},{20,16},{24,28},{28,24},{1,5},{5... | collective-permute-start | bytes 393224 | tf_op jit(solution)/shard_map/ppermute | solution.py:245
  33.6 1.2 %copy-start.3 = (bf16[256,2048]{1,0:T(8,128)(2,1)S(1)}, bf16[256,2048]{1,0:T(8,128)(2,1)}, u32[]{:S(2)}) copy-start(bf16[256,2048]{1,0:T(8,128)(2,1)} %refs_7_.3) | copy-start | bytes 3145732
  40.4 3.1 %collective-permute-start.22 = (f32[2,256]{1,0:T(2,128)S(1)}, f32[2,256]{1,0:T(2,128)S(1)}, u32[]{:S(2)}, u32[]{:S(2)}) collective-permute-start(f32[2,256]{1,0:T(2,128)S(1)} %get-tuple-element.136.refs_0_), channel_id=1, source_target_pairs={{0,3},{1,2},{2,1},{3,0},{4,7},{5,6},{6,5},{7,4},{8,11},{9,10},{10,... | collective-permute-start | bytes 6152 | tf_op jit(solution)/shard_map/ppermute | solution.py:333
  40.5 3.7 %collective-permute-start.21 = (f32[2,256]{1,0:T(2,128)S(1)}, f32[2,256]{1,0:T(2,128)S(1)}, u32[]{:S(2)}, u32[]{:S(2)}) collective-permute-start(f32[2,256]{1,0:T(2,128)S(1)} %get-tuple-element.136.refs_0_), channel_id=1, source_target_pairs={{0,2},{1,3},{2,0},{3,1},{4,6},{5,7},{6,4},{7,5},{8,10},{9,11},{10,... | collective-permute-start | bytes 6152 | tf_op jit(solution)/shard_map/ppermute | solution.py:333
  42.0 2.1 %collective-permute-start.20 = (f32[2,256]{1,0:T(2,128)S(1)}, f32[2,256]{1,0:T(2,128)S(1)}, u32[]{:S(2)}, u32[]{:S(2)}) collective-permute-start(f32[2,256]{1,0:T(2,128)S(1)} %get-tuple-element.136.refs_0_), channel_id=1, source_target_pairs={{0,1},{1,0},{2,3},{3,2},{4,5},{5,4},{6,7},{7,6},{8,9},{9,8},{10,11... | collective-permute-start | bytes 6152 | tf_op jit(solution)/shard_map/ppermute | solution.py:333
  44.5 6.4 %collective-permute-start.25 = (f32[2,128,128]{2,1,0:T(8,128)S(1)}, f32[2,128,128]{2,1,0:T(8,128)S(1)}, u32[]{:S(2)}, u32[]{:S(2)}) collective-permute-start(f32[2,128,128]{2,1,0:T(8,128)S(1)} %get-tuple-element.151), channel_id=1, source_target_pairs={{0,4},{4,0},{8,12},{12,8},{16,20},{20,16},{24,28},{28,24},{1,5},{5... | collective-permute-start | bytes 393224 | tf_op jit(solution)/shard_map/ppermute | solution.py:225
  46.4 7.4 %collective-permute-start.24 = (f32[2,128,128]{2,1,0:T(8,128)S(1)}, f32[2,128,128]{2,1,0:T(8,128)S(1)}, u32[]{:S(2)}, u32[]{:S(2)}) collective-permute-start(f32[2,128,128]{2,1,0:T(8,128)S(1)} %get-tuple-element.149), channel_id=1, source_target_pairs={{0,4},{4,0},{8,12},{12,8},{16,20},{20,16},{24,28},{28,24},{1,5},{5... | collective-permute-start | bytes 393224 | tf_op jit(solution)/shard_map/ppermute | solution.py:225
  47.1 9.4 %collective-permute-start.23 = (f32[2,128,128]{2,1,0:T(8,128)S(1)}, f32[2,128,128]{2,1,0:T(8,128)S(1)}, u32[]{:S(2)}, u32[]{:S(2)}) collective-permute-start(f32[2,128,128]{2,1,0:T(8,128)S(1)} %get-tuple-element.145), channel_id=1, source_target_pairs={{0,4},{4,0},{8,12},{12,8},{16,20},{20,16},{24,28},{28,24},{1,5},{5... | collective-permute-start | bytes 393224 | tf_op jit(solution)/shard_map/ppermute | solution.py:225
  51.0 6.3 %collective-permute-start.29 = (f32[2,128,128]{2,1,0:T(8,128)S(1)}, f32[2,128,128]{2,1,0:T(8,128)S(1)}, u32[]{:S(2)}, u32[]{:S(2)}) collective-permute-start(f32[2,128,128]{2,1,0:T(8,128)S(1)} %get-tuple-element.240), channel_id=1, source_target_pairs={{28,20},{24,16},{29,21},{25,17},{30,22},{26,18},{31,23},{27,19}} | collective-permute-start | bytes 393224 | tf_op jit(solution)/shard_map/ppermute | solution.py:190
  51.6 7.2 %collective-permute-start.28 = (f32[2,128,128]{2,1,0:T(8,128)S(1)}, f32[2,128,128]{2,1,0:T(8,128)S(1)}, u32[]{:S(2)}, u32[]{:S(2)}) collective-permute-start(f32[2,128,128]{2,1,0:T(8,128)S(1)} %get-tuple-element.156), channel_id=1, source_target_pairs={{0,4},{4,0},{8,12},{12,8},{16,20},{20,16},{24,28},{28,24},{1,5},{5... | collective-permute-start | bytes 393224 | tf_op jit(solution)/shard_map/ppermute | solution.py:225
  53.8 5.7 %collective-permute-start.27 = (f32[2,128,128]{2,1,0:T(8,128)S(1)}, f32[2,128,128]{2,1,0:T(8,128)S(1)}, u32[]{:S(2)}, u32[]{:S(2)}) collective-permute-start(f32[2,128,128]{2,1,0:T(8,128)S(1)} %get-tuple-element.238), channel_id=1, source_target_pairs={{28,20},{24,16},{29,21},{25,17},{30,22},{26,18},{31,23},{27,19}} | collective-permute-start | bytes 393224 | tf_op jit(solution)/shard_map/ppermute | solution.py:190
  56.6 3.7 %collective-permute-start.26 = (f32[2,128,128]{2,1,0:T(8,128)S(1)}, f32[2,128,128]{2,1,0:T(8,128)S(1)}, u32[]{:S(2)}, u32[]{:S(2)}) collective-permute-start(f32[2,128,128]{2,1,0:T(8,128)S(1)} %get-tuple-element.236), channel_id=1, source_target_pairs={{28,20},{24,16},{29,21},{25,17},{30,22},{26,18},{31,23},{27,19}} | collective-permute-start | bytes 393224 | tf_op jit(solution)/shard_map/ppermute | solution.py:190
  57.3 5.5 %collective-permute-start.31 = (f32[2,128,128]{2,1,0:T(8,128)S(1)}, f32[2,128,128]{2,1,0:T(8,128)S(1)}, u32[]{:S(2)}, u32[]{:S(2)}) collective-permute-start(f32[2,128,128]{2,1,0:T(8,128)S(1)} %add.176), channel_id=1, source_target_pairs={{20,12},{16,8},{21,13},{17,9},{22,14},{18,10},{23,15},{19,11}} | collective-permute-start | bytes 393224 | tf_op jit(solution)/shard_map/ppermute | solution.py:190
  58.8 5.3 %collective-permute-start.30 = (f32[2,128,128]{2,1,0:T(8,128)S(1)}, f32[2,128,128]{2,1,0:T(8,128)S(1)}, u32[]{:S(2)}, u32[]{:S(2)}) collective-permute-start(f32[2,128,128]{2,1,0:T(8,128)S(1)} %get-tuple-element.234), channel_id=1, source_target_pairs={{28,20},{24,16},{29,21},{25,17},{30,22},{26,18},{31,23},{27,19}} | collective-permute-start | bytes 393224 | tf_op jit(solution)/shard_map/ppermute | solution.py:190
  59.6 5.3 %collective-permute-start.35 = (f32[2,128,128]{2,1,0:T(8,128)S(1)}, f32[2,128,128]{2,1,0:T(8,128)S(1)}, u32[]{:S(2)}, u32[]{:S(2)}) collective-permute-start(f32[2,128,128]{2,1,0:T(8,128)S(1)} %add.178), channel_id=1, source_target_pairs={{20,12},{16,8},{21,13},{17,9},{22,14},{18,10},{23,15},{19,11}} | collective-permute-start | bytes 393224 | tf_op jit(solution)/shard_map/ppermute | solution.py:190
  60.3 5.9 %collective-permute-start.34 = (f32[2,128,128]{2,1,0:T(8,128)S(1)}, f32[2,128,128]{2,1,0:T(8,128)S(1)}, u32[]{:S(2)}, u32[]{:S(2)}) collective-permute-start(f32[2,128,128]{2,1,0:T(8,128)S(1)} %add.179), channel_id=1, source_target_pairs={{20,12},{16,8},{21,13},{17,9},{22,14},{18,10},{23,15},{19,11}} | collective-permute-start | bytes 393224 | tf_op jit(solution)/shard_map/ppermute | solution.py:190
  62.8 13.2 %collective-permute-start.33 = (f32[2,128,128]{2,1,0:T(8,128)S(1)}, f32[2,128,128]{2,1,0:T(8,128)S(1)}, u32[]{:S(2)}, u32[]{:S(2)}) collective-permute-start(f32[2,128,128]{2,1,0:T(8,128)S(1)} %get-tuple-element.215), channel_id=1, source_target_pairs={{12,4},{8,0},{13,5},{9,1},{14,6},{10,2},{15,7},{11,3}} | collective-permute-start | bytes 393224 | tf_op jit(solution)/shard_map/ppermute | solution.py:190
  64.2 13.1 %collective-permute-start.32 = (f32[2,128,128]{2,1,0:T(8,128)S(1)}, f32[2,128,128]{2,1,0:T(8,128)S(1)}, u32[]{:S(2)}, u32[]{:S(2)}) collective-permute-start(f32[2,128,128]{2,1,0:T(8,128)S(1)} %add.182), channel_id=1, source_target_pairs={{20,12},{16,8},{21,13},{17,9},{22,14},{18,10},{23,15},{19,11}} | collective-permute-start | bytes 393224 | tf_op jit(solution)/shard_map/ppermute | solution.py:190
  64.9 15.1 %collective-permute-start.38 = (f32[2,128,128]{2,1,0:T(8,128)S(1)}, f32[2,128,128]{2,1,0:T(8,128)S(1)}, u32[]{:S(2)}, u32[]{:S(2)}) collective-permute-start(f32[2,128,128]{2,1,0:T(8,128)S(1)} %get-tuple-element.213), channel_id=1, source_target_pairs={{12,4},{8,0},{13,5},{9,1},{14,6},{10,2},{15,7},{11,3}} | collective-permute-start | bytes 393224 | tf_op jit(solution)/shard_map/ppermute | solution.py:190
  66.2 16.0 %collective-permute-start.37 = (f32[2,128,128]{2,1,0:T(8,128)S(1)}, f32[2,128,128]{2,1,0:T(8,128)S(1)}, u32[]{:S(2)}, u32[]{:S(2)}) collective-permute-start(f32[2,128,128]{2,1,0:T(8,128)S(1)} %get-tuple-element.211), channel_id=1, source_target_pairs={{12,4},{8,0},{13,5},{9,1},{14,6},{10,2},{15,7},{11,3}} | collective-permute-start | bytes 393224 | tf_op jit(solution)/shard_map/ppermute | solution.py:190
  76.0 11.8 %collective-permute-start.41 = (f32[2,128,128]{2,1,0:T(8,128)S(1)}, f32[2,128,128]{2,1,0:T(8,128)S(1)}, u32[]{:S(2)}, u32[]{:S(2)}) collective-permute-start(f32[2,128,128]{2,1,0:T(8,128)S(1)} %get-tuple-element.209), channel_id=1, source_target_pairs={{0,4},{4,0},{8,12},{12,8},{16,20},{20,16},{24,28},{28,24},{1,5},{5... | collective-permute-start | bytes 393224 | tf_op jit(solution)/shard_map/ppermute | solution.py:245
  77.3 7.4 %collective-permute-start.36 = (f32[2,128,128]{2,1,0:T(8,128)S(1)}, f32[2,128,128]{2,1,0:T(8,128)S(1)}, u32[]{:S(2)}, u32[]{:S(2)}) collective-permute-start(f32[2,128,128]{2,1,0:T(8,128)S(1)} %get-tuple-element.207), channel_id=1, source_target_pairs={{12,4},{8,0},{13,5},{9,1},{14,6},{10,2},{15,7},{11,3}} | collective-permute-start | bytes 393224 | tf_op jit(solution)/shard_map/ppermute | solution.py:190
  80.0 7.8 %collective-permute-start.42 = (f32[2,128,128]{2,1,0:T(8,128)S(1)}, f32[2,128,128]{2,1,0:T(8,128)S(1)}, u32[]{:S(2)}, u32[]{:S(2)}) collective-permute-start(f32[2,128,128]{2,1,0:T(8,128)S(1)} %get-tuple-element.205), channel_id=1, source_target_pairs={{0,4},{4,0},{8,12},{12,8},{16,20},{20,16},{24,28},{28,24},{1,5},{5... | collective-permute-start | bytes 393224 | tf_op jit(solution)/shard_map/ppermute | solution.py:245
  82.2 7.5 %collective-permute-start.40 = (f32[2,128,128]{2,1,0:T(8,128)S(1)}, f32[2,128,128]{2,1,0:T(8,128)S(1)}, u32[]{:S(2)}, u32[]{:S(2)}) collective-permute-start(f32[2,128,128]{2,1,0:T(8,128)S(1)} %get-tuple-element.203), channel_id=1, source_target_pairs={{0,4},{4,0},{8,12},{12,8},{16,20},{20,16},{24,28},{28,24},{1,5},{5... | collective-permute-start | bytes 393224 | tf_op jit(solution)/shard_map/ppermute | solution.py:245
  84.7 6.2 %collective-permute-start.39 = (f32[2,128,128]{2,1,0:T(8,128)S(1)}, f32[2,128,128]{2,1,0:T(8,128)S(1)}, u32[]{:S(2)}, u32[]{:S(2)}) collective-permute-start(f32[2,128,128]{2,1,0:T(8,128)S(1)} %get-tuple-element.201), channel_id=1, source_target_pairs={{0,4},{4,0},{8,12},{12,8},{16,20},{20,16},{24,28},{28,24},{1,5},{5... | collective-permute-start | bytes 393224 | tf_op jit(solution)/shard_map/ppermute | solution.py:245

commit v14 on v13

--- a/solution.py
+++ b/solution.py
@@ -389,23 +389,21 @@
         query_made = []
         made = []
 
-        def one(c):
+        def pair(c):
             def work(out, sends):
-                made[:] = rest([(c, 0)], out, made)
+                made[:] = rest([(c, 0), (c + 1, 0)], out, made)
                 return made[0]
             return work
 
         beside = {
-            (2, 0): lambda out, sends: query(sends[1, 2]),
-            (long - 1, 1): one(0),
-            (long - 1, 2): one(1),
-            (long - 1, 3): one(2),
+            (2, 0): lambda out, sends: query(sends[1, 1]),
+            (long - 1, 2): pair(0),
         } if spread else {}
         after = scan(kept, sent, ends, True, [], beside)
         if not spread:
             query()
-        for c in range(3 if spread else 0, CHUNKS):
-            one(c)(after, None)
+        for c in range(2 if spread else 0, CHUNKS, 2):
+            pair(c)(after, None)
         made = rest([(0, 1), (1, 1)], after, made)
         for c in range(2, CHUNKS):
             made = rest([(c, 1)], after, made)

time: 92.7 us -> 94.4 us (1.018)
  waiting for transfers between devices: 21.6 us -> 23.2 us
  Pallas kernels: 20.2 us -> 18.9 us
    ppermute x8, starting transfers between devices: 11.6 us -> 9.3 us  [swap_after(): flight[c] = lax.ppermute(part_sent, 'seq', swap)]
    ppermute x24, starting transfers between devices: 25.2 us -> 27.4 us  [hop(): return lax.ppermute(array, 'seq', pairs)]
    pallas_call x19 -> x17, Pallas kernels: 20.2 us -> 18.9 us  [call(): pl.pallas_call(body, grid_spec=pltpu.PrefetchScalarGridSpec(num_scalar_pr...]
    ppermute x8, starting transfers between devices: 8.63 us -> 9.65 us  [scan(): out[c] = (carry[c], own[c], lax.ppermute(send, 'seq', swap))]
    ppermute x24, waiting for transfers between devices: 8.88 us -> 7.9 us  [hop(): return lax.ppermute(array, 'seq', pairs)]
  transfers between devices with their start and end apart: 43 -> 43, of which waited for: 12 -> 12; matrix products, arithmetic and copies ran while one was open for 2% -> 2% of each run, Pallas kernels for 18% -> 17%
where the time goes in v14:
time: 94.4 us; the launch traced here: 93.8 us
  starting transfers between devices  48.2 us (51%)
  waiting for transfers between devices  23.2 us (25%)
  Pallas kernels  18.9 us (20%)
  local copies, waits for them, and re-layouts  1.45 us (2%)
  between operations  1.33 us (1%)
    ppermute x24, starting transfers between devices, hop(): return lax.ppermute(array, 'seq', pairs)  27.4 us
    pallas_call x17, Pallas kernels, call(): pl.pallas_call(body, grid_spec=pltpu.PrefetchScalarGridSpec(num_scalar_pr...  18.9 us
    ppermute x8, starting transfers between devices, scan(): out[c] = (carry[c], own[c], lax.ppermute(send, 'seq', swap))  9.65 us
    ppermute x8, starting transfers between devices, swap_after(): flight[c] = lax.ppermute(part_sent, 'seq', swap)  9.3 us
    ppermute x24, waiting for transfers between devices, hop(): return lax.ppermute(array, 'seq', pairs)  7.9 us
    ppermute x8, waiting for transfers between devices, swap_after(): flight[c] = lax.ppermute(part_sent, 'seq', swap)  7.45 us
    ppermute x8, waiting for transfers between devices, scan(): out[c] = (carry[c], own[c], lax.ppermute(send, 'seq', swap))  5.14 us
    ppermute x3, waiting for transfers between devices, shards(): lax.ppermute(mine, 'head', [(i, i ^ step if paired else (i + step) % part...  2.67 us
  transfers between devices with their start and end apart: 43, of which 12 were waited for; matrix products, arithmetic and copies ran while one was open for 2% of the time, Pallas kernels for 17%

profile of v14, /device:TPU:0, one launch (start us, length us, event | category | flops | bytes accessed | tf_op | source)
XLA Modules:
  0.0 93.8 jit_solution(14047917580661937456)
XLA Ops:
  0.6 1.3 %shard_map.78 = (f32[2,128,128]{2,1,0:T(8,128)S(1)}, f32[2,128,128]{2,1,0:T(8,128)S(1)}) custom-call(s32[1]{0:T(128)} %bitcast.place, bf16[256,2048]{1,0:T(8,128)(2,1)} %k.15, bf16[256,2048]{1,0:T(8,128)(2,1)} %v.15), custom_call_target="tpu_custom_call" | custom-call | flops 1024 | bytes 1024 | tf_op jit(solution)/shard_map/pallas_call | solution.py:43
  2.0 3.0 %collective-permute-start = (f32[2,128,128]{2,1,0:T(8,128)S(1)}, f32[2,128,128]{2,1,0:T(8,128)S(1)}, u32[]{:S(2)}, u32[]{:S(2)}) collective-permute-start(f32[2,128,128]{2,1,0:T(8,128)S(1)} %get-tuple-element.103), channel_id=1, source_target_pairs={{0,4},{4,0},{8,12},{12,8},{16,20},{20,16},{24,28},{28,24},{1,5},{5... | collective-permute-start | bytes 393224 | tf_op jit(solution)/shard_map/ppermute | solution.py:225
  5.0 1.3 %shard_map.77 = (f32[2,128,128]{2,1,0:T(8,128)S(1)}, f32[2,128,128]{2,1,0:T(8,128)S(1)}) custom-call(s32[1]{0:T(128)} %bitcast.place, bf16[256,2048]{1,0:T(8,128)(2,1)} %k.15, bf16[256,2048]{1,0:T(8,128)(2,1)} %v.15), custom_call_target="tpu_custom_call" | custom-call | flops 1024 | bytes 1024 | tf_op jit(solution)/shard_map/pallas_call | solution.py:43
  6.4 2.0 %collective-permute-start.4 = (f32[2,128,128]{2,1,0:T(8,128)S(1)}, f32[2,128,128]{2,1,0:T(8,128)S(1)}, u32[]{:S(2)}, u32[]{:S(2)}) collective-permute-start(f32[2,128,128]{2,1,0:T(8,128)S(1)} %get-tuple-element.109), channel_id=1, source_target_pairs={{0,4},{4,0},{8,12},{12,8},{16,20},{20,16},{24,28},{28,24},{1,5},{5... | collective-permute-start | bytes 393224 | tf_op jit(solution)/shard_map/ppermute | solution.py:225
  8.4 2.6 %shard_map.76 = (f32[2,128,128]{2,1,0:T(8,128)S(1)}, f32[2,128,128]{2,1,0:T(8,128)S(1)}, f32[2,128,128]{2,1,0:T(8,128)S(1)}, f32[2,128,128]{2,1,0:T(8,128)S(1)}, f32[256,1024]{1,0:T(8,128)S(1)}) custom-call(s32[1]{0:T(128)} %bitcast.place, bf16[256,2048]{1,0:T(8,128)(2,1)} %q.13, bf16[256,2048]{1,0:T(8,128)(2,1)} %k.15, bf16[256,2048]{1,0:T(8,128)(2,1)} %v.15), custom_call_target="tpu_custom_call" | custom-call | flops 1024 | bytes 1024 | tf_op jit(solution)/shard_map/pallas_call | solution.py:43
  11.1 3.5 %collective-permute-start.2 = (f32[2,128,128]{2,1,0:T(8,128)S(1)}, f32[2,128,128]{2,1,0:T(8,128)S(1)}, u32[]{:S(2)}, u32[]{:S(2)}) collective-permute-start(f32[2,128,128]{2,1,0:T(8,128)S(1)} %get-tuple-element.234), channel_id=1, source_target_pairs={{0,8},{4,12},{1,9},{5,13},{2,10},{6,14},{3,11},{7,15}} | collective-permute-start | bytes 393224 | tf_op jit(solution)/shard_map/ppermute | solution.py:190
  15.2 2.9 %collective-permute-start.8 = (f32[2,128,128]{2,1,0:T(8,128)S(1)}, f32[2,128,128]{2,1,0:T(8,128)S(1)}, u32[]{:S(2)}, u32[]{:S(2)}) collective-permute-start(f32[2,128,128]{2,1,0:T(8,128)S(1)} %get-tuple-element.236), channel_id=1, source_target_pairs={{0,8},{4,12},{1,9},{5,13},{2,10},{6,14},{3,11},{7,15}} | collective-permute-start | bytes 393224 | tf_op jit(solution)/shard_map/ppermute | solution.py:190
  18.1 1.3 %collective-permute-start.7 = (f32[2,128,128]{2,1,0:T(8,128)S(1)}, f32[2,128,128]{2,1,0:T(8,128)S(1)}, u32[]{:S(2)}, u32[]{:S(2)}) collective-permute-start(f32[2,128,128]{2,1,0:T(8,128)S(1)} %get-tuple-element.238), channel_id=1, source_target_pairs={{0,8},{4,12},{1,9},{5,13},{2,10},{6,14},{3,11},{7,15}} | collective-permute-start | bytes 393224 | tf_op jit(solution)/shard_map/ppermute | solution.py:190
  20.2 3.5 %collective-permute-start.5 = (f32[2,128,128]{2,1,0:T(8,128)S(1)}, f32[2,128,128]{2,1,0:T(8,128)S(1)}, u32[]{:S(2)}, u32[]{:S(2)}) collective-permute-start(f32[2,128,128]{2,1,0:T(8,128)S(1)} %get-tuple-element.240), channel_id=1, source_target_pairs={{0,8},{4,12},{1,9},{5,13},{2,10},{6,14},{3,11},{7,15}} | collective-permute-start | bytes 393224 | tf_op jit(solution)/shard_map/ppermute | solution.py:190
  23.7 0.7 collective-permute-start.12
  25.1 0.7 collective-permute-start.10
  26.2 0.7 collective-permute-start.9
  28.3 1.9 %collective-permute-start.19 = (f32[2,128,128]{2,1,0:T(8,128)S(1)}, f32[2,128,128]{2,1,0:T(8,128)S(1)}, u32[]{:S(2)}, u32[]{:S(2)}) collective-permute-start(f32[2,128,128]{2,1,0:T(8,128)S(1)} %get-tuple-element.217), channel_id=1, source_target_pairs={{0,4},{4,0},{8,12},{12,8},{16,20},{20,16},{24,28},{28,24},{1,5},{5... | collective-permute-start | bytes 393224 | tf_op jit(solution)/shard_map/ppermute | solution.py:245
  30.3 0.8 collective-permute-start.13
  31.4 1.9 %collective-permute-start.17 = (f32[2,128,128]{2,1,0:T(8,128)S(1)}, f32[2,128,128]{2,1,0:T(8,128)S(1)}, u32[]{:S(2)}, u32[]{:S(2)}) collective-permute-start(f32[2,128,128]{2,1,0:T(8,128)S(1)} %get-tuple-element.211), channel_id=1, source_target_pairs={{0,4},{4,0},{8,12},{12,8},{16,20},{20,16},{24,28},{28,24},{1,5},{5... | collective-permute-start | bytes 393224 | tf_op jit(solution)/shard_map/ppermute | solution.py:245
  34.1 1.1 %shard_map.79.al_o = f32[256,1024]{1,0:T(8,128)S(1)} custom-call(s32[1]{0:T(128)} %bitcast.place, bf16[256,2048]{1,0:T(8,128)(2,1)S(1)} %copy-done, bf16[256,2048]{1,0:T(8,128)(2,1)S(1)} %copy-done.1, bf16[256,2048]{1,0:T(8,128)(2,1)S(1)} %copy-done.2, f32[2,128,128]{2,1,0:T(8,128)S(1)} %get-tuple-element.210.refs_0_.e), custom_call_target="tpu_custom_call" | custom-call | flops 1024 | bytes 1024 | tf_op jit(solution)/shard_map/pallas_call | solution.py:43
  35.6 2.1 %collective-permute-done.18.other = f32[2,128,128]{2,1,0:T(8,128)S(1)} collective-permute-done((f32[2,128,128]{2,1,0:T(8,128)S(1)}, f32[2,128,128]{2,1,0:T(8,128)S(1)}, u32[]{:S(2)}, u32[]{:S(2)}) %collective-permute-start.18) | collective-permute-done | bytes 131104 | tf_op jit(solution)/shard_map/ppermute | solution.py:245
  37.9 2.0 %collective-permute-done.17.other = f32[2,128,128]{2,1,0:T(8,128)S(1)} collective-permute-done((f32[2,128,128]{2,1,0:T(8,128)S(1)}, f32[2,128,128]{2,1,0:T(8,128)S(1)}, u32[]{:S(2)}, u32[]{:S(2)}) %collective-permute-start.17) | collective-permute-done | bytes 131104 | tf_op jit(solution)/shard_map/ppermute | solution.py:245
  40.2 1.1 %collective-permute-done.16.other = f32[2,128,128]{2,1,0:T(8,128)S(1)} collective-permute-done((f32[2,128,128]{2,1,0:T(8,128)S(1)}, f32[2,128,128]{2,1,0:T(8,128)S(1)}, u32[]{:S(2)}, u32[]{:S(2)}) %collective-permute-start.16) | collective-permute-done | bytes 131104 | tf_op jit(solution)/shard_map/ppermute | solution.py:245
  41.8 1.5 %collective-permute-start.21 = (f32[2,256]{1,0:T(2,128)S(1)}, f32[2,256]{1,0:T(2,128)S(1)}, u32[]{:S(2)}, u32[]{:S(2)}) collective-permute-start(f32[2,256]{1,0:T(2,128)S(1)} %get-tuple-element.132.refs_0_), channel_id=1, source_target_pairs={{0,2},{1,3},{2,0},{3,1},{4,6},{5,7},{6,4},{7,5},{8,10},{9,11},{10,... | collective-permute-start | bytes 6152 | tf_op jit(solution)/shard_map/ppermute | solution.py:333
  43.7 1.8 %collective-permute-done.21.refs_2_ = f32[2,256]{1,0:T(2,128)S(1)} collective-permute-done((f32[2,256]{1,0:T(2,128)S(1)}, f32[2,256]{1,0:T(2,128)S(1)}, u32[]{:S(2)}, u32[]{:S(2)}) %collective-permute-start.21) | collective-permute-done | bytes 2080 | tf_op jit(solution)/shard_map/ppermute | solution.py:333
  45.5 0.9 collective-permute-done.22.refs_3_
  46.7 0.8 collective-permute-start.24
  47.5 1.3 %collective-permute-start.23 = (f32[2,128,128]{2,1,0:T(8,128)S(1)}, f32[2,128,128]{2,1,0:T(8,128)S(1)}, u32[]{:S(2)}, u32[]{:S(2)}) collective-permute-start(f32[2,128,128]{2,1,0:T(8,128)S(1)} %get-tuple-element.141), channel_id=1, source_target_pairs={{0,4},{4,0},{8,12},{12,8},{16,20},{20,16},{24,28},{28,24},{1,5},{5... | collective-permute-start | bytes 393224 | tf_op jit(solution)/shard_map/ppermute | solution.py:225
  49.3 0.8 collective-permute-start.28
  50.7 2.5 %collective-permute-done.24 = f32[2,128,128]{2,1,0:T(8,128)S(1)} collective-permute-done((f32[2,128,128]{2,1,0:T(8,128)S(1)}, f32[2,128,128]{2,1,0:T(8,128)S(1)}, u32[]{:S(2)}, u32[]{:S(2)}) %collective-permute-start.24) | collective-permute-done | bytes 131104 | tf_op jit(solution)/shard_map/ppermute | solution.py:225
  53.2 0.7 collective-permute-start.27
  53.9 2.1 %collective-permute-done.23 = f32[2,128,128]{2,1,0:T(8,128)S(1)} collective-permute-done((f32[2,128,128]{2,1,0:T(8,128)S(1)}, f32[2,128,128]{2,1,0:T(8,128)S(1)}, u32[]{:S(2)}, u32[]{:S(2)}) %collective-permute-start.23) | collective-permute-done | bytes 131104 | tf_op jit(solution)/shard_map/ppermute | solution.py:225
  56.7 0.8 collective-permute-start.26
  58.1 0.7 collective-permute-start.31
  59.5 2.2 %collective-permute-done.26 = f32[2,128,128]{2,1,0:T(8,128)S(1)} collective-permute-done((f32[2,128,128]{2,1,0:T(8,128)S(1)}, f32[2,128,128]{2,1,0:T(8,128)S(1)}, u32[]{:S(2)}, u32[]{:S(2)}) %collective-permute-start.26) | collective-permute-done | bytes 131104 | tf_op jit(solution)/shard_map/ppermute | solution.py:225
  63.8 1.8 %shard_map.87 = bf16[256,2048]{1,0:T(8,128)(2,1)S(1)} custom-call(s32[1]{0:T(128)} %bitcast.place, bf16[256,2048]{1,0:T(8,128)(2,1)S(1)} %copy-done.1, bf16[256,2048]{1,0:T(8,128)(2,1)S(1)} %copy-done.2, bf16[256,256]{1,0:T(8,128)(2,1)S(1)} %get-tuple-element.156.refs_0_, bf16[256,256]{1,0:T(8,128)(2,1)S(1)} %get-tuple-element.157.refs_1_.refs_0_, ...), custom_call_target="tpu_custom_call" | custom-call | flops 1024 | bytes 1024 | tf_op jit(solution)/shard_map/pallas_call | solution.py:43
  65.7 1.3 %collective-permute-start.33 = (f32[2,128,128]{2,1,0:T(8,128)S(1)}, f32[2,128,128]{2,1,0:T(8,128)S(1)}, u32[]{:S(2)}, u32[]{:S(2)}) collective-permute-start(f32[2,128,128]{2,1,0:T(8,128)S(1)} %get-tuple-element.207), channel_id=1, source_target_pairs={{12,4},{8,0},{13,5},{9,1},{14,6},{10,2},{15,7},{11,3}} | collective-permute-start | bytes 393224 | tf_op jit(solution)/shard_map/ppermute | solution.py:190
  67.8 1.3 %collective-permute-start.38 = (f32[2,128,128]{2,1,0:T(8,128)S(1)}, f32[2,128,128]{2,1,0:T(8,128)S(1)}, u32[]{:S(2)}, u32[]{:S(2)}) collective-permute-start(f32[2,128,128]{2,1,0:T(8,128)S(1)} %get-tuple-element.205), channel_id=1, source_target_pairs={{12,4},{8,0},{13,5},{9,1},{14,6},{10,2},{15,7},{11,3}} | collective-permute-start | bytes 393224 | tf_op jit(solution)/shard_map/ppermute | solution.py:190
  69.1 1.3 %collective-permute-start.37 = (f32[2,128,128]{2,1,0:T(8,128)S(1)}, f32[2,128,128]{2,1,0:T(8,128)S(1)}, u32[]{:S(2)}, u32[]{:S(2)}) collective-permute-start(f32[2,128,128]{2,1,0:T(8,128)S(1)} %get-tuple-element.203), channel_id=1, source_target_pairs={{12,4},{8,0},{13,5},{9,1},{14,6},{10,2},{15,7},{11,3}} | collective-permute-start | bytes 393224 | tf_op jit(solution)/shard_map/ppermute | solution.py:190
  70.4 6.7 %collective-permute-done.33 = f32[2,128,128]{2,1,0:T(8,128)S(1)} collective-permute-done((f32[2,128,128]{2,1,0:T(8,128)S(1)}, f32[2,128,128]{2,1,0:T(8,128)S(1)}, u32[]{:S(2)}, u32[]{:S(2)}) %collective-permute-start.33) | collective-permute-done | bytes 131104 | tf_op jit(solution)/shard_map/ppermute | solution.py:190
  77.1 1.8 %collective-permute-start.41 = (f32[2,128,128]{2,1,0:T(8,128)S(1)}, f32[2,128,128]{2,1,0:T(8,128)S(1)}, u32[]{:S(2)}, u32[]{:S(2)}) collective-permute-start(f32[2,128,128]{2,1,0:T(8,128)S(1)} %get-tuple-element.201), channel_id=1, source_target_pairs={{0,4},{4,0},{8,12},{12,8},{16,20},{20,16},{24,28},{28,24},{1,5},{5... | collective-permute-start | bytes 393224 | tf_op jit(solution)/shard_map/ppermute | solution.py:245
  79.0 1.5 %collective-permute-start.36 = (f32[2,128,128]{2,1,0:T(8,128)S(1)}, f32[2,128,128]{2,1,0:T(8,128)S(1)}, u32[]{:S(2)}, u32[]{:S(2)}) collective-permute-start(f32[2,128,128]{2,1,0:T(8,128)S(1)} %get-tuple-element.199), channel_id=1, source_target_pairs={{12,4},{8,0},{13,5},{9,1},{14,6},{10,2},{15,7},{11,3}} | collective-permute-start | bytes 393224 | tf_op jit(solution)/shard_map/ppermute | solution.py:190
  80.5 1.9 %collective-permute-start.42 = (f32[2,128,128]{2,1,0:T(8,128)S(1)}, f32[2,128,128]{2,1,0:T(8,128)S(1)}, u32[]{:S(2)}, u32[]{:S(2)}) collective-permute-start(f32[2,128,128]{2,1,0:T(8,128)S(1)} %get-tuple-element.197), channel_id=1, source_target_pairs={{0,4},{4,0},{8,12},{12,8},{16,20},{20,16},{24,28},{28,24},{1,5},{5... | collective-permute-start | bytes 393224 | tf_op jit(solution)/shard_map/ppermute | solution.py:245
  82.4 1.8 %shard_map.88 = (bf16[256,2048]{1,0:T(8,128)(2,1)}, bf16[256,2048]{1,0:T(8,128)(2,1)}) custom-call(s32[1]{0:T(128)} %bitcast.place, bf16[256,2048]{1,0:T(8,128)(2,1)S(1)} %copy-done, bf16[256,2048]{1,0:T(8,128)(2,1)S(1)} %copy-done.1, bf16[256,2048]{1,0:T(8,128)(2,1)S(1)} %copy-done.2, bf16[256,256]{1,0:T(8,128)(2,1)S(1)} %get-tuple-element.156.refs_0_, ...), custom_call_target="tpu_custom_call" | custom-call | flops 1024 | bytes 1024 | tf_op jit(solution)/shard_map/pallas_call | solution.py:43
  84.2 0.8 collective-permute-start.40
  85.0 0.8 collective-permute-done.36
  85.8 0.9 collective-permute-start.39
  86.7 1.0 %copy.24 = bf16[256,2048]{1,0:T(8,128)(2,1)} copy(bf16[256,2048]{1,0:T(8,128)(2,1)S(1)} %shard_map.87) | data formatting | bytes 2097152
  87.7 1.8 %shard_map.89 = (bf16[256,2048]{1,0:T(8,128)(2,1)}, bf16[256,2048]{1,0:T(8,128)(2,1)}) custom-call(s32[1]{0:T(128)} %bitcast.place, bf16[256,2048]{1,0:T(8,128)(2,1)S(1)} %copy-done, bf16[256,2048]{1,0:T(8,128)(2,1)S(1)} %copy-done.1, bf16[256,2048]{1,0:T(8,128)(2,1)S(1)} %copy-done.2, ...), custom_call_target="tpu_custom_call", output_to_operand_aliasing={{0}: (10, {}), {1}: (11, {})} | custom-call | flops 1024 | bytes 1024 | tf_op jit(solution)/shard_map/pallas_call | solution.py:43
  89.5 1.9 %shard_map.90 = (bf16[256,2048]{1,0:T(8,128)(2,1)}, bf16[256,2048]{1,0:T(8,128)(2,1)}) custom-call(s32[1]{0:T(128)} %bitcast.place, bf16[256,2048]{1,0:T(8,128)(2,1)S(1)} %copy-done, bf16[256,2048]{1,0:T(8,128)(2,1)S(1)} %copy-done.1, bf16[256,2048]{1,0:T(8,128)(2,1)S(1)} %copy-done.2, ...), custom_call_target="tpu_custom_call", output_to_operand_aliasing={{0}: (8, {}), {1}: (9, {})} | custom-call | flops 1024 | bytes 1024 | tf_op jit(solution)/shard_map/pallas_call | solution.py:43
  91.4 1.2 %shard_map.91 = (bf16[256,2048]{1,0:T(8,128)(2,1)}, bf16[256,2048]{1,0:T(8,128)(2,1)}) custom-call(s32[1]{0:T(128)} %bitcast.place, bf16[256,2048]{1,0:T(8,128)(2,1)S(1)} %copy-done, bf16[256,2048]{1,0:T(8,128)(2,1)S(1)} %copy-done.1, bf16[256,2048]{1,0:T(8,128)(2,1)S(1)} %copy-done.2, ...), custom_call_target="tpu_custom_call", output_to_operand_aliasing={{0}: (6, {}), {1}: (7, {})} | custom-call | flops 1024 | bytes 1024 | tf_op jit(solution)/shard_map/pallas_call | solution.py:43
  92.6 1.2 %shard_map.92 = (bf16[256,2048]{1,0:T(8,128)(2,1)}, bf16[256,2048]{1,0:T(8,128)(2,1)}) custom-call(s32[1]{0:T(128)} %bitcast.place, bf16[256,2048]{1,0:T(8,128)(2,1)S(1)} %copy-done, bf16[256,2048]{1,0:T(8,128)(2,1)S(1)} %copy-done.1, bf16[256,2048]{1,0:T(8,128)(2,1)S(1)} %copy-done.2, ...), custom_call_target="tpu_custom_call", output_to_operand_aliasing={{0}: (6, {}), {1}: (7, {})} | custom-call | flops 1024 | bytes 1024 | tf_op jit(solution)/shard_map/pallas_call | solution.py:43
  (99 shorter events, 13.3 us)
Async XLA Ops:
  2.0 9.1 %collective-permute-start = (f32[2,128,128]{2,1,0:T(8,128)S(1)}, f32[2,128,128]{2,1,0:T(8,128)S(1)}, u32[]{:S(2)}, u32[]{:S(2)}) collective-permute-start(f32[2,128,128]{2,1,0:T(8,128)S(1)} %get-tuple-element.103), channel_id=1, source_target_pairs={{0,4},{4,0},{8,12},{12,8},{16,20},{20,16},{24,28},{28,24},{1,5},{5... | collective-permute-start | bytes 393224 | tf_op jit(solution)/shard_map/ppermute | solution.py:225
  6.3 11.8 %collective-permute-start.3 = (f32[2,128,128]{2,1,0:T(8,128)S(1)}, f32[2,128,128]{2,1,0:T(8,128)S(1)}, u32[]{:S(2)}, u32[]{:S(2)}) collective-permute-start(f32[2,128,128]{2,1,0:T(8,128)S(1)} %get-tuple-element.107), channel_id=1, source_target_pairs={{0,4},{4,0},{8,12},{12,8},{16,20},{20,16},{24,28},{28,24},{1,5},{5... | collective-permute-start | bytes 393224 | tf_op jit(solution)/shard_map/ppermute | solution.py:225
  6.4 8.8 %collective-permute-start.4 = (f32[2,128,128]{2,1,0:T(8,128)S(1)}, f32[2,128,128]{2,1,0:T(8,128)S(1)}, u32[]{:S(2)}, u32[]{:S(2)}) collective-permute-start(f32[2,128,128]{2,1,0:T(8,128)S(1)} %get-tuple-element.109), channel_id=1, source_target_pairs={{0,4},{4,0},{8,12},{12,8},{16,20},{20,16},{24,28},{28,24},{1,5},{5... | collective-permute-start | bytes 393224 | tf_op jit(solution)/shard_map/ppermute | solution.py:225
  11.1 8.3 %collective-permute-start.2 = (f32[2,128,128]{2,1,0:T(8,128)S(1)}, f32[2,128,128]{2,1,0:T(8,128)S(1)}, u32[]{:S(2)}, u32[]{:S(2)}) collective-permute-start(f32[2,128,128]{2,1,0:T(8,128)S(1)} %get-tuple-element.234), channel_id=1, source_target_pairs={{0,8},{4,12},{1,9},{5,13},{2,10},{6,14},{3,11},{7,15}} | collective-permute-start | bytes 393224 | tf_op jit(solution)/shard_map/ppermute | solution.py:190
  14.6 5.6 %collective-permute-start.1 = (f32[2,128,128]{2,1,0:T(8,128)S(1)}, f32[2,128,128]{2,1,0:T(8,128)S(1)}, u32[]{:S(2)}, u32[]{:S(2)}) collective-permute-start(f32[2,128,128]{2,1,0:T(8,128)S(1)} %get-tuple-element.105), channel_id=1, source_target_pairs={{0,4},{4,0},{8,12},{12,8},{16,20},{20,16},{24,28},{28,24},{1,5},{5... | collective-permute-start | bytes 393224 | tf_op jit(solution)/shard_map/ppermute | solution.py:225
  15.2 8.5 %collective-permute-start.8 = (f32[2,128,128]{2,1,0:T(8,128)S(1)}, f32[2,128,128]{2,1,0:T(8,128)S(1)}, u32[]{:S(2)}, u32[]{:S(2)}) collective-permute-start(f32[2,128,128]{2,1,0:T(8,128)S(1)} %get-tuple-element.236), channel_id=1, source_target_pairs={{0,8},{4,12},{1,9},{5,13},{2,10},{6,14},{3,11},{7,15}} | collective-permute-start | bytes 393224 | tf_op jit(solution)/shard_map/ppermute | solution.py:190
  18.1 6.3 %collective-permute-start.7 = (f32[2,128,128]{2,1,0:T(8,128)S(1)}, f32[2,128,128]{2,1,0:T(8,128)S(1)}, u32[]{:S(2)}, u32[]{:S(2)}) collective-permute-start(f32[2,128,128]{2,1,0:T(8,128)S(1)} %get-tuple-element.238), channel_id=1, source_target_pairs={{0,8},{4,12},{1,9},{5,13},{2,10},{6,14},{3,11},{7,15}} | collective-permute-start | bytes 393224 | tf_op jit(solution)/shard_map/ppermute | solution.py:190
  19.4 5.6 %collective-permute-start.6 = (f32[2,128,128]{2,1,0:T(8,128)S(1)}, f32[2,128,128]{2,1,0:T(8,128)S(1)}, u32[]{:S(2)}, u32[]{:S(2)}) collective-permute-start(f32[2,128,128]{2,1,0:T(8,128)S(1)} %add.152), channel_id=1, source_target_pairs={{8,16},{12,20},{9,17},{13,21},{10,18},{14,22},{11,19},{15,23}} | collective-permute-start | bytes 393224 | tf_op jit(solution)/shard_map/ppermute | solution.py:190
  20.2 6.0 %collective-permute-start.5 = (f32[2,128,128]{2,1,0:T(8,128)S(1)}, f32[2,128,128]{2,1,0:T(8,128)S(1)}, u32[]{:S(2)}, u32[]{:S(2)}) collective-permute-start(f32[2,128,128]{2,1,0:T(8,128)S(1)} %get-tuple-element.240), channel_id=1, source_target_pairs={{0,8},{4,12},{1,9},{5,13},{2,10},{6,14},{3,11},{7,15}} | collective-permute-start | bytes 393224 | tf_op jit(solution)/shard_map/ppermute | solution.py:190
  23.7 3.2 %collective-permute-start.12 = (f32[2,128,128]{2,1,0:T(8,128)S(1)}, f32[2,128,128]{2,1,0:T(8,128)S(1)}, u32[]{:S(2)}, u32[]{:S(2)}) collective-permute-start(f32[2,128,128]{2,1,0:T(8,128)S(1)} %add.154), channel_id=1, source_target_pairs={{8,16},{12,20},{9,17},{13,21},{10,18},{14,22},{11,19},{15,23}} | collective-permute-start | bytes 393224 | tf_op jit(solution)/shard_map/ppermute | solution.py:190
  24.4 3.2 %collective-permute-start.11 = (f32[2,128,128]{2,1,0:T(8,128)S(1)}, f32[2,128,128]{2,1,0:T(8,128)S(1)}, u32[]{:S(2)}, u32[]{:S(2)}) collective-permute-start(f32[2,128,128]{2,1,0:T(8,128)S(1)} %add.155), channel_id=1, source_target_pairs={{8,16},{12,20},{9,17},{13,21},{10,18},{14,22},{11,19},{15,23}} | collective-permute-start | bytes 393224 | tf_op jit(solution)/shard_map/ppermute | solution.py:190
  25.1 3.2 %collective-permute-start.10 = (f32[2,128,128]{2,1,0:T(8,128)S(1)}, f32[2,128,128]{2,1,0:T(8,128)S(1)}, u32[]{:S(2)}, u32[]{:S(2)}) collective-permute-start(f32[2,128,128]{2,1,0:T(8,128)S(1)} %get-tuple-element.223), channel_id=1, source_target_pairs={{16,24},{20,28},{17,25},{21,29},{18,26},{22,30},{19,27},{23,31}} | collective-permute-start | bytes 393224 | tf_op jit(solution)/shard_map/ppermute | solution.py:190
  26.2 4.1 %collective-permute-start.9 = (f32[2,128,128]{2,1,0:T(8,128)S(1)}, f32[2,128,128]{2,1,0:T(8,128)S(1)}, u32[]{:S(2)}, u32[]{:S(2)}) collective-permute-start(f32[2,128,128]{2,1,0:T(8,128)S(1)} %add.158), channel_id=1, source_target_pairs={{8,16},{12,20},{9,17},{13,21},{10,18},{14,22},{11,19},{15,23}} | collective-permute-start | bytes 393224 | tf_op jit(solution)/shard_map/ppermute | solution.py:190
  26.9 4.2 %collective-permute-start.15 = (f32[2,128,128]{2,1,0:T(8,128)S(1)}, f32[2,128,128]{2,1,0:T(8,128)S(1)}, u32[]{:S(2)}, u32[]{:S(2)}) collective-permute-start(f32[2,128,128]{2,1,0:T(8,128)S(1)} %get-tuple-element.221), channel_id=1, source_target_pairs={{16,24},{20,28},{17,25},{21,29},{18,26},{22,30},{19,27},{23,31}} | collective-permute-start | bytes 393224 | tf_op jit(solution)/shard_map/ppermute | solution.py:190
  27.6 3.8 %collective-permute-start.14 = (f32[2,128,128]{2,1,0:T(8,128)S(1)}, f32[2,128,128]{2,1,0:T(8,128)S(1)}, u32[]{:S(2)}, u32[]{:S(2)}) collective-permute-start(f32[2,128,128]{2,1,0:T(8,128)S(1)} %get-tuple-element.219), channel_id=1, source_target_pairs={{16,24},{20,28},{17,25},{21,29},{18,26},{22,30},{19,27},{23,31}} | collective-permute-start | bytes 393224 | tf_op jit(solution)/shard_map/ppermute | solution.py:190
  28.3 5.7 %copy-start.2 = (bf16[256,2048]{1,0:T(8,128)(2,1)S(1)}, bf16[256,2048]{1,0:T(8,128)(2,1)}, u32[]{:S(2)}) copy-start(bf16[256,2048]{1,0:T(8,128)(2,1)} %v.15) | copy-start | bytes 3145732
  28.3 6.9 %collective-permute-start.19 = (f32[2,128,128]{2,1,0:T(8,128)S(1)}, f32[2,128,128]{2,1,0:T(8,128)S(1)}, u32[]{:S(2)}, u32[]{:S(2)}) collective-permute-start(f32[2,128,128]{2,1,0:T(8,128)S(1)} %get-tuple-element.217), channel_id=1, source_target_pairs={{0,4},{4,0},{8,12},{12,8},{16,20},{20,16},{24,28},{28,24},{1,5},{5... | collective-permute-start | bytes 393224 | tf_op jit(solution)/shard_map/ppermute | solution.py:245
  30.2 3.8 %copy-start.1 = (bf16[256,2048]{1,0:T(8,128)(2,1)S(1)}, bf16[256,2048]{1,0:T(8,128)(2,1)}, u32[]{:S(2)}) copy-start(bf16[256,2048]{1,0:T(8,128)(2,1)} %k.15) | copy-start | bytes 3145732
  30.3 3.8 %copy-start = (bf16[256,2048]{1,0:T(8,128)(2,1)S(1)}, bf16[256,2048]{1,0:T(8,128)(2,1)}, u32[]{:S(2)}) copy-start(bf16[256,2048]{1,0:T(8,128)(2,1)} %q.13) | copy-start | bytes 3145732
  30.3 3.0 %collective-permute-start.13 = (f32[2,128,128]{2,1,0:T(8,128)S(1)}, f32[2,128,128]{2,1,0:T(8,128)S(1)}, u32[]{:S(2)}, u32[]{:S(2)}) collective-permute-start(f32[2,128,128]{2,1,0:T(8,128)S(1)} %get-tuple-element.215), channel_id=1, source_target_pairs={{16,24},{20,28},{17,25},{21,29},{18,26},{22,30},{19,27},{23,31}} | collective-permute-start | bytes 393224 | tf_op jit(solution)/shard_map/ppermute | solution.py:190
  31.1 6.5 %collective-permute-start.18 = (f32[2,128,128]{2,1,0:T(8,128)S(1)}, f32[2,128,128]{2,1,0:T(8,128)S(1)}, u32[]{:S(2)}, u32[]{:S(2)}) collective-permute-start(f32[2,128,128]{2,1,0:T(8,128)S(1)} %get-tuple-element.213), channel_id=1, source_target_pairs={{0,4},{4,0},{8,12},{12,8},{16,20},{20,16},{24,28},{28,24},{1,5},{5... | collective-permute-start | bytes 393224 | tf_op jit(solution)/shard_map/ppermute | solution.py:245
  31.4 8.5 %collective-permute-start.17 = (f32[2,128,128]{2,1,0:T(8,128)S(1)}, f32[2,128,128]{2,1,0:T(8,128)S(1)}, u32[]{:S(2)}, u32[]{:S(2)}) collective-permute-start(f32[2,128,128]{2,1,0:T(8,128)S(1)} %get-tuple-element.211), channel_id=1, source_target_pairs={{0,4},{4,0},{8,12},{12,8},{16,20},{20,16},{24,28},{28,24},{1,5},{5... | collective-permute-start | bytes 393224 | tf_op jit(solution)/shard_map/ppermute | solution.py:245
  33.3 0.7 copy-start.4
  33.4 8.0 %collective-permute-start.16 = (f32[2,128,128]{2,1,0:T(8,128)S(1)}, f32[2,128,128]{2,1,0:T(8,128)S(1)}, u32[]{:S(2)}, u32[]{:S(2)}) collective-permute-start(f32[2,128,128]{2,1,0:T(8,128)S(1)} %get-tuple-element.209), channel_id=1, source_target_pairs={{0,4},{4,0},{8,12},{12,8},{16,20},{20,16},{24,28},{28,24},{1,5},{5... | collective-permute-start | bytes 393224 | tf_op jit(solution)/shard_map/ppermute | solution.py:245
  34.0 1.2 %copy-start.3 = (bf16[256,2048]{1,0:T(8,128)(2,1)S(1)}, bf16[256,2048]{1,0:T(8,128)(2,1)}, u32[]{:S(2)}) copy-start(bf16[256,2048]{1,0:T(8,128)(2,1)} %refs_7_.3) | copy-start | bytes 3145732
  41.7 1.9 %collective-permute-start.20 = (f32[2,256]{1,0:T(2,128)S(1)}, f32[2,256]{1,0:T(2,128)S(1)}, u32[]{:S(2)}, u32[]{:S(2)}) collective-permute-start(f32[2,256]{1,0:T(2,128)S(1)} %get-tuple-element.132.refs_0_), channel_id=1, source_target_pairs={{0,1},{1,0},{2,3},{3,2},{4,5},{5,4},{6,7},{7,6},{8,9},{9,8},{10,11... | collective-permute-start | bytes 6152 | tf_op jit(solution)/shard_map/ppermute | solution.py:333
  41.8 3.7 %collective-permute-start.21 = (f32[2,256]{1,0:T(2,128)S(1)}, f32[2,256]{1,0:T(2,128)S(1)}, u32[]{:S(2)}, u32[]{:S(2)}) collective-permute-start(f32[2,256]{1,0:T(2,128)S(1)} %get-tuple-element.132.refs_0_), channel_id=1, source_target_pairs={{0,2},{1,3},{2,0},{3,1},{4,6},{5,7},{6,4},{7,5},{8,10},{9,11},{10,... | collective-permute-start | bytes 6152 | tf_op jit(solution)/shard_map/ppermute | solution.py:333
  43.3 3.0 %collective-permute-start.22 = (f32[2,256]{1,0:T(2,128)S(1)}, f32[2,256]{1,0:T(2,128)S(1)}, u32[]{:S(2)}, u32[]{:S(2)}) collective-permute-start(f32[2,256]{1,0:T(2,128)S(1)} %get-tuple-element.132.refs_0_), channel_id=1, source_target_pairs={{0,3},{1,2},{2,1},{3,0},{4,7},{5,6},{6,5},{7,4},{8,11},{9,10},{10,... | collective-permute-start | bytes 6152 | tf_op jit(solution)/shard_map/ppermute | solution.py:333
  46.7 6.4 %collective-permute-start.24 = (f32[2,128,128]{2,1,0:T(8,128)S(1)}, f32[2,128,128]{2,1,0:T(8,128)S(1)}, u32[]{:S(2)}, u32[]{:S(2)}) collective-permute-start(f32[2,128,128]{2,1,0:T(8,128)S(1)} %get-tuple-element.143), channel_id=1, source_target_pairs={{0,4},{4,0},{8,12},{12,8},{16,20},{20,16},{24,28},{28,24},{1,5},{5... | collective-permute-start | bytes 393224 | tf_op jit(solution)/shard_map/ppermute | solution.py:225
  47.5 8.4 %collective-permute-start.23 = (f32[2,128,128]{2,1,0:T(8,128)S(1)}, f32[2,128,128]{2,1,0:T(8,128)S(1)}, u32[]{:S(2)}, u32[]{:S(2)}) collective-permute-start(f32[2,128,128]{2,1,0:T(8,128)S(1)} %get-tuple-element.141), channel_id=1, source_target_pairs={{0,4},{4,0},{8,12},{12,8},{16,20},{20,16},{24,28},{28,24},{1,5},{5... | collective-permute-start | bytes 393224 | tf_op jit(solution)/shard_map/ppermute | solution.py:225
  49.3 8.8 %collective-permute-start.28 = (f32[2,128,128]{2,1,0:T(8,128)S(1)}, f32[2,128,128]{2,1,0:T(8,128)S(1)}, u32[]{:S(2)}, u32[]{:S(2)}) collective-permute-start(f32[2,128,128]{2,1,0:T(8,128)S(1)} %get-tuple-element.151), channel_id=1, source_target_pairs={{0,4},{4,0},{8,12},{12,8},{16,20},{20,16},{24,28},{28,24},{1,5},{5... | collective-permute-start | bytes 393224 | tf_op jit(solution)/shard_map/ppermute | solution.py:225
  53.2 5.6 %collective-permute-start.27 = (f32[2,128,128]{2,1,0:T(8,128)S(1)}, f32[2,128,128]{2,1,0:T(8,128)S(1)}, u32[]{:S(2)}, u32[]{:S(2)}) collective-permute-start(f32[2,128,128]{2,1,0:T(8,128)S(1)} %get-tuple-element.232), channel_id=1, source_target_pairs={{28,20},{24,16},{29,21},{25,17},{30,22},{26,18},{31,23},{27,19}} | collective-permute-start | bytes 393224 | tf_op jit(solution)/shard_map/ppermute | solution.py:190
  56.0 6.4 %collective-permute-start.25 = (f32[2,128,128]{2,1,0:T(8,128)S(1)}, f32[2,128,128]{2,1,0:T(8,128)S(1)}, u32[]{:S(2)}, u32[]{:S(2)}) collective-permute-start(f32[2,128,128]{2,1,0:T(8,128)S(1)} %get-tuple-element.230), channel_id=1, source_target_pairs={{28,20},{24,16},{29,21},{25,17},{30,22},{26,18},{31,23},{27,19}} | collective-permute-start | bytes 393224 | tf_op jit(solution)/shard_map/ppermute | solution.py:190
  56.7 5.0 %collective-permute-start.26 = (f32[2,128,128]{2,1,0:T(8,128)S(1)}, f32[2,128,128]{2,1,0:T(8,128)S(1)}, u32[]{:S(2)}, u32[]{:S(2)}) collective-permute-start(f32[2,128,128]{2,1,0:T(8,128)S(1)} %get-tuple-element.149), channel_id=1, source_target_pairs={{0,4},{4,0},{8,12},{12,8},{16,20},{20,16},{24,28},{28,24},{1,5},{5... | collective-permute-start | bytes 393224 | tf_op jit(solution)/shard_map/ppermute | solution.py:225
  58.1 5.0 %collective-permute-start.31 = (f32[2,128,128]{2,1,0:T(8,128)S(1)}, f32[2,128,128]{2,1,0:T(8,128)S(1)}, u32[]{:S(2)}, u32[]{:S(2)}) collective-permute-start(f32[2,128,128]{2,1,0:T(8,128)S(1)} %get-tuple-element.228), channel_id=1, source_target_pairs={{28,20},{24,16},{29,21},{25,17},{30,22},{26,18},{31,23},{27,19}} | collective-permute-start | bytes 393224 | tf_op jit(solution)/shard_map/ppermute | solution.py:190
  58.8 6.9 %collective-permute-start.30 = (f32[2,128,128]{2,1,0:T(8,128)S(1)}, f32[2,128,128]{2,1,0:T(8,128)S(1)}, u32[]{:S(2)}, u32[]{:S(2)}) collective-permute-start(f32[2,128,128]{2,1,0:T(8,128)S(1)} %add.176), channel_id=1, source_target_pairs={{20,12},{16,8},{21,13},{17,9},{22,14},{18,10},{23,15},{19,11}} | collective-permute-start | bytes 393224 | tf_op jit(solution)/shard_map/ppermute | solution.py:190
  61.7 5.3 %collective-permute-start.29 = (f32[2,128,128]{2,1,0:T(8,128)S(1)}, f32[2,128,128]{2,1,0:T(8,128)S(1)}, u32[]{:S(2)}, u32[]{:S(2)}) collective-permute-start(f32[2,128,128]{2,1,0:T(8,128)S(1)} %get-tuple-element.226), channel_id=1, source_target_pairs={{28,20},{24,16},{29,21},{25,17},{30,22},{26,18},{31,23},{27,19}} | collective-permute-start | bytes 393224 | tf_op jit(solution)/shard_map/ppermute | solution.py:190
  62.4 5.3 %collective-permute-start.35 = (f32[2,128,128]{2,1,0:T(8,128)S(1)}, f32[2,128,128]{2,1,0:T(8,128)S(1)}, u32[]{:S(2)}, u32[]{:S(2)}) collective-permute-start(f32[2,128,128]{2,1,0:T(8,128)S(1)} %add.178), channel_id=1, source_target_pairs={{20,12},{16,8},{21,13},{17,9},{22,14},{18,10},{23,15},{19,11}} | collective-permute-start | bytes 393224 | tf_op jit(solution)/shard_map/ppermute | solution.py:190
  63.1 5.9 %collective-permute-start.34 = (f32[2,128,128]{2,1,0:T(8,128)S(1)}, f32[2,128,128]{2,1,0:T(8,128)S(1)}, u32[]{:S(2)}, u32[]{:S(2)}) collective-permute-start(f32[2,128,128]{2,1,0:T(8,128)S(1)} %add.179), channel_id=1, source_target_pairs={{20,12},{16,8},{21,13},{17,9},{22,14},{18,10},{23,15},{19,11}} | collective-permute-start | bytes 393224 | tf_op jit(solution)/shard_map/ppermute | solution.py:190
  65.7 11.4 %collective-permute-start.33 = (f32[2,128,128]{2,1,0:T(8,128)S(1)}, f32[2,128,128]{2,1,0:T(8,128)S(1)}, u32[]{:S(2)}, u32[]{:S(2)}) collective-permute-start(f32[2,128,128]{2,1,0:T(8,128)S(1)} %get-tuple-element.207), channel_id=1, source_target_pairs={{12,4},{8,0},{13,5},{9,1},{14,6},{10,2},{15,7},{11,3}} | collective-permute-start | bytes 393224 | tf_op jit(solution)/shard_map/ppermute | solution.py:190
  67.0 11.9 %collective-permute-start.32 = (f32[2,128,128]{2,1,0:T(8,128)S(1)}, f32[2,128,128]{2,1,0:T(8,128)S(1)}, u32[]{:S(2)}, u32[]{:S(2)}) collective-permute-start(f32[2,128,128]{2,1,0:T(8,128)S(1)} %add.182), channel_id=1, source_target_pairs={{20,12},{16,8},{21,13},{17,9},{22,14},{18,10},{23,15},{19,11}} | collective-permute-start | bytes 393224 | tf_op jit(solution)/shard_map/ppermute | solution.py:190
  67.8 12.7 %collective-permute-start.38 = (f32[2,128,128]{2,1,0:T(8,128)S(1)}, f32[2,128,128]{2,1,0:T(8,128)S(1)}, u32[]{:S(2)}, u32[]{:S(2)}) collective-permute-start(f32[2,128,128]{2,1,0:T(8,128)S(1)} %get-tuple-element.205), channel_id=1, source_target_pairs={{12,4},{8,0},{13,5},{9,1},{14,6},{10,2},{15,7},{11,3}} | collective-permute-start | bytes 393224 | tf_op jit(solution)/shard_map/ppermute | solution.py:190
  69.1 15.1 %collective-permute-start.37 = (f32[2,128,128]{2,1,0:T(8,128)S(1)}, f32[2,128,128]{2,1,0:T(8,128)S(1)}, u32[]{:S(2)}, u32[]{:S(2)}) collective-permute-start(f32[2,128,128]{2,1,0:T(8,128)S(1)} %get-tuple-element.203), channel_id=1, source_target_pairs={{12,4},{8,0},{13,5},{9,1},{14,6},{10,2},{15,7},{11,3}} | collective-permute-start | bytes 393224 | tf_op jit(solution)/shard_map/ppermute | solution.py:190
  77.1 12.4 %collective-permute-start.41 = (f32[2,128,128]{2,1,0:T(8,128)S(1)}, f32[2,128,128]{2,1,0:T(8,128)S(1)}, u32[]{:S(2)}, u32[]{:S(2)}) collective-permute-start(f32[2,128,128]{2,1,0:T(8,128)S(1)} %get-tuple-element.201), channel_id=1, source_target_pairs={{0,4},{4,0},{8,12},{12,8},{16,20},{20,16},{24,28},{28,24},{1,5},{5... | collective-permute-start | bytes 393224 | tf_op jit(solution)/shard_map/ppermute | solution.py:245
  79.0 6.9 %collective-permute-start.36 = (f32[2,128,128]{2,1,0:T(8,128)S(1)}, f32[2,128,128]{2,1,0:T(8,128)S(1)}, u32[]{:S(2)}, u32[]{:S(2)}) collective-permute-start(f32[2,128,128]{2,1,0:T(8,128)S(1)} %get-tuple-element.199), channel_id=1, source_target_pairs={{12,4},{8,0},{13,5},{9,1},{14,6},{10,2},{15,7},{11,3}} | collective-permute-start | bytes 393224 | tf_op jit(solution)/shard_map/ppermute | solution.py:190
  80.5 9.0 %collective-permute-start.42 = (f32[2,128,128]{2,1,0:T(8,128)S(1)}, f32[2,128,128]{2,1,0:T(8,128)S(1)}, u32[]{:S(2)}, u32[]{:S(2)}) collective-permute-start(f32[2,128,128]{2,1,0:T(8,128)S(1)} %get-tuple-element.197), channel_id=1, source_target_pairs={{0,4},{4,0},{8,12},{12,8},{16,20},{20,16},{24,28},{28,24},{1,5},{5... | collective-permute-start | bytes 393224 | tf_op jit(solution)/shard_map/ppermute | solution.py:245
  84.2 7.2 %collective-permute-start.40 = (f32[2,128,128]{2,1,0:T(8,128)S(1)}, f32[2,128,128]{2,1,0:T(8,128)S(1)}, u32[]{:S(2)}, u32[]{:S(2)}) collective-permute-start(f32[2,128,128]{2,1,0:T(8,128)S(1)} %get-tuple-element.195), channel_id=1, source_target_pairs={{0,4},{4,0},{8,12},{12,8},{16,20},{20,16},{24,28},{28,24},{1,5},{5... | collective-permute-start | bytes 393224 | tf_op jit(solution)/shard_map/ppermute | solution.py:245
  85.8 6.8 %collective-permute-start.39 = (f32[2,128,128]{2,1,0:T(8,128)S(1)}, f32[2,128,128]{2,1,0:T(8,128)S(1)}, u32[]{:S(2)}, u32[]{:S(2)}) collective-permute-start(f32[2,128,128]{2,1,0:T(8,128)S(1)} %get-tuple-element.193), channel_id=1, source_target_pairs={{0,4},{4,0},{8,12},{12,8},{16,20},{20,16},{24,28},{28,24},{1,5},{5... | collective-permute-start | bytes 393224 | tf_op jit(solution)/shard_map/ppermute | solution.py:245

commit v15 on v14

--- a/solution.py
+++ b/solution.py
@@ -389,21 +389,23 @@
         query_made = []
         made = []
 
-        def pair(c):
+        def kept_units(first, count=1):
             def work(out, sends):
-                made[:] = rest([(c, 0), (c + 1, 0)], out, made)
+                made[:] = rest([(c, 0) for c in range(first, first + count)], out, made)
                 return made[0]
             return work
 
         beside = {
-            (2, 0): lambda out, sends: query(sends[1, 1]),
-            (long - 1, 2): pair(0),
+            (2, 0): lambda out, sends: query(sends[1, 2]),
+            (long - 1, 2): kept_units(0, 2),
+            (long - 1, 3): kept_units(2, 1),
         } if spread else {}
         after = scan(kept, sent, ends, True, [], beside)
         if not spread:
             query()
-        for c in range(2 if spread else 0, CHUNKS, 2):
-            pair(c)(after, None)
+        if not spread:
+            kept_units(0, 3)(after, None)
+        kept_units(3, 1)(after, None)
         made = rest([(0, 1), (1, 1)], after, made)
         for c in range(2, CHUNKS):
             made = rest([(c, 1)], after, made)

time: 94.4 us -> 92.8 us (0.983)
  waiting for transfers between devices: 23.2 us -> 22 us
    ppermute x8, starting transfers between devices: 9.3 us -> 11.6 us  [swap_after(): flight[c] = lax.ppermute(part_sent, 'seq', swap)]
    ppermute x24, starting transfers between devices: 27.4 us -> 25.2 us  [hop(): return lax.ppermute(array, 'seq', pairs)]
    ppermute x24, waiting for transfers between devices: 7.9 us -> 9.3 us  [hop(): return lax.ppermute(array, 'seq', pairs)]
    pallas_call x17 -> x18, Pallas kernels: 18.9 us -> 19.5 us  [call(): pl.pallas_call(body, grid_spec=pltpu.PrefetchScalarGridSpec(num_scalar_pr...]
  transfers between devices with their start and end apart: 43 -> 43, of which waited for: 12 -> 13; matrix products, arithmetic and copies ran while one was open for 2% -> 2% of each run, Pallas kernels for 17% -> 18%
where the time goes in v15:
time: 92.8 us; the launch traced here: 92.2 us
  starting transfers between devices  47.6 us (51%)
  waiting for transfers between devices  22 us (24%)
  Pallas kernels  19.5 us (21%)
  between operations  1.3 us (1%)
  local copies, waits for them, and re-layouts  1.05 us (1%)
    ppermute x24, starting transfers between devices, hop(): return lax.ppermute(array, 'seq', pairs)  25.2 us
    pallas_call x18, Pallas kernels, call(): pl.pallas_call(body, grid_spec=pltpu.PrefetchScalarGridSpec(num_scalar_pr...  19.5 us
    ppermute x8, starting transfers between devices, swap_after(): flight[c] = lax.ppermute(part_sent, 'seq', swap)  11.6 us
    ppermute x24, waiting for transfers between devices, hop(): return lax.ppermute(array, 'seq', pairs)  9.3 us
    ppermute x8, starting transfers between devices, scan(): out[c] = (carry[c], own[c], lax.ppermute(send, 'seq', swap))  8.91 us
    ppermute x8, waiting for transfers between devices, swap_after(): flight[c] = lax.ppermute(part_sent, 'seq', swap)  6.69 us
    ppermute x8, waiting for transfers between devices, scan(): out[c] = (carry[c], own[c], lax.ppermute(send, 'seq', swap))  4.22 us
    ppermute x3, starting transfers between devices, shards(): lax.ppermute(mine, 'head', [(i, i ^ step if paired else (i + step) % part...  1.92 us
  transfers between devices with their start and end apart: 43, of which 13 were waited for; matrix products, arithmetic and copies ran while one was open for 2% of the time, Pallas kernels for 18%

profile of v15, /device:TPU:0, one launch (start us, length us, event | category | flops | bytes accessed | tf_op | source)
XLA Modules:
  0.0 92.2 jit_solution(16262851326747642664)
XLA Ops:
  0.6 1.3 %shard_map.78 = (f32[2,128,128]{2,1,0:T(8,128)S(1)}, f32[2,128,128]{2,1,0:T(8,128)S(1)}) custom-call(s32[1]{0:T(128)} %bitcast.place, bf16[256,2048]{1,0:T(8,128)(2,1)} %k.17, bf16[256,2048]{1,0:T(8,128)(2,1)} %v.17), custom_call_target="tpu_custom_call" | custom-call | flops 1024 | bytes 1024 | tf_op jit(solution)/shard_map/pallas_call | solution.py:43
  2.0 3.0 %collective-permute-start = (f32[2,128,128]{2,1,0:T(8,128)S(1)}, f32[2,128,128]{2,1,0:T(8,128)S(1)}, u32[]{:S(2)}, u32[]{:S(2)}) collective-permute-start(f32[2,128,128]{2,1,0:T(8,128)S(1)} %get-tuple-element.105), channel_id=1, source_target_pairs={{0,4},{4,0},{8,12},{12,8},{16,20},{20,16},{24,28},{28,24},{1,5},{5... | collective-permute-start | bytes 393224 | tf_op jit(solution)/shard_map/ppermute | solution.py:225
  5.1 1.3 %shard_map.77 = (f32[2,128,128]{2,1,0:T(8,128)S(1)}, f32[2,128,128]{2,1,0:T(8,128)S(1)}) custom-call(s32[1]{0:T(128)} %bitcast.place, bf16[256,2048]{1,0:T(8,128)(2,1)} %k.17, bf16[256,2048]{1,0:T(8,128)(2,1)} %v.17), custom_call_target="tpu_custom_call" | custom-call | flops 1024 | bytes 1024 | tf_op jit(solution)/shard_map/pallas_call | solution.py:43
  6.4 2.0 %collective-permute-start.3 = (f32[2,128,128]{2,1,0:T(8,128)S(1)}, f32[2,128,128]{2,1,0:T(8,128)S(1)}, u32[]{:S(2)}, u32[]{:S(2)}) collective-permute-start(f32[2,128,128]{2,1,0:T(8,128)S(1)} %get-tuple-element.109), channel_id=1, source_target_pairs={{0,4},{4,0},{8,12},{12,8},{16,20},{20,16},{24,28},{28,24},{1,5},{5... | collective-permute-start | bytes 393224 | tf_op jit(solution)/shard_map/ppermute | solution.py:225
  8.4 2.6 %shard_map.76 = (f32[2,128,128]{2,1,0:T(8,128)S(1)}, f32[2,128,128]{2,1,0:T(8,128)S(1)}, f32[2,128,128]{2,1,0:T(8,128)S(1)}, f32[2,128,128]{2,1,0:T(8,128)S(1)}, f32[256,1024]{1,0:T(8,128)S(1)}) custom-call(s32[1]{0:T(128)} %bitcast.place, bf16[256,2048]{1,0:T(8,128)(2,1)} %q.15, bf16[256,2048]{1,0:T(8,128)(2,1)} %k.17, bf16[256,2048]{1,0:T(8,128)(2,1)} %v.17), custom_call_target="tpu_custom_call" | custom-call | flops 1024 | bytes 1024 | tf_op jit(solution)/shard_map/pallas_call | solution.py:43
  11.1 3.5 %collective-permute-start.2 = (f32[2,128,128]{2,1,0:T(8,128)S(1)}, f32[2,128,128]{2,1,0:T(8,128)S(1)}, u32[]{:S(2)}, u32[]{:S(2)}) collective-permute-start(f32[2,128,128]{2,1,0:T(8,128)S(1)} %get-tuple-element.238), channel_id=1, source_target_pairs={{0,8},{4,12},{1,9},{5,13},{2,10},{6,14},{3,11},{7,15}} | collective-permute-start | bytes 393224 | tf_op jit(solution)/shard_map/ppermute | solution.py:190
  14.6 1.6 %collective-permute-start.8 = (f32[2,128,128]{2,1,0:T(8,128)S(1)}, f32[2,128,128]{2,1,0:T(8,128)S(1)}, u32[]{:S(2)}, u32[]{:S(2)}) collective-permute-start(f32[2,128,128]{2,1,0:T(8,128)S(1)} %get-tuple-element.240), channel_id=1, source_target_pairs={{0,8},{4,12},{1,9},{5,13},{2,10},{6,14},{3,11},{7,15}} | collective-permute-start | bytes 393224 | tf_op jit(solution)/shard_map/ppermute | solution.py:190
  16.2 1.6 %collective-permute-start.1 = (f32[2,128,128]{2,1,0:T(8,128)S(1)}, f32[2,128,128]{2,1,0:T(8,128)S(1)}, u32[]{:S(2)}, u32[]{:S(2)}) collective-permute-start(f32[2,128,128]{2,1,0:T(8,128)S(1)} %get-tuple-element.107), channel_id=1, source_target_pairs={{0,4},{4,0},{8,12},{12,8},{16,20},{20,16},{24,28},{28,24},{1,5},{5... | collective-permute-start | bytes 393224 | tf_op jit(solution)/shard_map/ppermute | solution.py:225
  17.8 1.6 %collective-permute-start.7 = (f32[2,128,128]{2,1,0:T(8,128)S(1)}, f32[2,128,128]{2,1,0:T(8,128)S(1)}, u32[]{:S(2)}, u32[]{:S(2)}) collective-permute-start(f32[2,128,128]{2,1,0:T(8,128)S(1)} %get-tuple-element.242), channel_id=1, source_target_pairs={{0,8},{4,12},{1,9},{5,13},{2,10},{6,14},{3,11},{7,15}} | collective-permute-start | bytes 393224 | tf_op jit(solution)/shard_map/ppermute | solution.py:190
  20.1 1.2 %collective-permute-done.1 = f32[2,128,128]{2,1,0:T(8,128)S(1)} collective-permute-done((f32[2,128,128]{2,1,0:T(8,128)S(1)}, f32[2,128,128]{2,1,0:T(8,128)S(1)}, u32[]{:S(2)}, u32[]{:S(2)}) %collective-permute-start.1) | collective-permute-done | bytes 131104 | tf_op jit(solution)/shard_map/ppermute | solution.py:225
  21.2 2.4 %collective-permute-start.5 = (f32[2,128,128]{2,1,0:T(8,128)S(1)}, f32[2,128,128]{2,1,0:T(8,128)S(1)}, u32[]{:S(2)}, u32[]{:S(2)}) collective-permute-start(f32[2,128,128]{2,1,0:T(8,128)S(1)} %get-tuple-element.244), channel_id=1, source_target_pairs={{0,8},{4,12},{1,9},{5,13},{2,10},{6,14},{3,11},{7,15}} | collective-permute-start | bytes 393224 | tf_op jit(solution)/shard_map/ppermute | solution.py:190
  24.4 0.7 collective-permute-start.11
  28.3 0.8 collective-permute-start.19
  29.1 0.8 collective-permute-start.13
  30.0 1.4 %collective-permute-start.18 = (f32[2,128,128]{2,1,0:T(8,128)S(1)}, f32[2,128,128]{2,1,0:T(8,128)S(1)}, u32[]{:S(2)}, u32[]{:S(2)}) collective-permute-start(f32[2,128,128]{2,1,0:T(8,128)S(1)} %get-tuple-element.217), channel_id=1, source_target_pairs={{0,4},{4,0},{8,12},{12,8},{16,20},{20,16},{24,28},{28,24},{1,5},{5... | collective-permute-start | bytes 393224 | tf_op jit(solution)/shard_map/ppermute | solution.py:245
  31.4 0.8 collective-permute-start.17
  32.2 1.4 %collective-permute-start.16 = (f32[2,128,128]{2,1,0:T(8,128)S(1)}, f32[2,128,128]{2,1,0:T(8,128)S(1)}, u32[]{:S(2)}, u32[]{:S(2)}) collective-permute-start(f32[2,128,128]{2,1,0:T(8,128)S(1)} %get-tuple-element.213), channel_id=1, source_target_pairs={{0,4},{4,0},{8,12},{12,8},{16,20},{20,16},{24,28},{28,24},{1,5},{5... | collective-permute-start | bytes 393224 | tf_op jit(solution)/shard_map/ppermute | solution.py:245
  33.7 1.1 %shard_map.79.al_o = f32[256,1024]{1,0:T(8,128)S(1)} custom-call(s32[1]{0:T(128)} %bitcast.place, bf16[256,2048]{1,0:T(8,128)(2,1)S(1)} %copy-done, bf16[256,2048]{1,0:T(8,128)(2,1)S(1)} %copy-done.1, bf16[256,2048]{1,0:T(8,128)(2,1)S(1)} %copy-done.2, f32[2,128,128]{2,1,0:T(8,128)S(1)} %get-tuple-element.214.refs_0_.e), custom_call_target="tpu_custom_call" | custom-call | flops 1024 | bytes 1024 | tf_op jit(solution)/shard_map/pallas_call | solution.py:43
  35.2 2.0 %collective-permute-done.18.other = f32[2,128,128]{2,1,0:T(8,128)S(1)} collective-permute-done((f32[2,128,128]{2,1,0:T(8,128)S(1)}, f32[2,128,128]{2,1,0:T(8,128)S(1)}, u32[]{:S(2)}, u32[]{:S(2)}) %collective-permute-start.18) | collective-permute-done | bytes 131104 | tf_op jit(solution)/shard_map/ppermute | solution.py:245
  37.5 1.1 %collective-permute-done.17.other = f32[2,128,128]{2,1,0:T(8,128)S(1)} collective-permute-done((f32[2,128,128]{2,1,0:T(8,128)S(1)}, f32[2,128,128]{2,1,0:T(8,128)S(1)}, u32[]{:S(2)}, u32[]{:S(2)}) %collective-permute-start.17) | collective-permute-done | bytes 131104 | tf_op jit(solution)/shard_map/ppermute | solution.py:245
  38.9 1.1 %collective-permute-done.16.other = f32[2,128,128]{2,1,0:T(8,128)S(1)} collective-permute-done((f32[2,128,128]{2,1,0:T(8,128)S(1)}, f32[2,128,128]{2,1,0:T(8,128)S(1)}, u32[]{:S(2)}, u32[]{:S(2)}) %collective-permute-start.16) | collective-permute-done | bytes 131104 | tf_op jit(solution)/shard_map/ppermute | solution.py:245
  40.5 1.6 %collective-permute-start.21 = (f32[2,256]{1,0:T(2,128)S(1)}, f32[2,256]{1,0:T(2,128)S(1)}, u32[]{:S(2)}, u32[]{:S(2)}) collective-permute-start(f32[2,256]{1,0:T(2,128)S(1)} %get-tuple-element.134.refs_0_), channel_id=1, source_target_pairs={{0,2},{1,3},{2,0},{3,1},{4,6},{5,7},{6,4},{7,5},{8,10},{9,11},{10,... | collective-permute-start | bytes 6152 | tf_op jit(solution)/shard_map/ppermute | solution.py:333
  42.3 1.1 %collective-permute-done.22.refs_3_ = f32[2,256]{1,0:T(2,128)S(1)} collective-permute-done((f32[2,256]{1,0:T(2,128)S(1)}, f32[2,256]{1,0:T(2,128)S(1)}, u32[]{:S(2)}, u32[]{:S(2)}) %collective-permute-start.22) | collective-permute-done | bytes 2080 | tf_op jit(solution)/shard_map/ppermute | solution.py:333
  44.5 1.4 %collective-permute-start.25 = (f32[2,128,128]{2,1,0:T(8,128)S(1)}, f32[2,128,128]{2,1,0:T(8,128)S(1)}, u32[]{:S(2)}, u32[]{:S(2)}) collective-permute-start(f32[2,128,128]{2,1,0:T(8,128)S(1)} %get-tuple-element.149), channel_id=1, source_target_pairs={{0,4},{4,0},{8,12},{12,8},{16,20},{20,16},{24,28},{28,24},{1,5},{5... | collective-permute-start | bytes 393224 | tf_op jit(solution)/shard_map/ppermute | solution.py:225
  46.4 0.8 collective-permute-start.24
  47.1 1.3 %collective-permute-start.23 = (f32[2,128,128]{2,1,0:T(8,128)S(1)}, f32[2,128,128]{2,1,0:T(8,128)S(1)}, u32[]{:S(2)}, u32[]{:S(2)}) collective-permute-start(f32[2,128,128]{2,1,0:T(8,128)S(1)} %get-tuple-element.143), channel_id=1, source_target_pairs={{0,4},{4,0},{8,12},{12,8},{16,20},{20,16},{24,28},{28,24},{1,5},{5... | collective-permute-start | bytes 393224 | tf_op jit(solution)/shard_map/ppermute | solution.py:225
  49.1 1.8 %collective-permute-done.25 = f32[2,128,128]{2,1,0:T(8,128)S(1)} collective-permute-done((f32[2,128,128]{2,1,0:T(8,128)S(1)}, f32[2,128,128]{2,1,0:T(8,128)S(1)}, u32[]{:S(2)}, u32[]{:S(2)}) %collective-permute-start.25) | collective-permute-done | bytes 131104 | tf_op jit(solution)/shard_map/ppermute | solution.py:225
  51.6 1.4 %collective-permute-start.28 = (f32[2,128,128]{2,1,0:T(8,128)S(1)}, f32[2,128,128]{2,1,0:T(8,128)S(1)}, u32[]{:S(2)}, u32[]{:S(2)}) collective-permute-start(f32[2,128,128]{2,1,0:T(8,128)S(1)} %get-tuple-element.154), channel_id=1, source_target_pairs={{0,4},{4,0},{8,12},{12,8},{16,20},{20,16},{24,28},{28,24},{1,5},{5... | collective-permute-start | bytes 393224 | tf_op jit(solution)/shard_map/ppermute | solution.py:225
  53.0 0.7 collective-permute-done.24
  54.4 2.1 %collective-permute-done.23 = f32[2,128,128]{2,1,0:T(8,128)S(1)} collective-permute-done((f32[2,128,128]{2,1,0:T(8,128)S(1)}, f32[2,128,128]{2,1,0:T(8,128)S(1)}, u32[]{:S(2)}, u32[]{:S(2)}) %collective-permute-start.23) | collective-permute-done | bytes 131104 | tf_op jit(solution)/shard_map/ppermute | solution.py:225
  58.0 0.8 collective-permute-done.28
  60.9 1.8 %shard_map.87 = bf16[256,2048]{1,0:T(8,128)(2,1)S(1)} custom-call(s32[1]{0:T(128)} %bitcast.place, bf16[256,2048]{1,0:T(8,128)(2,1)S(1)} %copy-done.1, bf16[256,2048]{1,0:T(8,128)(2,1)S(1)} %copy-done.2, bf16[256,256]{1,0:T(8,128)(2,1)S(1)} %get-tuple-element.159.refs_0_, bf16[256,256]{1,0:T(8,128)(2,1)S(1)} %get-tuple-element.160.refs_1_.refs_0_, ...), custom_call_target="tpu_custom_call" | custom-call | flops 1024 | bytes 1024 | tf_op jit(solution)/shard_map/pallas_call | solution.py:43
  62.8 1.3 %collective-permute-start.33 = (f32[2,128,128]{2,1,0:T(8,128)S(1)}, f32[2,128,128]{2,1,0:T(8,128)S(1)}, u32[]{:S(2)}, u32[]{:S(2)}) collective-permute-start(f32[2,128,128]{2,1,0:T(8,128)S(1)} %get-tuple-element.211), channel_id=1, source_target_pairs={{12,4},{8,0},{13,5},{9,1},{14,6},{10,2},{15,7},{11,3}} | collective-permute-start | bytes 393224 | tf_op jit(solution)/shard_map/ppermute | solution.py:190
  64.9 1.3 %collective-permute-start.38 = (f32[2,128,128]{2,1,0:T(8,128)S(1)}, f32[2,128,128]{2,1,0:T(8,128)S(1)}, u32[]{:S(2)}, u32[]{:S(2)}) collective-permute-start(f32[2,128,128]{2,1,0:T(8,128)S(1)} %get-tuple-element.209), channel_id=1, source_target_pairs={{12,4},{8,0},{13,5},{9,1},{14,6},{10,2},{15,7},{11,3}} | collective-permute-start | bytes 393224 | tf_op jit(solution)/shard_map/ppermute | solution.py:190
  66.2 1.3 %collective-permute-start.37 = (f32[2,128,128]{2,1,0:T(8,128)S(1)}, f32[2,128,128]{2,1,0:T(8,128)S(1)}, u32[]{:S(2)}, u32[]{:S(2)}) collective-permute-start(f32[2,128,128]{2,1,0:T(8,128)S(1)} %get-tuple-element.207), channel_id=1, source_target_pairs={{12,4},{8,0},{13,5},{9,1},{14,6},{10,2},{15,7},{11,3}} | collective-permute-start | bytes 393224 | tf_op jit(solution)/shard_map/ppermute | solution.py:190
  67.5 8.5 %collective-permute-done.33 = f32[2,128,128]{2,1,0:T(8,128)S(1)} collective-permute-done((f32[2,128,128]{2,1,0:T(8,128)S(1)}, f32[2,128,128]{2,1,0:T(8,128)S(1)}, u32[]{:S(2)}, u32[]{:S(2)}) %collective-permute-start.33) | collective-permute-done | bytes 131104 | tf_op jit(solution)/shard_map/ppermute | solution.py:190
  76.0 1.2 %collective-permute-start.41 = (f32[2,128,128]{2,1,0:T(8,128)S(1)}, f32[2,128,128]{2,1,0:T(8,128)S(1)}, u32[]{:S(2)}, u32[]{:S(2)}) collective-permute-start(f32[2,128,128]{2,1,0:T(8,128)S(1)} %get-tuple-element.205), channel_id=1, source_target_pairs={{0,4},{4,0},{8,12},{12,8},{16,20},{20,16},{24,28},{28,24},{1,5},{5... | collective-permute-start | bytes 393224 | tf_op jit(solution)/shard_map/ppermute | solution.py:245
  77.3 1.5 %collective-permute-start.36 = (f32[2,128,128]{2,1,0:T(8,128)S(1)}, f32[2,128,128]{2,1,0:T(8,128)S(1)}, u32[]{:S(2)}, u32[]{:S(2)}) collective-permute-start(f32[2,128,128]{2,1,0:T(8,128)S(1)} %get-tuple-element.203), channel_id=1, source_target_pairs={{12,4},{8,0},{13,5},{9,1},{14,6},{10,2},{15,7},{11,3}} | collective-permute-start | bytes 393224 | tf_op jit(solution)/shard_map/ppermute | solution.py:190
  79.2 1.2 %collective-permute-start.42 = (f32[2,128,128]{2,1,0:T(8,128)S(1)}, f32[2,128,128]{2,1,0:T(8,128)S(1)}, u32[]{:S(2)}, u32[]{:S(2)}) collective-permute-start(f32[2,128,128]{2,1,0:T(8,128)S(1)} %get-tuple-element.201), channel_id=1, source_target_pairs={{0,4},{4,0},{8,12},{12,8},{16,20},{20,16},{24,28},{28,24},{1,5},{5... | collective-permute-start | bytes 393224 | tf_op jit(solution)/shard_map/ppermute | solution.py:245
  80.4 1.8 %shard_map.88 = (bf16[256,2048]{1,0:T(8,128)(2,1)}, bf16[256,2048]{1,0:T(8,128)(2,1)}) custom-call(s32[1]{0:T(128)} %bitcast.place, bf16[256,2048]{1,0:T(8,128)(2,1)S(1)} %copy-done, bf16[256,2048]{1,0:T(8,128)(2,1)S(1)} %copy-done.1, bf16[256,2048]{1,0:T(8,128)(2,1)S(1)} %copy-done.2, bf16[256,256]{1,0:T(8,128)(2,1)S(1)} %get-tuple-element.159.refs_0_, ...), custom_call_target="tpu_custom_call" | custom-call | flops 1024 | bytes 1024 | tf_op jit(solution)/shard_map/pallas_call | solution.py:43
  82.3 0.9 %collective-permute-start.40 = (f32[2,128,128]{2,1,0:T(8,128)S(1)}, f32[2,128,128]{2,1,0:T(8,128)S(1)}, u32[]{:S(2)}, u32[]{:S(2)}) collective-permute-start(f32[2,128,128]{2,1,0:T(8,128)S(1)} %get-tuple-element.199), channel_id=1, source_target_pairs={{0,4},{4,0},{8,12},{12,8},{16,20},{20,16},{24,28},{28,24},{1,5},{5... | collective-permute-start | bytes 393224 | tf_op jit(solution)/shard_map/ppermute | solution.py:245
  83.2 1.2 %shard_map.89 = (bf16[256,2048]{1,0:T(8,128)(2,1)}, bf16[256,2048]{1,0:T(8,128)(2,1)}) custom-call(s32[1]{0:T(128)} %bitcast.place, bf16[256,2048]{1,0:T(8,128)(2,1)S(1)} %copy-done, bf16[256,2048]{1,0:T(8,128)(2,1)S(1)} %copy-done.1, bf16[256,2048]{1,0:T(8,128)(2,1)S(1)} %copy-done.2, ...), custom_call_target="tpu_custom_call", output_to_operand_aliasing={{0}: (7, {}), {1}: (8, {})} | custom-call | flops 1024 | bytes 1024 | tf_op jit(solution)/shard_map/pallas_call | solution.py:43
  84.5 1.2 %collective-permute-start.39 = (f32[2,128,128]{2,1,0:T(8,128)S(1)}, f32[2,128,128]{2,1,0:T(8,128)S(1)}, u32[]{:S(2)}, u32[]{:S(2)}) collective-permute-start(f32[2,128,128]{2,1,0:T(8,128)S(1)} %get-tuple-element.197), channel_id=1, source_target_pairs={{0,4},{4,0},{8,12},{12,8},{16,20},{20,16},{24,28},{28,24},{1,5},{5... | collective-permute-start | bytes 393224 | tf_op jit(solution)/shard_map/ppermute | solution.py:245
  85.7 1.0 %copy.28 = bf16[256,2048]{1,0:T(8,128)(2,1)} copy(bf16[256,2048]{1,0:T(8,128)(2,1)S(1)} %shard_map.87) | data formatting | bytes 2097152
  86.7 1.2 %shard_map.90 = (bf16[256,2048]{1,0:T(8,128)(2,1)}, bf16[256,2048]{1,0:T(8,128)(2,1)}) custom-call(s32[1]{0:T(128)} %bitcast.place, bf16[256,2048]{1,0:T(8,128)(2,1)S(1)} %copy-done, bf16[256,2048]{1,0:T(8,128)(2,1)S(1)} %copy-done.1, bf16[256,2048]{1,0:T(8,128)(2,1)S(1)} %copy-done.2, ...), custom_call_target="tpu_custom_call", output_to_operand_aliasing={{0}: (7, {}), {1}: (8, {})} | custom-call | flops 1024 | bytes 1024 | tf_op jit(solution)/shard_map/pallas_call | solution.py:43
  87.9 1.9 %shard_map.91 = (bf16[256,2048]{1,0:T(8,128)(2,1)}, bf16[256,2048]{1,0:T(8,128)(2,1)}) custom-call(s32[1]{0:T(128)} %bitcast.place, bf16[256,2048]{1,0:T(8,128)(2,1)S(1)} %copy-done, bf16[256,2048]{1,0:T(8,128)(2,1)S(1)} %copy-done.1, bf16[256,2048]{1,0:T(8,128)(2,1)S(1)} %copy-done.2, ...), custom_call_target="tpu_custom_call", output_to_operand_aliasing={{0}: (8, {}), {1}: (9, {})} | custom-call | flops 1024 | bytes 1024 | tf_op jit(solution)/shard_map/pallas_call | solution.py:43
  89.8 1.2 %shard_map.92 = (bf16[256,2048]{1,0:T(8,128)(2,1)}, bf16[256,2048]{1,0:T(8,128)(2,1)}) custom-call(s32[1]{0:T(128)} %bitcast.place, bf16[256,2048]{1,0:T(8,128)(2,1)S(1)} %copy-done, bf16[256,2048]{1,0:T(8,128)(2,1)S(1)} %copy-done.1, bf16[256,2048]{1,0:T(8,128)(2,1)S(1)} %copy-done.2, ...), custom_call_target="tpu_custom_call", output_to_operand_aliasing={{0}: (6, {}), {1}: (7, {})} | custom-call | flops 1024 | bytes 1024 | tf_op jit(solution)/shard_map/pallas_call | solution.py:43
  91.0 1.2 %shard_map.93 = (bf16[256,2048]{1,0:T(8,128)(2,1)}, bf16[256,2048]{1,0:T(8,128)(2,1)}) custom-call(s32[1]{0:T(128)} %bitcast.place, bf16[256,2048]{1,0:T(8,128)(2,1)S(1)} %copy-done, bf16[256,2048]{1,0:T(8,128)(2,1)S(1)} %copy-done.1, bf16[256,2048]{1,0:T(8,128)(2,1)S(1)} %copy-done.2, ...), custom_call_target="tpu_custom_call", output_to_operand_aliasing={{0}: (6, {}), {1}: (7, {})} | custom-call | flops 1024 | bytes 1024 | tf_op jit(solution)/shard_map/pallas_call | solution.py:43
  (100 shorter events, 14.9 us)
Async XLA Ops:
  2.0 9.1 %collective-permute-start = (f32[2,128,128]{2,1,0:T(8,128)S(1)}, f32[2,128,128]{2,1,0:T(8,128)S(1)}, u32[]{:S(2)}, u32[]{:S(2)}) collective-permute-start(f32[2,128,128]{2,1,0:T(8,128)S(1)} %get-tuple-element.105), channel_id=1, source_target_pairs={{0,4},{4,0},{8,12},{12,8},{16,20},{20,16},{24,28},{28,24},{1,5},{5... | collective-permute-start | bytes 393224 | tf_op jit(solution)/shard_map/ppermute | solution.py:225
  5.0 9.6 %collective-permute-start.4 = (f32[2,128,128]{2,1,0:T(8,128)S(1)}, f32[2,128,128]{2,1,0:T(8,128)S(1)}, u32[]{:S(2)}, u32[]{:S(2)}) collective-permute-start(f32[2,128,128]{2,1,0:T(8,128)S(1)} %get-tuple-element.111), channel_id=1, source_target_pairs={{0,4},{4,0},{8,12},{12,8},{16,20},{20,16},{24,28},{28,24},{1,5},{5... | collective-permute-start | bytes 393224 | tf_op jit(solution)/shard_map/ppermute | solution.py:225
  6.4 9.8 %collective-permute-start.3 = (f32[2,128,128]{2,1,0:T(8,128)S(1)}, f32[2,128,128]{2,1,0:T(8,128)S(1)}, u32[]{:S(2)}, u32[]{:S(2)}) collective-permute-start(f32[2,128,128]{2,1,0:T(8,128)S(1)} %get-tuple-element.109), channel_id=1, source_target_pairs={{0,4},{4,0},{8,12},{12,8},{16,20},{20,16},{24,28},{28,24},{1,5},{5... | collective-permute-start | bytes 393224 | tf_op jit(solution)/shard_map/ppermute | solution.py:225
  11.1 8.3 %collective-permute-start.2 = (f32[2,128,128]{2,1,0:T(8,128)S(1)}, f32[2,128,128]{2,1,0:T(8,128)S(1)}, u32[]{:S(2)}, u32[]{:S(2)}) collective-permute-start(f32[2,128,128]{2,1,0:T(8,128)S(1)} %get-tuple-element.238), channel_id=1, source_target_pairs={{0,8},{4,12},{1,9},{5,13},{2,10},{6,14},{3,11},{7,15}} | collective-permute-start | bytes 393224 | tf_op jit(solution)/shard_map/ppermute | solution.py:190
  14.6 9.0 %collective-permute-start.8 = (f32[2,128,128]{2,1,0:T(8,128)S(1)}, f32[2,128,128]{2,1,0:T(8,128)S(1)}, u32[]{:S(2)}, u32[]{:S(2)}) collective-permute-start(f32[2,128,128]{2,1,0:T(8,128)S(1)} %get-tuple-element.240), channel_id=1, source_target_pairs={{0,8},{4,12},{1,9},{5,13},{2,10},{6,14},{3,11},{7,15}} | collective-permute-start | bytes 393224 | tf_op jit(solution)/shard_map/ppermute | solution.py:190
  16.2 5.0 %collective-permute-start.1 = (f32[2,128,128]{2,1,0:T(8,128)S(1)}, f32[2,128,128]{2,1,0:T(8,128)S(1)}, u32[]{:S(2)}, u32[]{:S(2)}) collective-permute-start(f32[2,128,128]{2,1,0:T(8,128)S(1)} %get-tuple-element.107), channel_id=1, source_target_pairs={{0,4},{4,0},{8,12},{12,8},{16,20},{20,16},{24,28},{28,24},{1,5},{5... | collective-permute-start | bytes 393224 | tf_op jit(solution)/shard_map/ppermute | solution.py:225
  17.8 6.5 %collective-permute-start.7 = (f32[2,128,128]{2,1,0:T(8,128)S(1)}, f32[2,128,128]{2,1,0:T(8,128)S(1)}, u32[]{:S(2)}, u32[]{:S(2)}) collective-permute-start(f32[2,128,128]{2,1,0:T(8,128)S(1)} %get-tuple-element.242), channel_id=1, source_target_pairs={{0,8},{4,12},{1,9},{5,13},{2,10},{6,14},{3,11},{7,15}} | collective-permute-start | bytes 393224 | tf_op jit(solution)/shard_map/ppermute | solution.py:190
  19.4 5.7 %collective-permute-start.6 = (f32[2,128,128]{2,1,0:T(8,128)S(1)}, f32[2,128,128]{2,1,0:T(8,128)S(1)}, u32[]{:S(2)}, u32[]{:S(2)}) collective-permute-start(f32[2,128,128]{2,1,0:T(8,128)S(1)} %add.152), channel_id=1, source_target_pairs={{8,16},{12,20},{9,17},{13,21},{10,18},{14,22},{11,19},{15,23}} | collective-permute-start | bytes 393224 | tf_op jit(solution)/shard_map/ppermute | solution.py:190
  21.2 4.9 %collective-permute-start.5 = (f32[2,128,128]{2,1,0:T(8,128)S(1)}, f32[2,128,128]{2,1,0:T(8,128)S(1)}, u32[]{:S(2)}, u32[]{:S(2)}) collective-permute-start(f32[2,128,128]{2,1,0:T(8,128)S(1)} %get-tuple-element.244), channel_id=1, source_target_pairs={{0,8},{4,12},{1,9},{5,13},{2,10},{6,14},{3,11},{7,15}} | collective-permute-start | bytes 393224 | tf_op jit(solution)/shard_map/ppermute | solution.py:190
  23.7 3.2 %collective-permute-start.12 = (f32[2,128,128]{2,1,0:T(8,128)S(1)}, f32[2,128,128]{2,1,0:T(8,128)S(1)}, u32[]{:S(2)}, u32[]{:S(2)}) collective-permute-start(f32[2,128,128]{2,1,0:T(8,128)S(1)} %add.154), channel_id=1, source_target_pairs={{8,16},{12,20},{9,17},{13,21},{10,18},{14,22},{11,19},{15,23}} | collective-permute-start | bytes 393224 | tf_op jit(solution)/shard_map/ppermute | solution.py:190
  24.4 3.2 %collective-permute-start.11 = (f32[2,128,128]{2,1,0:T(8,128)S(1)}, f32[2,128,128]{2,1,0:T(8,128)S(1)}, u32[]{:S(2)}, u32[]{:S(2)}) collective-permute-start(f32[2,128,128]{2,1,0:T(8,128)S(1)} %add.155), channel_id=1, source_target_pairs={{8,16},{12,20},{9,17},{13,21},{10,18},{14,22},{11,19},{15,23}} | collective-permute-start | bytes 393224 | tf_op jit(solution)/shard_map/ppermute | solution.py:190
  25.1 3.2 %collective-permute-start.10 = (f32[2,128,128]{2,1,0:T(8,128)S(1)}, f32[2,128,128]{2,1,0:T(8,128)S(1)}, u32[]{:S(2)}, u32[]{:S(2)}) collective-permute-start(f32[2,128,128]{2,1,0:T(8,128)S(1)} %get-tuple-element.227), channel_id=1, source_target_pairs={{16,24},{20,28},{17,25},{21,29},{18,26},{22,30},{19,27},{23,31}} | collective-permute-start | bytes 393224 | tf_op jit(solution)/shard_map/ppermute | solution.py:190
  26.1 2.9 %collective-permute-start.9 = (f32[2,128,128]{2,1,0:T(8,128)S(1)}, f32[2,128,128]{2,1,0:T(8,128)S(1)}, u32[]{:S(2)}, u32[]{:S(2)}) collective-permute-start(f32[2,128,128]{2,1,0:T(8,128)S(1)} %add.158), channel_id=1, source_target_pairs={{8,16},{12,20},{9,17},{13,21},{10,18},{14,22},{11,19},{15,23}} | collective-permute-start | bytes 393224 | tf_op jit(solution)/shard_map/ppermute | solution.py:190
  26.9 3.1 %collective-permute-start.15 = (f32[2,128,128]{2,1,0:T(8,128)S(1)}, f32[2,128,128]{2,1,0:T(8,128)S(1)}, u32[]{:S(2)}, u32[]{:S(2)}) collective-permute-start(f32[2,128,128]{2,1,0:T(8,128)S(1)} %get-tuple-element.225), channel_id=1, source_target_pairs={{16,24},{20,28},{17,25},{21,29},{18,26},{22,30},{19,27},{23,31}} | collective-permute-start | bytes 393224 | tf_op jit(solution)/shard_map/ppermute | solution.py:190
  27.6 3.8 %collective-permute-start.14 = (f32[2,128,128]{2,1,0:T(8,128)S(1)}, f32[2,128,128]{2,1,0:T(8,128)S(1)}, u32[]{:S(2)}, u32[]{:S(2)}) collective-permute-start(f32[2,128,128]{2,1,0:T(8,128)S(1)} %get-tuple-element.223), channel_id=1, source_target_pairs={{16,24},{20,28},{17,25},{21,29},{18,26},{22,30},{19,27},{23,31}} | collective-permute-start | bytes 393224 | tf_op jit(solution)/shard_map/ppermute | solution.py:190
  28.3 5.3 %copy-start.2 = (bf16[256,2048]{1,0:T(8,128)(2,1)S(1)}, bf16[256,2048]{1,0:T(8,128)(2,1)}, u32[]{:S(2)}) copy-start(bf16[256,2048]{1,0:T(8,128)(2,1)} %v.17) | copy-start | bytes 3145732
  28.3 6.5 %collective-permute-start.19 = (f32[2,128,128]{2,1,0:T(8,128)S(1)}, f32[2,128,128]{2,1,0:T(8,128)S(1)}, u32[]{:S(2)}, u32[]{:S(2)}) collective-permute-start(f32[2,128,128]{2,1,0:T(8,128)S(1)} %get-tuple-element.221), channel_id=1, source_target_pairs={{0,4},{4,0},{8,12},{12,8},{16,20},{20,16},{24,28},{28,24},{1,5},{5... | collective-permute-start | bytes 393224 | tf_op jit(solution)/shard_map/ppermute | solution.py:245
  29.1 4.5 %copy-start.1 = (bf16[256,2048]{1,0:T(8,128)(2,1)S(1)}, bf16[256,2048]{1,0:T(8,128)(2,1)}, u32[]{:S(2)}) copy-start(bf16[256,2048]{1,0:T(8,128)(2,1)} %k.17) | copy-start | bytes 3145732
  29.1 4.5 %copy-start = (bf16[256,2048]{1,0:T(8,128)(2,1)S(1)}, bf16[256,2048]{1,0:T(8,128)(2,1)}, u32[]{:S(2)}) copy-start(bf16[256,2048]{1,0:T(8,128)(2,1)} %q.15) | copy-start | bytes 3145732
  29.1 3.0 %collective-permute-start.13 = (f32[2,128,128]{2,1,0:T(8,128)S(1)}, f32[2,128,128]{2,1,0:T(8,128)S(1)}, u32[]{:S(2)}, u32[]{:S(2)}) collective-permute-start(f32[2,128,128]{2,1,0:T(8,128)S(1)} %get-tuple-element.219), channel_id=1, source_target_pairs={{16,24},{20,28},{17,25},{21,29},{18,26},{22,30},{19,27},{23,31}} | collective-permute-start | bytes 393224 | tf_op jit(solution)/shard_map/ppermute | solution.py:190
  30.0 7.2 %collective-permute-start.18 = (f32[2,128,128]{2,1,0:T(8,128)S(1)}, f32[2,128,128]{2,1,0:T(8,128)S(1)}, u32[]{:S(2)}, u32[]{:S(2)}) collective-permute-start(f32[2,128,128]{2,1,0:T(8,128)S(1)} %get-tuple-element.217), channel_id=1, source_target_pairs={{0,4},{4,0},{8,12},{12,8},{16,20},{20,16},{24,28},{28,24},{1,5},{5... | collective-permute-start | bytes 393224 | tf_op jit(solution)/shard_map/ppermute | solution.py:245
  31.4 7.2 %collective-permute-start.17 = (f32[2,128,128]{2,1,0:T(8,128)S(1)}, f32[2,128,128]{2,1,0:T(8,128)S(1)}, u32[]{:S(2)}, u32[]{:S(2)}) collective-permute-start(f32[2,128,128]{2,1,0:T(8,128)S(1)} %get-tuple-element.215), channel_id=1, source_target_pairs={{0,4},{4,0},{8,12},{12,8},{16,20},{20,16},{24,28},{28,24},{1,5},{5... | collective-permute-start | bytes 393224 | tf_op jit(solution)/shard_map/ppermute | solution.py:245
  32.2 1.4 %copy-start.4 = (bf16[2048]{0:T(1024)(128)(2,1)S(1)}, bf16[2048]{0:T(1024)(128)(2,1)}, u32[]{:S(2)}) copy-start(bf16[2048]{0:T(1024)(128)(2,1)} %param.9) | copy-start | bytes 12292
  32.2 7.8 %collective-permute-start.16 = (f32[2,128,128]{2,1,0:T(8,128)S(1)}, f32[2,128,128]{2,1,0:T(8,128)S(1)}, u32[]{:S(2)}, u32[]{:S(2)}) collective-permute-start(f32[2,128,128]{2,1,0:T(8,128)S(1)} %get-tuple-element.213), channel_id=1, source_target_pairs={{0,4},{4,0},{8,12},{12,8},{16,20},{20,16},{24,28},{28,24},{1,5},{5... | collective-permute-start | bytes 393224 | tf_op jit(solution)/shard_map/ppermute | solution.py:245
  33.6 1.2 %copy-start.3 = (bf16[256,2048]{1,0:T(8,128)(2,1)S(1)}, bf16[256,2048]{1,0:T(8,128)(2,1)}, u32[]{:S(2)}) copy-start(bf16[256,2048]{1,0:T(8,128)(2,1)} %refs_7_.3) | copy-start | bytes 3145732
  40.4 3.1 %collective-permute-start.22 = (f32[2,256]{1,0:T(2,128)S(1)}, f32[2,256]{1,0:T(2,128)S(1)}, u32[]{:S(2)}, u32[]{:S(2)}) collective-permute-start(f32[2,256]{1,0:T(2,128)S(1)} %get-tuple-element.134.refs_0_), channel_id=1, source_target_pairs={{0,3},{1,2},{2,1},{3,0},{4,7},{5,6},{6,5},{7,4},{8,11},{9,10},{10,... | collective-permute-start | bytes 6152 | tf_op jit(solution)/shard_map/ppermute | solution.py:333
  40.5 3.7 %collective-permute-start.21 = (f32[2,256]{1,0:T(2,128)S(1)}, f32[2,256]{1,0:T(2,128)S(1)}, u32[]{:S(2)}, u32[]{:S(2)}) collective-permute-start(f32[2,256]{1,0:T(2,128)S(1)} %get-tuple-element.134.refs_0_), channel_id=1, source_target_pairs={{0,2},{1,3},{2,0},{3,1},{4,6},{5,7},{6,4},{7,5},{8,10},{9,11},{10,... | collective-permute-start | bytes 6152 | tf_op jit(solution)/shard_map/ppermute | solution.py:333
  42.0 2.1 %collective-permute-start.20 = (f32[2,256]{1,0:T(2,128)S(1)}, f32[2,256]{1,0:T(2,128)S(1)}, u32[]{:S(2)}, u32[]{:S(2)}) collective-permute-start(f32[2,256]{1,0:T(2,128)S(1)} %get-tuple-element.134.refs_0_), channel_id=1, source_target_pairs={{0,1},{1,0},{2,3},{3,2},{4,5},{5,4},{6,7},{7,6},{8,9},{9,8},{10,11... | collective-permute-start | bytes 6152 | tf_op jit(solution)/shard_map/ppermute | solution.py:333
  44.5 6.4 %collective-permute-start.25 = (f32[2,128,128]{2,1,0:T(8,128)S(1)}, f32[2,128,128]{2,1,0:T(8,128)S(1)}, u32[]{:S(2)}, u32[]{:S(2)}) collective-permute-start(f32[2,128,128]{2,1,0:T(8,128)S(1)} %get-tuple-element.149), channel_id=1, source_target_pairs={{0,4},{4,0},{8,12},{12,8},{16,20},{20,16},{24,28},{28,24},{1,5},{5... | collective-permute-start | bytes 393224 | tf_op jit(solution)/shard_map/ppermute | solution.py:225
  46.4 7.4 %collective-permute-start.24 = (f32[2,128,128]{2,1,0:T(8,128)S(1)}, f32[2,128,128]{2,1,0:T(8,128)S(1)}, u32[]{:S(2)}, u32[]{:S(2)}) collective-permute-start(f32[2,128,128]{2,1,0:T(8,128)S(1)} %get-tuple-element.147), channel_id=1, source_target_pairs={{0,4},{4,0},{8,12},{12,8},{16,20},{20,16},{24,28},{28,24},{1,5},{5... | collective-permute-start | bytes 393224 | tf_op jit(solution)/shard_map/ppermute | solution.py:225
  47.1 9.4 %collective-permute-start.23 = (f32[2,128,128]{2,1,0:T(8,128)S(1)}, f32[2,128,128]{2,1,0:T(8,128)S(1)}, u32[]{:S(2)}, u32[]{:S(2)}) collective-permute-start(f32[2,128,128]{2,1,0:T(8,128)S(1)} %get-tuple-element.143), channel_id=1, source_target_pairs={{0,4},{4,0},{8,12},{12,8},{16,20},{20,16},{24,28},{28,24},{1,5},{5... | collective-permute-start | bytes 393224 | tf_op jit(solution)/shard_map/ppermute | solution.py:225
  51.0 6.3 %collective-permute-start.29 = (f32[2,128,128]{2,1,0:T(8,128)S(1)}, f32[2,128,128]{2,1,0:T(8,128)S(1)}, u32[]{:S(2)}, u32[]{:S(2)}) collective-permute-start(f32[2,128,128]{2,1,0:T(8,128)S(1)} %get-tuple-element.236), channel_id=1, source_target_pairs={{28,20},{24,16},{29,21},{25,17},{30,22},{26,18},{31,23},{27,19}} | collective-permute-start | bytes 393224 | tf_op jit(solution)/shard_map/ppermute | solution.py:190
  51.6 7.2 %collective-permute-start.28 = (f32[2,128,128]{2,1,0:T(8,128)S(1)}, f32[2,128,128]{2,1,0:T(8,128)S(1)}, u32[]{:S(2)}, u32[]{:S(2)}) collective-permute-start(f32[2,128,128]{2,1,0:T(8,128)S(1)} %get-tuple-element.154), channel_id=1, source_target_pairs={{0,4},{4,0},{8,12},{12,8},{16,20},{20,16},{24,28},{28,24},{1,5},{5... | collective-permute-start | bytes 393224 | tf_op jit(solution)/shard_map/ppermute | solution.py:225
  53.8 5.7 %collective-permute-start.27 = (f32[2,128,128]{2,1,0:T(8,128)S(1)}, f32[2,128,128]{2,1,0:T(8,128)S(1)}, u32[]{:S(2)}, u32[]{:S(2)}) collective-permute-start(f32[2,128,128]{2,1,0:T(8,128)S(1)} %get-tuple-element.234), channel_id=1, source_target_pairs={{28,20},{24,16},{29,21},{25,17},{30,22},{26,18},{31,23},{27,19}} | collective-permute-start | bytes 393224 | tf_op jit(solution)/shard_map/ppermute | solution.py:190
  56.6 3.7 %collective-permute-start.26 = (f32[2,128,128]{2,1,0:T(8,128)S(1)}, f32[2,128,128]{2,1,0:T(8,128)S(1)}, u32[]{:S(2)}, u32[]{:S(2)}) collective-permute-start(f32[2,128,128]{2,1,0:T(8,128)S(1)} %get-tuple-element.232), channel_id=1, source_target_pairs={{28,20},{24,16},{29,21},{25,17},{30,22},{26,18},{31,23},{27,19}} | collective-permute-start | bytes 393224 | tf_op jit(solution)/shard_map/ppermute | solution.py:190
  57.3 5.5 %collective-permute-start.31 = (f32[2,128,128]{2,1,0:T(8,128)S(1)}, f32[2,128,128]{2,1,0:T(8,128)S(1)}, u32[]{:S(2)}, u32[]{:S(2)}) collective-permute-start(f32[2,128,128]{2,1,0:T(8,128)S(1)} %add.176), channel_id=1, source_target_pairs={{20,12},{16,8},{21,13},{17,9},{22,14},{18,10},{23,15},{19,11}} | collective-permute-start | bytes 393224 | tf_op jit(solution)/shard_map/ppermute | solution.py:190
  58.8 5.3 %collective-permute-start.30 = (f32[2,128,128]{2,1,0:T(8,128)S(1)}, f32[2,128,128]{2,1,0:T(8,128)S(1)}, u32[]{:S(2)}, u32[]{:S(2)}) collective-permute-start(f32[2,128,128]{2,1,0:T(8,128)S(1)} %get-tuple-element.230), channel_id=1, source_target_pairs={{28,20},{24,16},{29,21},{25,17},{30,22},{26,18},{31,23},{27,19}} | collective-permute-start | bytes 393224 | tf_op jit(solution)/shard_map/ppermute | solution.py:190
  59.6 5.3 %collective-permute-start.35 = (f32[2,128,128]{2,1,0:T(8,128)S(1)}, f32[2,128,128]{2,1,0:T(8,128)S(1)}, u32[]{:S(2)}, u32[]{:S(2)}) collective-permute-start(f32[2,128,128]{2,1,0:T(8,128)S(1)} %add.178), channel_id=1, source_target_pairs={{20,12},{16,8},{21,13},{17,9},{22,14},{18,10},{23,15},{19,11}} | collective-permute-start | bytes 393224 | tf_op jit(solution)/shard_map/ppermute | solution.py:190
  60.3 5.9 %collective-permute-start.34 = (f32[2,128,128]{2,1,0:T(8,128)S(1)}, f32[2,128,128]{2,1,0:T(8,128)S(1)}, u32[]{:S(2)}, u32[]{:S(2)}) collective-permute-start(f32[2,128,128]{2,1,0:T(8,128)S(1)} %add.179), channel_id=1, source_target_pairs={{20,12},{16,8},{21,13},{17,9},{22,14},{18,10},{23,15},{19,11}} | collective-permute-start | bytes 393224 | tf_op jit(solution)/shard_map/ppermute | solution.py:190
  62.8 13.2 %collective-permute-start.33 = (f32[2,128,128]{2,1,0:T(8,128)S(1)}, f32[2,128,128]{2,1,0:T(8,128)S(1)}, u32[]{:S(2)}, u32[]{:S(2)}) collective-permute-start(f32[2,128,128]{2,1,0:T(8,128)S(1)} %get-tuple-element.211), channel_id=1, source_target_pairs={{12,4},{8,0},{13,5},{9,1},{14,6},{10,2},{15,7},{11,3}} | collective-permute-start | bytes 393224 | tf_op jit(solution)/shard_map/ppermute | solution.py:190
  64.2 13.1 %collective-permute-start.32 = (f32[2,128,128]{2,1,0:T(8,128)S(1)}, f32[2,128,128]{2,1,0:T(8,128)S(1)}, u32[]{:S(2)}, u32[]{:S(2)}) collective-permute-start(f32[2,128,128]{2,1,0:T(8,128)S(1)} %add.182), channel_id=1, source_target_pairs={{20,12},{16,8},{21,13},{17,9},{22,14},{18,10},{23,15},{19,11}} | collective-permute-start | bytes 393224 | tf_op jit(solution)/shard_map/ppermute | solution.py:190
  64.9 14.3 %collective-permute-start.38 = (f32[2,128,128]{2,1,0:T(8,128)S(1)}, f32[2,128,128]{2,1,0:T(8,128)S(1)}, u32[]{:S(2)}, u32[]{:S(2)}) collective-permute-start(f32[2,128,128]{2,1,0:T(8,128)S(1)} %get-tuple-element.209), channel_id=1, source_target_pairs={{12,4},{8,0},{13,5},{9,1},{14,6},{10,2},{15,7},{11,3}} | collective-permute-start | bytes 393224 | tf_op jit(solution)/shard_map/ppermute | solution.py:190
  66.2 16.0 %collective-permute-start.37 = (f32[2,128,128]{2,1,0:T(8,128)S(1)}, f32[2,128,128]{2,1,0:T(8,128)S(1)}, u32[]{:S(2)}, u32[]{:S(2)}) collective-permute-start(f32[2,128,128]{2,1,0:T(8,128)S(1)} %get-tuple-element.207), channel_id=1, source_target_pairs={{12,4},{8,0},{13,5},{9,1},{14,6},{10,2},{15,7},{11,3}} | collective-permute-start | bytes 393224 | tf_op jit(solution)/shard_map/ppermute | solution.py:190
  76.0 11.9 %collective-permute-start.41 = (f32[2,128,128]{2,1,0:T(8,128)S(1)}, f32[2,128,128]{2,1,0:T(8,128)S(1)}, u32[]{:S(2)}, u32[]{:S(2)}) collective-permute-start(f32[2,128,128]{2,1,0:T(8,128)S(1)} %get-tuple-element.205), channel_id=1, source_target_pairs={{0,4},{4,0},{8,12},{12,8},{16,20},{20,16},{24,28},{28,24},{1,5},{5... | collective-permute-start | bytes 393224 | tf_op jit(solution)/shard_map/ppermute | solution.py:245
  77.3 7.2 %collective-permute-start.36 = (f32[2,128,128]{2,1,0:T(8,128)S(1)}, f32[2,128,128]{2,1,0:T(8,128)S(1)}, u32[]{:S(2)}, u32[]{:S(2)}) collective-permute-start(f32[2,128,128]{2,1,0:T(8,128)S(1)} %get-tuple-element.203), channel_id=1, source_target_pairs={{12,4},{8,0},{13,5},{9,1},{14,6},{10,2},{15,7},{11,3}} | collective-permute-start | bytes 393224 | tf_op jit(solution)/shard_map/ppermute | solution.py:190
  79.2 8.7 %collective-permute-start.42 = (f32[2,128,128]{2,1,0:T(8,128)S(1)}, f32[2,128,128]{2,1,0:T(8,128)S(1)}, u32[]{:S(2)}, u32[]{:S(2)}) collective-permute-start(f32[2,128,128]{2,1,0:T(8,128)S(1)} %get-tuple-element.201), channel_id=1, source_target_pairs={{0,4},{4,0},{8,12},{12,8},{16,20},{20,16},{24,28},{28,24},{1,5},{5... | collective-permute-start | bytes 393224 | tf_op jit(solution)/shard_map/ppermute | solution.py:245
  82.3 7.5 %collective-permute-start.40 = (f32[2,128,128]{2,1,0:T(8,128)S(1)}, f32[2,128,128]{2,1,0:T(8,128)S(1)}, u32[]{:S(2)}, u32[]{:S(2)}) collective-permute-start(f32[2,128,128]{2,1,0:T(8,128)S(1)} %get-tuple-element.199), channel_id=1, source_target_pairs={{0,4},{4,0},{8,12},{12,8},{16,20},{20,16},{24,28},{28,24},{1,5},{5... | collective-permute-start | bytes 393224 | tf_op jit(solution)/shard_map/ppermute | solution.py:245
  84.5 6.5 %collective-permute-start.39 = (f32[2,128,128]{2,1,0:T(8,128)S(1)}, f32[2,128,128]{2,1,0:T(8,128)S(1)}, u32[]{:S(2)}, u32[]{:S(2)}) collective-permute-start(f32[2,128,128]{2,1,0:T(8,128)S(1)} %get-tuple-element.197), channel_id=1, source_target_pairs={{0,4},{4,0},{8,12},{12,8},{16,20},{20,16},{24,28},{28,24},{1,5},{5... | collective-permute-start | bytes 393224 | tf_op jit(solution)/shard_map/ppermute | solution.py:245

commit v16 on v15

--- a/solution.py
+++ b/solution.py
@@ -397,15 +397,15 @@
 
         beside = {
             (2, 0): lambda out, sends: query(sends[1, 2]),
-            (long - 1, 2): kept_units(0, 2),
-            (long - 1, 3): kept_units(2, 1),
+            (long - 1, 1): kept_units(0, 1),
+            (long - 1, 2): kept_units(1, 1),
         } if spread else {}
         after = scan(kept, sent, ends, True, [], beside)
         if not spread:
             query()
         if not spread:
-            kept_units(0, 3)(after, None)
-        kept_units(3, 1)(after, None)
+            kept_units(0, CHUNKS - 2)(after, None)
+        kept_units(2, 2)(after, None)
         made = rest([(0, 1), (1, 1)], after, made)
         for c in range(2, CHUNKS):
             made = rest([(c, 1)], after, made)

time: 92.8 us -> 92.8 us (level)
  no operation moved by 1% of the time
where the time goes in v16:
time: 92.8 us; the launch traced here: 92.2 us
  starting transfers between devices  47.3 us (51%)
  waiting for transfers between devices  22.3 us (24%)
  Pallas kernels  19.6 us (21%)
  between operations  1.31 us (1%)
  local copies, waits for them, and re-layouts  1.05 us (1%)
    ppermute x24, starting transfers between devices, hop(): return lax.ppermute(array, 'seq', pairs)  25.2 us
    pallas_call x18, Pallas kernels, call(): pl.pallas_call(body, grid_spec=pltpu.PrefetchScalarGridSpec(num_scalar_pr...  19.6 us
    ppermute x8, starting transfers between devices, swap_after(): flight[c] = lax.ppermute(part_sent, 'seq', swap)  11.6 us
    ppermute x24, waiting for transfers between devices, hop(): return lax.ppermute(array, 'seq', pairs)  9.58 us
    ppermute x8, starting transfers between devices, scan(): out[c] = (carry[c], own[c], lax.ppermute(send, 'seq', swap))  8.63 us
    ppermute x8, waiting for transfers between devices, swap_after(): flight[c] = lax.ppermute(part_sent, 'seq', swap)  6.7 us
    ppermute x8, waiting for transfers between devices, scan(): out[c] = (carry[c], own[c], lax.ppermute(send, 'seq', swap))  4.22 us
    ppermute x3, starting transfers between devices, shards(): lax.ppermute(mine, 'head', [(i, i ^ step if paired else (i + step) % part...  1.92 us
  transfers between devices with their start and end apart: 43, of which 13 were waited for; matrix products, arithmetic and copies ran while one was open for 2% of the time, Pallas kernels for 18%

profile of v16, /device:TPU:0, one launch (start us, length us, event | category | flops | bytes accessed | tf_op | source)
XLA Modules:
  0.0 92.2 jit_solution(9324369757412194512)
XLA Ops:
  0.6 1.3 %shard_map.78 = (f32[2,128,128]{2,1,0:T(8,128)S(1)}, f32[2,128,128]{2,1,0:T(8,128)S(1)}) custom-call(s32[1]{0:T(128)} %bitcast.place, bf16[256,2048]{1,0:T(8,128)(2,1)} %k.17, bf16[256,2048]{1,0:T(8,128)(2,1)} %v.17), custom_call_target="tpu_custom_call" | custom-call | flops 1024 | bytes 1024 | tf_op jit(solution)/shard_map/pallas_call | solution.py:43
  2.0 3.0 %collective-permute-start = (f32[2,128,128]{2,1,0:T(8,128)S(1)}, f32[2,128,128]{2,1,0:T(8,128)S(1)}, u32[]{:S(2)}, u32[]{:S(2)}) collective-permute-start(f32[2,128,128]{2,1,0:T(8,128)S(1)} %get-tuple-element.105), channel_id=1, source_target_pairs={{0,4},{4,0},{8,12},{12,8},{16,20},{20,16},{24,28},{28,24},{1,5},{5... | collective-permute-start | bytes 393224 | tf_op jit(solution)/shard_map/ppermute | solution.py:225
  5.1 1.3 %shard_map.77 = (f32[2,128,128]{2,1,0:T(8,128)S(1)}, f32[2,128,128]{2,1,0:T(8,128)S(1)}) custom-call(s32[1]{0:T(128)} %bitcast.place, bf16[256,2048]{1,0:T(8,128)(2,1)} %k.17, bf16[256,2048]{1,0:T(8,128)(2,1)} %v.17), custom_call_target="tpu_custom_call" | custom-call | flops 1024 | bytes 1024 | tf_op jit(solution)/shard_map/pallas_call | solution.py:43
  6.4 2.0 %collective-permute-start.3 = (f32[2,128,128]{2,1,0:T(8,128)S(1)}, f32[2,128,128]{2,1,0:T(8,128)S(1)}, u32[]{:S(2)}, u32[]{:S(2)}) collective-permute-start(f32[2,128,128]{2,1,0:T(8,128)S(1)} %get-tuple-element.109), channel_id=1, source_target_pairs={{0,4},{4,0},{8,12},{12,8},{16,20},{20,16},{24,28},{28,24},{1,5},{5... | collective-permute-start | bytes 393224 | tf_op jit(solution)/shard_map/ppermute | solution.py:225
  8.4 2.6 %shard_map.76 = (f32[2,128,128]{2,1,0:T(8,128)S(1)}, f32[2,128,128]{2,1,0:T(8,128)S(1)}, f32[2,128,128]{2,1,0:T(8,128)S(1)}, f32[2,128,128]{2,1,0:T(8,128)S(1)}, f32[256,1024]{1,0:T(8,128)S(1)}) custom-call(s32[1]{0:T(128)} %bitcast.place, bf16[256,2048]{1,0:T(8,128)(2,1)} %q.15, bf16[256,2048]{1,0:T(8,128)(2,1)} %k.17, bf16[256,2048]{1,0:T(8,128)(2,1)} %v.17), custom_call_target="tpu_custom_call" | custom-call | flops 1024 | bytes 1024 | tf_op jit(solution)/shard_map/pallas_call | solution.py:43
  11.1 3.5 %collective-permute-start.2 = (f32[2,128,128]{2,1,0:T(8,128)S(1)}, f32[2,128,128]{2,1,0:T(8,128)S(1)}, u32[]{:S(2)}, u32[]{:S(2)}) collective-permute-start(f32[2,128,128]{2,1,0:T(8,128)S(1)} %get-tuple-element.238), channel_id=1, source_target_pairs={{0,8},{4,12},{1,9},{5,13},{2,10},{6,14},{3,11},{7,15}} | collective-permute-start | bytes 393224 | tf_op jit(solution)/shard_map/ppermute | solution.py:190
  14.6 1.6 %collective-permute-start.8 = (f32[2,128,128]{2,1,0:T(8,128)S(1)}, f32[2,128,128]{2,1,0:T(8,128)S(1)}, u32[]{:S(2)}, u32[]{:S(2)}) collective-permute-start(f32[2,128,128]{2,1,0:T(8,128)S(1)} %get-tuple-element.240), channel_id=1, source_target_pairs={{0,8},{4,12},{1,9},{5,13},{2,10},{6,14},{3,11},{7,15}} | collective-permute-start | bytes 393224 | tf_op jit(solution)/shard_map/ppermute | solution.py:190
  16.2 1.6 %collective-permute-start.1 = (f32[2,128,128]{2,1,0:T(8,128)S(1)}, f32[2,128,128]{2,1,0:T(8,128)S(1)}, u32[]{:S(2)}, u32[]{:S(2)}) collective-permute-start(f32[2,128,128]{2,1,0:T(8,128)S(1)} %get-tuple-element.107), channel_id=1, source_target_pairs={{0,4},{4,0},{8,12},{12,8},{16,20},{20,16},{24,28},{28,24},{1,5},{5... | collective-permute-start | bytes 393224 | tf_op jit(solution)/shard_map/ppermute | solution.py:225
  17.8 1.6 %collective-permute-start.7 = (f32[2,128,128]{2,1,0:T(8,128)S(1)}, f32[2,128,128]{2,1,0:T(8,128)S(1)}, u32[]{:S(2)}, u32[]{:S(2)}) collective-permute-start(f32[2,128,128]{2,1,0:T(8,128)S(1)} %get-tuple-element.242), channel_id=1, source_target_pairs={{0,8},{4,12},{1,9},{5,13},{2,10},{6,14},{3,11},{7,15}} | collective-permute-start | bytes 393224 | tf_op jit(solution)/shard_map/ppermute | solution.py:190
  20.1 1.2 %collective-permute-done.1 = f32[2,128,128]{2,1,0:T(8,128)S(1)} collective-permute-done((f32[2,128,128]{2,1,0:T(8,128)S(1)}, f32[2,128,128]{2,1,0:T(8,128)S(1)}, u32[]{:S(2)}, u32[]{:S(2)}) %collective-permute-start.1) | collective-permute-done | bytes 131104 | tf_op jit(solution)/shard_map/ppermute | solution.py:225
  21.2 2.4 %collective-permute-start.5 = (f32[2,128,128]{2,1,0:T(8,128)S(1)}, f32[2,128,128]{2,1,0:T(8,128)S(1)}, u32[]{:S(2)}, u32[]{:S(2)}) collective-permute-start(f32[2,128,128]{2,1,0:T(8,128)S(1)} %get-tuple-element.244), channel_id=1, source_target_pairs={{0,8},{4,12},{1,9},{5,13},{2,10},{6,14},{3,11},{7,15}} | collective-permute-start | bytes 393224 | tf_op jit(solution)/shard_map/ppermute | solution.py:190
  28.3 0.8 collective-permute-start.19
  29.1 0.8 collective-permute-start.13
  30.0 1.4 %collective-permute-start.18 = (f32[2,128,128]{2,1,0:T(8,128)S(1)}, f32[2,128,128]{2,1,0:T(8,128)S(1)}, u32[]{:S(2)}, u32[]{:S(2)}) collective-permute-start(f32[2,128,128]{2,1,0:T(8,128)S(1)} %get-tuple-element.217), channel_id=1, source_target_pairs={{0,4},{4,0},{8,12},{12,8},{16,20},{20,16},{24,28},{28,24},{1,5},{5... | collective-permute-start | bytes 393224 | tf_op jit(solution)/shard_map/ppermute | solution.py:245
  31.4 0.8 collective-permute-start.17
  32.2 1.4 %collective-permute-start.16 = (f32[2,128,128]{2,1,0:T(8,128)S(1)}, f32[2,128,128]{2,1,0:T(8,128)S(1)}, u32[]{:S(2)}, u32[]{:S(2)}) collective-permute-start(f32[2,128,128]{2,1,0:T(8,128)S(1)} %get-tuple-element.213), channel_id=1, source_target_pairs={{0,4},{4,0},{8,12},{12,8},{16,20},{20,16},{24,28},{28,24},{1,5},{5... | collective-permute-start | bytes 393224 | tf_op jit(solution)/shard_map/ppermute | solution.py:245
  33.7 1.1 %shard_map.79.al_o = f32[256,1024]{1,0:T(8,128)S(1)} custom-call(s32[1]{0:T(128)} %bitcast.place, bf16[256,2048]{1,0:T(8,128)(2,1)S(1)} %copy-done, bf16[256,2048]{1,0:T(8,128)(2,1)S(1)} %copy-done.1, bf16[256,2048]{1,0:T(8,128)(2,1)S(1)} %copy-done.2, f32[2,128,128]{2,1,0:T(8,128)S(1)} %get-tuple-element.214.refs_0_.e), custom_call_target="tpu_custom_call" | custom-call | flops 1024 | bytes 1024 | tf_op jit(solution)/shard_map/pallas_call | solution.py:43
  35.2 2.0 %collective-permute-done.18.other = f32[2,128,128]{2,1,0:T(8,128)S(1)} collective-permute-done((f32[2,128,128]{2,1,0:T(8,128)S(1)}, f32[2,128,128]{2,1,0:T(8,128)S(1)}, u32[]{:S(2)}, u32[]{:S(2)}) %collective-permute-start.18) | collective-permute-done | bytes 131104 | tf_op jit(solution)/shard_map/ppermute | solution.py:245
  37.5 1.1 %collective-permute-done.17.other = f32[2,128,128]{2,1,0:T(8,128)S(1)} collective-permute-done((f32[2,128,128]{2,1,0:T(8,128)S(1)}, f32[2,128,128]{2,1,0:T(8,128)S(1)}, u32[]{:S(2)}, u32[]{:S(2)}) %collective-permute-start.17) | collective-permute-done | bytes 131104 | tf_op jit(solution)/shard_map/ppermute | solution.py:245
  38.9 1.1 %collective-permute-done.16.other = f32[2,128,128]{2,1,0:T(8,128)S(1)} collective-permute-done((f32[2,128,128]{2,1,0:T(8,128)S(1)}, f32[2,128,128]{2,1,0:T(8,128)S(1)}, u32[]{:S(2)}, u32[]{:S(2)}) %collective-permute-start.16) | collective-permute-done | bytes 131104 | tf_op jit(solution)/shard_map/ppermute | solution.py:245
  40.5 1.6 %collective-permute-start.21 = (f32[2,256]{1,0:T(2,128)S(1)}, f32[2,256]{1,0:T(2,128)S(1)}, u32[]{:S(2)}, u32[]{:S(2)}) collective-permute-start(f32[2,256]{1,0:T(2,128)S(1)} %get-tuple-element.134.refs_0_), channel_id=1, source_target_pairs={{0,2},{1,3},{2,0},{3,1},{4,6},{5,7},{6,4},{7,5},{8,10},{9,11},{10,... | collective-permute-start | bytes 6152 | tf_op jit(solution)/shard_map/ppermute | solution.py:333
  42.3 1.1 %collective-permute-done.22.refs_3_ = f32[2,256]{1,0:T(2,128)S(1)} collective-permute-done((f32[2,256]{1,0:T(2,128)S(1)}, f32[2,256]{1,0:T(2,128)S(1)}, u32[]{:S(2)}, u32[]{:S(2)}) %collective-permute-start.22) | collective-permute-done | bytes 2080 | tf_op jit(solution)/shard_map/ppermute | solution.py:333
  44.5 1.4 %collective-permute-start.25 = (f32[2,128,128]{2,1,0:T(8,128)S(1)}, f32[2,128,128]{2,1,0:T(8,128)S(1)}, u32[]{:S(2)}, u32[]{:S(2)}) collective-permute-start(f32[2,128,128]{2,1,0:T(8,128)S(1)} %get-tuple-element.149), channel_id=1, source_target_pairs={{0,4},{4,0},{8,12},{12,8},{16,20},{20,16},{24,28},{28,24},{1,5},{5... | collective-permute-start | bytes 393224 | tf_op jit(solution)/shard_map/ppermute | solution.py:225
  46.4 0.8 collective-permute-start.24
  47.1 1.3 %collective-permute-start.23 = (f32[2,128,128]{2,1,0:T(8,128)S(1)}, f32[2,128,128]{2,1,0:T(8,128)S(1)}, u32[]{:S(2)}, u32[]{:S(2)}) collective-permute-start(f32[2,128,128]{2,1,0:T(8,128)S(1)} %get-tuple-element.143), channel_id=1, source_target_pairs={{0,4},{4,0},{8,12},{12,8},{16,20},{20,16},{24,28},{28,24},{1,5},{5... | collective-permute-start | bytes 393224 | tf_op jit(solution)/shard_map/ppermute | solution.py:225
  49.1 1.8 %collective-permute-done.25 = f32[2,128,128]{2,1,0:T(8,128)S(1)} collective-permute-done((f32[2,128,128]{2,1,0:T(8,128)S(1)}, f32[2,128,128]{2,1,0:T(8,128)S(1)}, u32[]{:S(2)}, u32[]{:S(2)}) %collective-permute-start.25) | collective-permute-done | bytes 131104 | tf_op jit(solution)/shard_map/ppermute | solution.py:225
  51.6 1.4 %collective-permute-start.28 = (f32[2,128,128]{2,1,0:T(8,128)S(1)}, f32[2,128,128]{2,1,0:T(8,128)S(1)}, u32[]{:S(2)}, u32[]{:S(2)}) collective-permute-start(f32[2,128,128]{2,1,0:T(8,128)S(1)} %get-tuple-element.154), channel_id=1, source_target_pairs={{0,4},{4,0},{8,12},{12,8},{16,20},{20,16},{24,28},{28,24},{1,5},{5... | collective-permute-start | bytes 393224 | tf_op jit(solution)/shard_map/ppermute | solution.py:225
  53.0 0.7 collective-permute-done.24
  54.4 2.1 %collective-permute-done.23 = f32[2,128,128]{2,1,0:T(8,128)S(1)} collective-permute-done((f32[2,128,128]{2,1,0:T(8,128)S(1)}, f32[2,128,128]{2,1,0:T(8,128)S(1)}, u32[]{:S(2)}, u32[]{:S(2)}) %collective-permute-start.23) | collective-permute-done | bytes 131104 | tf_op jit(solution)/shard_map/ppermute | solution.py:225
  58.0 0.8 collective-permute-done.28
  60.9 1.8 %shard_map.87 = bf16[256,2048]{1,0:T(8,128)(2,1)S(1)} custom-call(s32[1]{0:T(128)} %bitcast.place, bf16[256,2048]{1,0:T(8,128)(2,1)S(1)} %copy-done.1, bf16[256,2048]{1,0:T(8,128)(2,1)S(1)} %copy-done.2, bf16[256,256]{1,0:T(8,128)(2,1)S(1)} %get-tuple-element.159.refs_0_, bf16[256,256]{1,0:T(8,128)(2,1)S(1)} %get-tuple-element.160.refs_1_.refs_0_, ...), custom_call_target="tpu_custom_call" | custom-call | flops 1024 | bytes 1024 | tf_op jit(solution)/shard_map/pallas_call | solution.py:43
  62.8 1.3 %collective-permute-start.33 = (f32[2,128,128]{2,1,0:T(8,128)S(1)}, f32[2,128,128]{2,1,0:T(8,128)S(1)}, u32[]{:S(2)}, u32[]{:S(2)}) collective-permute-start(f32[2,128,128]{2,1,0:T(8,128)S(1)} %get-tuple-element.211), channel_id=1, source_target_pairs={{12,4},{8,0},{13,5},{9,1},{14,6},{10,2},{15,7},{11,3}} | collective-permute-start | bytes 393224 | tf_op jit(solution)/shard_map/ppermute | solution.py:190
  64.9 1.3 %collective-permute-start.38 = (f32[2,128,128]{2,1,0:T(8,128)S(1)}, f32[2,128,128]{2,1,0:T(8,128)S(1)}, u32[]{:S(2)}, u32[]{:S(2)}) collective-permute-start(f32[2,128,128]{2,1,0:T(8,128)S(1)} %get-tuple-element.209), channel_id=1, source_target_pairs={{12,4},{8,0},{13,5},{9,1},{14,6},{10,2},{15,7},{11,3}} | collective-permute-start | bytes 393224 | tf_op jit(solution)/shard_map/ppermute | solution.py:190
  66.2 1.3 %collective-permute-start.37 = (f32[2,128,128]{2,1,0:T(8,128)S(1)}, f32[2,128,128]{2,1,0:T(8,128)S(1)}, u32[]{:S(2)}, u32[]{:S(2)}) collective-permute-start(f32[2,128,128]{2,1,0:T(8,128)S(1)} %get-tuple-element.207), channel_id=1, source_target_pairs={{12,4},{8,0},{13,5},{9,1},{14,6},{10,2},{15,7},{11,3}} | collective-permute-start | bytes 393224 | tf_op jit(solution)/shard_map/ppermute | solution.py:190
  67.5 8.5 %collective-permute-done.33 = f32[2,128,128]{2,1,0:T(8,128)S(1)} collective-permute-done((f32[2,128,128]{2,1,0:T(8,128)S(1)}, f32[2,128,128]{2,1,0:T(8,128)S(1)}, u32[]{:S(2)}, u32[]{:S(2)}) %collective-permute-start.33) | collective-permute-done | bytes 131104 | tf_op jit(solution)/shard_map/ppermute | solution.py:190
  76.0 1.2 %collective-permute-start.41 = (f32[2,128,128]{2,1,0:T(8,128)S(1)}, f32[2,128,128]{2,1,0:T(8,128)S(1)}, u32[]{:S(2)}, u32[]{:S(2)}) collective-permute-start(f32[2,128,128]{2,1,0:T(8,128)S(1)} %get-tuple-element.205), channel_id=1, source_target_pairs={{0,4},{4,0},{8,12},{12,8},{16,20},{20,16},{24,28},{28,24},{1,5},{5... | collective-permute-start | bytes 393224 | tf_op jit(solution)/shard_map/ppermute | solution.py:245
  77.3 1.5 %collective-permute-start.36 = (f32[2,128,128]{2,1,0:T(8,128)S(1)}, f32[2,128,128]{2,1,0:T(8,128)S(1)}, u32[]{:S(2)}, u32[]{:S(2)}) collective-permute-start(f32[2,128,128]{2,1,0:T(8,128)S(1)} %get-tuple-element.203), channel_id=1, source_target_pairs={{12,4},{8,0},{13,5},{9,1},{14,6},{10,2},{15,7},{11,3}} | collective-permute-start | bytes 393224 | tf_op jit(solution)/shard_map/ppermute | solution.py:190
  78.8 1.2 %shard_map.88 = (bf16[256,2048]{1,0:T(8,128)(2,1)}, bf16[256,2048]{1,0:T(8,128)(2,1)}) custom-call(s32[1]{0:T(128)} %bitcast.place, bf16[256,2048]{1,0:T(8,128)(2,1)S(1)} %copy-done, bf16[256,2048]{1,0:T(8,128)(2,1)S(1)} %copy-done.1, bf16[256,2048]{1,0:T(8,128)(2,1)S(1)} %copy-done.2, bf16[256,256]{1,0:T(8,128)(2,1)S(1)} %get-tuple-element.159.refs_0_, ...), custom_call_target="tpu_custom_call" | custom-call | flops 1024 | bytes 1024 | tf_op jit(solution)/shard_map/pallas_call | solution.py:43
  80.0 0.9 %collective-permute-start.42 = (f32[2,128,128]{2,1,0:T(8,128)S(1)}, f32[2,128,128]{2,1,0:T(8,128)S(1)}, u32[]{:S(2)}, u32[]{:S(2)}) collective-permute-start(f32[2,128,128]{2,1,0:T(8,128)S(1)} %get-tuple-element.201), channel_id=1, source_target_pairs={{0,4},{4,0},{8,12},{12,8},{16,20},{20,16},{24,28},{28,24},{1,5},{5... | collective-permute-start | bytes 393224 | tf_op jit(solution)/shard_map/ppermute | solution.py:245
  81.0 1.2 %shard_map.89 = (bf16[256,2048]{1,0:T(8,128)(2,1)}, bf16[256,2048]{1,0:T(8,128)(2,1)}) custom-call(s32[1]{0:T(128)} %bitcast.place, bf16[256,2048]{1,0:T(8,128)(2,1)S(1)} %copy-done, bf16[256,2048]{1,0:T(8,128)(2,1)S(1)} %copy-done.1, bf16[256,2048]{1,0:T(8,128)(2,1)S(1)} %copy-done.2, ...), custom_call_target="tpu_custom_call", output_to_operand_aliasing={{0}: (7, {}), {1}: (8, {})} | custom-call | flops 1024 | bytes 1024 | tf_op jit(solution)/shard_map/pallas_call | solution.py:43
  82.2 1.2 %collective-permute-start.40 = (f32[2,128,128]{2,1,0:T(8,128)S(1)}, f32[2,128,128]{2,1,0:T(8,128)S(1)}, u32[]{:S(2)}, u32[]{:S(2)}) collective-permute-start(f32[2,128,128]{2,1,0:T(8,128)S(1)} %get-tuple-element.199), channel_id=1, source_target_pairs={{0,4},{4,0},{8,12},{12,8},{16,20},{20,16},{24,28},{28,24},{1,5},{5... | collective-permute-start | bytes 393224 | tf_op jit(solution)/shard_map/ppermute | solution.py:245
  83.5 0.7 collective-permute-done.36
  84.2 0.9 %collective-permute-start.39 = (f32[2,128,128]{2,1,0:T(8,128)S(1)}, f32[2,128,128]{2,1,0:T(8,128)S(1)}, u32[]{:S(2)}, u32[]{:S(2)}) collective-permute-start(f32[2,128,128]{2,1,0:T(8,128)S(1)} %get-tuple-element.197), channel_id=1, source_target_pairs={{0,4},{4,0},{8,12},{12,8},{16,20},{20,16},{24,28},{28,24},{1,5},{5... | collective-permute-start | bytes 393224 | tf_op jit(solution)/shard_map/ppermute | solution.py:245
  85.1 1.0 %copy.28 = bf16[256,2048]{1,0:T(8,128)(2,1)} copy(bf16[256,2048]{1,0:T(8,128)(2,1)S(1)} %shard_map.87) | data formatting | bytes 2097152
  86.1 1.8 %shard_map.90 = (bf16[256,2048]{1,0:T(8,128)(2,1)}, bf16[256,2048]{1,0:T(8,128)(2,1)}) custom-call(s32[1]{0:T(128)} %bitcast.place, bf16[256,2048]{1,0:T(8,128)(2,1)S(1)} %copy-done, bf16[256,2048]{1,0:T(8,128)(2,1)S(1)} %copy-done.1, bf16[256,2048]{1,0:T(8,128)(2,1)S(1)} %copy-done.2, ...), custom_call_target="tpu_custom_call", output_to_operand_aliasing={{0}: (10, {}), {1}: (11, {})} | custom-call | flops 1024 | bytes 1024 | tf_op jit(solution)/shard_map/pallas_call | solution.py:43
  87.9 1.9 %shard_map.91 = (bf16[256,2048]{1,0:T(8,128)(2,1)}, bf16[256,2048]{1,0:T(8,128)(2,1)}) custom-call(s32[1]{0:T(128)} %bitcast.place, bf16[256,2048]{1,0:T(8,128)(2,1)S(1)} %copy-done, bf16[256,2048]{1,0:T(8,128)(2,1)S(1)} %copy-done.1, bf16[256,2048]{1,0:T(8,128)(2,1)S(1)} %copy-done.2, ...), custom_call_target="tpu_custom_call", output_to_operand_aliasing={{0}: (8, {}), {1}: (9, {})} | custom-call | flops 1024 | bytes 1024 | tf_op jit(solution)/shard_map/pallas_call | solution.py:43
  89.8 1.2 %shard_map.92 = (bf16[256,2048]{1,0:T(8,128)(2,1)}, bf16[256,2048]{1,0:T(8,128)(2,1)}) custom-call(s32[1]{0:T(128)} %bitcast.place, bf16[256,2048]{1,0:T(8,128)(2,1)S(1)} %copy-done, bf16[256,2048]{1,0:T(8,128)(2,1)S(1)} %copy-done.1, bf16[256,2048]{1,0:T(8,128)(2,1)S(1)} %copy-done.2, ...), custom_call_target="tpu_custom_call", output_to_operand_aliasing={{0}: (6, {}), {1}: (7, {})} | custom-call | flops 1024 | bytes 1024 | tf_op jit(solution)/shard_map/pallas_call | solution.py:43
  91.0 1.2 %shard_map.93 = (bf16[256,2048]{1,0:T(8,128)(2,1)}, bf16[256,2048]{1,0:T(8,128)(2,1)}) custom-call(s32[1]{0:T(128)} %bitcast.place, bf16[256,2048]{1,0:T(8,128)(2,1)S(1)} %copy-done, bf16[256,2048]{1,0:T(8,128)(2,1)S(1)} %copy-done.1, bf16[256,2048]{1,0:T(8,128)(2,1)S(1)} %copy-done.2, ...), custom_call_target="tpu_custom_call", output_to_operand_aliasing={{0}: (6, {}), {1}: (7, {})} | custom-call | flops 1024 | bytes 1024 | tf_op jit(solution)/shard_map/pallas_call | solution.py:43
  (100 shorter events, 15.1 us)
Async XLA Ops:
  2.0 9.1 %collective-permute-start = (f32[2,128,128]{2,1,0:T(8,128)S(1)}, f32[2,128,128]{2,1,0:T(8,128)S(1)}, u32[]{:S(2)}, u32[]{:S(2)}) collective-permute-start(f32[2,128,128]{2,1,0:T(8,128)S(1)} %get-tuple-element.105), channel_id=1, source_target_pairs={{0,4},{4,0},{8,12},{12,8},{16,20},{20,16},{24,28},{28,24},{1,5},{5... | collective-permute-start | bytes 393224 | tf_op jit(solution)/shard_map/ppermute | solution.py:225
  5.0 9.6 %collective-permute-start.4 = (f32[2,128,128]{2,1,0:T(8,128)S(1)}, f32[2,128,128]{2,1,0:T(8,128)S(1)}, u32[]{:S(2)}, u32[]{:S(2)}) collective-permute-start(f32[2,128,128]{2,1,0:T(8,128)S(1)} %get-tuple-element.111), channel_id=1, source_target_pairs={{0,4},{4,0},{8,12},{12,8},{16,20},{20,16},{24,28},{28,24},{1,5},{5... | collective-permute-start | bytes 393224 | tf_op jit(solution)/shard_map/ppermute | solution.py:225
  6.4 9.8 %collective-permute-start.3 = (f32[2,128,128]{2,1,0:T(8,128)S(1)}, f32[2,128,128]{2,1,0:T(8,128)S(1)}, u32[]{:S(2)}, u32[]{:S(2)}) collective-permute-start(f32[2,128,128]{2,1,0:T(8,128)S(1)} %get-tuple-element.109), channel_id=1, source_target_pairs={{0,4},{4,0},{8,12},{12,8},{16,20},{20,16},{24,28},{28,24},{1,5},{5... | collective-permute-start | bytes 393224 | tf_op jit(solution)/shard_map/ppermute | solution.py:225
  11.1 8.3 %collective-permute-start.2 = (f32[2,128,128]{2,1,0:T(8,128)S(1)}, f32[2,128,128]{2,1,0:T(8,128)S(1)}, u32[]{:S(2)}, u32[]{:S(2)}) collective-permute-start(f32[2,128,128]{2,1,0:T(8,128)S(1)} %get-tuple-element.238), channel_id=1, source_target_pairs={{0,8},{4,12},{1,9},{5,13},{2,10},{6,14},{3,11},{7,15}} | collective-permute-start | bytes 393224 | tf_op jit(solution)/shard_map/ppermute | solution.py:190
  14.6 9.0 %collective-permute-start.8 = (f32[2,128,128]{2,1,0:T(8,128)S(1)}, f32[2,128,128]{2,1,0:T(8,128)S(1)}, u32[]{:S(2)}, u32[]{:S(2)}) collective-permute-start(f32[2,128,128]{2,1,0:T(8,128)S(1)} %get-tuple-element.240), channel_id=1, source_target_pairs={{0,8},{4,12},{1,9},{5,13},{2,10},{6,14},{3,11},{7,15}} | collective-permute-start | bytes 393224 | tf_op jit(solution)/shard_map/ppermute | solution.py:190
  16.2 5.0 %collective-permute-start.1 = (f32[2,128,128]{2,1,0:T(8,128)S(1)}, f32[2,128,128]{2,1,0:T(8,128)S(1)}, u32[]{:S(2)}, u32[]{:S(2)}) collective-permute-start(f32[2,128,128]{2,1,0:T(8,128)S(1)} %get-tuple-element.107), channel_id=1, source_target_pairs={{0,4},{4,0},{8,12},{12,8},{16,20},{20,16},{24,28},{28,24},{1,5},{5... | collective-permute-start | bytes 393224 | tf_op jit(solution)/shard_map/ppermute | solution.py:225
  17.8 6.5 %collective-permute-start.7 = (f32[2,128,128]{2,1,0:T(8,128)S(1)}, f32[2,128,128]{2,1,0:T(8,128)S(1)}, u32[]{:S(2)}, u32[]{:S(2)}) collective-permute-start(f32[2,128,128]{2,1,0:T(8,128)S(1)} %get-tuple-element.242), channel_id=1, source_target_pairs={{0,8},{4,12},{1,9},{5,13},{2,10},{6,14},{3,11},{7,15}} | collective-permute-start | bytes 393224 | tf_op jit(solution)/shard_map/ppermute | solution.py:190
  19.4 5.7 %collective-permute-start.6 = (f32[2,128,128]{2,1,0:T(8,128)S(1)}, f32[2,128,128]{2,1,0:T(8,128)S(1)}, u32[]{:S(2)}, u32[]{:S(2)}) collective-permute-start(f32[2,128,128]{2,1,0:T(8,128)S(1)} %add.152), channel_id=1, source_target_pairs={{8,16},{12,20},{9,17},{13,21},{10,18},{14,22},{11,19},{15,23}} | collective-permute-start | bytes 393224 | tf_op jit(solution)/shard_map/ppermute | solution.py:190
  21.2 4.9 %collective-permute-start.5 = (f32[2,128,128]{2,1,0:T(8,128)S(1)}, f32[2,128,128]{2,1,0:T(8,128)S(1)}, u32[]{:S(2)}, u32[]{:S(2)}) collective-permute-start(f32[2,128,128]{2,1,0:T(8,128)S(1)} %get-tuple-element.244), channel_id=1, source_target_pairs={{0,8},{4,12},{1,9},{5,13},{2,10},{6,14},{3,11},{7,15}} | collective-permute-start | bytes 393224 | tf_op jit(solution)/shard_map/ppermute | solution.py:190
  23.7 3.2 %collective-permute-start.12 = (f32[2,128,128]{2,1,0:T(8,128)S(1)}, f32[2,128,128]{2,1,0:T(8,128)S(1)}, u32[]{:S(2)}, u32[]{:S(2)}) collective-permute-start(f32[2,128,128]{2,1,0:T(8,128)S(1)} %add.154), channel_id=1, source_target_pairs={{8,16},{12,20},{9,17},{13,21},{10,18},{14,22},{11,19},{15,23}} | collective-permute-start | bytes 393224 | tf_op jit(solution)/shard_map/ppermute | solution.py:190
  24.4 3.2 %collective-permute-start.11 = (f32[2,128,128]{2,1,0:T(8,128)S(1)}, f32[2,128,128]{2,1,0:T(8,128)S(1)}, u32[]{:S(2)}, u32[]{:S(2)}) collective-permute-start(f32[2,128,128]{2,1,0:T(8,128)S(1)} %add.155), channel_id=1, source_target_pairs={{8,16},{12,20},{9,17},{13,21},{10,18},{14,22},{11,19},{15,23}} | collective-permute-start | bytes 393224 | tf_op jit(solution)/shard_map/ppermute | solution.py:190
  25.1 3.2 %collective-permute-start.10 = (f32[2,128,128]{2,1,0:T(8,128)S(1)}, f32[2,128,128]{2,1,0:T(8,128)S(1)}, u32[]{:S(2)}, u32[]{:S(2)}) collective-permute-start(f32[2,128,128]{2,1,0:T(8,128)S(1)} %get-tuple-element.227), channel_id=1, source_target_pairs={{16,24},{20,28},{17,25},{21,29},{18,26},{22,30},{19,27},{23,31}} | collective-permute-start | bytes 393224 | tf_op jit(solution)/shard_map/ppermute | solution.py:190
  26.1 2.9 %collective-permute-start.9 = (f32[2,128,128]{2,1,0:T(8,128)S(1)}, f32[2,128,128]{2,1,0:T(8,128)S(1)}, u32[]{:S(2)}, u32[]{:S(2)}) collective-permute-start(f32[2,128,128]{2,1,0:T(8,128)S(1)} %add.158), channel_id=1, source_target_pairs={{8,16},{12,20},{9,17},{13,21},{10,18},{14,22},{11,19},{15,23}} | collective-permute-start | bytes 393224 | tf_op jit(solution)/shard_map/ppermute | solution.py:190
  26.9 3.1 %collective-permute-start.15 = (f32[2,128,128]{2,1,0:T(8,128)S(1)}, f32[2,128,128]{2,1,0:T(8,128)S(1)}, u32[]{:S(2)}, u32[]{:S(2)}) collective-permute-start(f32[2,128,128]{2,1,0:T(8,128)S(1)} %get-tuple-element.225), channel_id=1, source_target_pairs={{16,24},{20,28},{17,25},{21,29},{18,26},{22,30},{19,27},{23,31}} | collective-permute-start | bytes 393224 | tf_op jit(solution)/shard_map/ppermute | solution.py:190
  27.6 3.8 %collective-permute-start.14 = (f32[2,128,128]{2,1,0:T(8,128)S(1)}, f32[2,128,128]{2,1,0:T(8,128)S(1)}, u32[]{:S(2)}, u32[]{:S(2)}) collective-permute-start(f32[2,128,128]{2,1,0:T(8,128)S(1)} %get-tuple-element.223), channel_id=1, source_target_pairs={{16,24},{20,28},{17,25},{21,29},{18,26},{22,30},{19,27},{23,31}} | collective-permute-start | bytes 393224 | tf_op jit(solution)/shard_map/ppermute | solution.py:190
  28.3 5.3 %copy-start.2 = (bf16[256,2048]{1,0:T(8,128)(2,1)S(1)}, bf16[256,2048]{1,0:T(8,128)(2,1)}, u32[]{:S(2)}) copy-start(bf16[256,2048]{1,0:T(8,128)(2,1)} %v.17) | copy-start | bytes 3145732
  28.3 6.5 %collective-permute-start.19 = (f32[2,128,128]{2,1,0:T(8,128)S(1)}, f32[2,128,128]{2,1,0:T(8,128)S(1)}, u32[]{:S(2)}, u32[]{:S(2)}) collective-permute-start(f32[2,128,128]{2,1,0:T(8,128)S(1)} %get-tuple-element.221), channel_id=1, source_target_pairs={{0,4},{4,0},{8,12},{12,8},{16,20},{20,16},{24,28},{28,24},{1,5},{5... | collective-permute-start | bytes 393224 | tf_op jit(solution)/shard_map/ppermute | solution.py:245
  29.1 4.5 %copy-start.1 = (bf16[256,2048]{1,0:T(8,128)(2,1)S(1)}, bf16[256,2048]{1,0:T(8,128)(2,1)}, u32[]{:S(2)}) copy-start(bf16[256,2048]{1,0:T(8,128)(2,1)} %k.17) | copy-start | bytes 3145732
  29.1 4.5 %copy-start = (bf16[256,2048]{1,0:T(8,128)(2,1)S(1)}, bf16[256,2048]{1,0:T(8,128)(2,1)}, u32[]{:S(2)}) copy-start(bf16[256,2048]{1,0:T(8,128)(2,1)} %q.15) | copy-start | bytes 3145732
  29.1 3.0 %collective-permute-start.13 = (f32[2,128,128]{2,1,0:T(8,128)S(1)}, f32[2,128,128]{2,1,0:T(8,128)S(1)}, u32[]{:S(2)}, u32[]{:S(2)}) collective-permute-start(f32[2,128,128]{2,1,0:T(8,128)S(1)} %get-tuple-element.219), channel_id=1, source_target_pairs={{16,24},{20,28},{17,25},{21,29},{18,26},{22,30},{19,27},{23,31}} | collective-permute-start | bytes 393224 | tf_op jit(solution)/shard_map/ppermute | solution.py:190
  30.0 7.2 %collective-permute-start.18 = (f32[2,128,128]{2,1,0:T(8,128)S(1)}, f32[2,128,128]{2,1,0:T(8,128)S(1)}, u32[]{:S(2)}, u32[]{:S(2)}) collective-permute-start(f32[2,128,128]{2,1,0:T(8,128)S(1)} %get-tuple-element.217), channel_id=1, source_target_pairs={{0,4},{4,0},{8,12},{12,8},{16,20},{20,16},{24,28},{28,24},{1,5},{5... | collective-permute-start | bytes 393224 | tf_op jit(solution)/shard_map/ppermute | solution.py:245
  31.4 7.2 %collective-permute-start.17 = (f32[2,128,128]{2,1,0:T(8,128)S(1)}, f32[2,128,128]{2,1,0:T(8,128)S(1)}, u32[]{:S(2)}, u32[]{:S(2)}) collective-permute-start(f32[2,128,128]{2,1,0:T(8,128)S(1)} %get-tuple-element.215), channel_id=1, source_target_pairs={{0,4},{4,0},{8,12},{12,8},{16,20},{20,16},{24,28},{28,24},{1,5},{5... | collective-permute-start | bytes 393224 | tf_op jit(solution)/shard_map/ppermute | solution.py:245
  32.2 1.4 %copy-start.4 = (bf16[2048]{0:T(1024)(128)(2,1)S(1)}, bf16[2048]{0:T(1024)(128)(2,1)}, u32[]{:S(2)}) copy-start(bf16[2048]{0:T(1024)(128)(2,1)} %param.9) | copy-start | bytes 12292
  32.2 7.8 %collective-permute-start.16 = (f32[2,128,128]{2,1,0:T(8,128)S(1)}, f32[2,128,128]{2,1,0:T(8,128)S(1)}, u32[]{:S(2)}, u32[]{:S(2)}) collective-permute-start(f32[2,128,128]{2,1,0:T(8,128)S(1)} %get-tuple-element.213), channel_id=1, source_target_pairs={{0,4},{4,0},{8,12},{12,8},{16,20},{20,16},{24,28},{28,24},{1,5},{5... | collective-permute-start | bytes 393224 | tf_op jit(solution)/shard_map/ppermute | solution.py:245
  33.6 1.2 %copy-start.3 = (bf16[256,2048]{1,0:T(8,128)(2,1)S(1)}, bf16[256,2048]{1,0:T(8,128)(2,1)}, u32[]{:S(2)}) copy-start(bf16[256,2048]{1,0:T(8,128)(2,1)} %refs_7_.3) | copy-start | bytes 3145732
  40.4 3.1 %collective-permute-start.22 = (f32[2,256]{1,0:T(2,128)S(1)}, f32[2,256]{1,0:T(2,128)S(1)}, u32[]{:S(2)}, u32[]{:S(2)}) collective-permute-start(f32[2,256]{1,0:T(2,128)S(1)} %get-tuple-element.134.refs_0_), channel_id=1, source_target_pairs={{0,3},{1,2},{2,1},{3,0},{4,7},{5,6},{6,5},{7,4},{8,11},{9,10},{10,... | collective-permute-start | bytes 6152 | tf_op jit(solution)/shard_map/ppermute | solution.py:333
  40.5 3.7 %collective-permute-start.21 = (f32[2,256]{1,0:T(2,128)S(1)}, f32[2,256]{1,0:T(2,128)S(1)}, u32[]{:S(2)}, u32[]{:S(2)}) collective-permute-start(f32[2,256]{1,0:T(2,128)S(1)} %get-tuple-element.134.refs_0_), channel_id=1, source_target_pairs={{0,2},{1,3},{2,0},{3,1},{4,6},{5,7},{6,4},{7,5},{8,10},{9,11},{10,... | collective-permute-start | bytes 6152 | tf_op jit(solution)/shard_map/ppermute | solution.py:333
  42.0 2.1 %collective-permute-start.20 = (f32[2,256]{1,0:T(2,128)S(1)}, f32[2,256]{1,0:T(2,128)S(1)}, u32[]{:S(2)}, u32[]{:S(2)}) collective-permute-start(f32[2,256]{1,0:T(2,128)S(1)} %get-tuple-element.134.refs_0_), channel_id=1, source_target_pairs={{0,1},{1,0},{2,3},{3,2},{4,5},{5,4},{6,7},{7,6},{8,9},{9,8},{10,11... | collective-permute-start | bytes 6152 | tf_op jit(solution)/shard_map/ppermute | solution.py:333
  44.5 6.4 %collective-permute-start.25 = (f32[2,128,128]{2,1,0:T(8,128)S(1)}, f32[2,128,128]{2,1,0:T(8,128)S(1)}, u32[]{:S(2)}, u32[]{:S(2)}) collective-permute-start(f32[2,128,128]{2,1,0:T(8,128)S(1)} %get-tuple-element.149), channel_id=1, source_target_pairs={{0,4},{4,0},{8,12},{12,8},{16,20},{20,16},{24,28},{28,24},{1,5},{5... | collective-permute-start | bytes 393224 | tf_op jit(solution)/shard_map/ppermute | solution.py:225
  46.4 7.4 %collective-permute-start.24 = (f32[2,128,128]{2,1,0:T(8,128)S(1)}, f32[2,128,128]{2,1,0:T(8,128)S(1)}, u32[]{:S(2)}, u32[]{:S(2)}) collective-permute-start(f32[2,128,128]{2,1,0:T(8,128)S(1)} %get-tuple-element.147), channel_id=1, source_target_pairs={{0,4},{4,0},{8,12},{12,8},{16,20},{20,16},{24,28},{28,24},{1,5},{5... | collective-permute-start | bytes 393224 | tf_op jit(solution)/shard_map/ppermute | solution.py:225
  47.1 9.4 %collective-permute-start.23 = (f32[2,128,128]{2,1,0:T(8,128)S(1)}, f32[2,128,128]{2,1,0:T(8,128)S(1)}, u32[]{:S(2)}, u32[]{:S(2)}) collective-permute-start(f32[2,128,128]{2,1,0:T(8,128)S(1)} %get-tuple-element.143), channel_id=1, source_target_pairs={{0,4},{4,0},{8,12},{12,8},{16,20},{20,16},{24,28},{28,24},{1,5},{5... | collective-permute-start | bytes 393224 | tf_op jit(solution)/shard_map/ppermute | solution.py:225
  51.0 6.3 %collective-permute-start.29 = (f32[2,128,128]{2,1,0:T(8,128)S(1)}, f32[2,128,128]{2,1,0:T(8,128)S(1)}, u32[]{:S(2)}, u32[]{:S(2)}) collective-permute-start(f32[2,128,128]{2,1,0:T(8,128)S(1)} %get-tuple-element.236), channel_id=1, source_target_pairs={{28,20},{24,16},{29,21},{25,17},{30,22},{26,18},{31,23},{27,19}} | collective-permute-start | bytes 393224 | tf_op jit(solution)/shard_map/ppermute | solution.py:190
  51.6 7.2 %collective-permute-start.28 = (f32[2,128,128]{2,1,0:T(8,128)S(1)}, f32[2,128,128]{2,1,0:T(8,128)S(1)}, u32[]{:S(2)}, u32[]{:S(2)}) collective-permute-start(f32[2,128,128]{2,1,0:T(8,128)S(1)} %get-tuple-element.154), channel_id=1, source_target_pairs={{0,4},{4,0},{8,12},{12,8},{16,20},{20,16},{24,28},{28,24},{1,5},{5... | collective-permute-start | bytes 393224 | tf_op jit(solution)/shard_map/ppermute | solution.py:225
  53.8 5.7 %collective-permute-start.27 = (f32[2,128,128]{2,1,0:T(8,128)S(1)}, f32[2,128,128]{2,1,0:T(8,128)S(1)}, u32[]{:S(2)}, u32[]{:S(2)}) collective-permute-start(f32[2,128,128]{2,1,0:T(8,128)S(1)} %get-tuple-element.234), channel_id=1, source_target_pairs={{28,20},{24,16},{29,21},{25,17},{30,22},{26,18},{31,23},{27,19}} | collective-permute-start | bytes 393224 | tf_op jit(solution)/shard_map/ppermute | solution.py:190
  56.6 3.7 %collective-permute-start.26 = (f32[2,128,128]{2,1,0:T(8,128)S(1)}, f32[2,128,128]{2,1,0:T(8,128)S(1)}, u32[]{:S(2)}, u32[]{:S(2)}) collective-permute-start(f32[2,128,128]{2,1,0:T(8,128)S(1)} %get-tuple-element.232), channel_id=1, source_target_pairs={{28,20},{24,16},{29,21},{25,17},{30,22},{26,18},{31,23},{27,19}} | collective-permute-start | bytes 393224 | tf_op jit(solution)/shard_map/ppermute | solution.py:190
  57.3 5.5 %collective-permute-start.31 = (f32[2,128,128]{2,1,0:T(8,128)S(1)}, f32[2,128,128]{2,1,0:T(8,128)S(1)}, u32[]{:S(2)}, u32[]{:S(2)}) collective-permute-start(f32[2,128,128]{2,1,0:T(8,128)S(1)} %add.176), channel_id=1, source_target_pairs={{20,12},{16,8},{21,13},{17,9},{22,14},{18,10},{23,15},{19,11}} | collective-permute-start | bytes 393224 | tf_op jit(solution)/shard_map/ppermute | solution.py:190
  58.8 5.3 %collective-permute-start.30 = (f32[2,128,128]{2,1,0:T(8,128)S(1)}, f32[2,128,128]{2,1,0:T(8,128)S(1)}, u32[]{:S(2)}, u32[]{:S(2)}) collective-permute-start(f32[2,128,128]{2,1,0:T(8,128)S(1)} %get-tuple-element.230), channel_id=1, source_target_pairs={{28,20},{24,16},{29,21},{25,17},{30,22},{26,18},{31,23},{27,19}} | collective-permute-start | bytes 393224 | tf_op jit(solution)/shard_map/ppermute | solution.py:190
  59.6 5.3 %collective-permute-start.35 = (f32[2,128,128]{2,1,0:T(8,128)S(1)}, f32[2,128,128]{2,1,0:T(8,128)S(1)}, u32[]{:S(2)}, u32[]{:S(2)}) collective-permute-start(f32[2,128,128]{2,1,0:T(8,128)S(1)} %add.178), channel_id=1, source_target_pairs={{20,12},{16,8},{21,13},{17,9},{22,14},{18,10},{23,15},{19,11}} | collective-permute-start | bytes 393224 | tf_op jit(solution)/shard_map/ppermute | solution.py:190
  60.3 5.9 %collective-permute-start.34 = (f32[2,128,128]{2,1,0:T(8,128)S(1)}, f32[2,128,128]{2,1,0:T(8,128)S(1)}, u32[]{:S(2)}, u32[]{:S(2)}) collective-permute-start(f32[2,128,128]{2,1,0:T(8,128)S(1)} %add.179), channel_id=1, source_target_pairs={{20,12},{16,8},{21,13},{17,9},{22,14},{18,10},{23,15},{19,11}} | collective-permute-start | bytes 393224 | tf_op jit(solution)/shard_map/ppermute | solution.py:190
  62.8 13.2 %collective-permute-start.33 = (f32[2,128,128]{2,1,0:T(8,128)S(1)}, f32[2,128,128]{2,1,0:T(8,128)S(1)}, u32[]{:S(2)}, u32[]{:S(2)}) collective-permute-start(f32[2,128,128]{2,1,0:T(8,128)S(1)} %get-tuple-element.211), channel_id=1, source_target_pairs={{12,4},{8,0},{13,5},{9,1},{14,6},{10,2},{15,7},{11,3}} | collective-permute-start | bytes 393224 | tf_op jit(solution)/shard_map/ppermute | solution.py:190
  64.2 13.1 %collective-permute-start.32 = (f32[2,128,128]{2,1,0:T(8,128)S(1)}, f32[2,128,128]{2,1,0:T(8,128)S(1)}, u32[]{:S(2)}, u32[]{:S(2)}) collective-permute-start(f32[2,128,128]{2,1,0:T(8,128)S(1)} %add.182), channel_id=1, source_target_pairs={{20,12},{16,8},{21,13},{17,9},{22,14},{18,10},{23,15},{19,11}} | collective-permute-start | bytes 393224 | tf_op jit(solution)/shard_map/ppermute | solution.py:190
  64.9 15.1 %collective-permute-start.38 = (f32[2,128,128]{2,1,0:T(8,128)S(1)}, f32[2,128,128]{2,1,0:T(8,128)S(1)}, u32[]{:S(2)}, u32[]{:S(2)}) collective-permute-start(f32[2,128,128]{2,1,0:T(8,128)S(1)} %get-tuple-element.209), channel_id=1, source_target_pairs={{12,4},{8,0},{13,5},{9,1},{14,6},{10,2},{15,7},{11,3}} | collective-permute-start | bytes 393224 | tf_op jit(solution)/shard_map/ppermute | solution.py:190
  66.2 16.0 %collective-permute-start.37 = (f32[2,128,128]{2,1,0:T(8,128)S(1)}, f32[2,128,128]{2,1,0:T(8,128)S(1)}, u32[]{:S(2)}, u32[]{:S(2)}) collective-permute-start(f32[2,128,128]{2,1,0:T(8,128)S(1)} %get-tuple-element.207), channel_id=1, source_target_pairs={{12,4},{8,0},{13,5},{9,1},{14,6},{10,2},{15,7},{11,3}} | collective-permute-start | bytes 393224 | tf_op jit(solution)/shard_map/ppermute | solution.py:190
  76.0 11.9 %collective-permute-start.41 = (f32[2,128,128]{2,1,0:T(8,128)S(1)}, f32[2,128,128]{2,1,0:T(8,128)S(1)}, u32[]{:S(2)}, u32[]{:S(2)}) collective-permute-start(f32[2,128,128]{2,1,0:T(8,128)S(1)} %get-tuple-element.205), channel_id=1, source_target_pairs={{0,4},{4,0},{8,12},{12,8},{16,20},{20,16},{24,28},{28,24},{1,5},{5... | collective-permute-start | bytes 393224 | tf_op jit(solution)/shard_map/ppermute | solution.py:245
  77.3 6.9 %collective-permute-start.36 = (f32[2,128,128]{2,1,0:T(8,128)S(1)}, f32[2,128,128]{2,1,0:T(8,128)S(1)}, u32[]{:S(2)}, u32[]{:S(2)}) collective-permute-start(f32[2,128,128]{2,1,0:T(8,128)S(1)} %get-tuple-element.203), channel_id=1, source_target_pairs={{12,4},{8,0},{13,5},{9,1},{14,6},{10,2},{15,7},{11,3}} | collective-permute-start | bytes 393224 | tf_op jit(solution)/shard_map/ppermute | solution.py:190
  80.0 7.9 %collective-permute-start.42 = (f32[2,128,128]{2,1,0:T(8,128)S(1)}, f32[2,128,128]{2,1,0:T(8,128)S(1)}, u32[]{:S(2)}, u32[]{:S(2)}) collective-permute-start(f32[2,128,128]{2,1,0:T(8,128)S(1)} %get-tuple-element.201), channel_id=1, source_target_pairs={{0,4},{4,0},{8,12},{12,8},{16,20},{20,16},{24,28},{28,24},{1,5},{5... | collective-permute-start | bytes 393224 | tf_op jit(solution)/shard_map/ppermute | solution.py:245
  82.2 7.6 %collective-permute-start.40 = (f32[2,128,128]{2,1,0:T(8,128)S(1)}, f32[2,128,128]{2,1,0:T(8,128)S(1)}, u32[]{:S(2)}, u32[]{:S(2)}) collective-permute-start(f32[2,128,128]{2,1,0:T(8,128)S(1)} %get-tuple-element.199), channel_id=1, source_target_pairs={{0,4},{4,0},{8,12},{12,8},{16,20},{20,16},{24,28},{28,24},{1,5},{5... | collective-permute-start | bytes 393224 | tf_op jit(solution)/shard_map/ppermute | solution.py:245
  84.2 6.8 %collective-permute-start.39 = (f32[2,128,128]{2,1,0:T(8,128)S(1)}, f32[2,128,128]{2,1,0:T(8,128)S(1)}, u32[]{:S(2)}, u32[]{:S(2)}) collective-permute-start(f32[2,128,128]{2,1,0:T(8,128)S(1)} %get-tuple-element.197), channel_id=1, source_target_pairs={{0,4},{4,0},{8,12},{12,8},{16,20},{20,16},{24,28},{28,24},{1,5},{5... | collective-permute-start | bytes 393224 | tf_op jit(solution)/shard_map/ppermute | solution.py:245
